TPU v7x, 32 devices: a whole 2x2x4 slice. The times are simulated.
32 devices in a mesh: blk: 8 (over y, x, core), inner: 4 (over z).
Axes of the slice: x: 2, y: 2, z: 4, core: 2. Of those that a mesh axis runs over, the one named last changes fastest.
Arguments:
- teacher: bfloat16 [2048, 1536], P(('blk', 'inner')), may hold values from -50 to 50
- student: bfloat16 [2048, 768], P(('blk', 'inner')), may hold values from -50 to 50
Outputs:
- loss: float32 [], replicated
- student_grad: float32 [2048, 768], P(('blk', 'inner'))
All inputs are finite; a program needn't handle non-finite values.
Results may differ from a plain program's by a relative error of at most 0.00055.
The roundings to bfloat16 on the way count: a program that leaves them out, or rounds other values in their place, can miss the bound.
Values may be sent and summed in bfloat16 or wider, within the bound.
No kernel may reach another device: no remote copies, remote signals or barrier semaphores. Data moves between devices by JAX's collectives and lax.ppermute only.
A program may use at most 64 MiB of HBM per device.

v0:
```python
import math

import jax
import jax.numpy as jnp
from jax import lax
from jax.sharding import PartitionSpec as P

DS = 768


EPSILON = 1e-06


def coefficients(sq_student, sq_teacher, cross, total):
    norm_student = jnp.sqrt(sq_student + EPSILON)
    norm_teacher = jnp.sqrt(sq_teacher + EPSILON)
    factor = 2.0 * math.sqrt(total * DS) / total
    cubed = norm_student * norm_student * norm_student
    alpha = factor * (EPSILON / norm_student + cross / norm_teacher) / cubed
    beta = factor / (norm_student * norm_teacher)
    terms = (
        sq_student / (norm_student * norm_student)
        + sq_teacher / (norm_teacher * norm_teacher)
        - 2.0 * cross / (norm_student * norm_teacher)
    )
    return (alpha, beta, terms)


def tile_grams(rows_t, rows_s, piece_t, piece_s):
    gram_s = jnp.einsum("rd,cd->rc", rows_s, piece_s, preferred_element_type=jnp.float32)
    gram_t = jnp.einsum("rd,cd->rc", rows_t, piece_t, preferred_element_type=jnp.float32)
    return (gram_s, gram_t)


def per_device(teacher, student):
    rows = teacher.shape[0]
    blocks = lax.axis_size("blk")
    inner = lax.axis_size("inner")
    total = rows * blocks * inner
    group_t, group_s = (
        lax.all_gather(teacher, "inner", axis=0, tiled=True),
        lax.all_gather(student, "inner", axis=0, tiled=True),
    )
    pieces = (
        lax.all_gather(teacher, "blk", axis=0, tiled=True),
        lax.all_gather(student, "blk", axis=0, tiled=True),
    )
    gram_s, gram_t = tile_grams(group_t, group_s, pieces[0], pieces[1])
    sq_s = jnp.sum(gram_s * gram_s, 1)
    sq_t = jnp.sum(gram_t * gram_t, 1)
    cross = jnp.sum(gram_s * gram_t, 1)
    sum_s, sum_t, sum_c = lax.psum((sq_s, sq_t, cross), "inner")
    alpha, beta, terms = coefficients(sum_s, sum_t, sum_c, total)
    loss = lax.psum(jnp.sum(terms), "blk") / total
    pieces = (
        lax.all_gather(teacher, "blk", axis=0, tiled=True),
        lax.all_gather(student, "blk", axis=0, tiled=True),
    )
    gram_s, gram_t = tile_grams(group_t, group_s, pieces[0], pieces[1])
    weights = (alpha[:, None] * gram_s - beta[:, None] * gram_t).astype(jnp.bfloat16)
    row_acc = jnp.dot(weights, pieces[1], preferred_element_type=jnp.float32)
    col_term = jnp.einsum("rc,rd->cd", weights, group_s, preferred_element_type=jnp.float32)
    col_buf = col_term
    row_acc, col_buf = (row_acc, col_buf)
    row_mine = lax.psum_scatter(row_acc, "inner", scatter_dimension=0, tiled=True)
    col_mine = lax.psum_scatter(col_buf, "blk", scatter_dimension=0, tiled=True)
    return (loss, row_mine + col_mine)


def solution(mesh):
    return jax.shard_map(
        per_device,
        mesh=mesh,
        in_specs=(P(("blk", "inner"), None), P(("blk", "inner"), None)),
        out_specs=(P(), P(("blk", "inner"), None)),
        check_vma=False,
    )
```

profile of v0, /device:TPU:0, one launch (start us, length us, event | category | flops | bytes accessed | tf_op | source)
XLA Modules:
  0.0 143.4 jit_solution(2740398591827729677)
XLA Ops:
  7.2 0.0 copy-start
  7.2 0.0 all-gather.2.cloned.1.call-start
  7.2 0.7 all-gather.2.cloned.1.call-update
  7.9 0.0 reduce-scatter.3.cloned.1.call-start
  8.0 16.4 %all_gather.14 = bf16[256,768]{1,0:T(8,128)(2,1)S(1)} all-gather(bf16[64,768]{1,0:T(8,128)(2,1)} %param.3), channel_id=1, replica_groups=mesh['blk'=8,'inner'=4] {'inner'}, dimensions={0}, use_global_device_ids=true | all-gather | bytes 491520 | tf_op jit(solution)/shard_map/all_gather | solution.py:42
  24.4 12.4 %all_gather.15 = bf16[512,768]{1,0:T(8,128)(2,1)S(1)} all-gather(bf16[64,768]{1,0:T(8,128)(2,1)} %param.3), channel_id=1, replica_groups=mesh['blk'=8,'inner'=4] {'blk'}, dimensions={0}, use_global_device_ids=true | all-gather | bytes 884736 | tf_op jit(solution)/shard_map/all_gather | solution.py:46
  36.8 0.0 copy-done
  36.8 20.6 %all_gather.16 = bf16[256,1536]{1,0:T(8,128)(2,1)S(1)} all-gather(bf16[64,1536]{1,0:T(8,128)(2,1)S(1)} %copy-done), channel_id=1, replica_groups=mesh['blk'=8,'inner'=4] {'inner'}, dimensions={0}, use_global_device_ids=true | all-gather | bytes 983040 | tf_op jit(solution)/shard_map/all_gather | solution.py:41
  57.4 0.0 all-gather.2.cloned.1.call-done
  57.4 2.0 %fusion.4 = f32[256,512]{1,0:T(8,128)S(1)} fusion(bf16[256,1536]{1,0:T(8,128)(2,1)S(1)} %all_gather.16, bf16[512,1536]{1,0:T(8,128)(2,1)} %all-gather.2.cloned.1.call-done), kind=kOutput, calls=%fused_computation.14 | convolution fusion | flops 402653184 | bytes 2883584 | tf_op jit(solution)/shard_map/rd,cd->rc/dot_general | solution.py:31
  59.5 0.6 multiply_reduce_fusion.2
  60.0 10.2 %all-reduce = (f32[256]{0:T(256)S(1)}, f32[256]{0:T(256)S(1)}, f32[256]{0:T(256)S(1)}) all-reduce(f32[256]{0:T(256)S(1)} %get-tuple-element.3, f32[256]{0:T(256)S(1)} %get-tuple-element.4, f32[256]{0:T(256)S(1)} %get-tuple-element.2), channel_id=1, replica_groups=mesh['blk'=8,'inner'=4] {'inner'}, use_global_device_ids=true, to_apply=%region_5.0 | all-reduce | flops 768 | bytes 6144 | tf_op jit(solution)/shard_map/psum | solution.py:52
  70.2 0.6 fusion.1
  70.8 0.1 subtract_convert_fusion
  71.0 1.3 fusion.5
  72.3 0.0 reduce-scatter.3.cloned.1.call-update
  72.3 0.0 reduce-scatter.5.cloned.1.call-start
  72.3 1.6 %fusion.6 = f32[512,768]{1,0:T(8,128)} fusion(bf16[256,512]{1,0:T(8,128)(2,1)S(1)} %subtract_convert_fusion, bf16[256,768]{1,0:T(8,128)(2,1)S(1)} %all_gather.14), kind=kOutput, calls=%fused_computation.16 | convolution fusion | flops 201326592 | bytes 2228224 | tf_op jit(solution)/shard_map/rc,rd->cd/dot_general | solution.py:62
  73.9 0.0 reduce-scatter.5.cloned.1.call-update
  73.9 12.6 %psum.31 = f32[]{:T(128)} all-reduce(f32[]{:T(128)} %get-tuple-element.9), channel_id=1, replica_groups=mesh['blk'=8,'inner'=4] {'blk'}, use_global_device_ids=true, to_apply=%region_7.0 | all-reduce | flops 1 | bytes 8 | tf_op jit(solution)/shard_map/psum | solution.py:54
  87.1 5.8 %reduce-scatter.3.cloned.1.call-done = f32[64,768]{1,0:T(8,128)} async-done(((f32[256,768]{1,0:T(8,128)}), f32[64,768]{1,0:T(8,128)}) %reduce-scatter.3.cloned.1.call-update) | async-done | bytes 196624 | tf_op jit(solution)/shard_map/reduce_scatter | solution.py:65
  93.0 41.1 %reduce-scatter.5.cloned.1.call-done = f32[64,768]{1,0:T(8,128)} async-done(((f32[512,768]{1,0:T(8,128)}), f32[64,768]{1,0:T(8,128)}) %reduce-scatter.5.cloned.1.call-update) | async-done | bytes 196624 | tf_op jit(solution)/shard_map/reduce_scatter | solution.py:66
  134.0 1.7 %add.31 = f32[64,768]{1,0:T(8,128)} add(f32[64,768]{1,0:T(8,128)} %reduce-scatter.3.cloned.1.call-done, f32[64,768]{1,0:T(8,128)} %reduce-scatter.5.cloned.1.call-done) | non-fusion elementwise | flops 49152 | bytes 589824 | tf_op jit(solution)/shard_map/add | solution.py:67
Async XLA Ops:
  7.2 29.7 %copy-start = (bf16[64,1536]{1,0:T(8,128)(2,1)S(1)}, bf16[64,1536]{1,0:T(8,128)(2,1)}, u32[]{:S(2)}) copy-start(bf16[64,1536]{1,0:T(8,128)(2,1)} %param.2) | copy-start | bytes 589828
  7.2 50.3 %all-gather.2.cloned.1.call-start = ((), (), s32[]{:S(2)}) async-start(), calls=%async_computation.2 | async-start | bytes 1769472 | tf_op jit(solution)/shard_map/all_gather | solution.py:45
  7.9 85.1 %reduce-scatter.3.cloned.1.call-start = ((), (), s32[]{:S(2)}) async-start(), calls=%async_computation.3 | async-start | bytes 983040 | tf_op jit(solution)/shard_map/reduce_scatter | solution.py:65
  72.3 61.8 %reduce-scatter.5.cloned.1.call-start = ((), (), s32[]{:S(2)}) async-start(), calls=%async_computation.4 | async-start | bytes 1769472 | tf_op jit(solution)/shard_map/reduce_scatter | solution.py:66
Sparse Core Ops, SparseCore 0:
  9.9 29.4 all-gather.1
  72.4 20.5 reduce-scatter.2
  96.3 37.7 reduce-scatter.4
where the time goes:
time: 144 us; the launch traced here: 143 us
  blocking collectives  72.3 us (50%)
  waiting for transfers between devices  47.6 us (33%)
  between operations  15.6 us (11%)
  matrix products  5.39 us (4%)
  other arithmetic  2.47 us (2%)
    reduce_scatter x1, waiting for transfers between devices, per_device(): col_mine = lax.psum_scatter(col_buf, 'blk', scatter_dimension=0, tiled=True)  41.1 us
    all_gather x1, blocking collectives, per_device(): lax.all_gather(teacher, 'inner', axis=0, tiled=True)  20.6 us
    all_gather x1, blocking collectives, per_device(): lax.all_gather(student, 'inner', axis=0, tiled=True)  16.4 us
    psum x1, blocking collectives, per_device(): loss = lax.psum(jnp.sum(terms), 'blk') / total  12.6 us
    all_gather x1, blocking collectives, per_device(): lax.all_gather(student, 'blk', axis=0, tiled=True)  12.4 us
    psum x1, blocking collectives, per_device(): sum_s, sum_t, sum_c = lax.psum((sq_s, sq_t, cross), 'inner')  10.2 us
    reduce_scatter x1, waiting for transfers between devices, per_device(): lax.psum_scatter(row_acc, 'inner', scatter_dimension=0, tiled=True)  5.84 us
  transfers between devices with their start and end apart: 3, of which 2 were waited for; matrix products, arithmetic and copies ran while one was open for 1% of the time, Pallas kernels for 0%

commit v1 on v0

--- a/solution.py
+++ b/solution.py
@@ -6,6 +6,8 @@
 from jax.sharding import PartitionSpec as P
 
 DS = 768
+AXES = ("blk", "inner")
+GATHER_LIMIT = 24 * 2**20
 
 
 EPSILON = 1e-06
@@ -32,7 +34,7 @@
     return (gram_s, gram_t)
 
 
-def per_device(teacher, student):
+def per_device_tiled(teacher, student):
     rows = teacher.shape[0]
     blocks = lax.axis_size("blk")
     inner = lax.axis_size("inner")
@@ -41,37 +43,51 @@
         lax.all_gather(teacher, "inner", axis=0, tiled=True),
         lax.all_gather(student, "inner", axis=0, tiled=True),
     )
-    pieces = (
+    piece_t, piece_s = (
         lax.all_gather(teacher, "blk", axis=0, tiled=True),
         lax.all_gather(student, "blk", axis=0, tiled=True),
     )
-    gram_s, gram_t = tile_grams(group_t, group_s, pieces[0], pieces[1])
+    gram_s, gram_t = tile_grams(group_t, group_s, piece_t, piece_s)
     sq_s = jnp.sum(gram_s * gram_s, 1)
     sq_t = jnp.sum(gram_t * gram_t, 1)
     cross = jnp.sum(gram_s * gram_t, 1)
     sum_s, sum_t, sum_c = lax.psum((sq_s, sq_t, cross), "inner")
     alpha, beta, terms = coefficients(sum_s, sum_t, sum_c, total)
     loss = lax.psum(jnp.sum(terms), "blk") / total
-    pieces = (
-        lax.all_gather(teacher, "blk", axis=0, tiled=True),
-        lax.all_gather(student, "blk", axis=0, tiled=True),
-    )
-    gram_s, gram_t = tile_grams(group_t, group_s, pieces[0], pieces[1])
     weights = (alpha[:, None] * gram_s - beta[:, None] * gram_t).astype(jnp.bfloat16)
-    row_acc = jnp.dot(weights, pieces[1], preferred_element_type=jnp.float32)
+    row_acc = jnp.dot(weights, piece_s, preferred_element_type=jnp.float32)
     col_term = jnp.einsum("rc,rd->cd", weights, group_s, preferred_element_type=jnp.float32)
-    col_buf = col_term
-    row_acc, col_buf = (row_acc, col_buf)
     row_mine = lax.psum_scatter(row_acc, "inner", scatter_dimension=0, tiled=True)
-    col_mine = lax.psum_scatter(col_buf, "blk", scatter_dimension=0, tiled=True)
+    col_mine = lax.psum_scatter(col_term, "blk", scatter_dimension=0, tiled=True)
     return (loss, row_mine + col_mine)
+
+
+def per_device(teacher, student):
+    rows = teacher.shape[0]
+    total = rows * lax.axis_size("blk") * lax.axis_size("inner")
+    if total * (teacher.shape[1] + student.shape[1]) * 2 > GATHER_LIMIT:
+        return per_device_tiled(teacher, student)
+    all_t = lax.all_gather(teacher, AXES, axis=0, tiled=True)
+    all_s = lax.all_gather(student, AXES, axis=0, tiled=True)
+    gram_s, gram_t = tile_grams(teacher, student, all_t, all_s)
+    sq_s = jnp.sum(gram_s * gram_s, 1)
+    sq_t = jnp.sum(gram_t * gram_t, 1)
+    cross = jnp.sum(gram_s * gram_t, 1)
+    mine = jnp.stack(coefficients(sq_s, sq_t, cross, total))
+    alpha, beta, terms = lax.all_gather(mine, AXES, axis=1, tiled=True)
+    loss = jnp.sum(terms) / total
+    row_w = mine[0][:, None] * gram_s - mine[1][:, None] * gram_t
+    col_w = alpha[None, :] * gram_s - beta[None, :] * gram_t
+    weights = jnp.concatenate([row_w, col_w]).astype(jnp.bfloat16)
+    both = jnp.dot(weights, all_s, preferred_element_type=jnp.float32)
+    return (loss, both[:rows] + both[rows:])
 
 
 def solution(mesh):
     return jax.shard_map(
         per_device,
         mesh=mesh,
-        in_specs=(P(("blk", "inner"), None), P(("blk", "inner"), None)),
-        out_specs=(P(), P(("blk", "inner"), None)),
+        in_specs=(P(AXES, None), P(AXES, None)),
+        out_specs=(P(), P(AXES, None)),
         check_vma=False,
     )

time: 144 us -> 227 us (1.58)
  waiting for transfers between devices: 47.6 us -> 131 us
  blocking collectives: 72.3 us -> 66.7 us
  matrix products: 5.39 us -> 10.4 us
    all_gather x1 -> x2, waiting for transfers between devices: 0.01 us -> 129 us  [the longest x1 74.5 us: per_device(): all_t = lax.all_gather(teacher, AXES, axis=0, tiled=True)]
    reduce_scatter x2 -> x0, waiting for transfers between devices: 46.9 us -> none  [the longest x1 41.1 us: per_device(): col_mine = lax.psum_scatter(col_buf, 'blk', scatter_dimension=0, tiled=True)]
    psum x2 -> x0, blocking collectives: 22.8 us -> none  [the longest x1 12.6 us: per_device(): loss = lax.psum(jnp.sum(terms), 'blk') / total]
    all_gather x3 -> x1, blocking collectives: 49.5 us -> 66.7 us  [per_device(): alpha, beta, terms = lax.all_gather(mine, AXES, axis=1, tiled=True)]
    dot_general x1, matrix products: 2 us -> 5.7 us  [tile_grams(): jnp.einsum('rd,cd->rc', rows_t, piece_t, preferred_element_type=jnp.float32)]
    dot_general x1, matrix products: 0.56 us -> 4.12 us  [tile_grams(): jnp.einsum('rd,cd->rc', rows_s, piece_s, preferred_element_type=jnp.float32)]
  transfers between devices with their start and end apart: 3 -> 2, of which waited for: 2 -> 2; matrix products, arithmetic and copies ran while one was open for 1% -> 3% of each run, Pallas kernels for 0% -> 0%
where the time goes in v1:
time: 227 us
  waiting for transfers between devices  131 us (58%)
  blocking collectives  66.7 us (29%)
  between operations  15.9 us (7%)
  matrix products  10.4 us (5%)
  other arithmetic  2.7 us (1%)
    all_gather x1, waiting for transfers between devices, per_device(): all_t = lax.all_gather(teacher, AXES, axis=0, tiled=True)  74.5 us
    all_gather x1, blocking collectives, per_device(): alpha, beta, terms = lax.all_gather(mine, AXES, axis=1, tiled=True)  66.7 us
    all_gather x1, waiting for transfers between devices, per_device(): all_s = lax.all_gather(student, AXES, axis=0, tiled=True)  54.8 us
    dot_general x1, matrix products, tile_grams(): jnp.einsum('rd,cd->rc', rows_t, piece_t, preferred_element_type=jnp.float32)  5.7 us
  transfers between devices with their start and end apart: 2, of which 2 were waited for; matrix products, arithmetic and copies ran while one was open for 3% of the time, Pallas kernels for 0%

profile of v1, /device:TPU:0, one launch (start us, length us, event | category | flops | bytes accessed | tf_op | source)
XLA Modules:
  0.0 226.5 jit_solution(16757025682187373145)
XLA Ops:
  7.2 0.0 all-gather.6.cloned.1.call-start
  7.2 0.7 all-gather.6.cloned.1.call-update
  7.9 0.0 all-gather.4.cloned.1.call-start
  7.9 0.7 all-gather.4.cloned.1.call-update
  8.6 0.0 copy-start.1
  8.7 74.5 %all-gather.6.cloned.1.call-done = bf16[2048,1536]{1,0:T(8,128)(2,1)} async-done(((bf16[64,1536]{1,0:T(8,128)(2,1)}), bf16[2048,1536]{1,0:T(8,128)(2,1)}) %all-gather.6.cloned.1.call-update) | async-done | bytes 6291472 | tf_op jit(solution)/shard_map/all_gather | solution.py:70
  83.2 5.7 %fusion.14 = f32[64,2048]{1,0:T(8,128)} fusion(bf16[64,1536]{1,0:T(8,128)(2,1)} %param.2, bf16[2048,1536]{1,0:T(8,128)(2,1)} %all-gather.6.cloned.1.call-done), kind=kOutput, calls=%fused_computation.35 | convolution fusion | flops 402653184 | bytes 7012352 | tf_op jit(solution)/shard_map/rd,cd->rc/dot_general | solution.py:33
  88.9 54.8 %all-gather.4.cloned.1.call-done = bf16[2048,768]{1,0:T(8,128)(2,1)} async-done(((bf16[64,768]{1,0:T(8,128)(2,1)}), bf16[2048,768]{1,0:T(8,128)(2,1)}) %all-gather.4.cloned.1.call-update) | async-done | bytes 3145744 | tf_op jit(solution)/shard_map/all_gather | solution.py:71
  143.6 0.0 copy-done.1
  143.6 0.0 copy-start
  143.6 4.1 %multiply_reduce_fusion.2 = (f32[64]{0:T(128)S(1)}, f32[64]{0:T(128)S(1)}, f32[64]{0:T(128)S(1)}, f32[64,2048]{1,0:T(8,128)}) fusion(f32[64,2048]{1,0:T(8,128)} %fusion.14, bf16[64,768]{1,0:T(8,128)(2,1)S(1)} %copy-done.1, bf16[2048,768]{1,0:T(8,128)(2,1)} %all-gather.4.cloned.1.call-done), kind=kOutput, calls=%fused_computation.8 | convolution fusion | flops 202112832 | bytes 4293376 | tf_op jit(solution)/shard_map/rd,cd->rc/dot_general | solution.py:32
  147.8 66.7 %all-gather = f32[32,64,3]{1,2,0:T(4,128)S(1)} all-gather(f32[1,64,3]{1,2,0:T(4,128)S(1)} %maximum_bitcast_fusion), channel_id=1, replica_groups=mesh['blk'=8,'inner'=4] {'blk','inner'}, dimensions={0}, use_global_device_ids=true | all-gather | bytes 25344 | tf_op jit(solution)/shard_map/all_gather | solution.py:77
  214.6 0.1 reshape.124
  214.6 0.6 fusion.13
  215.3 1.3 subtract_convert_fusion.1
  216.6 0.0 copy-done
  216.6 0.6 fusion
  217.2 0.7 slice_add_fusion
  (4 shorter events, 0.1 us)
Async XLA Ops:
  7.2 76.0 %all-gather.6.cloned.1.call-start = ((), (), s32[]{:S(2)}) async-start(), calls=%async_computation.1 | async-start | bytes 6488064 | tf_op jit(solution)/shard_map/all_gather | solution.py:70
  7.9 135.7 %all-gather.4.cloned.1.call-start = ((), (), s32[]{:S(2)}) async-start(), calls=%async_computation | async-start | bytes 3244032 | tf_op jit(solution)/shard_map/all_gather | solution.py:71
  8.6 135.0 %copy-start.1 = (bf16[64,768]{1,0:T(8,128)(2,1)S(1)}, bf16[64,768]{1,0:T(8,128)(2,1)}, u32[]{:S(2)}) copy-start(bf16[64,768]{1,0:T(8,128)(2,1)} %param.3) | copy-start | bytes 294916
  143.6 73.0 %copy-start = (bf16[2048,768]{1,0:T(8,128)(2,1)S(1)}, bf16[2048,768]{1,0:T(8,128)(2,1)}, u32[]{:S(2)}) copy-start(bf16[2048,768]{1,0:T(8,128)(2,1)} %all-gather.4.cloned.1.call-done) | copy-start | bytes 9437188
Sparse Core Ops, SparseCore 0:
  10.9 72.2 all-gather.5
  86.1 57.5 all-gather.3

commit v2 on v0

v2 whole, which is shorter than its diff:
```python
import math

import jax
import jax.numpy as jnp
from jax import lax
from jax.sharding import PartitionSpec as P

DS = 768
AXES = ("blk", "inner")


EPSILON = 1e-06


def coefficients(sq_student, sq_teacher, cross, total):
    norm_student = jnp.sqrt(sq_student + EPSILON)
    norm_teacher = jnp.sqrt(sq_teacher + EPSILON)
    factor = 2.0 * math.sqrt(total * DS) / total
    cubed = norm_student * norm_student * norm_student
    alpha = factor * (EPSILON / norm_student + cross / norm_teacher) / cubed
    beta = factor / (norm_student * norm_teacher)
    terms = (
        sq_student / (norm_student * norm_student)
        + sq_teacher / (norm_teacher * norm_teacher)
        - 2.0 * cross / (norm_student * norm_teacher)
    )
    return (alpha, beta, terms)


def span(masks):
    out = [0]
    for mask in masks:
        out += [mask ^ other for other in out]
    return out


def subgroups(blocks, inner):
    bits = [1 << b for b in range((inner - 1).bit_length())]
    bits += [inner << b for b in range(1, (blocks - 1).bit_length())]
    return (bits[0::2], bits[1::2] + [inner])


def send(value, mask, count):
    return lax.ppermute(value, AXES, [(i, i ^ mask) for i in range(count)])


def gather(own, masks, count):
    pieces = [own]
    for mask in masks:
        pieces += [send(piece, mask, count) for piece in pieces]
    return pieces


def tree_sum(values):
    while len(values) > 1:
        values = [values[i] + values[i + 1] for i in range(0, len(values), 2)]
    return values[0]


def group_sum(parts, masks, count):
    places = len(masks)
    values = [parts]
    for place, mask in enumerate(span(masks)):
        if place:
            got = send(parts, mask, count)
            order = [k ^ place for k in range(1 << places)]
            values.append(jnp.stack([got[:, k] for k in order], 1))
    return tree_sum(values)


def per_device(teacher, student):
    rows = teacher.shape[0]
    blocks = lax.axis_size("blk")
    inner = lax.axis_size("inner")
    count = blocks * inner
    total = rows * count
    row_masks, col_masks = subgroups(blocks, inner)
    n_row, n_col = 1 << len(row_masks), 1 << len(col_masks)

    row_t = gather(teacher, row_masks, count)
    col_t = gather(teacher, col_masks, count)
    row_s = gather(student, row_masks, count)
    col_s = gather(student, col_masks, count)
    row_t, col_t, row_s, col_s = map(jnp.concatenate, (row_t, col_t, row_s, col_s))

    gram_s = jnp.einsum("rd,cd->rc", row_s, col_s, preferred_element_type=jnp.float32)
    gram_t = jnp.einsum("rd,cd->rc", row_t, col_t, preferred_element_type=jnp.float32)
    products = (gram_s * gram_s, gram_t * gram_t, gram_s * gram_t)
    row_part = jnp.stack([jnp.sum(p, 1) for p in products]).reshape(3, n_row, rows)
    col_part = jnp.stack([jnp.sum(p, 0) for p in products]).reshape(3, n_col, rows)
    row_sum = group_sum(row_part, row_masks, count).reshape(3, -1)
    col_sum = group_sum(col_part, col_masks, count).reshape(3, -1)

    row_alpha, row_beta, _ = coefficients(*row_sum, total)
    col_alpha, col_beta, terms = coefficients(*col_sum, total)
    row_w = row_alpha[:, None] * gram_s - row_beta[:, None] * gram_t
    col_w = col_alpha[None, :] * gram_s - col_beta[None, :] * gram_t
    out = jnp.dot(row_w.astype(jnp.bfloat16), col_s, preferred_element_type=jnp.float32)
    out += jnp.dot(col_w.astype(jnp.bfloat16), col_s, preferred_element_type=jnp.float32)
    out = out.reshape(n_row, rows, -1)
    term = jnp.full((1, 128), jnp.sum(terms))

    grads, losses = [out[0]], [term]
    for place, mask in enumerate(span(row_masks)):
        if place:
            grads.append(send(out[place], mask, count))
            losses.append(send(term, mask, count))
    return (tree_sum(losses)[0, 0] / total, tree_sum(grads))


def solution(mesh):
    return jax.shard_map(
        per_device,
        mesh=mesh,
        in_specs=(P(AXES, None), P(AXES, None)),
        out_specs=(P(), P(AXES, None)),
        check_vma=False,
    )
```

time: 144 us -> 84.8 us (0.59)
  blocking collectives: 72.3 us -> 0 us
  starting transfers between devices: 0.12 us -> 37.5 us
  between operations: 15.6 us -> 2.17 us
  waiting for transfers between devices: 47.6 us -> 37.1 us
  local copies, waits for them, and re-layouts: 0.01 us -> 3.87 us
  matrix products: 5.39 us -> 1.95 us
    all_gather x3 -> x0, blocking collectives: 49.5 us -> none  [the longest x1 20.6 us: per_device(): lax.all_gather(teacher, 'inner', axis=0, tiled=True)]
    reduce_scatter x2 -> x0, waiting for transfers between devices: 46.9 us -> none  [the longest x1 41.1 us: per_device(): col_mine = lax.psum_scatter(col_buf, 'blk', scatter_dimension=0, tiled=True)]
    ppermute x0 -> x36, starting transfers between devices: none -> 37.5 us  [send(): return lax.ppermute(value, AXES, [(i, i ^ mask) for i in range(count)])]
    ppermute x0 -> x36, waiting for transfers between devices: none -> 37.1 us  [send(): return lax.ppermute(value, AXES, [(i, i ^ mask) for i in range(count)])]
    psum x2 -> x0, blocking collectives: 22.8 us -> none  [the longest x1 12.6 us: per_device(): loss = lax.psum(jnp.sum(terms), 'blk') / total]
    dot_general x4, matrix products: 5.39 us -> 1.95 us  [the longest x1 0.6 us: per_device(): jnp.einsum('rd,cd->rc', row_t, col_t, preferred_element_type=jnp.float32)]
    unnamed x2 -> x22, local copies, waits for them, and re-layouts: 0.01 us -> 2.01 us
  transfers between devices with their start and end apart: 3 -> 36, of which waited for: 2 -> 13; matrix products, arithmetic and copies ran while one was open for 1% -> 6% of each run, Pallas kernels for 0% -> 0%
where the time goes in v2:
time: 84.8 us; the launch traced here: 84.6 us
  starting transfers between devices  37.5 us (44%)
  waiting for transfers between devices  37.1 us (44%)
  local copies, waits for them, and re-layouts  3.87 us (5%)
  between operations  2.17 us (3%)
  other arithmetic  2.09 us (2%)
  matrix products  1.95 us (2%)
    ppermute x36, starting transfers between devices, send(): return lax.ppermute(value, AXES, [(i, i ^ mask) for i in range(count)])  37.5 us
    ppermute x36, waiting for transfers between devices, send(): return lax.ppermute(value, AXES, [(i, i ^ mask) for i in range(count)])  37.1 us
    unnamed x22, local copies, waits for them, and re-layouts  2.01 us
  transfers between devices with their start and end apart: 36, of which 13 were waited for; matrix products, arithmetic and copies ran while one was open for 6% of the time, Pallas kernels for 0%

profile of v2, /device:TPU:0, one launch (start us, length us, event | category | flops | bytes accessed | tf_op | source)
XLA Modules:
  0.0 84.6 jit_solution(7999874121816418875)
XLA Ops:
  0.6 4.1 %collective-permute-start.13 = (bf16[64,1536]{1,0:T(8,128)(2,1)}, bf16[64,1536]{1,0:T(8,128)(2,1)S(1)}, u32[]{:S(2)}, u32[]{:S(2)}) collective-permute-start(bf16[64,1536]{1,0:T(8,128)(2,1)} %param.2), channel_id=1, source_target_pairs={{0,2},{1,3},{2,0},{3,1},{4,6},{5,7},{6,4},{7,5},{8,10},{9,11},{10,... | collective-permute-start | bytes 589832 | tf_op jit(solution)/shard_map/ppermute | solution.py:44
  4.7 1.5 %collective-permute-start.14 = (bf16[64,1536]{1,0:T(8,128)(2,1)}, bf16[64,1536]{1,0:T(8,128)(2,1)S(1)}, u32[]{:S(2)}, u32[]{:S(2)}) collective-permute-start(bf16[64,1536]{1,0:T(8,128)(2,1)} %param.2), channel_id=1, source_target_pairs={{0,16},{1,17},{2,18},{3,19},{4,20},{5,21},{6,22},{7,23},{8,24},{9,... | collective-permute-start | bytes 589832 | tf_op jit(solution)/shard_map/ppermute | solution.py:44
  6.3 1.6 %collective-permute-start.10 = (bf16[64,1536]{1,0:T(8,128)(2,1)}, bf16[64,1536]{1,0:T(8,128)(2,1)S(1)}, u32[]{:S(2)}, u32[]{:S(2)}) collective-permute-start(bf16[64,1536]{1,0:T(8,128)(2,1)} %param.2), channel_id=1, source_target_pairs={{0,1},{1,0},{2,3},{3,2},{4,5},{5,4},{6,7},{7,6},{8,9},{9,8},{10,11... | collective-permute-start | bytes 589832 | tf_op jit(solution)/shard_map/ppermute | solution.py:44
  8.2 0.9 %constant_dynamic-update-slice_fusion.15 = bf16[512,1536]{1,0:T(8,128)(2,1)S(1)} fusion(bf16[64,1536]{1,0:T(8,128)(2,1)} %param.2), kind=kLoop, calls=%fused_computation.47 | loop fusion | bytes 393216
  9.1 0.9 %constant_dynamic-update-slice_fusion.7 = bf16[512,768]{1,0:T(8,128)(2,1)S(1)} fusion(bf16[64,768]{1,0:T(8,128)(2,1)} %param.3), kind=kLoop, calls=%fused_computation.39 | loop fusion | bytes 196608
  10.0 8.4 %collective-permute-done.3 = bf16[64,768]{1,0:T(8,128)(2,1)S(1)} collective-permute-done((bf16[64,768]{1,0:T(8,128)(2,1)}, bf16[64,768]{1,0:T(8,128)(2,1)S(1)}, u32[]{:S(2)}, u32[]{:S(2)}) %collective-permute-start.3) | collective-permute-done | bytes 98336 | tf_op jit(solution)/shard_map/ppermute | solution.py:44
  18.4 1.5 %collective-permute-start.4 = (bf16[64,768]{1,0:T(8,128)(2,1)}, bf16[64,768]{1,0:T(8,128)(2,1)S(1)}, u32[]{:S(2)}, u32[]{:S(2)}) collective-permute-start(bf16[64,768]{1,0:T(8,128)(2,1)} %param.3), channel_id=1, source_target_pairs={{0,16},{1,17},{2,18},{3,19},{4,20},{5,21},{6,22},{7,23},{8,24},{9,... | collective-permute-start | bytes 294920 | tf_op jit(solution)/shard_map/ppermute | solution.py:44
  19.9 3.4 %collective-permute-done.4 = bf16[64,768]{1,0:T(8,128)(2,1)S(1)} collective-permute-done((bf16[64,768]{1,0:T(8,128)(2,1)}, bf16[64,768]{1,0:T(8,128)(2,1)S(1)}, u32[]{:S(2)}, u32[]{:S(2)}) %collective-permute-start.4) | collective-permute-done | bytes 98336 | tf_op jit(solution)/shard_map/ppermute | solution.py:44
  23.3 1.5 %collective-permute-start.11 = (bf16[64,1536]{1,0:T(8,128)(2,1)}, bf16[64,1536]{1,0:T(8,128)(2,1)S(1)}, u32[]{:S(2)}, u32[]{:S(2)}) collective-permute-start(bf16[64,1536]{1,0:T(8,128)(2,1)} %param.2), channel_id=1, source_target_pairs={{0,8},{1,9},{2,10},{3,11},{4,12},{5,13},{6,14},{7,15},{8,0},{9,1},... | collective-permute-start | bytes 589832 | tf_op jit(solution)/shard_map/ppermute | solution.py:44
  24.9 1.5 %collective-permute-start.5 = (bf16[64,768]{1,0:T(8,128)(2,1)S(1)}, bf16[64,768]{1,0:T(8,128)(2,1)S(1)}, u32[]{:S(2)}, u32[]{:S(2)}) collective-permute-start(bf16[64,768]{1,0:T(8,128)(2,1)S(1)} %collective-permute-done.3), channel_id=1, source_target_pairs={{0,16},{1,17},{2,18},{3,19},{4,20},{5,21},{6,22},{7,23},{8,24},{9,... | collective-permute-start | bytes 294920 | tf_op jit(solution)/shard_map/ppermute | solution.py:44
  26.4 3.7 %collective-permute-done.5 = bf16[64,768]{1,0:T(8,128)(2,1)S(1)} collective-permute-done((bf16[64,768]{1,0:T(8,128)(2,1)S(1)}, bf16[64,768]{1,0:T(8,128)(2,1)S(1)}, u32[]{:S(2)}, u32[]{:S(2)}) %collective-permute-start.5) | collective-permute-done | bytes 98336 | tf_op jit(solution)/shard_map/ppermute | solution.py:44
  31.5 1.4 %collective-permute-start.15 = (bf16[64,1536]{1,0:T(8,128)(2,1)S(1)}, bf16[64,1536]{1,0:T(8,128)(2,1)S(1)}, u32[]{:S(2)}, u32[]{:S(2)}) collective-permute-start(bf16[64,1536]{1,0:T(8,128)(2,1)S(1)} %collective-permute-done.13), channel_id=1, source_target_pairs={{0,16},{1,17},{2,18},{3,19},{4,20},{5,21},{6,22},{7,23},{8,24},{9,... | collective-permute-start | bytes 589832 | tf_op jit(solution)/shard_map/ppermute | solution.py:44
  33.0 1.3 %collective-permute-done.9 = bf16[64,768]{1,0:T(8,128)(2,1)S(1)} collective-permute-done((bf16[64,768]{1,0:T(8,128)(2,1)S(1)}, bf16[64,768]{1,0:T(8,128)(2,1)S(1)}, u32[]{:S(2)}, u32[]{:S(2)}) %collective-permute-start.9) | collective-permute-done | bytes 98336 | tf_op jit(solution)/shard_map/ppermute | solution.py:44
  34.3 0.9 %collective-permute-start = (bf16[64,768]{1,0:T(8,128)(2,1)S(1)}, bf16[64,768]{1,0:T(8,128)(2,1)S(1)}, u32[]{:S(2)}, u32[]{:S(2)}) collective-permute-start(bf16[64,768]{1,0:T(8,128)(2,1)S(1)} %copy-done.1), channel_id=1, source_target_pairs={{0,1},{1,0},{2,3},{3,2},{4,5},{5,4},{6,7},{7,6},{8,9},{9,8},{10,11... | collective-permute-start | bytes 294920 | tf_op jit(solution)/shard_map/ppermute | solution.py:44
  35.2 4.0 %collective-permute-done = bf16[64,768]{1,0:T(8,128)(2,1)S(1)} collective-permute-done((bf16[64,768]{1,0:T(8,128)(2,1)S(1)}, bf16[64,768]{1,0:T(8,128)(2,1)S(1)}, u32[]{:S(2)}, u32[]{:S(2)}) %collective-permute-start) | collective-permute-done | bytes 98336 | tf_op jit(solution)/shard_map/ppermute | solution.py:44
  39.7 1.5 %collective-permute-start.2 = (bf16[64,768]{1,0:T(8,128)(2,1)S(1)}, bf16[64,768]{1,0:T(8,128)(2,1)S(1)}, u32[]{:S(2)}, u32[]{:S(2)}) collective-permute-start(bf16[64,768]{1,0:T(8,128)(2,1)S(1)} %collective-permute-done), channel_id=1, source_target_pairs={{0,8},{1,9},{2,10},{3,11},{4,12},{5,13},{6,14},{7,15},{8,0},{9,1},... | collective-permute-start | bytes 294920 | tf_op jit(solution)/shard_map/ppermute | solution.py:44
  43.4 1.4 %collective-permute-done.19 = bf16[64,1536]{1,0:T(8,128)(2,1)S(1)} collective-permute-done((bf16[64,1536]{1,0:T(8,128)(2,1)S(1)}, bf16[64,1536]{1,0:T(8,128)(2,1)S(1)}, u32[]{:S(2)}, u32[]{:S(2)}) %collective-permute-start.19) | collective-permute-done | bytes 196640 | tf_op jit(solution)/shard_map/ppermute | solution.py:44
  44.8 4.8 %collective-permute-done.12 = bf16[64,1536]{1,0:T(8,128)(2,1)S(1)} collective-permute-done((bf16[64,1536]{1,0:T(8,128)(2,1)S(1)}, bf16[64,1536]{1,0:T(8,128)(2,1)S(1)}, u32[]{:S(2)}, u32[]{:S(2)}) %collective-permute-start.12) | collective-permute-done | bytes 196640 | tf_op jit(solution)/shard_map/ppermute | solution.py:44
  51.1 0.9 %collective-permute-start.32 = (f32[3,4,64]{2,1,0:T(4,128)S(1)}, f32[3,4,64]{2,1,0:T(4,128)S(1)}, u32[]{:S(2)}, u32[]{:S(2)}) collective-permute-start(f32[3,4,64]{2,1,0:T(4,128)S(1)} %constant_dynamic-update-slice_fusion.19), channel_id=1, source_target_pairs={{0,9},{1,8},{2,11},{3,10},{4,13},{5,12},{6,15},{7,14},{8,1},{9,0},... | collective-permute-start | bytes 9224 | tf_op jit(solution)/shard_map/ppermute | solution.py:44
  52.0 1.1 %collective-permute-start.30 = (f32[3,4,64]{2,1,0:T(4,128)S(1)}, f32[3,4,64]{2,1,0:T(4,128)S(1)}, u32[]{:S(2)}, u32[]{:S(2)}) collective-permute-start(f32[3,4,64]{2,1,0:T(4,128)S(1)} %constant_dynamic-update-slice_fusion.19), channel_id=1, source_target_pairs={{0,1},{1,0},{2,3},{3,2},{4,5},{5,4},{6,7},{7,6},{8,9},{9,8},{10,11... | collective-permute-start | bytes 9224 | tf_op jit(solution)/shard_map/ppermute | solution.py:44
  53.1 1.5 %collective-permute-start.31 = (f32[3,4,64]{2,1,0:T(4,128)S(1)}, f32[3,4,64]{2,1,0:T(4,128)S(1)}, u32[]{:S(2)}, u32[]{:S(2)}) collective-permute-start(f32[3,4,64]{2,1,0:T(4,128)S(1)} %constant_dynamic-update-slice_fusion.19), channel_id=1, source_target_pairs={{0,8},{1,9},{2,10},{3,11},{4,12},{5,13},{6,14},{7,15},{8,0},{9,1},... | collective-permute-start | bytes 9224 | tf_op jit(solution)/shard_map/ppermute | solution.py:44
  54.9 2.6 %collective-permute-start.20 = (f32[3,8,64]{2,1,0:T(8,128)S(1)}, f32[3,8,64]{2,1,0:T(8,128)S(1)}, u32[]{:S(2)}, u32[]{:S(2)}) collective-permute-start(f32[3,8,64]{2,1,0:T(8,128)S(1)} %constant_dynamic-update-slice_fusion.16), channel_id=1, source_target_pairs={{0,2},{1,3},{2,0},{3,1},{4,6},{5,7},{6,4},{7,5},{8,10},{9,11},{10,... | collective-permute-start | bytes 18440 | tf_op jit(solution)/shard_map/ppermute | solution.py:44
  57.4 2.6 %collective-permute-start.24 = (f32[3,8,64]{2,1,0:T(8,128)S(1)}, f32[3,8,64]{2,1,0:T(8,128)S(1)}, u32[]{:S(2)}, u32[]{:S(2)}) collective-permute-start(f32[3,8,64]{2,1,0:T(8,128)S(1)} %constant_dynamic-update-slice_fusion.16), channel_id=1, source_target_pairs={{0,6},{1,7},{2,4},{3,5},{4,2},{5,3},{6,0},{7,1},{8,14},{9,15},{10,... | collective-permute-start | bytes 18440 | tf_op jit(solution)/shard_map/ppermute | solution.py:44
  60.0 1.4 %collective-permute-start.22 = (f32[3,8,64]{2,1,0:T(8,128)S(1)}, f32[3,8,64]{2,1,0:T(8,128)S(1)}, u32[]{:S(2)}, u32[]{:S(2)}) collective-permute-start(f32[3,8,64]{2,1,0:T(8,128)S(1)} %constant_dynamic-update-slice_fusion.16), channel_id=1, source_target_pairs={{0,18},{1,19},{2,16},{3,17},{4,22},{5,23},{6,20},{7,21},{8,26},{9,... | collective-permute-start | bytes 18440 | tf_op jit(solution)/shard_map/ppermute | solution.py:44
  61.8 1.4 %collective-permute-start.21 = (f32[3,8,64]{2,1,0:T(8,128)S(1)}, f32[3,8,64]{2,1,0:T(8,128)S(1)}, u32[]{:S(2)}, u32[]{:S(2)}) collective-permute-start(f32[3,8,64]{2,1,0:T(8,128)S(1)} %constant_dynamic-update-slice_fusion.16), channel_id=1, source_target_pairs={{0,16},{1,17},{2,18},{3,19},{4,20},{5,21},{6,22},{7,23},{8,24},{9,... | collective-permute-start | bytes 18440 | tf_op jit(solution)/shard_map/ppermute | solution.py:44
  63.9 1.7 %collective-permute-done.22 = f32[3,8,64]{2,1,0:T(8,128)S(1)} collective-permute-done((f32[3,8,64]{2,1,0:T(8,128)S(1)}, f32[3,8,64]{2,1,0:T(8,128)S(1)}, u32[]{:S(2)}, u32[]{:S(2)}) %collective-permute-start.22) | collective-permute-done | bytes 6176 | tf_op jit(solution)/shard_map/ppermute | solution.py:44
  67.2 1.6 %collective-permute-start.27 = (f32[1,128]{1,0:T(1,128)S(1)}, f32[1,128]{1,0:T(1,128)S(1)}, u32[]{:S(2)}, u32[]{:S(2)}) collective-permute-start(f32[1,128]{1,0:T(1,128)S(1)} %broadcast_in_dim.2), channel_id=1, source_target_pairs={{0,1},{1,0},{2,3},{3,2},{4,5},{5,4},{6,7},{7,6},{8,9},{9,8},{10,11... | collective-permute-start | bytes 1544 | tf_op jit(solution)/shard_map/ppermute | solution.py:44
  69.4 1.4 %collective-permute-start.29 = (f32[1,128]{1,0:T(1,128)S(1)}, f32[1,128]{1,0:T(1,128)S(1)}, u32[]{:S(2)}, u32[]{:S(2)}) collective-permute-start(f32[1,128]{1,0:T(1,128)S(1)} %broadcast_in_dim.2), channel_id=1, source_target_pairs={{0,9},{1,8},{2,11},{3,10},{4,13},{5,12},{6,15},{7,14},{8,1},{9,0},... | collective-permute-start | bytes 1544 | tf_op jit(solution)/shard_map/ppermute | solution.py:44
  71.8 1.6 %collective-permute-start.33 = (f32[64,768]{1,0:T(8,128)S(1)}, f32[64,768]{1,0:T(8,128)S(1)}, u32[]{:S(2)}, u32[]{:S(2)}) collective-permute-start(f32[64,768]{1,0:T(8,128)S(1)} %get-tuple-element.10), channel_id=1, source_target_pairs={{0,1},{1,0},{2,3},{3,2},{4,5},{5,4},{6,7},{7,6},{8,9},{9,8},{10,11... | collective-permute-start | bytes 589832 | tf_op jit(solution)/shard_map/ppermute | solution.py:44
  74.0 1.4 %collective-permute-start.35 = (f32[64,768]{1,0:T(8,128)S(1)}, f32[64,768]{1,0:T(8,128)S(1)}, u32[]{:S(2)}, u32[]{:S(2)}) collective-permute-start(f32[64,768]{1,0:T(8,128)S(1)} %get-tuple-element.8), channel_id=1, source_target_pairs={{0,9},{1,8},{2,11},{3,10},{4,13},{5,12},{6,15},{7,14},{8,1},{9,0},... | collective-permute-start | bytes 589832 | tf_op jit(solution)/shard_map/ppermute | solution.py:44
  76.1 3.6 %collective-permute-done.33 = f32[64,768]{1,0:T(8,128)S(1)} collective-permute-done((f32[64,768]{1,0:T(8,128)S(1)}, f32[64,768]{1,0:T(8,128)S(1)}, u32[]{:S(2)}, u32[]{:S(2)}) %collective-permute-start.33) | collective-permute-done | bytes 196640 | tf_op jit(solution)/shard_map/ppermute | solution.py:44
  79.7 3.1 %collective-permute-done.34 = f32[64,768]{1,0:T(8,128)S(1)} collective-permute-done((f32[64,768]{1,0:T(8,128)S(1)}, f32[64,768]{1,0:T(8,128)S(1)}, u32[]{:S(2)}, u32[]{:S(2)}) %collective-permute-start.34) | collective-permute-done | bytes 196640 | tf_op jit(solution)/shard_map/ppermute | solution.py:44
  (106 shorter events, 12.2 us)
Async XLA Ops:
  0.6 24.2 %collective-permute-start.13 = (bf16[64,1536]{1,0:T(8,128)(2,1)}, bf16[64,1536]{1,0:T(8,128)(2,1)S(1)}, u32[]{:S(2)}, u32[]{:S(2)}) collective-permute-start(bf16[64,1536]{1,0:T(8,128)(2,1)} %param.2), channel_id=1, source_target_pairs={{0,2},{1,3},{2,0},{3,1},{4,6},{5,7},{6,4},{7,5},{8,10},{9,11},{10,... | collective-permute-start | bytes 589832 | tf_op jit(solution)/shard_map/ppermute | solution.py:44
  4.7 20.2 %collective-permute-start.14 = (bf16[64,1536]{1,0:T(8,128)(2,1)}, bf16[64,1536]{1,0:T(8,128)(2,1)S(1)}, u32[]{:S(2)}, u32[]{:S(2)}) collective-permute-start(bf16[64,1536]{1,0:T(8,128)(2,1)} %param.2), channel_id=1, source_target_pairs={{0,16},{1,17},{2,18},{3,19},{4,20},{5,21},{6,22},{7,23},{8,24},{9,... | collective-permute-start | bytes 589832 | tf_op jit(solution)/shard_map/ppermute | solution.py:44
  6.3 34.9 %collective-permute-start.16 = (bf16[64,1536]{1,0:T(8,128)(2,1)}, bf16[64,1536]{1,0:T(8,128)(2,1)S(1)}, u32[]{:S(2)}, u32[]{:S(2)}) collective-permute-start(bf16[64,1536]{1,0:T(8,128)(2,1)} %param.2), channel_id=1, source_target_pairs={{0,4},{1,5},{2,6},{3,7},{4,0},{5,1},{6,2},{7,3},{8,12},{9,13},{10,... | collective-permute-start | bytes 589832 | tf_op jit(solution)/shard_map/ppermute | solution.py:44
  6.3 35.0 %collective-permute-start.10 = (bf16[64,1536]{1,0:T(8,128)(2,1)}, bf16[64,1536]{1,0:T(8,128)(2,1)S(1)}, u32[]{:S(2)}, u32[]{:S(2)}) collective-permute-start(bf16[64,1536]{1,0:T(8,128)(2,1)} %param.2), channel_id=1, source_target_pairs={{0,1},{1,0},{2,3},{3,2},{4,5},{5,4},{6,7},{7,6},{8,9},{9,8},{10,11... | collective-permute-start | bytes 589832 | tf_op jit(solution)/shard_map/ppermute | solution.py:44
  7.8 10.6 %collective-permute-start.3 = (bf16[64,768]{1,0:T(8,128)(2,1)}, bf16[64,768]{1,0:T(8,128)(2,1)S(1)}, u32[]{:S(2)}, u32[]{:S(2)}) collective-permute-start(bf16[64,768]{1,0:T(8,128)(2,1)} %param.3), channel_id=1, source_target_pairs={{0,2},{1,3},{2,0},{3,1},{4,6},{5,7},{6,4},{7,5},{8,10},{9,11},{10,... | collective-permute-start | bytes 294920 | tf_op jit(solution)/shard_map/ppermute | solution.py:44
  18.4 4.8 %collective-permute-start.4 = (bf16[64,768]{1,0:T(8,128)(2,1)}, bf16[64,768]{1,0:T(8,128)(2,1)S(1)}, u32[]{:S(2)}, u32[]{:S(2)}) collective-permute-start(bf16[64,768]{1,0:T(8,128)(2,1)} %param.3), channel_id=1, source_target_pairs={{0,16},{1,17},{2,18},{3,19},{4,20},{5,21},{6,22},{7,23},{8,24},{9,... | collective-permute-start | bytes 294920 | tf_op jit(solution)/shard_map/ppermute | solution.py:44
  23.3 21.5 %collective-permute-start.11 = (bf16[64,1536]{1,0:T(8,128)(2,1)}, bf16[64,1536]{1,0:T(8,128)(2,1)S(1)}, u32[]{:S(2)}, u32[]{:S(2)}) collective-permute-start(bf16[64,1536]{1,0:T(8,128)(2,1)} %param.2), channel_id=1, source_target_pairs={{0,8},{1,9},{2,10},{3,11},{4,12},{5,13},{6,14},{7,15},{8,0},{9,1},... | collective-permute-start | bytes 589832 | tf_op jit(solution)/shard_map/ppermute | solution.py:44
  24.8 5.4 %collective-permute-start.6 = (bf16[64,768]{1,0:T(8,128)(2,1)}, bf16[64,768]{1,0:T(8,128)(2,1)S(1)}, u32[]{:S(2)}, u32[]{:S(2)}) collective-permute-start(bf16[64,768]{1,0:T(8,128)(2,1)} %param.3), channel_id=1, source_target_pairs={{0,4},{1,5},{2,6},{3,7},{4,0},{5,1},{6,2},{7,3},{8,12},{9,13},{10,... | collective-permute-start | bytes 294920 | tf_op jit(solution)/shard_map/ppermute | solution.py:44
  24.9 5.3 %collective-permute-start.5 = (bf16[64,768]{1,0:T(8,128)(2,1)S(1)}, bf16[64,768]{1,0:T(8,128)(2,1)S(1)}, u32[]{:S(2)}, u32[]{:S(2)}) collective-permute-start(bf16[64,768]{1,0:T(8,128)(2,1)S(1)} %collective-permute-done.3), channel_id=1, source_target_pairs={{0,16},{1,17},{2,18},{3,19},{4,20},{5,21},{6,22},{7,23},{8,24},{9,... | collective-permute-start | bytes 294920 | tf_op jit(solution)/shard_map/ppermute | solution.py:44
  30.2 2.7 %collective-permute-start.8 = (bf16[64,768]{1,0:T(8,128)(2,1)S(1)}, bf16[64,768]{1,0:T(8,128)(2,1)S(1)}, u32[]{:S(2)}, u32[]{:S(2)}) collective-permute-start(bf16[64,768]{1,0:T(8,128)(2,1)S(1)} %collective-permute-done.4), channel_id=1, source_target_pairs={{0,4},{1,5},{2,6},{3,7},{4,0},{5,1},{6,2},{7,3},{8,12},{9,13},{10,... | collective-permute-start | bytes 294920 | tf_op jit(solution)/shard_map/ppermute | solution.py:44
  31.5 8.2 %collective-permute-start.15 = (bf16[64,1536]{1,0:T(8,128)(2,1)S(1)}, bf16[64,1536]{1,0:T(8,128)(2,1)S(1)}, u32[]{:S(2)}, u32[]{:S(2)}) collective-permute-start(bf16[64,1536]{1,0:T(8,128)(2,1)S(1)} %collective-permute-done.13), channel_id=1, source_target_pairs={{0,16},{1,17},{2,18},{3,19},{4,20},{5,21},{6,22},{7,23},{8,24},{9,... | collective-permute-start | bytes 589832 | tf_op jit(solution)/shard_map/ppermute | solution.py:44
  34.3 4.9 %collective-permute-start = (bf16[64,768]{1,0:T(8,128)(2,1)S(1)}, bf16[64,768]{1,0:T(8,128)(2,1)S(1)}, u32[]{:S(2)}, u32[]{:S(2)}) collective-permute-start(bf16[64,768]{1,0:T(8,128)(2,1)S(1)} %copy-done.1), channel_id=1, source_target_pairs={{0,1},{1,0},{2,3},{3,2},{4,5},{5,4},{6,7},{7,6},{8,9},{9,8},{10,11... | collective-permute-start | bytes 294920 | tf_op jit(solution)/shard_map/ppermute | solution.py:44
  39.1 11.1 %collective-permute-start.1 = (bf16[64,768]{1,0:T(8,128)(2,1)S(1)}, bf16[64,768]{1,0:T(8,128)(2,1)S(1)}, u32[]{:S(2)}, u32[]{:S(2)}) collective-permute-start(bf16[64,768]{1,0:T(8,128)(2,1)S(1)} %copy-done.1), channel_id=1, source_target_pairs={{0,8},{1,9},{2,10},{3,11},{4,12},{5,13},{6,14},{7,15},{8,0},{9,1},... | collective-permute-start | bytes 294920 | tf_op jit(solution)/shard_map/ppermute | solution.py:44
  39.7 10.6 %collective-permute-start.2 = (bf16[64,768]{1,0:T(8,128)(2,1)S(1)}, bf16[64,768]{1,0:T(8,128)(2,1)S(1)}, u32[]{:S(2)}, u32[]{:S(2)}) collective-permute-start(bf16[64,768]{1,0:T(8,128)(2,1)S(1)} %collective-permute-done), channel_id=1, source_target_pairs={{0,8},{1,9},{2,10},{3,11},{4,12},{5,13},{6,14},{7,15},{8,0},{9,1},... | collective-permute-start | bytes 294920 | tf_op jit(solution)/shard_map/ppermute | solution.py:44
  41.3 1.9 %collective-permute-start.18 = (bf16[64,1536]{1,0:T(8,128)(2,1)S(1)}, bf16[64,1536]{1,0:T(8,128)(2,1)S(1)}, u32[]{:S(2)}, u32[]{:S(2)}) collective-permute-start(bf16[64,1536]{1,0:T(8,128)(2,1)S(1)} %collective-permute-done.14), channel_id=1, source_target_pairs={{0,4},{1,5},{2,6},{3,7},{4,0},{5,1},{6,2},{7,3},{8,12},{9,13},{10,... | collective-permute-start | bytes 589832 | tf_op jit(solution)/shard_map/ppermute | solution.py:44
  42.7 6.9 %collective-permute-start.12 = (bf16[64,1536]{1,0:T(8,128)(2,1)S(1)}, bf16[64,1536]{1,0:T(8,128)(2,1)S(1)}, u32[]{:S(2)}, u32[]{:S(2)}) collective-permute-start(bf16[64,1536]{1,0:T(8,128)(2,1)S(1)} %collective-permute-done.10), channel_id=1, source_target_pairs={{0,8},{1,9},{2,10},{3,11},{4,12},{5,13},{6,14},{7,15},{8,0},{9,1},... | collective-permute-start | bytes 589832 | tf_op jit(solution)/shard_map/ppermute | solution.py:44
  51.1 6.3 %collective-permute-start.32 = (f32[3,4,64]{2,1,0:T(4,128)S(1)}, f32[3,4,64]{2,1,0:T(4,128)S(1)}, u32[]{:S(2)}, u32[]{:S(2)}) collective-permute-start(f32[3,4,64]{2,1,0:T(4,128)S(1)} %constant_dynamic-update-slice_fusion.19), channel_id=1, source_target_pairs={{0,9},{1,8},{2,11},{3,10},{4,13},{5,12},{6,15},{7,14},{8,1},{9,0},... | collective-permute-start | bytes 9224 | tf_op jit(solution)/shard_map/ppermute | solution.py:44
  52.0 8.0 %collective-permute-start.30 = (f32[3,4,64]{2,1,0:T(4,128)S(1)}, f32[3,4,64]{2,1,0:T(4,128)S(1)}, u32[]{:S(2)}, u32[]{:S(2)}) collective-permute-start(f32[3,4,64]{2,1,0:T(4,128)S(1)} %constant_dynamic-update-slice_fusion.19), channel_id=1, source_target_pairs={{0,1},{1,0},{2,3},{3,2},{4,5},{5,4},{6,7},{7,6},{8,9},{9,8},{10,11... | collective-permute-start | bytes 9224 | tf_op jit(solution)/shard_map/ppermute | solution.py:44
  53.1 8.3 %collective-permute-start.31 = (f32[3,4,64]{2,1,0:T(4,128)S(1)}, f32[3,4,64]{2,1,0:T(4,128)S(1)}, u32[]{:S(2)}, u32[]{:S(2)}) collective-permute-start(f32[3,4,64]{2,1,0:T(4,128)S(1)} %constant_dynamic-update-slice_fusion.19), channel_id=1, source_target_pairs={{0,8},{1,9},{2,10},{3,11},{4,12},{5,13},{6,14},{7,15},{8,0},{9,1},... | collective-permute-start | bytes 9224 | tf_op jit(solution)/shard_map/ppermute | solution.py:44
  54.9 7.0 %collective-permute-start.20 = (f32[3,8,64]{2,1,0:T(8,128)S(1)}, f32[3,8,64]{2,1,0:T(8,128)S(1)}, u32[]{:S(2)}, u32[]{:S(2)}) collective-permute-start(f32[3,8,64]{2,1,0:T(8,128)S(1)} %constant_dynamic-update-slice_fusion.16), channel_id=1, source_target_pairs={{0,2},{1,3},{2,0},{3,1},{4,6},{5,7},{6,4},{7,5},{8,10},{9,11},{10,... | collective-permute-start | bytes 18440 | tf_op jit(solution)/shard_map/ppermute | solution.py:44
  57.4 5.9 %collective-permute-start.26 = (f32[3,8,64]{2,1,0:T(8,128)S(1)}, f32[3,8,64]{2,1,0:T(8,128)S(1)}, u32[]{:S(2)}, u32[]{:S(2)}) collective-permute-start(f32[3,8,64]{2,1,0:T(8,128)S(1)} %constant_dynamic-update-slice_fusion.16), channel_id=1, source_target_pairs={{0,22},{1,23},{2,20},{3,21},{4,18},{5,19},{6,16},{7,17},{8,30},{9,... | collective-permute-start | bytes 18440 | tf_op jit(solution)/shard_map/ppermute | solution.py:44
  57.4 6.4 %collective-permute-start.24 = (f32[3,8,64]{2,1,0:T(8,128)S(1)}, f32[3,8,64]{2,1,0:T(8,128)S(1)}, u32[]{:S(2)}, u32[]{:S(2)}) collective-permute-start(f32[3,8,64]{2,1,0:T(8,128)S(1)} %constant_dynamic-update-slice_fusion.16), channel_id=1, source_target_pairs={{0,6},{1,7},{2,4},{3,5},{4,2},{5,3},{6,0},{7,1},{8,14},{9,15},{10,... | collective-permute-start | bytes 18440 | tf_op jit(solution)/shard_map/ppermute | solution.py:44
  60.0 5.6 %collective-permute-start.22 = (f32[3,8,64]{2,1,0:T(8,128)S(1)}, f32[3,8,64]{2,1,0:T(8,128)S(1)}, u32[]{:S(2)}, u32[]{:S(2)}) collective-permute-start(f32[3,8,64]{2,1,0:T(8,128)S(1)} %constant_dynamic-update-slice_fusion.16), channel_id=1, source_target_pairs={{0,18},{1,19},{2,16},{3,17},{4,22},{5,23},{6,20},{7,21},{8,26},{9,... | collective-permute-start | bytes 18440 | tf_op jit(solution)/shard_map/ppermute | solution.py:44
  61.4 4.2 %collective-permute-start.25 = (f32[3,8,64]{2,1,0:T(8,128)S(1)}, f32[3,8,64]{2,1,0:T(8,128)S(1)}, u32[]{:S(2)}, u32[]{:S(2)}) collective-permute-start(f32[3,8,64]{2,1,0:T(8,128)S(1)} %constant_dynamic-update-slice_fusion.16), channel_id=1, source_target_pairs={{0,20},{1,21},{2,22},{3,23},{4,16},{5,17},{6,18},{7,19},{8,28},{9,... | collective-permute-start | bytes 18440 | tf_op jit(solution)/shard_map/ppermute | solution.py:44
  61.8 3.9 %collective-permute-start.21 = (f32[3,8,64]{2,1,0:T(8,128)S(1)}, f32[3,8,64]{2,1,0:T(8,128)S(1)}, u32[]{:S(2)}, u32[]{:S(2)}) collective-permute-start(f32[3,8,64]{2,1,0:T(8,128)S(1)} %constant_dynamic-update-slice_fusion.16), channel_id=1, source_target_pairs={{0,16},{1,17},{2,18},{3,19},{4,20},{5,21},{6,22},{7,23},{8,24},{9,... | collective-permute-start | bytes 18440 | tf_op jit(solution)/shard_map/ppermute | solution.py:44
  63.3 2.6 %collective-permute-start.23 = (f32[3,8,64]{2,1,0:T(8,128)S(1)}, f32[3,8,64]{2,1,0:T(8,128)S(1)}, u32[]{:S(2)}, u32[]{:S(2)}) collective-permute-start(f32[3,8,64]{2,1,0:T(8,128)S(1)} %constant_dynamic-update-slice_fusion.16), channel_id=1, source_target_pairs={{0,4},{1,5},{2,6},{3,7},{4,0},{5,1},{6,2},{7,3},{8,12},{9,13},{10,... | collective-permute-start | bytes 18440 | tf_op jit(solution)/shard_map/ppermute | solution.py:44
  67.2 6.8 %collective-permute-start.27 = (f32[1,128]{1,0:T(1,128)S(1)}, f32[1,128]{1,0:T(1,128)S(1)}, u32[]{:S(2)}, u32[]{:S(2)}) collective-permute-start(f32[1,128]{1,0:T(1,128)S(1)} %broadcast_in_dim.2), channel_id=1, source_target_pairs={{0,1},{1,0},{2,3},{3,2},{4,5},{5,4},{6,7},{7,6},{8,9},{9,8},{10,11... | collective-permute-start | bytes 1544 | tf_op jit(solution)/shard_map/ppermute | solution.py:44
  68.8 6.6 %collective-permute-start.28 = (f32[1,128]{1,0:T(1,128)S(1)}, f32[1,128]{1,0:T(1,128)S(1)}, u32[]{:S(2)}, u32[]{:S(2)}) collective-permute-start(f32[1,128]{1,0:T(1,128)S(1)} %broadcast_in_dim.2), channel_id=1, source_target_pairs={{0,8},{1,9},{2,10},{3,11},{4,12},{5,13},{6,14},{7,15},{8,0},{9,1},... | collective-permute-start | bytes 1544 | tf_op jit(solution)/shard_map/ppermute | solution.py:44
  69.4 6.1 %collective-permute-start.29 = (f32[1,128]{1,0:T(1,128)S(1)}, f32[1,128]{1,0:T(1,128)S(1)}, u32[]{:S(2)}, u32[]{:S(2)}) collective-permute-start(f32[1,128]{1,0:T(1,128)S(1)} %broadcast_in_dim.2), channel_id=1, source_target_pairs={{0,9},{1,8},{2,11},{3,10},{4,13},{5,12},{6,15},{7,14},{8,1},{9,0},... | collective-permute-start | bytes 1544 | tf_op jit(solution)/shard_map/ppermute | solution.py:44
  71.8 7.8 %collective-permute-start.33 = (f32[64,768]{1,0:T(8,128)S(1)}, f32[64,768]{1,0:T(8,128)S(1)}, u32[]{:S(2)}, u32[]{:S(2)}) collective-permute-start(f32[64,768]{1,0:T(8,128)S(1)} %get-tuple-element.10), channel_id=1, source_target_pairs={{0,1},{1,0},{2,3},{3,2},{4,5},{5,4},{6,7},{7,6},{8,9},{9,8},{10,11... | collective-permute-start | bytes 589832 | tf_op jit(solution)/shard_map/ppermute | solution.py:44
  73.5 9.3 %collective-permute-start.34 = (f32[64,768]{1,0:T(8,128)S(1)}, f32[64,768]{1,0:T(8,128)S(1)}, u32[]{:S(2)}, u32[]{:S(2)}) collective-permute-start(f32[64,768]{1,0:T(8,128)S(1)} %get-tuple-element.9), channel_id=1, source_target_pairs={{0,8},{1,9},{2,10},{3,11},{4,12},{5,13},{6,14},{7,15},{8,0},{9,1},... | collective-permute-start | bytes 589832 | tf_op jit(solution)/shard_map/ppermute | solution.py:44
  74.0 8.8 %collective-permute-start.35 = (f32[64,768]{1,0:T(8,128)S(1)}, f32[64,768]{1,0:T(8,128)S(1)}, u32[]{:S(2)}, u32[]{:S(2)}) collective-permute-start(f32[64,768]{1,0:T(8,128)S(1)} %get-tuple-element.8), channel_id=1, source_target_pairs={{0,9},{1,8},{2,11},{3,10},{4,13},{5,12},{6,15},{7,14},{8,1},{9,0},... | collective-permute-start | bytes 589832 | tf_op jit(solution)/shard_map/ppermute | solution.py:44
  (6 other events, 62.6 us)

commit v3 on v2

--- a/solution.py
+++ b/solution.py
@@ -51,21 +51,17 @@
     return pieces
 
 
-def tree_sum(values):
-    while len(values) > 1:
-        values = [values[i] + values[i + 1] for i in range(0, len(values), 2)]
-    return values[0]
+def after(value, other):
+    return lax.optimization_barrier((value, other))[0]
 
 
 def group_sum(parts, masks, count):
-    places = len(masks)
-    values = [parts]
-    for place, mask in enumerate(span(masks)):
-        if place:
-            got = send(parts, mask, count)
-            order = [k ^ place for k in range(1 << places)]
-            values.append(jnp.stack([got[:, k] for k in order], 1))
-    return tree_sum(values)
+    for place, mask in enumerate(masks):
+        got = send(parts, mask, count)
+        shape = (3, -1, 2, 1 << place, got.shape[-1])
+        got = jnp.flip(got.reshape(shape), 2).reshape(parts.shape)
+        parts = parts + got
+    return parts
 
 
 def per_device(teacher, student):
@@ -79,8 +75,9 @@
 
     row_t = gather(teacher, row_masks, count)
     col_t = gather(teacher, col_masks, count)
-    row_s = gather(student, row_masks, count)
-    col_s = gather(student, col_masks, count)
+    student_late = after(student, (row_t[2], col_t[2]))
+    row_s = gather(student_late, row_masks, count)
+    col_s = gather(student_late, col_masks, count)
     row_t, col_t, row_s, col_s = map(jnp.concatenate, (row_t, col_t, row_s, col_s))
 
     gram_s = jnp.einsum("rd,cd->rc", row_s, col_s, preferred_element_type=jnp.float32)
@@ -98,14 +95,15 @@
     out = jnp.dot(row_w.astype(jnp.bfloat16), col_s, preferred_element_type=jnp.float32)
     out += jnp.dot(col_w.astype(jnp.bfloat16), col_s, preferred_element_type=jnp.float32)
     out = out.reshape(n_row, rows, -1)
-    term = jnp.full((1, 128), jnp.sum(terms))
+    out = jnp.concatenate([out, jnp.full((n_row, 8, out.shape[2]), jnp.sum(terms))], 1)
 
-    grads, losses = [out[0]], [term]
+    parts = [out[0]]
     for place, mask in enumerate(span(row_masks)):
         if place:
-            grads.append(send(out[place], mask, count))
-            losses.append(send(term, mask, count))
-    return (tree_sum(losses)[0, 0] / total, tree_sum(grads))
+            parts.append(send(out[place], mask, count))
+    while len(parts) > 1:
+        parts = [parts[i] + parts[i + 1] for i in range(0, len(parts), 2)]
+    return (parts[0][rows, 0] / total, parts[0][:rows])
 
 
 def solution(mesh):

time: 84.8 us -> 74.1 us (0.87)
  starting transfers between devices: 37.5 us -> 27.5 us
  waiting for transfers between devices: 37.1 us -> 35.4 us
  local copies, waits for them, and re-layouts: 3.87 us -> 4.98 us
    ppermute x36 -> x28, starting transfers between devices: 37.5 us -> 27.5 us  [send(): return lax.ppermute(value, AXES, [(i, i ^ mask) for i in range(count)])]
    ppermute x36 -> x28, waiting for transfers between devices: 37.1 us -> 35.4 us  [send(): return lax.ppermute(value, AXES, [(i, i ^ mask) for i in range(count)])]
    slice x11 -> x2, local copies, waits for them, and re-layouts: 0.12 us -> 1.2 us  [per_device(): return (parts[0][rows, 0] / total, parts[0][:rows])]
  transfers between devices with their start and end apart: 36 -> 28, of which waited for: 13 -> 16; matrix products, arithmetic and copies ran while one was open for 6% -> 4% of each run, Pallas kernels for 0% -> 0%
where the time goes in v3:
time: 74.1 us; the launch traced here: 73.9 us
  waiting for transfers between devices  35.4 us (48%)
  starting transfers between devices  27.5 us (37%)
  local copies, waits for them, and re-layouts  4.98 us (7%)
  between operations  2.66 us (4%)
  matrix products  1.95 us (3%)
  other arithmetic  1.4 us (2%)
    ppermute x28, waiting for transfers between devices, send(): return lax.ppermute(value, AXES, [(i, i ^ mask) for i in range(count)])  35.4 us
    ppermute x28, starting transfers between devices, send(): return lax.ppermute(value, AXES, [(i, i ^ mask) for i in range(count)])  27.5 us
    unnamed x22, local copies, waits for them, and re-layouts  2.04 us
  transfers between devices with their start and end apart: 28, of which 16 were waited for; matrix products, arithmetic and copies ran while one was open for 4% of the time, Pallas kernels for 0%

profile of v3, /device:TPU:0, one launch (start us, length us, event | category | flops | bytes accessed | tf_op | source)
XLA Modules:
  0.0 73.9 jit_solution(2177571533462651779)
XLA Ops:
  0.6 3.0 %collective-permute-start.1 = (bf16[64,1536]{1,0:T(8,128)(2,1)}, bf16[64,1536]{1,0:T(8,128)(2,1)S(1)}, u32[]{:S(2)}, u32[]{:S(2)}) collective-permute-start(bf16[64,1536]{1,0:T(8,128)(2,1)} %param.2), channel_id=1, source_target_pairs={{0,16},{1,17},{2,18},{3,19},{4,20},{5,21},{6,22},{7,23},{8,24},{9,... | collective-permute-start | bytes 589832 | tf_op jit(solution)/shard_map/ppermute | solution.py:44
  3.7 1.5 %collective-permute-start = (bf16[64,1536]{1,0:T(8,128)(2,1)}, bf16[64,1536]{1,0:T(8,128)(2,1)S(1)}, u32[]{:S(2)}, u32[]{:S(2)}) collective-permute-start(bf16[64,1536]{1,0:T(8,128)(2,1)} %param.2), channel_id=1, source_target_pairs={{0,8},{1,9},{2,10},{3,11},{4,12},{5,13},{6,14},{7,15},{8,0},{9,1},... | collective-permute-start | bytes 589832 | tf_op jit(solution)/shard_map/ppermute | solution.py:44
  5.2 2.6 %collective-permute-start.14 = (bf16[64,1536]{1,0:T(8,128)(2,1)}, bf16[64,1536]{1,0:T(8,128)(2,1)S(1)}, u32[]{:S(2)}, u32[]{:S(2)}) collective-permute-start(bf16[64,1536]{1,0:T(8,128)(2,1)} %param.2), channel_id=1, source_target_pairs={{0,2},{1,3},{2,0},{3,1},{4,6},{5,7},{6,4},{7,5},{8,10},{9,11},{10,... | collective-permute-start | bytes 589832 | tf_op jit(solution)/shard_map/ppermute | solution.py:44
  7.8 1.6 %collective-permute-start.12 = (bf16[64,1536]{1,0:T(8,128)(2,1)}, bf16[64,1536]{1,0:T(8,128)(2,1)S(1)}, u32[]{:S(2)}, u32[]{:S(2)}) collective-permute-start(bf16[64,1536]{1,0:T(8,128)(2,1)} %param.2), channel_id=1, source_target_pairs={{0,1},{1,0},{2,3},{3,2},{4,5},{5,4},{6,7},{7,6},{8,9},{9,8},{10,11... | collective-permute-start | bytes 589832 | tf_op jit(solution)/shard_map/ppermute | solution.py:44
  9.3 1.0 %constant_dynamic-update-slice_fusion.15 = bf16[512,1536]{1,0:T(8,128)(2,1)S(1)} fusion(bf16[64,1536]{1,0:T(8,128)(2,1)} %param.2), kind=kLoop, calls=%fused_computation.55 | loop fusion | bytes 393216
  10.3 2.5 %collective-permute-start.5 = (bf16[64,768]{1,0:T(8,128)(2,1)}, bf16[64,768]{1,0:T(8,128)(2,1)S(1)}, u32[]{:S(2)}, u32[]{:S(2)}) collective-permute-start(bf16[64,768]{1,0:T(8,128)(2,1)} %param.3), channel_id=1, source_target_pairs={{0,2},{1,3},{2,0},{3,1},{4,6},{5,7},{6,4},{7,5},{8,10},{9,11},{10,... | collective-permute-start | bytes 294920 | tf_op jit(solution)/shard_map/ppermute | solution.py:44
  13.3 5.4 %collective-permute-done.14 = bf16[64,1536]{1,0:T(8,128)(2,1)S(1)} collective-permute-done((bf16[64,1536]{1,0:T(8,128)(2,1)}, bf16[64,1536]{1,0:T(8,128)(2,1)S(1)}, u32[]{:S(2)}, u32[]{:S(2)}) %collective-permute-start.14) | collective-permute-done | bytes 196640 | tf_op jit(solution)/shard_map/ppermute | solution.py:44
  18.8 0.9 %constant_dynamic-update-slice_fusion.7 = bf16[512,768]{1,0:T(8,128)(2,1)S(1)} fusion(bf16[64,768]{1,0:T(8,128)(2,1)} %param.3), kind=kLoop, calls=%fused_computation.47 | loop fusion | bytes 196608
  19.7 1.1 %collective-permute-done.5 = bf16[64,768]{1,0:T(8,128)(2,1)S(1)} collective-permute-done((bf16[64,768]{1,0:T(8,128)(2,1)}, bf16[64,768]{1,0:T(8,128)(2,1)S(1)}, u32[]{:S(2)}, u32[]{:S(2)}) %collective-permute-start.5) | collective-permute-done | bytes 98336 | tf_op jit(solution)/shard_map/ppermute | solution.py:44
  21.3 0.9 %collective-permute-start.2 = (bf16[64,768]{1,0:T(8,128)(2,1)S(1)}, bf16[64,768]{1,0:T(8,128)(2,1)S(1)}, u32[]{:S(2)}, u32[]{:S(2)}) collective-permute-start(bf16[64,768]{1,0:T(8,128)(2,1)S(1)} %copy-done.1), channel_id=1, source_target_pairs={{0,1},{1,0},{2,3},{3,2},{4,5},{5,4},{6,7},{7,6},{8,9},{9,8},{10,11... | collective-permute-start | bytes 294920 | tf_op jit(solution)/shard_map/ppermute | solution.py:44
  22.2 4.9 %collective-permute-done.15 = bf16[64,1536]{1,0:T(8,128)(2,1)S(1)} collective-permute-done((bf16[64,1536]{1,0:T(8,128)(2,1)S(1)}, bf16[64,1536]{1,0:T(8,128)(2,1)S(1)}, u32[]{:S(2)}, u32[]{:S(2)}) %collective-permute-start.15) | collective-permute-done | bytes 196640 | tf_op jit(solution)/shard_map/ppermute | solution.py:44
  28.3 0.8 %collective-permute-done.17 = bf16[64,1536]{1,0:T(8,128)(2,1)S(1)} collective-permute-done((bf16[64,1536]{1,0:T(8,128)(2,1)S(1)}, bf16[64,1536]{1,0:T(8,128)(2,1)S(1)}, u32[]{:S(2)}, u32[]{:S(2)}) %collective-permute-start.17) | collective-permute-done | bytes 196640 | tf_op jit(solution)/shard_map/ppermute | solution.py:44
  29.1 1.5 %collective-permute-start.13 = (bf16[64,1536]{1,0:T(8,128)(2,1)S(1)}, bf16[64,1536]{1,0:T(8,128)(2,1)S(1)}, u32[]{:S(2)}, u32[]{:S(2)}) collective-permute-start(bf16[64,1536]{1,0:T(8,128)(2,1)S(1)} %collective-permute-done.12), channel_id=1, source_target_pairs={{0,8},{1,9},{2,10},{3,11},{4,12},{5,13},{6,14},{7,15},{8,0},{9,1},... | collective-permute-start | bytes 589832 | tf_op jit(solution)/shard_map/ppermute | solution.py:44
  31.3 4.1 %collective-permute-done.7 = bf16[64,768]{1,0:T(8,128)(2,1)S(1)} collective-permute-done((bf16[64,768]{1,0:T(8,128)(2,1)S(1)}, bf16[64,768]{1,0:T(8,128)(2,1)S(1)}, u32[]{:S(2)}, u32[]{:S(2)}) %collective-permute-start.7) | collective-permute-done | bytes 98336 | tf_op jit(solution)/shard_map/ppermute | solution.py:44
  35.9 0.6 collective-permute-start.4
  37.2 0.7 collective-permute-done.11
  38.4 0.6 fusion
  39.0 1.7 %collective-permute-done.4 = bf16[64,768]{1,0:T(8,128)(2,1)S(1)} collective-permute-done((bf16[64,768]{1,0:T(8,128)(2,1)S(1)}, bf16[64,768]{1,0:T(8,128)(2,1)S(1)}, u32[]{:S(2)}, u32[]{:S(2)}) %collective-permute-start.4) | collective-permute-done | bytes 98336 | tf_op jit(solution)/shard_map/ppermute | solution.py:44
  41.8 4.6 %collective-permute-start.20 = (f32[3,4,64]{2,1,0:T(4,128)S(1)}, f32[3,4,64]{2,1,0:T(4,128)S(1)}, u32[]{:S(2)}, u32[]{:S(2)}) collective-permute-start(f32[3,4,64]{2,1,0:T(4,128)S(1)} %constant_dynamic-update-slice_fusion.16), channel_id=1, source_target_pairs={{0,1},{1,0},{2,3},{3,2},{4,5},{5,4},{6,7},{7,6},{8,9},{9,8},{10,11... | collective-permute-start | bytes 9224 | tf_op jit(solution)/shard_map/ppermute | solution.py:44
  46.4 1.6 %collective-permute-done.20 = f32[3,4,64]{2,1,0:T(4,128)S(1)} collective-permute-done((f32[3,4,64]{2,1,0:T(4,128)S(1)}, f32[3,4,64]{2,1,0:T(4,128)S(1)}, u32[]{:S(2)}, u32[]{:S(2)}) %collective-permute-start.20) | collective-permute-done | bytes 3104 | tf_op jit(solution)/shard_map/ppermute | solution.py:44
  48.1 0.7 collective-permute-start.21
  48.8 0.6 collective-permute-start.23
  49.4 2.4 %collective-permute-done.21 = f32[3,4,64]{2,1,0:T(4,128)S(1)} collective-permute-done((f32[3,4,64]{2,1,0:T(4,128)S(1)}, f32[3,4,64]{2,1,0:T(4,128)S(1)}, u32[]{:S(2)}, u32[]{:S(2)}) %collective-permute-start.21) | collective-permute-done | bytes 3104 | tf_op jit(solution)/shard_map/ppermute | solution.py:44
  52.7 1.1 %collective-permute-done.24 = f32[3,8,64]{2,1,0:T(8,128)S(1)} collective-permute-done((f32[3,8,64]{2,1,0:T(8,128)S(1)}, f32[3,8,64]{2,1,0:T(8,128)S(1)}, u32[]{:S(2)}, u32[]{:S(2)}) %collective-permute-start.24) | collective-permute-done | bytes 6176 | tf_op jit(solution)/shard_map/ppermute | solution.py:44
  53.8 0.6 subtract_reduce_fusion
  55.5 0.7 fusion.26
  56.2 2.1 %collective-permute-start.25 = (f32[72,768]{1,0:T(8,128)S(1)}, f32[72,768]{1,0:T(8,128)S(1)}, u32[]{:S(2)}, u32[]{:S(2)}) collective-permute-start(f32[72,768]{1,0:T(8,128)S(1)} %get-tuple-element.11), channel_id=1, source_target_pairs={{0,1},{1,0},{2,3},{3,2},{4,5},{5,4},{6,7},{7,6},{8,9},{9,8},{10,11... | collective-permute-start | bytes 663560 | tf_op jit(solution)/shard_map/ppermute | solution.py:44
  58.3 1.4 %collective-permute-start.26 = (f32[72,768]{1,0:T(8,128)S(1)}, f32[72,768]{1,0:T(8,128)S(1)}, u32[]{:S(2)}, u32[]{:S(2)}) collective-permute-start(f32[72,768]{1,0:T(8,128)S(1)} %get-tuple-element.12), channel_id=1, source_target_pairs={{0,8},{1,9},{2,10},{3,11},{4,12},{5,13},{6,14},{7,15},{8,0},{9,1},... | collective-permute-start | bytes 663560 | tf_op jit(solution)/shard_map/ppermute | solution.py:44
  59.8 4.7 %collective-permute-done.25 = f32[72,768]{1,0:T(8,128)S(1)} collective-permute-done((f32[72,768]{1,0:T(8,128)S(1)}, f32[72,768]{1,0:T(8,128)S(1)}, u32[]{:S(2)}, u32[]{:S(2)}) %collective-permute-start.25) | collective-permute-done | bytes 221216 | tf_op jit(solution)/shard_map/ppermute | solution.py:44
  64.5 5.8 %collective-permute-done.26 = f32[72,768]{1,0:T(8,128)S(1)} collective-permute-done((f32[72,768]{1,0:T(8,128)S(1)}, f32[72,768]{1,0:T(8,128)S(1)}, u32[]{:S(2)}, u32[]{:S(2)}) %collective-permute-start.26) | collective-permute-done | bytes 221216 | tf_op jit(solution)/shard_map/ppermute | solution.py:44
  70.2 0.7 fusion.23
  70.9 0.7 slice.31
  (84 shorter events, 8.2 us)
Async XLA Ops:
  0.6 20.7 %copy-start.1 = (bf16[64,768]{1,0:T(8,128)(2,1)S(1)}, bf16[64,768]{1,0:T(8,128)(2,1)}, u32[]{:S(2)}) copy-start(bf16[64,768]{1,0:T(8,128)(2,1)} %param.3) | copy-start | bytes 294916
  0.6 9.7 %collective-permute-start.1 = (bf16[64,1536]{1,0:T(8,128)(2,1)}, bf16[64,1536]{1,0:T(8,128)(2,1)S(1)}, u32[]{:S(2)}, u32[]{:S(2)}) collective-permute-start(bf16[64,1536]{1,0:T(8,128)(2,1)} %param.2), channel_id=1, source_target_pairs={{0,16},{1,17},{2,18},{3,19},{4,20},{5,21},{6,22},{7,23},{8,24},{9,... | collective-permute-start | bytes 589832 | tf_op jit(solution)/shard_map/ppermute | solution.py:44
  3.7 6.7 %collective-permute-start = (bf16[64,1536]{1,0:T(8,128)(2,1)}, bf16[64,1536]{1,0:T(8,128)(2,1)S(1)}, u32[]{:S(2)}, u32[]{:S(2)}) collective-permute-start(bf16[64,1536]{1,0:T(8,128)(2,1)} %param.2), channel_id=1, source_target_pairs={{0,8},{1,9},{2,10},{3,11},{4,12},{5,13},{6,14},{7,15},{8,0},{9,1},... | collective-permute-start | bytes 589832 | tf_op jit(solution)/shard_map/ppermute | solution.py:44
  5.2 13.6 %collective-permute-start.14 = (bf16[64,1536]{1,0:T(8,128)(2,1)}, bf16[64,1536]{1,0:T(8,128)(2,1)S(1)}, u32[]{:S(2)}, u32[]{:S(2)}) collective-permute-start(bf16[64,1536]{1,0:T(8,128)(2,1)} %param.2), channel_id=1, source_target_pairs={{0,2},{1,3},{2,0},{3,1},{4,6},{5,7},{6,4},{7,5},{8,10},{9,11},{10,... | collective-permute-start | bytes 589832 | tf_op jit(solution)/shard_map/ppermute | solution.py:44
  7.8 19.9 %collective-permute-start.16 = (bf16[64,1536]{1,0:T(8,128)(2,1)}, bf16[64,1536]{1,0:T(8,128)(2,1)S(1)}, u32[]{:S(2)}, u32[]{:S(2)}) collective-permute-start(bf16[64,1536]{1,0:T(8,128)(2,1)} %param.2), channel_id=1, source_target_pairs={{0,4},{1,5},{2,6},{3,7},{4,0},{5,1},{6,2},{7,3},{8,12},{9,13},{10,... | collective-permute-start | bytes 589832 | tf_op jit(solution)/shard_map/ppermute | solution.py:44
  7.8 20.0 %collective-permute-start.12 = (bf16[64,1536]{1,0:T(8,128)(2,1)}, bf16[64,1536]{1,0:T(8,128)(2,1)S(1)}, u32[]{:S(2)}, u32[]{:S(2)}) collective-permute-start(bf16[64,1536]{1,0:T(8,128)(2,1)} %param.2), channel_id=1, source_target_pairs={{0,1},{1,0},{2,3},{3,2},{4,5},{5,4},{6,7},{7,6},{8,9},{9,8},{10,11... | collective-permute-start | bytes 589832 | tf_op jit(solution)/shard_map/ppermute | solution.py:44
  10.3 10.5 %collective-permute-start.5 = (bf16[64,768]{1,0:T(8,128)(2,1)}, bf16[64,768]{1,0:T(8,128)(2,1)S(1)}, u32[]{:S(2)}, u32[]{:S(2)}) collective-permute-start(bf16[64,768]{1,0:T(8,128)(2,1)} %param.3), channel_id=1, source_target_pairs={{0,2},{1,3},{2,0},{3,1},{4,6},{5,7},{6,4},{7,5},{8,10},{9,11},{10,... | collective-permute-start | bytes 294920 | tf_op jit(solution)/shard_map/ppermute | solution.py:44
  12.8 8.5 %collective-permute-start.6 = (bf16[64,768]{1,0:T(8,128)(2,1)}, bf16[64,768]{1,0:T(8,128)(2,1)S(1)}, u32[]{:S(2)}, u32[]{:S(2)}) collective-permute-start(bf16[64,768]{1,0:T(8,128)(2,1)} %param.3), channel_id=1, source_target_pairs={{0,16},{1,17},{2,18},{3,19},{4,20},{5,21},{6,22},{7,23},{8,24},{9,... | collective-permute-start | bytes 294920 | tf_op jit(solution)/shard_map/ppermute | solution.py:44
  18.7 16.6 %collective-permute-start.8 = (bf16[64,768]{1,0:T(8,128)(2,1)}, bf16[64,768]{1,0:T(8,128)(2,1)S(1)}, u32[]{:S(2)}, u32[]{:S(2)}) collective-permute-start(bf16[64,768]{1,0:T(8,128)(2,1)} %param.3), channel_id=1, source_target_pairs={{0,4},{1,5},{2,6},{3,7},{4,0},{5,1},{6,2},{7,3},{8,12},{9,13},{10,... | collective-permute-start | bytes 294920 | tf_op jit(solution)/shard_map/ppermute | solution.py:44
  20.8 6.3 %collective-permute-start.15 = (bf16[64,1536]{1,0:T(8,128)(2,1)S(1)}, bf16[64,1536]{1,0:T(8,128)(2,1)S(1)}, u32[]{:S(2)}, u32[]{:S(2)}) collective-permute-start(bf16[64,1536]{1,0:T(8,128)(2,1)S(1)} %collective-permute-done.14), channel_id=1, source_target_pairs={{0,16},{1,17},{2,18},{3,19},{4,20},{5,21},{6,22},{7,23},{8,24},{9,... | collective-permute-start | bytes 589832 | tf_op jit(solution)/shard_map/ppermute | solution.py:44
  21.3 17.0 %copy-start = (bf16[64,1536]{1,0:T(8,128)(2,1)S(1)}, bf16[64,1536]{1,0:T(8,128)(2,1)}, u32[]{:S(2)}) copy-start(bf16[64,1536]{1,0:T(8,128)(2,1)} %param.2) | copy-start | bytes 589828
  21.3 14.6 %collective-permute-start.2 = (bf16[64,768]{1,0:T(8,128)(2,1)S(1)}, bf16[64,768]{1,0:T(8,128)(2,1)S(1)}, u32[]{:S(2)}, u32[]{:S(2)}) collective-permute-start(bf16[64,768]{1,0:T(8,128)(2,1)S(1)} %copy-done.1), channel_id=1, source_target_pairs={{0,1},{1,0},{2,3},{3,2},{4,5},{5,4},{6,7},{7,6},{8,9},{9,8},{10,11... | collective-permute-start | bytes 294920 | tf_op jit(solution)/shard_map/ppermute | solution.py:44
  27.1 11.9 %collective-permute-start.3 = (bf16[64,768]{1,0:T(8,128)(2,1)S(1)}, bf16[64,768]{1,0:T(8,128)(2,1)S(1)}, u32[]{:S(2)}, u32[]{:S(2)}) collective-permute-start(bf16[64,768]{1,0:T(8,128)(2,1)S(1)} %copy-done.1), channel_id=1, source_target_pairs={{0,8},{1,9},{2,10},{3,11},{4,12},{5,13},{6,14},{7,15},{8,0},{9,1},... | collective-permute-start | bytes 294920 | tf_op jit(solution)/shard_map/ppermute | solution.py:44
  27.6 1.5 %collective-permute-start.17 = (bf16[64,1536]{1,0:T(8,128)(2,1)S(1)}, bf16[64,1536]{1,0:T(8,128)(2,1)S(1)}, u32[]{:S(2)}, u32[]{:S(2)}) collective-permute-start(bf16[64,1536]{1,0:T(8,128)(2,1)S(1)} %collective-permute-done.14), channel_id=1, source_target_pairs={{0,4},{1,5},{2,6},{3,7},{4,0},{5,1},{6,2},{7,3},{8,12},{9,13},{10,... | collective-permute-start | bytes 589832 | tf_op jit(solution)/shard_map/ppermute | solution.py:44
  27.8 2.9 %collective-permute-start.18 = (bf16[64,1536]{1,0:T(8,128)(2,1)S(1)}, bf16[64,1536]{1,0:T(8,128)(2,1)S(1)}, u32[]{:S(2)}, u32[]{:S(2)}) collective-permute-start(bf16[64,1536]{1,0:T(8,128)(2,1)S(1)} %collective-permute-done.1), channel_id=1, source_target_pairs={{0,4},{1,5},{2,6},{3,7},{4,0},{5,1},{6,2},{7,3},{8,12},{9,13},{10,... | collective-permute-start | bytes 589832 | tf_op jit(solution)/shard_map/ppermute | solution.py:44
  29.1 9.2 %collective-permute-start.13 = (bf16[64,1536]{1,0:T(8,128)(2,1)S(1)}, bf16[64,1536]{1,0:T(8,128)(2,1)S(1)}, u32[]{:S(2)}, u32[]{:S(2)}) collective-permute-start(bf16[64,1536]{1,0:T(8,128)(2,1)S(1)} %collective-permute-done.12), channel_id=1, source_target_pairs={{0,8},{1,9},{2,10},{3,11},{4,12},{5,13},{6,14},{7,15},{8,0},{9,1},... | collective-permute-start | bytes 589832 | tf_op jit(solution)/shard_map/ppermute | solution.py:44
  30.7 4.7 %collective-permute-start.7 = (bf16[64,768]{1,0:T(8,128)(2,1)S(1)}, bf16[64,768]{1,0:T(8,128)(2,1)S(1)}, u32[]{:S(2)}, u32[]{:S(2)}) collective-permute-start(bf16[64,768]{1,0:T(8,128)(2,1)S(1)} %collective-permute-done.5), channel_id=1, source_target_pairs={{0,16},{1,17},{2,18},{3,19},{4,20},{5,21},{6,22},{7,23},{8,24},{9,... | collective-permute-start | bytes 294920 | tf_op jit(solution)/shard_map/ppermute | solution.py:44
  35.3 1.3 %collective-permute-start.9 = (bf16[64,768]{1,0:T(8,128)(2,1)S(1)}, bf16[64,768]{1,0:T(8,128)(2,1)S(1)}, u32[]{:S(2)}, u32[]{:S(2)}) collective-permute-start(bf16[64,768]{1,0:T(8,128)(2,1)S(1)} %collective-permute-done.5), channel_id=1, source_target_pairs={{0,4},{1,5},{2,6},{3,7},{4,0},{5,1},{6,2},{7,3},{8,12},{9,13},{10,... | collective-permute-start | bytes 294920 | tf_op jit(solution)/shard_map/ppermute | solution.py:44
  35.4 1.5 %collective-permute-start.10 = (bf16[64,768]{1,0:T(8,128)(2,1)S(1)}, bf16[64,768]{1,0:T(8,128)(2,1)S(1)}, u32[]{:S(2)}, u32[]{:S(2)}) collective-permute-start(bf16[64,768]{1,0:T(8,128)(2,1)S(1)} %collective-permute-done.6), channel_id=1, source_target_pairs={{0,4},{1,5},{2,6},{3,7},{4,0},{5,1},{6,2},{7,3},{8,12},{9,13},{10,... | collective-permute-start | bytes 294920 | tf_op jit(solution)/shard_map/ppermute | solution.py:44
  35.9 4.8 %collective-permute-start.4 = (bf16[64,768]{1,0:T(8,128)(2,1)S(1)}, bf16[64,768]{1,0:T(8,128)(2,1)S(1)}, u32[]{:S(2)}, u32[]{:S(2)}) collective-permute-start(bf16[64,768]{1,0:T(8,128)(2,1)S(1)} %collective-permute-done.2), channel_id=1, source_target_pairs={{0,8},{1,9},{2,10},{3,11},{4,12},{5,13},{6,14},{7,15},{8,0},{9,1},... | collective-permute-start | bytes 294920 | tf_op jit(solution)/shard_map/ppermute | solution.py:44
  36.6 1.3 %collective-permute-start.11 = (bf16[64,768]{1,0:T(8,128)(2,1)S(1)}, bf16[64,768]{1,0:T(8,128)(2,1)S(1)}, u32[]{:S(2)}, u32[]{:S(2)}) collective-permute-start(bf16[64,768]{1,0:T(8,128)(2,1)S(1)} %collective-permute-done.7), channel_id=1, source_target_pairs={{0,4},{1,5},{2,6},{3,7},{4,0},{5,1},{6,2},{7,3},{8,12},{9,13},{10,... | collective-permute-start | bytes 294920 | tf_op jit(solution)/shard_map/ppermute | solution.py:44
  36.9 1.4 %collective-permute-start.19 = (bf16[64,1536]{1,0:T(8,128)(2,1)S(1)}, bf16[64,1536]{1,0:T(8,128)(2,1)S(1)}, u32[]{:S(2)}, u32[]{:S(2)}) collective-permute-start(bf16[64,1536]{1,0:T(8,128)(2,1)S(1)} %collective-permute-done.15), channel_id=1, source_target_pairs={{0,4},{1,5},{2,6},{3,7},{4,0},{5,1},{6,2},{7,3},{8,12},{9,13},{10,... | collective-permute-start | bytes 589832 | tf_op jit(solution)/shard_map/ppermute | solution.py:44
  41.8 7.0 %collective-permute-start.22 = (f32[3,8,64]{2,1,0:T(8,128)S(1)}, f32[3,8,64]{2,1,0:T(8,128)S(1)}, u32[]{:S(2)}, u32[]{:S(2)}) collective-permute-start(f32[3,8,64]{2,1,0:T(8,128)S(1)} %constant_dynamic-update-slice_fusion.19), channel_id=1, source_target_pairs={{0,2},{1,3},{2,0},{3,1},{4,6},{5,7},{6,4},{7,5},{8,10},{9,11},{10,... | collective-permute-start | bytes 18440 | tf_op jit(solution)/shard_map/ppermute | solution.py:44
  41.8 6.2 %collective-permute-start.20 = (f32[3,4,64]{2,1,0:T(4,128)S(1)}, f32[3,4,64]{2,1,0:T(4,128)S(1)}, u32[]{:S(2)}, u32[]{:S(2)}) collective-permute-start(f32[3,4,64]{2,1,0:T(4,128)S(1)} %constant_dynamic-update-slice_fusion.16), channel_id=1, source_target_pairs={{0,1},{1,0},{2,3},{3,2},{4,5},{5,4},{6,7},{7,6},{8,9},{9,8},{10,11... | collective-permute-start | bytes 9224 | tf_op jit(solution)/shard_map/ppermute | solution.py:44
  48.1 3.7 %collective-permute-start.21 = (f32[3,4,64]{2,1,0:T(4,128)S(1)}, f32[3,4,64]{2,1,0:T(4,128)S(1)}, u32[]{:S(2)}, u32[]{:S(2)}) collective-permute-start(f32[3,4,64]{2,1,0:T(4,128)S(1)} %add.93), channel_id=1, source_target_pairs={{0,8},{1,9},{2,10},{3,11},{4,12},{5,13},{6,14},{7,15},{8,0},{9,1},... | collective-permute-start | bytes 9224 | tf_op jit(solution)/shard_map/ppermute | solution.py:44
  48.8 3.8 %collective-permute-start.23 = (f32[3,8,64]{2,1,0:T(8,128)S(1)}, f32[3,8,64]{2,1,0:T(8,128)S(1)}, u32[]{:S(2)}, u32[]{:S(2)}) collective-permute-start(f32[3,8,64]{2,1,0:T(8,128)S(1)} %add.98), channel_id=1, source_target_pairs={{0,16},{1,17},{2,18},{3,19},{4,20},{5,21},{6,22},{7,23},{8,24},{9,... | collective-permute-start | bytes 18440 | tf_op jit(solution)/shard_map/ppermute | solution.py:44
  52.6 1.2 %collective-permute-start.24 = (f32[3,8,64]{2,1,0:T(8,128)S(1)}, f32[3,8,64]{2,1,0:T(8,128)S(1)}, u32[]{:S(2)}, u32[]{:S(2)}) collective-permute-start(f32[3,8,64]{2,1,0:T(8,128)S(1)} %add.99), channel_id=1, source_target_pairs={{0,4},{1,5},{2,6},{3,7},{4,0},{5,1},{6,2},{7,3},{8,12},{9,13},{10,... | collective-permute-start | bytes 18440 | tf_op jit(solution)/shard_map/ppermute | solution.py:44
  56.2 8.3 %collective-permute-start.25 = (f32[72,768]{1,0:T(8,128)S(1)}, f32[72,768]{1,0:T(8,128)S(1)}, u32[]{:S(2)}, u32[]{:S(2)}) collective-permute-start(f32[72,768]{1,0:T(8,128)S(1)} %get-tuple-element.11), channel_id=1, source_target_pairs={{0,1},{1,0},{2,3},{3,2},{4,5},{5,4},{6,7},{7,6},{8,9},{9,8},{10,11... | collective-permute-start | bytes 663560 | tf_op jit(solution)/shard_map/ppermute | solution.py:44
  58.3 12.0 %collective-permute-start.26 = (f32[72,768]{1,0:T(8,128)S(1)}, f32[72,768]{1,0:T(8,128)S(1)}, u32[]{:S(2)}, u32[]{:S(2)}) collective-permute-start(f32[72,768]{1,0:T(8,128)S(1)} %get-tuple-element.12), channel_id=1, source_target_pairs={{0,8},{1,9},{2,10},{3,11},{4,12},{5,13},{6,14},{7,15},{8,0},{9,1},... | collective-permute-start | bytes 663560 | tf_op jit(solution)/shard_map/ppermute | solution.py:44
  59.7 10.5 %collective-permute-start.27 = (f32[72,768]{1,0:T(8,128)S(1)}, f32[72,768]{1,0:T(8,128)S(1)}, u32[]{:S(2)}, u32[]{:S(2)}) collective-permute-start(f32[72,768]{1,0:T(8,128)S(1)} %get-tuple-element.10), channel_id=1, source_target_pairs={{0,9},{1,8},{2,11},{3,10},{4,13},{5,12},{6,15},{7,14},{8,1},{9,0},... | collective-permute-start | bytes 663560 | tf_op jit(solution)/shard_map/ppermute | solution.py:44

commit v4 on v3

--- a/solution.py
+++ b/solution.py
@@ -44,15 +44,59 @@
     return lax.ppermute(value, AXES, [(i, i ^ mask) for i in range(count)])
 
 
-def gather(own, masks, count):
-    pieces = [own]
-    for mask in masks:
-        pieces += [send(piece, mask, count) for piece in pieces]
-    return pieces
+def after(value, other):
+    return lax.optimization_barrier((value, other))[0]
 
 
-def after(value, other):
-    return lax.optimization_barrier((value, other))[0]
+def forward(pieces, masks, level, count):
+    for place in range(1 << len(masks)):
+        if place.bit_count() == level and place not in pieces:
+            top = place.bit_length() - 1
+            pieces[place] = send(pieces[place ^ (1 << top)], masks[top], count)
+
+
+def gather(teacher, student, row_masks, col_masks, count):
+    *plane_masks, core_mask = col_masks
+    row_t, col_t = {0: teacher}, {0: teacher}
+    row_s, col_s = {0: student}, {0: student}
+    core_t, core_s = [], []
+    sides = ((row_t, row_s, row_masks), (col_t, col_s, plane_masks))
+    for side_t, _, masks in sides:
+        for b, mask in enumerate(masks):
+            side_t[1 << b] = send(teacher, mask, count)
+    late = after(student, (row_t[2], col_t[2]))
+    for _, side_s, masks in sides:
+        for b, mask in enumerate(masks):
+            if b:
+                side_s[1 << b] = send(late, mask, count)
+    late = after(student, (row_s[2], col_s[2]))
+    for _, side_s, masks in sides:
+        side_s[1] = send(late, masks[0], count)
+
+    early = (row_s[2], col_s[2])
+    for row, col, core in ((row_t, col_t, core_t), (row_s, col_s, core_s)):
+        row[1], col[1] = after((row[1], col[1]), early)
+        for level in range(1, len(row_masks) + 1):
+            if level > 1:
+                forward(row, row_masks, level, count)
+                forward(col, plane_masks, level, count)
+            ready = [p for p in range(1 << len(plane_masks)) if max(p.bit_count(), 1) == level]
+            if ready:
+                got = send(jnp.concatenate([col[p] for p in ready]), core_mask, count)
+                core += zip(ready, jnp.split(got, len(ready)))
+                if level == 1:
+                    early = (early, got)
+    out = []
+    for row, col, core in ((row_t, col_t, core_t), (row_s, col_s, core_s)):
+        col = [col[p] for p in sorted(col)] + [piece for _, piece in sorted(core, key=lambda c: c[0])]
+        out.append((jnp.concatenate([row[p] for p in sorted(row)]), jnp.concatenate(col)))
+    return out
+
+
+def tree_sum(values):
+    while len(values) > 1:
+        values = [values[i] + values[i + 1] for i in range(0, len(values), 2)]
+    return values[0]
 
 
 def group_sum(parts, masks, count):
@@ -73,12 +117,7 @@
     row_masks, col_masks = subgroups(blocks, inner)
     n_row, n_col = 1 << len(row_masks), 1 << len(col_masks)
 
-    row_t = gather(teacher, row_masks, count)
-    col_t = gather(teacher, col_masks, count)
-    student_late = after(student, (row_t[2], col_t[2]))
-    row_s = gather(student_late, row_masks, count)
-    col_s = gather(student_late, col_masks, count)
-    row_t, col_t, row_s, col_s = map(jnp.concatenate, (row_t, col_t, row_s, col_s))
+    (row_t, col_t), (row_s, col_s) = gather(teacher, student, row_masks, col_masks, count)
 
     gram_s = jnp.einsum("rd,cd->rc", row_s, col_s, preferred_element_type=jnp.float32)
     gram_t = jnp.einsum("rd,cd->rc", row_t, col_t, preferred_element_type=jnp.float32)
@@ -94,16 +133,12 @@
     col_w = col_alpha[None, :] * gram_s - col_beta[None, :] * gram_t
     out = jnp.dot(row_w.astype(jnp.bfloat16), col_s, preferred_element_type=jnp.float32)
     out += jnp.dot(col_w.astype(jnp.bfloat16), col_s, preferred_element_type=jnp.float32)
-    out = out.reshape(n_row, rows, -1)
-    out = jnp.concatenate([out, jnp.full((n_row, 8, out.shape[2]), jnp.sum(terms))], 1)
-
-    parts = [out[0]]
-    for place, mask in enumerate(span(row_masks)):
-        if place:
-            parts.append(send(out[place], mask, count))
-    while len(parts) > 1:
-        parts = [parts[i] + parts[i + 1] for i in range(0, len(parts), 2)]
-    return (parts[0][rows, 0] / total, parts[0][:rows])
+    out = jnp.split(out, n_row)
+    places = [(place, mask) for place, mask in enumerate(span(row_masks)) if place]
+    grads = out[:1] + [send(out[place], mask, count) for place, mask in places]
+    term = after(jnp.full((1, 128), jnp.sum(terms)), grads[2])
+    losses = [term] + [send(term, mask, count) for _, mask in places]
+    return (tree_sum(losses)[0, 0] / total, tree_sum(grads))
 
 
 def solution(mesh):

time: 74.1 us -> 64.3 us (0.87)
  waiting for transfers between devices: 35.4 us -> 21.3 us
  starting transfers between devices: 27.5 us -> 32.5 us
  local copies, waits for them, and re-layouts: 4.98 us -> 3.8 us
  other arithmetic: 1.4 us -> 2.41 us
    ppermute x28 -> x27, waiting for transfers between devices: 35.4 us -> 21.3 us  [send(): return lax.ppermute(value, AXES, [(i, i ^ mask) for i in range(count)])]
    ppermute x28 -> x27, starting transfers between devices: 27.5 us -> 32.5 us  [send(): return lax.ppermute(value, AXES, [(i, i ^ mask) for i in range(count)])]
    slice x2 -> x0, local copies, waits for them, and re-layouts: 1.2 us -> none  [per_device(): return (parts[0][rows, 0] / total, parts[0][:rows])]
    concatenate x0 -> x2, other arithmetic: none -> 0.98 us  [gather(): got = send(jnp.concatenate([col[p] for p in ready]), core_mask, count)]
    unnamed x22 -> x18, local copies, waits for them, and re-layouts: 2.04 us -> 2.07 us
  transfers between devices with their start and end apart: 28 -> 27, of which waited for: 16 -> 16; matrix products, arithmetic and copies ran while one was open for 4% -> 9% of each run, Pallas kernels for 0% -> 0%
where the time goes in v4:
time: 64.3 us; the launch traced here: 64.1 us
  starting transfers between devices  32.5 us (51%)
  waiting for transfers between devices  21.3 us (33%)
  local copies, waits for them, and re-layouts  3.8 us (6%)
  other arithmetic  2.41 us (4%)
  between operations  2.03 us (3%)
  matrix products  1.94 us (3%)
    ppermute x27, starting transfers between devices, send(): return lax.ppermute(value, AXES, [(i, i ^ mask) for i in range(count)])  32.5 us
    ppermute x27, waiting for transfers between devices, send(): return lax.ppermute(value, AXES, [(i, i ^ mask) for i in range(count)])  21.3 us
    unnamed x18, local copies, waits for them, and re-layouts  2.07 us
  transfers between devices with their start and end apart: 27, of which 16 were waited for; matrix products, arithmetic and copies ran while one was open for 9% of the time, Pallas kernels for 0%

profile of v4, /device:TPU:0, one launch (start us, length us, event | category | flops | bytes accessed | tf_op | source)
XLA Modules:
  0.0 64.1 jit_solution(12140058704867444039)
XLA Ops:
  0.6 3.1 %collective-permute-start.6 = (bf16[64,1536]{1,0:T(8,128)(2,1)}, bf16[64,1536]{1,0:T(8,128)(2,1)S(1)}, u32[]{:S(2)}, u32[]{:S(2)}) collective-permute-start(bf16[64,1536]{1,0:T(8,128)(2,1)} %param.2), channel_id=1, source_target_pairs={{0,1},{1,0},{2,3},{3,2},{4,5},{5,4},{6,7},{7,6},{8,9},{9,8},{10,11... | collective-permute-start | bytes 589832 | tf_op jit(solution)/shard_map/ppermute | solution.py:44
  3.7 2.6 %collective-permute-start.7 = (bf16[64,1536]{1,0:T(8,128)(2,1)}, bf16[64,1536]{1,0:T(8,128)(2,1)S(1)}, u32[]{:S(2)}, u32[]{:S(2)}) collective-permute-start(bf16[64,1536]{1,0:T(8,128)(2,1)} %param.2), channel_id=1, source_target_pairs={{0,2},{1,3},{2,0},{3,1},{4,6},{5,7},{6,4},{7,5},{8,10},{9,11},{10,... | collective-permute-start | bytes 589832 | tf_op jit(solution)/shard_map/ppermute | solution.py:44
  6.3 1.5 %collective-permute-start = (bf16[64,1536]{1,0:T(8,128)(2,1)}, bf16[64,1536]{1,0:T(8,128)(2,1)S(1)}, u32[]{:S(2)}, u32[]{:S(2)}) collective-permute-start(bf16[64,1536]{1,0:T(8,128)(2,1)} %param.2), channel_id=1, source_target_pairs={{0,8},{1,9},{2,10},{3,11},{4,12},{5,13},{6,14},{7,15},{8,0},{9,1},... | collective-permute-start | bytes 589832 | tf_op jit(solution)/shard_map/ppermute | solution.py:44
  7.8 1.5 %collective-permute-start.1 = (bf16[64,1536]{1,0:T(8,128)(2,1)}, bf16[64,1536]{1,0:T(8,128)(2,1)S(1)}, u32[]{:S(2)}, u32[]{:S(2)}) collective-permute-start(bf16[64,1536]{1,0:T(8,128)(2,1)} %param.2), channel_id=1, source_target_pairs={{0,16},{1,17},{2,18},{3,19},{4,20},{5,21},{6,22},{7,23},{8,24},{9,... | collective-permute-start | bytes 589832 | tf_op jit(solution)/shard_map/ppermute | solution.py:44
  9.3 1.0 %constant_dynamic-update-slice_fusion.11 = bf16[512,1536]{1,0:T(8,128)(2,1)S(1)} fusion(bf16[64,1536]{1,0:T(8,128)(2,1)} %param.2), kind=kLoop, calls=%fused_computation.45 | loop fusion | bytes 393216
  10.3 2.3 %collective-permute-done = bf16[64,1536]{1,0:T(8,128)(2,1)S(1)} collective-permute-done((bf16[64,1536]{1,0:T(8,128)(2,1)}, bf16[64,1536]{1,0:T(8,128)(2,1)S(1)}, u32[]{:S(2)}, u32[]{:S(2)}) %collective-permute-start) | collective-permute-done | bytes 196640 | tf_op jit(solution)/shard_map/ppermute | solution.py:44
  12.6 1.2 %collective-permute-done.1 = bf16[64,1536]{1,0:T(8,128)(2,1)S(1)} collective-permute-done((bf16[64,1536]{1,0:T(8,128)(2,1)}, bf16[64,1536]{1,0:T(8,128)(2,1)S(1)}, u32[]{:S(2)}, u32[]{:S(2)}) %collective-permute-start.1) | collective-permute-done | bytes 196640 | tf_op jit(solution)/shard_map/ppermute | solution.py:44
  14.4 1.5 %collective-permute-start.3 = (bf16[64,768]{1,0:T(8,128)(2,1)}, bf16[64,768]{1,0:T(8,128)(2,1)S(1)}, u32[]{:S(2)}, u32[]{:S(2)}) collective-permute-start(bf16[64,768]{1,0:T(8,128)(2,1)} %param.3), channel_id=1, source_target_pairs={{0,16},{1,17},{2,18},{3,19},{4,20},{5,21},{6,22},{7,23},{8,24},{9,... | collective-permute-start | bytes 294920 | tf_op jit(solution)/shard_map/ppermute | solution.py:44
  15.9 0.9 %constant_dynamic-update-slice_fusion.5 = bf16[512,768]{1,0:T(8,128)(2,1)S(1)} fusion(bf16[64,768]{1,0:T(8,128)(2,1)} %param.3), kind=kLoop, calls=%fused_computation.39 | loop fusion | bytes 196608
  16.8 1.8 %collective-permute-done.2 = bf16[64,768]{1,0:T(8,128)(2,1)S(1)} collective-permute-done((bf16[64,768]{1,0:T(8,128)(2,1)}, bf16[64,768]{1,0:T(8,128)(2,1)S(1)}, u32[]{:S(2)}, u32[]{:S(2)}) %collective-permute-start.2) | collective-permute-done | bytes 98336 | tf_op jit(solution)/shard_map/ppermute | solution.py:44
  19.9 1.6 %collective-permute-start.14 = (bf16[64,1536]{1,0:T(8,128)(2,1)S(1)}, bf16[64,1536]{1,0:T(8,128)(2,1)S(1)}, u32[]{:S(2)}, u32[]{:S(2)}) collective-permute-start(bf16[64,1536]{1,0:T(8,128)(2,1)S(1)} %collective-permute-done.7), channel_id=1, source_target_pairs={{0,16},{1,17},{2,18},{3,19},{4,20},{5,21},{6,22},{7,23},{8,24},{9,... | collective-permute-start | bytes 589832 | tf_op jit(solution)/shard_map/ppermute | solution.py:44
  21.5 1.0 %pad_maximum_fusion = bf16[192,1536]{1,0:T(8,128)(2,1)S(1)} fusion(bf16[64,1536]{1,0:T(8,128)(2,1)S(1)} %collective-permute-done.1, bf16[64,1536]{1,0:T(8,128)(2,1)S(1)} %collective-permute-done.7, bf16[64,1536]{1,0:T(8,128)(2,1)} %param.2), kind=kLoop, calls=%fused_computation.9 | loop fusion | flops 1769472 | bytes 1179648 | tf_op jit(solution)/shard_map/concatenate | solution.py:85
  22.5 1.6 %collective-permute-start.13 = (bf16[64,1536]{1,0:T(8,128)(2,1)S(1)}, bf16[64,1536]{1,0:T(8,128)(2,1)S(1)}, u32[]{:S(2)}, u32[]{:S(2)}) collective-permute-start(bf16[64,1536]{1,0:T(8,128)(2,1)S(1)} %collective-permute-done.6), channel_id=1, source_target_pairs={{0,8},{1,9},{2,10},{3,11},{4,12},{5,13},{6,14},{7,15},{8,0},{9,1},... | collective-permute-start | bytes 589832 | tf_op jit(solution)/shard_map/ppermute | solution.py:44
  24.2 1.4 %collective-permute-done.14 = bf16[64,1536]{1,0:T(8,128)(2,1)S(1)} collective-permute-done((bf16[64,1536]{1,0:T(8,128)(2,1)S(1)}, bf16[64,1536]{1,0:T(8,128)(2,1)S(1)}, u32[]{:S(2)}, u32[]{:S(2)}) %collective-permute-start.14) | collective-permute-done | bytes 196640 | tf_op jit(solution)/shard_map/ppermute | solution.py:44
  25.7 1.6 %collective-permute-start.10 = (bf16[64,768]{1,0:T(8,128)(2,1)S(1)}, bf16[64,768]{1,0:T(8,128)(2,1)S(1)}, u32[]{:S(2)}, u32[]{:S(2)}) collective-permute-start(bf16[64,768]{1,0:T(8,128)(2,1)S(1)} %collective-permute-done.5), channel_id=1, source_target_pairs={{0,16},{1,17},{2,18},{3,19},{4,20},{5,21},{6,22},{7,23},{8,24},{9,... | collective-permute-start | bytes 294920 | tf_op jit(solution)/shard_map/ppermute | solution.py:44
  27.6 1.5 %collective-permute-start.9 = (bf16[64,768]{1,0:T(8,128)(2,1)S(1)}, bf16[64,768]{1,0:T(8,128)(2,1)S(1)}, u32[]{:S(2)}, u32[]{:S(2)}) collective-permute-start(bf16[64,768]{1,0:T(8,128)(2,1)S(1)} %collective-permute-done.4), channel_id=1, source_target_pairs={{0,8},{1,9},{2,10},{3,11},{4,12},{5,13},{6,14},{7,15},{8,0},{9,1},... | collective-permute-start | bytes 294920 | tf_op jit(solution)/shard_map/ppermute | solution.py:44
  31.0 1.2 %collective-permute-done.12 = bf16[64,768]{1,0:T(8,128)(2,1)S(1)} collective-permute-done((bf16[64,768]{1,0:T(8,128)(2,1)S(1)}, bf16[64,768]{1,0:T(8,128)(2,1)S(1)}, u32[]{:S(2)}, u32[]{:S(2)}) %collective-permute-start.12) | collective-permute-done | bytes 98336 | tf_op jit(solution)/shard_map/ppermute | solution.py:44
  33.4 2.6 %collective-permute-start.16 = (f32[3,8,64]{2,1,0:T(8,128)S(1)}, f32[3,8,64]{2,1,0:T(8,128)S(1)}, u32[]{:S(2)}, u32[]{:S(2)}) collective-permute-start(f32[3,8,64]{2,1,0:T(8,128)S(1)} %constant_dynamic-update-slice_fusion.12), channel_id=1, source_target_pairs={{0,2},{1,3},{2,0},{3,1},{4,6},{5,7},{6,4},{7,5},{8,10},{9,11},{10,... | collective-permute-start | bytes 18440 | tf_op jit(solution)/shard_map/ppermute | solution.py:44
  36.3 1.8 %collective-permute-start.19 = (f32[3,4,64]{2,1,0:T(4,128)S(1)}, f32[3,4,64]{2,1,0:T(4,128)S(1)}, u32[]{:S(2)}, u32[]{:S(2)}) collective-permute-start(f32[3,4,64]{2,1,0:T(4,128)S(1)} %constant_dynamic-update-slice_fusion.15), channel_id=1, source_target_pairs={{0,1},{1,0},{2,3},{3,2},{4,5},{5,4},{6,7},{7,6},{8,9},{9,8},{10,11... | collective-permute-start | bytes 9224 | tf_op jit(solution)/shard_map/ppermute | solution.py:44
  38.1 1.8 %collective-permute-done.19 = f32[3,4,64]{2,1,0:T(4,128)S(1)} collective-permute-done((f32[3,4,64]{2,1,0:T(4,128)S(1)}, f32[3,4,64]{2,1,0:T(4,128)S(1)}, u32[]{:S(2)}, u32[]{:S(2)}) %collective-permute-start.19) | collective-permute-done | bytes 3104 | tf_op jit(solution)/shard_map/ppermute | solution.py:44
  39.9 1.6 %collective-permute-start.20 = (f32[3,4,64]{2,1,0:T(4,128)S(1)}, f32[3,4,64]{2,1,0:T(4,128)S(1)}, u32[]{:S(2)}, u32[]{:S(2)}) collective-permute-start(f32[3,4,64]{2,1,0:T(4,128)S(1)} %add.106), channel_id=1, source_target_pairs={{0,8},{1,9},{2,10},{3,11},{4,12},{5,13},{6,14},{7,15},{8,0},{9,1},... | collective-permute-start | bytes 9224 | tf_op jit(solution)/shard_map/ppermute | solution.py:44
  41.5 1.3 %collective-permute-start.17 = (f32[3,8,64]{2,1,0:T(8,128)S(1)}, f32[3,8,64]{2,1,0:T(8,128)S(1)}, u32[]{:S(2)}, u32[]{:S(2)}) collective-permute-start(f32[3,8,64]{2,1,0:T(8,128)S(1)} %add.100), channel_id=1, source_target_pairs={{0,16},{1,17},{2,18},{3,19},{4,20},{5,21},{6,22},{7,23},{8,24},{9,... | collective-permute-start | bytes 18440 | tf_op jit(solution)/shard_map/ppermute | solution.py:44
  42.8 0.8 %collective-permute-done.20 = f32[3,4,64]{2,1,0:T(4,128)S(1)} collective-permute-done((f32[3,4,64]{2,1,0:T(4,128)S(1)}, f32[3,4,64]{2,1,0:T(4,128)S(1)}, u32[]{:S(2)}, u32[]{:S(2)}) %collective-permute-start.20) | collective-permute-done | bytes 3104 | tf_op jit(solution)/shard_map/ppermute | solution.py:44
  43.9 1.4 %collective-permute-done.17 = f32[3,8,64]{2,1,0:T(8,128)S(1)} collective-permute-done((f32[3,8,64]{2,1,0:T(8,128)S(1)}, f32[3,8,64]{2,1,0:T(8,128)S(1)}, u32[]{:S(2)}, u32[]{:S(2)}) %collective-permute-start.17) | collective-permute-done | bytes 6176 | tf_op jit(solution)/shard_map/ppermute | solution.py:44
  45.4 1.1 %collective-permute-done.18 = f32[3,8,64]{2,1,0:T(8,128)S(1)} collective-permute-done((f32[3,8,64]{2,1,0:T(8,128)S(1)}, f32[3,8,64]{2,1,0:T(8,128)S(1)}, u32[]{:S(2)}, u32[]{:S(2)}) %collective-permute-start.18) | collective-permute-done | bytes 6176 | tf_op jit(solution)/shard_map/ppermute | solution.py:44
  48.9 1.8 %collective-permute-start.25 = (f32[64,768]{1,0:T(8,128)S(1)}, f32[64,768]{1,0:T(8,128)S(1)}, u32[]{:S(2)}, u32[]{:S(2)}) collective-permute-start(f32[64,768]{1,0:T(8,128)S(1)} %get-tuple-element.23), channel_id=1, source_target_pairs={{0,1},{1,0},{2,3},{3,2},{4,5},{5,4},{6,7},{7,6},{8,9},{9,8},{10,11... | collective-permute-start | bytes 589832 | tf_op jit(solution)/shard_map/ppermute | solution.py:44
  50.7 1.1 %collective-permute-start.26 = (f32[64,768]{1,0:T(8,128)S(1)}, f32[64,768]{1,0:T(8,128)S(1)}, u32[]{:S(2)}, u32[]{:S(2)}) collective-permute-start(f32[64,768]{1,0:T(8,128)S(1)} %get-tuple-element.22), channel_id=1, source_target_pairs={{0,9},{1,8},{2,11},{3,10},{4,13},{5,12},{6,15},{7,14},{8,1},{9,0},... | collective-permute-start | bytes 589832 | tf_op jit(solution)/shard_map/ppermute | solution.py:44
  51.8 3.5 %collective-permute-done.21 = f32[64,768]{1,0:T(8,128)S(1)} collective-permute-done((f32[64,768]{1,0:T(8,128)S(1)}, f32[64,768]{1,0:T(8,128)S(1)}, u32[]{:S(2)}, u32[]{:S(2)}) %collective-permute-start.21) | collective-permute-done | bytes 196640 | tf_op jit(solution)/shard_map/ppermute | solution.py:44
  56.6 2.8 %collective-permute-start.24 = (f32[1,128]{1,0:T(1,128)S(1)}, f32[1,128]{1,0:T(1,128)S(1)}, u32[]{:S(2)}, u32[]{:S(2)}) collective-permute-start(f32[1,128]{1,0:T(1,128)S(1)} %broadcast_in_dim.2), channel_id=1, source_target_pairs={{0,9},{1,8},{2,11},{3,10},{4,13},{5,12},{6,15},{7,14},{8,1},{9,0},... | collective-permute-start | bytes 1544 | tf_op jit(solution)/shard_map/ppermute | solution.py:44
  59.5 1.3 %collective-permute-done.26 = f32[64,768]{1,0:T(8,128)S(1)} collective-permute-done((f32[64,768]{1,0:T(8,128)S(1)}, f32[64,768]{1,0:T(8,128)S(1)}, u32[]{:S(2)}, u32[]{:S(2)}) %collective-permute-start.26) | collective-permute-done | bytes 196640 | tf_op jit(solution)/shard_map/ppermute | solution.py:44
  60.8 0.7 %fusion.21 = f32[64,768]{1,0:T(8,128)} fusion(f32[64,768]{1,0:T(8,128)S(1)} %collective-permute-done.25, f32[256,768]{1,0:T(8,128)S(1)} %convolution_add_fusion, f32[64,768]{1,0:T(8,128)S(1)} %collective-permute-done.21, f32[64,768]{1,0:T(8,128)S(1)} %collective-permute-done.26), kind=kLoop, calls=%fused_computation.33 | loop fusion | flops 147456 | bytes 983040 | tf_op jit(solution)/shard_map/add | solution.py:98
  61.6 1.3 %collective-permute-done.22 = f32[1,128]{1,0:T(1,128)S(1)} collective-permute-done((f32[1,128]{1,0:T(1,128)S(1)}, f32[1,128]{1,0:T(1,128)S(1)}, u32[]{:S(2)}, u32[]{:S(2)}) %collective-permute-start.22) | collective-permute-done | bytes 544 | tf_op jit(solution)/shard_map/ppermute | solution.py:44
  (80 shorter events, 9.7 us)
Async XLA Ops:
  0.6 26.7 %copy-start.1 = (bf16[64,768]{1,0:T(8,128)(2,1)S(1)}, bf16[64,768]{1,0:T(8,128)(2,1)}, u32[]{:S(2)}) copy-start(bf16[64,768]{1,0:T(8,128)(2,1)} %param.3) | copy-start | bytes 294916
  0.6 19.3 %collective-permute-start.6 = (bf16[64,1536]{1,0:T(8,128)(2,1)}, bf16[64,1536]{1,0:T(8,128)(2,1)S(1)}, u32[]{:S(2)}, u32[]{:S(2)}) collective-permute-start(bf16[64,1536]{1,0:T(8,128)(2,1)} %param.2), channel_id=1, source_target_pairs={{0,1},{1,0},{2,3},{3,2},{4,5},{5,4},{6,7},{7,6},{8,9},{9,8},{10,11... | collective-permute-start | bytes 589832 | tf_op jit(solution)/shard_map/ppermute | solution.py:44
  3.7 16.2 %collective-permute-start.7 = (bf16[64,1536]{1,0:T(8,128)(2,1)}, bf16[64,1536]{1,0:T(8,128)(2,1)S(1)}, u32[]{:S(2)}, u32[]{:S(2)}) collective-permute-start(bf16[64,1536]{1,0:T(8,128)(2,1)} %param.2), channel_id=1, source_target_pairs={{0,2},{1,3},{2,0},{3,1},{4,6},{5,7},{6,4},{7,5},{8,10},{9,11},{10,... | collective-permute-start | bytes 589832 | tf_op jit(solution)/shard_map/ppermute | solution.py:44
  6.3 6.3 %collective-permute-start = (bf16[64,1536]{1,0:T(8,128)(2,1)}, bf16[64,1536]{1,0:T(8,128)(2,1)S(1)}, u32[]{:S(2)}, u32[]{:S(2)}) collective-permute-start(bf16[64,1536]{1,0:T(8,128)(2,1)} %param.2), channel_id=1, source_target_pairs={{0,8},{1,9},{2,10},{3,11},{4,12},{5,13},{6,14},{7,15},{8,0},{9,1},... | collective-permute-start | bytes 589832 | tf_op jit(solution)/shard_map/ppermute | solution.py:44
  7.8 6.0 %collective-permute-start.1 = (bf16[64,1536]{1,0:T(8,128)(2,1)}, bf16[64,1536]{1,0:T(8,128)(2,1)S(1)}, u32[]{:S(2)}, u32[]{:S(2)}) collective-permute-start(bf16[64,1536]{1,0:T(8,128)(2,1)} %param.2), channel_id=1, source_target_pairs={{0,16},{1,17},{2,18},{3,19},{4,20},{5,21},{6,22},{7,23},{8,24},{9,... | collective-permute-start | bytes 589832 | tf_op jit(solution)/shard_map/ppermute | solution.py:44
  13.8 4.8 %collective-permute-start.2 = (bf16[64,768]{1,0:T(8,128)(2,1)}, bf16[64,768]{1,0:T(8,128)(2,1)S(1)}, u32[]{:S(2)}, u32[]{:S(2)}) collective-permute-start(bf16[64,768]{1,0:T(8,128)(2,1)} %param.3), channel_id=1, source_target_pairs={{0,8},{1,9},{2,10},{3,11},{4,12},{5,13},{6,14},{7,15},{8,0},{9,1},... | collective-permute-start | bytes 294920 | tf_op jit(solution)/shard_map/ppermute | solution.py:44
  14.4 4.8 %collective-permute-start.3 = (bf16[64,768]{1,0:T(8,128)(2,1)}, bf16[64,768]{1,0:T(8,128)(2,1)S(1)}, u32[]{:S(2)}, u32[]{:S(2)}) collective-permute-start(bf16[64,768]{1,0:T(8,128)(2,1)} %param.3), channel_id=1, source_target_pairs={{0,16},{1,17},{2,18},{3,19},{4,20},{5,21},{6,22},{7,23},{8,24},{9,... | collective-permute-start | bytes 294920 | tf_op jit(solution)/shard_map/ppermute | solution.py:44
  19.2 6.4 %collective-permute-start.4 = (bf16[64,768]{1,0:T(8,128)(2,1)}, bf16[64,768]{1,0:T(8,128)(2,1)S(1)}, u32[]{:S(2)}, u32[]{:S(2)}) collective-permute-start(bf16[64,768]{1,0:T(8,128)(2,1)} %param.3), channel_id=1, source_target_pairs={{0,1},{1,0},{2,3},{3,2},{4,5},{5,4},{6,7},{7,6},{8,9},{9,8},{10,11... | collective-permute-start | bytes 294920 | tf_op jit(solution)/shard_map/ppermute | solution.py:44
  19.6 6.0 %collective-permute-start.5 = (bf16[64,768]{1,0:T(8,128)(2,1)}, bf16[64,768]{1,0:T(8,128)(2,1)S(1)}, u32[]{:S(2)}, u32[]{:S(2)}) collective-permute-start(bf16[64,768]{1,0:T(8,128)(2,1)} %param.3), channel_id=1, source_target_pairs={{0,2},{1,3},{2,0},{3,1},{4,6},{5,7},{6,4},{7,5},{8,10},{9,11},{10,... | collective-permute-start | bytes 294920 | tf_op jit(solution)/shard_map/ppermute | solution.py:44
  19.9 5.7 %collective-permute-start.14 = (bf16[64,1536]{1,0:T(8,128)(2,1)S(1)}, bf16[64,1536]{1,0:T(8,128)(2,1)S(1)}, u32[]{:S(2)}, u32[]{:S(2)}) collective-permute-start(bf16[64,1536]{1,0:T(8,128)(2,1)S(1)} %collective-permute-done.7), channel_id=1, source_target_pairs={{0,16},{1,17},{2,18},{3,19},{4,20},{5,21},{6,22},{7,23},{8,24},{9,... | collective-permute-start | bytes 589832 | tf_op jit(solution)/shard_map/ppermute | solution.py:44
  22.5 3.2 %collective-permute-start.8 = (bf16[192,1536]{1,0:T(8,128)(2,1)S(1)}, bf16[192,1536]{1,0:T(8,128)(2,1)S(1)}, u32[]{:S(2)}, u32[]{:S(2)}) collective-permute-start(bf16[192,1536]{1,0:T(8,128)(2,1)S(1)} %pad_maximum_fusion), channel_id=1, source_target_pairs={{0,4},{1,5},{2,6},{3,7},{4,0},{5,1},{6,2},{7,3},{8,12},{9,13},{10,... | collective-permute-start | bytes 1769480 | tf_op jit(solution)/shard_map/ppermute | solution.py:44
  22.5 7.3 %collective-permute-start.13 = (bf16[64,1536]{1,0:T(8,128)(2,1)S(1)}, bf16[64,1536]{1,0:T(8,128)(2,1)S(1)}, u32[]{:S(2)}, u32[]{:S(2)}) collective-permute-start(bf16[64,1536]{1,0:T(8,128)(2,1)S(1)} %collective-permute-done.6), channel_id=1, source_target_pairs={{0,8},{1,9},{2,10},{3,11},{4,12},{5,13},{6,14},{7,15},{8,0},{9,1},... | collective-permute-start | bytes 589832 | tf_op jit(solution)/shard_map/ppermute | solution.py:44
  24.1 5.7 %copy-start = (bf16[64,1536]{1,0:T(8,128)(2,1)S(1)}, bf16[64,1536]{1,0:T(8,128)(2,1)}, u32[]{:S(2)}) copy-start(bf16[64,1536]{1,0:T(8,128)(2,1)} %param.2) | copy-start | bytes 589828
  25.6 3.5 %collective-permute-start.15 = (bf16[64,1536]{1,0:T(8,128)(2,1)S(1)}, bf16[64,1536]{1,0:T(8,128)(2,1)S(1)}, u32[]{:S(2)}, u32[]{:S(2)}) collective-permute-start(bf16[64,1536]{1,0:T(8,128)(2,1)S(1)} %collective-permute-done.14), channel_id=1, source_target_pairs={{0,4},{1,5},{2,6},{3,7},{4,0},{5,1},{6,2},{7,3},{8,12},{9,13},{10,... | collective-permute-start | bytes 589832 | tf_op jit(solution)/shard_map/ppermute | solution.py:44
  25.7 5.3 %collective-permute-start.10 = (bf16[64,768]{1,0:T(8,128)(2,1)S(1)}, bf16[64,768]{1,0:T(8,128)(2,1)S(1)}, u32[]{:S(2)}, u32[]{:S(2)}) collective-permute-start(bf16[64,768]{1,0:T(8,128)(2,1)S(1)} %collective-permute-done.5), channel_id=1, source_target_pairs={{0,16},{1,17},{2,18},{3,19},{4,20},{5,21},{6,22},{7,23},{8,24},{9,... | collective-permute-start | bytes 294920 | tf_op jit(solution)/shard_map/ppermute | solution.py:44
  27.3 3.6 %collective-permute-start.11 = (bf16[192,768]{1,0:T(8,128)(2,1)S(1)}, bf16[192,768]{1,0:T(8,128)(2,1)S(1)}, u32[]{:S(2)}, u32[]{:S(2)}) collective-permute-start(bf16[192,768]{1,0:T(8,128)(2,1)S(1)} %pad_maximum_fusion.1), channel_id=1, source_target_pairs={{0,4},{1,5},{2,6},{3,7},{4,0},{5,1},{6,2},{7,3},{8,12},{9,13},{10,... | collective-permute-start | bytes 884744 | tf_op jit(solution)/shard_map/ppermute | solution.py:44
  27.6 5.0 %collective-permute-start.9 = (bf16[64,768]{1,0:T(8,128)(2,1)S(1)}, bf16[64,768]{1,0:T(8,128)(2,1)S(1)}, u32[]{:S(2)}, u32[]{:S(2)}) collective-permute-start(bf16[64,768]{1,0:T(8,128)(2,1)S(1)} %collective-permute-done.4), channel_id=1, source_target_pairs={{0,8},{1,9},{2,10},{3,11},{4,12},{5,13},{6,14},{7,15},{8,0},{9,1},... | collective-permute-start | bytes 294920 | tf_op jit(solution)/shard_map/ppermute | solution.py:44
  30.9 1.3 %collective-permute-start.12 = (bf16[64,768]{1,0:T(8,128)(2,1)S(1)}, bf16[64,768]{1,0:T(8,128)(2,1)S(1)}, u32[]{:S(2)}, u32[]{:S(2)}) collective-permute-start(bf16[64,768]{1,0:T(8,128)(2,1)S(1)} %collective-permute-done.10), channel_id=1, source_target_pairs={{0,4},{1,5},{2,6},{3,7},{4,0},{5,1},{6,2},{7,3},{8,12},{9,13},{10,... | collective-permute-start | bytes 294920 | tf_op jit(solution)/shard_map/ppermute | solution.py:44
  33.4 8.1 %collective-permute-start.16 = (f32[3,8,64]{2,1,0:T(8,128)S(1)}, f32[3,8,64]{2,1,0:T(8,128)S(1)}, u32[]{:S(2)}, u32[]{:S(2)}) collective-permute-start(f32[3,8,64]{2,1,0:T(8,128)S(1)} %constant_dynamic-update-slice_fusion.12), channel_id=1, source_target_pairs={{0,2},{1,3},{2,0},{3,1},{4,6},{5,7},{6,4},{7,5},{8,10},{9,11},{10,... | collective-permute-start | bytes 18440 | tf_op jit(solution)/shard_map/ppermute | solution.py:44
  36.3 3.6 %collective-permute-start.19 = (f32[3,4,64]{2,1,0:T(4,128)S(1)}, f32[3,4,64]{2,1,0:T(4,128)S(1)}, u32[]{:S(2)}, u32[]{:S(2)}) collective-permute-start(f32[3,4,64]{2,1,0:T(4,128)S(1)} %constant_dynamic-update-slice_fusion.15), channel_id=1, source_target_pairs={{0,1},{1,0},{2,3},{3,2},{4,5},{5,4},{6,7},{7,6},{8,9},{9,8},{10,11... | collective-permute-start | bytes 9224 | tf_op jit(solution)/shard_map/ppermute | solution.py:44
  39.9 3.7 %collective-permute-start.20 = (f32[3,4,64]{2,1,0:T(4,128)S(1)}, f32[3,4,64]{2,1,0:T(4,128)S(1)}, u32[]{:S(2)}, u32[]{:S(2)}) collective-permute-start(f32[3,4,64]{2,1,0:T(4,128)S(1)} %add.106), channel_id=1, source_target_pairs={{0,8},{1,9},{2,10},{3,11},{4,12},{5,13},{6,14},{7,15},{8,0},{9,1},... | collective-permute-start | bytes 9224 | tf_op jit(solution)/shard_map/ppermute | solution.py:44
  41.5 3.8 %collective-permute-start.17 = (f32[3,8,64]{2,1,0:T(8,128)S(1)}, f32[3,8,64]{2,1,0:T(8,128)S(1)}, u32[]{:S(2)}, u32[]{:S(2)}) collective-permute-start(f32[3,8,64]{2,1,0:T(8,128)S(1)} %add.100), channel_id=1, source_target_pairs={{0,16},{1,17},{2,18},{3,19},{4,20},{5,21},{6,22},{7,23},{8,24},{9,... | collective-permute-start | bytes 18440 | tf_op jit(solution)/shard_map/ppermute | solution.py:44
  45.3 1.2 %collective-permute-start.18 = (f32[3,8,64]{2,1,0:T(8,128)S(1)}, f32[3,8,64]{2,1,0:T(8,128)S(1)}, u32[]{:S(2)}, u32[]{:S(2)}) collective-permute-start(f32[3,8,64]{2,1,0:T(8,128)S(1)} %add.101), channel_id=1, source_target_pairs={{0,4},{1,5},{2,6},{3,7},{4,0},{5,1},{6,2},{7,3},{8,12},{9,13},{10,... | collective-permute-start | bytes 18440 | tf_op jit(solution)/shard_map/ppermute | solution.py:44
  48.3 7.0 %collective-permute-start.21 = (f32[64,768]{1,0:T(8,128)S(1)}, f32[64,768]{1,0:T(8,128)S(1)}, u32[]{:S(2)}, u32[]{:S(2)}) collective-permute-start(f32[64,768]{1,0:T(8,128)S(1)} %get-tuple-element.24), channel_id=1, source_target_pairs={{0,8},{1,9},{2,10},{3,11},{4,12},{5,13},{6,14},{7,15},{8,0},{9,1},... | collective-permute-start | bytes 589832 | tf_op jit(solution)/shard_map/ppermute | solution.py:44
  48.9 10.6 %collective-permute-start.25 = (f32[64,768]{1,0:T(8,128)S(1)}, f32[64,768]{1,0:T(8,128)S(1)}, u32[]{:S(2)}, u32[]{:S(2)}) collective-permute-start(f32[64,768]{1,0:T(8,128)S(1)} %get-tuple-element.23), channel_id=1, source_target_pairs={{0,1},{1,0},{2,3},{3,2},{4,5},{5,4},{6,7},{7,6},{8,9},{9,8},{10,11... | collective-permute-start | bytes 589832 | tf_op jit(solution)/shard_map/ppermute | solution.py:44
  50.7 10.1 %collective-permute-start.26 = (f32[64,768]{1,0:T(8,128)S(1)}, f32[64,768]{1,0:T(8,128)S(1)}, u32[]{:S(2)}, u32[]{:S(2)}) collective-permute-start(f32[64,768]{1,0:T(8,128)S(1)} %get-tuple-element.22), channel_id=1, source_target_pairs={{0,9},{1,8},{2,11},{3,10},{4,13},{5,12},{6,15},{7,14},{8,1},{9,0},... | collective-permute-start | bytes 589832 | tf_op jit(solution)/shard_map/ppermute | solution.py:44
  56.0 5.6 %collective-permute-start.23 = (f32[1,128]{1,0:T(1,128)S(1)}, f32[1,128]{1,0:T(1,128)S(1)}, u32[]{:S(2)}, u32[]{:S(2)}) collective-permute-start(f32[1,128]{1,0:T(1,128)S(1)} %broadcast_in_dim.2), channel_id=1, source_target_pairs={{0,8},{1,9},{2,10},{3,11},{4,12},{5,13},{6,14},{7,15},{8,0},{9,1},... | collective-permute-start | bytes 1544 | tf_op jit(solution)/shard_map/ppermute | solution.py:44
  56.6 5.0 %collective-permute-start.24 = (f32[1,128]{1,0:T(1,128)S(1)}, f32[1,128]{1,0:T(1,128)S(1)}, u32[]{:S(2)}, u32[]{:S(2)}) collective-permute-start(f32[1,128]{1,0:T(1,128)S(1)} %broadcast_in_dim.2), channel_id=1, source_target_pairs={{0,9},{1,8},{2,11},{3,10},{4,13},{5,12},{6,15},{7,14},{8,1},{9,0},... | collective-permute-start | bytes 1544 | tf_op jit(solution)/shard_map/ppermute | solution.py:44
  59.4 3.5 %collective-permute-start.22 = (f32[1,128]{1,0:T(1,128)S(1)}, f32[1,128]{1,0:T(1,128)S(1)}, u32[]{:S(2)}, u32[]{:S(2)}) collective-permute-start(f32[1,128]{1,0:T(1,128)S(1)} %broadcast_in_dim.2), channel_id=1, source_target_pairs={{0,1},{1,0},{2,3},{3,2},{4,5},{5,4},{6,7},{7,6},{8,9},{9,8},{10,11... | collective-permute-start | bytes 1544 | tf_op jit(solution)/shard_map/ppermute | solution.py:44

commit v5 on v4

--- a/solution.py
+++ b/solution.py
@@ -60,20 +60,19 @@
     row_t, col_t = {0: teacher}, {0: teacher}
     row_s, col_s = {0: student}, {0: student}
     core_t, core_s = [], []
-    sides = ((row_t, row_s, row_masks), (col_t, col_s, plane_masks))
-    for side_t, _, masks in sides:
-        for b, mask in enumerate(masks):
-            side_t[1 << b] = send(teacher, mask, count)
-    late = after(student, (row_t[2], col_t[2]))
-    for _, side_s, masks in sides:
+    width = teacher.shape[1]
+    both = jnp.concatenate([teacher, student], 1)
+    row_t[1], col_t[1] = send(teacher, row_masks[0], count), send(teacher, plane_masks[0], count)
+    for side_t, side_s, masks in ((row_t, row_s, row_masks), (col_t, col_s, plane_masks)):
         for b, mask in enumerate(masks):
             if b:
-                side_s[1 << b] = send(late, mask, count)
-    late = after(student, (row_s[2], col_s[2]))
-    for _, side_s, masks in sides:
-        side_s[1] = send(late, masks[0], count)
+                got = send(both, mask, count)
+                side_t[1 << b], side_s[1 << b] = got[:, :width], got[:, width:]
+    col_s[1] = send(student, plane_masks[0], count)
+    row_t[1], col_t[1], late = lax.optimization_barrier((row_t[1], col_t[1], student))
+    row_s[1] = send(late, row_masks[0], count)
+    early = (row_t[2], col_t[2], row_s[2], col_s[2])
 
-    early = (row_s[2], col_s[2])
     for row, col, core in ((row_t, col_t, core_t), (row_s, col_s, core_s)):
         row[1], col[1] = after((row[1], col[1]), early)
         for level in range(1, len(row_masks) + 1):
@@ -85,7 +84,7 @@
                 got = send(jnp.concatenate([col[p] for p in ready]), core_mask, count)
                 core += zip(ready, jnp.split(got, len(ready)))
                 if level == 1:
-                    early = (early, got)
+                    early = got
     out = []
     for row, col, core in ((row_t, col_t, core_t), (row_s, col_s, core_s)):
         col = [col[p] for p in sorted(col)] + [piece for _, piece in sorted(core, key=lambda c: c[0])]
@@ -99,13 +98,10 @@
     return values[0]
 
 
-def group_sum(parts, masks, count):
-    for place, mask in enumerate(masks):
-        got = send(parts, mask, count)
-        shape = (3, -1, 2, 1 << place, got.shape[-1])
-        got = jnp.flip(got.reshape(shape), 2).reshape(parts.shape)
-        parts = parts + got
-    return parts
+def add_partner(parts, masks, place, count):
+    got = send(parts, masks[place], count)
+    shape = (3, -1, 2, 1 << place, got.shape[-1])
+    return parts + jnp.flip(got.reshape(shape), 2).reshape(parts.shape)
 
 
 def per_device(teacher, student):
@@ -124,8 +120,13 @@
     products = (gram_s * gram_s, gram_t * gram_t, gram_s * gram_t)
     row_part = jnp.stack([jnp.sum(p, 1) for p in products]).reshape(3, n_row, rows)
     col_part = jnp.stack([jnp.sum(p, 0) for p in products]).reshape(3, n_col, rows)
-    row_sum = group_sum(row_part, row_masks, count).reshape(3, -1)
-    col_sum = group_sum(col_part, col_masks, count).reshape(3, -1)
+    for place in range(max(len(row_masks), len(col_masks))):
+        if place < len(col_masks):
+            col_part = add_partner(col_part, col_masks, place, count)
+        if place < len(row_masks):
+            row_part = add_partner(row_part, row_masks, place, count)
+            row_part, col_part = lax.optimization_barrier((row_part, col_part))
+    row_sum, col_sum = row_part.reshape(3, -1), col_part.reshape(3, -1)
 
     row_alpha, row_beta, _ = coefficients(*row_sum, total)
     col_alpha, col_beta, terms = coefficients(*col_sum, total)

time: 64.3 us -> 65.7 us (1.022)
  waiting for transfers between devices: 21.3 us -> 32.9 us
  starting transfers between devices: 32.5 us -> 23.2 us
  other arithmetic: 2.41 us -> 1.48 us
    ppermute x27 -> x25, waiting for transfers between devices: 21.3 us -> 32.9 us  [send(): return lax.ppermute(value, AXES, [(i, i ^ mask) for i in range(count)])]
    ppermute x27 -> x25, starting transfers between devices: 32.5 us -> 23.2 us  [send(): return lax.ppermute(value, AXES, [(i, i ^ mask) for i in range(count)])]
    concatenate x2, other arithmetic: 0.98 us -> 0.06 us  [gather(): got = send(jnp.concatenate([col[p] for p in ready]), core_mask, count)]
    concatenate x0 -> x1, local copies, waits for them, and re-layouts: none -> 0.91 us  [gather(): both = jnp.concatenate([teacher, student], 1)]
    unnamed x18 -> x19, local copies, waits for them, and re-layouts: 2.07 us -> 1.18 us
  transfers between devices with their start and end apart: 27 -> 25, of which waited for: 16 -> 11; matrix products, arithmetic and copies ran while one was open for 9% -> 4% of each run, Pallas kernels for 0% -> 0%
where the time goes in v5:
time: 65.7 us; the launch traced here: 65.5 us
  waiting for transfers between devices  32.9 us (50%)
  starting transfers between devices  23.2 us (35%)
  local copies, waits for them, and re-layouts  3.86 us (6%)
  between operations  2.13 us (3%)
  matrix products  1.95 us (3%)
  other arithmetic  1.48 us (2%)
    ppermute x25, waiting for transfers between devices, send(): return lax.ppermute(value, AXES, [(i, i ^ mask) for i in range(count)])  32.9 us
    ppermute x25, starting transfers between devices, send(): return lax.ppermute(value, AXES, [(i, i ^ mask) for i in range(count)])  23.2 us
  transfers between devices with their start and end apart: 25, of which 11 were waited for; matrix products, arithmetic and copies ran while one was open for 4% of the time, Pallas kernels for 0%

profile of v5, /device:TPU:0, one launch (start us, length us, event | category | flops | bytes accessed | tf_op | source)
XLA Modules:
  0.0 65.5 jit_solution(12094564368077719786)
XLA Ops:
  0.6 1.0 %constant_dynamic-update-slice_fusion.13 = (bf16[512,1536]{1,0:T(8,128)(2,1)S(1)}, bf16[64,2304]{1,0:T(8,128)(2,1)S(1)}) fusion(bf16[64,1536]{1,0:T(8,128)(2,1)} %param.2), kind=kLoop, calls=%fused_computation.47 | loop fusion | bytes 589824
  1.7 0.9 %constant_dynamic-update-slice_fusion = (bf16[64,2304]{1,0:T(8,128)(2,1)S(1)}, bf16[512,768]{1,0:T(8,128)(2,1)S(1)}) fusion(bf16[64,2304]{1,0:T(8,128)(2,1)S(1)} %get-tuple-element.36, bf16[64,768]{1,0:T(8,128)(2,1)} %param.3), kind=kLoop, calls=%fused_computation.34 | loop fusion | bytes 294912 | tf_op jit(solution)/shard_map/concatenate | solution.py:64
  2.6 3.0 %collective-permute-start.5 = (bf16[64,2304]{1,0:T(8,128)(2,1)S(1)}, bf16[64,2304]{1,0:T(8,128)(2,1)S(1)}, u32[]{:S(2)}, u32[]{:S(2)}) collective-permute-start(bf16[64,2304]{1,0:T(8,128)(2,1)S(1)} %get-tuple-element.37), channel_id=1, source_target_pairs={{0,16},{1,17},{2,18},{3,19},{4,20},{5,21},{6,22},{7,23},{8,24},{9,... | collective-permute-start | bytes 884744 | tf_op jit(solution)/shard_map/ppermute | solution.py:44
  5.6 1.5 %collective-permute-start.4 = (bf16[64,2304]{1,0:T(8,128)(2,1)S(1)}, bf16[64,2304]{1,0:T(8,128)(2,1)S(1)}, u32[]{:S(2)}, u32[]{:S(2)}) collective-permute-start(bf16[64,2304]{1,0:T(8,128)(2,1)S(1)} %get-tuple-element.37), channel_id=1, source_target_pairs={{0,8},{1,9},{2,10},{3,11},{4,12},{5,13},{6,14},{7,15},{8,0},{9,1},... | collective-permute-start | bytes 884744 | tf_op jit(solution)/shard_map/ppermute | solution.py:44
  7.1 1.6 %collective-permute-start = (bf16[64,1536]{1,0:T(8,128)(2,1)}, bf16[64,1536]{1,0:T(8,128)(2,1)S(1)}, u32[]{:S(2)}, u32[]{:S(2)}) collective-permute-start(bf16[64,1536]{1,0:T(8,128)(2,1)} %param.2), channel_id=1, source_target_pairs={{0,1},{1,0},{2,3},{3,2},{4,5},{5,4},{6,7},{7,6},{8,9},{9,8},{10,11... | collective-permute-start | bytes 589832 | tf_op jit(solution)/shard_map/ppermute | solution.py:44
  8.7 2.6 %collective-permute-start.1 = (bf16[64,1536]{1,0:T(8,128)(2,1)}, bf16[64,1536]{1,0:T(8,128)(2,1)S(1)}, u32[]{:S(2)}, u32[]{:S(2)}) collective-permute-start(bf16[64,1536]{1,0:T(8,128)(2,1)} %param.2), channel_id=1, source_target_pairs={{0,2},{1,3},{2,0},{3,1},{4,6},{5,7},{6,4},{7,5},{8,10},{9,11},{10,... | collective-permute-start | bytes 589832 | tf_op jit(solution)/shard_map/ppermute | solution.py:44
  11.6 5.9 %collective-permute-done = bf16[64,1536]{1,0:T(8,128)(2,1)S(1)} collective-permute-done((bf16[64,1536]{1,0:T(8,128)(2,1)}, bf16[64,1536]{1,0:T(8,128)(2,1)S(1)}, u32[]{:S(2)}, u32[]{:S(2)}) %collective-permute-start) | collective-permute-done | bytes 196640 | tf_op jit(solution)/shard_map/ppermute | solution.py:44
  17.5 5.6 %collective-permute-done.1 = bf16[64,1536]{1,0:T(8,128)(2,1)S(1)} collective-permute-done((bf16[64,1536]{1,0:T(8,128)(2,1)}, bf16[64,1536]{1,0:T(8,128)(2,1)S(1)}, u32[]{:S(2)}, u32[]{:S(2)}) %collective-permute-start.1) | collective-permute-done | bytes 196640 | tf_op jit(solution)/shard_map/ppermute | solution.py:44
  23.2 0.6 collective-permute-start.12
  23.7 0.6 collective-permute-start.11
  24.4 4.5 %collective-permute-done.12 = bf16[64,1536]{1,0:T(8,128)(2,1)S(1)} collective-permute-done((bf16[64,1536]{1,0:T(8,128)(2,1)S(1)}, bf16[64,1536]{1,0:T(8,128)(2,1)S(1)}, u32[]{:S(2)}, u32[]{:S(2)}) %collective-permute-start.12) | collective-permute-done | bytes 196640 | tf_op jit(solution)/shard_map/ppermute | solution.py:44
  28.9 0.6 collective-permute-start.8
  30.5 0.6 collective-permute-done.11
  31.1 0.6 fusion
  31.8 2.5 %collective-permute-done.8 = bf16[64,768]{1,0:T(8,128)(2,1)S(1)} collective-permute-done((bf16[64,768]{1,0:T(8,128)(2,1)S(1)}, bf16[64,768]{1,0:T(8,128)(2,1)S(1)}, u32[]{:S(2)}, u32[]{:S(2)}) %collective-permute-start.8) | collective-permute-done | bytes 98336 | tf_op jit(solution)/shard_map/ppermute | solution.py:44
  34.3 1.2 %collective-permute-done.10 = bf16[64,768]{1,0:T(8,128)(2,1)S(1)} collective-permute-done((bf16[64,768]{1,0:T(8,128)(2,1)S(1)}, bf16[64,768]{1,0:T(8,128)(2,1)S(1)}, u32[]{:S(2)}, u32[]{:S(2)}) %collective-permute-start.10) | collective-permute-done | bytes 98336 | tf_op jit(solution)/shard_map/ppermute | solution.py:44
  35.5 0.6 multiply_reduce_fusion.4
  36.3 3.0 %collective-permute-start.15 = (f32[3,8,64]{2,1,0:T(8,128)S(1)}, f32[3,8,64]{2,1,0:T(8,128)S(1)}, u32[]{:S(2)}, u32[]{:S(2)}) collective-permute-start(f32[3,8,64]{2,1,0:T(8,128)S(1)} %constant_dynamic-update-slice_fusion.17), channel_id=1, source_target_pairs={{0,2},{1,3},{2,0},{3,1},{4,6},{5,7},{6,4},{7,5},{8,10},{9,11},{10,... | collective-permute-start | bytes 18440 | tf_op jit(solution)/shard_map/ppermute | solution.py:44
  39.7 3.6 %collective-permute-done.14 = f32[3,4,64]{2,1,0:T(4,128)S(1)} collective-permute-done((f32[3,4,64]{2,1,0:T(4,128)S(1)}, f32[3,4,64]{2,1,0:T(4,128)S(1)}, u32[]{:S(2)}, u32[]{:S(2)}) %collective-permute-start.14) | collective-permute-done | bytes 3104 | tf_op jit(solution)/shard_map/ppermute | solution.py:44
  43.4 0.9 %collective-permute-start.17 = (f32[3,8,64]{2,1,0:T(8,128)S(1)}, f32[3,8,64]{2,1,0:T(8,128)S(1)}, u32[]{:S(2)}, u32[]{:S(2)}) collective-permute-start(f32[3,8,64]{2,1,0:T(8,128)S(1)} %add.101), channel_id=1, source_target_pairs={{0,16},{1,17},{2,18},{3,19},{4,20},{5,21},{6,22},{7,23},{8,24},{9,... | collective-permute-start | bytes 18440 | tf_op jit(solution)/shard_map/ppermute | solution.py:44
  44.3 0.5 collective-permute-start.16
  44.8 3.1 %collective-permute-done.16 = f32[3,4,64]{2,1,0:T(4,128)S(1)} collective-permute-done((f32[3,4,64]{2,1,0:T(4,128)S(1)}, f32[3,4,64]{2,1,0:T(4,128)S(1)}, u32[]{:S(2)}, u32[]{:S(2)}) %collective-permute-start.16) | collective-permute-done | bytes 3104 | tf_op jit(solution)/shard_map/ppermute | solution.py:44
  48.2 1.2 %collective-permute-done.18 = f32[3,8,64]{2,1,0:T(8,128)S(1)} collective-permute-done((f32[3,8,64]{2,1,0:T(8,128)S(1)}, f32[3,8,64]{2,1,0:T(8,128)S(1)}, u32[]{:S(2)}, u32[]{:S(2)}) %collective-permute-start.18) | collective-permute-done | bytes 6176 | tf_op jit(solution)/shard_map/ppermute | solution.py:44
  49.4 0.6 rsqrt_multiply_fusion
  51.1 0.6 collective-permute-start.19
  51.7 2.9 %collective-permute-start.24 = (f32[64,768]{1,0:T(8,128)S(1)}, f32[64,768]{1,0:T(8,128)S(1)}, u32[]{:S(2)}, u32[]{:S(2)}) collective-permute-start(f32[64,768]{1,0:T(8,128)S(1)} %get-tuple-element.32), channel_id=1, source_target_pairs={{0,9},{1,8},{2,11},{3,10},{4,13},{5,12},{6,15},{7,14},{8,1},{9,0},... | collective-permute-start | bytes 589832 | tf_op jit(solution)/shard_map/ppermute | solution.py:44
  54.7 3.5 %collective-permute-done.19 = f32[64,768]{1,0:T(8,128)S(1)} collective-permute-done((f32[64,768]{1,0:T(8,128)S(1)}, f32[64,768]{1,0:T(8,128)S(1)}, u32[]{:S(2)}, u32[]{:S(2)}) %collective-permute-start.19) | collective-permute-done | bytes 196640 | tf_op jit(solution)/shard_map/ppermute | solution.py:44
  58.1 0.6 broadcast_in_dim.2
  58.9 0.6 collective-permute-start.21
  59.5 2.9 %collective-permute-start.22 = (f32[1,128]{1,0:T(1,128)S(1)}, f32[1,128]{1,0:T(1,128)S(1)}, u32[]{:S(2)}, u32[]{:S(2)}) collective-permute-start(f32[1,128]{1,0:T(1,128)S(1)} %broadcast_in_dim.2), channel_id=1, source_target_pairs={{0,9},{1,8},{2,11},{3,10},{4,13},{5,12},{6,15},{7,14},{8,1},{9,0},... | collective-permute-start | bytes 1544 | tf_op jit(solution)/shard_map/ppermute | solution.py:44
  62.4 1.2 %collective-permute-done.24 = f32[64,768]{1,0:T(8,128)S(1)} collective-permute-done((f32[64,768]{1,0:T(8,128)S(1)}, f32[64,768]{1,0:T(8,128)S(1)}, u32[]{:S(2)}, u32[]{:S(2)}) %collective-permute-start.24) | collective-permute-done | bytes 196640 | tf_op jit(solution)/shard_map/ppermute | solution.py:44
  63.6 0.7 %fusion.21 = f32[64,768]{1,0:T(8,128)} fusion(f32[64,768]{1,0:T(8,128)S(1)} %collective-permute-done.23, f32[256,768]{1,0:T(8,128)S(1)} %convolution_add_fusion, f32[64,768]{1,0:T(8,128)S(1)} %collective-permute-done.19, f32[64,768]{1,0:T(8,128)S(1)} %collective-permute-done.24), kind=kLoop, calls=%fused_computation.33 | loop fusion | flops 147456 | bytes 983040 | tf_op jit(solution)/shard_map/add | solution.py:97
  (84 shorter events, 3.5 us)
Async XLA Ops:
  0.6 22.5 %copy-start = (bf16[64,1536]{1,0:T(8,128)(2,1)S(1)}, bf16[64,1536]{1,0:T(8,128)(2,1)}, u32[]{:S(2)}) copy-start(bf16[64,1536]{1,0:T(8,128)(2,1)} %param.2) | copy-start | bytes 589828
  2.6 20.5 %collective-permute-start.5 = (bf16[64,2304]{1,0:T(8,128)(2,1)S(1)}, bf16[64,2304]{1,0:T(8,128)(2,1)S(1)}, u32[]{:S(2)}, u32[]{:S(2)}) collective-permute-start(bf16[64,2304]{1,0:T(8,128)(2,1)S(1)} %get-tuple-element.37), channel_id=1, source_target_pairs={{0,16},{1,17},{2,18},{3,19},{4,20},{5,21},{6,22},{7,23},{8,24},{9,... | collective-permute-start | bytes 884744 | tf_op jit(solution)/shard_map/ppermute | solution.py:44
  5.6 17.5 %collective-permute-start.4 = (bf16[64,2304]{1,0:T(8,128)(2,1)S(1)}, bf16[64,2304]{1,0:T(8,128)(2,1)S(1)}, u32[]{:S(2)}, u32[]{:S(2)}) collective-permute-start(bf16[64,2304]{1,0:T(8,128)(2,1)S(1)} %get-tuple-element.37), channel_id=1, source_target_pairs={{0,8},{1,9},{2,10},{3,11},{4,12},{5,13},{6,14},{7,15},{8,0},{9,1},... | collective-permute-start | bytes 884744 | tf_op jit(solution)/shard_map/ppermute | solution.py:44
  7.1 10.4 %collective-permute-start = (bf16[64,1536]{1,0:T(8,128)(2,1)}, bf16[64,1536]{1,0:T(8,128)(2,1)S(1)}, u32[]{:S(2)}, u32[]{:S(2)}) collective-permute-start(bf16[64,1536]{1,0:T(8,128)(2,1)} %param.2), channel_id=1, source_target_pairs={{0,1},{1,0},{2,3},{3,2},{4,5},{5,4},{6,7},{7,6},{8,9},{9,8},{10,11... | collective-permute-start | bytes 589832 | tf_op jit(solution)/shard_map/ppermute | solution.py:44
  8.7 14.3 %collective-permute-start.1 = (bf16[64,1536]{1,0:T(8,128)(2,1)}, bf16[64,1536]{1,0:T(8,128)(2,1)S(1)}, u32[]{:S(2)}, u32[]{:S(2)}) collective-permute-start(bf16[64,1536]{1,0:T(8,128)(2,1)} %param.2), channel_id=1, source_target_pairs={{0,2},{1,3},{2,0},{3,1},{4,6},{5,7},{6,4},{7,5},{8,10},{9,11},{10,... | collective-permute-start | bytes 589832 | tf_op jit(solution)/shard_map/ppermute | solution.py:44
  11.3 17.7 %collective-permute-start.3 = (bf16[64,768]{1,0:T(8,128)(2,1)}, bf16[64,768]{1,0:T(8,128)(2,1)S(1)}, u32[]{:S(2)}, u32[]{:S(2)}) collective-permute-start(bf16[64,768]{1,0:T(8,128)(2,1)} %param.3), channel_id=1, source_target_pairs={{0,2},{1,3},{2,0},{3,1},{4,6},{5,7},{6,4},{7,5},{8,10},{9,11},{10,... | collective-permute-start | bytes 294920 | tf_op jit(solution)/shard_map/ppermute | solution.py:44
  23.0 5.9 %collective-permute-start.2 = (bf16[64,768]{1,0:T(8,128)(2,1)}, bf16[64,768]{1,0:T(8,128)(2,1)S(1)}, u32[]{:S(2)}, u32[]{:S(2)}) collective-permute-start(bf16[64,768]{1,0:T(8,128)(2,1)} %param.3), channel_id=1, source_target_pairs={{0,1},{1,0},{2,3},{3,2},{4,5},{5,4},{6,7},{7,6},{8,9},{9,8},{10,11... | collective-permute-start | bytes 294920 | tf_op jit(solution)/shard_map/ppermute | solution.py:44
  23.0 6.5 %copy-start.1 = (bf16[64,768]{1,0:T(8,128)(2,1)S(1)}, bf16[64,768]{1,0:T(8,128)(2,1)}, u32[]{:S(2)}) copy-start(bf16[64,768]{1,0:T(8,128)(2,1)} %param.3) | copy-start | bytes 294916
  23.1 6.5 %copy-start.2 = (bf16[64,2304]{1,0:T(8,128)(2,1)}, bf16[64,2304]{1,0:T(8,128)(2,1)S(1)}, u32[]{:S(2)}) copy-start(bf16[64,2304]{1,0:T(8,128)(2,1)S(1)} %collective-permute-done.4) | copy-start | bytes 884740
  23.2 5.7 %collective-permute-start.12 = (bf16[64,1536]{1,0:T(8,128)(2,1)S(1)}, bf16[64,1536]{1,0:T(8,128)(2,1)S(1)}, u32[]{:S(2)}, u32[]{:S(2)}) collective-permute-start(bf16[64,1536]{1,0:T(8,128)(2,1)S(1)} %collective-permute-done.1), channel_id=1, source_target_pairs={{0,16},{1,17},{2,18},{3,19},{4,20},{5,21},{6,22},{7,23},{8,24},{9,... | collective-permute-start | bytes 589832 | tf_op jit(solution)/shard_map/ppermute | solution.py:44
  23.7 5.2 %collective-permute-start.6 = (bf16[192,1536]{1,0:T(8,128)(2,1)S(1)}, bf16[192,1536]{1,0:T(8,128)(2,1)S(1)}, u32[]{:S(2)}, u32[]{:S(2)}) collective-permute-start(bf16[192,1536]{1,0:T(8,128)(2,1)S(1)} %pad_maximum_fusion), channel_id=1, source_target_pairs={{0,4},{1,5},{2,6},{3,7},{4,0},{5,1},{6,2},{7,3},{8,12},{9,13},{10,... | collective-permute-start | bytes 1769480 | tf_op jit(solution)/shard_map/ppermute | solution.py:44
  23.7 7.4 %collective-permute-start.11 = (bf16[64,1536]{1,0:T(8,128)(2,1)S(1)}, bf16[64,1536]{1,0:T(8,128)(2,1)S(1)}, u32[]{:S(2)}, u32[]{:S(2)}) collective-permute-start(bf16[64,1536]{1,0:T(8,128)(2,1)S(1)} %collective-permute-done), channel_id=1, source_target_pairs={{0,8},{1,9},{2,10},{3,11},{4,12},{5,13},{6,14},{7,15},{8,0},{9,1},... | collective-permute-start | bytes 589832 | tf_op jit(solution)/shard_map/ppermute | solution.py:44
  28.9 1.6 %collective-permute-start.13 = (bf16[64,1536]{1,0:T(8,128)(2,1)S(1)}, bf16[64,1536]{1,0:T(8,128)(2,1)S(1)}, u32[]{:S(2)}, u32[]{:S(2)}) collective-permute-start(bf16[64,1536]{1,0:T(8,128)(2,1)S(1)} %collective-permute-done.12), channel_id=1, source_target_pairs={{0,4},{1,5},{2,6},{3,7},{4,0},{5,1},{6,2},{7,3},{8,12},{9,13},{10,... | collective-permute-start | bytes 589832 | tf_op jit(solution)/shard_map/ppermute | solution.py:44
  28.9 5.3 %collective-permute-start.8 = (bf16[64,768]{1,0:T(8,128)(2,1)S(1)}, bf16[64,768]{1,0:T(8,128)(2,1)S(1)}, u32[]{:S(2)}, u32[]{:S(2)}) collective-permute-start(bf16[64,768]{1,0:T(8,128)(2,1)S(1)} %collective-permute-done.3), channel_id=1, source_target_pairs={{0,16},{1,17},{2,18},{3,19},{4,20},{5,21},{6,22},{7,23},{8,24},{9,... | collective-permute-start | bytes 294920 | tf_op jit(solution)/shard_map/ppermute | solution.py:44
  29.6 1.6 %slice-start = ((bf16[64,2304]{1,0:T(8,128)(2,1)}), bf16[64,1536]{1,0:T(8,128)(2,1)S(1)}, s32[]{:S(2)}) async-start(bf16[64,2304]{1,0:T(8,128)(2,1)} %copy-done.2), calls=%async_computation | async-start | bytes 393216 | tf_op jit(solution)/shard_map/slice | solution.py:70
  29.6 4.7 %collective-permute-start.9 = (bf16[192,768]{1,0:T(8,128)(2,1)S(1)}, bf16[192,768]{1,0:T(8,128)(2,1)S(1)}, u32[]{:S(2)}, u32[]{:S(2)}) collective-permute-start(bf16[192,768]{1,0:T(8,128)(2,1)S(1)} %pad_maximum_fusion.1), channel_id=1, source_target_pairs={{0,4},{1,5},{2,6},{3,7},{4,0},{5,1},{6,2},{7,3},{8,12},{9,13},{10,... | collective-permute-start | bytes 884744 | tf_op jit(solution)/shard_map/ppermute | solution.py:44
  29.9 5.7 %collective-permute-start.7 = (bf16[64,768]{1,0:T(8,128)(2,1)S(1)}, bf16[64,768]{1,0:T(8,128)(2,1)S(1)}, u32[]{:S(2)}, u32[]{:S(2)}) collective-permute-start(bf16[64,768]{1,0:T(8,128)(2,1)S(1)} %collective-permute-done.2), channel_id=1, source_target_pairs={{0,8},{1,9},{2,10},{3,11},{4,12},{5,13},{6,14},{7,15},{8,0},{9,1},... | collective-permute-start | bytes 294920 | tf_op jit(solution)/shard_map/ppermute | solution.py:44
  30.5 5.1 %slice-start.1 = ((bf16[64,2304]{1,0:T(8,128)(2,1)}), bf16[64,768]{1,0:T(8,128)(2,1)S(1)}, s32[]{:S(2)}) async-start(bf16[64,2304]{1,0:T(8,128)(2,1)} %copy-done.2), calls=%async_computation.1 | async-start | bytes 196608 | tf_op jit(solution)/shard_map/slice | solution.py:70
  34.2 1.3 %collective-permute-start.10 = (bf16[64,768]{1,0:T(8,128)(2,1)S(1)}, bf16[64,768]{1,0:T(8,128)(2,1)S(1)}, u32[]{:S(2)}, u32[]{:S(2)}) collective-permute-start(bf16[64,768]{1,0:T(8,128)(2,1)S(1)} %collective-permute-done.8), channel_id=1, source_target_pairs={{0,4},{1,5},{2,6},{3,7},{4,0},{5,1},{6,2},{7,3},{8,12},{9,13},{10,... | collective-permute-start | bytes 294920 | tf_op jit(solution)/shard_map/ppermute | solution.py:44
  36.3 7.0 %collective-permute-start.15 = (f32[3,8,64]{2,1,0:T(8,128)S(1)}, f32[3,8,64]{2,1,0:T(8,128)S(1)}, u32[]{:S(2)}, u32[]{:S(2)}) collective-permute-start(f32[3,8,64]{2,1,0:T(8,128)S(1)} %constant_dynamic-update-slice_fusion.17), channel_id=1, source_target_pairs={{0,2},{1,3},{2,0},{3,1},{4,6},{5,7},{6,4},{7,5},{8,10},{9,11},{10,... | collective-permute-start | bytes 18440 | tf_op jit(solution)/shard_map/ppermute | solution.py:44
  39.6 3.6 %collective-permute-start.14 = (f32[3,4,64]{2,1,0:T(4,128)S(1)}, f32[3,4,64]{2,1,0:T(4,128)S(1)}, u32[]{:S(2)}, u32[]{:S(2)}) collective-permute-start(f32[3,4,64]{2,1,0:T(4,128)S(1)} %constant_dynamic-update-slice_fusion.14), channel_id=1, source_target_pairs={{0,1},{1,0},{2,3},{3,2},{4,5},{5,4},{6,7},{7,6},{8,9},{9,8},{10,11... | collective-permute-start | bytes 9224 | tf_op jit(solution)/shard_map/ppermute | solution.py:44
  43.4 4.5 %collective-permute-start.17 = (f32[3,8,64]{2,1,0:T(8,128)S(1)}, f32[3,8,64]{2,1,0:T(8,128)S(1)}, u32[]{:S(2)}, u32[]{:S(2)}) collective-permute-start(f32[3,8,64]{2,1,0:T(8,128)S(1)} %add.101), channel_id=1, source_target_pairs={{0,16},{1,17},{2,18},{3,19},{4,20},{5,21},{6,22},{7,23},{8,24},{9,... | collective-permute-start | bytes 18440 | tf_op jit(solution)/shard_map/ppermute | solution.py:44
  44.3 3.6 %collective-permute-start.16 = (f32[3,4,64]{2,1,0:T(4,128)S(1)}, f32[3,4,64]{2,1,0:T(4,128)S(1)}, u32[]{:S(2)}, u32[]{:S(2)}) collective-permute-start(f32[3,4,64]{2,1,0:T(4,128)S(1)} %add.100), channel_id=1, source_target_pairs={{0,8},{1,9},{2,10},{3,11},{4,12},{5,13},{6,14},{7,15},{8,0},{9,1},... | collective-permute-start | bytes 9224 | tf_op jit(solution)/shard_map/ppermute | solution.py:44
  48.2 1.2 %collective-permute-start.18 = (f32[3,8,64]{2,1,0:T(8,128)S(1)}, f32[3,8,64]{2,1,0:T(8,128)S(1)}, u32[]{:S(2)}, u32[]{:S(2)}) collective-permute-start(f32[3,8,64]{2,1,0:T(8,128)S(1)} %add.103), channel_id=1, source_target_pairs={{0,4},{1,5},{2,6},{3,7},{4,0},{5,1},{6,2},{7,3},{8,12},{9,13},{10,... | collective-permute-start | bytes 18440 | tf_op jit(solution)/shard_map/ppermute | solution.py:44
  51.1 7.0 %collective-permute-start.19 = (f32[64,768]{1,0:T(8,128)S(1)}, f32[64,768]{1,0:T(8,128)S(1)}, u32[]{:S(2)}, u32[]{:S(2)}) collective-permute-start(f32[64,768]{1,0:T(8,128)S(1)} %get-tuple-element.34), channel_id=1, source_target_pairs={{0,8},{1,9},{2,10},{3,11},{4,12},{5,13},{6,14},{7,15},{8,0},{9,1},... | collective-permute-start | bytes 589832 | tf_op jit(solution)/shard_map/ppermute | solution.py:44
  51.7 10.6 %collective-permute-start.23 = (f32[64,768]{1,0:T(8,128)S(1)}, f32[64,768]{1,0:T(8,128)S(1)}, u32[]{:S(2)}, u32[]{:S(2)}) collective-permute-start(f32[64,768]{1,0:T(8,128)S(1)} %get-tuple-element.33), channel_id=1, source_target_pairs={{0,1},{1,0},{2,3},{3,2},{4,5},{5,4},{6,7},{7,6},{8,9},{9,8},{10,11... | collective-permute-start | bytes 589832 | tf_op jit(solution)/shard_map/ppermute | solution.py:44
  51.7 11.8 %collective-permute-start.24 = (f32[64,768]{1,0:T(8,128)S(1)}, f32[64,768]{1,0:T(8,128)S(1)}, u32[]{:S(2)}, u32[]{:S(2)}) collective-permute-start(f32[64,768]{1,0:T(8,128)S(1)} %get-tuple-element.32), channel_id=1, source_target_pairs={{0,9},{1,8},{2,11},{3,10},{4,13},{5,12},{6,15},{7,14},{8,1},{9,0},... | collective-permute-start | bytes 589832 | tf_op jit(solution)/shard_map/ppermute | solution.py:44
  58.8 5.5 %collective-permute-start.20 = (f32[1,128]{1,0:T(1,128)S(1)}, f32[1,128]{1,0:T(1,128)S(1)}, u32[]{:S(2)}, u32[]{:S(2)}) collective-permute-start(f32[1,128]{1,0:T(1,128)S(1)} %broadcast_in_dim.2), channel_id=1, source_target_pairs={{0,1},{1,0},{2,3},{3,2},{4,5},{5,4},{6,7},{7,6},{8,9},{9,8},{10,11... | collective-permute-start | bytes 1544 | tf_op jit(solution)/shard_map/ppermute | solution.py:44
  58.9 5.4 %collective-permute-start.21 = (f32[1,128]{1,0:T(1,128)S(1)}, f32[1,128]{1,0:T(1,128)S(1)}, u32[]{:S(2)}, u32[]{:S(2)}) collective-permute-start(f32[1,128]{1,0:T(1,128)S(1)} %broadcast_in_dim.2), channel_id=1, source_target_pairs={{0,8},{1,9},{2,10},{3,11},{4,12},{5,13},{6,14},{7,15},{8,0},{9,1},... | collective-permute-start | bytes 1544 | tf_op jit(solution)/shard_map/ppermute | solution.py:44
  59.5 4.8 %collective-permute-start.22 = (f32[1,128]{1,0:T(1,128)S(1)}, f32[1,128]{1,0:T(1,128)S(1)}, u32[]{:S(2)}, u32[]{:S(2)}) collective-permute-start(f32[1,128]{1,0:T(1,128)S(1)} %broadcast_in_dim.2), channel_id=1, source_target_pairs={{0,9},{1,8},{2,11},{3,10},{4,13},{5,12},{6,15},{7,14},{8,1},{9,0},... | collective-permute-start | bytes 1544 | tf_op jit(solution)/shard_map/ppermute | solution.py:44

commit v6 on v5

--- a/solution.py
+++ b/solution.py
@@ -61,7 +61,8 @@
     row_s, col_s = {0: student}, {0: student}
     core_t, core_s = [], []
     width = teacher.shape[1]
-    both = jnp.concatenate([teacher, student], 1)
+    core_s.append((0, send(student, core_mask, count)))
+    both = after(jnp.concatenate([teacher, student], 1), core_s[0])
     row_t[1], col_t[1] = send(teacher, row_masks[0], count), send(teacher, plane_masks[0], count)
     for side_t, side_s, masks in ((row_t, row_s, row_masks), (col_t, col_s, plane_masks)):
         for b, mask in enumerate(masks):
@@ -80,6 +81,7 @@
                 forward(row, row_masks, level, count)
                 forward(col, plane_masks, level, count)
             ready = [p for p in range(1 << len(plane_masks)) if max(p.bit_count(), 1) == level]
+            ready = [p for p in ready if p or core is core_t]
             if ready:
                 got = send(jnp.concatenate([col[p] for p in ready]), core_mask, count)
                 core += zip(ready, jnp.split(got, len(ready)))
@@ -124,8 +126,7 @@
         if place < len(col_masks):
             col_part = add_partner(col_part, col_masks, place, count)
         if place < len(row_masks):
-            row_part = add_partner(row_part, row_masks, place, count)
-            row_part, col_part = lax.optimization_barrier((row_part, col_part))
+            row_part = after(add_partner(row_part, row_masks, place, count), col_part)
     row_sum, col_sum = row_part.reshape(3, -1), col_part.reshape(3, -1)
 
     row_alpha, row_beta, _ = coefficients(*row_sum, total)

time: 65.7 us -> 62.2 us (0.947)
  waiting for transfers between devices: 32.9 us -> 22.9 us
  starting transfers between devices: 23.2 us -> 28.7 us
  other arithmetic: 1.48 us -> 2.47 us
    ppermute x25 -> x26, waiting for transfers between devices: 32.9 us -> 22.9 us  [send(): return lax.ppermute(value, AXES, [(i, i ^ mask) for i in range(count)])]
    ppermute x25 -> x26, starting transfers between devices: 23.2 us -> 28.7 us  [send(): return lax.ppermute(value, AXES, [(i, i ^ mask) for i in range(count)])]
    concatenate x0 -> x1, other arithmetic: none -> 0.99 us  [gather(): both = after(jnp.concatenate([teacher, student], 1), core_s[0])]
    concatenate x1 -> x0, local copies, waits for them, and re-layouts: 0.91 us -> none  [gather(): both = jnp.concatenate([teacher, student], 1)]
    unnamed x19 -> x21, local copies, waits for them, and re-layouts: 1.18 us -> 2.01 us
  transfers between devices with their start and end apart: 25 -> 26, of which waited for: 11 -> 14; matrix products, arithmetic and copies ran while one was open for 4% -> 9% of each run, Pallas kernels for 0% -> 0%
where the time goes in v6:
time: 62.2 us; the launch traced here: 62 us
  starting transfers between devices  28.7 us (46%)
  waiting for transfers between devices  22.9 us (37%)
  local copies, waits for them, and re-layouts  3.78 us (6%)
  other arithmetic  2.47 us (4%)
  between operations  2.12 us (3%)
  matrix products  1.95 us (3%)
    ppermute x26, starting transfers between devices, send(): return lax.ppermute(value, AXES, [(i, i ^ mask) for i in range(count)])  28.7 us
    ppermute x26, waiting for transfers between devices, send(): return lax.ppermute(value, AXES, [(i, i ^ mask) for i in range(count)])  22.9 us
    unnamed x21, local copies, waits for them, and re-layouts  2.01 us
  transfers between devices with their start and end apart: 26, of which 14 were waited for; matrix products, arithmetic and copies ran while one was open for 9% of the time, Pallas kernels for 0%

profile of v6, /device:TPU:0, one launch (start us, length us, event | category | flops | bytes accessed | tf_op | source)
XLA Modules:
  0.0 62.0 jit_solution(4485987910140741628)
XLA Ops:
  0.6 3.1 %collective-permute-start = (bf16[64,1536]{1,0:T(8,128)(2,1)}, bf16[64,1536]{1,0:T(8,128)(2,1)S(1)}, u32[]{:S(2)}, u32[]{:S(2)}) collective-permute-start(bf16[64,1536]{1,0:T(8,128)(2,1)} %param.2), channel_id=1, source_target_pairs={{0,1},{1,0},{2,3},{3,2},{4,5},{5,4},{6,7},{7,6},{8,9},{9,8},{10,11... | collective-permute-start | bytes 589832 | tf_op jit(solution)/shard_map/ppermute | solution.py:44
  3.7 2.6 %collective-permute-start.1 = (bf16[64,1536]{1,0:T(8,128)(2,1)}, bf16[64,1536]{1,0:T(8,128)(2,1)S(1)}, u32[]{:S(2)}, u32[]{:S(2)}) collective-permute-start(bf16[64,1536]{1,0:T(8,128)(2,1)} %param.2), channel_id=1, source_target_pairs={{0,2},{1,3},{2,0},{3,1},{4,6},{5,7},{6,4},{7,5},{8,10},{9,11},{10,... | collective-permute-start | bytes 589832 | tf_op jit(solution)/shard_map/ppermute | solution.py:44
  6.7 1.0 %pad_maximum_fusion.1 = bf16[64,2304]{1,0:T(8,128)(2,1)S(1)} fusion(bf16[64,768]{1,0:T(8,128)(2,1)} %param.3, bf16[64,1536]{1,0:T(8,128)(2,1)} %param.2), kind=kLoop, calls=%fused_computation.24 | loop fusion | flops 589824 | bytes 589824 | tf_op jit(solution)/shard_map/concatenate | solution.py:65
  7.8 1.5 %collective-permute-start.6 = (bf16[64,2304]{1,0:T(8,128)(2,1)S(1)}, bf16[64,2304]{1,0:T(8,128)(2,1)S(1)}, u32[]{:S(2)}, u32[]{:S(2)}) collective-permute-start(bf16[64,2304]{1,0:T(8,128)(2,1)S(1)} %pad_maximum_fusion.1), channel_id=1, source_target_pairs={{0,16},{1,17},{2,18},{3,19},{4,20},{5,21},{6,22},{7,23},{8,24},{9,... | collective-permute-start | bytes 884744 | tf_op jit(solution)/shard_map/ppermute | solution.py:44
  9.4 1.5 %collective-permute-start.5 = (bf16[64,2304]{1,0:T(8,128)(2,1)S(1)}, bf16[64,2304]{1,0:T(8,128)(2,1)S(1)}, u32[]{:S(2)}, u32[]{:S(2)}) collective-permute-start(bf16[64,2304]{1,0:T(8,128)(2,1)S(1)} %pad_maximum_fusion.1), channel_id=1, source_target_pairs={{0,8},{1,9},{2,10},{3,11},{4,12},{5,13},{6,14},{7,15},{8,0},{9,1},... | collective-permute-start | bytes 884744 | tf_op jit(solution)/shard_map/ppermute | solution.py:44
  10.8 0.9 %constant_dynamic-update-slice_fusion.6 = bf16[512,768]{1,0:T(8,128)(2,1)S(1)} fusion(bf16[64,768]{1,0:T(8,128)(2,1)} %param.3), kind=kLoop, calls=%fused_computation.41 | loop fusion | bytes 196608
  11.7 0.9 %constant_dynamic-update-slice_fusion.12 = bf16[512,1536]{1,0:T(8,128)(2,1)S(1)} fusion(bf16[64,1536]{1,0:T(8,128)(2,1)} %param.2), kind=kLoop, calls=%fused_computation.47 | loop fusion | bytes 393216
  12.9 5.6 %collective-permute-done.1 = bf16[64,1536]{1,0:T(8,128)(2,1)S(1)} collective-permute-done((bf16[64,1536]{1,0:T(8,128)(2,1)}, bf16[64,1536]{1,0:T(8,128)(2,1)S(1)}, u32[]{:S(2)}, u32[]{:S(2)}) %collective-permute-start.1) | collective-permute-done | bytes 196640 | tf_op jit(solution)/shard_map/ppermute | solution.py:44
  18.6 1.6 %collective-permute-start.13 = (bf16[64,1536]{1,0:T(8,128)(2,1)S(1)}, bf16[64,1536]{1,0:T(8,128)(2,1)S(1)}, u32[]{:S(2)}, u32[]{:S(2)}) collective-permute-start(bf16[64,1536]{1,0:T(8,128)(2,1)S(1)} %collective-permute-done.1), channel_id=1, source_target_pairs={{0,16},{1,17},{2,18},{3,19},{4,20},{5,21},{6,22},{7,23},{8,24},{9,... | collective-permute-start | bytes 589832 | tf_op jit(solution)/shard_map/ppermute | solution.py:44
  20.4 1.6 %collective-permute-start.12 = (bf16[64,1536]{1,0:T(8,128)(2,1)S(1)}, bf16[64,1536]{1,0:T(8,128)(2,1)S(1)}, u32[]{:S(2)}, u32[]{:S(2)}) collective-permute-start(bf16[64,1536]{1,0:T(8,128)(2,1)S(1)} %collective-permute-done), channel_id=1, source_target_pairs={{0,8},{1,9},{2,10},{3,11},{4,12},{5,13},{6,14},{7,15},{8,0},{9,1},... | collective-permute-start | bytes 589832 | tf_op jit(solution)/shard_map/ppermute | solution.py:44
  21.9 2.4 %collective-permute-done.13 = bf16[64,1536]{1,0:T(8,128)(2,1)S(1)} collective-permute-done((bf16[64,1536]{1,0:T(8,128)(2,1)S(1)}, bf16[64,1536]{1,0:T(8,128)(2,1)S(1)}, u32[]{:S(2)}, u32[]{:S(2)}) %collective-permute-start.13) | collective-permute-done | bytes 196640 | tf_op jit(solution)/shard_map/ppermute | solution.py:44
  24.4 1.6 %collective-permute-start.9 = (bf16[64,768]{1,0:T(8,128)(2,1)S(1)}, bf16[64,768]{1,0:T(8,128)(2,1)S(1)}, u32[]{:S(2)}, u32[]{:S(2)}) collective-permute-start(bf16[64,768]{1,0:T(8,128)(2,1)S(1)} %collective-permute-done.3), channel_id=1, source_target_pairs={{0,16},{1,17},{2,18},{3,19},{4,20},{5,21},{6,22},{7,23},{8,24},{9,... | collective-permute-start | bytes 294920 | tf_op jit(solution)/shard_map/ppermute | solution.py:44
  26.4 1.5 %collective-permute-start.8 = (bf16[64,768]{1,0:T(8,128)(2,1)S(1)}, bf16[64,768]{1,0:T(8,128)(2,1)S(1)}, u32[]{:S(2)}, u32[]{:S(2)}) collective-permute-start(bf16[64,768]{1,0:T(8,128)(2,1)S(1)} %collective-permute-done.2), channel_id=1, source_target_pairs={{0,8},{1,9},{2,10},{3,11},{4,12},{5,13},{6,14},{7,15},{8,0},{9,1},... | collective-permute-start | bytes 294920 | tf_op jit(solution)/shard_map/ppermute | solution.py:44
  28.6 1.1 %collective-permute-done.9 = bf16[64,768]{1,0:T(8,128)(2,1)S(1)} collective-permute-done((bf16[64,768]{1,0:T(8,128)(2,1)S(1)}, bf16[64,768]{1,0:T(8,128)(2,1)S(1)}, u32[]{:S(2)}, u32[]{:S(2)}) %collective-permute-start.9) | collective-permute-done | bytes 98336 | tf_op jit(solution)/shard_map/ppermute | solution.py:44
  29.8 1.2 %collective-permute-done.11 = bf16[64,768]{1,0:T(8,128)(2,1)S(1)} collective-permute-done((bf16[64,768]{1,0:T(8,128)(2,1)S(1)}, bf16[64,768]{1,0:T(8,128)(2,1)S(1)}, u32[]{:S(2)}, u32[]{:S(2)}) %collective-permute-start.11) | collective-permute-done | bytes 98336 | tf_op jit(solution)/shard_map/ppermute | solution.py:44
  32.4 3.1 %collective-permute-start.15 = (f32[3,8,64]{2,1,0:T(8,128)S(1)}, f32[3,8,64]{2,1,0:T(8,128)S(1)}, u32[]{:S(2)}, u32[]{:S(2)}) collective-permute-start(f32[3,8,64]{2,1,0:T(8,128)S(1)} %constant_dynamic-update-slice_fusion.13), channel_id=1, source_target_pairs={{0,2},{1,3},{2,0},{3,1},{4,6},{5,7},{6,4},{7,5},{8,10},{9,11},{10,... | collective-permute-start | bytes 18440 | tf_op jit(solution)/shard_map/ppermute | solution.py:44
  35.5 1.7 %collective-permute-done.15 = f32[3,8,64]{2,1,0:T(8,128)S(1)} collective-permute-done((f32[3,8,64]{2,1,0:T(8,128)S(1)}, f32[3,8,64]{2,1,0:T(8,128)S(1)}, u32[]{:S(2)}, u32[]{:S(2)}) %collective-permute-start.15) | collective-permute-done | bytes 6176 | tf_op jit(solution)/shard_map/ppermute | solution.py:44
  37.2 1.3 %collective-permute-start.16 = (f32[3,8,64]{2,1,0:T(8,128)S(1)}, f32[3,8,64]{2,1,0:T(8,128)S(1)}, u32[]{:S(2)}, u32[]{:S(2)}) collective-permute-start(f32[3,8,64]{2,1,0:T(8,128)S(1)} %add.100), channel_id=1, source_target_pairs={{0,16},{1,17},{2,18},{3,19},{4,20},{5,21},{6,22},{7,23},{8,24},{9,... | collective-permute-start | bytes 18440 | tf_op jit(solution)/shard_map/ppermute | solution.py:44
  39.2 1.6 %collective-permute-start.19 = (f32[3,4,64]{2,1,0:T(4,128)S(1)}, f32[3,4,64]{2,1,0:T(4,128)S(1)}, u32[]{:S(2)}, u32[]{:S(2)}) collective-permute-start(f32[3,4,64]{2,1,0:T(4,128)S(1)} %add.106), channel_id=1, source_target_pairs={{0,8},{1,9},{2,10},{3,11},{4,12},{5,13},{6,14},{7,15},{8,0},{9,1},... | collective-permute-start | bytes 9224 | tf_op jit(solution)/shard_map/ppermute | solution.py:44
  40.7 2.1 %collective-permute-done.19 = f32[3,4,64]{2,1,0:T(4,128)S(1)} collective-permute-done((f32[3,4,64]{2,1,0:T(4,128)S(1)}, f32[3,4,64]{2,1,0:T(4,128)S(1)}, u32[]{:S(2)}, u32[]{:S(2)}) %collective-permute-start.19) | collective-permute-done | bytes 3104 | tf_op jit(solution)/shard_map/ppermute | solution.py:44
  43.3 0.9 %collective-permute-done.17 = f32[3,8,64]{2,1,0:T(8,128)S(1)} collective-permute-done((f32[3,8,64]{2,1,0:T(8,128)S(1)}, f32[3,8,64]{2,1,0:T(8,128)S(1)}, u32[]{:S(2)}, u32[]{:S(2)}) %collective-permute-start.17) | collective-permute-done | bytes 6176 | tf_op jit(solution)/shard_map/ppermute | solution.py:44
  45.9 1.6 %collective-permute-start.20 = (f32[64,768]{1,0:T(8,128)S(1)}, f32[64,768]{1,0:T(8,128)S(1)}, u32[]{:S(2)}, u32[]{:S(2)}) collective-permute-start(f32[64,768]{1,0:T(8,128)S(1)} %get-tuple-element.32), channel_id=1, source_target_pairs={{0,8},{1,9},{2,10},{3,11},{4,12},{5,13},{6,14},{7,15},{8,0},{9,1},... | collective-permute-start | bytes 589832 | tf_op jit(solution)/shard_map/ppermute | solution.py:44
  47.4 1.2 %collective-permute-start.24 = (f32[64,768]{1,0:T(8,128)S(1)}, f32[64,768]{1,0:T(8,128)S(1)}, u32[]{:S(2)}, u32[]{:S(2)}) collective-permute-start(f32[64,768]{1,0:T(8,128)S(1)} %get-tuple-element.31), channel_id=1, source_target_pairs={{0,1},{1,0},{2,3},{3,2},{4,5},{5,4},{6,7},{7,6},{8,9},{9,8},{10,11... | collective-permute-start | bytes 589832 | tf_op jit(solution)/shard_map/ppermute | solution.py:44
  48.7 0.8 %collective-permute-start.25 = (f32[64,768]{1,0:T(8,128)S(1)}, f32[64,768]{1,0:T(8,128)S(1)}, u32[]{:S(2)}, u32[]{:S(2)}) collective-permute-start(f32[64,768]{1,0:T(8,128)S(1)} %get-tuple-element.30), channel_id=1, source_target_pairs={{0,9},{1,8},{2,11},{3,10},{4,13},{5,12},{6,15},{7,14},{8,1},{9,0},... | collective-permute-start | bytes 589832 | tf_op jit(solution)/shard_map/ppermute | solution.py:44
  49.4 3.5 %collective-permute-done.20 = f32[64,768]{1,0:T(8,128)S(1)} collective-permute-done((f32[64,768]{1,0:T(8,128)S(1)}, f32[64,768]{1,0:T(8,128)S(1)}, u32[]{:S(2)}, u32[]{:S(2)}) %collective-permute-start.20) | collective-permute-done | bytes 196640 | tf_op jit(solution)/shard_map/ppermute | solution.py:44
  52.9 0.6 %broadcast_in_dim.2 = f32[1,128]{1,0:T(1,128)S(1)} broadcast(f32[]{:T(128)} %get-tuple-element.34), dimensions={} | broadcast | bytes 516 | tf_op jit(solution)/shard_map/broadcast_in_dim | solution.py:141
  53.6 1.3 %collective-permute-start.21 = (f32[1,128]{1,0:T(1,128)S(1)}, f32[1,128]{1,0:T(1,128)S(1)}, u32[]{:S(2)}, u32[]{:S(2)}) collective-permute-start(f32[1,128]{1,0:T(1,128)S(1)} %broadcast_in_dim.2), channel_id=1, source_target_pairs={{0,1},{1,0},{2,3},{3,2},{4,5},{5,4},{6,7},{7,6},{8,9},{9,8},{10,11... | collective-permute-start | bytes 1544 | tf_op jit(solution)/shard_map/ppermute | solution.py:44
  54.9 1.5 %collective-permute-start.22 = (f32[1,128]{1,0:T(1,128)S(1)}, f32[1,128]{1,0:T(1,128)S(1)}, u32[]{:S(2)}, u32[]{:S(2)}) collective-permute-start(f32[1,128]{1,0:T(1,128)S(1)} %broadcast_in_dim.2), channel_id=1, source_target_pairs={{0,8},{1,9},{2,10},{3,11},{4,12},{5,13},{6,14},{7,15},{8,0},{9,1},... | collective-permute-start | bytes 1544 | tf_op jit(solution)/shard_map/ppermute | solution.py:44
  56.3 0.8 %collective-permute-start.23 = (f32[1,128]{1,0:T(1,128)S(1)}, f32[1,128]{1,0:T(1,128)S(1)}, u32[]{:S(2)}, u32[]{:S(2)}) collective-permute-start(f32[1,128]{1,0:T(1,128)S(1)} %broadcast_in_dim.2), channel_id=1, source_target_pairs={{0,9},{1,8},{2,11},{3,10},{4,13},{5,12},{6,15},{7,14},{8,1},{9,0},... | collective-permute-start | bytes 1544 | tf_op jit(solution)/shard_map/ppermute | solution.py:44
  57.1 1.2 %collective-permute-done.25 = f32[64,768]{1,0:T(8,128)S(1)} collective-permute-done((f32[64,768]{1,0:T(8,128)S(1)}, f32[64,768]{1,0:T(8,128)S(1)}, u32[]{:S(2)}, u32[]{:S(2)}) %collective-permute-start.25) | collective-permute-done | bytes 196640 | tf_op jit(solution)/shard_map/ppermute | solution.py:44
  58.3 0.7 %fusion.21 = f32[64,768]{1,0:T(8,128)} fusion(f32[64,768]{1,0:T(8,128)S(1)} %collective-permute-done.24, f32[256,768]{1,0:T(8,128)S(1)} %convolution_add_fusion, f32[64,768]{1,0:T(8,128)S(1)} %collective-permute-done.20, f32[64,768]{1,0:T(8,128)S(1)} %collective-permute-done.25), kind=kLoop, calls=%fused_computation.33 | loop fusion | flops 147456 | bytes 983040 | tf_op jit(solution)/shard_map/add | solution.py:99
  59.1 1.7 %collective-permute-done.23 = f32[1,128]{1,0:T(1,128)S(1)} collective-permute-done((f32[1,128]{1,0:T(1,128)S(1)}, f32[1,128]{1,0:T(1,128)S(1)}, u32[]{:S(2)}, u32[]{:S(2)}) %collective-permute-start.23) | collective-permute-done | bytes 544 | tf_op jit(solution)/shard_map/ppermute | solution.py:44
  (88 shorter events, 6.2 us)
Async XLA Ops:
  0.6 19.6 %copy-start = (bf16[64,1536]{1,0:T(8,128)(2,1)S(1)}, bf16[64,1536]{1,0:T(8,128)(2,1)}, u32[]{:S(2)}) copy-start(bf16[64,1536]{1,0:T(8,128)(2,1)} %param.2) | copy-start | bytes 589828
  0.6 12.3 %collective-permute-start = (bf16[64,1536]{1,0:T(8,128)(2,1)}, bf16[64,1536]{1,0:T(8,128)(2,1)S(1)}, u32[]{:S(2)}, u32[]{:S(2)}) collective-permute-start(bf16[64,1536]{1,0:T(8,128)(2,1)} %param.2), channel_id=1, source_target_pairs={{0,1},{1,0},{2,3},{3,2},{4,5},{5,4},{6,7},{7,6},{8,9},{9,8},{10,11... | collective-permute-start | bytes 589832 | tf_op jit(solution)/shard_map/ppermute | solution.py:44
  3.7 14.8 %collective-permute-start.1 = (bf16[64,1536]{1,0:T(8,128)(2,1)}, bf16[64,1536]{1,0:T(8,128)(2,1)S(1)}, u32[]{:S(2)}, u32[]{:S(2)}) collective-permute-start(bf16[64,1536]{1,0:T(8,128)(2,1)} %param.2), channel_id=1, source_target_pairs={{0,2},{1,3},{2,0},{3,1},{4,6},{5,7},{6,4},{7,5},{8,10},{9,11},{10,... | collective-permute-start | bytes 589832 | tf_op jit(solution)/shard_map/ppermute | solution.py:44
  6.3 1.5 %collective-permute-start.4 = (bf16[64,768]{1,0:T(8,128)(2,1)}, bf16[64,768]{1,0:T(8,128)(2,1)S(1)}, u32[]{:S(2)}, u32[]{:S(2)}) collective-permute-start(bf16[64,768]{1,0:T(8,128)(2,1)} %param.3), channel_id=1, source_target_pairs={{0,4},{1,5},{2,6},{3,7},{4,0},{5,1},{6,2},{7,3},{8,12},{9,13},{10,... | collective-permute-start | bytes 294920 | tf_op jit(solution)/shard_map/ppermute | solution.py:44
  6.3 18.1 %collective-permute-start.3 = (bf16[64,768]{1,0:T(8,128)(2,1)}, bf16[64,768]{1,0:T(8,128)(2,1)S(1)}, u32[]{:S(2)}, u32[]{:S(2)}) collective-permute-start(bf16[64,768]{1,0:T(8,128)(2,1)} %param.3), channel_id=1, source_target_pairs={{0,2},{1,3},{2,0},{3,1},{4,6},{5,7},{6,4},{7,5},{8,10},{9,11},{10,... | collective-permute-start | bytes 294920 | tf_op jit(solution)/shard_map/ppermute | solution.py:44
  7.8 10.7 %collective-permute-start.6 = (bf16[64,2304]{1,0:T(8,128)(2,1)S(1)}, bf16[64,2304]{1,0:T(8,128)(2,1)S(1)}, u32[]{:S(2)}, u32[]{:S(2)}) collective-permute-start(bf16[64,2304]{1,0:T(8,128)(2,1)S(1)} %pad_maximum_fusion.1), channel_id=1, source_target_pairs={{0,16},{1,17},{2,18},{3,19},{4,20},{5,21},{6,22},{7,23},{8,24},{9,... | collective-permute-start | bytes 884744 | tf_op jit(solution)/shard_map/ppermute | solution.py:44
  9.4 9.3 %collective-permute-start.5 = (bf16[64,2304]{1,0:T(8,128)(2,1)S(1)}, bf16[64,2304]{1,0:T(8,128)(2,1)S(1)}, u32[]{:S(2)}, u32[]{:S(2)}) collective-permute-start(bf16[64,2304]{1,0:T(8,128)(2,1)S(1)} %pad_maximum_fusion.1), channel_id=1, source_target_pairs={{0,8},{1,9},{2,10},{3,11},{4,12},{5,13},{6,14},{7,15},{8,0},{9,1},... | collective-permute-start | bytes 884744 | tf_op jit(solution)/shard_map/ppermute | solution.py:44
  18.6 5.8 %collective-permute-start.2 = (bf16[64,768]{1,0:T(8,128)(2,1)}, bf16[64,768]{1,0:T(8,128)(2,1)S(1)}, u32[]{:S(2)}, u32[]{:S(2)}) collective-permute-start(bf16[64,768]{1,0:T(8,128)(2,1)} %param.3), channel_id=1, source_target_pairs={{0,1},{1,0},{2,3},{3,2},{4,5},{5,4},{6,7},{7,6},{8,9},{9,8},{10,11... | collective-permute-start | bytes 294920 | tf_op jit(solution)/shard_map/ppermute | solution.py:44
  18.6 7.4 %copy-start.2 = (bf16[64,2304]{1,0:T(8,128)(2,1)}, bf16[64,2304]{1,0:T(8,128)(2,1)S(1)}, u32[]{:S(2)}) copy-start(bf16[64,2304]{1,0:T(8,128)(2,1)S(1)} %collective-permute-done.5) | copy-start | bytes 884740
  18.6 5.7 %collective-permute-start.13 = (bf16[64,1536]{1,0:T(8,128)(2,1)S(1)}, bf16[64,1536]{1,0:T(8,128)(2,1)S(1)}, u32[]{:S(2)}, u32[]{:S(2)}) collective-permute-start(bf16[64,1536]{1,0:T(8,128)(2,1)S(1)} %collective-permute-done.1), channel_id=1, source_target_pairs={{0,16},{1,17},{2,18},{3,19},{4,20},{5,21},{6,22},{7,23},{8,24},{9,... | collective-permute-start | bytes 589832 | tf_op jit(solution)/shard_map/ppermute | solution.py:44
  20.3 4.1 %collective-permute-start.7 = (bf16[192,1536]{1,0:T(8,128)(2,1)S(1)}, bf16[192,1536]{1,0:T(8,128)(2,1)S(1)}, u32[]{:S(2)}, u32[]{:S(2)}) collective-permute-start(bf16[192,1536]{1,0:T(8,128)(2,1)S(1)} %pad_maximum_fusion), channel_id=1, source_target_pairs={{0,4},{1,5},{2,6},{3,7},{4,0},{5,1},{6,2},{7,3},{8,12},{9,13},{10,... | collective-permute-start | bytes 1769480 | tf_op jit(solution)/shard_map/ppermute | solution.py:44
  20.4 7.6 %collective-permute-start.12 = (bf16[64,1536]{1,0:T(8,128)(2,1)S(1)}, bf16[64,1536]{1,0:T(8,128)(2,1)S(1)}, u32[]{:S(2)}, u32[]{:S(2)}) collective-permute-start(bf16[64,1536]{1,0:T(8,128)(2,1)S(1)} %collective-permute-done), channel_id=1, source_target_pairs={{0,8},{1,9},{2,10},{3,11},{4,12},{5,13},{6,14},{7,15},{8,0},{9,1},... | collective-permute-start | bytes 589832 | tf_op jit(solution)/shard_map/ppermute | solution.py:44
  24.4 3.5 %collective-permute-start.14 = (bf16[64,1536]{1,0:T(8,128)(2,1)S(1)}, bf16[64,1536]{1,0:T(8,128)(2,1)S(1)}, u32[]{:S(2)}, u32[]{:S(2)}) collective-permute-start(bf16[64,1536]{1,0:T(8,128)(2,1)S(1)} %collective-permute-done.13), channel_id=1, source_target_pairs={{0,4},{1,5},{2,6},{3,7},{4,0},{5,1},{6,2},{7,3},{8,12},{9,13},{10,... | collective-permute-start | bytes 589832 | tf_op jit(solution)/shard_map/ppermute | solution.py:44
  24.4 5.3 %collective-permute-start.9 = (bf16[64,768]{1,0:T(8,128)(2,1)S(1)}, bf16[64,768]{1,0:T(8,128)(2,1)S(1)}, u32[]{:S(2)}, u32[]{:S(2)}) collective-permute-start(bf16[64,768]{1,0:T(8,128)(2,1)S(1)} %collective-permute-done.3), channel_id=1, source_target_pairs={{0,16},{1,17},{2,18},{3,19},{4,20},{5,21},{6,22},{7,23},{8,24},{9,... | collective-permute-start | bytes 294920 | tf_op jit(solution)/shard_map/ppermute | solution.py:44
  26.1 1.9 %slice-start = ((bf16[64,2304]{1,0:T(8,128)(2,1)}), bf16[64,1536]{1,0:T(8,128)(2,1)S(1)}, s32[]{:S(2)}) async-start(bf16[64,2304]{1,0:T(8,128)(2,1)} %copy-done.2), calls=%async_computation | async-start | bytes 393216 | tf_op jit(solution)/shard_map/slice | solution.py:71
  26.1 3.7 %collective-permute-start.10 = (bf16[128,768]{1,0:T(8,128)(2,1)S(1)}, bf16[128,768]{1,0:T(8,128)(2,1)S(1)}, u32[]{:S(2)}, u32[]{:S(2)}) collective-permute-start(bf16[128,768]{1,0:T(8,128)(2,1)S(1)} %pad_maximum_fusion.2), channel_id=1, source_target_pairs={{0,4},{1,5},{2,6},{3,7},{4,0},{5,1},{6,2},{7,3},{8,12},{9,13},{10,... | collective-permute-start | bytes 589832 | tf_op jit(solution)/shard_map/ppermute | solution.py:44
  26.4 5.0 %collective-permute-start.8 = (bf16[64,768]{1,0:T(8,128)(2,1)S(1)}, bf16[64,768]{1,0:T(8,128)(2,1)S(1)}, u32[]{:S(2)}, u32[]{:S(2)}) collective-permute-start(bf16[64,768]{1,0:T(8,128)(2,1)S(1)} %collective-permute-done.2), channel_id=1, source_target_pairs={{0,8},{1,9},{2,10},{3,11},{4,12},{5,13},{6,14},{7,15},{8,0},{9,1},... | collective-permute-start | bytes 294920 | tf_op jit(solution)/shard_map/ppermute | solution.py:44
  27.9 3.4 %copy-start.1 = (bf16[64,768]{1,0:T(8,128)(2,1)S(1)}, bf16[64,768]{1,0:T(8,128)(2,1)}, u32[]{:S(2)}) copy-start(bf16[64,768]{1,0:T(8,128)(2,1)} %param.3) | copy-start | bytes 294916
  27.9 3.4 %slice-start.1 = ((bf16[64,2304]{1,0:T(8,128)(2,1)}), bf16[64,768]{1,0:T(8,128)(2,1)S(1)}, s32[]{:S(2)}) async-start(bf16[64,2304]{1,0:T(8,128)(2,1)} %copy-done.2), calls=%async_computation.1 | async-start | bytes 196608 | tf_op jit(solution)/shard_map/slice | solution.py:71
  29.7 1.3 %collective-permute-start.11 = (bf16[64,768]{1,0:T(8,128)(2,1)S(1)}, bf16[64,768]{1,0:T(8,128)(2,1)S(1)}, u32[]{:S(2)}, u32[]{:S(2)}) collective-permute-start(bf16[64,768]{1,0:T(8,128)(2,1)S(1)} %collective-permute-done.9), channel_id=1, source_target_pairs={{0,4},{1,5},{2,6},{3,7},{4,0},{5,1},{6,2},{7,3},{8,12},{9,13},{10,... | collective-permute-start | bytes 294920 | tf_op jit(solution)/shard_map/ppermute | solution.py:44
  32.4 4.8 %collective-permute-start.15 = (f32[3,8,64]{2,1,0:T(8,128)S(1)}, f32[3,8,64]{2,1,0:T(8,128)S(1)}, u32[]{:S(2)}, u32[]{:S(2)}) collective-permute-start(f32[3,8,64]{2,1,0:T(8,128)S(1)} %constant_dynamic-update-slice_fusion.13), channel_id=1, source_target_pairs={{0,2},{1,3},{2,0},{3,1},{4,6},{5,7},{6,4},{7,5},{8,10},{9,11},{10,... | collective-permute-start | bytes 18440 | tf_op jit(solution)/shard_map/ppermute | solution.py:44
  35.5 3.6 %collective-permute-start.18 = (f32[3,4,64]{2,1,0:T(4,128)S(1)}, f32[3,4,64]{2,1,0:T(4,128)S(1)}, u32[]{:S(2)}, u32[]{:S(2)}) collective-permute-start(f32[3,4,64]{2,1,0:T(4,128)S(1)} %constant_dynamic-update-slice_fusion.16), channel_id=1, source_target_pairs={{0,1},{1,0},{2,3},{3,2},{4,5},{5,4},{6,7},{7,6},{8,9},{9,8},{10,11... | collective-permute-start | bytes 9224 | tf_op jit(solution)/shard_map/ppermute | solution.py:44
  37.2 5.7 %collective-permute-start.16 = (f32[3,8,64]{2,1,0:T(8,128)S(1)}, f32[3,8,64]{2,1,0:T(8,128)S(1)}, u32[]{:S(2)}, u32[]{:S(2)}) collective-permute-start(f32[3,8,64]{2,1,0:T(8,128)S(1)} %add.100), channel_id=1, source_target_pairs={{0,16},{1,17},{2,18},{3,19},{4,20},{5,21},{6,22},{7,23},{8,24},{9,... | collective-permute-start | bytes 18440 | tf_op jit(solution)/shard_map/ppermute | solution.py:44
  39.2 3.7 %collective-permute-start.19 = (f32[3,4,64]{2,1,0:T(4,128)S(1)}, f32[3,4,64]{2,1,0:T(4,128)S(1)}, u32[]{:S(2)}, u32[]{:S(2)}) collective-permute-start(f32[3,4,64]{2,1,0:T(4,128)S(1)} %add.106), channel_id=1, source_target_pairs={{0,8},{1,9},{2,10},{3,11},{4,12},{5,13},{6,14},{7,15},{8,0},{9,1},... | collective-permute-start | bytes 9224 | tf_op jit(solution)/shard_map/ppermute | solution.py:44
  42.9 1.2 %collective-permute-start.17 = (f32[3,8,64]{2,1,0:T(8,128)S(1)}, f32[3,8,64]{2,1,0:T(8,128)S(1)}, u32[]{:S(2)}, u32[]{:S(2)}) collective-permute-start(f32[3,8,64]{2,1,0:T(8,128)S(1)} %add.101), channel_id=1, source_target_pairs={{0,4},{1,5},{2,6},{3,7},{4,0},{5,1},{6,2},{7,3},{8,12},{9,13},{10,... | collective-permute-start | bytes 18440 | tf_op jit(solution)/shard_map/ppermute | solution.py:44
  45.9 7.0 %collective-permute-start.20 = (f32[64,768]{1,0:T(8,128)S(1)}, f32[64,768]{1,0:T(8,128)S(1)}, u32[]{:S(2)}, u32[]{:S(2)}) collective-permute-start(f32[64,768]{1,0:T(8,128)S(1)} %get-tuple-element.32), channel_id=1, source_target_pairs={{0,8},{1,9},{2,10},{3,11},{4,12},{5,13},{6,14},{7,15},{8,0},{9,1},... | collective-permute-start | bytes 589832 | tf_op jit(solution)/shard_map/ppermute | solution.py:44
  47.4 9.7 %collective-permute-start.24 = (f32[64,768]{1,0:T(8,128)S(1)}, f32[64,768]{1,0:T(8,128)S(1)}, u32[]{:S(2)}, u32[]{:S(2)}) collective-permute-start(f32[64,768]{1,0:T(8,128)S(1)} %get-tuple-element.31), channel_id=1, source_target_pairs={{0,1},{1,0},{2,3},{3,2},{4,5},{5,4},{6,7},{7,6},{8,9},{9,8},{10,11... | collective-permute-start | bytes 589832 | tf_op jit(solution)/shard_map/ppermute | solution.py:44
  48.7 9.7 %collective-permute-start.25 = (f32[64,768]{1,0:T(8,128)S(1)}, f32[64,768]{1,0:T(8,128)S(1)}, u32[]{:S(2)}, u32[]{:S(2)}) collective-permute-start(f32[64,768]{1,0:T(8,128)S(1)} %get-tuple-element.30), channel_id=1, source_target_pairs={{0,9},{1,8},{2,11},{3,10},{4,13},{5,12},{6,15},{7,14},{8,1},{9,0},... | collective-permute-start | bytes 589832 | tf_op jit(solution)/shard_map/ppermute | solution.py:44
  53.6 5.5 %collective-permute-start.21 = (f32[1,128]{1,0:T(1,128)S(1)}, f32[1,128]{1,0:T(1,128)S(1)}, u32[]{:S(2)}, u32[]{:S(2)}) collective-permute-start(f32[1,128]{1,0:T(1,128)S(1)} %broadcast_in_dim.2), channel_id=1, source_target_pairs={{0,1},{1,0},{2,3},{3,2},{4,5},{5,4},{6,7},{7,6},{8,9},{9,8},{10,11... | collective-permute-start | bytes 1544 | tf_op jit(solution)/shard_map/ppermute | solution.py:44
  54.9 4.2 %collective-permute-start.22 = (f32[1,128]{1,0:T(1,128)S(1)}, f32[1,128]{1,0:T(1,128)S(1)}, u32[]{:S(2)}, u32[]{:S(2)}) collective-permute-start(f32[1,128]{1,0:T(1,128)S(1)} %broadcast_in_dim.2), channel_id=1, source_target_pairs={{0,8},{1,9},{2,10},{3,11},{4,12},{5,13},{6,14},{7,15},{8,0},{9,1},... | collective-permute-start | bytes 1544 | tf_op jit(solution)/shard_map/ppermute | solution.py:44
  56.3 4.4 %collective-permute-start.23 = (f32[1,128]{1,0:T(1,128)S(1)}, f32[1,128]{1,0:T(1,128)S(1)}, u32[]{:S(2)}, u32[]{:S(2)}) collective-permute-start(f32[1,128]{1,0:T(1,128)S(1)} %broadcast_in_dim.2), channel_id=1, source_target_pairs={{0,9},{1,8},{2,11},{3,10},{4,13},{5,12},{6,15},{7,14},{8,1},{9,0},... | collective-permute-start | bytes 1544 | tf_op jit(solution)/shard_map/ppermute | solution.py:44

commit v7 on v6

--- a/solution.py
+++ b/solution.py
@@ -1,12 +1,17 @@
+import functools
 import math
 
 import jax
 import jax.numpy as jnp
 from jax import lax
+from jax.experimental import pallas as pl
+from jax.experimental.pallas import tpu as pltpu
 from jax.sharding import PartitionSpec as P
 
 DS = 768
 AXES = ("blk", "inner")
+VMEM = 48 * 2**20
+SHARE_SCALE = 8.0
 
 
 EPSILON = 1e-06
@@ -69,7 +74,7 @@
             if b:
                 got = send(both, mask, count)
                 side_t[1 << b], side_s[1 << b] = got[:, :width], got[:, width:]
-    col_s[1] = send(student, plane_masks[0], count)
+    col_s[1] = send(after(student, core_s[0]), plane_masks[0], count)
     row_t[1], col_t[1], late = lax.optimization_barrier((row_t[1], col_t[1], student))
     row_s[1] = send(late, row_masks[0], count)
     early = (row_t[2], col_t[2], row_s[2], col_s[2])
@@ -100,6 +105,45 @@
     return values[0]
 
 
+def output_kernel(n_row, total, gram_s, gram_t, row_sum, col_sum, col_s, own, share, *pieces):
+    row_alpha, row_beta, _ = coefficients(*(row_sum[k] for k in range(3)), total)
+    col_alpha, col_beta, terms = coefficients(*(col_sum[k] for k in range(3)), total)
+    row_ab = jnp.transpose(jnp.concatenate([row_alpha, row_beta] * 4))
+    row_w = row_ab[:, 0:1] * gram_s[...] - row_ab[:, 1:2] * gram_t[...]
+    col_w = col_alpha * gram_s[...] - col_beta * gram_t[...]
+    out = jnp.dot(row_w.astype(jnp.bfloat16), col_s[...], preferred_element_type=jnp.float32)
+    out += jnp.dot(col_w.astype(jnp.bfloat16), col_s[...], preferred_element_type=jnp.float32)
+
+    rows, width = own.shape
+    own[...] = out[:rows]
+    term = jnp.sum(terms, axis=1, keepdims=True)
+    share[...] = jnp.broadcast_to(term, share.shape)
+    largest = jnp.max(jnp.max(jnp.abs(out), axis=0, keepdims=True), axis=1, keepdims=True)
+    power = jnp.clip(jnp.floor(jnp.log2(largest)), -100.0, 100.0)
+    term = term * SHARE_SCALE
+    high = term.astype(jnp.bfloat16).astype(jnp.float32)
+    middle = (term - high).astype(jnp.bfloat16).astype(jnp.float32)
+    low = term - high - middle
+    lane = lax.broadcasted_iota(jnp.int32, (rows, 128), 1)
+    extra = jnp.where(lane == 0, power, jnp.where(lane == 1, high, jnp.where(lane == 2, middle, low)))
+    scaled = out * jnp.exp2(13.0 - power)
+    for k, piece in enumerate(pieces):
+        piece[:, :width] = scaled[(k + 1) * rows : (k + 2) * rows]
+        piece[:, width:] = extra
+
+
+def final_kernel(total, own, share, *refs):
+    *pieces, grad, loss = refs
+    width = own.shape[1]
+    grads, terms = [own[...]], [share[0:1, 0:1]]
+    for piece in pieces:
+        extra = piece[:, width:]
+        grads.append(piece[:, :width] * jnp.exp2(extra[:, 0:1] - 13.0))
+        terms.append((extra[0:1, 1:2] + extra[0:1, 2:3] + extra[0:1, 3:4]) * (1.0 / SHARE_SCALE))
+    grad[...] = tree_sum(grads)
+    loss[...] = tree_sum(terms) * (1.0 / total)
+
+
 def add_partner(parts, masks, place, count):
     got = send(parts, masks[place], count)
     shape = (3, -1, 2, 1 << place, got.shape[-1])
@@ -127,20 +171,29 @@
             col_part = add_partner(col_part, col_masks, place, count)
         if place < len(row_masks):
             row_part = after(add_partner(row_part, row_masks, place, count), col_part)
-    row_sum, col_sum = row_part.reshape(3, -1), col_part.reshape(3, -1)
-
-    row_alpha, row_beta, _ = coefficients(*row_sum, total)
-    col_alpha, col_beta, terms = coefficients(*col_sum, total)
-    row_w = row_alpha[:, None] * gram_s - row_beta[:, None] * gram_t
-    col_w = col_alpha[None, :] * gram_s - col_beta[None, :] * gram_t
-    out = jnp.dot(row_w.astype(jnp.bfloat16), col_s, preferred_element_type=jnp.float32)
-    out += jnp.dot(col_w.astype(jnp.bfloat16), col_s, preferred_element_type=jnp.float32)
-    out = jnp.split(out, n_row)
-    places = [(place, mask) for place, mask in enumerate(span(row_masks)) if place]
-    grads = out[:1] + [send(out[place], mask, count) for place, mask in places]
-    term = after(jnp.full((1, 128), jnp.sum(terms)), grads[2])
-    losses = [term] + [send(term, mask, count) for _, mask in places]
-    return (tree_sum(losses)[0, 0] / total, tree_sum(grads))
+    row_sum, col_sum = row_part.reshape(3, 1, -1), col_part.reshape(3, 1, -1)
+
+    width = student.shape[1]
+    piece = jax.ShapeDtypeStruct((rows, width + 128), jnp.float32)
+    own, share, *pieces = pl.pallas_call(
+        functools.partial(output_kernel, n_row, total),
+        out_shape=[
+            jax.ShapeDtypeStruct((rows, width), jnp.float32),
+            jax.ShapeDtypeStruct((8, 128), jnp.float32),
+        ]
+        + [piece] * (n_row - 1),
+        compiler_params=pltpu.CompilerParams(vmem_limit_bytes=VMEM),
+    )(gram_s, gram_t, row_sum, col_sum, col_s)
+    got = [
+        send(value.astype(jnp.float16), mask, count).astype(jnp.float32)
+        for value, mask in zip(pieces, span(row_masks)[1:])
+    ]
+    grad, loss = pl.pallas_call(
+        functools.partial(final_kernel, total),
+        out_shape=[jax.ShapeDtypeStruct((rows, width), jnp.float32), jax.ShapeDtypeStruct((1, 1), jnp.float32)],
+        compiler_params=pltpu.CompilerParams(vmem_limit_bytes=VMEM),
+    )(own, share, *got)
+    return (loss[0, 0], grad)
 
 
 def solution(mesh):

time: 62.2 us -> 56.2 us (0.904)
  waiting for transfers between devices: 22.9 us -> 18.9 us
  Pallas kernels: 0 us -> 1.7 us
  other arithmetic: 2.47 us -> 1.21 us
  between operations: 2.12 us -> 0.92 us
  local copies, waits for them, and re-layouts: 3.78 us -> 2.96 us
  matrix products: 1.95 us -> 1.16 us
    ppermute x26 -> x23, waiting for transfers between devices: 22.9 us -> 18.9 us  [send(): return lax.ppermute(value, AXES, [(i, i ^ mask) for i in range(count)])]
    pallas_call x0 -> x2, Pallas kernels: none -> 1.7 us  [the longest x1 0.89 us: per_device(): pl.pallas_call(functools.partial(output_kernel, n_row, total), out_shape=...]
    dot_general x2 -> x0, matrix products: 0.79 us -> none  [the longest x1 0.42 us: per_device(): jnp.dot(row_w.astype(jnp.bfloat16), col_s, preferred_element_type=jnp.flo...]
    add x2 -> x0, other arithmetic: 0.73 us -> none  [tree_sum(): values = [values[i] + values[i + 1] for i in range(0, len(values), 2)]]
    div x4 -> x0, other arithmetic: 0.65 us -> none  [coefficients(): alpha = factor * (EPSILON / norm_student + cross / norm_teacher) / cubed]
    broadcast_in_dim x1 -> x0, local copies, waits for them, and re-layouts: 0.65 us -> none  [per_device(): term = after(jnp.full((1, 128), jnp.sum(terms)), grads[2])]
    ppermute x26 -> x23, starting transfers between devices: 28.7 us -> 29.1 us  [send(): return lax.ppermute(value, AXES, [(i, i ^ mask) for i in range(count)])]
  transfers between devices with their start and end apart: 26 -> 23, of which waited for: 14 -> 13; matrix products, arithmetic and copies ran while one was open for 9% -> 7% of each run, Pallas kernels for 0% -> 0%
where the time goes in v7:
time: 56.2 us; the launch traced here: 56 us
  starting transfers between devices  29.1 us (52%)
  waiting for transfers between devices  18.9 us (34%)
  local copies, waits for them, and re-layouts  2.96 us (5%)
  Pallas kernels  1.7 us (3%)
  other arithmetic  1.21 us (2%)
  matrix products  1.16 us (2%)
  between operations  0.92 us (2%)
    ppermute x23, starting transfers between devices, send(): return lax.ppermute(value, AXES, [(i, i ^ mask) for i in range(count)])  29.1 us
    ppermute x23, waiting for transfers between devices, send(): return lax.ppermute(value, AXES, [(i, i ^ mask) for i in range(count)])  18.9 us
    unnamed x21, local copies, waits for them, and re-layouts  2.01 us
  transfers between devices with their start and end apart: 23, of which 13 were waited for; matrix products, arithmetic and copies ran while one was open for 7% of the time, Pallas kernels for 0%

profile of v7, /device:TPU:0, one launch (start us, length us, event | category | flops | bytes accessed | tf_op | source)
XLA Modules:
  0.0 56.0 jit_solution(17170992124431901947)
XLA Ops:
  0.6 3.1 %collective-permute-start = (bf16[64,1536]{1,0:T(8,128)(2,1)}, bf16[64,1536]{1,0:T(8,128)(2,1)S(1)}, u32[]{:S(2)}, u32[]{:S(2)}) collective-permute-start(bf16[64,1536]{1,0:T(8,128)(2,1)} %param.2), channel_id=1, source_target_pairs={{0,1},{1,0},{2,3},{3,2},{4,5},{5,4},{6,7},{7,6},{8,9},{9,8},{10,11... | collective-permute-start | bytes 589832 | tf_op jit(solution)/shard_map/ppermute | solution.py:49
  3.7 2.6 %collective-permute-start.1 = (bf16[64,1536]{1,0:T(8,128)(2,1)}, bf16[64,1536]{1,0:T(8,128)(2,1)S(1)}, u32[]{:S(2)}, u32[]{:S(2)}) collective-permute-start(bf16[64,1536]{1,0:T(8,128)(2,1)} %param.2), channel_id=1, source_target_pairs={{0,2},{1,3},{2,0},{3,1},{4,6},{5,7},{6,4},{7,5},{8,10},{9,11},{10,... | collective-permute-start | bytes 589832 | tf_op jit(solution)/shard_map/ppermute | solution.py:49
  6.3 1.0 %pad_maximum_fusion.1 = bf16[64,2304]{1,0:T(8,128)(2,1)S(1)} fusion(bf16[64,768]{1,0:T(8,128)(2,1)} %param.3, bf16[64,1536]{1,0:T(8,128)(2,1)} %param.2), kind=kLoop, calls=%fused_computation.21 | loop fusion | flops 589824 | bytes 589824 | tf_op jit(solution)/shard_map/concatenate | solution.py:70
  7.8 1.5 %collective-permute-start.5 = (bf16[64,2304]{1,0:T(8,128)(2,1)S(1)}, bf16[64,2304]{1,0:T(8,128)(2,1)S(1)}, u32[]{:S(2)}, u32[]{:S(2)}) collective-permute-start(bf16[64,2304]{1,0:T(8,128)(2,1)S(1)} %pad_maximum_fusion.1), channel_id=1, source_target_pairs={{0,8},{1,9},{2,10},{3,11},{4,12},{5,13},{6,14},{7,15},{8,0},{9,1},... | collective-permute-start | bytes 884744 | tf_op jit(solution)/shard_map/ppermute | solution.py:49
  9.3 1.5 %collective-permute-start.6 = (bf16[64,2304]{1,0:T(8,128)(2,1)S(1)}, bf16[64,2304]{1,0:T(8,128)(2,1)S(1)}, u32[]{:S(2)}, u32[]{:S(2)}) collective-permute-start(bf16[64,2304]{1,0:T(8,128)(2,1)S(1)} %pad_maximum_fusion.1), channel_id=1, source_target_pairs={{0,16},{1,17},{2,18},{3,19},{4,20},{5,21},{6,22},{7,23},{8,24},{9,... | collective-permute-start | bytes 884744 | tf_op jit(solution)/shard_map/ppermute | solution.py:49
  10.8 0.9 %constant_dynamic-update-slice_fusion.6 = bf16[512,768]{1,0:T(8,128)(2,1)S(1)} fusion(bf16[64,768]{1,0:T(8,128)(2,1)} %param.3), kind=kLoop, calls=%fused_computation.31 | loop fusion | bytes 196608
  11.7 0.9 %constant_dynamic-update-slice_fusion.12 = bf16[512,1536]{1,0:T(8,128)(2,1)S(1)} fusion(bf16[64,1536]{1,0:T(8,128)(2,1)} %param.2), kind=kLoop, calls=%fused_computation.37 | loop fusion | bytes 393216
  13.1 2.4 %collective-permute-done.1 = bf16[64,1536]{1,0:T(8,128)(2,1)S(1)} collective-permute-done((bf16[64,1536]{1,0:T(8,128)(2,1)}, bf16[64,1536]{1,0:T(8,128)(2,1)S(1)}, u32[]{:S(2)}, u32[]{:S(2)}) %collective-permute-start.1) | collective-permute-done | bytes 196640 | tf_op jit(solution)/shard_map/ppermute | solution.py:49
  15.5 2.9 %collective-permute-start.2 = (bf16[64,768]{1,0:T(8,128)(2,1)}, bf16[64,768]{1,0:T(8,128)(2,1)S(1)}, u32[]{:S(2)}, u32[]{:S(2)}) collective-permute-start(bf16[64,768]{1,0:T(8,128)(2,1)} %param.3), channel_id=1, source_target_pairs={{0,1},{1,0},{2,3},{3,2},{4,5},{5,4},{6,7},{7,6},{8,9},{9,8},{10,11... | collective-permute-start | bytes 294920 | tf_op jit(solution)/shard_map/ppermute | solution.py:49
  18.4 1.6 %collective-permute-start.13 = (bf16[64,1536]{1,0:T(8,128)(2,1)S(1)}, bf16[64,1536]{1,0:T(8,128)(2,1)S(1)}, u32[]{:S(2)}, u32[]{:S(2)}) collective-permute-start(bf16[64,1536]{1,0:T(8,128)(2,1)S(1)} %collective-permute-done.1), channel_id=1, source_target_pairs={{0,16},{1,17},{2,18},{3,19},{4,20},{5,21},{6,22},{7,23},{8,24},{9,... | collective-permute-start | bytes 589832 | tf_op jit(solution)/shard_map/ppermute | solution.py:49
  20.2 1.6 %collective-permute-start.12 = (bf16[64,1536]{1,0:T(8,128)(2,1)S(1)}, bf16[64,1536]{1,0:T(8,128)(2,1)S(1)}, u32[]{:S(2)}, u32[]{:S(2)}) collective-permute-start(bf16[64,1536]{1,0:T(8,128)(2,1)S(1)} %collective-permute-done), channel_id=1, source_target_pairs={{0,8},{1,9},{2,10},{3,11},{4,12},{5,13},{6,14},{7,15},{8,0},{9,1},... | collective-permute-start | bytes 589832 | tf_op jit(solution)/shard_map/ppermute | solution.py:49
  21.7 2.4 %collective-permute-done.13 = bf16[64,1536]{1,0:T(8,128)(2,1)S(1)} collective-permute-done((bf16[64,1536]{1,0:T(8,128)(2,1)S(1)}, bf16[64,1536]{1,0:T(8,128)(2,1)S(1)}, u32[]{:S(2)}, u32[]{:S(2)}) %collective-permute-start.13) | collective-permute-done | bytes 196640 | tf_op jit(solution)/shard_map/ppermute | solution.py:49
  24.2 1.6 %collective-permute-start.9 = (bf16[64,768]{1,0:T(8,128)(2,1)S(1)}, bf16[64,768]{1,0:T(8,128)(2,1)S(1)}, u32[]{:S(2)}, u32[]{:S(2)}) collective-permute-start(bf16[64,768]{1,0:T(8,128)(2,1)S(1)} %collective-permute-done.4), channel_id=1, source_target_pairs={{0,16},{1,17},{2,18},{3,19},{4,20},{5,21},{6,22},{7,23},{8,24},{9,... | collective-permute-start | bytes 294920 | tf_op jit(solution)/shard_map/ppermute | solution.py:49
  26.1 1.5 %collective-permute-start.8 = (bf16[64,768]{1,0:T(8,128)(2,1)S(1)}, bf16[64,768]{1,0:T(8,128)(2,1)S(1)}, u32[]{:S(2)}, u32[]{:S(2)}) collective-permute-start(bf16[64,768]{1,0:T(8,128)(2,1)S(1)} %collective-permute-done.2), channel_id=1, source_target_pairs={{0,8},{1,9},{2,10},{3,11},{4,12},{5,13},{6,14},{7,15},{8,0},{9,1},... | collective-permute-start | bytes 294920 | tf_op jit(solution)/shard_map/ppermute | solution.py:49
  28.4 1.1 %collective-permute-done.9 = bf16[64,768]{1,0:T(8,128)(2,1)S(1)} collective-permute-done((bf16[64,768]{1,0:T(8,128)(2,1)S(1)}, bf16[64,768]{1,0:T(8,128)(2,1)S(1)}, u32[]{:S(2)}, u32[]{:S(2)}) %collective-permute-start.9) | collective-permute-done | bytes 98336 | tf_op jit(solution)/shard_map/ppermute | solution.py:49
  29.6 1.2 %collective-permute-done.11 = bf16[64,768]{1,0:T(8,128)(2,1)S(1)} collective-permute-done((bf16[64,768]{1,0:T(8,128)(2,1)S(1)}, bf16[64,768]{1,0:T(8,128)(2,1)S(1)}, u32[]{:S(2)}, u32[]{:S(2)}) %collective-permute-start.11) | collective-permute-done | bytes 98336 | tf_op jit(solution)/shard_map/ppermute | solution.py:49
  32.1 3.3 %collective-permute-start.16 = (f32[3,8,64]{2,1,0:T(8,128)S(1)}, f32[3,8,64]{2,1,0:T(8,128)S(1)}, u32[]{:S(2)}, u32[]{:S(2)}) collective-permute-start(f32[3,8,64]{2,1,0:T(8,128)S(1)} %constant_dynamic-update-slice_fusion.16), channel_id=1, source_target_pairs={{0,2},{1,3},{2,0},{3,1},{4,6},{5,7},{6,4},{7,5},{8,10},{9,11},{10,... | collective-permute-start | bytes 18440 | tf_op jit(solution)/shard_map/ppermute | solution.py:49
  35.5 1.6 %collective-permute-done.16 = f32[3,8,64]{2,1,0:T(8,128)S(1)} collective-permute-done((f32[3,8,64]{2,1,0:T(8,128)S(1)}, f32[3,8,64]{2,1,0:T(8,128)S(1)}, u32[]{:S(2)}, u32[]{:S(2)}) %collective-permute-start.16) | collective-permute-done | bytes 6176 | tf_op jit(solution)/shard_map/ppermute | solution.py:49
  37.1 1.3 %collective-permute-start.18 = (f32[3,8,64]{2,1,0:T(8,128)S(1)}, f32[3,8,64]{2,1,0:T(8,128)S(1)}, u32[]{:S(2)}, u32[]{:S(2)}) collective-permute-start(f32[3,8,64]{2,1,0:T(8,128)S(1)} %add.41), channel_id=1, source_target_pairs={{0,16},{1,17},{2,18},{3,19},{4,20},{5,21},{6,22},{7,23},{8,24},{9,... | collective-permute-start | bytes 18440 | tf_op jit(solution)/shard_map/ppermute | solution.py:49
  38.4 0.7 %collective-permute-start.15 = (f32[3,4,64]{2,1,0:T(4,128)S(1)}, f32[3,4,64]{2,1,0:T(4,128)S(1)}, u32[]{:S(2)}, u32[]{:S(2)}) collective-permute-start(f32[3,4,64]{2,1,0:T(4,128)S(1)} %constant_dynamic-update-slice_fusion.13), channel_id=1, source_target_pairs={{0,1},{1,0},{2,3},{3,2},{4,5},{5,4},{6,7},{7,6},{8,9},{9,8},{10,11... | collective-permute-start | bytes 9224 | tf_op jit(solution)/shard_map/ppermute | solution.py:49
  39.1 1.8 %collective-permute-done.18 = f32[3,8,64]{2,1,0:T(8,128)S(1)} collective-permute-done((f32[3,8,64]{2,1,0:T(8,128)S(1)}, f32[3,8,64]{2,1,0:T(8,128)S(1)}, u32[]{:S(2)}, u32[]{:S(2)}) %collective-permute-start.18) | collective-permute-done | bytes 6176 | tf_op jit(solution)/shard_map/ppermute | solution.py:49
  41.0 1.1 %collective-permute-done.15 = f32[3,4,64]{2,1,0:T(4,128)S(1)} collective-permute-done((f32[3,4,64]{2,1,0:T(4,128)S(1)}, f32[3,4,64]{2,1,0:T(4,128)S(1)}, u32[]{:S(2)}, u32[]{:S(2)}) %collective-permute-start.15) | collective-permute-done | bytes 3104 | tf_op jit(solution)/shard_map/ppermute | solution.py:49
  42.1 1.5 %collective-permute-start.17 = (f32[3,4,64]{2,1,0:T(4,128)S(1)}, f32[3,4,64]{2,1,0:T(4,128)S(1)}, u32[]{:S(2)}, u32[]{:S(2)}) collective-permute-start(f32[3,4,64]{2,1,0:T(4,128)S(1)} %add.40), channel_id=1, source_target_pairs={{0,8},{1,9},{2,10},{3,11},{4,12},{5,13},{6,14},{7,15},{8,0},{9,1},... | collective-permute-start | bytes 9224 | tf_op jit(solution)/shard_map/ppermute | solution.py:49
  43.7 2.1 %collective-permute-done.17 = f32[3,4,64]{2,1,0:T(4,128)S(1)} collective-permute-done((f32[3,4,64]{2,1,0:T(4,128)S(1)}, f32[3,4,64]{2,1,0:T(4,128)S(1)}, u32[]{:S(2)}, u32[]{:S(2)}) %collective-permute-start.17) | collective-permute-done | bytes 3104 | tf_op jit(solution)/shard_map/ppermute | solution.py:49
  46.1 0.9 %shard_map.41 = (f32[64,768]{1,0:T(8,128)S(1)}, f32[8,128]{1,0:T(8,128)S(1)}, f32[64,896]{1,0:T(8,128)S(1)}, f32[64,896]{1,0:T(8,128)S(1)}, f32[64,896]{1,0:T(8,128)S(1)}) custom-call(f32[256,512]{1,0:T(8,128)S(1)} %get-tuple-element.44.gram_s, f32[256,512]{1,0:T(8,128)S(1)} %fusion.gram_t, f32[3,1,256]{2,1,0:T(1,128)S(1)} %reshape.136.row_sum, ...), custom_call_target="tpu_custom_call" | custom-call | tf_op jit(solution)/shard_map/pallas_call | solution.py:178
  47.0 0.8 %collective-permute-start.20 = (f16[64,896]{1,0:T(8,128)(2,1)S(1)}, f16[64,896]{1,0:T(8,128)(2,1)S(1)}, u32[]{:S(2)}, u32[]{:S(2)}) collective-permute-start(f16[64,896]{1,0:T(8,128)(2,1)S(1)} %convert_element_type.18), channel_id=1, source_target_pairs={{0,1},{1,0},{2,3},{3,2},{4,5},{5,4},{6,7},{7,6},{8,9},{9,8},{10,11... | collective-permute-start | bytes 344072 | tf_op jit(solution)/shard_map/ppermute | solution.py:49
  47.8 1.7 %collective-permute-start.21 = (f16[64,896]{1,0:T(8,128)(2,1)S(1)}, f16[64,896]{1,0:T(8,128)(2,1)S(1)}, u32[]{:S(2)}, u32[]{:S(2)}) collective-permute-start(f16[64,896]{1,0:T(8,128)(2,1)S(1)} %convert_element_type.20), channel_id=1, source_target_pairs={{0,8},{1,9},{2,10},{3,11},{4,12},{5,13},{6,14},{7,15},{8,0},{9,1},... | collective-permute-start | bytes 344072 | tf_op jit(solution)/shard_map/ppermute | solution.py:49
  49.5 1.3 %collective-permute-start.22 = (f16[64,896]{1,0:T(8,128)(2,1)S(1)}, f16[64,896]{1,0:T(8,128)(2,1)S(1)}, u32[]{:S(2)}, u32[]{:S(2)}) collective-permute-start(f16[64,896]{1,0:T(8,128)(2,1)S(1)} %convert_element_type.22), channel_id=1, source_target_pairs={{0,9},{1,8},{2,11},{3,10},{4,13},{5,12},{6,15},{7,14},{8,1},{9,0},... | collective-permute-start | bytes 344072 | tf_op jit(solution)/shard_map/ppermute | solution.py:49
  50.7 1.4 %collective-permute-done.20 = f16[64,896]{1,0:T(8,128)(2,1)S(1)} collective-permute-done((f16[64,896]{1,0:T(8,128)(2,1)S(1)}, f16[64,896]{1,0:T(8,128)(2,1)S(1)}, u32[]{:S(2)}, u32[]{:S(2)}) %collective-permute-start.20) | collective-permute-done | bytes 114720 | tf_op jit(solution)/shard_map/ppermute | solution.py:49
  52.2 1.0 %collective-permute-done.21 = f16[64,896]{1,0:T(8,128)(2,1)S(1)} collective-permute-done((f16[64,896]{1,0:T(8,128)(2,1)S(1)}, f16[64,896]{1,0:T(8,128)(2,1)S(1)}, u32[]{:S(2)}, u32[]{:S(2)}) %collective-permute-start.21) | collective-permute-done | bytes 114720 | tf_op jit(solution)/shard_map/ppermute | solution.py:49
  53.2 2.0 %collective-permute-done.22 = f16[64,896]{1,0:T(8,128)(2,1)S(1)} collective-permute-done((f16[64,896]{1,0:T(8,128)(2,1)S(1)}, f16[64,896]{1,0:T(8,128)(2,1)S(1)}, u32[]{:S(2)}, u32[]{:S(2)}) %collective-permute-start.22) | collective-permute-done | bytes 114720 | tf_op jit(solution)/shard_map/ppermute | solution.py:49
  55.2 0.8 %shard_map.42 = (f32[64,768]{1,0:T(8,128)}, f32[1,1]{1,0:T(1,128)}) custom-call(f32[64,768]{1,0:T(8,128)S(1)} %get-tuple-element.31.own, f32[8,128]{1,0:T(8,128)S(1)} %get-tuple-element.32.share, f32[64,896]{1,0:T(8,128)S(1)} %convert_element_type.19.refs_0_, f32[64,896]{1,0:T(8,128)S(1)} %convert_element_type.21.refs_1_, ...), custom_call_target="tpu_custom_call" | custom-call | tf_op jit(solution)/shard_map/pallas_call | solution.py:191
  (78 shorter events, 4.1 us)
Async XLA Ops:
  0.6 19.4 %copy-start = (bf16[64,1536]{1,0:T(8,128)(2,1)S(1)}, bf16[64,1536]{1,0:T(8,128)(2,1)}, u32[]{:S(2)}) copy-start(bf16[64,1536]{1,0:T(8,128)(2,1)} %param.2) | copy-start | bytes 589828
  0.6 12.4 %collective-permute-start = (bf16[64,1536]{1,0:T(8,128)(2,1)}, bf16[64,1536]{1,0:T(8,128)(2,1)S(1)}, u32[]{:S(2)}, u32[]{:S(2)}) collective-permute-start(bf16[64,1536]{1,0:T(8,128)(2,1)} %param.2), channel_id=1, source_target_pairs={{0,1},{1,0},{2,3},{3,2},{4,5},{5,4},{6,7},{7,6},{8,9},{9,8},{10,11... | collective-permute-start | bytes 589832 | tf_op jit(solution)/shard_map/ppermute | solution.py:49
  3.7 11.7 %collective-permute-start.1 = (bf16[64,1536]{1,0:T(8,128)(2,1)}, bf16[64,1536]{1,0:T(8,128)(2,1)S(1)}, u32[]{:S(2)}, u32[]{:S(2)}) collective-permute-start(bf16[64,1536]{1,0:T(8,128)(2,1)} %param.2), channel_id=1, source_target_pairs={{0,2},{1,3},{2,0},{3,1},{4,6},{5,7},{6,4},{7,5},{8,10},{9,11},{10,... | collective-permute-start | bytes 589832 | tf_op jit(solution)/shard_map/ppermute | solution.py:49
  6.3 1.5 %collective-permute-start.3 = (bf16[64,768]{1,0:T(8,128)(2,1)}, bf16[64,768]{1,0:T(8,128)(2,1)S(1)}, u32[]{:S(2)}, u32[]{:S(2)}) collective-permute-start(bf16[64,768]{1,0:T(8,128)(2,1)} %param.3), channel_id=1, source_target_pairs={{0,4},{1,5},{2,6},{3,7},{4,0},{5,1},{6,2},{7,3},{8,12},{9,13},{10,... | collective-permute-start | bytes 294920 | tf_op jit(solution)/shard_map/ppermute | solution.py:49
  7.8 10.6 %collective-permute-start.5 = (bf16[64,2304]{1,0:T(8,128)(2,1)S(1)}, bf16[64,2304]{1,0:T(8,128)(2,1)S(1)}, u32[]{:S(2)}, u32[]{:S(2)}) collective-permute-start(bf16[64,2304]{1,0:T(8,128)(2,1)S(1)} %pad_maximum_fusion.1), channel_id=1, source_target_pairs={{0,8},{1,9},{2,10},{3,11},{4,12},{5,13},{6,14},{7,15},{8,0},{9,1},... | collective-permute-start | bytes 884744 | tf_op jit(solution)/shard_map/ppermute | solution.py:49
  9.3 9.1 %collective-permute-start.6 = (bf16[64,2304]{1,0:T(8,128)(2,1)S(1)}, bf16[64,2304]{1,0:T(8,128)(2,1)S(1)}, u32[]{:S(2)}, u32[]{:S(2)}) collective-permute-start(bf16[64,2304]{1,0:T(8,128)(2,1)S(1)} %pad_maximum_fusion.1), channel_id=1, source_target_pairs={{0,16},{1,17},{2,18},{3,19},{4,20},{5,21},{6,22},{7,23},{8,24},{9,... | collective-permute-start | bytes 884744 | tf_op jit(solution)/shard_map/ppermute | solution.py:49
  12.7 11.5 %collective-permute-start.4 = (bf16[64,768]{1,0:T(8,128)(2,1)}, bf16[64,768]{1,0:T(8,128)(2,1)S(1)}, u32[]{:S(2)}, u32[]{:S(2)}) collective-permute-start(bf16[64,768]{1,0:T(8,128)(2,1)} %param.3), channel_id=1, source_target_pairs={{0,2},{1,3},{2,0},{3,1},{4,6},{5,7},{6,4},{7,5},{8,10},{9,11},{10,... | collective-permute-start | bytes 294920 | tf_op jit(solution)/shard_map/ppermute | solution.py:49
  15.5 8.7 %collective-permute-start.2 = (bf16[64,768]{1,0:T(8,128)(2,1)}, bf16[64,768]{1,0:T(8,128)(2,1)S(1)}, u32[]{:S(2)}, u32[]{:S(2)}) collective-permute-start(bf16[64,768]{1,0:T(8,128)(2,1)} %param.3), channel_id=1, source_target_pairs={{0,1},{1,0},{2,3},{3,2},{4,5},{5,4},{6,7},{7,6},{8,9},{9,8},{10,11... | collective-permute-start | bytes 294920 | tf_op jit(solution)/shard_map/ppermute | solution.py:49
  18.4 3.4 %copy-start.2 = (bf16[64,2304]{1,0:T(8,128)(2,1)}, bf16[64,2304]{1,0:T(8,128)(2,1)S(1)}, u32[]{:S(2)}) copy-start(bf16[64,2304]{1,0:T(8,128)(2,1)S(1)} %collective-permute-done.5) | copy-start | bytes 884740
  18.4 5.7 %collective-permute-start.13 = (bf16[64,1536]{1,0:T(8,128)(2,1)S(1)}, bf16[64,1536]{1,0:T(8,128)(2,1)S(1)}, u32[]{:S(2)}, u32[]{:S(2)}) collective-permute-start(bf16[64,1536]{1,0:T(8,128)(2,1)S(1)} %collective-permute-done.1), channel_id=1, source_target_pairs={{0,16},{1,17},{2,18},{3,19},{4,20},{5,21},{6,22},{7,23},{8,24},{9,... | collective-permute-start | bytes 589832 | tf_op jit(solution)/shard_map/ppermute | solution.py:49
  20.1 4.1 %collective-permute-start.7 = (bf16[192,1536]{1,0:T(8,128)(2,1)S(1)}, bf16[192,1536]{1,0:T(8,128)(2,1)S(1)}, u32[]{:S(2)}, u32[]{:S(2)}) collective-permute-start(bf16[192,1536]{1,0:T(8,128)(2,1)S(1)} %pad_maximum_fusion), channel_id=1, source_target_pairs={{0,4},{1,5},{2,6},{3,7},{4,0},{5,1},{6,2},{7,3},{8,12},{9,13},{10,... | collective-permute-start | bytes 1769480 | tf_op jit(solution)/shard_map/ppermute | solution.py:49
  20.2 7.6 %collective-permute-start.12 = (bf16[64,1536]{1,0:T(8,128)(2,1)S(1)}, bf16[64,1536]{1,0:T(8,128)(2,1)S(1)}, u32[]{:S(2)}, u32[]{:S(2)}) collective-permute-start(bf16[64,1536]{1,0:T(8,128)(2,1)S(1)} %collective-permute-done), channel_id=1, source_target_pairs={{0,8},{1,9},{2,10},{3,11},{4,12},{5,13},{6,14},{7,15},{8,0},{9,1},... | collective-permute-start | bytes 589832 | tf_op jit(solution)/shard_map/ppermute | solution.py:49
  24.2 3.6 %slice-start = ((bf16[64,2304]{1,0:T(8,128)(2,1)}), bf16[64,1536]{1,0:T(8,128)(2,1)S(1)}, s32[]{:S(2)}) async-start(bf16[64,2304]{1,0:T(8,128)(2,1)} %copy-done.2), calls=%async_computation | async-start | bytes 393216 | tf_op jit(solution)/shard_map/slice | solution.py:76
  24.2 3.5 %collective-permute-start.14 = (bf16[64,1536]{1,0:T(8,128)(2,1)S(1)}, bf16[64,1536]{1,0:T(8,128)(2,1)S(1)}, u32[]{:S(2)}, u32[]{:S(2)}) collective-permute-start(bf16[64,1536]{1,0:T(8,128)(2,1)S(1)} %collective-permute-done.13), channel_id=1, source_target_pairs={{0,4},{1,5},{2,6},{3,7},{4,0},{5,1},{6,2},{7,3},{8,12},{9,13},{10,... | collective-permute-start | bytes 589832 | tf_op jit(solution)/shard_map/ppermute | solution.py:49
  24.2 5.3 %collective-permute-start.9 = (bf16[64,768]{1,0:T(8,128)(2,1)S(1)}, bf16[64,768]{1,0:T(8,128)(2,1)S(1)}, u32[]{:S(2)}, u32[]{:S(2)}) collective-permute-start(bf16[64,768]{1,0:T(8,128)(2,1)S(1)} %collective-permute-done.4), channel_id=1, source_target_pairs={{0,16},{1,17},{2,18},{3,19},{4,20},{5,21},{6,22},{7,23},{8,24},{9,... | collective-permute-start | bytes 294920 | tf_op jit(solution)/shard_map/ppermute | solution.py:49
  25.8 3.7 %collective-permute-start.10 = (bf16[128,768]{1,0:T(8,128)(2,1)S(1)}, bf16[128,768]{1,0:T(8,128)(2,1)S(1)}, u32[]{:S(2)}, u32[]{:S(2)}) collective-permute-start(bf16[128,768]{1,0:T(8,128)(2,1)S(1)} %pad_maximum_fusion.2), channel_id=1, source_target_pairs={{0,4},{1,5},{2,6},{3,7},{4,0},{5,1},{6,2},{7,3},{8,12},{9,13},{10,... | collective-permute-start | bytes 589832 | tf_op jit(solution)/shard_map/ppermute | solution.py:49
  26.1 5.0 %collective-permute-start.8 = (bf16[64,768]{1,0:T(8,128)(2,1)S(1)}, bf16[64,768]{1,0:T(8,128)(2,1)S(1)}, u32[]{:S(2)}, u32[]{:S(2)}) collective-permute-start(bf16[64,768]{1,0:T(8,128)(2,1)S(1)} %collective-permute-done.2), channel_id=1, source_target_pairs={{0,8},{1,9},{2,10},{3,11},{4,12},{5,13},{6,14},{7,15},{8,0},{9,1},... | collective-permute-start | bytes 294920 | tf_op jit(solution)/shard_map/ppermute | solution.py:49
  27.7 3.4 %copy-start.1 = (bf16[64,768]{1,0:T(8,128)(2,1)S(1)}, bf16[64,768]{1,0:T(8,128)(2,1)}, u32[]{:S(2)}) copy-start(bf16[64,768]{1,0:T(8,128)(2,1)} %param.3) | copy-start | bytes 294916
  27.7 3.4 %slice-start.1 = ((bf16[64,2304]{1,0:T(8,128)(2,1)}), bf16[64,768]{1,0:T(8,128)(2,1)S(1)}, s32[]{:S(2)}) async-start(bf16[64,2304]{1,0:T(8,128)(2,1)} %copy-done.2), calls=%async_computation.1 | async-start | bytes 196608 | tf_op jit(solution)/shard_map/slice | solution.py:76
  29.5 1.3 %collective-permute-start.11 = (bf16[64,768]{1,0:T(8,128)(2,1)S(1)}, bf16[64,768]{1,0:T(8,128)(2,1)S(1)}, u32[]{:S(2)}, u32[]{:S(2)}) collective-permute-start(bf16[64,768]{1,0:T(8,128)(2,1)S(1)} %collective-permute-done.9), channel_id=1, source_target_pairs={{0,4},{1,5},{2,6},{3,7},{4,0},{5,1},{6,2},{7,3},{8,12},{9,13},{10,... | collective-permute-start | bytes 294920 | tf_op jit(solution)/shard_map/ppermute | solution.py:49
  32.1 5.0 %collective-permute-start.16 = (f32[3,8,64]{2,1,0:T(8,128)S(1)}, f32[3,8,64]{2,1,0:T(8,128)S(1)}, u32[]{:S(2)}, u32[]{:S(2)}) collective-permute-start(f32[3,8,64]{2,1,0:T(8,128)S(1)} %constant_dynamic-update-slice_fusion.16), channel_id=1, source_target_pairs={{0,2},{1,3},{2,0},{3,1},{4,6},{5,7},{6,4},{7,5},{8,10},{9,11},{10,... | collective-permute-start | bytes 18440 | tf_op jit(solution)/shard_map/ppermute | solution.py:49
  37.1 3.8 %collective-permute-start.18 = (f32[3,8,64]{2,1,0:T(8,128)S(1)}, f32[3,8,64]{2,1,0:T(8,128)S(1)}, u32[]{:S(2)}, u32[]{:S(2)}) collective-permute-start(f32[3,8,64]{2,1,0:T(8,128)S(1)} %add.41), channel_id=1, source_target_pairs={{0,16},{1,17},{2,18},{3,19},{4,20},{5,21},{6,22},{7,23},{8,24},{9,... | collective-permute-start | bytes 18440 | tf_op jit(solution)/shard_map/ppermute | solution.py:49
  38.4 3.6 %collective-permute-start.15 = (f32[3,4,64]{2,1,0:T(4,128)S(1)}, f32[3,4,64]{2,1,0:T(4,128)S(1)}, u32[]{:S(2)}, u32[]{:S(2)}) collective-permute-start(f32[3,4,64]{2,1,0:T(4,128)S(1)} %constant_dynamic-update-slice_fusion.13), channel_id=1, source_target_pairs={{0,1},{1,0},{2,3},{3,2},{4,5},{5,4},{6,7},{7,6},{8,9},{9,8},{10,11... | collective-permute-start | bytes 9224 | tf_op jit(solution)/shard_map/ppermute | solution.py:49
  40.9 5.1 %collective-permute-start.19 = (f32[3,8,64]{2,1,0:T(8,128)S(1)}, f32[3,8,64]{2,1,0:T(8,128)S(1)}, u32[]{:S(2)}, u32[]{:S(2)}) collective-permute-start(f32[3,8,64]{2,1,0:T(8,128)S(1)} %add.43), channel_id=1, source_target_pairs={{0,4},{1,5},{2,6},{3,7},{4,0},{5,1},{6,2},{7,3},{8,12},{9,13},{10,... | collective-permute-start | bytes 18440 | tf_op jit(solution)/shard_map/ppermute | solution.py:49
  42.1 3.7 %collective-permute-start.17 = (f32[3,4,64]{2,1,0:T(4,128)S(1)}, f32[3,4,64]{2,1,0:T(4,128)S(1)}, u32[]{:S(2)}, u32[]{:S(2)}) collective-permute-start(f32[3,4,64]{2,1,0:T(4,128)S(1)} %add.40), channel_id=1, source_target_pairs={{0,8},{1,9},{2,10},{3,11},{4,12},{5,13},{6,14},{7,15},{8,0},{9,1},... | collective-permute-start | bytes 9224 | tf_op jit(solution)/shard_map/ppermute | solution.py:49
  47.0 5.2 %collective-permute-start.20 = (f16[64,896]{1,0:T(8,128)(2,1)S(1)}, f16[64,896]{1,0:T(8,128)(2,1)S(1)}, u32[]{:S(2)}, u32[]{:S(2)}) collective-permute-start(f16[64,896]{1,0:T(8,128)(2,1)S(1)} %convert_element_type.18), channel_id=1, source_target_pairs={{0,1},{1,0},{2,3},{3,2},{4,5},{5,4},{6,7},{7,6},{8,9},{9,8},{10,11... | collective-permute-start | bytes 344072 | tf_op jit(solution)/shard_map/ppermute | solution.py:49
  47.8 5.4 %collective-permute-start.21 = (f16[64,896]{1,0:T(8,128)(2,1)S(1)}, f16[64,896]{1,0:T(8,128)(2,1)S(1)}, u32[]{:S(2)}, u32[]{:S(2)}) collective-permute-start(f16[64,896]{1,0:T(8,128)(2,1)S(1)} %convert_element_type.20), channel_id=1, source_target_pairs={{0,8},{1,9},{2,10},{3,11},{4,12},{5,13},{6,14},{7,15},{8,0},{9,1},... | collective-permute-start | bytes 344072 | tf_op jit(solution)/shard_map/ppermute | solution.py:49
  49.5 5.8 %collective-permute-start.22 = (f16[64,896]{1,0:T(8,128)(2,1)S(1)}, f16[64,896]{1,0:T(8,128)(2,1)S(1)}, u32[]{:S(2)}, u32[]{:S(2)}) collective-permute-start(f16[64,896]{1,0:T(8,128)(2,1)S(1)} %convert_element_type.22), channel_id=1, source_target_pairs={{0,9},{1,8},{2,11},{3,10},{4,13},{5,12},{6,15},{7,14},{8,1},{9,0},... | collective-permute-start | bytes 344072 | tf_op jit(solution)/shard_map/ppermute | solution.py:49

commit v8 on v7

--- a/solution.py
+++ b/solution.py
@@ -64,37 +64,44 @@
     *plane_masks, core_mask = col_masks
     row_t, col_t = {0: teacher}, {0: teacher}
     row_s, col_s = {0: student}, {0: student}
-    core_t, core_s = [], []
+    core_t, core_s = {}, {}
     width = teacher.shape[1]
-    core_s.append((0, send(student, core_mask, count)))
-    both = after(jnp.concatenate([teacher, student], 1), core_s[0])
-    row_t[1], col_t[1] = send(teacher, row_masks[0], count), send(teacher, plane_masks[0], count)
-    for side_t, side_s, masks in ((row_t, row_s, row_masks), (col_t, col_s, plane_masks)):
+    sides = ((row_t, row_s, row_masks), (col_t, col_s, plane_masks))
+
+    def to_core(places):
+        got = send(jnp.concatenate([col[p] for col, _, p in places], 1), core_mask, count)
+        start = 0
+        for col, core, p in places:
+            end = start + col[p].shape[1]
+            core[p] = got[:, start:end]
+            start = end
+
+    col_s[1], row_s[1] = send(student, plane_masks[0], count), send(student, row_masks[0], count)
+    core_s[0] = send(student, core_mask, count)
+    col_t[1], row_t[1] = send(teacher, plane_masks[0], count), send(teacher, row_masks[0], count)
+    both = after(jnp.concatenate([teacher, student], 1), (row_s[1], col_s[1], core_s[0]))
+    arrived = []
+    for side_t, side_s, masks in sides:
         for b, mask in enumerate(masks):
             if b:
                 got = send(both, mask, count)
                 side_t[1 << b], side_s[1 << b] = got[:, :width], got[:, width:]
-    col_s[1] = send(after(student, core_s[0]), plane_masks[0], count)
-    row_t[1], col_t[1], late = lax.optimization_barrier((row_t[1], col_t[1], student))
-    row_s[1] = send(late, row_masks[0], count)
-    early = (row_t[2], col_t[2], row_s[2], col_s[2])
-
-    for row, col, core in ((row_t, col_t, core_t), (row_s, col_s, core_s)):
-        row[1], col[1] = after((row[1], col[1]), early)
-        for level in range(1, len(row_masks) + 1):
-            if level > 1:
-                forward(row, row_masks, level, count)
-                forward(col, plane_masks, level, count)
-            ready = [p for p in range(1 << len(plane_masks)) if max(p.bit_count(), 1) == level]
-            ready = [p for p in ready if p or core is core_t]
-            if ready:
-                got = send(jnp.concatenate([col[p] for p in ready]), core_mask, count)
-                core += zip(ready, jnp.split(got, len(ready)))
-                if level == 1:
-                    early = got
+                arrived.append(got)
+    others = [1 << b for b in range(1, len(plane_masks))]
+    to_core([(col_t, core_t, p) for p in [0] + others] + [(col_s, core_s, p) for p in [1] + others])
+    for level in range(2, len(row_masks) + 1):
+        forward(row_s, row_masks, level, count)
+        forward(col_s, plane_masks, level, count)
+    row_t[1], col_t[1] = after((row_t[1], col_t[1]), arrived)
+    rest = [p for p in range(1 << len(plane_masks)) if p.bit_count() > 1]
+    to_core([(col_t, core_t, 1)] + [(col_s, core_s, p) for p in rest])
+    for level in range(2, len(row_masks) + 1):
+        forward(row_t, row_masks, level, count)
+        forward(col_t, plane_masks, level, count)
+    to_core([(col_t, core_t, p) for p in rest])
     out = []
     for row, col, core in ((row_t, col_t, core_t), (row_s, col_s, core_s)):
-        col = [col[p] for p in sorted(col)] + [piece for _, piece in sorted(core, key=lambda c: c[0])]
+        col = [col[p] for p in sorted(col)] + [core[p] for p in sorted(core)]
         out.append((jnp.concatenate([row[p] for p in sorted(row)]), jnp.concatenate(col)))
     return out
 

time: 56.2 us -> 58.2 us (1.036)
  waiting for transfers between devices: 18.9 us -> 22.1 us
  starting transfers between devices: 29.1 us -> 27.9 us
    ppermute x23 -> x22, waiting for transfers between devices: 18.9 us -> 22.1 us  [send(): return lax.ppermute(value, AXES, [(i, i ^ mask) for i in range(count)])]
    ppermute x23 -> x22, starting transfers between devices: 29.1 us -> 27.9 us  [send(): return lax.ppermute(value, AXES, [(i, i ^ mask) for i in range(count)])]
    unnamed x21 -> x23, local copies, waits for them, and re-layouts: 2.01 us -> 2.02 us
  transfers between devices with their start and end apart: 23 -> 22, of which waited for: 13 -> 12; matrix products, arithmetic and copies ran while one was open for 7% -> 7% of each run, Pallas kernels for 0% -> 0%
where the time goes in v8:
time: 58.2 us; the launch traced here: 58 us
  starting transfers between devices  27.9 us (48%)
  waiting for transfers between devices  22.1 us (38%)
  local copies, waits for them, and re-layouts  2.97 us (5%)
  Pallas kernels  1.7 us (3%)
  other arithmetic  1.22 us (2%)
  matrix products  1.16 us (2%)
  between operations  0.94 us (2%)
    ppermute x22, starting transfers between devices, send(): return lax.ppermute(value, AXES, [(i, i ^ mask) for i in range(count)])  27.9 us
    ppermute x22, waiting for transfers between devices, send(): return lax.ppermute(value, AXES, [(i, i ^ mask) for i in range(count)])  22.1 us
    unnamed x23, local copies, waits for them, and re-layouts  2.02 us
  transfers between devices with their start and end apart: 22, of which 12 were waited for; matrix products, arithmetic and copies ran while one was open for 7% of the time, Pallas kernels for 0%

profile of v8, /device:TPU:0, one launch (start us, length us, event | category | flops | bytes accessed | tf_op | source)
XLA Modules:
  0.0 58.0 jit_solution(3732084782776895759)
XLA Ops:
  0.6 4.1 %collective-permute-start.1 = (bf16[64,768]{1,0:T(8,128)(2,1)}, bf16[64,768]{1,0:T(8,128)(2,1)S(1)}, u32[]{:S(2)}, u32[]{:S(2)}) collective-permute-start(bf16[64,768]{1,0:T(8,128)(2,1)} %param.3), channel_id=1, source_target_pairs={{0,2},{1,3},{2,0},{3,1},{4,6},{5,7},{6,4},{7,5},{8,10},{9,11},{10,... | collective-permute-start | bytes 294920 | tf_op jit(solution)/shard_map/ppermute | solution.py:49
  4.7 1.6 %collective-permute-start = (bf16[64,768]{1,0:T(8,128)(2,1)}, bf16[64,768]{1,0:T(8,128)(2,1)S(1)}, u32[]{:S(2)}, u32[]{:S(2)}) collective-permute-start(bf16[64,768]{1,0:T(8,128)(2,1)} %param.3), channel_id=1, source_target_pairs={{0,1},{1,0},{2,3},{3,2},{4,5},{5,4},{6,7},{7,6},{8,9},{9,8},{10,11... | collective-permute-start | bytes 294920 | tf_op jit(solution)/shard_map/ppermute | solution.py:49
  6.9 1.0 %pad_maximum_fusion.1 = bf16[64,2304]{1,0:T(8,128)(2,1)S(1)} fusion(bf16[64,768]{1,0:T(8,128)(2,1)} %param.3, bf16[64,1536]{1,0:T(8,128)(2,1)} %param.2), kind=kLoop, calls=%fused_computation.21 | loop fusion | flops 589824 | bytes 589824 | tf_op jit(solution)/shard_map/concatenate | solution.py:82
  7.9 1.9 %collective-permute-done.1 = bf16[64,768]{1,0:T(8,128)(2,1)S(1)} collective-permute-done((bf16[64,768]{1,0:T(8,128)(2,1)}, bf16[64,768]{1,0:T(8,128)(2,1)S(1)}, u32[]{:S(2)}, u32[]{:S(2)}) %collective-permute-start.1) | collective-permute-done | bytes 98336 | tf_op jit(solution)/shard_map/ppermute | solution.py:49
  9.7 0.9 %collective-permute-done = bf16[64,768]{1,0:T(8,128)(2,1)S(1)} collective-permute-done((bf16[64,768]{1,0:T(8,128)(2,1)}, bf16[64,768]{1,0:T(8,128)(2,1)S(1)}, u32[]{:S(2)}, u32[]{:S(2)}) %collective-permute-start) | collective-permute-done | bytes 98336 | tf_op jit(solution)/shard_map/ppermute | solution.py:49
  10.7 1.6 %collective-permute-start.3 = (bf16[64,2304]{1,0:T(8,128)(2,1)S(1)}, bf16[64,2304]{1,0:T(8,128)(2,1)S(1)}, u32[]{:S(2)}, u32[]{:S(2)}) collective-permute-start(bf16[64,2304]{1,0:T(8,128)(2,1)S(1)} %pad_maximum_fusion.1), channel_id=1, source_target_pairs={{0,8},{1,9},{2,10},{3,11},{4,12},{5,13},{6,14},{7,15},{8,0},{9,1},... | collective-permute-start | bytes 884744 | tf_op jit(solution)/shard_map/ppermute | solution.py:49
  12.2 1.5 %collective-permute-start.5 = (bf16[64,2304]{1,0:T(8,128)(2,1)S(1)}, bf16[64,2304]{1,0:T(8,128)(2,1)S(1)}, u32[]{:S(2)}, u32[]{:S(2)}) collective-permute-start(bf16[64,2304]{1,0:T(8,128)(2,1)S(1)} %pad_maximum_fusion.1), channel_id=1, source_target_pairs={{0,16},{1,17},{2,18},{3,19},{4,20},{5,21},{6,22},{7,23},{8,24},{9,... | collective-permute-start | bytes 884744 | tf_op jit(solution)/shard_map/ppermute | solution.py:49
  13.7 0.9 %constant_dynamic-update-slice_fusion.9 = bf16[512,1536]{1,0:T(8,128)(2,1)S(1)} fusion(bf16[64,1536]{1,0:T(8,128)(2,1)} %param.2), kind=kLoop, calls=%fused_computation.40 | loop fusion | bytes 393216
  14.7 0.9 %constant_dynamic-update-slice_fusion.4 = bf16[512,768]{1,0:T(8,128)(2,1)S(1)} fusion(bf16[64,768]{1,0:T(8,128)(2,1)} %param.3), kind=kLoop, calls=%fused_computation.35 | loop fusion | bytes 196608
  16.1 2.5 %collective-permute-done.8 = bf16[64,1536]{1,0:T(8,128)(2,1)S(1)} collective-permute-done((bf16[64,1536]{1,0:T(8,128)(2,1)}, bf16[64,1536]{1,0:T(8,128)(2,1)S(1)}, u32[]{:S(2)}, u32[]{:S(2)}) %collective-permute-start.8) | collective-permute-done | bytes 196640 | tf_op jit(solution)/shard_map/ppermute | solution.py:49
  18.6 1.5 %collective-permute-start.4 = (bf16[64,768]{1,0:T(8,128)(2,1)S(1)}, bf16[64,768]{1,0:T(8,128)(2,1)S(1)}, u32[]{:S(2)}, u32[]{:S(2)}) collective-permute-start(bf16[64,768]{1,0:T(8,128)(2,1)S(1)} %collective-permute-done), channel_id=1, source_target_pairs={{0,8},{1,9},{2,10},{3,11},{4,12},{5,13},{6,14},{7,15},{8,0},{9,1},... | collective-permute-start | bytes 294920 | tf_op jit(solution)/shard_map/ppermute | solution.py:49
  20.2 1.6 %collective-permute-start.12 = (bf16[64,1536]{1,0:T(8,128)(2,1)S(1)}, bf16[64,1536]{1,0:T(8,128)(2,1)S(1)}, u32[]{:S(2)}, u32[]{:S(2)}) collective-permute-start(bf16[64,1536]{1,0:T(8,128)(2,1)S(1)} %collective-permute-done.9), channel_id=1, source_target_pairs={{0,16},{1,17},{2,18},{3,19},{4,20},{5,21},{6,22},{7,23},{8,24},{9,... | collective-permute-start | bytes 589832 | tf_op jit(solution)/shard_map/ppermute | solution.py:49
  23.1 3.3 %collective-permute-done.12 = bf16[64,1536]{1,0:T(8,128)(2,1)S(1)} collective-permute-done((bf16[64,1536]{1,0:T(8,128)(2,1)S(1)}, bf16[64,1536]{1,0:T(8,128)(2,1)S(1)}, u32[]{:S(2)}, u32[]{:S(2)}) %collective-permute-start.12) | collective-permute-done | bytes 196640 | tf_op jit(solution)/shard_map/ppermute | solution.py:49
  26.5 1.3 %collective-permute-done.13 = bf16[64,1536]{1,0:T(8,128)(2,1)S(1)} collective-permute-done((bf16[64,1536]{1,0:T(8,128)(2,1)S(1)}, bf16[64,1536]{1,0:T(8,128)(2,1)S(1)}, u32[]{:S(2)}, u32[]{:S(2)}) %collective-permute-start.13) | collective-permute-done | bytes 196640 | tf_op jit(solution)/shard_map/ppermute | solution.py:49
  27.9 1.6 %collective-permute-done.11 = bf16[64,1536]{1,0:T(8,128)(2,1)S(1)} collective-permute-done((bf16[64,1536]{1,0:T(8,128)(2,1)S(1)}, bf16[64,1536]{1,0:T(8,128)(2,1)S(1)}, u32[]{:S(2)}, u32[]{:S(2)}) %collective-permute-start.11) | collective-permute-done | bytes 196640 | tf_op jit(solution)/shard_map/ppermute | solution.py:49
  29.5 0.6 %fusion.gram_t = f32[256,512]{1,0:T(8,128)S(1)} fusion(bf16[512,1536]{1,0:T(8,128)(2,1)S(1)} %constant_dynamic-update-slice_fusion.5, bf16[64,1536]{1,0:T(8,128)(2,1)S(1)} %collective-permute-done.11, bf16[64,1536]{1,0:T(8,128)(2,1)S(1)} %slice-done, bf16[64,1536]{1,0:T(8,128)(2,1)S(1)} %collective-permute-done.8, bf16[64,1536]{1,0:T(8,128)(2,1)S(1)} %copy-done), kind=kOutput, calls=%fused_computation | convolution fusion | flops 405798912 | bytes 2883584 | tf_op jit(solution)/shard_map/rd,cd->rc/dot_general | solution.py:172
  30.1 0.6 multiply_reduce_fusion.4
  30.9 4.9 %collective-permute-start.15 = (f32[3,8,64]{2,1,0:T(8,128)S(1)}, f32[3,8,64]{2,1,0:T(8,128)S(1)}, u32[]{:S(2)}, u32[]{:S(2)}) collective-permute-start(f32[3,8,64]{2,1,0:T(8,128)S(1)} %constant_dynamic-update-slice_fusion.13), channel_id=1, source_target_pairs={{0,2},{1,3},{2,0},{3,1},{4,6},{5,7},{6,4},{7,5},{8,10},{9,11},{10,... | collective-permute-start | bytes 18440 | tf_op jit(solution)/shard_map/ppermute | solution.py:49
  36.0 1.4 %collective-permute-done.15 = f32[3,8,64]{2,1,0:T(8,128)S(1)} collective-permute-done((f32[3,8,64]{2,1,0:T(8,128)S(1)}, f32[3,8,64]{2,1,0:T(8,128)S(1)}, u32[]{:S(2)}, u32[]{:S(2)}) %collective-permute-start.15) | collective-permute-done | bytes 6176 | tf_op jit(solution)/shard_map/ppermute | solution.py:49
  37.5 1.6 %collective-permute-start.17 = (f32[3,8,64]{2,1,0:T(8,128)S(1)}, f32[3,8,64]{2,1,0:T(8,128)S(1)}, u32[]{:S(2)}, u32[]{:S(2)}) collective-permute-start(f32[3,8,64]{2,1,0:T(8,128)S(1)} %add.41), channel_id=1, source_target_pairs={{0,16},{1,17},{2,18},{3,19},{4,20},{5,21},{6,22},{7,23},{8,24},{9,... | collective-permute-start | bytes 18440 | tf_op jit(solution)/shard_map/ppermute | solution.py:49
  39.1 3.0 %collective-permute-start.14 = (f32[3,4,64]{2,1,0:T(4,128)S(1)}, f32[3,4,64]{2,1,0:T(4,128)S(1)}, u32[]{:S(2)}, u32[]{:S(2)}) collective-permute-start(f32[3,4,64]{2,1,0:T(4,128)S(1)} %constant_dynamic-update-slice_fusion.10), channel_id=1, source_target_pairs={{0,1},{1,0},{2,3},{3,2},{4,5},{5,4},{6,7},{7,6},{8,9},{9,8},{10,11... | collective-permute-start | bytes 9224 | tf_op jit(solution)/shard_map/ppermute | solution.py:49
  42.2 1.5 %collective-permute-done.14 = f32[3,4,64]{2,1,0:T(4,128)S(1)} collective-permute-done((f32[3,4,64]{2,1,0:T(4,128)S(1)}, f32[3,4,64]{2,1,0:T(4,128)S(1)}, u32[]{:S(2)}, u32[]{:S(2)}) %collective-permute-start.14) | collective-permute-done | bytes 3104 | tf_op jit(solution)/shard_map/ppermute | solution.py:49
  43.7 0.6 %collective-permute-start.16 = (f32[3,4,64]{2,1,0:T(4,128)S(1)}, f32[3,4,64]{2,1,0:T(4,128)S(1)}, u32[]{:S(2)}, u32[]{:S(2)}) collective-permute-start(f32[3,4,64]{2,1,0:T(4,128)S(1)} %add.40), channel_id=1, source_target_pairs={{0,8},{1,9},{2,10},{3,11},{4,12},{5,13},{6,14},{7,15},{8,0},{9,1},... | collective-permute-start | bytes 9224 | tf_op jit(solution)/shard_map/ppermute | solution.py:49
  44.4 3.0 %collective-permute-done.16 = f32[3,4,64]{2,1,0:T(4,128)S(1)} collective-permute-done((f32[3,4,64]{2,1,0:T(4,128)S(1)}, f32[3,4,64]{2,1,0:T(4,128)S(1)}, u32[]{:S(2)}, u32[]{:S(2)}) %collective-permute-start.16) | collective-permute-done | bytes 3104 | tf_op jit(solution)/shard_map/ppermute | solution.py:49
  47.7 0.9 %shard_map.41 = (f32[64,768]{1,0:T(8,128)S(1)}, f32[8,128]{1,0:T(8,128)S(1)}, f32[64,896]{1,0:T(8,128)S(1)}, f32[64,896]{1,0:T(8,128)S(1)}, f32[64,896]{1,0:T(8,128)S(1)}) custom-call(f32[256,512]{1,0:T(8,128)S(1)} %get-tuple-element.36.gram_s, f32[256,512]{1,0:T(8,128)S(1)} %fusion.gram_t, f32[3,1,256]{2,1,0:T(1,128)S(1)} %reshape.136.row_sum, ...), custom_call_target="tpu_custom_call" | custom-call | tf_op jit(solution)/shard_map/pallas_call | solution.py:185
  48.7 2.1 %collective-permute-start.19 = (f16[64,896]{1,0:T(8,128)(2,1)S(1)}, f16[64,896]{1,0:T(8,128)(2,1)S(1)}, u32[]{:S(2)}, u32[]{:S(2)}) collective-permute-start(f16[64,896]{1,0:T(8,128)(2,1)S(1)} %convert_element_type.18), channel_id=1, source_target_pairs={{0,1},{1,0},{2,3},{3,2},{4,5},{5,4},{6,7},{7,6},{8,9},{9,8},{10,11... | collective-permute-start | bytes 344072 | tf_op jit(solution)/shard_map/ppermute | solution.py:49
  50.8 0.6 %collective-permute-start.20 = (f16[64,896]{1,0:T(8,128)(2,1)S(1)}, f16[64,896]{1,0:T(8,128)(2,1)S(1)}, u32[]{:S(2)}, u32[]{:S(2)}) collective-permute-start(f16[64,896]{1,0:T(8,128)(2,1)S(1)} %convert_element_type.20), channel_id=1, source_target_pairs={{0,8},{1,9},{2,10},{3,11},{4,12},{5,13},{6,14},{7,15},{8,0},{9,1},... | collective-permute-start | bytes 344072 | tf_op jit(solution)/shard_map/ppermute | solution.py:49
  51.4 1.0 %collective-permute-start.21 = (f16[64,896]{1,0:T(8,128)(2,1)S(1)}, f16[64,896]{1,0:T(8,128)(2,1)S(1)}, u32[]{:S(2)}, u32[]{:S(2)}) collective-permute-start(f16[64,896]{1,0:T(8,128)(2,1)S(1)} %convert_element_type.22), channel_id=1, source_target_pairs={{0,9},{1,8},{2,11},{3,10},{4,13},{5,12},{6,15},{7,14},{8,1},{9,0},... | collective-permute-start | bytes 344072 | tf_op jit(solution)/shard_map/ppermute | solution.py:49
  52.4 1.9 %collective-permute-done.19 = f16[64,896]{1,0:T(8,128)(2,1)S(1)} collective-permute-done((f16[64,896]{1,0:T(8,128)(2,1)S(1)}, f16[64,896]{1,0:T(8,128)(2,1)S(1)}, u32[]{:S(2)}, u32[]{:S(2)}) %collective-permute-start.19) | collective-permute-done | bytes 114720 | tf_op jit(solution)/shard_map/ppermute | solution.py:49
  54.3 1.6 %collective-permute-done.20 = f16[64,896]{1,0:T(8,128)(2,1)S(1)} collective-permute-done((f16[64,896]{1,0:T(8,128)(2,1)S(1)}, f16[64,896]{1,0:T(8,128)(2,1)S(1)}, u32[]{:S(2)}, u32[]{:S(2)}) %collective-permute-start.20) | collective-permute-done | bytes 114720 | tf_op jit(solution)/shard_map/ppermute | solution.py:49
  56.0 1.2 %collective-permute-done.21 = f16[64,896]{1,0:T(8,128)(2,1)S(1)} collective-permute-done((f16[64,896]{1,0:T(8,128)(2,1)S(1)}, f16[64,896]{1,0:T(8,128)(2,1)S(1)}, u32[]{:S(2)}, u32[]{:S(2)}) %collective-permute-start.21) | collective-permute-done | bytes 114720 | tf_op jit(solution)/shard_map/ppermute | solution.py:49
  57.2 0.8 %shard_map.42 = (f32[64,768]{1,0:T(8,128)}, f32[1,1]{1,0:T(1,128)}) custom-call(f32[64,768]{1,0:T(8,128)S(1)} %get-tuple-element.19.own, f32[8,128]{1,0:T(8,128)S(1)} %get-tuple-element.20.share, f32[64,896]{1,0:T(8,128)S(1)} %convert_element_type.19.refs_0_, f32[64,896]{1,0:T(8,128)S(1)} %convert_element_type.21.refs_1_, ...), custom_call_target="tpu_custom_call" | custom-call | tf_op jit(solution)/shard_map/pallas_call | solution.py:198
  (77 shorter events, 3.6 us)
Async XLA Ops:
  0.6 21.2 %copy-start = (bf16[64,1536]{1,0:T(8,128)(2,1)S(1)}, bf16[64,1536]{1,0:T(8,128)(2,1)}, u32[]{:S(2)}) copy-start(bf16[64,1536]{1,0:T(8,128)(2,1)} %param.2) | copy-start | bytes 589828
  0.6 9.1 %collective-permute-start.1 = (bf16[64,768]{1,0:T(8,128)(2,1)}, bf16[64,768]{1,0:T(8,128)(2,1)S(1)}, u32[]{:S(2)}, u32[]{:S(2)}) collective-permute-start(bf16[64,768]{1,0:T(8,128)(2,1)} %param.3), channel_id=1, source_target_pairs={{0,2},{1,3},{2,0},{3,1},{4,6},{5,7},{6,4},{7,5},{8,10},{9,11},{10,... | collective-permute-start | bytes 294920 | tf_op jit(solution)/shard_map/ppermute | solution.py:49
  4.7 5.9 %collective-permute-start = (bf16[64,768]{1,0:T(8,128)(2,1)}, bf16[64,768]{1,0:T(8,128)(2,1)S(1)}, u32[]{:S(2)}, u32[]{:S(2)}) collective-permute-start(bf16[64,768]{1,0:T(8,128)(2,1)} %param.3), channel_id=1, source_target_pairs={{0,1},{1,0},{2,3},{3,2},{4,5},{5,4},{6,7},{7,6},{8,9},{9,8},{10,11... | collective-permute-start | bytes 294920 | tf_op jit(solution)/shard_map/ppermute | solution.py:49
  6.3 4.3 %collective-permute-start.2 = (bf16[64,768]{1,0:T(8,128)(2,1)}, bf16[64,768]{1,0:T(8,128)(2,1)S(1)}, u32[]{:S(2)}, u32[]{:S(2)}) collective-permute-start(bf16[64,768]{1,0:T(8,128)(2,1)} %param.3), channel_id=1, source_target_pairs={{0,4},{1,5},{2,6},{3,7},{4,0},{5,1},{6,2},{7,3},{8,12},{9,13},{10,... | collective-permute-start | bytes 294920 | tf_op jit(solution)/shard_map/ppermute | solution.py:49
  6.3 12.3 %collective-permute-start.8 = (bf16[64,1536]{1,0:T(8,128)(2,1)}, bf16[64,1536]{1,0:T(8,128)(2,1)S(1)}, u32[]{:S(2)}, u32[]{:S(2)}) collective-permute-start(bf16[64,1536]{1,0:T(8,128)(2,1)} %param.2), channel_id=1, source_target_pairs={{0,1},{1,0},{2,3},{3,2},{4,5},{5,4},{6,7},{7,6},{8,9},{9,8},{10,11... | collective-permute-start | bytes 589832 | tf_op jit(solution)/shard_map/ppermute | solution.py:49
  6.8 13.4 %collective-permute-start.9 = (bf16[64,1536]{1,0:T(8,128)(2,1)}, bf16[64,1536]{1,0:T(8,128)(2,1)S(1)}, u32[]{:S(2)}, u32[]{:S(2)}) collective-permute-start(bf16[64,1536]{1,0:T(8,128)(2,1)} %param.2), channel_id=1, source_target_pairs={{0,2},{1,3},{2,0},{3,1},{4,6},{5,7},{6,4},{7,5},{8,10},{9,11},{10,... | collective-permute-start | bytes 589832 | tf_op jit(solution)/shard_map/ppermute | solution.py:49
  10.7 9.5 %collective-permute-start.3 = (bf16[64,2304]{1,0:T(8,128)(2,1)S(1)}, bf16[64,2304]{1,0:T(8,128)(2,1)S(1)}, u32[]{:S(2)}, u32[]{:S(2)}) collective-permute-start(bf16[64,2304]{1,0:T(8,128)(2,1)S(1)} %pad_maximum_fusion.1), channel_id=1, source_target_pairs={{0,8},{1,9},{2,10},{3,11},{4,12},{5,13},{6,14},{7,15},{8,0},{9,1},... | collective-permute-start | bytes 884744 | tf_op jit(solution)/shard_map/ppermute | solution.py:49
  12.2 7.9 %collective-permute-start.5 = (bf16[64,2304]{1,0:T(8,128)(2,1)S(1)}, bf16[64,2304]{1,0:T(8,128)(2,1)S(1)}, u32[]{:S(2)}, u32[]{:S(2)}) collective-permute-start(bf16[64,2304]{1,0:T(8,128)(2,1)S(1)} %pad_maximum_fusion.1), channel_id=1, source_target_pairs={{0,16},{1,17},{2,18},{3,19},{4,20},{5,21},{6,22},{7,23},{8,24},{9,... | collective-permute-start | bytes 884744 | tf_op jit(solution)/shard_map/ppermute | solution.py:49
  15.6 6.4 %collective-permute-start.6 = (bf16[64,768]{1,0:T(8,128)(2,1)S(1)}, bf16[64,768]{1,0:T(8,128)(2,1)S(1)}, u32[]{:S(2)}, u32[]{:S(2)}) collective-permute-start(bf16[64,768]{1,0:T(8,128)(2,1)S(1)} %collective-permute-done.1), channel_id=1, source_target_pairs={{0,16},{1,17},{2,18},{3,19},{4,20},{5,21},{6,22},{7,23},{8,24},{9,... | collective-permute-start | bytes 294920 | tf_op jit(solution)/shard_map/ppermute | solution.py:49
  18.6 11.5 %collective-permute-start.4 = (bf16[64,768]{1,0:T(8,128)(2,1)S(1)}, bf16[64,768]{1,0:T(8,128)(2,1)S(1)}, u32[]{:S(2)}, u32[]{:S(2)}) collective-permute-start(bf16[64,768]{1,0:T(8,128)(2,1)S(1)} %collective-permute-done), channel_id=1, source_target_pairs={{0,8},{1,9},{2,10},{3,11},{4,12},{5,13},{6,14},{7,15},{8,0},{9,1},... | collective-permute-start | bytes 294920 | tf_op jit(solution)/shard_map/ppermute | solution.py:49
  20.2 2.9 %copy-start.2 = (bf16[64,2304]{1,0:T(8,128)(2,1)}, bf16[64,2304]{1,0:T(8,128)(2,1)S(1)}, u32[]{:S(2)}) copy-start(bf16[64,2304]{1,0:T(8,128)(2,1)S(1)} %collective-permute-done.3) | copy-start | bytes 884740
  20.2 6.2 %collective-permute-start.12 = (bf16[64,1536]{1,0:T(8,128)(2,1)S(1)}, bf16[64,1536]{1,0:T(8,128)(2,1)S(1)}, u32[]{:S(2)}, u32[]{:S(2)}) collective-permute-start(bf16[64,1536]{1,0:T(8,128)(2,1)S(1)} %collective-permute-done.9), channel_id=1, source_target_pairs={{0,16},{1,17},{2,18},{3,19},{4,20},{5,21},{6,22},{7,23},{8,24},{9,... | collective-permute-start | bytes 589832 | tf_op jit(solution)/shard_map/ppermute | solution.py:49
  21.9 4.5 %collective-permute-start.7 = (bf16[64,4608]{1,0:T(8,128)(2,1)S(1)}, bf16[64,4608]{1,0:T(8,128)(2,1)S(1)}, u32[]{:S(2)}, u32[]{:S(2)}) collective-permute-start(bf16[64,4608]{1,0:T(8,128)(2,1)S(1)} %pad_maximum_fusion), channel_id=1, source_target_pairs={{0,4},{1,5},{2,6},{3,7},{4,0},{5,1},{6,2},{7,3},{8,12},{9,13},{10,... | collective-permute-start | bytes 1769480 | tf_op jit(solution)/shard_map/ppermute | solution.py:49
  22.0 4.4 %collective-permute-start.10 = (bf16[64,2304]{1,0:T(8,128)(2,1)S(1)}, bf16[64,2304]{1,0:T(8,128)(2,1)S(1)}, u32[]{:S(2)}, u32[]{:S(2)}) collective-permute-start(bf16[64,2304]{1,0:T(8,128)(2,1)S(1)} %pad_maximum_fusion.2), channel_id=1, source_target_pairs={{0,4},{1,5},{2,6},{3,7},{4,0},{5,1},{6,2},{7,3},{8,12},{9,13},{10,... | collective-permute-start | bytes 884744 | tf_op jit(solution)/shard_map/ppermute | solution.py:49
  22.6 6.9 %collective-permute-start.11 = (bf16[64,1536]{1,0:T(8,128)(2,1)S(1)}, bf16[64,1536]{1,0:T(8,128)(2,1)S(1)}, u32[]{:S(2)}, u32[]{:S(2)}) collective-permute-start(bf16[64,1536]{1,0:T(8,128)(2,1)S(1)} %collective-permute-done.8), channel_id=1, source_target_pairs={{0,8},{1,9},{2,10},{3,11},{4,12},{5,13},{6,14},{7,15},{8,0},{9,1},... | collective-permute-start | bytes 589832 | tf_op jit(solution)/shard_map/ppermute | solution.py:49
  23.1 6.3 %slice-start = ((bf16[64,2304]{1,0:T(8,128)(2,1)}), bf16[64,1536]{1,0:T(8,128)(2,1)S(1)}, s32[]{:S(2)}) async-start(bf16[64,2304]{1,0:T(8,128)(2,1)} %copy-done.2), calls=%async_computation | async-start | bytes 393216 | tf_op jit(solution)/shard_map/slice | solution.py:88
  26.4 1.4 %collective-permute-start.13 = (bf16[64,1536]{1,0:T(8,128)(2,1)S(1)}, bf16[64,1536]{1,0:T(8,128)(2,1)S(1)}, u32[]{:S(2)}, u32[]{:S(2)}) collective-permute-start(bf16[64,1536]{1,0:T(8,128)(2,1)S(1)} %collective-permute-done.12), channel_id=1, source_target_pairs={{0,4},{1,5},{2,6},{3,7},{4,0},{5,1},{6,2},{7,3},{8,12},{9,13},{10,... | collective-permute-start | bytes 589832 | tf_op jit(solution)/shard_map/ppermute | solution.py:49
  27.9 2.2 %copy-start.1 = (bf16[64,768]{1,0:T(8,128)(2,1)S(1)}, bf16[64,768]{1,0:T(8,128)(2,1)}, u32[]{:S(2)}) copy-start(bf16[64,768]{1,0:T(8,128)(2,1)} %param.3) | copy-start | bytes 294916
  27.9 2.2 %slice-start.1 = ((bf16[64,2304]{1,0:T(8,128)(2,1)}), bf16[64,768]{1,0:T(8,128)(2,1)S(1)}, s32[]{:S(2)}) async-start(bf16[64,2304]{1,0:T(8,128)(2,1)} %copy-done.2), calls=%async_computation.1 | async-start | bytes 196608 | tf_op jit(solution)/shard_map/slice | solution.py:88
  30.9 6.5 %collective-permute-start.15 = (f32[3,8,64]{2,1,0:T(8,128)S(1)}, f32[3,8,64]{2,1,0:T(8,128)S(1)}, u32[]{:S(2)}, u32[]{:S(2)}) collective-permute-start(f32[3,8,64]{2,1,0:T(8,128)S(1)} %constant_dynamic-update-slice_fusion.13), channel_id=1, source_target_pairs={{0,2},{1,3},{2,0},{3,1},{4,6},{5,7},{6,4},{7,5},{8,10},{9,11},{10,... | collective-permute-start | bytes 18440 | tf_op jit(solution)/shard_map/ppermute | solution.py:49
  37.5 4.6 %collective-permute-start.17 = (f32[3,8,64]{2,1,0:T(8,128)S(1)}, f32[3,8,64]{2,1,0:T(8,128)S(1)}, u32[]{:S(2)}, u32[]{:S(2)}) collective-permute-start(f32[3,8,64]{2,1,0:T(8,128)S(1)} %add.41), channel_id=1, source_target_pairs={{0,16},{1,17},{2,18},{3,19},{4,20},{5,21},{6,22},{7,23},{8,24},{9,... | collective-permute-start | bytes 18440 | tf_op jit(solution)/shard_map/ppermute | solution.py:49
  39.1 4.6 %collective-permute-start.14 = (f32[3,4,64]{2,1,0:T(4,128)S(1)}, f32[3,4,64]{2,1,0:T(4,128)S(1)}, u32[]{:S(2)}, u32[]{:S(2)}) collective-permute-start(f32[3,4,64]{2,1,0:T(4,128)S(1)} %constant_dynamic-update-slice_fusion.10), channel_id=1, source_target_pairs={{0,1},{1,0},{2,3},{3,2},{4,5},{5,4},{6,7},{7,6},{8,9},{9,8},{10,11... | collective-permute-start | bytes 9224 | tf_op jit(solution)/shard_map/ppermute | solution.py:49
  42.1 5.5 %collective-permute-start.18 = (f32[3,8,64]{2,1,0:T(8,128)S(1)}, f32[3,8,64]{2,1,0:T(8,128)S(1)}, u32[]{:S(2)}, u32[]{:S(2)}) collective-permute-start(f32[3,8,64]{2,1,0:T(8,128)S(1)} %add.43), channel_id=1, source_target_pairs={{0,4},{1,5},{2,6},{3,7},{4,0},{5,1},{6,2},{7,3},{8,12},{9,13},{10,... | collective-permute-start | bytes 18440 | tf_op jit(solution)/shard_map/ppermute | solution.py:49
  43.7 3.7 %collective-permute-start.16 = (f32[3,4,64]{2,1,0:T(4,128)S(1)}, f32[3,4,64]{2,1,0:T(4,128)S(1)}, u32[]{:S(2)}, u32[]{:S(2)}) collective-permute-start(f32[3,4,64]{2,1,0:T(4,128)S(1)} %add.40), channel_id=1, source_target_pairs={{0,8},{1,9},{2,10},{3,11},{4,12},{5,13},{6,14},{7,15},{8,0},{9,1},... | collective-permute-start | bytes 9224 | tf_op jit(solution)/shard_map/ppermute | solution.py:49
  48.7 5.6 %collective-permute-start.19 = (f16[64,896]{1,0:T(8,128)(2,1)S(1)}, f16[64,896]{1,0:T(8,128)(2,1)S(1)}, u32[]{:S(2)}, u32[]{:S(2)}) collective-permute-start(f16[64,896]{1,0:T(8,128)(2,1)S(1)} %convert_element_type.18), channel_id=1, source_target_pairs={{0,1},{1,0},{2,3},{3,2},{4,5},{5,4},{6,7},{7,6},{8,9},{9,8},{10,11... | collective-permute-start | bytes 344072 | tf_op jit(solution)/shard_map/ppermute | solution.py:49
  50.8 5.2 %collective-permute-start.20 = (f16[64,896]{1,0:T(8,128)(2,1)S(1)}, f16[64,896]{1,0:T(8,128)(2,1)S(1)}, u32[]{:S(2)}, u32[]{:S(2)}) collective-permute-start(f16[64,896]{1,0:T(8,128)(2,1)S(1)} %convert_element_type.20), channel_id=1, source_target_pairs={{0,8},{1,9},{2,10},{3,11},{4,12},{5,13},{6,14},{7,15},{8,0},{9,1},... | collective-permute-start | bytes 344072 | tf_op jit(solution)/shard_map/ppermute | solution.py:49
  51.4 5.8 %collective-permute-start.21 = (f16[64,896]{1,0:T(8,128)(2,1)S(1)}, f16[64,896]{1,0:T(8,128)(2,1)S(1)}, u32[]{:S(2)}, u32[]{:S(2)}) collective-permute-start(f16[64,896]{1,0:T(8,128)(2,1)S(1)} %convert_element_type.22), channel_id=1, source_target_pairs={{0,9},{1,8},{2,11},{3,10},{4,13},{5,12},{6,15},{7,14},{8,1},{9,0},... | collective-permute-start | bytes 344072 | tf_op jit(solution)/shard_map/ppermute | solution.py:49

commit v9 on v7

v9 whole, which is shorter than its diff:
```python
import functools
import math

import jax
import jax.numpy as jnp
from jax import lax
from jax.experimental import pallas as pl
from jax.experimental.pallas import tpu as pltpu
from jax.sharding import PartitionSpec as P

DS = 768
AXES = ("blk", "inner")
VMEM = 48 * 2**20
SHARE_SCALE = 8.0


EPSILON = 1e-06


def coefficients(sq_student, sq_teacher, cross, total):
    norm_student = jnp.sqrt(sq_student + EPSILON)
    norm_teacher = jnp.sqrt(sq_teacher + EPSILON)
    factor = 2.0 * math.sqrt(total * DS) / total
    cubed = norm_student * norm_student * norm_student
    alpha = factor * (EPSILON / norm_student + cross / norm_teacher) / cubed
    beta = factor / (norm_student * norm_teacher)
    terms = (
        sq_student / (norm_student * norm_student)
        + sq_teacher / (norm_teacher * norm_teacher)
        - 2.0 * cross / (norm_student * norm_teacher)
    )
    return (alpha, beta, terms)


def span(masks):
    out = [0]
    for mask in masks:
        out += [mask ^ other for other in out]
    return out


def subgroups(blocks, inner):
    bits = [1 << b for b in range((inner - 1).bit_length())]
    bits += [inner << b for b in range(1, (blocks - 1).bit_length())]
    return (bits[0::2], bits[1::2] + [inner])


def send(value, mask, count):
    return lax.ppermute(value, AXES, [(i, i ^ mask) for i in range(count)])


def after(value, other):
    return lax.optimization_barrier((value, other))[0]


def gather(own, row_masks, col_masks, count):
    *plane_masks, core_mask = col_masks
    row, col, core = {0: own}, {0: own}, []
    col[1] = send(own, plane_masks[0], count)
    row[1] = send(own, row_masks[0], count)
    core.append(send(own, core_mask, count))
    late = after(own, core[0])
    sides = ((row, row_masks), (col, plane_masks))
    for side, masks in sides:
        for b, mask in enumerate(masks):
            if b:
                side[1 << b] = send(late, mask, count)
    row[1], col[1] = after((row[1], col[1]), (row[2], col[2]))
    places = [0]
    for level in range(1, len(row_masks) + 1):
        for side, masks in sides:
            for place in range(1 << len(masks)):
                if place.bit_count() == level and place not in side:
                    top = place.bit_length() - 1
                    side[place] = send(side[place ^ (1 << top)], masks[top], count)
        ready = [p for p in range(1 << len(plane_masks)) if p.bit_count() == level]
        if ready:
            core.append(send(jnp.concatenate([col[p] for p in ready]), core_mask, count))
            places += ready
    return [row[p] for p in sorted(row)], [col[p] for p in places] + core, places


def tree_sum(values):
    while len(values) > 1:
        values = [values[i] + values[i + 1] for i in range(0, len(values), 2)]
    return values[0]


def join_kernel(teacher, student, own):
    own[:, : teacher.shape[1]] = teacher[...]
    own[:, teacher.shape[1] :] = student[...]


def put_sums(parts, row_part, col_part):
    pad = jnp.zeros((parts[0].shape[0], 128 - len(parts)), jnp.float32)
    by_row = jnp.transpose(jnp.concatenate([jnp.sum(p, 1, keepdims=True) for p in parts] + [pad], 1))
    for k, part in enumerate(parts):
        by_col = jnp.sum(part, 0, keepdims=True)
        for source, sums in ((by_row[k : k + 1], row_part), (by_col, col_part)):
            rows = sums.shape[2]
            for p in range(sums.shape[1]):
                sums[k, p : p + 1, :] = source[:, p * rows : (p + 1) * rows]


def gram_kernel(n_row, width, *refs):
    *pieces, gram_s, gram_t, row_part, col_part = refs
    grams = []
    for part in (slice(width, None), slice(0, width)):
        tops, sides = [jnp.concatenate([p[:, part] for p in group]) for group in (pieces[:n_row], pieces[n_row:])]
        grams.append(
            lax.dot_general(tops, sides, (((1,), (1,)), ((), ())), preferred_element_type=jnp.float32)
        )
    student, teacher = grams
    gram_s[...], gram_t[...] = grams
    put_sums([student * student, teacher * teacher, student * teacher], row_part, col_part)


def call(kernel, operands, outputs, flops=0):
    size = sum(math.prod(a.shape) * a.dtype.itemsize for a in [*operands, *jax.tree.leaves(outputs)])
    return pl.pallas_call(
        kernel,
        out_shape=outputs,
        compiler_params=pltpu.CompilerParams(vmem_limit_bytes=VMEM),
        cost_estimate=pl.CostEstimate(flops=flops, bytes_accessed=size, transcendentals=0),
    )(*operands)


def output_kernel(n_row, n_side, first, total, gram_s, gram_t, row_sum, col_sum, *refs):
    sides, (own, share, *pieces) = refs[:n_side], refs[n_side:]
    col_s = jnp.concatenate([side[:, first:] for side in sides])
    row_alpha, row_beta, _ = coefficients(row_sum[0], row_sum[1], row_sum[2], total)
    col_alpha, col_beta, terms = coefficients(col_sum[0], col_sum[1], col_sum[2], total)
    row_ab = jnp.transpose(jnp.concatenate([row_alpha, row_beta] * 4))
    row_w = row_ab[:, 0:1] * gram_s[...] - row_ab[:, 1:2] * gram_t[...]
    col_w = col_alpha * gram_s[...] - col_beta * gram_t[...]
    out = jnp.dot(row_w.astype(jnp.bfloat16), col_s, preferred_element_type=jnp.float32)
    out += jnp.dot(col_w.astype(jnp.bfloat16), col_s, preferred_element_type=jnp.float32)

    rows, width = own.shape
    own[...] = out[:rows]
    term = jnp.sum(terms, axis=1, keepdims=True)
    share[...] = jnp.broadcast_to(term, share.shape)
    largest = jnp.max(jnp.max(jnp.abs(out), axis=0, keepdims=True), axis=1, keepdims=True)
    power = jnp.clip(jnp.floor(jnp.log2(largest)), -100.0, 100.0)
    term = term * SHARE_SCALE
    high = term.astype(jnp.bfloat16).astype(jnp.float32)
    middle = (term - high).astype(jnp.bfloat16).astype(jnp.float32)
    low = term - high - middle
    lane = lax.broadcasted_iota(jnp.int32, (rows, 128), 1)
    extra = jnp.where(lane == 0, power, jnp.where(lane == 1, high, jnp.where(lane == 2, middle, low)))
    scaled = out * jnp.exp2(13.0 - power)
    for k, piece in enumerate(pieces):
        piece[:, :width] = scaled[(k + 1) * rows : (k + 2) * rows]
        piece[:, width:] = extra


def final_kernel(total, own, share, *refs):
    *pieces, grad, loss = refs
    width = own.shape[1]
    grads, terms = [own[...]], [share[0:1, 0:1]]
    for piece in pieces:
        extra = piece[:, width:]
        grads.append(piece[:, :width] * jnp.exp2(extra[:, 0:1] - 13.0))
        terms.append((extra[0:1, 1:2] + extra[0:1, 2:3] + extra[0:1, 3:4]) * (1.0 / SHARE_SCALE))
    grad[...] = tree_sum(grads)
    loss[...] = tree_sum(terms) * (1.0 / total)


def add_partner(parts, masks, place, count):
    got = send(parts, masks[place], count)
    shape = (3, -1, 2, 1 << place, got.shape[-1])
    return parts + jnp.flip(got.reshape(shape), 2).reshape(parts.shape)


def per_device(teacher, student):
    rows = teacher.shape[0]
    blocks = lax.axis_size("blk")
    inner = lax.axis_size("inner")
    count = blocks * inner
    total = rows * count
    row_masks, col_masks = subgroups(blocks, inner)
    n_row, n_col = 1 << len(row_masks), 1 << len(col_masks)

    depth = teacher.shape[1] + student.shape[1]
    own = call(join_kernel, [teacher, student], jax.ShapeDtypeStruct((rows, depth), teacher.dtype))
    row, col, places = gather(own, row_masks, col_masks, count)
    shape, width = (n_row * rows, n_col * rows), student.shape[1]

    def f32(*dims):
        return jax.ShapeDtypeStruct(dims, jnp.float32)

    gram_s, gram_t, row_part, col_part = call(
        functools.partial(gram_kernel, n_row, teacher.shape[1]),
        row + col,
        [f32(*shape), f32(*shape), f32(3, n_row, rows), f32(3, n_col, rows)],
        2 * math.prod(shape) * depth,
    )
    for place in range(max(len(row_masks), len(col_masks))):
        if place < len(col_masks):
            col_part = add_partner(col_part, col_masks, place, count)
        if place < len(row_masks):
            row_part = after(add_partner(row_part, row_masks, place, count), col_part)
    row_sum, col_sum = row_part.reshape(3, 1, -1), col_part.reshape(3, 1, -1)

    own, share, *pieces = call(
        functools.partial(output_kernel, n_row, len(col), teacher.shape[1], total),
        [gram_s, gram_t, row_sum, col_sum, *col],
        [f32(rows, width), f32(8, 128)] + [f32(rows, width + 128)] * (n_row - 1),
        4 * math.prod(shape) * width,
    )
    got = [
        send(value.astype(jnp.float16), mask, count).astype(jnp.float32)
        for value, mask in zip(pieces, span(row_masks)[1:])
    ]
    grad, loss = call(
        functools.partial(final_kernel, total), [own, share, *got], [f32(rows, width), f32(1, 1)]
    )
    return (loss[0, 0], grad)


def solution(mesh):
    return jax.shard_map(
        per_device,
        mesh=mesh,
        in_specs=(P(AXES, None), P(AXES, None)),
        out_specs=(P(), P(AXES, None)),
        check_vma=False,
    )
```

time: 56.2 us -> 55.7 us (level)
  waiting for transfers between devices: 18.9 us -> 29.1 us
  starting transfers between devices: 29.1 us -> 20.7 us
  matrix products: 1.16 us -> 0 us
  Pallas kernels: 1.7 us -> 2.75 us
  other arithmetic: 1.21 us -> 0.17 us
  local copies, waits for them, and re-layouts: 2.96 us -> 2.05 us
    ppermute x23 -> x17, waiting for transfers between devices: 18.9 us -> 29.1 us  [send(): return lax.ppermute(value, AXES, [(i, i ^ mask) for i in range(count)])]
    ppermute x23 -> x17, starting transfers between devices: 29.1 us -> 20.7 us  [send(): return lax.ppermute(value, AXES, [(i, i ^ mask) for i in range(count)])]
    dot_general x2 -> x0, matrix products: 1.16 us -> none  [the longest x1 0.6 us: per_device(): jnp.einsum('rd,cd->rc', row_t, col_t, preferred_element_type=jnp.float32)]
    pallas_call x2 -> x4, Pallas kernels: 1.7 us -> 2.75 us  [call(): pl.pallas_call(kernel, out_shape=outputs, compiler_params=pltpu.CompilerP...]
    concatenate x3 -> x1, other arithmetic: 1.07 us -> 0.04 us  [gather(): jnp.concatenate([col[p] for p in ready])]
    unnamed x21 -> x4, local copies, waits for them, and re-layouts: 2.01 us -> 1.81 us
  transfers between devices with their start and end apart: 23 -> 17, of which waited for: 13 -> 11; matrix products, arithmetic and copies ran while one was open for 7% -> 0% of each run, Pallas kernels for 0% -> 0%
where the time goes in v9:
time: 55.7 us; the launch traced here: 55.6 us
  waiting for transfers between devices  29.1 us (52%)
  starting transfers between devices  20.7 us (37%)
  Pallas kernels  2.75 us (5%)
  local copies, waits for them, and re-layouts  2.05 us (4%)
  between operations  0.74 us (1%)
    ppermute x17, waiting for transfers between devices, send(): return lax.ppermute(value, AXES, [(i, i ^ mask) for i in range(count)])  29.1 us
    ppermute x17, starting transfers between devices, send(): return lax.ppermute(value, AXES, [(i, i ^ mask) for i in range(count)])  20.7 us
    pallas_call x4, Pallas kernels, call(): pl.pallas_call(kernel, out_shape=outputs, compiler_params=pltpu.CompilerP...  2.75 us
    unnamed x4, local copies, waits for them, and re-layouts  1.81 us
  transfers between devices with their start and end apart: 17, of which 11 were waited for; matrix products, arithmetic and copies ran while one was open for 0% of the time, Pallas kernels for 0%

profile of v9, /device:TPU:0, one launch (start us, length us, event | category | flops | bytes accessed | tf_op | source)
XLA Modules:
  0.0 55.6 jit_solution(12936929224442238100)
XLA Ops:
  0.6 0.9 %copy-done = bf16[64,1536]{1,0:T(8,128)(2,1)S(1)} copy-done((bf16[64,1536]{1,0:T(8,128)(2,1)S(1)}, bf16[64,1536]{1,0:T(8,128)(2,1)}, u32[]{:S(2)}) %copy-start) | copy-done | bytes 196632
  1.6 0.9 %copy-done.1 = bf16[64,768]{1,0:T(8,128)(2,1)S(1)} copy-done((bf16[64,768]{1,0:T(8,128)(2,1)S(1)}, bf16[64,768]{1,0:T(8,128)(2,1)}, u32[]{:S(2)}) %copy-start.1) | copy-done | bytes 98328
  2.5 0.5 collective-permute-start.2
  3.0 3.7 %collective-permute-start.1 = (bf16[64,2304]{1,0:T(8,128)(2,1)S(1)}, bf16[64,2304]{1,0:T(8,128)(2,1)S(1)}, u32[]{:S(2)}, u32[]{:S(2)}) collective-permute-start(bf16[64,2304]{1,0:T(8,128)(2,1)S(1)} %shard_map.41.refs_0_.refs_4_), channel_id=1, source_target_pairs={{0,2},{1,3},{2,0},{3,1},{4,6},{5,7},{6,4},{7,5},{8,10},{9,11},{10,... | collective-permute-start | bytes 884744 | tf_op jit(solution)/shard_map/ppermute | solution.py:49
  6.7 1.6 %collective-permute-start = (bf16[64,2304]{1,0:T(8,128)(2,1)S(1)}, bf16[64,2304]{1,0:T(8,128)(2,1)S(1)}, u32[]{:S(2)}, u32[]{:S(2)}) collective-permute-start(bf16[64,2304]{1,0:T(8,128)(2,1)S(1)} %shard_map.41.refs_0_.refs_4_), channel_id=1, source_target_pairs={{0,1},{1,0},{2,3},{3,2},{4,5},{5,4},{6,7},{7,6},{8,9},{9,8},{10,11... | collective-permute-start | bytes 884744 | tf_op jit(solution)/shard_map/ppermute | solution.py:49
  8.2 1.5 %collective-permute-start.4 = (bf16[64,2304]{1,0:T(8,128)(2,1)S(1)}, bf16[64,2304]{1,0:T(8,128)(2,1)S(1)}, u32[]{:S(2)}, u32[]{:S(2)}) collective-permute-start(bf16[64,2304]{1,0:T(8,128)(2,1)S(1)} %shard_map.41.refs_0_.refs_4_), channel_id=1, source_target_pairs={{0,16},{1,17},{2,18},{3,19},{4,20},{5,21},{6,22},{7,23},{8,24},{9,... | collective-permute-start | bytes 884744 | tf_op jit(solution)/shard_map/ppermute | solution.py:49
  9.8 1.5 %collective-permute-start.3 = (bf16[64,2304]{1,0:T(8,128)(2,1)S(1)}, bf16[64,2304]{1,0:T(8,128)(2,1)S(1)}, u32[]{:S(2)}, u32[]{:S(2)}) collective-permute-start(bf16[64,2304]{1,0:T(8,128)(2,1)S(1)} %shard_map.41.refs_0_.refs_4_), channel_id=1, source_target_pairs={{0,8},{1,9},{2,10},{3,11},{4,12},{5,13},{6,14},{7,15},{8,0},{9,1},... | collective-permute-start | bytes 884744 | tf_op jit(solution)/shard_map/ppermute | solution.py:49
  11.2 9.4 %collective-permute-done.1.refs_5_.refs_1_ = bf16[64,2304]{1,0:T(8,128)(2,1)S(1)} collective-permute-done((bf16[64,2304]{1,0:T(8,128)(2,1)S(1)}, bf16[64,2304]{1,0:T(8,128)(2,1)S(1)}, u32[]{:S(2)}, u32[]{:S(2)}) %collective-permute-start.1) | collective-permute-done | bytes 294944 | tf_op jit(solution)/shard_map/ppermute | solution.py:49
  20.7 0.2 collective-permute-done.refs_1_
  20.9 1.6 %collective-permute-start.6 = (bf16[64,2304]{1,0:T(8,128)(2,1)S(1)}, bf16[64,2304]{1,0:T(8,128)(2,1)S(1)}, u32[]{:S(2)}, u32[]{:S(2)}) collective-permute-start(bf16[64,2304]{1,0:T(8,128)(2,1)S(1)} %collective-permute-done.1.refs_5_.refs_1_), channel_id=1, source_target_pairs={{0,16},{1,17},{2,18},{3,19},{4,20},{5,21},{6,22},{7,23},{8,24},{9,... | collective-permute-start | bytes 884744 | tf_op jit(solution)/shard_map/ppermute | solution.py:49
  22.6 1.6 %collective-permute-start.5 = (bf16[64,2304]{1,0:T(8,128)(2,1)S(1)}, bf16[64,2304]{1,0:T(8,128)(2,1)S(1)}, u32[]{:S(2)}, u32[]{:S(2)}) collective-permute-start(bf16[64,2304]{1,0:T(8,128)(2,1)S(1)} %collective-permute-done.refs_1_), channel_id=1, source_target_pairs={{0,8},{1,9},{2,10},{3,11},{4,12},{5,13},{6,14},{7,15},{8,0},{9,1},... | collective-permute-start | bytes 884744 | tf_op jit(solution)/shard_map/ppermute | solution.py:49
  24.1 5.3 %collective-permute-done.6.refs_7_.refs_3_ = bf16[64,2304]{1,0:T(8,128)(2,1)S(1)} collective-permute-done((bf16[64,2304]{1,0:T(8,128)(2,1)S(1)}, bf16[64,2304]{1,0:T(8,128)(2,1)S(1)}, u32[]{:S(2)}, u32[]{:S(2)}) %collective-permute-start.6) | collective-permute-done | bytes 294944 | tf_op jit(solution)/shard_map/ppermute | solution.py:49
  29.5 2.5 %collective-permute-done.5.refs_3_ = bf16[64,2304]{1,0:T(8,128)(2,1)S(1)} collective-permute-done((bf16[64,2304]{1,0:T(8,128)(2,1)S(1)}, bf16[64,2304]{1,0:T(8,128)(2,1)S(1)}, u32[]{:S(2)}, u32[]{:S(2)}) %collective-permute-start.5) | collective-permute-done | bytes 294944 | tf_op jit(solution)/shard_map/ppermute | solution.py:49
  32.0 1.0 %shard_map.42 = (f32[256,512]{1,0:T(8,128)S(1)}, f32[256,512]{1,0:T(8,128)S(1)}, f32[3,4,64]{2,1,0:T(4,128)S(1)}, f32[3,8,64]{2,1,0:T(8,128)S(1)}) custom-call(bf16[64,2304]{1,0:T(8,128)(2,1)S(1)} %shard_map.41.refs_0_.refs_4_, bf16[64,2304]{1,0:T(8,128)(2,1)S(1)} %collective-permute-done.refs_1_, bf16[64,2304]{1,0:T(8,128)(2,1)S(1)} %collective-permute-done.3.refs_2_, ...), custom_call_target="tpu_custom_call" | custom-call | flops 603979776 | bytes 4596736 | tf_op jit(solution)/shard_map/pallas_call | solution.py:120
  33.1 1.3 %collective-permute-start.10 = (f32[3,8,64]{2,1,0:T(8,128)S(1)}, f32[3,8,64]{2,1,0:T(8,128)S(1)}, u32[]{:S(2)}, u32[]{:S(2)}) collective-permute-start(f32[3,8,64]{2,1,0:T(8,128)S(1)} %get-tuple-element.24), channel_id=1, source_target_pairs={{0,2},{1,3},{2,0},{3,1},{4,6},{5,7},{6,4},{7,5},{8,10},{9,11},{10,... | collective-permute-start | bytes 18440 | tf_op jit(solution)/shard_map/ppermute | solution.py:49
  34.4 3.3 %collective-permute-done.10 = f32[3,8,64]{2,1,0:T(8,128)S(1)} collective-permute-done((f32[3,8,64]{2,1,0:T(8,128)S(1)}, f32[3,8,64]{2,1,0:T(8,128)S(1)}, u32[]{:S(2)}, u32[]{:S(2)}) %collective-permute-start.10) | collective-permute-done | bytes 6176 | tf_op jit(solution)/shard_map/ppermute | solution.py:49
  37.7 0.5 collective-permute-start.12
  38.2 1.6 %collective-permute-start.9 = (f32[3,4,64]{2,1,0:T(4,128)S(1)}, f32[3,4,64]{2,1,0:T(4,128)S(1)}, u32[]{:S(2)}, u32[]{:S(2)}) collective-permute-start(f32[3,4,64]{2,1,0:T(4,128)S(1)} %get-tuple-element.23), channel_id=1, source_target_pairs={{0,1},{1,0},{2,3},{3,2},{4,5},{5,4},{6,7},{7,6},{8,9},{9,8},{10,11... | collective-permute-start | bytes 9224 | tf_op jit(solution)/shard_map/ppermute | solution.py:49
  39.8 1.7 %collective-permute-done.12 = f32[3,8,64]{2,1,0:T(8,128)S(1)} collective-permute-done((f32[3,8,64]{2,1,0:T(8,128)S(1)}, f32[3,8,64]{2,1,0:T(8,128)S(1)}, u32[]{:S(2)}, u32[]{:S(2)}) %collective-permute-start.12) | collective-permute-done | bytes 6176 | tf_op jit(solution)/shard_map/ppermute | solution.py:49
  41.6 0.3 collective-permute-done.9
  41.9 1.6 %collective-permute-start.11 = (f32[3,4,64]{2,1,0:T(4,128)S(1)}, f32[3,4,64]{2,1,0:T(4,128)S(1)}, u32[]{:S(2)}, u32[]{:S(2)}) collective-permute-start(f32[3,4,64]{2,1,0:T(4,128)S(1)} %add.15), channel_id=1, source_target_pairs={{0,8},{1,9},{2,10},{3,11},{4,12},{5,13},{6,14},{7,15},{8,0},{9,1},... | collective-permute-start | bytes 9224 | tf_op jit(solution)/shard_map/ppermute | solution.py:49
  43.5 2.1 %collective-permute-done.11 = f32[3,4,64]{2,1,0:T(4,128)S(1)} collective-permute-done((f32[3,4,64]{2,1,0:T(4,128)S(1)}, f32[3,4,64]{2,1,0:T(4,128)S(1)}, u32[]{:S(2)}, u32[]{:S(2)}) %collective-permute-start.11) | collective-permute-done | bytes 3104 | tf_op jit(solution)/shard_map/ppermute | solution.py:49
  45.6 0.1 reshape.48.row_sum
  45.7 0.1 reshape.51.col_sum
  45.8 0.9 %shard_map.43 = (f32[64,768]{1,0:T(8,128)S(1)}, f32[8,128]{1,0:T(8,128)S(1)}, f32[64,896]{1,0:T(8,128)S(1)}, f32[64,896]{1,0:T(8,128)S(1)}, f32[64,896]{1,0:T(8,128)S(1)}) custom-call(f32[256,512]{1,0:T(8,128)S(1)} %get-tuple-element.21.gram_s, f32[256,512]{1,0:T(8,128)S(1)} %get-tuple-element.22.gram_t, f32[3,1,256]{2,1,0:T(1,128)S(1)} %reshape.48.row_sum, ...), custom_call_target="tpu_custom_call" | custom-call | flops 402653184 | bytes 4305920 | tf_op jit(solution)/shard_map/pallas_call | solution.py:120
  46.7 2.6 %collective-permute-start.16 = (f16[64,896]{1,0:T(8,128)(2,1)S(1)}, f16[64,896]{1,0:T(8,128)(2,1)S(1)}, u32[]{:S(2)}, u32[]{:S(2)}) collective-permute-start(f16[64,896]{1,0:T(8,128)(2,1)S(1)} %convert_element_type.22), channel_id=1, source_target_pairs={{0,9},{1,8},{2,11},{3,10},{4,13},{5,12},{6,15},{7,14},{8,1},{9,0},... | collective-permute-start | bytes 344072 | tf_op jit(solution)/shard_map/ppermute | solution.py:49
  49.3 0.5 collective-permute-start.15
  49.9 0.5 collective-permute-start.14
  50.4 2.9 %collective-permute-done.16 = f16[64,896]{1,0:T(8,128)(2,1)S(1)} collective-permute-done((f16[64,896]{1,0:T(8,128)(2,1)S(1)}, f16[64,896]{1,0:T(8,128)(2,1)S(1)}, u32[]{:S(2)}, u32[]{:S(2)}) %collective-permute-start.16) | collective-permute-done | bytes 114720 | tf_op jit(solution)/shard_map/ppermute | solution.py:49
  53.2 1.0 %collective-permute-done.15 = f16[64,896]{1,0:T(8,128)(2,1)S(1)} collective-permute-done((f16[64,896]{1,0:T(8,128)(2,1)S(1)}, f16[64,896]{1,0:T(8,128)(2,1)S(1)}, u32[]{:S(2)}, u32[]{:S(2)}) %collective-permute-start.15) | collective-permute-done | bytes 114720 | tf_op jit(solution)/shard_map/ppermute | solution.py:49
  54.3 0.4 collective-permute-done.14
  54.8 0.8 %shard_map.44 = (f32[64,768]{1,0:T(8,128)}, f32[1,1]{1,0:T(1,128)}) custom-call(f32[64,768]{1,0:T(8,128)S(1)} %get-tuple-element.27.own, f32[8,128]{1,0:T(8,128)S(1)} %get-tuple-element.28.share, f32[64,896]{1,0:T(8,128)S(1)} %convert_element_type.19.refs_0_, f32[64,896]{1,0:T(8,128)S(1)} %convert_element_type.21.refs_1_, ...), custom_call_target="tpu_custom_call" | custom-call | bytes 1085444 | tf_op jit(solution)/shard_map/pallas_call | solution.py:120
  (29 shorter events, 0.4 us)
Async XLA Ops:
  0.6 0.9 %copy-start = (bf16[64,1536]{1,0:T(8,128)(2,1)S(1)}, bf16[64,1536]{1,0:T(8,128)(2,1)}, u32[]{:S(2)}) copy-start(bf16[64,1536]{1,0:T(8,128)(2,1)} %teacher.1) | copy-start | bytes 589828
  1.6 0.9 %copy-start.1 = (bf16[64,768]{1,0:T(8,128)(2,1)S(1)}, bf16[64,768]{1,0:T(8,128)(2,1)}, u32[]{:S(2)}) copy-start(bf16[64,768]{1,0:T(8,128)(2,1)} %student.1) | copy-start | bytes 294916
  2.5 5.8 %collective-permute-start.2 = (bf16[64,2304]{1,0:T(8,128)(2,1)S(1)}, bf16[64,2304]{1,0:T(8,128)(2,1)S(1)}, u32[]{:S(2)}, u32[]{:S(2)}) collective-permute-start(bf16[64,2304]{1,0:T(8,128)(2,1)S(1)} %shard_map.41.refs_0_.refs_4_), channel_id=1, source_target_pairs={{0,4},{1,5},{2,6},{3,7},{4,0},{5,1},{6,2},{7,3},{8,12},{9,13},{10,... | collective-permute-start | bytes 884744 | tf_op jit(solution)/shard_map/ppermute | solution.py:49
  3.0 17.7 %collective-permute-start.1 = (bf16[64,2304]{1,0:T(8,128)(2,1)S(1)}, bf16[64,2304]{1,0:T(8,128)(2,1)S(1)}, u32[]{:S(2)}, u32[]{:S(2)}) collective-permute-start(bf16[64,2304]{1,0:T(8,128)(2,1)S(1)} %shard_map.41.refs_0_.refs_4_), channel_id=1, source_target_pairs={{0,2},{1,3},{2,0},{3,1},{4,6},{5,7},{6,4},{7,5},{8,10},{9,11},{10,... | collective-permute-start | bytes 884744 | tf_op jit(solution)/shard_map/ppermute | solution.py:49
  6.7 14.2 %collective-permute-start = (bf16[64,2304]{1,0:T(8,128)(2,1)S(1)}, bf16[64,2304]{1,0:T(8,128)(2,1)S(1)}, u32[]{:S(2)}, u32[]{:S(2)}) collective-permute-start(bf16[64,2304]{1,0:T(8,128)(2,1)S(1)} %shard_map.41.refs_0_.refs_4_), channel_id=1, source_target_pairs={{0,1},{1,0},{2,3},{3,2},{4,5},{5,4},{6,7},{7,6},{8,9},{9,8},{10,11... | collective-permute-start | bytes 884744 | tf_op jit(solution)/shard_map/ppermute | solution.py:49
  8.2 12.6 %collective-permute-start.4 = (bf16[64,2304]{1,0:T(8,128)(2,1)S(1)}, bf16[64,2304]{1,0:T(8,128)(2,1)S(1)}, u32[]{:S(2)}, u32[]{:S(2)}) collective-permute-start(bf16[64,2304]{1,0:T(8,128)(2,1)S(1)} %shard_map.41.refs_0_.refs_4_), channel_id=1, source_target_pairs={{0,16},{1,17},{2,18},{3,19},{4,20},{5,21},{6,22},{7,23},{8,24},{9,... | collective-permute-start | bytes 884744 | tf_op jit(solution)/shard_map/ppermute | solution.py:49
  9.8 11.1 %collective-permute-start.3 = (bf16[64,2304]{1,0:T(8,128)(2,1)S(1)}, bf16[64,2304]{1,0:T(8,128)(2,1)S(1)}, u32[]{:S(2)}, u32[]{:S(2)}) collective-permute-start(bf16[64,2304]{1,0:T(8,128)(2,1)S(1)} %shard_map.41.refs_0_.refs_4_), channel_id=1, source_target_pairs={{0,8},{1,9},{2,10},{3,11},{4,12},{5,13},{6,14},{7,15},{8,0},{9,1},... | collective-permute-start | bytes 884744 | tf_op jit(solution)/shard_map/ppermute | solution.py:49
  20.9 8.6 %collective-permute-start.6 = (bf16[64,2304]{1,0:T(8,128)(2,1)S(1)}, bf16[64,2304]{1,0:T(8,128)(2,1)S(1)}, u32[]{:S(2)}, u32[]{:S(2)}) collective-permute-start(bf16[64,2304]{1,0:T(8,128)(2,1)S(1)} %collective-permute-done.1.refs_5_.refs_1_), channel_id=1, source_target_pairs={{0,16},{1,17},{2,18},{3,19},{4,20},{5,21},{6,22},{7,23},{8,24},{9,... | collective-permute-start | bytes 884744 | tf_op jit(solution)/shard_map/ppermute | solution.py:49
  22.5 9.5 %collective-permute-start.7 = (bf16[128,2304]{1,0:T(8,128)(2,1)S(1)}, bf16[128,2304]{1,0:T(8,128)(2,1)S(1)}, u32[]{:S(2)}, u32[]{:S(2)}) collective-permute-start(bf16[128,2304]{1,0:T(8,128)(2,1)S(1)} %pad_maximum_fusion), channel_id=1, source_target_pairs={{0,4},{1,5},{2,6},{3,7},{4,0},{5,1},{6,2},{7,3},{8,12},{9,13},{10,... | collective-permute-start | bytes 1769480 | tf_op jit(solution)/shard_map/ppermute | solution.py:49
  22.6 9.4 %collective-permute-start.5 = (bf16[64,2304]{1,0:T(8,128)(2,1)S(1)}, bf16[64,2304]{1,0:T(8,128)(2,1)S(1)}, u32[]{:S(2)}, u32[]{:S(2)}) collective-permute-start(bf16[64,2304]{1,0:T(8,128)(2,1)S(1)} %collective-permute-done.refs_1_), channel_id=1, source_target_pairs={{0,8},{1,9},{2,10},{3,11},{4,12},{5,13},{6,14},{7,15},{8,0},{9,1},... | collective-permute-start | bytes 884744 | tf_op jit(solution)/shard_map/ppermute | solution.py:49
  29.5 2.6 %collective-permute-start.8 = (bf16[64,2304]{1,0:T(8,128)(2,1)S(1)}, bf16[64,2304]{1,0:T(8,128)(2,1)S(1)}, u32[]{:S(2)}, u32[]{:S(2)}) collective-permute-start(bf16[64,2304]{1,0:T(8,128)(2,1)S(1)} %collective-permute-done.6.refs_7_.refs_3_), channel_id=1, source_target_pairs={{0,4},{1,5},{2,6},{3,7},{4,0},{5,1},{6,2},{7,3},{8,12},{9,13},{10,... | collective-permute-start | bytes 884744 | tf_op jit(solution)/shard_map/ppermute | solution.py:49
  33.1 4.6 %collective-permute-start.10 = (f32[3,8,64]{2,1,0:T(8,128)S(1)}, f32[3,8,64]{2,1,0:T(8,128)S(1)}, u32[]{:S(2)}, u32[]{:S(2)}) collective-permute-start(f32[3,8,64]{2,1,0:T(8,128)S(1)} %get-tuple-element.24), channel_id=1, source_target_pairs={{0,2},{1,3},{2,0},{3,1},{4,6},{5,7},{6,4},{7,5},{8,10},{9,11},{10,... | collective-permute-start | bytes 18440 | tf_op jit(solution)/shard_map/ppermute | solution.py:49
  37.7 3.8 %collective-permute-start.12 = (f32[3,8,64]{2,1,0:T(8,128)S(1)}, f32[3,8,64]{2,1,0:T(8,128)S(1)}, u32[]{:S(2)}, u32[]{:S(2)}) collective-permute-start(f32[3,8,64]{2,1,0:T(8,128)S(1)} %add.16), channel_id=1, source_target_pairs={{0,16},{1,17},{2,18},{3,19},{4,20},{5,21},{6,22},{7,23},{8,24},{9,... | collective-permute-start | bytes 18440 | tf_op jit(solution)/shard_map/ppermute | solution.py:49
  38.2 3.6 %collective-permute-start.9 = (f32[3,4,64]{2,1,0:T(4,128)S(1)}, f32[3,4,64]{2,1,0:T(4,128)S(1)}, u32[]{:S(2)}, u32[]{:S(2)}) collective-permute-start(f32[3,4,64]{2,1,0:T(4,128)S(1)} %get-tuple-element.23), channel_id=1, source_target_pairs={{0,1},{1,0},{2,3},{3,2},{4,5},{5,4},{6,7},{7,6},{8,9},{9,8},{10,11... | collective-permute-start | bytes 9224 | tf_op jit(solution)/shard_map/ppermute | solution.py:49
  41.5 4.2 %collective-permute-start.13 = (f32[3,8,64]{2,1,0:T(8,128)S(1)}, f32[3,8,64]{2,1,0:T(8,128)S(1)}, u32[]{:S(2)}, u32[]{:S(2)}) collective-permute-start(f32[3,8,64]{2,1,0:T(8,128)S(1)} %add.18), channel_id=1, source_target_pairs={{0,4},{1,5},{2,6},{3,7},{4,0},{5,1},{6,2},{7,3},{8,12},{9,13},{10,... | collective-permute-start | bytes 18440 | tf_op jit(solution)/shard_map/ppermute | solution.py:49
  41.9 3.7 %collective-permute-start.11 = (f32[3,4,64]{2,1,0:T(4,128)S(1)}, f32[3,4,64]{2,1,0:T(4,128)S(1)}, u32[]{:S(2)}, u32[]{:S(2)}) collective-permute-start(f32[3,4,64]{2,1,0:T(4,128)S(1)} %add.15), channel_id=1, source_target_pairs={{0,8},{1,9},{2,10},{3,11},{4,12},{5,13},{6,14},{7,15},{8,0},{9,1},... | collective-permute-start | bytes 9224 | tf_op jit(solution)/shard_map/ppermute | solution.py:49
  46.7 6.5 %collective-permute-start.16 = (f16[64,896]{1,0:T(8,128)(2,1)S(1)}, f16[64,896]{1,0:T(8,128)(2,1)S(1)}, u32[]{:S(2)}, u32[]{:S(2)}) collective-permute-start(f16[64,896]{1,0:T(8,128)(2,1)S(1)} %convert_element_type.22), channel_id=1, source_target_pairs={{0,9},{1,8},{2,11},{3,10},{4,13},{5,12},{6,15},{7,14},{8,1},{9,0},... | collective-permute-start | bytes 344072 | tf_op jit(solution)/shard_map/ppermute | solution.py:49
  49.3 5.0 %collective-permute-start.15 = (f16[64,896]{1,0:T(8,128)(2,1)S(1)}, f16[64,896]{1,0:T(8,128)(2,1)S(1)}, u32[]{:S(2)}, u32[]{:S(2)}) collective-permute-start(f16[64,896]{1,0:T(8,128)(2,1)S(1)} %convert_element_type.20), channel_id=1, source_target_pairs={{0,8},{1,9},{2,10},{3,11},{4,12},{5,13},{6,14},{7,15},{8,0},{9,1},... | collective-permute-start | bytes 344072 | tf_op jit(solution)/shard_map/ppermute | solution.py:49
  49.9 4.9 %collective-permute-start.14 = (f16[64,896]{1,0:T(8,128)(2,1)S(1)}, f16[64,896]{1,0:T(8,128)(2,1)S(1)}, u32[]{:S(2)}, u32[]{:S(2)}) collective-permute-start(f16[64,896]{1,0:T(8,128)(2,1)S(1)} %convert_element_type.18), channel_id=1, source_target_pairs={{0,1},{1,0},{2,3},{3,2},{4,5},{5,4},{6,7},{7,6},{8,9},{9,8},{10,11... | collective-permute-start | bytes 344072 | tf_op jit(solution)/shard_map/ppermute | solution.py:49

commit v10 on v9

--- a/solution.py
+++ b/solution.py
@@ -86,9 +86,16 @@
     return values[0]
 
 
-def join_kernel(teacher, student, own):
-    own[:, : teacher.shape[1]] = teacher[...]
-    own[:, teacher.shape[1] :] = student[...]
+def join_kernel(teacher, student, own, sems):
+    width = teacher.shape[1]
+    copies = [
+        pltpu.make_async_copy(teacher, own.at[:, pl.ds(0, width)], sems.at[0]),
+        pltpu.make_async_copy(student, own.at[:, pl.ds(width, student.shape[1])], sems.at[1]),
+    ]
+    for copy in copies:
+        copy.start()
+    for copy in copies:
+        copy.wait()
 
 
 def put_sums(parts, row_part, col_part):
@@ -115,12 +122,13 @@
     put_sums([student * student, teacher * teacher, student * teacher], row_part, col_part)
 
 
-def call(kernel, operands, outputs, flops=0):
+def call(kernel, operands, outputs, flops=0, vmem=VMEM, **options):
     size = sum(math.prod(a.shape) * a.dtype.itemsize for a in [*operands, *jax.tree.leaves(outputs)])
     return pl.pallas_call(
         kernel,
         out_shape=outputs,
-        compiler_params=pltpu.CompilerParams(vmem_limit_bytes=VMEM),
+        **options,
+        compiler_params=pltpu.CompilerParams(vmem_limit_bytes=vmem),
         cost_estimate=pl.CostEstimate(flops=flops, bytes_accessed=size, transcendentals=0),
     )(*operands)
 
@@ -166,10 +174,20 @@
     loss[...] = tree_sum(terms) * (1.0 / total)
 
 
-def add_partner(parts, masks, place, count):
-    got = send(parts, masks[place], count)
-    shape = (3, -1, 2, 1 << place, got.shape[-1])
-    return parts + jnp.flip(got.reshape(shape), 2).reshape(parts.shape)
+def group_sum(parts, masks, count):
+    members = span(masks)
+    spanned = set(members)
+    heads = [i for i in range(count) if i == min(i ^ m for m in spanned)]
+    groups = [[head ^ m for m in members] for head in heads]
+    outgoing = jnp.stack([jnp.stack([parts[:, k ^ r] for k in range(len(members))], 1) for r in range(len(members))])
+    place = lax.axis_index(AXES)
+    for b, mask in enumerate(masks):
+        bit = (place & mask) != 0
+        shape = (-1, 2, 1 << b) + parts.shape
+        flipped = jnp.flip(outgoing.reshape(shape), 1).reshape(outgoing.shape)
+        outgoing = jnp.where(bit, flipped, outgoing)
+    got = lax.all_to_all(outgoing, AXES, 0, 0, axis_index_groups=groups, tiled=True)
+    return tree_sum([got[i] for i in range(len(members))])
 
 
 def per_device(teacher, student):
@@ -182,7 +200,14 @@
     n_row, n_col = 1 << len(row_masks), 1 << len(col_masks)
 
     depth = teacher.shape[1] + student.shape[1]
-    own = call(join_kernel, [teacher, student], jax.ShapeDtypeStruct((rows, depth), teacher.dtype))
+    own = call(
+        join_kernel,
+        [teacher, student],
+        jax.ShapeDtypeStruct((rows, depth), teacher.dtype),
+        in_specs=[pl.BlockSpec(memory_space=pl.ANY)] * 2,
+        vmem=60 * 2**20,
+        scratch_shapes=[pltpu.SemaphoreType.DMA((2,))],
+    )
     row, col, places = gather(own, row_masks, col_masks, count)
     shape, width = (n_row * rows, n_col * rows), student.shape[1]
 
@@ -195,11 +220,8 @@
         [f32(*shape), f32(*shape), f32(3, n_row, rows), f32(3, n_col, rows)],
         2 * math.prod(shape) * depth,
     )
-    for place in range(max(len(row_masks), len(col_masks))):
-        if place < len(col_masks):
-            col_part = add_partner(col_part, col_masks, place, count)
-        if place < len(row_masks):
-            row_part = after(add_partner(row_part, row_masks, place, count), col_part)
+    col_part = group_sum(col_part, col_masks, count)
+    row_part = group_sum(row_part, row_masks, count)
     row_sum, col_sum = row_part.reshape(3, 1, -1), col_part.reshape(3, 1, -1)
 
     own, share, *pieces = call(

time: 55.7 us -> 85.6 us (1.54)
  local copies, waits for them, and re-layouts: 2.05 us -> 18.6 us
  other arithmetic: 0.17 us -> 8.06 us
  starting transfers between devices: 20.7 us -> 23.8 us
  Pallas kernels: 2.75 us -> 4.43 us
    unnamed x4 -> x34, local copies, waits for them, and re-layouts: 1.81 us -> 10.4 us
    all_to_all x0 -> x2, starting transfers between devices: none -> 8.29 us  [group_sum(): lax.all_to_all(outgoing, AXES, 0, 0, axis_index_groups=groups, tiled=True)]
    ppermute x17 -> x12, waiting for transfers between devices: 29.1 us -> 23 us  [send(): return lax.ppermute(value, AXES, [(i, i ^ mask) for i in range(count)])]
    all_to_all x0 -> x2, waiting for transfers between devices: none -> 6.03 us  [group_sum(): lax.all_to_all(outgoing, AXES, 0, 0, axis_index_groups=groups, tiled=True)]
    ppermute x17 -> x12, starting transfers between devices: 20.7 us -> 15.5 us  [send(): return lax.ppermute(value, AXES, [(i, i ^ mask) for i in range(count)])]
    rev x5, local copies, waits for them, and re-layouts: 0.08 us -> 5.08 us  [group_sum(): flipped = jnp.flip(outgoing.reshape(shape), 1).reshape(outgoing.shape)]
    select_n x0 -> x5, other arithmetic: none -> 4.95 us  [group_sum(): outgoing = jnp.where(bit, flipped, outgoing)]
    all_to_all x0 -> x2, other arithmetic: none -> 2.06 us  [group_sum(): lax.all_to_all(outgoing, AXES, 0, 0, axis_index_groups=groups, tiled=True)]
  transfers between devices with their start and end apart: 17 -> 14, of which waited for: 11 -> 8; matrix products, arithmetic and copies ran while one was open for 0% -> 7% of each run, Pallas kernels for 0% -> 0%
where the time goes in v10:
time: 85.6 us; the launch traced here: 84.7 us
  waiting for transfers between devices  29 us (34%)
  starting transfers between devices  23.8 us (28%)
  local copies, waits for them, and re-layouts  18.6 us (22%)
  other arithmetic  8.06 us (9%)
  Pallas kernels  4.43 us (5%)
    ppermute x12, waiting for transfers between devices, send(): return lax.ppermute(value, AXES, [(i, i ^ mask) for i in range(count)])  23 us
    ppermute x12, starting transfers between devices, send(): return lax.ppermute(value, AXES, [(i, i ^ mask) for i in range(count)])  15.5 us
    unnamed x34, local copies, waits for them, and re-layouts  10.4 us
    all_to_all x2, starting transfers between devices, group_sum(): lax.all_to_all(outgoing, AXES, 0, 0, axis_index_groups=groups, tiled=True)  8.29 us
    all_to_all x2, waiting for transfers between devices, group_sum(): lax.all_to_all(outgoing, AXES, 0, 0, axis_index_groups=groups, tiled=True)  6.03 us
    rev x5, local copies, waits for them, and re-layouts, group_sum(): flipped = jnp.flip(outgoing.reshape(shape), 1).reshape(outgoing.shape)  5.08 us
    select_n x5, other arithmetic, group_sum(): outgoing = jnp.where(bit, flipped, outgoing)  4.95 us
    pallas_call x4, Pallas kernels, call(): pl.pallas_call(kernel, out_shape=outputs, **options, compiler_params=pltp...  4.43 us
  transfers between devices with their start and end apart: 14, of which 8 were waited for; matrix products, arithmetic and copies ran while one was open for 7% of the time, Pallas kernels for 0%

profile of v10, /device:TPU:0, one launch (start us, length us, event | category | flops | bytes accessed | tf_op | source)
XLA Modules:
  0.0 84.7 jit_solution(12807817402466726282)
XLA Ops:
  0.6 1.7 %shard_map.41.refs_0_.refs_4_ = bf16[64,2304]{1,0:T(8,128)(2,1)} custom-call(bf16[64,1536]{1,0:T(8,128)(2,1)} %teacher.1, bf16[64,768]{1,0:T(8,128)(2,1)} %student.1), custom_call_target="tpu_custom_call" | custom-call | bytes 589824 | tf_op jit(solution)/shard_map/pallas_call | solution.py:127
  2.9 2.6 %collective-permute-start = (bf16[64,2304]{1,0:T(8,128)(2,1)}, bf16[64,2304]{1,0:T(8,128)(2,1)S(1)}, u32[]{:S(2)}, u32[]{:S(2)}) collective-permute-start(bf16[64,2304]{1,0:T(8,128)(2,1)} %shard_map.41.refs_0_.refs_4_), channel_id=1, source_target_pairs={{0,1},{1,0},{2,3},{3,2},{4,5},{5,4},{6,7},{7,6},{8,9},{9,8},{10,11... | collective-permute-start | bytes 884744 | tf_op jit(solution)/shard_map/ppermute | solution.py:49
  5.5 2.6 %collective-permute-start.1 = (bf16[64,2304]{1,0:T(8,128)(2,1)}, bf16[64,2304]{1,0:T(8,128)(2,1)S(1)}, u32[]{:S(2)}, u32[]{:S(2)}) collective-permute-start(bf16[64,2304]{1,0:T(8,128)(2,1)} %shard_map.41.refs_0_.refs_4_), channel_id=1, source_target_pairs={{0,2},{1,3},{2,0},{3,1},{4,6},{5,7},{6,4},{7,5},{8,10},{9,11},{10,... | collective-permute-start | bytes 884744 | tf_op jit(solution)/shard_map/ppermute | solution.py:49
  8.1 1.5 %collective-permute-start.4 = (bf16[64,2304]{1,0:T(8,128)(2,1)}, bf16[64,2304]{1,0:T(8,128)(2,1)S(1)}, u32[]{:S(2)}, u32[]{:S(2)}) collective-permute-start(bf16[64,2304]{1,0:T(8,128)(2,1)} %shard_map.41.refs_0_.refs_4_), channel_id=1, source_target_pairs={{0,16},{1,17},{2,18},{3,19},{4,20},{5,21},{6,22},{7,23},{8,24},{9,... | collective-permute-start | bytes 884744 | tf_op jit(solution)/shard_map/ppermute | solution.py:49
  9.6 1.5 %collective-permute-start.3 = (bf16[64,2304]{1,0:T(8,128)(2,1)}, bf16[64,2304]{1,0:T(8,128)(2,1)S(1)}, u32[]{:S(2)}, u32[]{:S(2)}) collective-permute-start(bf16[64,2304]{1,0:T(8,128)(2,1)} %shard_map.41.refs_0_.refs_4_), channel_id=1, source_target_pairs={{0,8},{1,9},{2,10},{3,11},{4,12},{5,13},{6,14},{7,15},{8,0},{9,1},... | collective-permute-start | bytes 884744 | tf_op jit(solution)/shard_map/ppermute | solution.py:49
  11.1 8.4 %collective-permute-done.refs_1_ = bf16[64,2304]{1,0:T(8,128)(2,1)S(1)} collective-permute-done((bf16[64,2304]{1,0:T(8,128)(2,1)}, bf16[64,2304]{1,0:T(8,128)(2,1)S(1)}, u32[]{:S(2)}, u32[]{:S(2)}) %collective-permute-start) | collective-permute-done | bytes 294944 | tf_op jit(solution)/shard_map/ppermute | solution.py:49
  19.5 2.6 %collective-permute-done.1.refs_5_.refs_1_ = bf16[64,2304]{1,0:T(8,128)(2,1)S(1)} collective-permute-done((bf16[64,2304]{1,0:T(8,128)(2,1)}, bf16[64,2304]{1,0:T(8,128)(2,1)S(1)}, u32[]{:S(2)}, u32[]{:S(2)}) %collective-permute-start.1) | collective-permute-done | bytes 294944 | tf_op jit(solution)/shard_map/ppermute | solution.py:49
  22.8 1.5 %collective-permute-start.6 = (bf16[64,2304]{1,0:T(8,128)(2,1)S(1)}, bf16[64,2304]{1,0:T(8,128)(2,1)S(1)}, u32[]{:S(2)}, u32[]{:S(2)}) collective-permute-start(bf16[64,2304]{1,0:T(8,128)(2,1)S(1)} %collective-permute-done.1.refs_5_.refs_1_), channel_id=1, source_target_pairs={{0,16},{1,17},{2,18},{3,19},{4,20},{5,21},{6,22},{7,23},{8,24},{9,... | collective-permute-start | bytes 884744 | tf_op jit(solution)/shard_map/ppermute | solution.py:49
  25.2 1.5 %collective-permute-start.5 = (bf16[64,2304]{1,0:T(8,128)(2,1)S(1)}, bf16[64,2304]{1,0:T(8,128)(2,1)S(1)}, u32[]{:S(2)}, u32[]{:S(2)}) collective-permute-start(bf16[64,2304]{1,0:T(8,128)(2,1)S(1)} %collective-permute-done.refs_1_), channel_id=1, source_target_pairs={{0,8},{1,9},{2,10},{3,11},{4,12},{5,13},{6,14},{7,15},{8,0},{9,1},... | collective-permute-start | bytes 884744 | tf_op jit(solution)/shard_map/ppermute | solution.py:49
  26.7 2.8 %collective-permute-done.6.refs_7_.refs_3_ = bf16[64,2304]{1,0:T(8,128)(2,1)S(1)} collective-permute-done((bf16[64,2304]{1,0:T(8,128)(2,1)S(1)}, bf16[64,2304]{1,0:T(8,128)(2,1)S(1)}, u32[]{:S(2)}, u32[]{:S(2)}) %collective-permute-start.6) | collective-permute-done | bytes 294944 | tf_op jit(solution)/shard_map/ppermute | solution.py:49
  29.5 5.1 %collective-permute-done.5.refs_3_ = bf16[64,2304]{1,0:T(8,128)(2,1)S(1)} collective-permute-done((bf16[64,2304]{1,0:T(8,128)(2,1)S(1)}, bf16[64,2304]{1,0:T(8,128)(2,1)S(1)}, u32[]{:S(2)}, u32[]{:S(2)}) %collective-permute-start.5) | collective-permute-done | bytes 294944 | tf_op jit(solution)/shard_map/ppermute | solution.py:49
  35.4 1.0 %copy-done.2 = bf16[64,2304]{1,0:T(8,128)(2,1)S(1)} copy-done((bf16[64,2304]{1,0:T(8,128)(2,1)S(1)}, bf16[64,2304]{1,0:T(8,128)(2,1)}, u32[]{:S(2)}) %copy-start.2) | copy-done | bytes 294936
  36.3 1.0 %copy-done.4 = bf16[64,2304]{1,0:T(8,128)(2,1)S(1)} copy-done((bf16[64,2304]{1,0:T(8,128)(2,1)S(1)}, bf16[64,2304]{1,0:T(8,128)(2,1)}, u32[]{:S(2)}) %copy-start.4) | copy-done | bytes 294936
  37.3 1.0 %copy-done.6 = bf16[64,2304]{1,0:T(8,128)(2,1)S(1)} copy-done((bf16[64,2304]{1,0:T(8,128)(2,1)S(1)}, bf16[64,2304]{1,0:T(8,128)(2,1)}, u32[]{:S(2)}) %copy-start.6) | copy-done | bytes 294936
  38.3 1.0 %shard_map.42 = (f32[256,512]{1,0:T(8,128)S(1)}, f32[256,512]{1,0:T(8,128)S(1)}, f32[3,4,64]{2,1,0:T(4,128)S(1)}, f32[3,8,64]{2,1,0:T(8,128)S(1)}) custom-call(bf16[64,2304]{1,0:T(8,128)(2,1)S(1)} %copy-done, bf16[64,2304]{1,0:T(8,128)(2,1)S(1)} %copy-done.2, bf16[64,2304]{1,0:T(8,128)(2,1)S(1)} %copy-done.4, bf16[64,2304]{1,0:T(8,128)(2,1)S(1)} %copy-done.6, ...), custom_call_target="tpu_custom_call" | custom-call | flops 603979776 | bytes 4596736 | tf_op jit(solution)/shard_map/pallas_call | solution.py:127
  44.6 1.5 %rev.23 = f32[2,2,2,3,8,64]{5,4,3,2,1,0:T(8,128)} reverse(f32[2,2,2,3,8,64]{5,4,3,2,1,0:T(8,128)} %broadcast_select_fusion), dimensions={1} | reverse | bytes 98304 | tf_op jit(solution)/shard_map/jit(_flip)/rev | solution.py:187
  46.8 1.5 %rev.24 = f32[1,2,4,3,8,64]{5,4,3,2,1,0:T(8,128)} reverse(f32[1,2,4,3,8,64]{5,4,3,2,1,0:T(8,128)} %select_select_fusion), dimensions={1} | reverse | bytes 98304 | tf_op jit(solution)/shard_map/jit(_flip)/rev | solution.py:187
  51.0 1.4 %fusion.2 = f32[4,3,4,64]{3,2,1,0:T(4,128)} fusion(f32[2,2,1,3,4,64]{5,4,3,1,0,2:T(4,128)} %rev.20, f32[1,2,2,3,4,64]{5,4,3,2,1,0:T(4,128)S(1)} %rev.21, pred[]{:T(512)S(6)} %ne.16, pred[]{:T(512)S(6)} %ne.15, f32[1,3,4,64]{3,2,1,0:T(4,128)} %copy-done.7, f32[1,3,4,64]{3,2,1,0:T(4,128)S(1)} %maximum_bitcast_fusion.4, ...), kind=kLoop, calls=%fused_computation.8 | loop fusion | flops 15360 | bytes 49154 | tf_op jit(solution)/shard_map/jit(_where)/select_n | solution.py:188
  52.4 1.4 %reshape.219 = f32[4,1,768]{2,1,0:T(1,128)} reshape(f32[4,3,4,64]{3,2,1,0:T(4,128)} %fusion.2) | data formatting | bytes 24576
  53.8 3.2 %all-to-all-start = ((f32[4,1,768]{2,1,0:T(1,128)}), f32[4,1,768]{2,1,0:T(1,128)S(1)}, u32[]{:S(2)}, u32[]{:S(2)}) async-start(f32[4,1,768]{2,1,0:T(1,128)} %reshape.219), calls=%async_computation | async-start | bytes 24576 | tf_op jit(solution)/shard_map/all_to_all | solution.py:189
  57.0 1.7 %fusion.1 = f32[8,3,8,64]{3,2,1,0:T(8,128)} fusion(f32[8,3,8,64]{3,2,1,0:T(8,128)S(1)} %constant_dynamic-update-slice_fusion, f32[4,2,1,3,8,64]{5,4,3,1,0,2:T(8,128)} %rev.22, f32[2,2,2,3,8,64]{5,4,3,2,1,0:T(8,128)} %rev.23, f32[1,2,4,3,8,64]{5,4,3,2,1,0:T(8,128)} %rev.24, pred[]{:T(512)S(6)} %ne.19, pred[]{:T(512)S(6)} %ne.18, pred[]{:T(512)S(6)} %ne.17), kind=kLoop, calls=%fused_computation.3 | loop fusion | flops 36864 | bytes 245763 | tf_op jit(solution)/shard_map/jit(_where)/select_n | solution.py:188
  58.7 1.6 %reshape.221 = f32[8,1,1536]{2,1,0:T(1,128)} reshape(f32[8,3,8,64]{3,2,1,0:T(8,128)} %fusion.1) | data formatting | bytes 98304
  60.3 1.4 %all-to-all-done = f32[4,1,768]{2,1,0:T(1,128)S(1)} async-done(((f32[4,1,768]{2,1,0:T(1,128)}), f32[4,1,768]{2,1,0:T(1,128)S(1)}, u32[]{:S(2)}, u32[]{:S(2)}) %all-to-all-start) | async-done | bytes 12320 | tf_op jit(solution)/shard_map/all_to_all | solution.py:189
  61.7 5.1 %all-to-all-start.1 = ((f32[8,1,1536]{2,1,0:T(1,128)}), f32[8,1,1536]{2,1,0:T(1,128)S(1)}, u32[]{:S(2)}, u32[]{:S(2)}) async-start(f32[8,1,1536]{2,1,0:T(1,128)} %reshape.221), calls=%async_computation.1 | async-start | bytes 98304 | tf_op jit(solution)/shard_map/all_to_all | solution.py:189
  68.1 4.6 %all-to-all-done.1 = f32[8,1,1536]{2,1,0:T(1,128)S(1)} async-done(((f32[8,1,1536]{2,1,0:T(1,128)}), f32[8,1,1536]{2,1,0:T(1,128)S(1)}, u32[]{:S(2)}, u32[]{:S(2)}) %all-to-all-start.1) | async-done | bytes 49184 | tf_op jit(solution)/shard_map/all_to_all | solution.py:189
  72.8 1.4 %reduce.1 = f32[8,1536]{1,0:T(8,128)} reduce(f32[8,1,1536]{2,1,0:T(1,128)S(1)} %all-to-all-done.1, f32[]{:T(128)} %broadcast.22), dimensions={1}, to_apply=%all_to_all.7.reduce_sub_computation | reduce | bytes 98308 | tf_op jit(solution)/shard_map/all_to_all | solution.py:189
  74.2 0.9 %reshape.222 = f32[8,3,8,64]{3,2,1,0:T(8,128)S(1)} reshape(f32[8,1536]{1,0:T(8,128)} %reduce.1) | data formatting | bytes 98304
  75.1 0.9 %shard_map.43 = (f32[64,768]{1,0:T(8,128)S(1)}, f32[8,128]{1,0:T(8,128)S(1)}, f32[64,896]{1,0:T(8,128)S(1)}, f32[64,896]{1,0:T(8,128)S(1)}, f32[64,896]{1,0:T(8,128)S(1)}) custom-call(f32[256,512]{1,0:T(8,128)S(1)} %get-tuple-element.19.gram_s, f32[256,512]{1,0:T(8,128)S(1)} %get-tuple-element.20.gram_t, f32[3,1,256]{2,1,0:T(1,128)S(1)} %add.122.row_sum, ...), custom_call_target="tpu_custom_call" | custom-call | flops 402653184 | bytes 4305920 | tf_op jit(solution)/shard_map/pallas_call | solution.py:127
  76.5 1.5 %collective-permute-start.10 = (f16[64,896]{1,0:T(8,128)(2,1)S(1)}, f16[64,896]{1,0:T(8,128)(2,1)S(1)}, u32[]{:S(2)}, u32[]{:S(2)}) collective-permute-start(f16[64,896]{1,0:T(8,128)(2,1)S(1)} %convert_element_type.20), channel_id=1, source_target_pairs={{0,8},{1,9},{2,10},{3,11},{4,12},{5,13},{6,14},{7,15},{8,0},{9,1},... | collective-permute-start | bytes 344072 | tf_op jit(solution)/shard_map/ppermute | solution.py:49
  78.0 1.7 %collective-permute-start.11 = (f16[64,896]{1,0:T(8,128)(2,1)S(1)}, f16[64,896]{1,0:T(8,128)(2,1)S(1)}, u32[]{:S(2)}, u32[]{:S(2)}) collective-permute-start(f16[64,896]{1,0:T(8,128)(2,1)S(1)} %convert_element_type.22), channel_id=1, source_target_pairs={{0,9},{1,8},{2,11},{3,10},{4,13},{5,12},{6,15},{7,14},{8,1},{9,0},... | collective-permute-start | bytes 344072 | tf_op jit(solution)/shard_map/ppermute | solution.py:49
  79.8 2.3 %collective-permute-done.9 = f16[64,896]{1,0:T(8,128)(2,1)S(1)} collective-permute-done((f16[64,896]{1,0:T(8,128)(2,1)S(1)}, f16[64,896]{1,0:T(8,128)(2,1)S(1)}, u32[]{:S(2)}, u32[]{:S(2)}) %collective-permute-start.9) | collective-permute-done | bytes 114720 | tf_op jit(solution)/shard_map/ppermute | solution.py:49
  82.1 1.7 %collective-permute-done.10 = f16[64,896]{1,0:T(8,128)(2,1)S(1)} collective-permute-done((f16[64,896]{1,0:T(8,128)(2,1)S(1)}, f16[64,896]{1,0:T(8,128)(2,1)S(1)}, u32[]{:S(2)}, u32[]{:S(2)}) %collective-permute-start.10) | collective-permute-done | bytes 114720 | tf_op jit(solution)/shard_map/ppermute | solution.py:49
  (72 shorter events, 14.2 us)
Async XLA Ops:
  2.4 33.0 %copy-start = (bf16[64,2304]{1,0:T(8,128)(2,1)S(1)}, bf16[64,2304]{1,0:T(8,128)(2,1)}, u32[]{:S(2)}) copy-start(bf16[64,2304]{1,0:T(8,128)(2,1)} %shard_map.41.refs_0_.refs_4_) | copy-start | bytes 884740
  2.4 5.8 %collective-permute-start.2 = (bf16[64,2304]{1,0:T(8,128)(2,1)}, bf16[64,2304]{1,0:T(8,128)(2,1)S(1)}, u32[]{:S(2)}, u32[]{:S(2)}) collective-permute-start(bf16[64,2304]{1,0:T(8,128)(2,1)} %shard_map.41.refs_0_.refs_4_), channel_id=1, source_target_pairs={{0,4},{1,5},{2,6},{3,7},{4,0},{5,1},{6,2},{7,3},{8,12},{9,13},{10,... | collective-permute-start | bytes 884744 | tf_op jit(solution)/shard_map/ppermute | solution.py:49
  2.9 16.6 %collective-permute-start = (bf16[64,2304]{1,0:T(8,128)(2,1)}, bf16[64,2304]{1,0:T(8,128)(2,1)S(1)}, u32[]{:S(2)}, u32[]{:S(2)}) collective-permute-start(bf16[64,2304]{1,0:T(8,128)(2,1)} %shard_map.41.refs_0_.refs_4_), channel_id=1, source_target_pairs={{0,1},{1,0},{2,3},{3,2},{4,5},{5,4},{6,7},{7,6},{8,9},{9,8},{10,11... | collective-permute-start | bytes 884744 | tf_op jit(solution)/shard_map/ppermute | solution.py:49
  5.5 16.6 %collective-permute-start.1 = (bf16[64,2304]{1,0:T(8,128)(2,1)}, bf16[64,2304]{1,0:T(8,128)(2,1)S(1)}, u32[]{:S(2)}, u32[]{:S(2)}) collective-permute-start(bf16[64,2304]{1,0:T(8,128)(2,1)} %shard_map.41.refs_0_.refs_4_), channel_id=1, source_target_pairs={{0,2},{1,3},{2,0},{3,1},{4,6},{5,7},{6,4},{7,5},{8,10},{9,11},{10,... | collective-permute-start | bytes 884744 | tf_op jit(solution)/shard_map/ppermute | solution.py:49
  8.1 14.0 %collective-permute-start.4 = (bf16[64,2304]{1,0:T(8,128)(2,1)}, bf16[64,2304]{1,0:T(8,128)(2,1)S(1)}, u32[]{:S(2)}, u32[]{:S(2)}) collective-permute-start(bf16[64,2304]{1,0:T(8,128)(2,1)} %shard_map.41.refs_0_.refs_4_), channel_id=1, source_target_pairs={{0,16},{1,17},{2,18},{3,19},{4,20},{5,21},{6,22},{7,23},{8,24},{9,... | collective-permute-start | bytes 884744 | tf_op jit(solution)/shard_map/ppermute | solution.py:49
  9.6 12.5 %collective-permute-start.3 = (bf16[64,2304]{1,0:T(8,128)(2,1)}, bf16[64,2304]{1,0:T(8,128)(2,1)S(1)}, u32[]{:S(2)}, u32[]{:S(2)}) collective-permute-start(bf16[64,2304]{1,0:T(8,128)(2,1)} %shard_map.41.refs_0_.refs_4_), channel_id=1, source_target_pairs={{0,8},{1,9},{2,10},{3,11},{4,12},{5,13},{6,14},{7,15},{8,0},{9,1},... | collective-permute-start | bytes 884744 | tf_op jit(solution)/shard_map/ppermute | solution.py:49
  19.5 10.0 %copy-start.1 = (bf16[64,2304]{1,0:T(8,128)(2,1)}, bf16[64,2304]{1,0:T(8,128)(2,1)S(1)}, u32[]{:S(2)}) copy-start(bf16[64,2304]{1,0:T(8,128)(2,1)S(1)} %collective-permute-done.refs_1_) | copy-start | bytes 884740
  22.1 0.7 copy-start.3
  22.8 6.7 %collective-permute-start.6 = (bf16[64,2304]{1,0:T(8,128)(2,1)S(1)}, bf16[64,2304]{1,0:T(8,128)(2,1)S(1)}, u32[]{:S(2)}, u32[]{:S(2)}) collective-permute-start(bf16[64,2304]{1,0:T(8,128)(2,1)S(1)} %collective-permute-done.1.refs_5_.refs_1_), channel_id=1, source_target_pairs={{0,16},{1,17},{2,18},{3,19},{4,20},{5,21},{6,22},{7,23},{8,24},{9,... | collective-permute-start | bytes 884744 | tf_op jit(solution)/shard_map/ppermute | solution.py:49
  25.2 10.2 %collective-permute-start.7 = (bf16[128,2304]{1,0:T(8,128)(2,1)}, bf16[128,2304]{1,0:T(8,128)(2,1)S(1)}, u32[]{:S(2)}, u32[]{:S(2)}) collective-permute-start(bf16[128,2304]{1,0:T(8,128)(2,1)} %pad_maximum_fusion), channel_id=1, source_target_pairs={{0,4},{1,5},{2,6},{3,7},{4,0},{5,1},{6,2},{7,3},{8,12},{9,13},{10,... | collective-permute-start | bytes 1769480 | tf_op jit(solution)/shard_map/ppermute | solution.py:49
  25.2 9.4 %collective-permute-start.5 = (bf16[64,2304]{1,0:T(8,128)(2,1)S(1)}, bf16[64,2304]{1,0:T(8,128)(2,1)S(1)}, u32[]{:S(2)}, u32[]{:S(2)}) collective-permute-start(bf16[64,2304]{1,0:T(8,128)(2,1)S(1)} %collective-permute-done.refs_1_), channel_id=1, source_target_pairs={{0,8},{1,9},{2,10},{3,11},{4,12},{5,13},{6,14},{7,15},{8,0},{9,1},... | collective-permute-start | bytes 884744 | tf_op jit(solution)/shard_map/ppermute | solution.py:49
  29.5 5.8 %collective-permute-start.8 = (bf16[64,2304]{1,0:T(8,128)(2,1)S(1)}, bf16[64,2304]{1,0:T(8,128)(2,1)S(1)}, u32[]{:S(2)}, u32[]{:S(2)}) collective-permute-start(bf16[64,2304]{1,0:T(8,128)(2,1)S(1)} %collective-permute-done.6.refs_7_.refs_3_), channel_id=1, source_target_pairs={{0,4},{1,5},{2,6},{3,7},{4,0},{5,1},{6,2},{7,3},{8,12},{9,13},{10,... | collective-permute-start | bytes 884744 | tf_op jit(solution)/shard_map/ppermute | solution.py:49
  34.6 0.7 copy-start.5
  35.4 1.0 %copy-start.2 = (bf16[64,2304]{1,0:T(8,128)(2,1)S(1)}, bf16[64,2304]{1,0:T(8,128)(2,1)}, u32[]{:S(2)}) copy-start(bf16[64,2304]{1,0:T(8,128)(2,1)} %copy-done.1) | copy-start | bytes 884740
  36.3 1.0 %copy-start.4 = (bf16[64,2304]{1,0:T(8,128)(2,1)S(1)}, bf16[64,2304]{1,0:T(8,128)(2,1)}, u32[]{:S(2)}) copy-start(bf16[64,2304]{1,0:T(8,128)(2,1)} %copy-done.3) | copy-start | bytes 884740
  37.3 1.0 %copy-start.6 = (bf16[64,2304]{1,0:T(8,128)(2,1)S(1)}, bf16[64,2304]{1,0:T(8,128)(2,1)}, u32[]{:S(2)}) copy-start(bf16[64,2304]{1,0:T(8,128)(2,1)} %copy-done.5) | copy-start | bytes 884740
  43.9 4.4 %copy-start.8 = (f32[3,2,64]{2,1,0:T(2,128)S(1)}, f32[3,2,64]{2,1,0:T(2,128)}, u32[]{:S(2)}) copy-start(f32[3,2,64]{2,1,0:T(2,128)} %get-tuple-element.53) | copy-start | bytes 4612
  43.9 4.4 %copy-start.9 = (f32[3,1,64]{2,1,0:T(1,128)S(1)}, f32[3,1,64]{2,1,0:T(1,128)}, u32[]{:S(2)}) copy-start(f32[3,1,64]{2,1,0:T(1,128)} %get-tuple-element.54) | copy-start | bytes 2308
  43.9 4.5 %copy-start.10 = (f32[3,1,64]{2,1,0:T(1,128)S(1)}, f32[3,1,64]{2,1,0:T(1,128)}, u32[]{:S(2)}) copy-start(f32[3,1,64]{2,1,0:T(1,128)} %get-tuple-element.55) | copy-start | bytes 2308
  43.9 4.5 %copy-start.11 = (f32[3,1,64]{2,1,0:T(1,128)S(1)}, f32[3,1,64]{2,1,0:T(1,128)}, u32[]{:S(2)}) copy-start(f32[3,1,64]{2,1,0:T(1,128)} %get-tuple-element.56) | copy-start | bytes 2308
  43.9 4.5 %copy-start.12 = (f32[3,1,64]{2,1,0:T(1,128)S(1)}, f32[3,1,64]{2,1,0:T(1,128)}, u32[]{:S(2)}) copy-start(f32[3,1,64]{2,1,0:T(1,128)} %get-tuple-element.57) | copy-start | bytes 2308
  48.4 0.6 copy-start.7
  53.8 7.9 %all-to-all-start = ((f32[4,1,768]{2,1,0:T(1,128)}), f32[4,1,768]{2,1,0:T(1,128)S(1)}, u32[]{:S(2)}, u32[]{:S(2)}) async-start(f32[4,1,768]{2,1,0:T(1,128)} %reshape.219), calls=%async_computation | async-start | bytes 24576 | tf_op jit(solution)/shard_map/all_to_all | solution.py:189
  61.7 11.1 %all-to-all-start.1 = ((f32[8,1,1536]{2,1,0:T(1,128)}), f32[8,1,1536]{2,1,0:T(1,128)S(1)}, u32[]{:S(2)}, u32[]{:S(2)}) async-start(f32[8,1,1536]{2,1,0:T(1,128)} %reshape.221), calls=%async_computation.1 | async-start | bytes 98304 | tf_op jit(solution)/shard_map/all_to_all | solution.py:189
  76.1 6.1 %collective-permute-start.9 = (f16[64,896]{1,0:T(8,128)(2,1)S(1)}, f16[64,896]{1,0:T(8,128)(2,1)S(1)}, u32[]{:S(2)}, u32[]{:S(2)}) collective-permute-start(f16[64,896]{1,0:T(8,128)(2,1)S(1)} %convert_element_type.18), channel_id=1, source_target_pairs={{0,1},{1,0},{2,3},{3,2},{4,5},{5,4},{6,7},{7,6},{8,9},{9,8},{10,11... | collective-permute-start | bytes 344072 | tf_op jit(solution)/shard_map/ppermute | solution.py:49
  76.5 7.4 %collective-permute-start.10 = (f16[64,896]{1,0:T(8,128)(2,1)S(1)}, f16[64,896]{1,0:T(8,128)(2,1)S(1)}, u32[]{:S(2)}, u32[]{:S(2)}) collective-permute-start(f16[64,896]{1,0:T(8,128)(2,1)S(1)} %convert_element_type.20), channel_id=1, source_target_pairs={{0,8},{1,9},{2,10},{3,11},{4,12},{5,13},{6,14},{7,15},{8,0},{9,1},... | collective-permute-start | bytes 344072 | tf_op jit(solution)/shard_map/ppermute | solution.py:49
  78.0 5.9 %collective-permute-start.11 = (f16[64,896]{1,0:T(8,128)(2,1)S(1)}, f16[64,896]{1,0:T(8,128)(2,1)S(1)}, u32[]{:S(2)}, u32[]{:S(2)}) collective-permute-start(f16[64,896]{1,0:T(8,128)(2,1)S(1)} %convert_element_type.22), channel_id=1, source_target_pairs={{0,9},{1,8},{2,11},{3,10},{4,13},{5,12},{6,15},{7,14},{8,1},{9,0},... | collective-permute-start | bytes 344072 | tf_op jit(solution)/shard_map/ppermute | solution.py:49

commit v11 on v9

--- a/solution.py
+++ b/solution.py
@@ -53,19 +53,28 @@
     return lax.optimization_barrier((value, other))[0]
 
 
-def gather(own, row_masks, col_masks, count):
+def gather(teacher, student, row_masks, col_masks, count):
     *plane_masks, core_mask = col_masks
-    row, col, core = {0: own}, {0: own}, []
-    col[1] = send(own, plane_masks[0], count)
-    row[1] = send(own, row_masks[0], count)
-    core.append(send(own, core_mask, count))
-    late = after(own, core[0])
+
+    def join(pair):
+        shape = (pair[0].shape[0], sum(value.shape[1] for value in pair))
+        return call(join_kernel, pair, jax.ShapeDtypeStruct(shape, pair[0].dtype))
+
+    col_t, row_t = send(teacher, plane_masks[0], count), send(teacher, row_masks[0], count)
+    swapped = [send(value, core_mask, count) for value in (teacher, student)]
+    late_t, late_s = after((teacher, student), swapped)
+    own = join([late_t, late_s])
+    row, col, core = {0: own}, {0: own}, [join(swapped)]
     sides = ((row, row_masks), (col, plane_masks))
     for side, masks in sides:
         for b, mask in enumerate(masks):
             if b:
-                side[1 << b] = send(late, mask, count)
-    row[1], col[1] = after((row[1], col[1]), (row[2], col[2]))
+                side[1 << b] = send(own, mask, count)
+    col_s = send(late_s, plane_masks[0], count)
+    row_t, col_t, late = lax.optimization_barrier((row_t, col_t, student))
+    row_s = send(late, row_masks[0], count)
+    pairs = (row_t, row_s), (col_t, col_s)
+    row[1], col[1] = map(join, after(pairs, (row[2], col[2])))
     places = [0]
     for level in range(1, len(row_masks) + 1):
         for side, masks in sides:
@@ -86,9 +95,9 @@
     return values[0]
 
 
-def join_kernel(teacher, student, own):
-    own[:, : teacher.shape[1]] = teacher[...]
-    own[:, teacher.shape[1] :] = student[...]
+def join_kernel(left, right, both):
+    both[:, : left.shape[1]] = left[...]
+    both[:, left.shape[1] :] = right[...]
 
 
 def put_sums(parts, row_part, col_part):
@@ -115,11 +124,12 @@
     put_sums([student * student, teacher * teacher, student * teacher], row_part, col_part)
 
 
-def call(kernel, operands, outputs, flops=0):
+def call(kernel, operands, outputs, flops=0, **options):
     size = sum(math.prod(a.shape) * a.dtype.itemsize for a in [*operands, *jax.tree.leaves(outputs)])
     return pl.pallas_call(
         kernel,
         out_shape=outputs,
+        **options,
         compiler_params=pltpu.CompilerParams(vmem_limit_bytes=VMEM),
         cost_estimate=pl.CostEstimate(flops=flops, bytes_accessed=size, transcendentals=0),
     )(*operands)
@@ -182,8 +192,7 @@
     n_row, n_col = 1 << len(row_masks), 1 << len(col_masks)
 
     depth = teacher.shape[1] + student.shape[1]
-    own = call(join_kernel, [teacher, student], jax.ShapeDtypeStruct((rows, depth), teacher.dtype))
-    row, col, places = gather(own, row_masks, col_masks, count)
+    row, col, places = gather(teacher, student, row_masks, col_masks, count)
     shape, width = (n_row * rows, n_col * rows), student.shape[1]
 
     def f32(*dims):
@@ -199,7 +208,9 @@
         if place < len(col_masks):
             col_part = add_partner(col_part, col_masks, place, count)
         if place < len(row_masks):
-            row_part = after(add_partner(row_part, row_masks, place, count), col_part)
+            row_part = add_partner(row_part, row_masks, place, count)
+        if place + 1 < len(row_masks):
+            row_part, col_part = lax.optimization_barrier((row_part, col_part))
     row_sum, col_sum = row_part.reshape(3, 1, -1), col_part.reshape(3, 1, -1)
 
     own, share, *pieces = call(

time: 55.7 us -> 57.4 us (1.031)
  starting transfers between devices: 20.7 us -> 25.4 us
  waiting for transfers between devices: 29.1 us -> 25.9 us
    ppermute x17 -> x20, starting transfers between devices: 20.7 us -> 25.4 us  [send(): return lax.ppermute(value, AXES, [(i, i ^ mask) for i in range(count)])]
    ppermute x17 -> x20, waiting for transfers between devices: 29.1 us -> 25.9 us  [send(): return lax.ppermute(value, AXES, [(i, i ^ mask) for i in range(count)])]
    pallas_call x4 -> x7, Pallas kernels: 2.75 us -> 2.82 us  [call(): pl.pallas_call(kernel, out_shape=outputs, **options, compiler_params=pltp...]
  transfers between devices with their start and end apart: 17 -> 20, of which waited for: 11 -> 11; matrix products, arithmetic and copies ran while one was open for 0% -> 0% of each run, Pallas kernels for 0% -> 0%
where the time goes in v11:
time: 57.4 us; the launch traced here: 57.2 us
  waiting for transfers between devices  25.9 us (45%)
  starting transfers between devices  25.4 us (44%)
  Pallas kernels  2.82 us (5%)
  local copies, waits for them, and re-layouts  2.09 us (4%)
  between operations  0.76 us (1%)
    ppermute x20, waiting for transfers between devices, send(): return lax.ppermute(value, AXES, [(i, i ^ mask) for i in range(count)])  25.9 us
    ppermute x20, starting transfers between devices, send(): return lax.ppermute(value, AXES, [(i, i ^ mask) for i in range(count)])  25.4 us
    pallas_call x7, Pallas kernels, call(): pl.pallas_call(kernel, out_shape=outputs, **options, compiler_params=pltp...  2.82 us
    unnamed x4, local copies, waits for them, and re-layouts  1.84 us
  transfers between devices with their start and end apart: 20, of which 11 were waited for; matrix products, arithmetic and copies ran while one was open for 0% of the time, Pallas kernels for 0%

profile of v11, /device:TPU:0, one launch (start us, length us, event | category | flops | bytes accessed | tf_op | source)
XLA Modules:
  0.0 57.2 jit_solution(15707301134229378076)
XLA Ops:
  0.6 0.5 collective-permute-start
  1.2 4.0 %collective-permute-start.3 = (bf16[64,1536]{1,0:T(8,128)(2,1)}, bf16[64,1536]{1,0:T(8,128)(2,1)S(1)}, u32[]{:S(2)}, u32[]{:S(2)}) collective-permute-start(bf16[64,1536]{1,0:T(8,128)(2,1)} %left), channel_id=1, source_target_pairs={{0,2},{1,3},{2,0},{3,1},{4,6},{5,7},{6,4},{7,5},{8,10},{9,11},{10,... | collective-permute-start | bytes 589832 | tf_op jit(solution)/shard_map/ppermute | solution.py:49
  5.2 1.6 %collective-permute-start.2 = (bf16[64,1536]{1,0:T(8,128)(2,1)}, bf16[64,1536]{1,0:T(8,128)(2,1)S(1)}, u32[]{:S(2)}, u32[]{:S(2)}) collective-permute-start(bf16[64,1536]{1,0:T(8,128)(2,1)} %left), channel_id=1, source_target_pairs={{0,1},{1,0},{2,3},{3,2},{4,5},{5,4},{6,7},{7,6},{8,9},{9,8},{10,11... | collective-permute-start | bytes 589832 | tf_op jit(solution)/shard_map/ppermute | solution.py:49
  6.8 0.9 %copy-done = bf16[64,1536]{1,0:T(8,128)(2,1)S(1)} copy-done((bf16[64,1536]{1,0:T(8,128)(2,1)S(1)}, bf16[64,1536]{1,0:T(8,128)(2,1)}, u32[]{:S(2)}) %copy-start) | copy-done | bytes 196632
  7.8 0.9 %copy-done.1 = bf16[64,768]{1,0:T(8,128)(2,1)S(1)} copy-done((bf16[64,768]{1,0:T(8,128)(2,1)S(1)}, bf16[64,768]{1,0:T(8,128)(2,1)}, u32[]{:S(2)}) %copy-start.1) | copy-done | bytes 98328
  8.7 1.6 %collective-permute-start.7 = (bf16[64,2304]{1,0:T(8,128)(2,1)S(1)}, bf16[64,2304]{1,0:T(8,128)(2,1)S(1)}, u32[]{:S(2)}, u32[]{:S(2)}) collective-permute-start(bf16[64,2304]{1,0:T(8,128)(2,1)S(1)} %shard_map.41.refs_0_.refs_4_), channel_id=1, source_target_pairs={{0,16},{1,17},{2,18},{3,19},{4,20},{5,21},{6,22},{7,23},{8,24},{9,... | collective-permute-start | bytes 884744 | tf_op jit(solution)/shard_map/ppermute | solution.py:49
  10.3 1.5 %collective-permute-start.6 = (bf16[64,2304]{1,0:T(8,128)(2,1)S(1)}, bf16[64,2304]{1,0:T(8,128)(2,1)S(1)}, u32[]{:S(2)}, u32[]{:S(2)}) collective-permute-start(bf16[64,2304]{1,0:T(8,128)(2,1)S(1)} %shard_map.41.refs_0_.refs_4_), channel_id=1, source_target_pairs={{0,8},{1,9},{2,10},{3,11},{4,12},{5,13},{6,14},{7,15},{8,0},{9,1},... | collective-permute-start | bytes 884744 | tf_op jit(solution)/shard_map/ppermute | solution.py:49
  11.8 0.3 collective-permute-start.5
  12.1 3.7 %collective-permute-done.3.left = bf16[64,1536]{1,0:T(8,128)(2,1)S(1)} collective-permute-done((bf16[64,1536]{1,0:T(8,128)(2,1)}, bf16[64,1536]{1,0:T(8,128)(2,1)S(1)}, u32[]{:S(2)}, u32[]{:S(2)}) %collective-permute-start.3) | collective-permute-done | bytes 196640 | tf_op jit(solution)/shard_map/ppermute | solution.py:49
  15.8 1.7 %collective-permute-start.4 = (bf16[64,768]{1,0:T(8,128)(2,1)S(1)}, bf16[64,768]{1,0:T(8,128)(2,1)S(1)}, u32[]{:S(2)}, u32[]{:S(2)}) collective-permute-start(bf16[64,768]{1,0:T(8,128)(2,1)S(1)} %copy-done.1), channel_id=1, source_target_pairs={{0,1},{1,0},{2,3},{3,2},{4,5},{5,4},{6,7},{7,6},{8,9},{9,8},{10,11... | collective-permute-start | bytes 294920 | tf_op jit(solution)/shard_map/ppermute | solution.py:49
  17.5 1.6 %collective-permute-done.5.right = bf16[64,768]{1,0:T(8,128)(2,1)S(1)} collective-permute-done((bf16[64,768]{1,0:T(8,128)(2,1)S(1)}, bf16[64,768]{1,0:T(8,128)(2,1)S(1)}, u32[]{:S(2)}, u32[]{:S(2)}) %collective-permute-start.5) | collective-permute-done | bytes 98336 | tf_op jit(solution)/shard_map/ppermute | solution.py:49
  19.1 1.3 %collective-permute-done.4.right = bf16[64,768]{1,0:T(8,128)(2,1)S(1)} collective-permute-done((bf16[64,768]{1,0:T(8,128)(2,1)S(1)}, bf16[64,768]{1,0:T(8,128)(2,1)S(1)}, u32[]{:S(2)}, u32[]{:S(2)}) %collective-permute-start.4) | collective-permute-done | bytes 98336 | tf_op jit(solution)/shard_map/ppermute | solution.py:49
  20.4 2.3 %collective-permute-start.9 = (bf16[64,2304]{1,0:T(8,128)(2,1)S(1)}, bf16[64,2304]{1,0:T(8,128)(2,1)S(1)}, u32[]{:S(2)}, u32[]{:S(2)}) collective-permute-start(bf16[64,2304]{1,0:T(8,128)(2,1)S(1)} %shard_map.43.refs_5_.refs_1_), channel_id=1, source_target_pairs={{0,16},{1,17},{2,18},{3,19},{4,20},{5,21},{6,22},{7,23},{8,24},{9,... | collective-permute-start | bytes 884744 | tf_op jit(solution)/shard_map/ppermute | solution.py:49
  22.9 1.6 %collective-permute-start.8 = (bf16[64,2304]{1,0:T(8,128)(2,1)S(1)}, bf16[64,2304]{1,0:T(8,128)(2,1)S(1)}, u32[]{:S(2)}, u32[]{:S(2)}) collective-permute-start(bf16[64,2304]{1,0:T(8,128)(2,1)S(1)} %shard_map.42.refs_1_), channel_id=1, source_target_pairs={{0,8},{1,9},{2,10},{3,11},{4,12},{5,13},{6,14},{7,15},{8,0},{9,1},... | collective-permute-start | bytes 884744 | tf_op jit(solution)/shard_map/ppermute | solution.py:49
  24.5 3.0 %collective-permute-done.9.refs_7_.refs_3_ = bf16[64,2304]{1,0:T(8,128)(2,1)S(1)} collective-permute-done((bf16[64,2304]{1,0:T(8,128)(2,1)S(1)}, bf16[64,2304]{1,0:T(8,128)(2,1)S(1)}, u32[]{:S(2)}, u32[]{:S(2)}) %collective-permute-start.9) | collective-permute-done | bytes 294944 | tf_op jit(solution)/shard_map/ppermute | solution.py:49
  27.5 4.9 %collective-permute-done.8.refs_3_ = bf16[64,2304]{1,0:T(8,128)(2,1)S(1)} collective-permute-done((bf16[64,2304]{1,0:T(8,128)(2,1)S(1)}, bf16[64,2304]{1,0:T(8,128)(2,1)S(1)}, u32[]{:S(2)}, u32[]{:S(2)}) %collective-permute-start.8) | collective-permute-done | bytes 294944 | tf_op jit(solution)/shard_map/ppermute | solution.py:49
  32.4 1.0 %shard_map.45 = (f32[256,512]{1,0:T(8,128)S(1)}, f32[256,512]{1,0:T(8,128)S(1)}, f32[3,4,64]{2,1,0:T(4,128)S(1)}, f32[3,8,64]{2,1,0:T(8,128)S(1)}) custom-call(bf16[64,2304]{1,0:T(8,128)(2,1)S(1)} %shard_map.41.refs_0_.refs_4_, bf16[64,2304]{1,0:T(8,128)(2,1)S(1)} %shard_map.42.refs_1_, bf16[64,2304]{1,0:T(8,128)(2,1)S(1)} %collective-permute-done.6.refs_2_, ...), custom_call_target="tpu_custom_call" | custom-call | flops 603979776 | bytes 4596736 | tf_op jit(solution)/shard_map/pallas_call | solution.py:129
  33.4 1.6 %collective-permute-start.13 = (f32[3,8,64]{2,1,0:T(8,128)S(1)}, f32[3,8,64]{2,1,0:T(8,128)S(1)}, u32[]{:S(2)}, u32[]{:S(2)}) collective-permute-start(f32[3,8,64]{2,1,0:T(8,128)S(1)} %get-tuple-element.36), channel_id=1, source_target_pairs={{0,2},{1,3},{2,0},{3,1},{4,6},{5,7},{6,4},{7,5},{8,10},{9,11},{10,... | collective-permute-start | bytes 18440 | tf_op jit(solution)/shard_map/ppermute | solution.py:49
  35.0 2.5 %collective-permute-start.12 = (f32[3,4,64]{2,1,0:T(4,128)S(1)}, f32[3,4,64]{2,1,0:T(4,128)S(1)}, u32[]{:S(2)}, u32[]{:S(2)}) collective-permute-start(f32[3,4,64]{2,1,0:T(4,128)S(1)} %get-tuple-element.35), channel_id=1, source_target_pairs={{0,1},{1,0},{2,3},{3,2},{4,5},{5,4},{6,7},{7,6},{8,9},{9,8},{10,11... | collective-permute-start | bytes 9224 | tf_op jit(solution)/shard_map/ppermute | solution.py:49
  37.5 1.6 %collective-permute-done.12 = f32[3,4,64]{2,1,0:T(4,128)S(1)} collective-permute-done((f32[3,4,64]{2,1,0:T(4,128)S(1)}, f32[3,4,64]{2,1,0:T(4,128)S(1)}, u32[]{:S(2)}, u32[]{:S(2)}) %collective-permute-start.12) | collective-permute-done | bytes 3104 | tf_op jit(solution)/shard_map/ppermute | solution.py:49
  39.2 0.7 %collective-permute-start.15 = (f32[3,8,64]{2,1,0:T(8,128)S(1)}, f32[3,8,64]{2,1,0:T(8,128)S(1)}, u32[]{:S(2)}, u32[]{:S(2)}) collective-permute-start(f32[3,8,64]{2,1,0:T(8,128)S(1)} %add.16), channel_id=1, source_target_pairs={{0,16},{1,17},{2,18},{3,19},{4,20},{5,21},{6,22},{7,23},{8,24},{9,... | collective-permute-start | bytes 18440 | tf_op jit(solution)/shard_map/ppermute | solution.py:49
  40.0 3.0 %collective-permute-done.15 = f32[3,8,64]{2,1,0:T(8,128)S(1)} collective-permute-done((f32[3,8,64]{2,1,0:T(8,128)S(1)}, f32[3,8,64]{2,1,0:T(8,128)S(1)}, u32[]{:S(2)}, u32[]{:S(2)}) %collective-permute-start.15) | collective-permute-done | bytes 6176 | tf_op jit(solution)/shard_map/ppermute | solution.py:49
  43.1 1.6 %collective-permute-start.14 = (f32[3,4,64]{2,1,0:T(4,128)S(1)}, f32[3,4,64]{2,1,0:T(4,128)S(1)}, u32[]{:S(2)}, u32[]{:S(2)}) collective-permute-start(f32[3,4,64]{2,1,0:T(4,128)S(1)} %add.15), channel_id=1, source_target_pairs={{0,8},{1,9},{2,10},{3,11},{4,12},{5,13},{6,14},{7,15},{8,0},{9,1},... | collective-permute-start | bytes 9224 | tf_op jit(solution)/shard_map/ppermute | solution.py:49
  44.6 2.1 %collective-permute-done.14 = f32[3,4,64]{2,1,0:T(4,128)S(1)} collective-permute-done((f32[3,4,64]{2,1,0:T(4,128)S(1)}, f32[3,4,64]{2,1,0:T(4,128)S(1)}, u32[]{:S(2)}, u32[]{:S(2)}) %collective-permute-start.14) | collective-permute-done | bytes 3104 | tf_op jit(solution)/shard_map/ppermute | solution.py:49
  47.0 0.9 %shard_map.46 = (f32[64,768]{1,0:T(8,128)S(1)}, f32[8,128]{1,0:T(8,128)S(1)}, f32[64,896]{1,0:T(8,128)S(1)}, f32[64,896]{1,0:T(8,128)S(1)}, f32[64,896]{1,0:T(8,128)S(1)}) custom-call(f32[256,512]{1,0:T(8,128)S(1)} %get-tuple-element.33.gram_s, f32[256,512]{1,0:T(8,128)S(1)} %get-tuple-element.34.gram_t, f32[3,1,256]{2,1,0:T(1,128)S(1)} %reshape.46.row_sum, ...), custom_call_target="tpu_custom_call" | custom-call | flops 402653184 | bytes 4305920 | tf_op jit(solution)/shard_map/pallas_call | solution.py:129
  47.9 3.0 %collective-permute-start.19 = (f16[64,896]{1,0:T(8,128)(2,1)S(1)}, f16[64,896]{1,0:T(8,128)(2,1)S(1)}, u32[]{:S(2)}, u32[]{:S(2)}) collective-permute-start(f16[64,896]{1,0:T(8,128)(2,1)S(1)} %convert_element_type.22), channel_id=1, source_target_pairs={{0,9},{1,8},{2,11},{3,10},{4,13},{5,12},{6,15},{7,14},{8,1},{9,0},... | collective-permute-start | bytes 344072 | tf_op jit(solution)/shard_map/ppermute | solution.py:49
  50.9 0.5 collective-permute-start.18
  51.5 0.2 collective-permute-start.17
  51.7 2.4 %collective-permute-done.19 = f16[64,896]{1,0:T(8,128)(2,1)S(1)} collective-permute-done((f16[64,896]{1,0:T(8,128)(2,1)S(1)}, f16[64,896]{1,0:T(8,128)(2,1)S(1)}, u32[]{:S(2)}, u32[]{:S(2)}) %collective-permute-start.19) | collective-permute-done | bytes 114720 | tf_op jit(solution)/shard_map/ppermute | solution.py:49
  54.1 2.1 %collective-permute-done.18 = f16[64,896]{1,0:T(8,128)(2,1)S(1)} collective-permute-done((f16[64,896]{1,0:T(8,128)(2,1)S(1)}, f16[64,896]{1,0:T(8,128)(2,1)S(1)}, u32[]{:S(2)}, u32[]{:S(2)}) %collective-permute-start.18) | collective-permute-done | bytes 114720 | tf_op jit(solution)/shard_map/ppermute | solution.py:49
  56.2 0.2 collective-permute-done.17
  56.4 0.8 %shard_map.47 = (f32[64,768]{1,0:T(8,128)}, f32[1,1]{1,0:T(1,128)}) custom-call(f32[64,768]{1,0:T(8,128)S(1)} %get-tuple-element.39.own, f32[8,128]{1,0:T(8,128)S(1)} %get-tuple-element.40.share, f32[64,896]{1,0:T(8,128)S(1)} %convert_element_type.19.refs_0_, f32[64,896]{1,0:T(8,128)S(1)} %convert_element_type.21.refs_1_, ...), custom_call_target="tpu_custom_call" | custom-call | bytes 1085444 | tf_op jit(solution)/shard_map/pallas_call | solution.py:129
  (38 shorter events, 0.7 us)
Async XLA Ops:
  0.6 6.2 %collective-permute-start = (bf16[64,1536]{1,0:T(8,128)(2,1)}, bf16[64,1536]{1,0:T(8,128)(2,1)S(1)}, u32[]{:S(2)}, u32[]{:S(2)}) collective-permute-start(bf16[64,1536]{1,0:T(8,128)(2,1)} %left), channel_id=1, source_target_pairs={{0,4},{1,5},{2,6},{3,7},{4,0},{5,1},{6,2},{7,3},{8,12},{9,13},{10,... | collective-permute-start | bytes 589832 | tf_op jit(solution)/shard_map/ppermute | solution.py:49
  1.1 5.7 %collective-permute-start.1 = (bf16[64,768]{1,0:T(8,128)(2,1)}, bf16[64,768]{1,0:T(8,128)(2,1)S(1)}, u32[]{:S(2)}, u32[]{:S(2)}) collective-permute-start(bf16[64,768]{1,0:T(8,128)(2,1)} %right), channel_id=1, source_target_pairs={{0,4},{1,5},{2,6},{3,7},{4,0},{5,1},{6,2},{7,3},{8,12},{9,13},{10,... | collective-permute-start | bytes 294920 | tf_op jit(solution)/shard_map/ppermute | solution.py:49
  1.2 14.5 %collective-permute-start.3 = (bf16[64,1536]{1,0:T(8,128)(2,1)}, bf16[64,1536]{1,0:T(8,128)(2,1)S(1)}, u32[]{:S(2)}, u32[]{:S(2)}) collective-permute-start(bf16[64,1536]{1,0:T(8,128)(2,1)} %left), channel_id=1, source_target_pairs={{0,2},{1,3},{2,0},{3,1},{4,6},{5,7},{6,4},{7,5},{8,10},{9,11},{10,... | collective-permute-start | bytes 589832 | tf_op jit(solution)/shard_map/ppermute | solution.py:49
  5.2 10.5 %collective-permute-start.2 = (bf16[64,1536]{1,0:T(8,128)(2,1)}, bf16[64,1536]{1,0:T(8,128)(2,1)S(1)}, u32[]{:S(2)}, u32[]{:S(2)}) collective-permute-start(bf16[64,1536]{1,0:T(8,128)(2,1)} %left), channel_id=1, source_target_pairs={{0,1},{1,0},{2,3},{3,2},{4,5},{5,4},{6,7},{7,6},{8,9},{9,8},{10,11... | collective-permute-start | bytes 589832 | tf_op jit(solution)/shard_map/ppermute | solution.py:49
  6.8 1.0 %copy-start = (bf16[64,1536]{1,0:T(8,128)(2,1)S(1)}, bf16[64,1536]{1,0:T(8,128)(2,1)}, u32[]{:S(2)}) copy-start(bf16[64,1536]{1,0:T(8,128)(2,1)} %left) | copy-start | bytes 589828
  7.8 0.9 %copy-start.1 = (bf16[64,768]{1,0:T(8,128)(2,1)S(1)}, bf16[64,768]{1,0:T(8,128)(2,1)}, u32[]{:S(2)}) copy-start(bf16[64,768]{1,0:T(8,128)(2,1)} %right) | copy-start | bytes 294916
  8.7 11.7 %collective-permute-start.7 = (bf16[64,2304]{1,0:T(8,128)(2,1)S(1)}, bf16[64,2304]{1,0:T(8,128)(2,1)S(1)}, u32[]{:S(2)}, u32[]{:S(2)}) collective-permute-start(bf16[64,2304]{1,0:T(8,128)(2,1)S(1)} %shard_map.41.refs_0_.refs_4_), channel_id=1, source_target_pairs={{0,16},{1,17},{2,18},{3,19},{4,20},{5,21},{6,22},{7,23},{8,24},{9,... | collective-permute-start | bytes 884744 | tf_op jit(solution)/shard_map/ppermute | solution.py:49
  10.3 10.1 %collective-permute-start.6 = (bf16[64,2304]{1,0:T(8,128)(2,1)S(1)}, bf16[64,2304]{1,0:T(8,128)(2,1)S(1)}, u32[]{:S(2)}, u32[]{:S(2)}) collective-permute-start(bf16[64,2304]{1,0:T(8,128)(2,1)S(1)} %shard_map.41.refs_0_.refs_4_), channel_id=1, source_target_pairs={{0,8},{1,9},{2,10},{3,11},{4,12},{5,13},{6,14},{7,15},{8,0},{9,1},... | collective-permute-start | bytes 884744 | tf_op jit(solution)/shard_map/ppermute | solution.py:49
  11.8 7.3 %collective-permute-start.5 = (bf16[64,768]{1,0:T(8,128)(2,1)S(1)}, bf16[64,768]{1,0:T(8,128)(2,1)S(1)}, u32[]{:S(2)}, u32[]{:S(2)}) collective-permute-start(bf16[64,768]{1,0:T(8,128)(2,1)S(1)} %copy-done.1), channel_id=1, source_target_pairs={{0,2},{1,3},{2,0},{3,1},{4,6},{5,7},{6,4},{7,5},{8,10},{9,11},{10,... | collective-permute-start | bytes 294920 | tf_op jit(solution)/shard_map/ppermute | solution.py:49
  15.8 4.6 %collective-permute-start.4 = (bf16[64,768]{1,0:T(8,128)(2,1)S(1)}, bf16[64,768]{1,0:T(8,128)(2,1)S(1)}, u32[]{:S(2)}, u32[]{:S(2)}) collective-permute-start(bf16[64,768]{1,0:T(8,128)(2,1)S(1)} %copy-done.1), channel_id=1, source_target_pairs={{0,1},{1,0},{2,3},{3,2},{4,5},{5,4},{6,7},{7,6},{8,9},{9,8},{10,11... | collective-permute-start | bytes 294920 | tf_op jit(solution)/shard_map/ppermute | solution.py:49
  20.4 7.0 %collective-permute-start.9 = (bf16[64,2304]{1,0:T(8,128)(2,1)S(1)}, bf16[64,2304]{1,0:T(8,128)(2,1)S(1)}, u32[]{:S(2)}, u32[]{:S(2)}) collective-permute-start(bf16[64,2304]{1,0:T(8,128)(2,1)S(1)} %shard_map.43.refs_5_.refs_1_), channel_id=1, source_target_pairs={{0,16},{1,17},{2,18},{3,19},{4,20},{5,21},{6,22},{7,23},{8,24},{9,... | collective-permute-start | bytes 884744 | tf_op jit(solution)/shard_map/ppermute | solution.py:49
  22.8 9.6 %collective-permute-start.10 = (bf16[128,2304]{1,0:T(8,128)(2,1)S(1)}, bf16[128,2304]{1,0:T(8,128)(2,1)S(1)}, u32[]{:S(2)}, u32[]{:S(2)}) collective-permute-start(bf16[128,2304]{1,0:T(8,128)(2,1)S(1)} %pad_maximum_fusion), channel_id=1, source_target_pairs={{0,4},{1,5},{2,6},{3,7},{4,0},{5,1},{6,2},{7,3},{8,12},{9,13},{10,... | collective-permute-start | bytes 1769480 | tf_op jit(solution)/shard_map/ppermute | solution.py:49
  22.9 9.5 %collective-permute-start.8 = (bf16[64,2304]{1,0:T(8,128)(2,1)S(1)}, bf16[64,2304]{1,0:T(8,128)(2,1)S(1)}, u32[]{:S(2)}, u32[]{:S(2)}) collective-permute-start(bf16[64,2304]{1,0:T(8,128)(2,1)S(1)} %shard_map.42.refs_1_), channel_id=1, source_target_pairs={{0,8},{1,9},{2,10},{3,11},{4,12},{5,13},{6,14},{7,15},{8,0},{9,1},... | collective-permute-start | bytes 884744 | tf_op jit(solution)/shard_map/ppermute | solution.py:49
  27.4 4.9 %collective-permute-start.11 = (bf16[64,2304]{1,0:T(8,128)(2,1)S(1)}, bf16[64,2304]{1,0:T(8,128)(2,1)S(1)}, u32[]{:S(2)}, u32[]{:S(2)}) collective-permute-start(bf16[64,2304]{1,0:T(8,128)(2,1)S(1)} %collective-permute-done.9.refs_7_.refs_3_), channel_id=1, source_target_pairs={{0,4},{1,5},{2,6},{3,7},{4,0},{5,1},{6,2},{7,3},{8,12},{9,13},{10,... | collective-permute-start | bytes 884744 | tf_op jit(solution)/shard_map/ppermute | solution.py:49
  33.4 5.8 %collective-permute-start.13 = (f32[3,8,64]{2,1,0:T(8,128)S(1)}, f32[3,8,64]{2,1,0:T(8,128)S(1)}, u32[]{:S(2)}, u32[]{:S(2)}) collective-permute-start(f32[3,8,64]{2,1,0:T(8,128)S(1)} %get-tuple-element.36), channel_id=1, source_target_pairs={{0,2},{1,3},{2,0},{3,1},{4,6},{5,7},{6,4},{7,5},{8,10},{9,11},{10,... | collective-permute-start | bytes 18440 | tf_op jit(solution)/shard_map/ppermute | solution.py:49
  35.0 4.1 %collective-permute-start.12 = (f32[3,4,64]{2,1,0:T(4,128)S(1)}, f32[3,4,64]{2,1,0:T(4,128)S(1)}, u32[]{:S(2)}, u32[]{:S(2)}) collective-permute-start(f32[3,4,64]{2,1,0:T(4,128)S(1)} %get-tuple-element.35), channel_id=1, source_target_pairs={{0,1},{1,0},{2,3},{3,2},{4,5},{5,4},{6,7},{7,6},{8,9},{9,8},{10,11... | collective-permute-start | bytes 9224 | tf_op jit(solution)/shard_map/ppermute | solution.py:49
  39.2 3.8 %collective-permute-start.15 = (f32[3,8,64]{2,1,0:T(8,128)S(1)}, f32[3,8,64]{2,1,0:T(8,128)S(1)}, u32[]{:S(2)}, u32[]{:S(2)}) collective-permute-start(f32[3,8,64]{2,1,0:T(8,128)S(1)} %add.16), channel_id=1, source_target_pairs={{0,16},{1,17},{2,18},{3,19},{4,20},{5,21},{6,22},{7,23},{8,24},{9,... | collective-permute-start | bytes 18440 | tf_op jit(solution)/shard_map/ppermute | solution.py:49
  43.0 3.9 %collective-permute-start.16 = (f32[3,8,64]{2,1,0:T(8,128)S(1)}, f32[3,8,64]{2,1,0:T(8,128)S(1)}, u32[]{:S(2)}, u32[]{:S(2)}) collective-permute-start(f32[3,8,64]{2,1,0:T(8,128)S(1)} %add.18), channel_id=1, source_target_pairs={{0,4},{1,5},{2,6},{3,7},{4,0},{5,1},{6,2},{7,3},{8,12},{9,13},{10,... | collective-permute-start | bytes 18440 | tf_op jit(solution)/shard_map/ppermute | solution.py:49
  43.1 3.7 %collective-permute-start.14 = (f32[3,4,64]{2,1,0:T(4,128)S(1)}, f32[3,4,64]{2,1,0:T(4,128)S(1)}, u32[]{:S(2)}, u32[]{:S(2)}) collective-permute-start(f32[3,4,64]{2,1,0:T(4,128)S(1)} %add.15), channel_id=1, source_target_pairs={{0,8},{1,9},{2,10},{3,11},{4,12},{5,13},{6,14},{7,15},{8,0},{9,1},... | collective-permute-start | bytes 9224 | tf_op jit(solution)/shard_map/ppermute | solution.py:49
  47.9 6.2 %collective-permute-start.19 = (f16[64,896]{1,0:T(8,128)(2,1)S(1)}, f16[64,896]{1,0:T(8,128)(2,1)S(1)}, u32[]{:S(2)}, u32[]{:S(2)}) collective-permute-start(f16[64,896]{1,0:T(8,128)(2,1)S(1)} %convert_element_type.22), channel_id=1, source_target_pairs={{0,9},{1,8},{2,11},{3,10},{4,13},{5,12},{6,15},{7,14},{8,1},{9,0},... | collective-permute-start | bytes 344072 | tf_op jit(solution)/shard_map/ppermute | solution.py:49
  50.9 5.2 %collective-permute-start.18 = (f16[64,896]{1,0:T(8,128)(2,1)S(1)}, f16[64,896]{1,0:T(8,128)(2,1)S(1)}, u32[]{:S(2)}, u32[]{:S(2)}) collective-permute-start(f16[64,896]{1,0:T(8,128)(2,1)S(1)} %convert_element_type.20), channel_id=1, source_target_pairs={{0,8},{1,9},{2,10},{3,11},{4,12},{5,13},{6,14},{7,15},{8,0},{9,1},... | collective-permute-start | bytes 344072 | tf_op jit(solution)/shard_map/ppermute | solution.py:49
  51.5 4.9 %collective-permute-start.17 = (f16[64,896]{1,0:T(8,128)(2,1)S(1)}, f16[64,896]{1,0:T(8,128)(2,1)S(1)}, u32[]{:S(2)}, u32[]{:S(2)}) collective-permute-start(f16[64,896]{1,0:T(8,128)(2,1)S(1)} %convert_element_type.18), channel_id=1, source_target_pairs={{0,1},{1,0},{2,3},{3,2},{4,5},{5,4},{6,7},{7,6},{8,9},{9,8},{10,11... | collective-permute-start | bytes 344072 | tf_op jit(solution)/shard_map/ppermute | solution.py:49

commit v12 on v11

--- a/solution.py
+++ b/solution.py
@@ -53,40 +53,91 @@
     return lax.optimization_barrier((value, other))[0]
 
 
+def join(*values):
+    shape = (values[0].shape[0], sum(value.shape[1] for value in values))
+    return call(join_kernel, values, jax.ShapeDtypeStruct(shape, values[0].dtype))
+
+
 def gather(teacher, student, row_masks, col_masks, count):
     *plane_masks, core_mask = col_masks
-
-    def join(pair):
-        shape = (pair[0].shape[0], sum(value.shape[1] for value in pair))
-        return call(join_kernel, pair, jax.ShapeDtypeStruct(shape, pair[0].dtype))
-
-    col_t, row_t = send(teacher, plane_masks[0], count), send(teacher, row_masks[0], count)
-    swapped = [send(value, core_mask, count) for value in (teacher, student)]
-    late_t, late_s = after((teacher, student), swapped)
-    own = join([late_t, late_s])
-    row, col, core = {0: own}, {0: own}, [join(swapped)]
-    sides = ((row, row_masks), (col, plane_masks))
-    for side, masks in sides:
+    row_t, row_s, col_t, col_s = {}, {}, {}, {}
+    sides = ((row_t, row_s, row_masks), (col_t, col_s, plane_masks))
+
+    def whole(value):
+        return (value, 0, value.shape[1])
+
+    def forward(side, masks, keep):
+        for level in range(2, len(masks) + 1):
+            for place in range(1 << len(masks)):
+                if place.bit_count() == level and keep(place):
+                    top = place.bit_length() - 1
+                    side[place] = whole(send(side[place ^ (1 << top)][0], masks[top], count))
+
+    for side_t, _, masks in reversed(sides):
+        side_t[1] = whole(send(teacher, masks[0], count))
+    for _, side_s, masks in reversed(sides):
         for b, mask in enumerate(masks):
             if b:
-                side[1 << b] = send(own, mask, count)
-    col_s = send(late_s, plane_masks[0], count)
-    row_t, col_t, late = lax.optimization_barrier((row_t, col_t, student))
-    row_s = send(late, row_masks[0], count)
-    pairs = (row_t, row_s), (col_t, col_s)
-    row[1], col[1] = map(join, after(pairs, (row[2], col[2])))
-    places = [0]
-    for level in range(1, len(row_masks) + 1):
-        for side, masks in sides:
-            for place in range(1 << len(masks)):
-                if place.bit_count() == level and place not in side:
-                    top = place.bit_length() - 1
-                    side[place] = send(side[place ^ (1 << top)], masks[top], count)
-        ready = [p for p in range(1 << len(plane_masks)) if p.bit_count() == level]
-        if ready:
-            core.append(send(jnp.concatenate([col[p] for p in ready]), core_mask, count))
-            places += ready
-    return [row[p] for p in sorted(row)], [col[p] for p in places] + core, places
+                side_s[1 << b] = whole(send(student, mask, count))
+    own = join(teacher, student)
+    late = after(teacher, (row_s[2][0], col_s[2][0], own))
+    for side_t, _, masks in reversed(sides):
+        side_t[0] = (own, 0, teacher.shape[1])
+        for b, mask in enumerate(masks):
+            if b:
+                side_t[1 << b] = whole(send(late, mask, count))
+
+    def long_way(side_s, masks, gate):
+        forward(side_s, masks, lambda place: not place & 1)
+        half = range(0, 1 << len(masks), 2)
+        parts = [own[:, teacher.shape[1] :]] + [side_s[p][0] for p in half if p]
+        side_s[0] = (own, teacher.shape[1], own.shape[1])
+        got = send(after(join(*parts), gate), masks[0], count)
+        for k, p in enumerate(half):
+            side_s[p | 1] = (got, k * student.shape[1], (k + 1) * student.shape[1])
+
+    first = (row_t[1][0], col_t[1][0])
+    long_way(col_s, plane_masks, ())
+    long_way(row_s, row_masks, first)
+    row_t[1], col_t[1] = map(whole, after(first, (row_t[2][0], col_t[2][0])))
+    for side_t, _, masks in reversed(sides):
+        forward(side_t, masks, lambda place: True)
+
+    core_t, core_s = {}, {}
+    ones = [0] + [1 << b for b in range(len(plane_masks))]
+    rest = [p for p in range(1 << len(plane_masks)) if p.bit_count() > 1]
+    swaps = [
+        [(col_t, core_t, p) for p in ones] + [(col_s, core_s, p) for p in col_s if not p & 1],
+        [(col_t, core_t, p) for p in rest],
+        [(col_s, core_s, p) for p in col_s if p & 1],
+    ]
+    for swap in swaps:
+        arrays = list({id(side[p][0]): side[p][0] for side, _, p in swap}.values())
+        got = send(join(*arrays) if len(arrays) > 1 else arrays[0], core_mask, count)
+        starts = {id(array): sum(a.shape[1] for a in arrays[:k]) for k, array in enumerate(arrays)}
+        for side, core, p in swap:
+            array, start, stop = side[p]
+            core[p] = (got, starts[id(array)] + start, starts[id(array)] + stop)
+    places = sorted(col_t)
+    return (
+        [row_t[p] for p in sorted(row_t)],
+        [row_s[p] for p in sorted(row_s)],
+        [col_t[p] for p in places] + [core_t[p] for p in places],
+        [col_s[p] for p in places] + [core_s[p] for p in places],
+    )
+
+
+def operands_of(*groups):
+    arrays = []
+    for array, _, _ in sum(groups, []):
+        if not any(array is other for other in arrays):
+            arrays.append(array)
+    number = {id(array): k for k, array in enumerate(arrays)}
+    return arrays, [[(number[id(array)], start, stop) for array, start, stop in group] for group in groups]
+
+
+def load(refs, group):
+    return jnp.concatenate([refs[k][:, start:stop] for k, start, stop in group])
 
 
 def tree_sum(values):
@@ -95,9 +146,12 @@
     return values[0]
 
 
-def join_kernel(left, right, both):
-    both[:, : left.shape[1]] = left[...]
-    both[:, left.shape[1] :] = right[...]
+def join_kernel(*refs):
+    *parts, both = refs
+    start = 0
+    for part in parts:
+        both[:, start : start + part.shape[1]] = part[...]
+        start += part.shape[1]
 
 
 def put_sums(parts, row_part, col_part):
@@ -111,16 +165,13 @@
                 sums[k, p : p + 1, :] = source[:, p * rows : (p + 1) * rows]
 
 
-def gram_kernel(n_row, width, *refs):
-    *pieces, gram_s, gram_t, row_part, col_part = refs
-    grams = []
-    for part in (slice(width, None), slice(0, width)):
-        tops, sides = [jnp.concatenate([p[:, part] for p in group]) for group in (pieces[:n_row], pieces[n_row:])]
-        grams.append(
-            lax.dot_general(tops, sides, (((1,), (1,)), ((), ())), preferred_element_type=jnp.float32)
-        )
-    student, teacher = grams
-    gram_s[...], gram_t[...] = grams
+def gram_kernel(groups, *refs):
+    *arrays, gram_s, gram_t, row_part, col_part = refs
+    row_t, row_s, col_t, col_s = [load(arrays, group) for group in groups]
+    dims = (((1,), (1,)), ((), ()))
+    student = lax.dot_general(row_s, col_s, dims, preferred_element_type=jnp.float32)
+    teacher = lax.dot_general(row_t, col_t, dims, preferred_element_type=jnp.float32)
+    gram_s[...], gram_t[...] = student, teacher
     put_sums([student * student, teacher * teacher, student * teacher], row_part, col_part)
 
 
@@ -135,9 +186,9 @@
     )(*operands)
 
 
-def output_kernel(n_row, n_side, first, total, gram_s, gram_t, row_sum, col_sum, *refs):
-    sides, (own, share, *pieces) = refs[:n_side], refs[n_side:]
-    col_s = jnp.concatenate([side[:, first:] for side in sides])
+def output_kernel(n_arrays, group, total, gram_s, gram_t, row_sum, col_sum, *refs):
+    col_s = load(refs[:n_arrays], group)
+    own, share, *pieces = refs[n_arrays:]
     row_alpha, row_beta, _ = coefficients(row_sum[0], row_sum[1], row_sum[2], total)
     col_alpha, col_beta, terms = coefficients(col_sum[0], col_sum[1], col_sum[2], total)
     row_ab = jnp.transpose(jnp.concatenate([row_alpha, row_beta] * 4))
@@ -191,31 +242,32 @@
     row_masks, col_masks = subgroups(blocks, inner)
     n_row, n_col = 1 << len(row_masks), 1 << len(col_masks)
 
-    depth = teacher.shape[1] + student.shape[1]
-    row, col, places = gather(teacher, student, row_masks, col_masks, count)
+    pieces = gather(teacher, student, row_masks, col_masks, count)
     shape, width = (n_row * rows, n_col * rows), student.shape[1]
 
     def f32(*dims):
         return jax.ShapeDtypeStruct(dims, jnp.float32)
 
+    arrays, groups = operands_of(*pieces)
     gram_s, gram_t, row_part, col_part = call(
-        functools.partial(gram_kernel, n_row, teacher.shape[1]),
-        row + col,
+        functools.partial(gram_kernel, groups),
+        arrays,
         [f32(*shape), f32(*shape), f32(3, n_row, rows), f32(3, n_col, rows)],
-        2 * math.prod(shape) * depth,
+        2 * math.prod(shape) * (teacher.shape[1] + width),
     )
     for place in range(max(len(row_masks), len(col_masks))):
         if place < len(col_masks):
             col_part = add_partner(col_part, col_masks, place, count)
         if place < len(row_masks):
             row_part = add_partner(row_part, row_masks, place, count)
-        if place + 1 < len(row_masks):
+        if place < min(len(row_masks), len(col_masks)):
             row_part, col_part = lax.optimization_barrier((row_part, col_part))
     row_sum, col_sum = row_part.reshape(3, 1, -1), col_part.reshape(3, 1, -1)
 
+    arrays, (group,) = operands_of(pieces[3])
     own, share, *pieces = call(
-        functools.partial(output_kernel, n_row, len(col), teacher.shape[1], total),
-        [gram_s, gram_t, row_sum, col_sum, *col],
+        functools.partial(output_kernel, len(arrays), group, total),
+        [gram_s, gram_t, row_sum, col_sum, *arrays],
         [f32(rows, width), f32(8, 128)] + [f32(rows, width + 128)] * (n_row - 1),
         4 * math.prod(shape) * width,
     )

time: 57.4 us -> 54.9 us (0.956)
  starting transfers between devices: 25.4 us -> 22.1 us
  Pallas kernels: 2.82 us -> 3.77 us
  local copies, waits for them, and re-layouts: 2.09 us -> 1.14 us
  waiting for transfers between devices: 25.9 us -> 26.8 us
    ppermute x20 -> x21, starting transfers between devices: 25.4 us -> 22.1 us  [send(): return lax.ppermute(value, AXES, [(i, i ^ mask) for i in range(count)])]
    unnamed x4 -> x2, local copies, waits for them, and re-layouts: 1.84 us -> 0.89 us
    pallas_call x7, Pallas kernels: 2.82 us -> 3.77 us  [call(): pl.pallas_call(kernel, out_shape=outputs, **options, compiler_params=pltp...]
    ppermute x20 -> x21, waiting for transfers between devices: 25.9 us -> 26.8 us  [send(): return lax.ppermute(value, AXES, [(i, i ^ mask) for i in range(count)])]
  transfers between devices with their start and end apart: 20 -> 21, of which waited for: 11 -> 11; matrix products, arithmetic and copies ran while one was open for 0% -> 0% of each run, Pallas kernels for 0% -> 2%
where the time goes in v12:
time: 54.9 us; the launch traced here: 54.7 us
  waiting for transfers between devices  26.8 us (49%)
  starting transfers between devices  22.1 us (40%)
  Pallas kernels  3.77 us (7%)
  local copies, waits for them, and re-layouts  1.14 us (2%)
  between operations  0.79 us (1%)
    ppermute x21, waiting for transfers between devices, send(): return lax.ppermute(value, AXES, [(i, i ^ mask) for i in range(count)])  26.8 us
    ppermute x21, starting transfers between devices, send(): return lax.ppermute(value, AXES, [(i, i ^ mask) for i in range(count)])  22.1 us
    pallas_call x7, Pallas kernels, call(): pl.pallas_call(kernel, out_shape=outputs, **options, compiler_params=pltp...  3.77 us
  transfers between devices with their start and end apart: 21, of which 11 were waited for; matrix products, arithmetic and copies ran while one was open for 0% of the time, Pallas kernels for 2%

profile of v12, /device:TPU:0, one launch (start us, length us, event | category | flops | bytes accessed | tf_op | source)
XLA Modules:
  0.0 54.7 jit_solution(18293838877851242036)
XLA Ops:
  0.6 3.0 %collective-permute-start.3 = (bf16[64,768]{1,0:T(8,128)(2,1)}, bf16[64,768]{1,0:T(8,128)(2,1)S(1)}, u32[]{:S(2)}, u32[]{:S(2)}) collective-permute-start(bf16[64,768]{1,0:T(8,128)(2,1)} %refs_1_.1), channel_id=1, source_target_pairs={{0,16},{1,17},{2,18},{3,19},{4,20},{5,21},{6,22},{7,23},{8,24},{9,... | collective-permute-start | bytes 294920 | tf_op jit(solution)/shard_map/ppermute | solution.py:49
  3.7 1.5 %collective-permute-start.2 = (bf16[64,768]{1,0:T(8,128)(2,1)}, bf16[64,768]{1,0:T(8,128)(2,1)S(1)}, u32[]{:S(2)}, u32[]{:S(2)}) collective-permute-start(bf16[64,768]{1,0:T(8,128)(2,1)} %refs_1_.1), channel_id=1, source_target_pairs={{0,8},{1,9},{2,10},{3,11},{4,12},{5,13},{6,14},{7,15},{8,0},{9,1},... | collective-permute-start | bytes 294920 | tf_op jit(solution)/shard_map/ppermute | solution.py:49
  5.2 1.6 %collective-permute-start = (bf16[64,1536]{1,0:T(8,128)(2,1)}, bf16[64,1536]{1,0:T(8,128)(2,1)S(1)}, u32[]{:S(2)}, u32[]{:S(2)}) collective-permute-start(bf16[64,1536]{1,0:T(8,128)(2,1)} %refs_0_.1), channel_id=1, source_target_pairs={{0,1},{1,0},{2,3},{3,2},{4,5},{5,4},{6,7},{7,6},{8,9},{9,8},{10,11... | collective-permute-start | bytes 589832 | tf_op jit(solution)/shard_map/ppermute | solution.py:49
  6.7 2.6 %collective-permute-start.1 = (bf16[64,1536]{1,0:T(8,128)(2,1)}, bf16[64,1536]{1,0:T(8,128)(2,1)S(1)}, u32[]{:S(2)}, u32[]{:S(2)}) collective-permute-start(bf16[64,1536]{1,0:T(8,128)(2,1)} %refs_0_.1), channel_id=1, source_target_pairs={{0,2},{1,3},{2,0},{3,1},{4,6},{5,7},{6,4},{7,5},{8,10},{9,11},{10,... | collective-permute-start | bytes 589832 | tf_op jit(solution)/shard_map/ppermute | solution.py:49
  9.3 0.9 %copy-done = bf16[64,768]{1,0:T(8,128)(2,1)S(1)} copy-done((bf16[64,768]{1,0:T(8,128)(2,1)S(1)}, bf16[64,768]{1,0:T(8,128)(2,1)}, u32[]{:S(2)}) %copy-start) | copy-done | bytes 98328
  10.2 0.9 %shard_map.41.refs_0_ = bf16[64,2304]{1,0:T(8,128)(2,1)S(1)} custom-call(bf16[64,1536]{1,0:T(8,128)(2,1)} %refs_0_.1, bf16[64,768]{1,0:T(8,128)(2,1)S(1)} %copy-done), custom_call_target="tpu_custom_call" | custom-call | bytes 589824 | tf_op jit(solution)/shard_map/pallas_call | solution.py:180
  11.2 0.6 %collective-permute-start.5 = (bf16[64,1536]{1,0:T(8,128)(2,1)}, bf16[64,1536]{1,0:T(8,128)(2,1)S(1)}, u32[]{:S(2)}, u32[]{:S(2)}) collective-permute-start(bf16[64,1536]{1,0:T(8,128)(2,1)} %refs_0_.1), channel_id=1, source_target_pairs={{0,16},{1,17},{2,18},{3,19},{4,20},{5,21},{6,22},{7,23},{8,24},{9,... | collective-permute-start | bytes 589832 | tf_op jit(solution)/shard_map/ppermute | solution.py:49
  11.8 0.5 collective-permute-start.4
  12.3 3.2 %collective-permute-done.refs_1_ = bf16[64,1536]{1,0:T(8,128)(2,1)S(1)} collective-permute-done((bf16[64,1536]{1,0:T(8,128)(2,1)}, bf16[64,1536]{1,0:T(8,128)(2,1)S(1)}, u32[]{:S(2)}, u32[]{:S(2)}) %collective-permute-start) | collective-permute-done | bytes 196640 | tf_op jit(solution)/shard_map/ppermute | solution.py:49
  15.5 2.4 %collective-permute-done.1.refs_1_.refs_6_ = bf16[64,1536]{1,0:T(8,128)(2,1)S(1)} collective-permute-done((bf16[64,1536]{1,0:T(8,128)(2,1)}, bf16[64,1536]{1,0:T(8,128)(2,1)S(1)}, u32[]{:S(2)}, u32[]{:S(2)}) %collective-permute-start.1) | collective-permute-done | bytes 196640 | tf_op jit(solution)/shard_map/ppermute | solution.py:49
  18.1 0.4 collective-permute-start.11
  18.5 1.2 %collective-permute-start.8 = (bf16[64,1536]{1,0:T(8,128)(2,1)S(1)}, bf16[64,1536]{1,0:T(8,128)(2,1)S(1)}, u32[]{:S(2)}, u32[]{:S(2)}) collective-permute-start(bf16[64,1536]{1,0:T(8,128)(2,1)S(1)} %collective-permute-done.1.refs_1_.refs_6_), channel_id=1, source_target_pairs={{0,16},{1,17},{2,18},{3,19},{4,20},{5,21},{6,22},{7,23},{8,24},{9,... | collective-permute-start | bytes 589832 | tf_op jit(solution)/shard_map/ppermute | solution.py:49
  19.7 2.0 %collective-permute-start.7 = (bf16[64,1536]{1,0:T(8,128)(2,1)S(1)}, bf16[64,1536]{1,0:T(8,128)(2,1)S(1)}, u32[]{:S(2)}, u32[]{:S(2)}) collective-permute-start(bf16[64,1536]{1,0:T(8,128)(2,1)S(1)} %shard_map.42), channel_id=1, source_target_pairs={{0,1},{1,0},{2,3},{3,2},{4,5},{5,4},{6,7},{7,6},{8,9},{9,8},{10,11... | collective-permute-start | bytes 589832 | tf_op jit(solution)/shard_map/ppermute | solution.py:49
  21.8 0.6 %collective-permute-start.6 = (bf16[64,1536]{1,0:T(8,128)(2,1)S(1)}, bf16[64,1536]{1,0:T(8,128)(2,1)S(1)}, u32[]{:S(2)}, u32[]{:S(2)}) collective-permute-start(bf16[64,1536]{1,0:T(8,128)(2,1)S(1)} %collective-permute-done.refs_1_), channel_id=1, source_target_pairs={{0,8},{1,9},{2,10},{3,11},{4,12},{5,13},{6,14},{7,15},{8,0},{9,1},... | collective-permute-start | bytes 589832 | tf_op jit(solution)/shard_map/ppermute | solution.py:49
  22.4 8.2 %collective-permute-done.11.refs_11_.refs_1_ = bf16[64,1536]{1,0:T(8,128)(2,1)S(1)} collective-permute-done((bf16[64,1536]{1,0:T(8,128)(2,1)S(1)}, bf16[64,1536]{1,0:T(8,128)(2,1)S(1)}, u32[]{:S(2)}, u32[]{:S(2)}) %collective-permute-start.11) | collective-permute-done | bytes 196640 | tf_op jit(solution)/shard_map/ppermute | solution.py:49
  30.6 0.5 collective-permute-start.10
  31.1 0.9 %collective-permute-done.12.refs_13_.refs_4_ = bf16[64,1536]{1,0:T(8,128)(2,1)S(1)} collective-permute-done((bf16[64,1536]{1,0:T(8,128)(2,1)S(1)}, bf16[64,1536]{1,0:T(8,128)(2,1)S(1)}, u32[]{:S(2)}, u32[]{:S(2)}) %collective-permute-start.12) | collective-permute-done | bytes 196640 | tf_op jit(solution)/shard_map/ppermute | solution.py:49
  32.3 1.0 %shard_map.45 = (f32[256,512]{1,0:T(8,128)S(1)}, f32[256,512]{1,0:T(8,128)S(1)}, f32[3,4,64]{2,1,0:T(4,128)S(1)}, f32[3,8,64]{2,1,0:T(8,128)S(1)}) custom-call(bf16[64,2304]{1,0:T(8,128)(2,1)S(1)} %shard_map.41.refs_0_, bf16[64,1536]{1,0:T(8,128)(2,1)S(1)} %collective-permute-done.refs_1_, bf16[64,1536]{1,0:T(8,128)(2,1)S(1)} %collective-permute-done.4.refs_2_, ...), custom_call_target="tpu_custom_call" | custom-call | flops 603979776 | bytes 4301824 | tf_op jit(solution)/shard_map/pallas_call | solution.py:180
  33.3 1.9 %collective-permute-start.13 = (f32[3,4,64]{2,1,0:T(4,128)S(1)}, f32[3,4,64]{2,1,0:T(4,128)S(1)}, u32[]{:S(2)}, u32[]{:S(2)}) collective-permute-start(f32[3,4,64]{2,1,0:T(4,128)S(1)} %get-tuple-element.27), channel_id=1, source_target_pairs={{0,1},{1,0},{2,3},{3,2},{4,5},{5,4},{6,7},{7,6},{8,9},{9,8},{10,11... | collective-permute-start | bytes 9224 | tf_op jit(solution)/shard_map/ppermute | solution.py:49
  35.2 1.8 %collective-permute-done.13 = f32[3,4,64]{2,1,0:T(4,128)S(1)} collective-permute-done((f32[3,4,64]{2,1,0:T(4,128)S(1)}, f32[3,4,64]{2,1,0:T(4,128)S(1)}, u32[]{:S(2)}, u32[]{:S(2)}) %collective-permute-start.13) | collective-permute-done | bytes 3104 | tf_op jit(solution)/shard_map/ppermute | solution.py:49
  37.1 0.8 %collective-permute-done.14 = f32[3,8,64]{2,1,0:T(8,128)S(1)} collective-permute-done((f32[3,8,64]{2,1,0:T(8,128)S(1)}, f32[3,8,64]{2,1,0:T(8,128)S(1)}, u32[]{:S(2)}, u32[]{:S(2)}) %collective-permute-start.14) | collective-permute-done | bytes 6176 | tf_op jit(solution)/shard_map/ppermute | solution.py:49
  38.0 1.3 %collective-permute-start.16 = (f32[3,8,64]{2,1,0:T(8,128)S(1)}, f32[3,8,64]{2,1,0:T(8,128)S(1)}, u32[]{:S(2)}, u32[]{:S(2)}) collective-permute-start(f32[3,8,64]{2,1,0:T(8,128)S(1)} %add.16), channel_id=1, source_target_pairs={{0,16},{1,17},{2,18},{3,19},{4,20},{5,21},{6,22},{7,23},{8,24},{9,... | collective-permute-start | bytes 18440 | tf_op jit(solution)/shard_map/ppermute | solution.py:49
  39.3 0.5 collective-permute-start.15
  39.8 3.1 %collective-permute-done.15 = f32[3,4,64]{2,1,0:T(4,128)S(1)} collective-permute-done((f32[3,4,64]{2,1,0:T(4,128)S(1)}, f32[3,4,64]{2,1,0:T(4,128)S(1)}, u32[]{:S(2)}, u32[]{:S(2)}) %collective-permute-start.15) | collective-permute-done | bytes 3104 | tf_op jit(solution)/shard_map/ppermute | solution.py:49
  43.1 1.1 %collective-permute-done.17 = f32[3,8,64]{2,1,0:T(8,128)S(1)} collective-permute-done((f32[3,8,64]{2,1,0:T(8,128)S(1)}, f32[3,8,64]{2,1,0:T(8,128)S(1)}, u32[]{:S(2)}, u32[]{:S(2)}) %collective-permute-start.17) | collective-permute-done | bytes 6176 | tf_op jit(solution)/shard_map/ppermute | solution.py:49
  44.3 0.9 %shard_map.46 = (f32[64,768]{1,0:T(8,128)S(1)}, f32[8,128]{1,0:T(8,128)S(1)}, f32[64,896]{1,0:T(8,128)S(1)}, f32[64,896]{1,0:T(8,128)S(1)}, f32[64,896]{1,0:T(8,128)S(1)}) custom-call(f32[256,512]{1,0:T(8,128)S(1)} %get-tuple-element.25.gram_s, f32[256,512]{1,0:T(8,128)S(1)} %get-tuple-element.26.gram_t, f32[3,1,256]{2,1,0:T(1,128)S(1)} %reshape.48.row_sum, ...), custom_call_target="tpu_custom_call" | custom-call | flops 402653184 | bytes 3519488 | tf_op jit(solution)/shard_map/pallas_call | solution.py:180
  45.2 1.5 %collective-permute-start.20 = (f16[64,896]{1,0:T(8,128)(2,1)S(1)}, f16[64,896]{1,0:T(8,128)(2,1)S(1)}, u32[]{:S(2)}, u32[]{:S(2)}) collective-permute-start(f16[64,896]{1,0:T(8,128)(2,1)S(1)} %convert_element_type.22), channel_id=1, source_target_pairs={{0,9},{1,8},{2,11},{3,10},{4,13},{5,12},{6,15},{7,14},{8,1},{9,0},... | collective-permute-start | bytes 344072 | tf_op jit(solution)/shard_map/ppermute | solution.py:49
  46.7 1.0 %collective-permute-start.19 = (f16[64,896]{1,0:T(8,128)(2,1)S(1)}, f16[64,896]{1,0:T(8,128)(2,1)S(1)}, u32[]{:S(2)}, u32[]{:S(2)}) collective-permute-start(f16[64,896]{1,0:T(8,128)(2,1)S(1)} %convert_element_type.20), channel_id=1, source_target_pairs={{0,8},{1,9},{2,10},{3,11},{4,12},{5,13},{6,14},{7,15},{8,0},{9,1},... | collective-permute-start | bytes 344072 | tf_op jit(solution)/shard_map/ppermute | solution.py:49
  47.8 1.1 %collective-permute-start.18 = (f16[64,896]{1,0:T(8,128)(2,1)S(1)}, f16[64,896]{1,0:T(8,128)(2,1)S(1)}, u32[]{:S(2)}, u32[]{:S(2)}) collective-permute-start(f16[64,896]{1,0:T(8,128)(2,1)S(1)} %convert_element_type.18), channel_id=1, source_target_pairs={{0,1},{1,0},{2,3},{3,2},{4,5},{5,4},{6,7},{7,6},{8,9},{9,8},{10,11... | collective-permute-start | bytes 344072 | tf_op jit(solution)/shard_map/ppermute | solution.py:49
  48.9 3.3 %collective-permute-done.20 = f16[64,896]{1,0:T(8,128)(2,1)S(1)} collective-permute-done((f16[64,896]{1,0:T(8,128)(2,1)S(1)}, f16[64,896]{1,0:T(8,128)(2,1)S(1)}, u32[]{:S(2)}, u32[]{:S(2)}) %collective-permute-start.20) | collective-permute-done | bytes 114720 | tf_op jit(solution)/shard_map/ppermute | solution.py:49
  52.2 1.7 %collective-permute-done.19 = f16[64,896]{1,0:T(8,128)(2,1)S(1)} collective-permute-done((f16[64,896]{1,0:T(8,128)(2,1)S(1)}, f16[64,896]{1,0:T(8,128)(2,1)S(1)}, u32[]{:S(2)}, u32[]{:S(2)}) %collective-permute-start.19) | collective-permute-done | bytes 114720 | tf_op jit(solution)/shard_map/ppermute | solution.py:49
  53.9 0.8 %shard_map.47 = (f32[64,768]{1,0:T(8,128)}, f32[1,1]{1,0:T(1,128)}) custom-call(f32[64,768]{1,0:T(8,128)S(1)} %get-tuple-element.33.own, f32[8,128]{1,0:T(8,128)S(1)} %get-tuple-element.34.share, f32[64,896]{1,0:T(8,128)S(1)} %convert_element_type.19.refs_0_, f32[64,896]{1,0:T(8,128)S(1)} %convert_element_type.21.refs_1_, ...), custom_call_target="tpu_custom_call" | custom-call | bytes 1085444 | tf_op jit(solution)/shard_map/pallas_call | solution.py:180
  (38 shorter events, 0.9 us)
Async XLA Ops:
  0.6 10.5 %collective-permute-start.3 = (bf16[64,768]{1,0:T(8,128)(2,1)}, bf16[64,768]{1,0:T(8,128)(2,1)S(1)}, u32[]{:S(2)}, u32[]{:S(2)}) collective-permute-start(bf16[64,768]{1,0:T(8,128)(2,1)} %refs_1_.1), channel_id=1, source_target_pairs={{0,16},{1,17},{2,18},{3,19},{4,20},{5,21},{6,22},{7,23},{8,24},{9,... | collective-permute-start | bytes 294920 | tf_op jit(solution)/shard_map/ppermute | solution.py:49
  3.7 7.5 %collective-permute-start.2 = (bf16[64,768]{1,0:T(8,128)(2,1)}, bf16[64,768]{1,0:T(8,128)(2,1)S(1)}, u32[]{:S(2)}, u32[]{:S(2)}) collective-permute-start(bf16[64,768]{1,0:T(8,128)(2,1)} %refs_1_.1), channel_id=1, source_target_pairs={{0,8},{1,9},{2,10},{3,11},{4,12},{5,13},{6,14},{7,15},{8,0},{9,1},... | collective-permute-start | bytes 294920 | tf_op jit(solution)/shard_map/ppermute | solution.py:49
  5.2 10.4 %collective-permute-start = (bf16[64,1536]{1,0:T(8,128)(2,1)}, bf16[64,1536]{1,0:T(8,128)(2,1)S(1)}, u32[]{:S(2)}, u32[]{:S(2)}) collective-permute-start(bf16[64,1536]{1,0:T(8,128)(2,1)} %refs_0_.1), channel_id=1, source_target_pairs={{0,1},{1,0},{2,3},{3,2},{4,5},{5,4},{6,7},{7,6},{8,9},{9,8},{10,11... | collective-permute-start | bytes 589832 | tf_op jit(solution)/shard_map/ppermute | solution.py:49
  6.7 11.2 %collective-permute-start.1 = (bf16[64,1536]{1,0:T(8,128)(2,1)}, bf16[64,1536]{1,0:T(8,128)(2,1)S(1)}, u32[]{:S(2)}, u32[]{:S(2)}) collective-permute-start(bf16[64,1536]{1,0:T(8,128)(2,1)} %refs_0_.1), channel_id=1, source_target_pairs={{0,2},{1,3},{2,0},{3,1},{4,6},{5,7},{6,4},{7,5},{8,10},{9,11},{10,... | collective-permute-start | bytes 589832 | tf_op jit(solution)/shard_map/ppermute | solution.py:49
  9.3 0.9 %copy-start = (bf16[64,768]{1,0:T(8,128)(2,1)S(1)}, bf16[64,768]{1,0:T(8,128)(2,1)}, u32[]{:S(2)}) copy-start(bf16[64,768]{1,0:T(8,128)(2,1)} %refs_1_.1) | copy-start | bytes 294916
  11.2 6.7 %collective-permute-start.5 = (bf16[64,1536]{1,0:T(8,128)(2,1)}, bf16[64,1536]{1,0:T(8,128)(2,1)S(1)}, u32[]{:S(2)}, u32[]{:S(2)}) collective-permute-start(bf16[64,1536]{1,0:T(8,128)(2,1)} %refs_0_.1), channel_id=1, source_target_pairs={{0,16},{1,17},{2,18},{3,19},{4,20},{5,21},{6,22},{7,23},{8,24},{9,... | collective-permute-start | bytes 589832 | tf_op jit(solution)/shard_map/ppermute | solution.py:49
  11.8 6.2 %collective-permute-start.4 = (bf16[64,1536]{1,0:T(8,128)(2,1)}, bf16[64,1536]{1,0:T(8,128)(2,1)S(1)}, u32[]{:S(2)}, u32[]{:S(2)}) collective-permute-start(bf16[64,1536]{1,0:T(8,128)(2,1)} %refs_0_.1), channel_id=1, source_target_pairs={{0,8},{1,9},{2,10},{3,11},{4,12},{5,13},{6,14},{7,15},{8,0},{9,1},... | collective-permute-start | bytes 589832 | tf_op jit(solution)/shard_map/ppermute | solution.py:49
  18.0 14.3 %collective-permute-start.9 = (bf16[64,6144]{1,0:T(8,128)(2,1)S(1)}, bf16[64,6144]{1,0:T(8,128)(2,1)S(1)}, u32[]{:S(2)}, u32[]{:S(2)}) collective-permute-start(bf16[64,6144]{1,0:T(8,128)(2,1)S(1)} %shard_map.43), channel_id=1, source_target_pairs={{0,4},{1,5},{2,6},{3,7},{4,0},{5,1},{6,2},{7,3},{8,12},{9,13},{10,... | collective-permute-start | bytes 2359304 | tf_op jit(solution)/shard_map/ppermute | solution.py:49
  18.1 12.4 %collective-permute-start.11 = (bf16[64,1536]{1,0:T(8,128)(2,1)S(1)}, bf16[64,1536]{1,0:T(8,128)(2,1)S(1)}, u32[]{:S(2)}, u32[]{:S(2)}) collective-permute-start(bf16[64,1536]{1,0:T(8,128)(2,1)S(1)} %shard_map.44), channel_id=1, source_target_pairs={{0,2},{1,3},{2,0},{3,1},{4,6},{5,7},{6,4},{7,5},{8,10},{9,11},{10,... | collective-permute-start | bytes 589832 | tf_op jit(solution)/shard_map/ppermute | solution.py:49
  18.5 12.1 %collective-permute-start.8 = (bf16[64,1536]{1,0:T(8,128)(2,1)S(1)}, bf16[64,1536]{1,0:T(8,128)(2,1)S(1)}, u32[]{:S(2)}, u32[]{:S(2)}) collective-permute-start(bf16[64,1536]{1,0:T(8,128)(2,1)S(1)} %collective-permute-done.1.refs_1_.refs_6_), channel_id=1, source_target_pairs={{0,16},{1,17},{2,18},{3,19},{4,20},{5,21},{6,22},{7,23},{8,24},{9,... | collective-permute-start | bytes 589832 | tf_op jit(solution)/shard_map/ppermute | solution.py:49
  19.7 11.3 %collective-permute-start.7 = (bf16[64,1536]{1,0:T(8,128)(2,1)S(1)}, bf16[64,1536]{1,0:T(8,128)(2,1)S(1)}, u32[]{:S(2)}, u32[]{:S(2)}) collective-permute-start(bf16[64,1536]{1,0:T(8,128)(2,1)S(1)} %shard_map.42), channel_id=1, source_target_pairs={{0,1},{1,0},{2,3},{3,2},{4,5},{5,4},{6,7},{7,6},{8,9},{9,8},{10,11... | collective-permute-start | bytes 589832 | tf_op jit(solution)/shard_map/ppermute | solution.py:49
  21.8 10.2 %collective-permute-start.6 = (bf16[64,1536]{1,0:T(8,128)(2,1)S(1)}, bf16[64,1536]{1,0:T(8,128)(2,1)S(1)}, u32[]{:S(2)}, u32[]{:S(2)}) collective-permute-start(bf16[64,1536]{1,0:T(8,128)(2,1)S(1)} %collective-permute-done.refs_1_), channel_id=1, source_target_pairs={{0,8},{1,9},{2,10},{3,11},{4,12},{5,13},{6,14},{7,15},{8,0},{9,1},... | collective-permute-start | bytes 589832 | tf_op jit(solution)/shard_map/ppermute | solution.py:49
  30.5 1.4 %collective-permute-start.12 = (bf16[64,1536]{1,0:T(8,128)(2,1)S(1)}, bf16[64,1536]{1,0:T(8,128)(2,1)S(1)}, u32[]{:S(2)}, u32[]{:S(2)}) collective-permute-start(bf16[64,1536]{1,0:T(8,128)(2,1)S(1)} %collective-permute-done.11.refs_11_.refs_1_), channel_id=1, source_target_pairs={{0,4},{1,5},{2,6},{3,7},{4,0},{5,1},{6,2},{7,3},{8,12},{9,13},{10,... | collective-permute-start | bytes 589832 | tf_op jit(solution)/shard_map/ppermute | solution.py:49
  30.6 1.7 %collective-permute-start.10 = (bf16[64,1536]{1,0:T(8,128)(2,1)S(1)}, bf16[64,1536]{1,0:T(8,128)(2,1)S(1)}, u32[]{:S(2)}, u32[]{:S(2)}) collective-permute-start(bf16[64,1536]{1,0:T(8,128)(2,1)S(1)} %collective-permute-done.8.refs_8_), channel_id=1, source_target_pairs={{0,4},{1,5},{2,6},{3,7},{4,0},{5,1},{6,2},{7,3},{8,12},{9,13},{10,... | collective-permute-start | bytes 589832 | tf_op jit(solution)/shard_map/ppermute | solution.py:49
  33.3 4.6 %collective-permute-start.14 = (f32[3,8,64]{2,1,0:T(8,128)S(1)}, f32[3,8,64]{2,1,0:T(8,128)S(1)}, u32[]{:S(2)}, u32[]{:S(2)}) collective-permute-start(f32[3,8,64]{2,1,0:T(8,128)S(1)} %get-tuple-element.28), channel_id=1, source_target_pairs={{0,2},{1,3},{2,0},{3,1},{4,6},{5,7},{6,4},{7,5},{8,10},{9,11},{10,... | collective-permute-start | bytes 18440 | tf_op jit(solution)/shard_map/ppermute | solution.py:49
  33.3 3.7 %collective-permute-start.13 = (f32[3,4,64]{2,1,0:T(4,128)S(1)}, f32[3,4,64]{2,1,0:T(4,128)S(1)}, u32[]{:S(2)}, u32[]{:S(2)}) collective-permute-start(f32[3,4,64]{2,1,0:T(4,128)S(1)} %get-tuple-element.27), channel_id=1, source_target_pairs={{0,1},{1,0},{2,3},{3,2},{4,5},{5,4},{6,7},{7,6},{8,9},{9,8},{10,11... | collective-permute-start | bytes 9224 | tf_op jit(solution)/shard_map/ppermute | solution.py:49
  38.0 5.0 %collective-permute-start.16 = (f32[3,8,64]{2,1,0:T(8,128)S(1)}, f32[3,8,64]{2,1,0:T(8,128)S(1)}, u32[]{:S(2)}, u32[]{:S(2)}) collective-permute-start(f32[3,8,64]{2,1,0:T(8,128)S(1)} %add.16), channel_id=1, source_target_pairs={{0,16},{1,17},{2,18},{3,19},{4,20},{5,21},{6,22},{7,23},{8,24},{9,... | collective-permute-start | bytes 18440 | tf_op jit(solution)/shard_map/ppermute | solution.py:49
  39.3 3.6 %collective-permute-start.15 = (f32[3,4,64]{2,1,0:T(4,128)S(1)}, f32[3,4,64]{2,1,0:T(4,128)S(1)}, u32[]{:S(2)}, u32[]{:S(2)}) collective-permute-start(f32[3,4,64]{2,1,0:T(4,128)S(1)} %add.15), channel_id=1, source_target_pairs={{0,8},{1,9},{2,10},{3,11},{4,12},{5,13},{6,14},{7,15},{8,0},{9,1},... | collective-permute-start | bytes 9224 | tf_op jit(solution)/shard_map/ppermute | solution.py:49
  43.0 1.2 %collective-permute-start.17 = (f32[3,8,64]{2,1,0:T(8,128)S(1)}, f32[3,8,64]{2,1,0:T(8,128)S(1)}, u32[]{:S(2)}, u32[]{:S(2)}) collective-permute-start(f32[3,8,64]{2,1,0:T(8,128)S(1)} %add.18), channel_id=1, source_target_pairs={{0,4},{1,5},{2,6},{3,7},{4,0},{5,1},{6,2},{7,3},{8,12},{9,13},{10,... | collective-permute-start | bytes 18440 | tf_op jit(solution)/shard_map/ppermute | solution.py:49
  45.2 7.0 %collective-permute-start.20 = (f16[64,896]{1,0:T(8,128)(2,1)S(1)}, f16[64,896]{1,0:T(8,128)(2,1)S(1)}, u32[]{:S(2)}, u32[]{:S(2)}) collective-permute-start(f16[64,896]{1,0:T(8,128)(2,1)S(1)} %convert_element_type.22), channel_id=1, source_target_pairs={{0,9},{1,8},{2,11},{3,10},{4,13},{5,12},{6,15},{7,14},{8,1},{9,0},... | collective-permute-start | bytes 344072 | tf_op jit(solution)/shard_map/ppermute | solution.py:49
  46.7 7.2 %collective-permute-start.19 = (f16[64,896]{1,0:T(8,128)(2,1)S(1)}, f16[64,896]{1,0:T(8,128)(2,1)S(1)}, u32[]{:S(2)}, u32[]{:S(2)}) collective-permute-start(f16[64,896]{1,0:T(8,128)(2,1)S(1)} %convert_element_type.20), channel_id=1, source_target_pairs={{0,8},{1,9},{2,10},{3,11},{4,12},{5,13},{6,14},{7,15},{8,0},{9,1},... | collective-permute-start | bytes 344072 | tf_op jit(solution)/shard_map/ppermute | solution.py:49
  47.8 6.1 %collective-permute-start.18 = (f16[64,896]{1,0:T(8,128)(2,1)S(1)}, f16[64,896]{1,0:T(8,128)(2,1)S(1)}, u32[]{:S(2)}, u32[]{:S(2)}) collective-permute-start(f16[64,896]{1,0:T(8,128)(2,1)S(1)} %convert_element_type.18), channel_id=1, source_target_pairs={{0,1},{1,0},{2,3},{3,2},{4,5},{5,4},{6,7},{7,6},{8,9},{9,8},{10,11... | collective-permute-start | bytes 344072 | tf_op jit(solution)/shard_map/ppermute | solution.py:49

commit v13 on v9

v13 whole, which is shorter than its diff:
```python
import functools
import math

import jax
import jax.numpy as jnp
from jax import lax
from jax.experimental import pallas as pl
from jax.experimental.pallas import tpu as pltpu
from jax.sharding import PartitionSpec as P

DS = 768
AXES = ("blk", "inner")
VMEM = 48 * 2**20
SHARE_SCALE = 8.0


EPSILON = 1e-06


def coefficients(sq_student, sq_teacher, cross, total):
    norm_student = jnp.sqrt(sq_student + EPSILON)
    norm_teacher = jnp.sqrt(sq_teacher + EPSILON)
    factor = 2.0 * math.sqrt(total * DS) / total
    cubed = norm_student * norm_student * norm_student
    alpha = factor * (EPSILON / norm_student + cross / norm_teacher) / cubed
    beta = factor / (norm_student * norm_teacher)
    terms = (
        sq_student / (norm_student * norm_student)
        + sq_teacher / (norm_teacher * norm_teacher)
        - 2.0 * cross / (norm_student * norm_teacher)
    )
    return (alpha, beta, terms)


def span(masks):
    out = [0]
    for mask in masks:
        out += [mask ^ other for other in out]
    return out


def subgroups(blocks, inner):
    bits = [1 << b for b in range((inner - 1).bit_length())]
    bits += [inner << b for b in range(1, (blocks - 1).bit_length())]
    return bits[0::2], bits[1::2], inner


def after(value, other):
    return lax.optimization_barrier((value, other))[0]


class Partners:
    def __init__(self, blocks, inner):
        self.count = blocks * inner
        self.rows, self.columns, self.core = subgroups(blocks, inner)

    def swap(self, value):
        return self.row(value, self.core)

    def row(self, value, mask):
        return lax.ppermute(value, AXES, [(i, i ^ mask) for i in range(self.count)])

    def step(self, value, b):
        pairs = []
        for i in range(self.count):
            masks = self.columns if i & self.core else self.rows
            if b < len(masks):
                pairs.append((i, i ^ masks[b]))
        return lax.ppermute(value, AXES, pairs)


def join(*values, axis=1):
    shape = list(values[0].shape)
    shape[axis] = sum(value.shape[axis] for value in values)
    kernel = functools.partial(join_kernel, axis)
    return call(kernel, values, jax.ShapeDtypeStruct(tuple(shape), values[0].dtype))


def gather(teacher, student, partners):
    levels = len(partners.rows)
    swapped = [partners.swap(value) for value in (teacher, student)]
    mine_t, mine_s = {0: join(teacher, swapped[0], axis=0)}, {0: join(student, swapped[1], axis=0)}
    for level in range(1, levels + 1):
        for mine in (mine_t, mine_s):
            for place in range(1, 1 << levels):
                if place.bit_count() == level:
                    top = place.bit_length() - 1
                    mine[place] = partners.step(mine[place ^ (1 << top)], top)

    other_t, other_s = {0: None}, {0: None}
    ones = [1 << b for b in range(levels)]
    rest = [place for place in range(1 << levels) if place.bit_count() > 1]
    groups = [
        [(mine_t, other_t, p) for p in ones] + [(mine_s, other_s, p) for p in ones[1:]],
        [(mine_s, other_s, 1)] + [(mine_t, other_t, p) for p in rest],
        [(mine_s, other_s, p) for p in rest],
    ]
    for group in groups:
        values = [mine[p] for mine, _, p in group]
        got, start = partners.swap(join(*values) if len(values) > 1 else values[0]), 0
        for (_, other, p), value in zip(group, values):
            other[p] = (got, start, start + value.shape[1])
            start += value.shape[1]
    places = range(1 << levels)
    mine = [[(side[p], 0, side[p].shape[1]) for p in places] for side in (mine_t, mine_s)]
    return mine, [[side[p] for p in places] for side in (other_t, other_s)]


def tile_rows(mine, other, n_row, core):
    if core == 0:
        return [(*mine[p], 0) for p in range(n_row)]
    return [(*mine[0], 0)] + [(*other[p], 1) for p in range(1, n_row)]


def tile_columns(mine, other, n_col, core):
    if core == 1:
        return [(*mine[p], half) for half in (0, 1) for p in range(n_col)]
    return [(*(other[p] if p else mine[0]), half if p else 1 - half) for half in (0, 1) for p in range(n_col)]


def operands_of(*groups):
    arrays = []
    for array, *_ in sum(groups, []):
        if not any(array is other for other in arrays):
            arrays.append(array)
    number = {id(array): k for k, array in enumerate(arrays)}
    return arrays, [[(number[id(array)], *place) for array, *place in group] for group in groups]


def load(refs, group):
    rows = refs[0].shape[0] // 2
    return jnp.concatenate([refs[k][half * rows : (half + 1) * rows, a:b] for k, a, b, half in group])


def by_core(body, choices):
    core = lax.rem(lax.axis_index("blk"), 2)
    for k, choice in enumerate(choices):
        pl.when(core == k)(functools.partial(body, choice))


def tree_sum(values):
    while len(values) > 1:
        values = [values[i] + values[i + 1] for i in range(0, len(values), 2)]
    return values[0]


def join_kernel(axis, *refs):
    *parts, both = refs
    start = 0
    for part in parts:
        stop = start + part.shape[axis]
        both[(slice(None),) * axis + (slice(start, stop),)] = part[...]
        start = stop


def put_sums(parts, row_part, col_part):
    pad = jnp.zeros((parts[0].shape[0], 128 - len(parts)), jnp.float32)
    by_row = jnp.transpose(jnp.concatenate([jnp.sum(p, 1, keepdims=True) for p in parts] + [pad], 1))
    for k, part in enumerate(parts):
        by_col = jnp.sum(part, 0, keepdims=True)
        for source, sums in ((by_row[k : k + 1], row_part), (by_col, col_part)):
            rows = sums.shape[2]
            for p in range(sums.shape[1]):
                sums[k, p : p + 1, :] = source[:, p * rows : (p + 1) * rows]


def gram_kernel(choices, *refs):
    *arrays, gram_s, gram_t, row_part, col_part = refs

    def multiply(groups):
        row_t, row_s, col_t, col_s = [load(arrays, group) for group in groups]
        dims = (((1,), (1,)), ((), ()))
        gram_s[...] = lax.dot_general(row_s, col_s, dims, preferred_element_type=jnp.float32)
        gram_t[...] = lax.dot_general(row_t, col_t, dims, preferred_element_type=jnp.float32)

    by_core(multiply, choices)
    student, teacher = gram_s[...], gram_t[...]
    put_sums([student * student, teacher * teacher, student * teacher], row_part, col_part)


def call(kernel, operands, outputs, flops=0, **options):
    size = sum(math.prod(a.shape) * a.dtype.itemsize for a in [*operands, *jax.tree.leaves(outputs)])
    return pl.pallas_call(
        kernel,
        out_shape=outputs,
        **options,
        compiler_params=pltpu.CompilerParams(vmem_limit_bytes=VMEM),
        cost_estimate=pl.CostEstimate(flops=flops, bytes_accessed=size, transcendentals=0),
    )(*operands)


def output_kernel(n_arrays, choices, total, gram_s, gram_t, row_sum, col_sum, *refs):
    *refs, students = refs
    own, share, *pieces = refs[n_arrays:]

    def fetch(group):
        students[...] = load(refs[:n_arrays], group)

    by_core(fetch, choices)
    col_s = students[...]
    row_alpha, row_beta, _ = coefficients(row_sum[0], row_sum[1], row_sum[2], total)
    col_alpha, col_beta, terms = coefficients(col_sum[0], col_sum[1], col_sum[2], total)
    row_ab = jnp.transpose(jnp.concatenate([row_alpha, row_beta] * 4))
    row_w = row_ab[:, 0:1] * gram_s[...] - row_ab[:, 1:2] * gram_t[...]
    col_w = col_alpha * gram_s[...] - col_beta * gram_t[...]
    out = jnp.dot(row_w.astype(jnp.bfloat16), col_s, preferred_element_type=jnp.float32)
    out += jnp.dot(col_w.astype(jnp.bfloat16), col_s, preferred_element_type=jnp.float32)

    rows, width = own.shape
    own[...] = out[:rows]
    term = jnp.sum(terms, axis=1, keepdims=True)
    share[...] = jnp.broadcast_to(term, share.shape)
    largest = jnp.max(jnp.max(jnp.abs(out), axis=0, keepdims=True), axis=1, keepdims=True)
    power = jnp.clip(jnp.floor(jnp.log2(largest)), -100.0, 100.0)
    term = term * SHARE_SCALE
    high = term.astype(jnp.bfloat16).astype(jnp.float32)
    middle = (term - high).astype(jnp.bfloat16).astype(jnp.float32)
    low = term - high - middle
    lane = lax.broadcasted_iota(jnp.int32, (rows, 128), 1)
    extra = jnp.where(lane == 0, power, jnp.where(lane == 1, high, jnp.where(lane == 2, middle, low)))
    scaled = out * jnp.exp2(13.0 - power)
    for k, piece in enumerate(pieces):
        piece[:, :width] = scaled[(k + 1) * rows : (k + 2) * rows]
        piece[:, width:] = extra


def final_kernel(total, own, share, *refs):
    *pieces, grad, loss = refs
    width = own.shape[1]
    grads, terms = [own[...]], [share[0:1, 0:1]]
    for piece in pieces:
        extra = piece[:, width:]
        grads.append(piece[:, :width] * jnp.exp2(extra[:, 0:1] - 13.0))
        terms.append((extra[0:1, 1:2] + extra[0:1, 2:3] + extra[0:1, 3:4]) * (1.0 / SHARE_SCALE))
    grad[...] = tree_sum(grads)
    loss[...] = tree_sum(terms) * (1.0 / total)


def exchange_sums(row_part, col_part, partners):
    n_row, n_col, rows = row_part.shape[1], col_part.shape[1], row_part.shape[2]
    got = partners.swap(jnp.concatenate([row_part, col_part], 1))
    all_rows = jnp.concatenate([row_part, got[:, :n_row]], 1)
    all_cols = col_part + got[:, n_row:]
    all_cols = jnp.pad(all_cols, ((0, 0), (0, 2 * n_row - n_col), (0, 0)))
    first = lax.axis_index("blk") % 2 == 0
    sums = jnp.where(first, all_rows, all_cols)
    for b in range(len(partners.rows)):
        got = partners.step(sums, b).reshape(3, -1, 2, 1 << b, rows)
        sums += jnp.flip(got, 2).reshape(sums.shape)
    got = partners.swap(sums)
    return (
        jnp.where(first, sums[:, :n_row], got[:, n_row:]),
        jnp.where(first, got[:, :n_col], sums[:, :n_col]),
    )


def per_device(teacher, student):
    rows = teacher.shape[0]
    partners = Partners(lax.axis_size("blk"), lax.axis_size("inner"))
    total = rows * partners.count
    n_row, n_col = 1 << len(partners.rows), 1 << len(partners.columns)
    shape, width = (n_row * rows, 2 * n_col * rows), student.shape[1]

    def f32(*dims):
        return jax.ShapeDtypeStruct(dims, jnp.float32)

    mine, other = gather(teacher, student, partners)
    tiles = []
    for core in (0, 1):
        tiles += [tile_rows(*pair, n_row, core) for pair in zip(mine, other)]
        tiles += [tile_columns(*pair, n_col, core) for pair in zip(mine, other)]
    arrays, groups = operands_of(*tiles)
    gram_s, gram_t, row_part, col_part = call(
        functools.partial(gram_kernel, [groups[:4], groups[4:]]),
        arrays,
        [f32(*shape), f32(*shape), f32(3, n_row, rows), f32(3, 2 * n_col, rows)],
        2 * math.prod(shape) * (teacher.shape[1] + width),
    )
    row_sum, col_sum = exchange_sums(row_part, col_part, partners)
    row_sum, col_sum = row_sum.reshape(3, 1, -1), col_sum.reshape(3, 1, -1)

    arrays, groups = operands_of(tiles[3], tiles[7])
    own, share, *pieces = call(
        functools.partial(output_kernel, len(arrays), groups, total),
        [gram_s, gram_t, row_sum, col_sum, *arrays],
        [f32(rows, width), f32(8, 128)] + [f32(rows, width + 128)] * (n_row - 1),
        4 * math.prod(shape) * width,
        scratch_shapes=[pltpu.VMEM((shape[1], width), student.dtype)],
    )
    got = [
        partners.row(value.astype(jnp.float16), mask).astype(jnp.float32)
        for value, mask in zip(pieces, span(partners.rows)[1:])
    ]
    grad, loss = call(
        functools.partial(final_kernel, total), [own, share, *got], [f32(rows, width), f32(1, 1)]
    )
    return (loss[0, 0], grad)


def solution(mesh):
    return jax.shard_map(
        per_device,
        mesh=mesh,
        in_specs=(P(AXES, None), P(AXES, None)),
        out_specs=(P(), P(AXES, None)),
        check_vma=False,
    )
```

time: 55.7 us -> 57.6 us (1.034)
  waiting for transfers between devices: 29.1 us -> 31.9 us
  starting transfers between devices: 20.7 us -> 18.7 us
  local copies, waits for them, and re-layouts: 2.05 us -> 2.98 us
    ppermute x17 -> x18, waiting for transfers between devices: 29.1 us -> 31.9 us  [the longest x8 20.9 us: step(): return lax.ppermute(value, AXES, pairs)]
    ppermute x17 -> x18, starting transfers between devices: 20.7 us -> 18.7 us  [the longest x8 13.4 us: step(): return lax.ppermute(value, AXES, pairs)]
    unnamed x4 -> x8, local copies, waits for them, and re-layouts: 1.81 us -> 2.77 us
    pallas_call x4 -> x7, Pallas kernels: 2.75 us -> 3.02 us  [call(): pl.pallas_call(kernel, out_shape=outputs, **options, compiler_params=pltp...]
  transfers between devices with their start and end apart: 17 -> 18, of which waited for: 11 -> 12; matrix products, arithmetic and copies ran while one was open for 0% -> 0% of each run, Pallas kernels for 0% -> 0%
where the time goes in v13:
time: 57.6 us; the launch traced here: 57.4 us
  waiting for transfers between devices  31.9 us (55%)
  starting transfers between devices  18.7 us (32%)
  Pallas kernels  3.02 us (5%)
  local copies, waits for them, and re-layouts  2.98 us (5%)
  between operations  0.76 us (1%)
    ppermute x8, waiting for transfers between devices, step(): return lax.ppermute(value, AXES, pairs)  20.9 us
    ppermute x8, starting transfers between devices, step(): return lax.ppermute(value, AXES, pairs)  13.4 us
    ppermute x10, waiting for transfers between devices, row(): return lax.ppermute(value, AXES, [(i, i ^ mask) for i in range(self.count)])  10.9 us
    ppermute x10, starting transfers between devices, row(): return lax.ppermute(value, AXES, [(i, i ^ mask) for i in range(self.count)])  5.23 us
    pallas_call x7, Pallas kernels, call(): pl.pallas_call(kernel, out_shape=outputs, **options, compiler_params=pltp...  3.02 us
    unnamed x8, local copies, waits for them, and re-layouts  2.77 us
  transfers between devices with their start and end apart: 18, of which 12 were waited for; matrix products, arithmetic and copies ran while one was open for 0% of the time, Pallas kernels for 0%

profile of v13, /device:TPU:0, one launch (start us, length us, event | category | flops | bytes accessed | tf_op | source)
XLA Modules:
  0.0 57.4 jit_solution(7916879349866422382)
XLA Ops:
  0.6 0.5 collective-permute-start
  1.1 1.3 %collective-permute-done.refs_1_ = bf16[64,1536]{1,0:T(8,128)(2,1)S(1)} collective-permute-done((bf16[64,1536]{1,0:T(8,128)(2,1)}, bf16[64,1536]{1,0:T(8,128)(2,1)S(1)}, u32[]{:S(2)}, u32[]{:S(2)}) %collective-permute-start) | collective-permute-done | bytes 196640 | tf_op jit(solution)/shard_map/ppermute | solution.py:61
  2.4 0.9 %copy-done.2 = bf16[64,1536]{1,0:T(8,128)(2,1)S(1)} copy-done((bf16[64,1536]{1,0:T(8,128)(2,1)S(1)}, bf16[64,1536]{1,0:T(8,128)(2,1)}, u32[]{:S(2)}) %copy-start.2) | copy-done | bytes 196632
  3.4 3.0 %collective-permute-start.1 = (bf16[128,1536]{1,0:T(8,128)(2,1)S(1)}, bf16[128,1536]{1,0:T(8,128)(2,1)S(1)}, u32[]{:S(2)}, u32[]{:S(2)}) collective-permute-start(bf16[128,1536]{1,0:T(8,128)(2,1)S(1)} %shard_map.41.refs_0_), channel_id=1, source_target_pairs={{0,1},{1,0},{2,3},{3,2},{4,6},{5,7},{6,4},{7,5},{8,9},{9,8},{10,11... | collective-permute-start | bytes 1179656 | tf_op jit(solution)/shard_map/ppermute | solution.py:69
  6.4 1.5 %collective-permute-start.2 = (bf16[128,1536]{1,0:T(8,128)(2,1)S(1)}, bf16[128,1536]{1,0:T(8,128)(2,1)S(1)}, u32[]{:S(2)}, u32[]{:S(2)}) collective-permute-start(bf16[128,1536]{1,0:T(8,128)(2,1)S(1)} %shard_map.41.refs_0_), channel_id=1, source_target_pairs={{0,8},{1,9},{2,10},{3,11},{4,20},{5,21},{6,22},{7,23},{8,0},{9,1},... | collective-permute-start | bytes 1179656 | tf_op jit(solution)/shard_map/ppermute | solution.py:69
  7.9 0.6 %collective-permute-start.4 = (bf16[64,768]{1,0:T(8,128)(2,1)S(1)}, bf16[64,768]{1,0:T(8,128)(2,1)S(1)}, u32[]{:S(2)}, u32[]{:S(2)}) collective-permute-start(bf16[64,768]{1,0:T(8,128)(2,1)S(1)} %copy-done.3), channel_id=1, source_target_pairs={{0,4},{1,5},{2,6},{3,7},{4,0},{5,1},{6,2},{7,3},{8,12},{9,13},{10,... | collective-permute-start | bytes 294920 | tf_op jit(solution)/shard_map/ppermute | solution.py:61
  8.5 0.9 %collective-permute-done.4.refs_1_ = bf16[64,768]{1,0:T(8,128)(2,1)S(1)} collective-permute-done((bf16[64,768]{1,0:T(8,128)(2,1)S(1)}, bf16[64,768]{1,0:T(8,128)(2,1)S(1)}, u32[]{:S(2)}, u32[]{:S(2)}) %collective-permute-start.4) | collective-permute-done | bytes 98336 | tf_op jit(solution)/shard_map/ppermute | solution.py:61
  9.5 1.6 %collective-permute-start.6 = (bf16[128,768]{1,0:T(8,128)(2,1)S(1)}, bf16[128,768]{1,0:T(8,128)(2,1)S(1)}, u32[]{:S(2)}, u32[]{:S(2)}) collective-permute-start(bf16[128,768]{1,0:T(8,128)(2,1)S(1)} %shard_map.42.refs_4_.refs_0_), channel_id=1, source_target_pairs={{0,8},{1,9},{2,10},{3,11},{4,20},{5,21},{6,22},{7,23},{8,0},{9,1},... | collective-permute-start | bytes 589832 | tf_op jit(solution)/shard_map/ppermute | solution.py:69
  11.0 4.9 %collective-permute-done.1.refs_0_.refs_1_ = bf16[128,1536]{1,0:T(8,128)(2,1)S(1)} collective-permute-done((bf16[128,1536]{1,0:T(8,128)(2,1)S(1)}, bf16[128,1536]{1,0:T(8,128)(2,1)S(1)}, u32[]{:S(2)}, u32[]{:S(2)}) %collective-permute-start.1) | collective-permute-done | bytes 393248 | tf_op jit(solution)/shard_map/ppermute | solution.py:69
  15.9 2.3 %collective-permute-start.3 = (bf16[128,1536]{1,0:T(8,128)(2,1)S(1)}, bf16[128,1536]{1,0:T(8,128)(2,1)S(1)}, u32[]{:S(2)}, u32[]{:S(2)}) collective-permute-start(bf16[128,1536]{1,0:T(8,128)(2,1)S(1)} %collective-permute-done.1.refs_0_.refs_1_), channel_id=1, source_target_pairs={{0,8},{1,9},{2,10},{3,11},{4,20},{5,21},{6,22},{7,23},{8,0},{9,1},... | collective-permute-start | bytes 1179656 | tf_op jit(solution)/shard_map/ppermute | solution.py:69
  18.4 1.5 %collective-permute-start.5 = (bf16[128,768]{1,0:T(8,128)(2,1)S(1)}, bf16[128,768]{1,0:T(8,128)(2,1)S(1)}, u32[]{:S(2)}, u32[]{:S(2)}) collective-permute-start(bf16[128,768]{1,0:T(8,128)(2,1)S(1)} %shard_map.42.refs_4_.refs_0_), channel_id=1, source_target_pairs={{0,1},{1,0},{2,3},{3,2},{4,6},{5,7},{6,4},{7,5},{8,9},{9,8},{10,11... | collective-permute-start | bytes 589832 | tf_op jit(solution)/shard_map/ppermute | solution.py:69
  19.9 6.3 %collective-permute-done.5.refs_0_.refs_5_.refs_4_ = bf16[128,768]{1,0:T(8,128)(2,1)S(1)} collective-permute-done((bf16[128,768]{1,0:T(8,128)(2,1)S(1)}, bf16[128,768]{1,0:T(8,128)(2,1)S(1)}, u32[]{:S(2)}, u32[]{:S(2)}) %collective-permute-start.5) | collective-permute-done | bytes 196640 | tf_op jit(solution)/shard_map/ppermute | solution.py:69
  26.4 1.1 %collective-permute-start.7 = (bf16[128,768]{1,0:T(8,128)(2,1)S(1)}, bf16[128,768]{1,0:T(8,128)(2,1)S(1)}, u32[]{:S(2)}, u32[]{:S(2)}) collective-permute-start(bf16[128,768]{1,0:T(8,128)(2,1)S(1)} %collective-permute-done.5.refs_0_.refs_5_.refs_4_), channel_id=1, source_target_pairs={{0,8},{1,9},{2,10},{3,11},{4,20},{5,21},{6,22},{7,23},{8,0},{9,1},... | collective-permute-start | bytes 589832 | tf_op jit(solution)/shard_map/ppermute | solution.py:69
  27.5 4.6 %collective-permute-done.7.refs_7_.refs_6_ = bf16[128,768]{1,0:T(8,128)(2,1)S(1)} collective-permute-done((bf16[128,768]{1,0:T(8,128)(2,1)S(1)}, bf16[128,768]{1,0:T(8,128)(2,1)S(1)}, u32[]{:S(2)}, u32[]{:S(2)}) %collective-permute-start.7) | collective-permute-done | bytes 196640 | tf_op jit(solution)/shard_map/ppermute | solution.py:69
  32.1 1.4 %collective-permute-done.10.refs_10_.refs_3_ = bf16[128,768]{1,0:T(8,128)(2,1)S(1)} collective-permute-done((bf16[128,768]{1,0:T(8,128)(2,1)S(1)}, bf16[128,768]{1,0:T(8,128)(2,1)S(1)}, u32[]{:S(2)}, u32[]{:S(2)}) %collective-permute-start.10) | collective-permute-done | bytes 196640 | tf_op jit(solution)/shard_map/ppermute | solution.py:61
  33.5 1.1 %shard_map.45 = (f32[256,512]{1,0:T(8,128)S(1)}, f32[256,512]{1,0:T(8,128)S(1)}, f32[3,4,64]{2,1,0:T(4,128)S(1)}, f32[3,8,64]{2,1,0:T(8,128)S(1)}) custom-call(bf16[128,1536]{1,0:T(8,128)(2,1)S(1)} %shard_map.41.refs_0_, bf16[128,1536]{1,0:T(8,128)(2,1)S(1)} %collective-permute-done.1.refs_0_.refs_1_, ...), custom_call_target="tpu_custom_call" | custom-call | flops 603979776 | bytes 5186560 | tf_op jit(solution)/shard_map/pallas_call | solution.py:183
  34.7 0.8 %copy-done = f32[256,512]{1,0:T(8,128)} copy-done((f32[256,512]{1,0:T(8,128)}, f32[256,512]{1,0:T(8,128)S(1)}, u32[]{:S(2)}) %copy-start) | copy-done | bytes 524312
  35.5 0.2 collective-permute-start.11
  35.7 1.1 %collective-permute-done.11 = f32[3,12,64]{2,1,0:T(8,128)S(1)} collective-permute-done((f32[3,12,64]{2,1,0:T(8,128)S(1)}, f32[3,12,64]{2,1,0:T(8,128)S(1)}, u32[]{:S(2)}, u32[]{:S(2)}) %collective-permute-start.11) | collective-permute-done | bytes 9248 | tf_op jit(solution)/shard_map/ppermute | solution.py:61
  36.8 1.3 %collective-permute-start.12 = (f32[3,8,64]{2,1,0:T(8,128)S(1)}, f32[3,8,64]{2,1,0:T(8,128)S(1)}, u32[]{:S(2)}, u32[]{:S(2)}) collective-permute-start(f32[3,8,64]{2,1,0:T(8,128)S(1)} %fusion), channel_id=1, source_target_pairs={{0,1},{1,0},{2,3},{3,2},{4,6},{5,7},{6,4},{7,5},{8,9},{9,8},{10,11... | collective-permute-start | bytes 18440 | tf_op jit(solution)/shard_map/ppermute | solution.py:69
  38.1 2.5 %collective-permute-done.12 = f32[3,8,64]{2,1,0:T(8,128)S(1)} collective-permute-done((f32[3,8,64]{2,1,0:T(8,128)S(1)}, f32[3,8,64]{2,1,0:T(8,128)S(1)}, u32[]{:S(2)}, u32[]{:S(2)}) %collective-permute-start.12) | collective-permute-done | bytes 6176 | tf_op jit(solution)/shard_map/ppermute | solution.py:69
  40.6 1.1 %collective-permute-start.13 = (f32[3,8,64]{2,1,0:T(8,128)S(1)}, f32[3,8,64]{2,1,0:T(8,128)S(1)}, u32[]{:S(2)}, u32[]{:S(2)}) collective-permute-start(f32[3,8,64]{2,1,0:T(8,128)S(1)} %add.15), channel_id=1, source_target_pairs={{0,8},{1,9},{2,10},{3,11},{4,20},{5,21},{6,22},{7,23},{8,0},{9,1},... | collective-permute-start | bytes 18440 | tf_op jit(solution)/shard_map/ppermute | solution.py:69
  41.7 2.6 %collective-permute-done.13 = f32[3,8,64]{2,1,0:T(8,128)S(1)} collective-permute-done((f32[3,8,64]{2,1,0:T(8,128)S(1)}, f32[3,8,64]{2,1,0:T(8,128)S(1)}, u32[]{:S(2)}, u32[]{:S(2)}) %collective-permute-start.13) | collective-permute-done | bytes 6176 | tf_op jit(solution)/shard_map/ppermute | solution.py:69
  44.4 1.2 %collective-permute-done.14 = f32[3,8,64]{2,1,0:T(8,128)S(1)} collective-permute-done((f32[3,8,64]{2,1,0:T(8,128)S(1)}, f32[3,8,64]{2,1,0:T(8,128)S(1)}, u32[]{:S(2)}, u32[]{:S(2)}) %collective-permute-start.14) | collective-permute-done | bytes 6176 | tf_op jit(solution)/shard_map/ppermute | solution.py:61
  45.8 1.0 %copy-done.1 = f32[256,512]{1,0:T(8,128)S(1)} copy-done((f32[256,512]{1,0:T(8,128)S(1)}, f32[256,512]{1,0:T(8,128)}, u32[]{:S(2)}) %copy-start.1) | copy-done | bytes 524312
  46.8 0.9 %shard_map.46 = (f32[64,768]{1,0:T(8,128)S(1)}, f32[8,128]{1,0:T(8,128)S(1)}, f32[64,896]{1,0:T(8,128)S(1)}, f32[64,896]{1,0:T(8,128)S(1)}, f32[64,896]{1,0:T(8,128)S(1)}) custom-call(f32[256,512]{1,0:T(8,128)S(1)} %get-tuple-element.13.gram_s, f32[256,512]{1,0:T(8,128)S(1)} %copy-done.1, f32[3,1,256]{2,1,0:T(1,128)S(1)} %reshape.26.row_sum, ...), custom_call_target="tpu_custom_call" | custom-call | flops 402653184 | bytes 4502528 | tf_op jit(solution)/shard_map/pallas_call | solution.py:183
  47.8 1.3 %collective-permute-start.15 = (f16[64,896]{1,0:T(8,128)(2,1)S(1)}, f16[64,896]{1,0:T(8,128)(2,1)S(1)}, u32[]{:S(2)}, u32[]{:S(2)}) collective-permute-start(f16[64,896]{1,0:T(8,128)(2,1)S(1)} %convert_element_type.18), channel_id=1, source_target_pairs={{0,1},{1,0},{2,3},{3,2},{4,5},{5,4},{6,7},{7,6},{8,9},{9,8},{10,11... | collective-permute-start | bytes 344072 | tf_op jit(solution)/shard_map/ppermute | solution.py:61
  49.1 0.6 %collective-permute-start.16 = (f16[64,896]{1,0:T(8,128)(2,1)S(1)}, f16[64,896]{1,0:T(8,128)(2,1)S(1)}, u32[]{:S(2)}, u32[]{:S(2)}) collective-permute-start(f16[64,896]{1,0:T(8,128)(2,1)S(1)} %convert_element_type.20), channel_id=1, source_target_pairs={{0,8},{1,9},{2,10},{3,11},{4,12},{5,13},{6,14},{7,15},{8,0},{9,1},... | collective-permute-start | bytes 344072 | tf_op jit(solution)/shard_map/ppermute | solution.py:61
  49.8 1.7 %collective-permute-start.17 = (f16[64,896]{1,0:T(8,128)(2,1)S(1)}, f16[64,896]{1,0:T(8,128)(2,1)S(1)}, u32[]{:S(2)}, u32[]{:S(2)}) collective-permute-start(f16[64,896]{1,0:T(8,128)(2,1)S(1)} %convert_element_type.22), channel_id=1, source_target_pairs={{0,9},{1,8},{2,11},{3,10},{4,13},{5,12},{6,15},{7,14},{8,1},{9,0},... | collective-permute-start | bytes 344072 | tf_op jit(solution)/shard_map/ppermute | solution.py:61
  51.5 1.6 %collective-permute-done.15 = f16[64,896]{1,0:T(8,128)(2,1)S(1)} collective-permute-done((f16[64,896]{1,0:T(8,128)(2,1)S(1)}, f16[64,896]{1,0:T(8,128)(2,1)S(1)}, u32[]{:S(2)}, u32[]{:S(2)}) %collective-permute-start.15) | collective-permute-done | bytes 114720 | tf_op jit(solution)/shard_map/ppermute | solution.py:61
  53.2 3.4 %collective-permute-done.16 = f16[64,896]{1,0:T(8,128)(2,1)S(1)} collective-permute-done((f16[64,896]{1,0:T(8,128)(2,1)S(1)}, f16[64,896]{1,0:T(8,128)(2,1)S(1)}, u32[]{:S(2)}, u32[]{:S(2)}) %collective-permute-start.16) | collective-permute-done | bytes 114720 | tf_op jit(solution)/shard_map/ppermute | solution.py:61
  56.6 0.8 %shard_map.47 = (f32[64,768]{1,0:T(8,128)}, f32[1,1]{1,0:T(1,128)}) custom-call(f32[64,768]{1,0:T(8,128)S(1)} %get-tuple-element.17.own, f32[8,128]{1,0:T(8,128)S(1)} %get-tuple-element.18.share, f32[64,896]{1,0:T(8,128)S(1)} %convert_element_type.19.refs_0_, f32[64,896]{1,0:T(8,128)S(1)} %convert_element_type.21.refs_1_, ...), custom_call_target="tpu_custom_call" | custom-call | bytes 1085444 | tf_op jit(solution)/shard_map/pallas_call | solution.py:183
  (36 shorter events, 0.7 us)
Async XLA Ops:
  0.6 1.8 %collective-permute-start = (bf16[64,1536]{1,0:T(8,128)(2,1)}, bf16[64,1536]{1,0:T(8,128)(2,1)S(1)}, u32[]{:S(2)}, u32[]{:S(2)}) collective-permute-start(bf16[64,1536]{1,0:T(8,128)(2,1)} %refs_0_.2), channel_id=1, source_target_pairs={{0,4},{1,5},{2,6},{3,7},{4,0},{5,1},{6,2},{7,3},{8,12},{9,13},{10,... | collective-permute-start | bytes 589832 | tf_op jit(solution)/shard_map/ppermute | solution.py:61
  2.4 0.9 %copy-start.2 = (bf16[64,1536]{1,0:T(8,128)(2,1)S(1)}, bf16[64,1536]{1,0:T(8,128)(2,1)}, u32[]{:S(2)}) copy-start(bf16[64,1536]{1,0:T(8,128)(2,1)} %refs_0_.2) | copy-start | bytes 589828
  3.4 4.5 %copy-start.3 = (bf16[64,768]{1,0:T(8,128)(2,1)S(1)}, bf16[64,768]{1,0:T(8,128)(2,1)}, u32[]{:S(2)}) copy-start(bf16[64,768]{1,0:T(8,128)(2,1)} %refs_0_.3) | copy-start | bytes 294916
  3.4 12.6 %collective-permute-start.1 = (bf16[128,1536]{1,0:T(8,128)(2,1)S(1)}, bf16[128,1536]{1,0:T(8,128)(2,1)S(1)}, u32[]{:S(2)}, u32[]{:S(2)}) collective-permute-start(bf16[128,1536]{1,0:T(8,128)(2,1)S(1)} %shard_map.41.refs_0_), channel_id=1, source_target_pairs={{0,1},{1,0},{2,3},{3,2},{4,6},{5,7},{6,4},{7,5},{8,9},{9,8},{10,11... | collective-permute-start | bytes 1179656 | tf_op jit(solution)/shard_map/ppermute | solution.py:69
  6.4 11.8 %collective-permute-start.2 = (bf16[128,1536]{1,0:T(8,128)(2,1)S(1)}, bf16[128,1536]{1,0:T(8,128)(2,1)S(1)}, u32[]{:S(2)}, u32[]{:S(2)}) collective-permute-start(bf16[128,1536]{1,0:T(8,128)(2,1)S(1)} %shard_map.41.refs_0_), channel_id=1, source_target_pairs={{0,8},{1,9},{2,10},{3,11},{4,20},{5,21},{6,22},{7,23},{8,0},{9,1},... | collective-permute-start | bytes 1179656 | tf_op jit(solution)/shard_map/ppermute | solution.py:69
  7.9 1.6 %collective-permute-start.4 = (bf16[64,768]{1,0:T(8,128)(2,1)S(1)}, bf16[64,768]{1,0:T(8,128)(2,1)S(1)}, u32[]{:S(2)}, u32[]{:S(2)}) collective-permute-start(bf16[64,768]{1,0:T(8,128)(2,1)S(1)} %copy-done.3), channel_id=1, source_target_pairs={{0,4},{1,5},{2,6},{3,7},{4,0},{5,1},{6,2},{7,3},{8,12},{9,13},{10,... | collective-permute-start | bytes 294920 | tf_op jit(solution)/shard_map/ppermute | solution.py:61
  9.5 8.8 %collective-permute-start.6 = (bf16[128,768]{1,0:T(8,128)(2,1)S(1)}, bf16[128,768]{1,0:T(8,128)(2,1)S(1)}, u32[]{:S(2)}, u32[]{:S(2)}) collective-permute-start(bf16[128,768]{1,0:T(8,128)(2,1)S(1)} %shard_map.42.refs_4_.refs_0_), channel_id=1, source_target_pairs={{0,8},{1,9},{2,10},{3,11},{4,20},{5,21},{6,22},{7,23},{8,0},{9,1},... | collective-permute-start | bytes 589832 | tf_op jit(solution)/shard_map/ppermute | solution.py:69
  15.9 10.3 %collective-permute-start.3 = (bf16[128,1536]{1,0:T(8,128)(2,1)S(1)}, bf16[128,1536]{1,0:T(8,128)(2,1)S(1)}, u32[]{:S(2)}, u32[]{:S(2)}) collective-permute-start(bf16[128,1536]{1,0:T(8,128)(2,1)S(1)} %collective-permute-done.1.refs_0_.refs_1_), channel_id=1, source_target_pairs={{0,8},{1,9},{2,10},{3,11},{4,20},{5,21},{6,22},{7,23},{8,0},{9,1},... | collective-permute-start | bytes 1179656 | tf_op jit(solution)/shard_map/ppermute | solution.py:69
  18.3 15.2 %collective-permute-start.8 = (bf16[128,3840]{1,0:T(8,128)(2,1)S(1)}, bf16[128,3840]{1,0:T(8,128)(2,1)S(1)}, u32[]{:S(2)}, u32[]{:S(2)}) collective-permute-start(bf16[128,3840]{1,0:T(8,128)(2,1)S(1)} %shard_map.43), channel_id=1, source_target_pairs={{0,4},{1,5},{2,6},{3,7},{4,0},{5,1},{6,2},{7,3},{8,12},{9,13},{10,... | collective-permute-start | bytes 2949128 | tf_op jit(solution)/shard_map/ppermute | solution.py:61
  18.4 7.8 %collective-permute-start.5 = (bf16[128,768]{1,0:T(8,128)(2,1)S(1)}, bf16[128,768]{1,0:T(8,128)(2,1)S(1)}, u32[]{:S(2)}, u32[]{:S(2)}) collective-permute-start(bf16[128,768]{1,0:T(8,128)(2,1)S(1)} %shard_map.42.refs_4_.refs_0_), channel_id=1, source_target_pairs={{0,1},{1,0},{2,3},{3,2},{4,6},{5,7},{6,4},{7,5},{8,9},{9,8},{10,11... | collective-permute-start | bytes 589832 | tf_op jit(solution)/shard_map/ppermute | solution.py:69
  26.3 7.3 %collective-permute-start.9 = (bf16[128,2304]{1,0:T(8,128)(2,1)S(1)}, bf16[128,2304]{1,0:T(8,128)(2,1)S(1)}, u32[]{:S(2)}, u32[]{:S(2)}) collective-permute-start(bf16[128,2304]{1,0:T(8,128)(2,1)S(1)} %shard_map.44), channel_id=1, source_target_pairs={{0,4},{1,5},{2,6},{3,7},{4,0},{5,1},{6,2},{7,3},{8,12},{9,13},{10,... | collective-permute-start | bytes 1769480 | tf_op jit(solution)/shard_map/ppermute | solution.py:61
  26.4 5.7 %collective-permute-start.7 = (bf16[128,768]{1,0:T(8,128)(2,1)S(1)}, bf16[128,768]{1,0:T(8,128)(2,1)S(1)}, u32[]{:S(2)}, u32[]{:S(2)}) collective-permute-start(bf16[128,768]{1,0:T(8,128)(2,1)S(1)} %collective-permute-done.5.refs_0_.refs_5_.refs_4_), channel_id=1, source_target_pairs={{0,8},{1,9},{2,10},{3,11},{4,20},{5,21},{6,22},{7,23},{8,0},{9,1},... | collective-permute-start | bytes 589832 | tf_op jit(solution)/shard_map/ppermute | solution.py:69
  32.1 1.4 %collective-permute-start.10 = (bf16[128,768]{1,0:T(8,128)(2,1)S(1)}, bf16[128,768]{1,0:T(8,128)(2,1)S(1)}, u32[]{:S(2)}, u32[]{:S(2)}) collective-permute-start(bf16[128,768]{1,0:T(8,128)(2,1)S(1)} %collective-permute-done.7.refs_7_.refs_6_), channel_id=1, source_target_pairs={{0,4},{1,5},{2,6},{3,7},{4,0},{5,1},{6,2},{7,3},{8,12},{9,13},{10,... | collective-permute-start | bytes 589832 | tf_op jit(solution)/shard_map/ppermute | solution.py:61
  34.7 0.8 %copy-start = (f32[256,512]{1,0:T(8,128)}, f32[256,512]{1,0:T(8,128)S(1)}, u32[]{:S(2)}) copy-start(f32[256,512]{1,0:T(8,128)S(1)} %get-tuple-element.14.gram_t) | copy-start | bytes 1572868
  35.5 1.3 %collective-permute-start.11 = (f32[3,12,64]{2,1,0:T(8,128)S(1)}, f32[3,12,64]{2,1,0:T(8,128)S(1)}, u32[]{:S(2)}, u32[]{:S(2)}) collective-permute-start(f32[3,12,64]{2,1,0:T(8,128)S(1)} %pad_maximum_fusion), channel_id=1, source_target_pairs={{0,4},{1,5},{2,6},{3,7},{4,0},{5,1},{6,2},{7,3},{8,12},{9,13},{10,... | collective-permute-start | bytes 27656 | tf_op jit(solution)/shard_map/ppermute | solution.py:61
  36.8 3.8 %collective-permute-start.12 = (f32[3,8,64]{2,1,0:T(8,128)S(1)}, f32[3,8,64]{2,1,0:T(8,128)S(1)}, u32[]{:S(2)}, u32[]{:S(2)}) collective-permute-start(f32[3,8,64]{2,1,0:T(8,128)S(1)} %fusion), channel_id=1, source_target_pairs={{0,1},{1,0},{2,3},{3,2},{4,6},{5,7},{6,4},{7,5},{8,9},{9,8},{10,11... | collective-permute-start | bytes 18440 | tf_op jit(solution)/shard_map/ppermute | solution.py:69
  40.6 3.8 %collective-permute-start.13 = (f32[3,8,64]{2,1,0:T(8,128)S(1)}, f32[3,8,64]{2,1,0:T(8,128)S(1)}, u32[]{:S(2)}, u32[]{:S(2)}) collective-permute-start(f32[3,8,64]{2,1,0:T(8,128)S(1)} %add.15), channel_id=1, source_target_pairs={{0,8},{1,9},{2,10},{3,11},{4,20},{5,21},{6,22},{7,23},{8,0},{9,1},... | collective-permute-start | bytes 18440 | tf_op jit(solution)/shard_map/ppermute | solution.py:69
  44.4 1.2 %collective-permute-start.14 = (f32[3,8,64]{2,1,0:T(8,128)S(1)}, f32[3,8,64]{2,1,0:T(8,128)S(1)}, u32[]{:S(2)}, u32[]{:S(2)}) collective-permute-start(f32[3,8,64]{2,1,0:T(8,128)S(1)} %add.16), channel_id=1, source_target_pairs={{0,4},{1,5},{2,6},{3,7},{4,0},{5,1},{6,2},{7,3},{8,12},{9,13},{10,... | collective-permute-start | bytes 18440 | tf_op jit(solution)/shard_map/ppermute | solution.py:61
  45.8 1.0 %copy-start.1 = (f32[256,512]{1,0:T(8,128)S(1)}, f32[256,512]{1,0:T(8,128)}, u32[]{:S(2)}) copy-start(f32[256,512]{1,0:T(8,128)} %copy-done) | copy-start | bytes 1572868
  47.8 5.4 %collective-permute-start.15 = (f16[64,896]{1,0:T(8,128)(2,1)S(1)}, f16[64,896]{1,0:T(8,128)(2,1)S(1)}, u32[]{:S(2)}, u32[]{:S(2)}) collective-permute-start(f16[64,896]{1,0:T(8,128)(2,1)S(1)} %convert_element_type.18), channel_id=1, source_target_pairs={{0,1},{1,0},{2,3},{3,2},{4,5},{5,4},{6,7},{7,6},{8,9},{9,8},{10,11... | collective-permute-start | bytes 344072 | tf_op jit(solution)/shard_map/ppermute | solution.py:61
  49.1 7.5 %collective-permute-start.16 = (f16[64,896]{1,0:T(8,128)(2,1)S(1)}, f16[64,896]{1,0:T(8,128)(2,1)S(1)}, u32[]{:S(2)}, u32[]{:S(2)}) collective-permute-start(f16[64,896]{1,0:T(8,128)(2,1)S(1)} %convert_element_type.20), channel_id=1, source_target_pairs={{0,8},{1,9},{2,10},{3,11},{4,12},{5,13},{6,14},{7,15},{8,0},{9,1},... | collective-permute-start | bytes 344072 | tf_op jit(solution)/shard_map/ppermute | solution.py:61
  49.8 6.8 %collective-permute-start.17 = (f16[64,896]{1,0:T(8,128)(2,1)S(1)}, f16[64,896]{1,0:T(8,128)(2,1)S(1)}, u32[]{:S(2)}, u32[]{:S(2)}) collective-permute-start(f16[64,896]{1,0:T(8,128)(2,1)S(1)} %convert_element_type.22), channel_id=1, source_target_pairs={{0,9},{1,8},{2,11},{3,10},{4,13},{5,12},{6,15},{7,14},{8,1},{9,0},... | collective-permute-start | bytes 344072 | tf_op jit(solution)/shard_map/ppermute | solution.py:61

commit v14 on v12

--- a/solution.py
+++ b/solution.py
@@ -227,10 +227,32 @@
     loss[...] = tree_sum(terms) * (1.0 / total)
 
 
-def add_partner(parts, masks, place, count):
-    got = send(parts, masks[place], count)
-    shape = (3, -1, 2, 1 << place, got.shape[-1])
-    return parts + jnp.flip(got.reshape(shape), 2).reshape(parts.shape)
+def exchange_sums(row_part, col_part, row_masks, col_masks, count):
+    *plane_masks, core_mask = col_masks
+    n_row, n_col, rows = row_part.shape[1], col_part.shape[1], row_part.shape[2]
+
+    def other_core_first(cols):
+        return jnp.roll(cols, n_col // 2, 1)
+
+    got = send(jnp.concatenate([row_part, col_part], 1), core_mask, count)
+    all_rows = jnp.concatenate([row_part, got[:, :n_row]], 1)
+    all_cols = col_part + other_core_first(got[:, n_row:])
+    all_cols = jnp.pad(all_cols, ((0, 0), (0, 2 * n_row - n_col), (0, 0)))
+    first = (lax.axis_index("blk") & 1) == 0
+    sums = jnp.where(first, all_rows, all_cols)
+    for b in range(len(row_masks)):
+        pairs = []
+        for i in range(count):
+            masks = plane_masks if i & core_mask else row_masks
+            if b < len(masks):
+                pairs.append((i, i ^ masks[b]))
+        got = lax.ppermute(sums, AXES, pairs).reshape(3, -1, 2, 1 << b, rows)
+        sums += jnp.flip(got, 2).reshape(sums.shape)
+    got = send(sums, core_mask, count)
+    return (
+        jnp.where(first, sums[:, :n_row], got[:, n_row:]),
+        jnp.where(first, other_core_first(got[:, :n_col]), sums[:, :n_col]),
+    )
 
 
 def per_device(teacher, student):
@@ -255,13 +277,7 @@
         [f32(*shape), f32(*shape), f32(3, n_row, rows), f32(3, n_col, rows)],
         2 * math.prod(shape) * (teacher.shape[1] + width),
     )
-    for place in range(max(len(row_masks), len(col_masks))):
-        if place < len(col_masks):
-            col_part = add_partner(col_part, col_masks, place, count)
-        if place < len(row_masks):
-            row_part = add_partner(row_part, row_masks, place, count)
-        if place < min(len(row_masks), len(col_masks)):
-            row_part, col_part = lax.optimization_barrier((row_part, col_part))
+    row_part, col_part = exchange_sums(row_part, col_part, row_masks, col_masks, count)
     row_sum, col_sum = row_part.reshape(3, 1, -1), col_part.reshape(3, 1, -1)
 
     arrays, (group,) = operands_of(pieces[3])

time: 54.9 us -> 53.4 us (0.973)
  starting transfers between devices: 22.1 us -> 19.3 us
  waiting for transfers between devices: 26.8 us -> 28.1 us
    ppermute x0 -> x2, waiting for transfers between devices: none -> 6.84 us  [exchange_sums(): got = lax.ppermute(sums, AXES, pairs).reshape(3, -1, 2, 1 << b, rows)]
    ppermute x21 -> x18, waiting for transfers between devices: 26.8 us -> 21.2 us  [send(): return lax.ppermute(value, AXES, [(i, i ^ mask) for i in range(count)])]
    ppermute x21 -> x18, starting transfers between devices: 22.1 us -> 18.7 us  [send(): return lax.ppermute(value, AXES, [(i, i ^ mask) for i in range(count)])]
    ppermute x0 -> x2, starting transfers between devices: none -> 0.67 us  [exchange_sums(): got = lax.ppermute(sums, AXES, pairs).reshape(3, -1, 2, 1 << b, rows)]
  transfers between devices with their start and end apart: 21 -> 20, of which waited for: 11 -> 11; matrix products, arithmetic and copies ran while one was open for 0% -> 0% of each run, Pallas kernels for 2% -> 2%
where the time goes in v14:
time: 53.4 us; the launch traced here: 53.3 us
  waiting for transfers between devices  28.1 us (53%)
  starting transfers between devices  19.3 us (36%)
  Pallas kernels  3.76 us (7%)
  local copies, waits for them, and re-layouts  1.11 us (2%)
  between operations  0.79 us (1%)
    ppermute x18, waiting for transfers between devices, send(): return lax.ppermute(value, AXES, [(i, i ^ mask) for i in range(count)])  21.2 us
    ppermute x18, starting transfers between devices, send(): return lax.ppermute(value, AXES, [(i, i ^ mask) for i in range(count)])  18.7 us
    ppermute x2, waiting for transfers between devices, exchange_sums(): got = lax.ppermute(sums, AXES, pairs).reshape(3, -1, 2, 1 << b, rows)  6.84 us
    pallas_call x7, Pallas kernels, call(): pl.pallas_call(kernel, out_shape=outputs, **options, compiler_params=pltp...  3.76 us
  transfers between devices with their start and end apart: 20, of which 11 were waited for; matrix products, arithmetic and copies ran while one was open for 0% of the time, Pallas kernels for 2%

profile of v14, /device:TPU:0, one launch (start us, length us, event | category | flops | bytes accessed | tf_op | source)
XLA Modules:
  0.0 53.3 jit_solution(12852633368524513138)
XLA Ops:
  0.6 3.0 %collective-permute-start.3 = (bf16[64,768]{1,0:T(8,128)(2,1)}, bf16[64,768]{1,0:T(8,128)(2,1)S(1)}, u32[]{:S(2)}, u32[]{:S(2)}) collective-permute-start(bf16[64,768]{1,0:T(8,128)(2,1)} %refs_1_.1), channel_id=1, source_target_pairs={{0,16},{1,17},{2,18},{3,19},{4,20},{5,21},{6,22},{7,23},{8,24},{9,... | collective-permute-start | bytes 294920 | tf_op jit(solution)/shard_map/ppermute | solution.py:49
  3.7 1.5 %collective-permute-start.2 = (bf16[64,768]{1,0:T(8,128)(2,1)}, bf16[64,768]{1,0:T(8,128)(2,1)S(1)}, u32[]{:S(2)}, u32[]{:S(2)}) collective-permute-start(bf16[64,768]{1,0:T(8,128)(2,1)} %refs_1_.1), channel_id=1, source_target_pairs={{0,8},{1,9},{2,10},{3,11},{4,12},{5,13},{6,14},{7,15},{8,0},{9,1},... | collective-permute-start | bytes 294920 | tf_op jit(solution)/shard_map/ppermute | solution.py:49
  5.2 1.6 %collective-permute-start = (bf16[64,1536]{1,0:T(8,128)(2,1)}, bf16[64,1536]{1,0:T(8,128)(2,1)S(1)}, u32[]{:S(2)}, u32[]{:S(2)}) collective-permute-start(bf16[64,1536]{1,0:T(8,128)(2,1)} %refs_0_.1), channel_id=1, source_target_pairs={{0,1},{1,0},{2,3},{3,2},{4,5},{5,4},{6,7},{7,6},{8,9},{9,8},{10,11... | collective-permute-start | bytes 589832 | tf_op jit(solution)/shard_map/ppermute | solution.py:49
  6.7 2.6 %collective-permute-start.1 = (bf16[64,1536]{1,0:T(8,128)(2,1)}, bf16[64,1536]{1,0:T(8,128)(2,1)S(1)}, u32[]{:S(2)}, u32[]{:S(2)}) collective-permute-start(bf16[64,1536]{1,0:T(8,128)(2,1)} %refs_0_.1), channel_id=1, source_target_pairs={{0,2},{1,3},{2,0},{3,1},{4,6},{5,7},{6,4},{7,5},{8,10},{9,11},{10,... | collective-permute-start | bytes 589832 | tf_op jit(solution)/shard_map/ppermute | solution.py:49
  9.3 0.9 %copy-done = bf16[64,768]{1,0:T(8,128)(2,1)S(1)} copy-done((bf16[64,768]{1,0:T(8,128)(2,1)S(1)}, bf16[64,768]{1,0:T(8,128)(2,1)}, u32[]{:S(2)}) %copy-start) | copy-done | bytes 98328
  10.2 0.9 %shard_map.41.refs_0_ = bf16[64,2304]{1,0:T(8,128)(2,1)S(1)} custom-call(bf16[64,1536]{1,0:T(8,128)(2,1)} %refs_0_.1, bf16[64,768]{1,0:T(8,128)(2,1)S(1)} %copy-done), custom_call_target="tpu_custom_call" | custom-call | bytes 589824 | tf_op jit(solution)/shard_map/pallas_call | solution.py:180
  11.2 0.6 %collective-permute-start.5 = (bf16[64,1536]{1,0:T(8,128)(2,1)}, bf16[64,1536]{1,0:T(8,128)(2,1)S(1)}, u32[]{:S(2)}, u32[]{:S(2)}) collective-permute-start(bf16[64,1536]{1,0:T(8,128)(2,1)} %refs_0_.1), channel_id=1, source_target_pairs={{0,16},{1,17},{2,18},{3,19},{4,20},{5,21},{6,22},{7,23},{8,24},{9,... | collective-permute-start | bytes 589832 | tf_op jit(solution)/shard_map/ppermute | solution.py:49
  11.8 0.5 %collective-permute-start.4 = (bf16[64,1536]{1,0:T(8,128)(2,1)}, bf16[64,1536]{1,0:T(8,128)(2,1)S(1)}, u32[]{:S(2)}, u32[]{:S(2)}) collective-permute-start(bf16[64,1536]{1,0:T(8,128)(2,1)} %refs_0_.1), channel_id=1, source_target_pairs={{0,8},{1,9},{2,10},{3,11},{4,12},{5,13},{6,14},{7,15},{8,0},{9,1},... | collective-permute-start | bytes 589832 | tf_op jit(solution)/shard_map/ppermute | solution.py:49
  12.3 3.2 %collective-permute-done.refs_1_ = bf16[64,1536]{1,0:T(8,128)(2,1)S(1)} collective-permute-done((bf16[64,1536]{1,0:T(8,128)(2,1)}, bf16[64,1536]{1,0:T(8,128)(2,1)S(1)}, u32[]{:S(2)}, u32[]{:S(2)}) %collective-permute-start) | collective-permute-done | bytes 196640 | tf_op jit(solution)/shard_map/ppermute | solution.py:49
  15.5 2.4 %collective-permute-done.1.refs_1_.refs_6_ = bf16[64,1536]{1,0:T(8,128)(2,1)S(1)} collective-permute-done((bf16[64,1536]{1,0:T(8,128)(2,1)}, bf16[64,1536]{1,0:T(8,128)(2,1)S(1)}, u32[]{:S(2)}, u32[]{:S(2)}) %collective-permute-start.1) | collective-permute-done | bytes 196640 | tf_op jit(solution)/shard_map/ppermute | solution.py:49
  18.1 0.4 collective-permute-start.11
  18.5 1.2 %collective-permute-start.8 = (bf16[64,1536]{1,0:T(8,128)(2,1)S(1)}, bf16[64,1536]{1,0:T(8,128)(2,1)S(1)}, u32[]{:S(2)}, u32[]{:S(2)}) collective-permute-start(bf16[64,1536]{1,0:T(8,128)(2,1)S(1)} %collective-permute-done.1.refs_1_.refs_6_), channel_id=1, source_target_pairs={{0,16},{1,17},{2,18},{3,19},{4,20},{5,21},{6,22},{7,23},{8,24},{9,... | collective-permute-start | bytes 589832 | tf_op jit(solution)/shard_map/ppermute | solution.py:49
  19.7 2.0 %collective-permute-start.7 = (bf16[64,1536]{1,0:T(8,128)(2,1)S(1)}, bf16[64,1536]{1,0:T(8,128)(2,1)S(1)}, u32[]{:S(2)}, u32[]{:S(2)}) collective-permute-start(bf16[64,1536]{1,0:T(8,128)(2,1)S(1)} %shard_map.42), channel_id=1, source_target_pairs={{0,1},{1,0},{2,3},{3,2},{4,5},{5,4},{6,7},{7,6},{8,9},{9,8},{10,11... | collective-permute-start | bytes 589832 | tf_op jit(solution)/shard_map/ppermute | solution.py:49
  21.8 0.6 %collective-permute-start.6 = (bf16[64,1536]{1,0:T(8,128)(2,1)S(1)}, bf16[64,1536]{1,0:T(8,128)(2,1)S(1)}, u32[]{:S(2)}, u32[]{:S(2)}) collective-permute-start(bf16[64,1536]{1,0:T(8,128)(2,1)S(1)} %collective-permute-done.refs_1_), channel_id=1, source_target_pairs={{0,8},{1,9},{2,10},{3,11},{4,12},{5,13},{6,14},{7,15},{8,0},{9,1},... | collective-permute-start | bytes 589832 | tf_op jit(solution)/shard_map/ppermute | solution.py:49
  22.4 8.2 %collective-permute-done.11.refs_11_.refs_1_ = bf16[64,1536]{1,0:T(8,128)(2,1)S(1)} collective-permute-done((bf16[64,1536]{1,0:T(8,128)(2,1)S(1)}, bf16[64,1536]{1,0:T(8,128)(2,1)S(1)}, u32[]{:S(2)}, u32[]{:S(2)}) %collective-permute-start.11) | collective-permute-done | bytes 196640 | tf_op jit(solution)/shard_map/ppermute | solution.py:49
  30.6 0.5 collective-permute-start.10
  31.1 0.9 %collective-permute-done.12.refs_13_.refs_4_ = bf16[64,1536]{1,0:T(8,128)(2,1)S(1)} collective-permute-done((bf16[64,1536]{1,0:T(8,128)(2,1)S(1)}, bf16[64,1536]{1,0:T(8,128)(2,1)S(1)}, u32[]{:S(2)}, u32[]{:S(2)}) %collective-permute-start.12) | collective-permute-done | bytes 196640 | tf_op jit(solution)/shard_map/ppermute | solution.py:49
  32.0 0.3 collective-permute-done.10.refs_10_
  32.3 1.0 %shard_map.45 = (f32[256,512]{1,0:T(8,128)S(1)}, f32[256,512]{1,0:T(8,128)S(1)}, f32[3,4,64]{2,1,0:T(4,128)S(1)}, f32[3,8,64]{2,1,0:T(8,128)S(1)}) custom-call(bf16[64,2304]{1,0:T(8,128)(2,1)S(1)} %shard_map.41.refs_0_, bf16[64,1536]{1,0:T(8,128)(2,1)S(1)} %collective-permute-done.refs_1_, bf16[64,1536]{1,0:T(8,128)(2,1)S(1)} %collective-permute-done.4.refs_2_, ...), custom_call_target="tpu_custom_call" | custom-call | flops 603979776 | bytes 4301824 | tf_op jit(solution)/shard_map/pallas_call | solution.py:180
  33.3 0.3 collective-permute-start.13
  33.6 1.0 %collective-permute-done.13 = f32[3,12,64]{2,1,0:T(8,128)S(1)} collective-permute-done((f32[3,12,64]{2,1,0:T(8,128)S(1)}, f32[3,12,64]{2,1,0:T(8,128)S(1)}, u32[]{:S(2)}, u32[]{:S(2)}) %collective-permute-start.13) | collective-permute-done | bytes 9248 | tf_op jit(solution)/shard_map/ppermute | solution.py:49
  34.7 3.7 %collective-permute-done.14 = f32[3,8,64]{2,1,0:T(8,128)S(1)} collective-permute-done((f32[3,8,64]{2,1,0:T(8,128)S(1)}, f32[3,8,64]{2,1,0:T(8,128)S(1)}, u32[]{:S(2)}, u32[]{:S(2)}) %collective-permute-start.14) | collective-permute-done | bytes 6176 | tf_op jit(solution)/shard_map/ppermute | solution.py:249
  38.4 0.6 %collective-permute-start.15 = (f32[3,8,64]{2,1,0:T(8,128)S(1)}, f32[3,8,64]{2,1,0:T(8,128)S(1)}, u32[]{:S(2)}, u32[]{:S(2)}) collective-permute-start(f32[3,8,64]{2,1,0:T(8,128)S(1)} %add.10), channel_id=1, source_target_pairs={{0,8},{1,9},{2,10},{3,11},{4,20},{5,21},{6,22},{7,23},{8,0},{9,1},... | collective-permute-start | bytes 18440 | tf_op jit(solution)/shard_map/ppermute | solution.py:249
  39.0 3.2 %collective-permute-done.15 = f32[3,8,64]{2,1,0:T(8,128)S(1)} collective-permute-done((f32[3,8,64]{2,1,0:T(8,128)S(1)}, f32[3,8,64]{2,1,0:T(8,128)S(1)}, u32[]{:S(2)}, u32[]{:S(2)}) %collective-permute-start.15) | collective-permute-done | bytes 6176 | tf_op jit(solution)/shard_map/ppermute | solution.py:249
  42.3 1.2 %collective-permute-done.16 = f32[3,8,64]{2,1,0:T(8,128)S(1)} collective-permute-done((f32[3,8,64]{2,1,0:T(8,128)S(1)}, f32[3,8,64]{2,1,0:T(8,128)S(1)}, u32[]{:S(2)}, u32[]{:S(2)}) %collective-permute-start.16) | collective-permute-done | bytes 6176 | tf_op jit(solution)/shard_map/ppermute | solution.py:49
  43.5 0.1 reshape.26.row_sum
  43.6 0.9 %shard_map.46 = (f32[64,768]{1,0:T(8,128)S(1)}, f32[8,128]{1,0:T(8,128)S(1)}, f32[64,896]{1,0:T(8,128)S(1)}, f32[64,896]{1,0:T(8,128)S(1)}, f32[64,896]{1,0:T(8,128)S(1)}) custom-call(f32[256,512]{1,0:T(8,128)S(1)} %get-tuple-element.21.gram_s, f32[256,512]{1,0:T(8,128)S(1)} %get-tuple-element.22.gram_t, f32[3,1,256]{2,1,0:T(1,128)S(1)} %reshape.26.row_sum, ...), custom_call_target="tpu_custom_call" | custom-call | flops 402653184 | bytes 3519488 | tf_op jit(solution)/shard_map/pallas_call | solution.py:180
  44.6 0.6 %collective-permute-start.18 = (f16[64,896]{1,0:T(8,128)(2,1)S(1)}, f16[64,896]{1,0:T(8,128)(2,1)S(1)}, u32[]{:S(2)}, u32[]{:S(2)}) collective-permute-start(f16[64,896]{1,0:T(8,128)(2,1)S(1)} %convert_element_type.20), channel_id=1, source_target_pairs={{0,8},{1,9},{2,10},{3,11},{4,12},{5,13},{6,14},{7,15},{8,0},{9,1},... | collective-permute-start | bytes 344072 | tf_op jit(solution)/shard_map/ppermute | solution.py:49
  45.3 3.0 %collective-permute-start.19 = (f16[64,896]{1,0:T(8,128)(2,1)S(1)}, f16[64,896]{1,0:T(8,128)(2,1)S(1)}, u32[]{:S(2)}, u32[]{:S(2)}) collective-permute-start(f16[64,896]{1,0:T(8,128)(2,1)S(1)} %convert_element_type.22), channel_id=1, source_target_pairs={{0,9},{1,8},{2,11},{3,10},{4,13},{5,12},{6,15},{7,14},{8,1},{9,0},... | collective-permute-start | bytes 344072 | tf_op jit(solution)/shard_map/ppermute | solution.py:49
  48.3 2.3 %collective-permute-done.17 = f16[64,896]{1,0:T(8,128)(2,1)S(1)} collective-permute-done((f16[64,896]{1,0:T(8,128)(2,1)S(1)}, f16[64,896]{1,0:T(8,128)(2,1)S(1)}, u32[]{:S(2)}, u32[]{:S(2)}) %collective-permute-start.17) | collective-permute-done | bytes 114720 | tf_op jit(solution)/shard_map/ppermute | solution.py:49
  50.6 1.8 %collective-permute-done.18 = f16[64,896]{1,0:T(8,128)(2,1)S(1)} collective-permute-done((f16[64,896]{1,0:T(8,128)(2,1)S(1)}, f16[64,896]{1,0:T(8,128)(2,1)S(1)}, u32[]{:S(2)}, u32[]{:S(2)}) %collective-permute-start.18) | collective-permute-done | bytes 114720 | tf_op jit(solution)/shard_map/ppermute | solution.py:49
  52.4 0.8 %shard_map.47 = (f32[64,768]{1,0:T(8,128)}, f32[1,1]{1,0:T(1,128)}) custom-call(f32[64,768]{1,0:T(8,128)S(1)} %get-tuple-element.25.own, f32[8,128]{1,0:T(8,128)S(1)} %get-tuple-element.26.share, f32[64,896]{1,0:T(8,128)S(1)} %convert_element_type.19.refs_0_, f32[64,896]{1,0:T(8,128)S(1)} %convert_element_type.21.refs_1_, ...), custom_call_target="tpu_custom_call" | custom-call | bytes 1085444 | tf_op jit(solution)/shard_map/pallas_call | solution.py:180
  (35 shorter events, 0.7 us)
Async XLA Ops:
  0.6 10.5 %collective-permute-start.3 = (bf16[64,768]{1,0:T(8,128)(2,1)}, bf16[64,768]{1,0:T(8,128)(2,1)S(1)}, u32[]{:S(2)}, u32[]{:S(2)}) collective-permute-start(bf16[64,768]{1,0:T(8,128)(2,1)} %refs_1_.1), channel_id=1, source_target_pairs={{0,16},{1,17},{2,18},{3,19},{4,20},{5,21},{6,22},{7,23},{8,24},{9,... | collective-permute-start | bytes 294920 | tf_op jit(solution)/shard_map/ppermute | solution.py:49
  3.7 7.5 %collective-permute-start.2 = (bf16[64,768]{1,0:T(8,128)(2,1)}, bf16[64,768]{1,0:T(8,128)(2,1)S(1)}, u32[]{:S(2)}, u32[]{:S(2)}) collective-permute-start(bf16[64,768]{1,0:T(8,128)(2,1)} %refs_1_.1), channel_id=1, source_target_pairs={{0,8},{1,9},{2,10},{3,11},{4,12},{5,13},{6,14},{7,15},{8,0},{9,1},... | collective-permute-start | bytes 294920 | tf_op jit(solution)/shard_map/ppermute | solution.py:49
  5.2 10.4 %collective-permute-start = (bf16[64,1536]{1,0:T(8,128)(2,1)}, bf16[64,1536]{1,0:T(8,128)(2,1)S(1)}, u32[]{:S(2)}, u32[]{:S(2)}) collective-permute-start(bf16[64,1536]{1,0:T(8,128)(2,1)} %refs_0_.1), channel_id=1, source_target_pairs={{0,1},{1,0},{2,3},{3,2},{4,5},{5,4},{6,7},{7,6},{8,9},{9,8},{10,11... | collective-permute-start | bytes 589832 | tf_op jit(solution)/shard_map/ppermute | solution.py:49
  6.7 11.2 %collective-permute-start.1 = (bf16[64,1536]{1,0:T(8,128)(2,1)}, bf16[64,1536]{1,0:T(8,128)(2,1)S(1)}, u32[]{:S(2)}, u32[]{:S(2)}) collective-permute-start(bf16[64,1536]{1,0:T(8,128)(2,1)} %refs_0_.1), channel_id=1, source_target_pairs={{0,2},{1,3},{2,0},{3,1},{4,6},{5,7},{6,4},{7,5},{8,10},{9,11},{10,... | collective-permute-start | bytes 589832 | tf_op jit(solution)/shard_map/ppermute | solution.py:49
  9.3 0.9 %copy-start = (bf16[64,768]{1,0:T(8,128)(2,1)S(1)}, bf16[64,768]{1,0:T(8,128)(2,1)}, u32[]{:S(2)}) copy-start(bf16[64,768]{1,0:T(8,128)(2,1)} %refs_1_.1) | copy-start | bytes 294916
  11.2 6.7 %collective-permute-start.5 = (bf16[64,1536]{1,0:T(8,128)(2,1)}, bf16[64,1536]{1,0:T(8,128)(2,1)S(1)}, u32[]{:S(2)}, u32[]{:S(2)}) collective-permute-start(bf16[64,1536]{1,0:T(8,128)(2,1)} %refs_0_.1), channel_id=1, source_target_pairs={{0,16},{1,17},{2,18},{3,19},{4,20},{5,21},{6,22},{7,23},{8,24},{9,... | collective-permute-start | bytes 589832 | tf_op jit(solution)/shard_map/ppermute | solution.py:49
  11.8 6.2 %collective-permute-start.4 = (bf16[64,1536]{1,0:T(8,128)(2,1)}, bf16[64,1536]{1,0:T(8,128)(2,1)S(1)}, u32[]{:S(2)}, u32[]{:S(2)}) collective-permute-start(bf16[64,1536]{1,0:T(8,128)(2,1)} %refs_0_.1), channel_id=1, source_target_pairs={{0,8},{1,9},{2,10},{3,11},{4,12},{5,13},{6,14},{7,15},{8,0},{9,1},... | collective-permute-start | bytes 589832 | tf_op jit(solution)/shard_map/ppermute | solution.py:49
  18.0 14.3 %collective-permute-start.9 = (bf16[64,6144]{1,0:T(8,128)(2,1)S(1)}, bf16[64,6144]{1,0:T(8,128)(2,1)S(1)}, u32[]{:S(2)}, u32[]{:S(2)}) collective-permute-start(bf16[64,6144]{1,0:T(8,128)(2,1)S(1)} %shard_map.43), channel_id=1, source_target_pairs={{0,4},{1,5},{2,6},{3,7},{4,0},{5,1},{6,2},{7,3},{8,12},{9,13},{10,... | collective-permute-start | bytes 2359304 | tf_op jit(solution)/shard_map/ppermute | solution.py:49
  18.1 12.4 %collective-permute-start.11 = (bf16[64,1536]{1,0:T(8,128)(2,1)S(1)}, bf16[64,1536]{1,0:T(8,128)(2,1)S(1)}, u32[]{:S(2)}, u32[]{:S(2)}) collective-permute-start(bf16[64,1536]{1,0:T(8,128)(2,1)S(1)} %shard_map.44), channel_id=1, source_target_pairs={{0,2},{1,3},{2,0},{3,1},{4,6},{5,7},{6,4},{7,5},{8,10},{9,11},{10,... | collective-permute-start | bytes 589832 | tf_op jit(solution)/shard_map/ppermute | solution.py:49
  18.5 12.1 %collective-permute-start.8 = (bf16[64,1536]{1,0:T(8,128)(2,1)S(1)}, bf16[64,1536]{1,0:T(8,128)(2,1)S(1)}, u32[]{:S(2)}, u32[]{:S(2)}) collective-permute-start(bf16[64,1536]{1,0:T(8,128)(2,1)S(1)} %collective-permute-done.1.refs_1_.refs_6_), channel_id=1, source_target_pairs={{0,16},{1,17},{2,18},{3,19},{4,20},{5,21},{6,22},{7,23},{8,24},{9,... | collective-permute-start | bytes 589832 | tf_op jit(solution)/shard_map/ppermute | solution.py:49
  19.7 11.3 %collective-permute-start.7 = (bf16[64,1536]{1,0:T(8,128)(2,1)S(1)}, bf16[64,1536]{1,0:T(8,128)(2,1)S(1)}, u32[]{:S(2)}, u32[]{:S(2)}) collective-permute-start(bf16[64,1536]{1,0:T(8,128)(2,1)S(1)} %shard_map.42), channel_id=1, source_target_pairs={{0,1},{1,0},{2,3},{3,2},{4,5},{5,4},{6,7},{7,6},{8,9},{9,8},{10,11... | collective-permute-start | bytes 589832 | tf_op jit(solution)/shard_map/ppermute | solution.py:49
  21.8 9.3 %collective-permute-start.6 = (bf16[64,1536]{1,0:T(8,128)(2,1)S(1)}, bf16[64,1536]{1,0:T(8,128)(2,1)S(1)}, u32[]{:S(2)}, u32[]{:S(2)}) collective-permute-start(bf16[64,1536]{1,0:T(8,128)(2,1)S(1)} %collective-permute-done.refs_1_), channel_id=1, source_target_pairs={{0,8},{1,9},{2,10},{3,11},{4,12},{5,13},{6,14},{7,15},{8,0},{9,1},... | collective-permute-start | bytes 589832 | tf_op jit(solution)/shard_map/ppermute | solution.py:49
  30.5 1.4 %collective-permute-start.12 = (bf16[64,1536]{1,0:T(8,128)(2,1)S(1)}, bf16[64,1536]{1,0:T(8,128)(2,1)S(1)}, u32[]{:S(2)}, u32[]{:S(2)}) collective-permute-start(bf16[64,1536]{1,0:T(8,128)(2,1)S(1)} %collective-permute-done.11.refs_11_.refs_1_), channel_id=1, source_target_pairs={{0,4},{1,5},{2,6},{3,7},{4,0},{5,1},{6,2},{7,3},{8,12},{9,13},{10,... | collective-permute-start | bytes 589832 | tf_op jit(solution)/shard_map/ppermute | solution.py:49
  30.6 1.7 %collective-permute-start.10 = (bf16[64,1536]{1,0:T(8,128)(2,1)S(1)}, bf16[64,1536]{1,0:T(8,128)(2,1)S(1)}, u32[]{:S(2)}, u32[]{:S(2)}) collective-permute-start(bf16[64,1536]{1,0:T(8,128)(2,1)S(1)} %collective-permute-done.8.refs_8_), channel_id=1, source_target_pairs={{0,4},{1,5},{2,6},{3,7},{4,0},{5,1},{6,2},{7,3},{8,12},{9,13},{10,... | collective-permute-start | bytes 589832 | tf_op jit(solution)/shard_map/ppermute | solution.py:49
  33.3 1.3 %collective-permute-start.13 = (f32[3,12,64]{2,1,0:T(8,128)S(1)}, f32[3,12,64]{2,1,0:T(8,128)S(1)}, u32[]{:S(2)}, u32[]{:S(2)}) collective-permute-start(f32[3,12,64]{2,1,0:T(8,128)S(1)} %pad_maximum_fusion), channel_id=1, source_target_pairs={{0,4},{1,5},{2,6},{3,7},{4,0},{5,1},{6,2},{7,3},{8,12},{9,13},{10,... | collective-permute-start | bytes 27656 | tf_op jit(solution)/shard_map/ppermute | solution.py:49
  34.6 3.8 %collective-permute-start.14 = (f32[3,8,64]{2,1,0:T(8,128)S(1)}, f32[3,8,64]{2,1,0:T(8,128)S(1)}, u32[]{:S(2)}, u32[]{:S(2)}) collective-permute-start(f32[3,8,64]{2,1,0:T(8,128)S(1)} %maximum_select_fusion), channel_id=1, source_target_pairs={{0,1},{1,0},{2,3},{3,2},{4,6},{5,7},{6,4},{7,5},{8,9},{9,8},{10,11... | collective-permute-start | bytes 18440 | tf_op jit(solution)/shard_map/ppermute | solution.py:249
  38.4 3.8 %collective-permute-start.15 = (f32[3,8,64]{2,1,0:T(8,128)S(1)}, f32[3,8,64]{2,1,0:T(8,128)S(1)}, u32[]{:S(2)}, u32[]{:S(2)}) collective-permute-start(f32[3,8,64]{2,1,0:T(8,128)S(1)} %add.10), channel_id=1, source_target_pairs={{0,8},{1,9},{2,10},{3,11},{4,20},{5,21},{6,22},{7,23},{8,0},{9,1},... | collective-permute-start | bytes 18440 | tf_op jit(solution)/shard_map/ppermute | solution.py:249
  42.2 1.2 %collective-permute-start.16 = (f32[3,8,64]{2,1,0:T(8,128)S(1)}, f32[3,8,64]{2,1,0:T(8,128)S(1)}, u32[]{:S(2)}, u32[]{:S(2)}) collective-permute-start(f32[3,8,64]{2,1,0:T(8,128)S(1)} %add.11), channel_id=1, source_target_pairs={{0,4},{1,5},{2,6},{3,7},{4,0},{5,1},{6,2},{7,3},{8,12},{9,13},{10,... | collective-permute-start | bytes 18440 | tf_op jit(solution)/shard_map/ppermute | solution.py:49
  44.5 6.1 %collective-permute-start.17 = (f16[64,896]{1,0:T(8,128)(2,1)S(1)}, f16[64,896]{1,0:T(8,128)(2,1)S(1)}, u32[]{:S(2)}, u32[]{:S(2)}) collective-permute-start(f16[64,896]{1,0:T(8,128)(2,1)S(1)} %convert_element_type.18), channel_id=1, source_target_pairs={{0,1},{1,0},{2,3},{3,2},{4,5},{5,4},{6,7},{7,6},{8,9},{9,8},{10,11... | collective-permute-start | bytes 344072 | tf_op jit(solution)/shard_map/ppermute | solution.py:49
  44.6 7.7 %collective-permute-start.18 = (f16[64,896]{1,0:T(8,128)(2,1)S(1)}, f16[64,896]{1,0:T(8,128)(2,1)S(1)}, u32[]{:S(2)}, u32[]{:S(2)}) collective-permute-start(f16[64,896]{1,0:T(8,128)(2,1)S(1)} %convert_element_type.20), channel_id=1, source_target_pairs={{0,8},{1,9},{2,10},{3,11},{4,12},{5,13},{6,14},{7,15},{8,0},{9,1},... | collective-permute-start | bytes 344072 | tf_op jit(solution)/shard_map/ppermute | solution.py:49
  45.3 7.1 %collective-permute-start.19 = (f16[64,896]{1,0:T(8,128)(2,1)S(1)}, f16[64,896]{1,0:T(8,128)(2,1)S(1)}, u32[]{:S(2)}, u32[]{:S(2)}) collective-permute-start(f16[64,896]{1,0:T(8,128)(2,1)S(1)} %convert_element_type.22), channel_id=1, source_target_pairs={{0,9},{1,8},{2,11},{3,10},{4,13},{5,12},{6,15},{7,14},{8,1},{9,0},... | collective-permute-start | bytes 344072 | tf_op jit(solution)/shard_map/ppermute | solution.py:49

commit v15 on v14

--- a/solution.py
+++ b/solution.py
@@ -75,17 +75,15 @@
 
     for side_t, _, masks in reversed(sides):
         side_t[1] = whole(send(teacher, masks[0], count))
-    for _, side_s, masks in reversed(sides):
-        for b, mask in enumerate(masks):
-            if b:
-                side_s[1 << b] = whole(send(student, mask, count))
+    swapped = [send(value, core_mask, count) for value in (teacher, student)]
     own = join(teacher, student)
-    late = after(teacher, (row_s[2][0], col_s[2][0], own))
-    for side_t, _, masks in reversed(sides):
+    late_t, late_s = after((teacher, student), (*swapped, own))
+    for side_t, side_s, masks in reversed(sides):
         side_t[0] = (own, 0, teacher.shape[1])
         for b, mask in enumerate(masks):
             if b:
-                side_t[1 << b] = whole(send(late, mask, count))
+                side_s[1 << b] = whole(send(late_s, mask, count))
+                side_t[1 << b] = whole(send(late_t, mask, count))
 
     def long_way(side_s, masks, gate):
         forward(side_s, masks, lambda place: not place & 1)
@@ -103,11 +101,11 @@
     for side_t, _, masks in reversed(sides):
         forward(side_t, masks, lambda place: True)
 
-    core_t, core_s = {}, {}
-    ones = [0] + [1 << b for b in range(len(plane_masks))]
+    core_t, core_s = {0: whole(swapped[0])}, {0: whole(swapped[1])}
+    ones = [1 << b for b in range(len(plane_masks))]
     rest = [p for p in range(1 << len(plane_masks)) if p.bit_count() > 1]
     swaps = [
-        [(col_t, core_t, p) for p in ones] + [(col_s, core_s, p) for p in col_s if not p & 1],
+        [(col_t, core_t, p) for p in ones] + [(col_s, core_s, p) for p in col_s if p and not p & 1],
         [(col_t, core_t, p) for p in rest],
         [(col_s, core_s, p) for p in col_s if p & 1],
     ]

time: 53.4 us -> 55.9 us (1.047)
  starting transfers between devices: 19.3 us -> 22.4 us
  local copies, waits for them, and re-layouts: 1.11 us -> 2.08 us
  Pallas kernels: 3.76 us -> 2.84 us
  waiting for transfers between devices: 28.1 us -> 27.4 us
    ppermute x18 -> x20, starting transfers between devices: 18.7 us -> 20.8 us  [send(): return lax.ppermute(value, AXES, [(i, i ^ mask) for i in range(count)])]
    unnamed x2 -> x6, local copies, waits for them, and re-layouts: 0.89 us -> 1.86 us
    ppermute x2, starting transfers between devices: 0.67 us -> 1.61 us  [exchange_sums(): got = lax.ppermute(sums, AXES, pairs).reshape(3, -1, 2, 1 << b, rows)]
    ppermute x2, waiting for transfers between devices: 6.84 us -> 5.91 us  [exchange_sums(): got = lax.ppermute(sums, AXES, pairs).reshape(3, -1, 2, 1 << b, rows)]
    pallas_call x7, Pallas kernels: 3.76 us -> 2.84 us  [call(): pl.pallas_call(kernel, out_shape=outputs, **options, compiler_params=pltp...]
    ppermute x18 -> x20, waiting for transfers between devices: 21.2 us -> 21.5 us  [send(): return lax.ppermute(value, AXES, [(i, i ^ mask) for i in range(count)])]
  transfers between devices with their start and end apart: 20 -> 22, of which waited for: 11 -> 13; matrix products, arithmetic and copies ran while one was open for 0% -> 0% of each run, Pallas kernels for 2% -> 0%
where the time goes in v15:
time: 55.9 us; the launch traced here: 55.8 us
  waiting for transfers between devices  27.4 us (49%)
  starting transfers between devices  22.4 us (40%)
  Pallas kernels  2.84 us (5%)
  local copies, waits for them, and re-layouts  2.08 us (4%)
  between operations  0.82 us (1%)
    ppermute x20, waiting for transfers between devices, send(): return lax.ppermute(value, AXES, [(i, i ^ mask) for i in range(count)])  21.5 us
    ppermute x20, starting transfers between devices, send(): return lax.ppermute(value, AXES, [(i, i ^ mask) for i in range(count)])  20.8 us
    ppermute x2, waiting for transfers between devices, exchange_sums(): got = lax.ppermute(sums, AXES, pairs).reshape(3, -1, 2, 1 << b, rows)  5.91 us
    pallas_call x7, Pallas kernels, call(): pl.pallas_call(kernel, out_shape=outputs, **options, compiler_params=pltp...  2.84 us
    unnamed x6, local copies, waits for them, and re-layouts  1.86 us
    ppermute x2, starting transfers between devices, exchange_sums(): got = lax.ppermute(sums, AXES, pairs).reshape(3, -1, 2, 1 << b, rows)  1.61 us
  transfers between devices with their start and end apart: 22, of which 13 were waited for; matrix products, arithmetic and copies ran while one was open for 0% of the time, Pallas kernels for 0%

profile of v15, /device:TPU:0, one launch (start us, length us, event | category | flops | bytes accessed | tf_op | source)
XLA Modules:
  0.0 55.8 jit_solution(6850259966743438060)
XLA Ops:
  0.6 0.5 collective-permute-start.2
  1.2 3.0 %collective-permute-start = (bf16[64,1536]{1,0:T(8,128)(2,1)}, bf16[64,1536]{1,0:T(8,128)(2,1)S(1)}, u32[]{:S(2)}, u32[]{:S(2)}) collective-permute-start(bf16[64,1536]{1,0:T(8,128)(2,1)} %refs_0_.1), channel_id=1, source_target_pairs={{0,1},{1,0},{2,3},{3,2},{4,5},{5,4},{6,7},{7,6},{8,9},{9,8},{10,11... | collective-permute-start | bytes 589832 | tf_op jit(solution)/shard_map/ppermute | solution.py:49
  4.2 2.6 %collective-permute-start.1 = (bf16[64,1536]{1,0:T(8,128)(2,1)}, bf16[64,1536]{1,0:T(8,128)(2,1)S(1)}, u32[]{:S(2)}, u32[]{:S(2)}) collective-permute-start(bf16[64,1536]{1,0:T(8,128)(2,1)} %refs_0_.1), channel_id=1, source_target_pairs={{0,2},{1,3},{2,0},{3,1},{4,6},{5,7},{6,4},{7,5},{8,10},{9,11},{10,... | collective-permute-start | bytes 589832 | tf_op jit(solution)/shard_map/ppermute | solution.py:49
  6.8 1.0 %copy-done = bf16[64,1536]{1,0:T(8,128)(2,1)S(1)} copy-done((bf16[64,1536]{1,0:T(8,128)(2,1)S(1)}, bf16[64,1536]{1,0:T(8,128)(2,1)}, u32[]{:S(2)}) %copy-start) | copy-done | bytes 196632
  7.8 0.9 %copy-done.1 = bf16[64,768]{1,0:T(8,128)(2,1)S(1)} copy-done((bf16[64,768]{1,0:T(8,128)(2,1)S(1)}, bf16[64,768]{1,0:T(8,128)(2,1)}, u32[]{:S(2)}) %copy-start.1) | copy-done | bytes 98328
  8.7 1.6 %collective-permute-start.5 = (bf16[64,1536]{1,0:T(8,128)(2,1)S(1)}, bf16[64,1536]{1,0:T(8,128)(2,1)S(1)}, u32[]{:S(2)}, u32[]{:S(2)}) collective-permute-start(bf16[64,1536]{1,0:T(8,128)(2,1)S(1)} %copy-done), channel_id=1, source_target_pairs={{0,16},{1,17},{2,18},{3,19},{4,20},{5,21},{6,22},{7,23},{8,24},{9,... | collective-permute-start | bytes 589832 | tf_op jit(solution)/shard_map/ppermute | solution.py:49
  10.3 1.5 %collective-permute-start.4 = (bf16[64,1536]{1,0:T(8,128)(2,1)S(1)}, bf16[64,1536]{1,0:T(8,128)(2,1)S(1)}, u32[]{:S(2)}, u32[]{:S(2)}) collective-permute-start(bf16[64,1536]{1,0:T(8,128)(2,1)S(1)} %copy-done), channel_id=1, source_target_pairs={{0,8},{1,9},{2,10},{3,11},{4,12},{5,13},{6,14},{7,15},{8,0},{9,1},... | collective-permute-start | bytes 589832 | tf_op jit(solution)/shard_map/ppermute | solution.py:49
  11.8 0.5 collective-permute-start.10
  12.3 1.4 %collective-permute-done.refs_1_ = bf16[64,1536]{1,0:T(8,128)(2,1)S(1)} collective-permute-done((bf16[64,1536]{1,0:T(8,128)(2,1)}, bf16[64,1536]{1,0:T(8,128)(2,1)S(1)}, u32[]{:S(2)}, u32[]{:S(2)}) %collective-permute-start) | collective-permute-done | bytes 196640 | tf_op jit(solution)/shard_map/ppermute | solution.py:49
  13.7 2.6 %collective-permute-done.1.refs_0_.refs_6_ = bf16[64,1536]{1,0:T(8,128)(2,1)S(1)} collective-permute-done((bf16[64,1536]{1,0:T(8,128)(2,1)}, bf16[64,1536]{1,0:T(8,128)(2,1)S(1)}, u32[]{:S(2)}, u32[]{:S(2)}) %collective-permute-start.1) | collective-permute-done | bytes 196640 | tf_op jit(solution)/shard_map/ppermute | solution.py:49
  16.4 0.9 %collective-permute-done.10.refs_2_.refs_1_.refs_13_ = bf16[64,768]{1,0:T(8,128)(2,1)S(1)} collective-permute-done((bf16[64,768]{1,0:T(8,128)(2,1)S(1)}, bf16[64,768]{1,0:T(8,128)(2,1)S(1)}, u32[]{:S(2)}, u32[]{:S(2)}) %collective-permute-start.10) | collective-permute-done | bytes 98336 | tf_op jit(solution)/shard_map/ppermute | solution.py:49
  17.4 0.4 collective-permute-start.13
  17.8 1.5 %collective-permute-start.9 = (bf16[64,1536]{1,0:T(8,128)(2,1)S(1)}, bf16[64,1536]{1,0:T(8,128)(2,1)S(1)}, u32[]{:S(2)}, u32[]{:S(2)}) collective-permute-start(bf16[64,1536]{1,0:T(8,128)(2,1)S(1)} %collective-permute-done.1.refs_0_.refs_6_), channel_id=1, source_target_pairs={{0,16},{1,17},{2,18},{3,19},{4,20},{5,21},{6,22},{7,23},{8,24},{9,... | collective-permute-start | bytes 589832 | tf_op jit(solution)/shard_map/ppermute | solution.py:49
  19.3 1.5 %collective-permute-start.7 = (bf16[64,768]{1,0:T(8,128)(2,1)S(1)}, bf16[64,768]{1,0:T(8,128)(2,1)S(1)}, u32[]{:S(2)}, u32[]{:S(2)}) collective-permute-start(bf16[64,768]{1,0:T(8,128)(2,1)S(1)} %copy-done.2), channel_id=1, source_target_pairs={{0,8},{1,9},{2,10},{3,11},{4,12},{5,13},{6,14},{7,15},{8,0},{9,1},... | collective-permute-start | bytes 294920 | tf_op jit(solution)/shard_map/ppermute | solution.py:49
  20.8 3.1 %collective-permute-done.7.refs_1_.refs_5_ = bf16[64,768]{1,0:T(8,128)(2,1)S(1)} collective-permute-done((bf16[64,768]{1,0:T(8,128)(2,1)S(1)}, bf16[64,768]{1,0:T(8,128)(2,1)S(1)}, u32[]{:S(2)}, u32[]{:S(2)}) %collective-permute-start.7) | collective-permute-done | bytes 98336 | tf_op jit(solution)/shard_map/ppermute | solution.py:49
  24.0 1.7 %collective-permute-start.8 = (bf16[64,1536]{1,0:T(8,128)(2,1)S(1)}, bf16[64,1536]{1,0:T(8,128)(2,1)S(1)}, u32[]{:S(2)}, u32[]{:S(2)}) collective-permute-start(bf16[64,1536]{1,0:T(8,128)(2,1)S(1)} %shard_map.42), channel_id=1, source_target_pairs={{0,1},{1,0},{2,3},{3,2},{4,5},{5,4},{6,7},{7,6},{8,9},{9,8},{10,11... | collective-permute-start | bytes 589832 | tf_op jit(solution)/shard_map/ppermute | solution.py:49
  25.7 1.5 %collective-permute-start.6 = (bf16[64,1536]{1,0:T(8,128)(2,1)S(1)}, bf16[64,1536]{1,0:T(8,128)(2,1)S(1)}, u32[]{:S(2)}, u32[]{:S(2)}) collective-permute-start(bf16[64,1536]{1,0:T(8,128)(2,1)S(1)} %collective-permute-done.refs_1_), channel_id=1, source_target_pairs={{0,8},{1,9},{2,10},{3,11},{4,12},{5,13},{6,14},{7,15},{8,0},{9,1},... | collective-permute-start | bytes 589832 | tf_op jit(solution)/shard_map/ppermute | solution.py:49
  27.2 2.6 %collective-permute-done.13.refs_12_.refs_1_ = bf16[64,1536]{1,0:T(8,128)(2,1)S(1)} collective-permute-done((bf16[64,1536]{1,0:T(8,128)(2,1)S(1)}, bf16[64,1536]{1,0:T(8,128)(2,1)S(1)}, u32[]{:S(2)}, u32[]{:S(2)}) %collective-permute-start.13) | collective-permute-done | bytes 196640 | tf_op jit(solution)/shard_map/ppermute | solution.py:49
  29.8 0.5 collective-permute-start.12
  30.3 3.6 %collective-permute-done.8.refs_4_ = bf16[64,1536]{1,0:T(8,128)(2,1)S(1)} collective-permute-done((bf16[64,1536]{1,0:T(8,128)(2,1)S(1)}, bf16[64,1536]{1,0:T(8,128)(2,1)S(1)}, u32[]{:S(2)}, u32[]{:S(2)}) %collective-permute-start.8) | collective-permute-done | bytes 196640 | tf_op jit(solution)/shard_map/ppermute | solution.py:49
  34.0 1.1 %shard_map.45 = (f32[256,512]{1,0:T(8,128)S(1)}, f32[256,512]{1,0:T(8,128)S(1)}, f32[3,4,64]{2,1,0:T(4,128)S(1)}, f32[3,8,64]{2,1,0:T(8,128)S(1)}) custom-call(bf16[64,2304]{1,0:T(8,128)(2,1)S(1)} %shard_map.41.refs_0_, bf16[64,1536]{1,0:T(8,128)(2,1)S(1)} %collective-permute-done.refs_1_, bf16[64,1536]{1,0:T(8,128)(2,1)S(1)} %collective-permute-done.4.refs_2_, ...), custom_call_target="tpu_custom_call" | custom-call | flops 603979776 | bytes 4301824 | tf_op jit(solution)/shard_map/pallas_call | solution.py:178
  35.1 1.2 %collective-permute-done.15 = f32[3,12,64]{2,1,0:T(8,128)S(1)} collective-permute-done((f32[3,12,64]{2,1,0:T(8,128)S(1)}, f32[3,12,64]{2,1,0:T(8,128)S(1)}, u32[]{:S(2)}, u32[]{:S(2)}) %collective-permute-start.15) | collective-permute-done | bytes 9248 | tf_op jit(solution)/shard_map/ppermute | solution.py:49
  36.4 3.7 %collective-permute-done.16 = f32[3,8,64]{2,1,0:T(8,128)S(1)} collective-permute-done((f32[3,8,64]{2,1,0:T(8,128)S(1)}, f32[3,8,64]{2,1,0:T(8,128)S(1)}, u32[]{:S(2)}, u32[]{:S(2)}) %collective-permute-start.16) | collective-permute-done | bytes 6176 | tf_op jit(solution)/shard_map/ppermute | solution.py:247
  40.1 1.5 %collective-permute-start.17 = (f32[3,8,64]{2,1,0:T(8,128)S(1)}, f32[3,8,64]{2,1,0:T(8,128)S(1)}, u32[]{:S(2)}, u32[]{:S(2)}) collective-permute-start(f32[3,8,64]{2,1,0:T(8,128)S(1)} %add.10), channel_id=1, source_target_pairs={{0,8},{1,9},{2,10},{3,11},{4,20},{5,21},{6,22},{7,23},{8,0},{9,1},... | collective-permute-start | bytes 18440 | tf_op jit(solution)/shard_map/ppermute | solution.py:247
  41.7 2.2 %collective-permute-done.17 = f32[3,8,64]{2,1,0:T(8,128)S(1)} collective-permute-done((f32[3,8,64]{2,1,0:T(8,128)S(1)}, f32[3,8,64]{2,1,0:T(8,128)S(1)}, u32[]{:S(2)}, u32[]{:S(2)}) %collective-permute-start.17) | collective-permute-done | bytes 6176 | tf_op jit(solution)/shard_map/ppermute | solution.py:247
  44.0 1.2 %collective-permute-done.18 = f32[3,8,64]{2,1,0:T(8,128)S(1)} collective-permute-done((f32[3,8,64]{2,1,0:T(8,128)S(1)}, f32[3,8,64]{2,1,0:T(8,128)S(1)}, u32[]{:S(2)}, u32[]{:S(2)}) %collective-permute-start.18) | collective-permute-done | bytes 6176 | tf_op jit(solution)/shard_map/ppermute | solution.py:49
  45.3 0.9 %shard_map.46 = (f32[64,768]{1,0:T(8,128)S(1)}, f32[8,128]{1,0:T(8,128)S(1)}, f32[64,896]{1,0:T(8,128)S(1)}, f32[64,896]{1,0:T(8,128)S(1)}, f32[64,896]{1,0:T(8,128)S(1)}) custom-call(f32[256,512]{1,0:T(8,128)S(1)} %get-tuple-element.23.gram_s, f32[256,512]{1,0:T(8,128)S(1)} %get-tuple-element.24.gram_t, f32[3,1,256]{2,1,0:T(1,128)S(1)} %reshape.26.row_sum, ...), custom_call_target="tpu_custom_call" | custom-call | flops 402653184 | bytes 3322880 | tf_op jit(solution)/shard_map/pallas_call | solution.py:178
  46.4 1.5 %collective-permute-start.20 = (f16[64,896]{1,0:T(8,128)(2,1)S(1)}, f16[64,896]{1,0:T(8,128)(2,1)S(1)}, u32[]{:S(2)}, u32[]{:S(2)}) collective-permute-start(f16[64,896]{1,0:T(8,128)(2,1)S(1)} %convert_element_type.20), channel_id=1, source_target_pairs={{0,8},{1,9},{2,10},{3,11},{4,12},{5,13},{6,14},{7,15},{8,0},{9,1},... | collective-permute-start | bytes 344072 | tf_op jit(solution)/shard_map/ppermute | solution.py:49
  47.9 2.1 %collective-permute-start.21 = (f16[64,896]{1,0:T(8,128)(2,1)S(1)}, f16[64,896]{1,0:T(8,128)(2,1)S(1)}, u32[]{:S(2)}, u32[]{:S(2)}) collective-permute-start(f16[64,896]{1,0:T(8,128)(2,1)S(1)} %convert_element_type.22), channel_id=1, source_target_pairs={{0,9},{1,8},{2,11},{3,10},{4,13},{5,12},{6,15},{7,14},{8,1},{9,0},... | collective-permute-start | bytes 344072 | tf_op jit(solution)/shard_map/ppermute | solution.py:49
  50.0 2.3 %collective-permute-done.19 = f16[64,896]{1,0:T(8,128)(2,1)S(1)} collective-permute-done((f16[64,896]{1,0:T(8,128)(2,1)S(1)}, f16[64,896]{1,0:T(8,128)(2,1)S(1)}, u32[]{:S(2)}, u32[]{:S(2)}) %collective-permute-start.19) | collective-permute-done | bytes 114720 | tf_op jit(solution)/shard_map/ppermute | solution.py:49
  52.4 2.5 %collective-permute-done.21 = f16[64,896]{1,0:T(8,128)(2,1)S(1)} collective-permute-done((f16[64,896]{1,0:T(8,128)(2,1)S(1)}, f16[64,896]{1,0:T(8,128)(2,1)S(1)}, u32[]{:S(2)}, u32[]{:S(2)}) %collective-permute-start.21) | collective-permute-done | bytes 114720 | tf_op jit(solution)/shard_map/ppermute | solution.py:49
  54.9 0.8 %shard_map.47 = (f32[64,768]{1,0:T(8,128)}, f32[1,1]{1,0:T(1,128)}) custom-call(f32[64,768]{1,0:T(8,128)S(1)} %get-tuple-element.27.own, f32[8,128]{1,0:T(8,128)S(1)} %get-tuple-element.28.share, f32[64,896]{1,0:T(8,128)S(1)} %convert_element_type.19.refs_0_, f32[64,896]{1,0:T(8,128)S(1)} %convert_element_type.21.refs_1_, ...), custom_call_target="tpu_custom_call" | custom-call | bytes 1085444 | tf_op jit(solution)/shard_map/pallas_call | solution.py:178
  (43 shorter events, 1.1 us)
Async XLA Ops:
  0.6 8.1 %collective-permute-start.2 = (bf16[64,1536]{1,0:T(8,128)(2,1)}, bf16[64,1536]{1,0:T(8,128)(2,1)S(1)}, u32[]{:S(2)}, u32[]{:S(2)}) collective-permute-start(bf16[64,1536]{1,0:T(8,128)(2,1)} %refs_0_.1), channel_id=1, source_target_pairs={{0,4},{1,5},{2,6},{3,7},{4,0},{5,1},{6,2},{7,3},{8,12},{9,13},{10,... | collective-permute-start | bytes 589832 | tf_op jit(solution)/shard_map/ppermute | solution.py:49
  1.1 7.6 %collective-permute-start.3 = (bf16[64,768]{1,0:T(8,128)(2,1)}, bf16[64,768]{1,0:T(8,128)(2,1)S(1)}, u32[]{:S(2)}, u32[]{:S(2)}) collective-permute-start(bf16[64,768]{1,0:T(8,128)(2,1)} %refs_1_.1), channel_id=1, source_target_pairs={{0,4},{1,5},{2,6},{3,7},{4,0},{5,1},{6,2},{7,3},{8,12},{9,13},{10,... | collective-permute-start | bytes 294920 | tf_op jit(solution)/shard_map/ppermute | solution.py:49
  1.2 12.4 %collective-permute-start = (bf16[64,1536]{1,0:T(8,128)(2,1)}, bf16[64,1536]{1,0:T(8,128)(2,1)S(1)}, u32[]{:S(2)}, u32[]{:S(2)}) collective-permute-start(bf16[64,1536]{1,0:T(8,128)(2,1)} %refs_0_.1), channel_id=1, source_target_pairs={{0,1},{1,0},{2,3},{3,2},{4,5},{5,4},{6,7},{7,6},{8,9},{9,8},{10,11... | collective-permute-start | bytes 589832 | tf_op jit(solution)/shard_map/ppermute | solution.py:49
  4.2 12.0 %collective-permute-start.1 = (bf16[64,1536]{1,0:T(8,128)(2,1)}, bf16[64,1536]{1,0:T(8,128)(2,1)S(1)}, u32[]{:S(2)}, u32[]{:S(2)}) collective-permute-start(bf16[64,1536]{1,0:T(8,128)(2,1)} %refs_0_.1), channel_id=1, source_target_pairs={{0,2},{1,3},{2,0},{3,1},{4,6},{5,7},{6,4},{7,5},{8,10},{9,11},{10,... | collective-permute-start | bytes 589832 | tf_op jit(solution)/shard_map/ppermute | solution.py:49
  6.8 1.0 %copy-start = (bf16[64,1536]{1,0:T(8,128)(2,1)S(1)}, bf16[64,1536]{1,0:T(8,128)(2,1)}, u32[]{:S(2)}) copy-start(bf16[64,1536]{1,0:T(8,128)(2,1)} %refs_0_.1) | copy-start | bytes 589828
  7.8 0.9 %copy-start.1 = (bf16[64,768]{1,0:T(8,128)(2,1)S(1)}, bf16[64,768]{1,0:T(8,128)(2,1)}, u32[]{:S(2)}) copy-start(bf16[64,768]{1,0:T(8,128)(2,1)} %refs_1_.1) | copy-start | bytes 294916
  8.7 3.1 %copy-start.2 = (bf16[64,768]{1,0:T(8,128)(2,1)S(1)}, bf16[64,768]{1,0:T(8,128)(2,1)}, u32[]{:S(2)}) copy-start(bf16[64,768]{1,0:T(8,128)(2,1)} %refs_1_.1) | copy-start | bytes 294916
  8.7 7.5 %collective-permute-start.5 = (bf16[64,1536]{1,0:T(8,128)(2,1)S(1)}, bf16[64,1536]{1,0:T(8,128)(2,1)S(1)}, u32[]{:S(2)}, u32[]{:S(2)}) collective-permute-start(bf16[64,1536]{1,0:T(8,128)(2,1)S(1)} %copy-done), channel_id=1, source_target_pairs={{0,16},{1,17},{2,18},{3,19},{4,20},{5,21},{6,22},{7,23},{8,24},{9,... | collective-permute-start | bytes 589832 | tf_op jit(solution)/shard_map/ppermute | solution.py:49
  10.3 6.0 %collective-permute-start.4 = (bf16[64,1536]{1,0:T(8,128)(2,1)S(1)}, bf16[64,1536]{1,0:T(8,128)(2,1)S(1)}, u32[]{:S(2)}, u32[]{:S(2)}) collective-permute-start(bf16[64,1536]{1,0:T(8,128)(2,1)S(1)} %copy-done), channel_id=1, source_target_pairs={{0,8},{1,9},{2,10},{3,11},{4,12},{5,13},{6,14},{7,15},{8,0},{9,1},... | collective-permute-start | bytes 589832 | tf_op jit(solution)/shard_map/ppermute | solution.py:49
  11.8 5.4 %collective-permute-start.10 = (bf16[64,768]{1,0:T(8,128)(2,1)S(1)}, bf16[64,768]{1,0:T(8,128)(2,1)S(1)}, u32[]{:S(2)}, u32[]{:S(2)}) collective-permute-start(bf16[64,768]{1,0:T(8,128)(2,1)S(1)} %copy-done.2), channel_id=1, source_target_pairs={{0,16},{1,17},{2,18},{3,19},{4,20},{5,21},{6,22},{7,23},{8,24},{9,... | collective-permute-start | bytes 294920 | tf_op jit(solution)/shard_map/ppermute | solution.py:49
  17.3 16.7 %collective-permute-start.11 = (bf16[64,3840]{1,0:T(8,128)(2,1)S(1)}, bf16[64,3840]{1,0:T(8,128)(2,1)S(1)}, u32[]{:S(2)}, u32[]{:S(2)}) collective-permute-start(bf16[64,3840]{1,0:T(8,128)(2,1)S(1)} %shard_map.43), channel_id=1, source_target_pairs={{0,4},{1,5},{2,6},{3,7},{4,0},{5,1},{6,2},{7,3},{8,12},{9,13},{10,... | collective-permute-start | bytes 1474568 | tf_op jit(solution)/shard_map/ppermute | solution.py:49
  17.4 12.5 %collective-permute-start.13 = (bf16[64,1536]{1,0:T(8,128)(2,1)S(1)}, bf16[64,1536]{1,0:T(8,128)(2,1)S(1)}, u32[]{:S(2)}, u32[]{:S(2)}) collective-permute-start(bf16[64,1536]{1,0:T(8,128)(2,1)S(1)} %shard_map.44), channel_id=1, source_target_pairs={{0,2},{1,3},{2,0},{3,1},{4,6},{5,7},{6,4},{7,5},{8,10},{9,11},{10,... | collective-permute-start | bytes 589832 | tf_op jit(solution)/shard_map/ppermute | solution.py:49
  17.8 12.1 %collective-permute-start.9 = (bf16[64,1536]{1,0:T(8,128)(2,1)S(1)}, bf16[64,1536]{1,0:T(8,128)(2,1)S(1)}, u32[]{:S(2)}, u32[]{:S(2)}) collective-permute-start(bf16[64,1536]{1,0:T(8,128)(2,1)S(1)} %collective-permute-done.1.refs_0_.refs_6_), channel_id=1, source_target_pairs={{0,16},{1,17},{2,18},{3,19},{4,20},{5,21},{6,22},{7,23},{8,24},{9,... | collective-permute-start | bytes 589832 | tf_op jit(solution)/shard_map/ppermute | solution.py:49
  19.3 4.6 %collective-permute-start.7 = (bf16[64,768]{1,0:T(8,128)(2,1)S(1)}, bf16[64,768]{1,0:T(8,128)(2,1)S(1)}, u32[]{:S(2)}, u32[]{:S(2)}) collective-permute-start(bf16[64,768]{1,0:T(8,128)(2,1)S(1)} %copy-done.2), channel_id=1, source_target_pairs={{0,8},{1,9},{2,10},{3,11},{4,12},{5,13},{6,14},{7,15},{8,0},{9,1},... | collective-permute-start | bytes 294920 | tf_op jit(solution)/shard_map/ppermute | solution.py:49
  24.0 10.0 %collective-permute-start.8 = (bf16[64,1536]{1,0:T(8,128)(2,1)S(1)}, bf16[64,1536]{1,0:T(8,128)(2,1)S(1)}, u32[]{:S(2)}, u32[]{:S(2)}) collective-permute-start(bf16[64,1536]{1,0:T(8,128)(2,1)S(1)} %shard_map.42), channel_id=1, source_target_pairs={{0,1},{1,0},{2,3},{3,2},{4,5},{5,4},{6,7},{7,6},{8,9},{9,8},{10,11... | collective-permute-start | bytes 589832 | tf_op jit(solution)/shard_map/ppermute | solution.py:49
  25.7 8.2 %collective-permute-start.6 = (bf16[64,1536]{1,0:T(8,128)(2,1)S(1)}, bf16[64,1536]{1,0:T(8,128)(2,1)S(1)}, u32[]{:S(2)}, u32[]{:S(2)}) collective-permute-start(bf16[64,1536]{1,0:T(8,128)(2,1)S(1)} %collective-permute-done.refs_1_), channel_id=1, source_target_pairs={{0,8},{1,9},{2,10},{3,11},{4,12},{5,13},{6,14},{7,15},{8,0},{9,1},... | collective-permute-start | bytes 589832 | tf_op jit(solution)/shard_map/ppermute | solution.py:49
  29.8 4.1 %collective-permute-start.14 = (bf16[64,1536]{1,0:T(8,128)(2,1)S(1)}, bf16[64,1536]{1,0:T(8,128)(2,1)S(1)}, u32[]{:S(2)}, u32[]{:S(2)}) collective-permute-start(bf16[64,1536]{1,0:T(8,128)(2,1)S(1)} %collective-permute-done.13.refs_12_.refs_1_), channel_id=1, source_target_pairs={{0,4},{1,5},{2,6},{3,7},{4,0},{5,1},{6,2},{7,3},{8,12},{9,13},{10,... | collective-permute-start | bytes 589832 | tf_op jit(solution)/shard_map/ppermute | solution.py:49
  29.8 4.1 %collective-permute-start.12 = (bf16[64,1536]{1,0:T(8,128)(2,1)S(1)}, bf16[64,1536]{1,0:T(8,128)(2,1)S(1)}, u32[]{:S(2)}, u32[]{:S(2)}) collective-permute-start(bf16[64,1536]{1,0:T(8,128)(2,1)S(1)} %collective-permute-done.9.refs_8_), channel_id=1, source_target_pairs={{0,4},{1,5},{2,6},{3,7},{4,0},{5,1},{6,2},{7,3},{8,12},{9,13},{10,... | collective-permute-start | bytes 589832 | tf_op jit(solution)/shard_map/ppermute | solution.py:49
  35.0 1.3 %collective-permute-start.15 = (f32[3,12,64]{2,1,0:T(8,128)S(1)}, f32[3,12,64]{2,1,0:T(8,128)S(1)}, u32[]{:S(2)}, u32[]{:S(2)}) collective-permute-start(f32[3,12,64]{2,1,0:T(8,128)S(1)} %pad_maximum_fusion), channel_id=1, source_target_pairs={{0,4},{1,5},{2,6},{3,7},{4,0},{5,1},{6,2},{7,3},{8,12},{9,13},{10,... | collective-permute-start | bytes 27656 | tf_op jit(solution)/shard_map/ppermute | solution.py:49
  36.3 3.8 %collective-permute-start.16 = (f32[3,8,64]{2,1,0:T(8,128)S(1)}, f32[3,8,64]{2,1,0:T(8,128)S(1)}, u32[]{:S(2)}, u32[]{:S(2)}) collective-permute-start(f32[3,8,64]{2,1,0:T(8,128)S(1)} %maximum_select_fusion), channel_id=1, source_target_pairs={{0,1},{1,0},{2,3},{3,2},{4,6},{5,7},{6,4},{7,5},{8,9},{9,8},{10,11... | collective-permute-start | bytes 18440 | tf_op jit(solution)/shard_map/ppermute | solution.py:247
  40.1 3.8 %collective-permute-start.17 = (f32[3,8,64]{2,1,0:T(8,128)S(1)}, f32[3,8,64]{2,1,0:T(8,128)S(1)}, u32[]{:S(2)}, u32[]{:S(2)}) collective-permute-start(f32[3,8,64]{2,1,0:T(8,128)S(1)} %add.10), channel_id=1, source_target_pairs={{0,8},{1,9},{2,10},{3,11},{4,20},{5,21},{6,22},{7,23},{8,0},{9,1},... | collective-permute-start | bytes 18440 | tf_op jit(solution)/shard_map/ppermute | solution.py:247
  43.9 1.2 %collective-permute-start.18 = (f32[3,8,64]{2,1,0:T(8,128)S(1)}, f32[3,8,64]{2,1,0:T(8,128)S(1)}, u32[]{:S(2)}, u32[]{:S(2)}) collective-permute-start(f32[3,8,64]{2,1,0:T(8,128)S(1)} %add.11), channel_id=1, source_target_pairs={{0,4},{1,5},{2,6},{3,7},{4,0},{5,1},{6,2},{7,3},{8,12},{9,13},{10,... | collective-permute-start | bytes 18440 | tf_op jit(solution)/shard_map/ppermute | solution.py:49
  46.3 6.1 %collective-permute-start.19 = (f16[64,896]{1,0:T(8,128)(2,1)S(1)}, f16[64,896]{1,0:T(8,128)(2,1)S(1)}, u32[]{:S(2)}, u32[]{:S(2)}) collective-permute-start(f16[64,896]{1,0:T(8,128)(2,1)S(1)} %convert_element_type.18), channel_id=1, source_target_pairs={{0,1},{1,0},{2,3},{3,2},{4,5},{5,4},{6,7},{7,6},{8,9},{9,8},{10,11... | collective-permute-start | bytes 344072 | tf_op jit(solution)/shard_map/ppermute | solution.py:49
  46.4 6.0 %collective-permute-start.20 = (f16[64,896]{1,0:T(8,128)(2,1)S(1)}, f16[64,896]{1,0:T(8,128)(2,1)S(1)}, u32[]{:S(2)}, u32[]{:S(2)}) collective-permute-start(f16[64,896]{1,0:T(8,128)(2,1)S(1)} %convert_element_type.20), channel_id=1, source_target_pairs={{0,8},{1,9},{2,10},{3,11},{4,12},{5,13},{6,14},{7,15},{8,0},{9,1},... | collective-permute-start | bytes 344072 | tf_op jit(solution)/shard_map/ppermute | solution.py:49
  47.9 7.0 %collective-permute-start.21 = (f16[64,896]{1,0:T(8,128)(2,1)S(1)}, f16[64,896]{1,0:T(8,128)(2,1)S(1)}, u32[]{:S(2)}, u32[]{:S(2)}) collective-permute-start(f16[64,896]{1,0:T(8,128)(2,1)S(1)} %convert_element_type.22), channel_id=1, source_target_pairs={{0,9},{1,8},{2,11},{3,10},{4,13},{5,12},{6,15},{7,14},{8,1},{9,0},... | collective-permute-start | bytes 344072 | tf_op jit(solution)/shard_map/ppermute | solution.py:49

commit v16 on v15

--- a/solution.py
+++ b/solution.py
@@ -83,7 +83,8 @@
         for b, mask in enumerate(masks):
             if b:
                 side_s[1 << b] = whole(send(late_s, mask, count))
-                side_t[1 << b] = whole(send(late_t, mask, count))
+                if side_t is col_t:
+                    side_t[1 << b] = whole(send(late_t, mask, count))
 
     def long_way(side_s, masks, gate):
         forward(side_s, masks, lambda place: not place & 1)
@@ -95,11 +96,17 @@
             side_s[p | 1] = (got, k * student.shape[1], (k + 1) * student.shape[1])
 
     first = (row_t[1][0], col_t[1][0])
-    long_way(col_s, plane_masks, ())
+    long_way(col_s, plane_masks, row_s[2][0])
     long_way(row_s, row_masks, first)
-    row_t[1], col_t[1] = map(whole, after(first, (row_t[2][0], col_t[2][0])))
-    for side_t, _, masks in reversed(sides):
-        forward(side_t, masks, lambda place: True)
+    row_t[1], col_t[1] = map(whole, after(first, col_t[2][0]))
+    forward(col_t, plane_masks, lambda place: True)
+    for b, mask in enumerate(row_masks):
+        if b:
+            parts = [row_t[p] for p in range(1 << b)]
+            got, start = send(join(*(array[:, i:j] for array, i, j in parts)), mask, count), 0
+            for p, (_, i, j) in enumerate(parts):
+                row_t[p | 1 << b] = (got, start, start + j - i)
+                start += j - i
 
     core_t, core_s = {0: whole(swapped[0])}, {0: whole(swapped[1])}
     ones = [1 << b for b in range(len(plane_masks))]

time: 55.9 us -> 53.5 us (0.957)
  waiting for transfers between devices: 27.4 us -> 25.8 us
  Pallas kernels: 2.84 us -> 3.74 us
  local copies, waits for them, and re-layouts: 2.08 us -> 1.19 us
  starting transfers between devices: 22.4 us -> 21.7 us
    ppermute x20 -> x19, starting transfers between devices: 20.8 us -> 19.6 us  [send(): return lax.ppermute(value, AXES, [(i, i ^ mask) for i in range(count)])]
    ppermute x20 -> x19, waiting for transfers between devices: 21.5 us -> 20.3 us  [send(): return lax.ppermute(value, AXES, [(i, i ^ mask) for i in range(count)])]
    pallas_call x7 -> x8, Pallas kernels: 2.84 us -> 3.74 us  [call(): pl.pallas_call(kernel, out_shape=outputs, **options, compiler_params=pltp...]
    unnamed x6 -> x2, local copies, waits for them, and re-layouts: 1.86 us -> 0.96 us
  transfers between devices with their start and end apart: 22 -> 21, of which waited for: 13 -> 12; matrix products, arithmetic and copies ran while one was open for 0% -> 0% of each run, Pallas kernels for 0% -> 2%
where the time goes in v16:
time: 53.5 us; the launch traced here: 53.4 us
  waiting for transfers between devices  25.8 us (48%)
  starting transfers between devices  21.7 us (41%)
  Pallas kernels  3.74 us (7%)
  local copies, waits for them, and re-layouts  1.19 us (2%)
  between operations  0.79 us (1%)
    ppermute x19, waiting for transfers between devices, send(): return lax.ppermute(value, AXES, [(i, i ^ mask) for i in range(count)])  20.3 us
    ppermute x19, starting transfers between devices, send(): return lax.ppermute(value, AXES, [(i, i ^ mask) for i in range(count)])  19.6 us
    ppermute x2, waiting for transfers between devices, exchange_sums(): got = lax.ppermute(sums, AXES, pairs).reshape(3, -1, 2, 1 << b, rows)  5.45 us
    pallas_call x8, Pallas kernels, call(): pl.pallas_call(kernel, out_shape=outputs, **options, compiler_params=pltp...  3.74 us
    ppermute x2, starting transfers between devices, exchange_sums(): got = lax.ppermute(sums, AXES, pairs).reshape(3, -1, 2, 1 << b, rows)  2.07 us
  transfers between devices with their start and end apart: 21, of which 12 were waited for; matrix products, arithmetic and copies ran while one was open for 0% of the time, Pallas kernels for 2%

profile of v16, /device:TPU:0, one launch (start us, length us, event | category | flops | bytes accessed | tf_op | source)
XLA Modules:
  0.0 53.4 jit_solution(7021190005470780781)
XLA Ops:
  0.6 0.5 collective-permute-start.2
  1.2 3.0 %collective-permute-start = (bf16[64,1536]{1,0:T(8,128)(2,1)}, bf16[64,1536]{1,0:T(8,128)(2,1)S(1)}, u32[]{:S(2)}, u32[]{:S(2)}) collective-permute-start(bf16[64,1536]{1,0:T(8,128)(2,1)} %refs_0_.1), channel_id=1, source_target_pairs={{0,1},{1,0},{2,3},{3,2},{4,5},{5,4},{6,7},{7,6},{8,9},{9,8},{10,11... | collective-permute-start | bytes 589832 | tf_op jit(solution)/shard_map/ppermute | solution.py:49
  4.2 2.6 %collective-permute-start.1 = (bf16[64,1536]{1,0:T(8,128)(2,1)}, bf16[64,1536]{1,0:T(8,128)(2,1)S(1)}, u32[]{:S(2)}, u32[]{:S(2)}) collective-permute-start(bf16[64,1536]{1,0:T(8,128)(2,1)} %refs_0_.1), channel_id=1, source_target_pairs={{0,2},{1,3},{2,0},{3,1},{4,6},{5,7},{6,4},{7,5},{8,10},{9,11},{10,... | collective-permute-start | bytes 589832 | tf_op jit(solution)/shard_map/ppermute | solution.py:49
  6.8 1.0 %copy-done = bf16[64,1536]{1,0:T(8,128)(2,1)S(1)} copy-done((bf16[64,1536]{1,0:T(8,128)(2,1)S(1)}, bf16[64,1536]{1,0:T(8,128)(2,1)}, u32[]{:S(2)}) %copy-start) | copy-done | bytes 196632
  7.8 0.9 %shard_map.41.refs_0_ = bf16[64,2304]{1,0:T(8,128)(2,1)S(1)} custom-call(bf16[64,1536]{1,0:T(8,128)(2,1)S(1)} %copy-done, bf16[64,768]{1,0:T(8,128)(2,1)} %refs_1_.1), custom_call_target="tpu_custom_call" | custom-call | bytes 589824 | tf_op jit(solution)/shard_map/pallas_call | solution.py:185
  8.7 1.6 %collective-permute-start.4 = (bf16[64,1536]{1,0:T(8,128)(2,1)S(1)}, bf16[64,1536]{1,0:T(8,128)(2,1)S(1)}, u32[]{:S(2)}, u32[]{:S(2)}) collective-permute-start(bf16[64,1536]{1,0:T(8,128)(2,1)S(1)} %copy-done), channel_id=1, source_target_pairs={{0,16},{1,17},{2,18},{3,19},{4,20},{5,21},{6,22},{7,23},{8,24},{9,... | collective-permute-start | bytes 589832 | tf_op jit(solution)/shard_map/ppermute | solution.py:49
  10.3 0.5 collective-permute-start.9
  10.8 1.5 %collective-permute-start.6 = (bf16[64,768]{1,0:T(8,128)(2,1)}, bf16[64,768]{1,0:T(8,128)(2,1)S(1)}, u32[]{:S(2)}, u32[]{:S(2)}) collective-permute-start(bf16[64,768]{1,0:T(8,128)(2,1)} %refs_1_.1), channel_id=1, source_target_pairs={{0,8},{1,9},{2,10},{3,11},{4,12},{5,13},{6,14},{7,15},{8,0},{9,1},... | collective-permute-start | bytes 294920 | tf_op jit(solution)/shard_map/ppermute | solution.py:49
  12.3 1.4 %collective-permute-done.refs_1_ = bf16[64,1536]{1,0:T(8,128)(2,1)S(1)} collective-permute-done((bf16[64,1536]{1,0:T(8,128)(2,1)}, bf16[64,1536]{1,0:T(8,128)(2,1)S(1)}, u32[]{:S(2)}, u32[]{:S(2)}) %collective-permute-start) | collective-permute-done | bytes 196640 | tf_op jit(solution)/shard_map/ppermute | solution.py:49
  13.7 2.6 %collective-permute-done.1.refs_0_.refs_5_ = bf16[64,1536]{1,0:T(8,128)(2,1)S(1)} collective-permute-done((bf16[64,1536]{1,0:T(8,128)(2,1)}, bf16[64,1536]{1,0:T(8,128)(2,1)S(1)}, u32[]{:S(2)}, u32[]{:S(2)}) %collective-permute-start.1) | collective-permute-done | bytes 196640 | tf_op jit(solution)/shard_map/ppermute | solution.py:49
  16.2 1.0 %collective-permute-done.9.refs_2_.refs_1_.refs_12_ = bf16[64,768]{1,0:T(8,128)(2,1)S(1)} collective-permute-done((bf16[64,768]{1,0:T(8,128)(2,1)}, bf16[64,768]{1,0:T(8,128)(2,1)S(1)}, u32[]{:S(2)}, u32[]{:S(2)}) %collective-permute-start.9) | collective-permute-done | bytes 98336 | tf_op jit(solution)/shard_map/ppermute | solution.py:49
  17.8 1.5 %collective-permute-start.8 = (bf16[64,1536]{1,0:T(8,128)(2,1)S(1)}, bf16[64,1536]{1,0:T(8,128)(2,1)S(1)}, u32[]{:S(2)}, u32[]{:S(2)}) collective-permute-start(bf16[64,1536]{1,0:T(8,128)(2,1)S(1)} %collective-permute-done.1.refs_0_.refs_5_), channel_id=1, source_target_pairs={{0,16},{1,17},{2,18},{3,19},{4,20},{5,21},{6,22},{7,23},{8,24},{9,... | collective-permute-start | bytes 589832 | tf_op jit(solution)/shard_map/ppermute | solution.py:49
  19.4 1.6 %collective-permute-start.5 = (bf16[64,3072]{1,0:T(8,128)(2,1)S(1)}, bf16[64,3072]{1,0:T(8,128)(2,1)S(1)}, u32[]{:S(2)}, u32[]{:S(2)}) collective-permute-start(bf16[64,3072]{1,0:T(8,128)(2,1)S(1)} %shard_map.42), channel_id=1, source_target_pairs={{0,8},{1,9},{2,10},{3,11},{4,12},{5,13},{6,14},{7,15},{8,0},{9,1},... | collective-permute-start | bytes 1179656 | tf_op jit(solution)/shard_map/ppermute | solution.py:49
  20.9 1.7 %collective-permute-start.7 = (bf16[64,1536]{1,0:T(8,128)(2,1)S(1)}, bf16[64,1536]{1,0:T(8,128)(2,1)S(1)}, u32[]{:S(2)}, u32[]{:S(2)}) collective-permute-start(bf16[64,1536]{1,0:T(8,128)(2,1)S(1)} %shard_map.43), channel_id=1, source_target_pairs={{0,1},{1,0},{2,3},{3,2},{4,5},{5,4},{6,7},{7,6},{8,9},{9,8},{10,11... | collective-permute-start | bytes 589832 | tf_op jit(solution)/shard_map/ppermute | solution.py:49
  22.7 7.2 %collective-permute-done.12.refs_11_.refs_1_ = bf16[64,1536]{1,0:T(8,128)(2,1)S(1)} collective-permute-done((bf16[64,1536]{1,0:T(8,128)(2,1)S(1)}, bf16[64,1536]{1,0:T(8,128)(2,1)S(1)}, u32[]{:S(2)}, u32[]{:S(2)}) %collective-permute-start.12) | collective-permute-done | bytes 196640 | tf_op jit(solution)/shard_map/ppermute | solution.py:49
  29.9 0.5 collective-permute-start.11
  30.4 1.2 %collective-permute-done.7.refs_3_ = bf16[64,1536]{1,0:T(8,128)(2,1)S(1)} collective-permute-done((bf16[64,1536]{1,0:T(8,128)(2,1)S(1)}, bf16[64,1536]{1,0:T(8,128)(2,1)S(1)}, u32[]{:S(2)}, u32[]{:S(2)}) %collective-permute-start.7) | collective-permute-done | bytes 196640 | tf_op jit(solution)/shard_map/ppermute | solution.py:49
  31.6 1.0 %shard_map.46 = (f32[256,512]{1,0:T(8,128)S(1)}, f32[256,512]{1,0:T(8,128)S(1)}, f32[3,4,64]{2,1,0:T(4,128)S(1)}, f32[3,8,64]{2,1,0:T(8,128)S(1)}) custom-call(bf16[64,2304]{1,0:T(8,128)(2,1)S(1)} %shard_map.41.refs_0_, bf16[64,1536]{1,0:T(8,128)(2,1)S(1)} %collective-permute-done.refs_1_, bf16[64,3072]{1,0:T(8,128)(2,1)S(1)} %collective-permute-done.5.refs_2_, ...), custom_call_target="tpu_custom_call" | custom-call | flops 603979776 | bytes 4301824 | tf_op jit(solution)/shard_map/pallas_call | solution.py:185
  32.9 1.0 %collective-permute-done.14 = f32[3,12,64]{2,1,0:T(8,128)S(1)} collective-permute-done((f32[3,12,64]{2,1,0:T(8,128)S(1)}, f32[3,12,64]{2,1,0:T(8,128)S(1)}, u32[]{:S(2)}, u32[]{:S(2)}) %collective-permute-start.14) | collective-permute-done | bytes 9248 | tf_op jit(solution)/shard_map/ppermute | solution.py:49
  33.9 0.5 %collective-permute-start.15 = (f32[3,8,64]{2,1,0:T(8,128)S(1)}, f32[3,8,64]{2,1,0:T(8,128)S(1)}, u32[]{:S(2)}, u32[]{:S(2)}) collective-permute-start(f32[3,8,64]{2,1,0:T(8,128)S(1)} %maximum_select_fusion), channel_id=1, source_target_pairs={{0,1},{1,0},{2,3},{3,2},{4,6},{5,7},{6,4},{7,5},{8,9},{9,8},{10,11... | collective-permute-start | bytes 18440 | tf_op jit(solution)/shard_map/ppermute | solution.py:254
  34.5 3.2 %collective-permute-done.15 = f32[3,8,64]{2,1,0:T(8,128)S(1)} collective-permute-done((f32[3,8,64]{2,1,0:T(8,128)S(1)}, f32[3,8,64]{2,1,0:T(8,128)S(1)}, u32[]{:S(2)}, u32[]{:S(2)}) %collective-permute-start.15) | collective-permute-done | bytes 6176 | tf_op jit(solution)/shard_map/ppermute | solution.py:254
  37.8 1.5 %collective-permute-start.16 = (f32[3,8,64]{2,1,0:T(8,128)S(1)}, f32[3,8,64]{2,1,0:T(8,128)S(1)}, u32[]{:S(2)}, u32[]{:S(2)}) collective-permute-start(f32[3,8,64]{2,1,0:T(8,128)S(1)} %add.10), channel_id=1, source_target_pairs={{0,8},{1,9},{2,10},{3,11},{4,20},{5,21},{6,22},{7,23},{8,0},{9,1},... | collective-permute-start | bytes 18440 | tf_op jit(solution)/shard_map/ppermute | solution.py:254
  39.3 2.2 %collective-permute-done.16 = f32[3,8,64]{2,1,0:T(8,128)S(1)} collective-permute-done((f32[3,8,64]{2,1,0:T(8,128)S(1)}, f32[3,8,64]{2,1,0:T(8,128)S(1)}, u32[]{:S(2)}, u32[]{:S(2)}) %collective-permute-start.16) | collective-permute-done | bytes 6176 | tf_op jit(solution)/shard_map/ppermute | solution.py:254
  41.6 1.2 %collective-permute-done.17 = f32[3,8,64]{2,1,0:T(8,128)S(1)} collective-permute-done((f32[3,8,64]{2,1,0:T(8,128)S(1)}, f32[3,8,64]{2,1,0:T(8,128)S(1)}, u32[]{:S(2)}, u32[]{:S(2)}) %collective-permute-start.17) | collective-permute-done | bytes 6176 | tf_op jit(solution)/shard_map/ppermute | solution.py:49
  43.0 0.9 %shard_map.47 = (f32[64,768]{1,0:T(8,128)S(1)}, f32[8,128]{1,0:T(8,128)S(1)}, f32[64,896]{1,0:T(8,128)S(1)}, f32[64,896]{1,0:T(8,128)S(1)}, f32[64,896]{1,0:T(8,128)S(1)}) custom-call(f32[256,512]{1,0:T(8,128)S(1)} %get-tuple-element.25.gram_s, f32[256,512]{1,0:T(8,128)S(1)} %get-tuple-element.26.gram_t, f32[3,1,256]{2,1,0:T(1,128)S(1)} %reshape.26.row_sum, ...), custom_call_target="tpu_custom_call" | custom-call | flops 402653184 | bytes 3322880 | tf_op jit(solution)/shard_map/pallas_call | solution.py:185
  43.9 0.6 %collective-permute-start.18 = (f16[64,896]{1,0:T(8,128)(2,1)S(1)}, f16[64,896]{1,0:T(8,128)(2,1)S(1)}, u32[]{:S(2)}, u32[]{:S(2)}) collective-permute-start(f16[64,896]{1,0:T(8,128)(2,1)S(1)} %convert_element_type.18), channel_id=1, source_target_pairs={{0,1},{1,0},{2,3},{3,2},{4,5},{5,4},{6,7},{7,6},{8,9},{9,8},{10,11... | collective-permute-start | bytes 344072 | tf_op jit(solution)/shard_map/ppermute | solution.py:49
  44.5 1.6 %collective-permute-start.19 = (f16[64,896]{1,0:T(8,128)(2,1)S(1)}, f16[64,896]{1,0:T(8,128)(2,1)S(1)}, u32[]{:S(2)}, u32[]{:S(2)}) collective-permute-start(f16[64,896]{1,0:T(8,128)(2,1)S(1)} %convert_element_type.20), channel_id=1, source_target_pairs={{0,8},{1,9},{2,10},{3,11},{4,12},{5,13},{6,14},{7,15},{8,0},{9,1},... | collective-permute-start | bytes 344072 | tf_op jit(solution)/shard_map/ppermute | solution.py:49
  46.1 1.6 %collective-permute-start.20 = (f16[64,896]{1,0:T(8,128)(2,1)S(1)}, f16[64,896]{1,0:T(8,128)(2,1)S(1)}, u32[]{:S(2)}, u32[]{:S(2)}) collective-permute-start(f16[64,896]{1,0:T(8,128)(2,1)S(1)} %convert_element_type.22), channel_id=1, source_target_pairs={{0,9},{1,8},{2,11},{3,10},{4,13},{5,12},{6,15},{7,14},{8,1},{9,0},... | collective-permute-start | bytes 344072 | tf_op jit(solution)/shard_map/ppermute | solution.py:49
  47.6 2.3 %collective-permute-done.18 = f16[64,896]{1,0:T(8,128)(2,1)S(1)} collective-permute-done((f16[64,896]{1,0:T(8,128)(2,1)S(1)}, f16[64,896]{1,0:T(8,128)(2,1)S(1)}, u32[]{:S(2)}, u32[]{:S(2)}) %collective-permute-start.18) | collective-permute-done | bytes 114720 | tf_op jit(solution)/shard_map/ppermute | solution.py:49
  50.0 1.0 %collective-permute-done.19 = f16[64,896]{1,0:T(8,128)(2,1)S(1)} collective-permute-done((f16[64,896]{1,0:T(8,128)(2,1)S(1)}, f16[64,896]{1,0:T(8,128)(2,1)S(1)}, u32[]{:S(2)}, u32[]{:S(2)}) %collective-permute-start.19) | collective-permute-done | bytes 114720 | tf_op jit(solution)/shard_map/ppermute | solution.py:49
  51.0 1.5 %collective-permute-done.20 = f16[64,896]{1,0:T(8,128)(2,1)S(1)} collective-permute-done((f16[64,896]{1,0:T(8,128)(2,1)S(1)}, f16[64,896]{1,0:T(8,128)(2,1)S(1)}, u32[]{:S(2)}, u32[]{:S(2)}) %collective-permute-start.20) | collective-permute-done | bytes 114720 | tf_op jit(solution)/shard_map/ppermute | solution.py:49
  52.5 0.8 %shard_map.48 = (f32[64,768]{1,0:T(8,128)}, f32[1,1]{1,0:T(1,128)}) custom-call(f32[64,768]{1,0:T(8,128)S(1)} %get-tuple-element.29.own, f32[8,128]{1,0:T(8,128)S(1)} %get-tuple-element.30.share, f32[64,896]{1,0:T(8,128)S(1)} %convert_element_type.19.refs_0_, f32[64,896]{1,0:T(8,128)S(1)} %convert_element_type.21.refs_1_, ...), custom_call_target="tpu_custom_call" | custom-call | bytes 1085444 | tf_op jit(solution)/shard_map/pallas_call | solution.py:185
  (39 shorter events, 1.4 us)
Async XLA Ops:
  0.6 8.1 %collective-permute-start.2 = (bf16[64,1536]{1,0:T(8,128)(2,1)}, bf16[64,1536]{1,0:T(8,128)(2,1)S(1)}, u32[]{:S(2)}, u32[]{:S(2)}) collective-permute-start(bf16[64,1536]{1,0:T(8,128)(2,1)} %refs_0_.1), channel_id=1, source_target_pairs={{0,4},{1,5},{2,6},{3,7},{4,0},{5,1},{6,2},{7,3},{8,12},{9,13},{10,... | collective-permute-start | bytes 589832 | tf_op jit(solution)/shard_map/ppermute | solution.py:49
  1.1 7.5 %collective-permute-start.3 = (bf16[64,768]{1,0:T(8,128)(2,1)}, bf16[64,768]{1,0:T(8,128)(2,1)S(1)}, u32[]{:S(2)}, u32[]{:S(2)}) collective-permute-start(bf16[64,768]{1,0:T(8,128)(2,1)} %refs_1_.1), channel_id=1, source_target_pairs={{0,4},{1,5},{2,6},{3,7},{4,0},{5,1},{6,2},{7,3},{8,12},{9,13},{10,... | collective-permute-start | bytes 294920 | tf_op jit(solution)/shard_map/ppermute | solution.py:49
  1.2 12.4 %collective-permute-start = (bf16[64,1536]{1,0:T(8,128)(2,1)}, bf16[64,1536]{1,0:T(8,128)(2,1)S(1)}, u32[]{:S(2)}, u32[]{:S(2)}) collective-permute-start(bf16[64,1536]{1,0:T(8,128)(2,1)} %refs_0_.1), channel_id=1, source_target_pairs={{0,1},{1,0},{2,3},{3,2},{4,5},{5,4},{6,7},{7,6},{8,9},{9,8},{10,11... | collective-permute-start | bytes 589832 | tf_op jit(solution)/shard_map/ppermute | solution.py:49
  4.2 12.0 %collective-permute-start.1 = (bf16[64,1536]{1,0:T(8,128)(2,1)}, bf16[64,1536]{1,0:T(8,128)(2,1)S(1)}, u32[]{:S(2)}, u32[]{:S(2)}) collective-permute-start(bf16[64,1536]{1,0:T(8,128)(2,1)} %refs_0_.1), channel_id=1, source_target_pairs={{0,2},{1,3},{2,0},{3,1},{4,6},{5,7},{6,4},{7,5},{8,10},{9,11},{10,... | collective-permute-start | bytes 589832 | tf_op jit(solution)/shard_map/ppermute | solution.py:49
  6.8 1.0 %copy-start = (bf16[64,1536]{1,0:T(8,128)(2,1)S(1)}, bf16[64,1536]{1,0:T(8,128)(2,1)}, u32[]{:S(2)}) copy-start(bf16[64,1536]{1,0:T(8,128)(2,1)} %refs_0_.1) | copy-start | bytes 589828
  8.7 7.5 %collective-permute-start.4 = (bf16[64,1536]{1,0:T(8,128)(2,1)S(1)}, bf16[64,1536]{1,0:T(8,128)(2,1)S(1)}, u32[]{:S(2)}, u32[]{:S(2)}) collective-permute-start(bf16[64,1536]{1,0:T(8,128)(2,1)S(1)} %copy-done), channel_id=1, source_target_pairs={{0,16},{1,17},{2,18},{3,19},{4,20},{5,21},{6,22},{7,23},{8,24},{9,... | collective-permute-start | bytes 589832 | tf_op jit(solution)/shard_map/ppermute | solution.py:49
  10.3 6.9 %collective-permute-start.9 = (bf16[64,768]{1,0:T(8,128)(2,1)}, bf16[64,768]{1,0:T(8,128)(2,1)S(1)}, u32[]{:S(2)}, u32[]{:S(2)}) collective-permute-start(bf16[64,768]{1,0:T(8,128)(2,1)} %refs_1_.1), channel_id=1, source_target_pairs={{0,16},{1,17},{2,18},{3,19},{4,20},{5,21},{6,22},{7,23},{8,24},{9,... | collective-permute-start | bytes 294920 | tf_op jit(solution)/shard_map/ppermute | solution.py:49
  10.8 6.6 %collective-permute-start.6 = (bf16[64,768]{1,0:T(8,128)(2,1)}, bf16[64,768]{1,0:T(8,128)(2,1)S(1)}, u32[]{:S(2)}, u32[]{:S(2)}) collective-permute-start(bf16[64,768]{1,0:T(8,128)(2,1)} %refs_1_.1), channel_id=1, source_target_pairs={{0,8},{1,9},{2,10},{3,11},{4,12},{5,13},{6,14},{7,15},{8,0},{9,1},... | collective-permute-start | bytes 294920 | tf_op jit(solution)/shard_map/ppermute | solution.py:49
  17.2 14.3 %collective-permute-start.10 = (bf16[64,3840]{1,0:T(8,128)(2,1)S(1)}, bf16[64,3840]{1,0:T(8,128)(2,1)S(1)}, u32[]{:S(2)}, u32[]{:S(2)}) collective-permute-start(bf16[64,3840]{1,0:T(8,128)(2,1)S(1)} %shard_map.44), channel_id=1, source_target_pairs={{0,4},{1,5},{2,6},{3,7},{4,0},{5,1},{6,2},{7,3},{8,12},{9,13},{10,... | collective-permute-start | bytes 1474568 | tf_op jit(solution)/shard_map/ppermute | solution.py:49
  17.4 12.5 %collective-permute-start.12 = (bf16[64,1536]{1,0:T(8,128)(2,1)S(1)}, bf16[64,1536]{1,0:T(8,128)(2,1)S(1)}, u32[]{:S(2)}, u32[]{:S(2)}) collective-permute-start(bf16[64,1536]{1,0:T(8,128)(2,1)S(1)} %shard_map.45), channel_id=1, source_target_pairs={{0,2},{1,3},{2,0},{3,1},{4,6},{5,7},{6,4},{7,5},{8,10},{9,11},{10,... | collective-permute-start | bytes 589832 | tf_op jit(solution)/shard_map/ppermute | solution.py:49
  17.8 12.1 %collective-permute-start.8 = (bf16[64,1536]{1,0:T(8,128)(2,1)S(1)}, bf16[64,1536]{1,0:T(8,128)(2,1)S(1)}, u32[]{:S(2)}, u32[]{:S(2)}) collective-permute-start(bf16[64,1536]{1,0:T(8,128)(2,1)S(1)} %collective-permute-done.1.refs_0_.refs_5_), channel_id=1, source_target_pairs={{0,16},{1,17},{2,18},{3,19},{4,20},{5,21},{6,22},{7,23},{8,24},{9,... | collective-permute-start | bytes 589832 | tf_op jit(solution)/shard_map/ppermute | solution.py:49
  19.4 12.2 %collective-permute-start.5 = (bf16[64,3072]{1,0:T(8,128)(2,1)S(1)}, bf16[64,3072]{1,0:T(8,128)(2,1)S(1)}, u32[]{:S(2)}, u32[]{:S(2)}) collective-permute-start(bf16[64,3072]{1,0:T(8,128)(2,1)S(1)} %shard_map.42), channel_id=1, source_target_pairs={{0,8},{1,9},{2,10},{3,11},{4,12},{5,13},{6,14},{7,15},{8,0},{9,1},... | collective-permute-start | bytes 1179656 | tf_op jit(solution)/shard_map/ppermute | solution.py:49
  20.9 10.6 %collective-permute-start.7 = (bf16[64,1536]{1,0:T(8,128)(2,1)S(1)}, bf16[64,1536]{1,0:T(8,128)(2,1)S(1)}, u32[]{:S(2)}, u32[]{:S(2)}) collective-permute-start(bf16[64,1536]{1,0:T(8,128)(2,1)S(1)} %shard_map.43), channel_id=1, source_target_pairs={{0,1},{1,0},{2,3},{3,2},{4,5},{5,4},{6,7},{7,6},{8,9},{9,8},{10,11... | collective-permute-start | bytes 589832 | tf_op jit(solution)/shard_map/ppermute | solution.py:49
  29.9 1.7 %collective-permute-start.13 = (bf16[64,1536]{1,0:T(8,128)(2,1)S(1)}, bf16[64,1536]{1,0:T(8,128)(2,1)S(1)}, u32[]{:S(2)}, u32[]{:S(2)}) collective-permute-start(bf16[64,1536]{1,0:T(8,128)(2,1)S(1)} %collective-permute-done.12.refs_11_.refs_1_), channel_id=1, source_target_pairs={{0,4},{1,5},{2,6},{3,7},{4,0},{5,1},{6,2},{7,3},{8,12},{9,13},{10,... | collective-permute-start | bytes 589832 | tf_op jit(solution)/shard_map/ppermute | solution.py:49
  29.9 1.7 %collective-permute-start.11 = (bf16[64,1536]{1,0:T(8,128)(2,1)S(1)}, bf16[64,1536]{1,0:T(8,128)(2,1)S(1)}, u32[]{:S(2)}, u32[]{:S(2)}) collective-permute-start(bf16[64,1536]{1,0:T(8,128)(2,1)S(1)} %collective-permute-done.8.refs_7_), channel_id=1, source_target_pairs={{0,4},{1,5},{2,6},{3,7},{4,0},{5,1},{6,2},{7,3},{8,12},{9,13},{10,... | collective-permute-start | bytes 589832 | tf_op jit(solution)/shard_map/ppermute | solution.py:49
  32.7 1.3 %collective-permute-start.14 = (f32[3,12,64]{2,1,0:T(8,128)S(1)}, f32[3,12,64]{2,1,0:T(8,128)S(1)}, u32[]{:S(2)}, u32[]{:S(2)}) collective-permute-start(f32[3,12,64]{2,1,0:T(8,128)S(1)} %pad_maximum_fusion), channel_id=1, source_target_pairs={{0,4},{1,5},{2,6},{3,7},{4,0},{5,1},{6,2},{7,3},{8,12},{9,13},{10,... | collective-permute-start | bytes 27656 | tf_op jit(solution)/shard_map/ppermute | solution.py:49
  33.9 3.8 %collective-permute-start.15 = (f32[3,8,64]{2,1,0:T(8,128)S(1)}, f32[3,8,64]{2,1,0:T(8,128)S(1)}, u32[]{:S(2)}, u32[]{:S(2)}) collective-permute-start(f32[3,8,64]{2,1,0:T(8,128)S(1)} %maximum_select_fusion), channel_id=1, source_target_pairs={{0,1},{1,0},{2,3},{3,2},{4,6},{5,7},{6,4},{7,5},{8,9},{9,8},{10,11... | collective-permute-start | bytes 18440 | tf_op jit(solution)/shard_map/ppermute | solution.py:254
  37.8 3.8 %collective-permute-start.16 = (f32[3,8,64]{2,1,0:T(8,128)S(1)}, f32[3,8,64]{2,1,0:T(8,128)S(1)}, u32[]{:S(2)}, u32[]{:S(2)}) collective-permute-start(f32[3,8,64]{2,1,0:T(8,128)S(1)} %add.10), channel_id=1, source_target_pairs={{0,8},{1,9},{2,10},{3,11},{4,20},{5,21},{6,22},{7,23},{8,0},{9,1},... | collective-permute-start | bytes 18440 | tf_op jit(solution)/shard_map/ppermute | solution.py:254
  41.5 1.2 %collective-permute-start.17 = (f32[3,8,64]{2,1,0:T(8,128)S(1)}, f32[3,8,64]{2,1,0:T(8,128)S(1)}, u32[]{:S(2)}, u32[]{:S(2)}) collective-permute-start(f32[3,8,64]{2,1,0:T(8,128)S(1)} %add.11), channel_id=1, source_target_pairs={{0,4},{1,5},{2,6},{3,7},{4,0},{5,1},{6,2},{7,3},{8,12},{9,13},{10,... | collective-permute-start | bytes 18440 | tf_op jit(solution)/shard_map/ppermute | solution.py:49
  43.9 6.1 %collective-permute-start.18 = (f16[64,896]{1,0:T(8,128)(2,1)S(1)}, f16[64,896]{1,0:T(8,128)(2,1)S(1)}, u32[]{:S(2)}, u32[]{:S(2)}) collective-permute-start(f16[64,896]{1,0:T(8,128)(2,1)S(1)} %convert_element_type.18), channel_id=1, source_target_pairs={{0,1},{1,0},{2,3},{3,2},{4,5},{5,4},{6,7},{7,6},{8,9},{9,8},{10,11... | collective-permute-start | bytes 344072 | tf_op jit(solution)/shard_map/ppermute | solution.py:49
  44.5 6.5 %collective-permute-start.19 = (f16[64,896]{1,0:T(8,128)(2,1)S(1)}, f16[64,896]{1,0:T(8,128)(2,1)S(1)}, u32[]{:S(2)}, u32[]{:S(2)}) collective-permute-start(f16[64,896]{1,0:T(8,128)(2,1)S(1)} %convert_element_type.20), channel_id=1, source_target_pairs={{0,8},{1,9},{2,10},{3,11},{4,12},{5,13},{6,14},{7,15},{8,0},{9,1},... | collective-permute-start | bytes 344072 | tf_op jit(solution)/shard_map/ppermute | solution.py:49
  46.1 6.5 %collective-permute-start.20 = (f16[64,896]{1,0:T(8,128)(2,1)S(1)}, f16[64,896]{1,0:T(8,128)(2,1)S(1)}, u32[]{:S(2)}, u32[]{:S(2)}) collective-permute-start(f16[64,896]{1,0:T(8,128)(2,1)S(1)} %convert_element_type.22), channel_id=1, source_target_pairs={{0,9},{1,8},{2,11},{3,10},{4,13},{5,12},{6,15},{7,14},{8,1},{9,0},... | collective-permute-start | bytes 344072 | tf_op jit(solution)/shard_map/ppermute | solution.py:49

commit v17 on v16

--- a/solution.py
+++ b/solution.py
@@ -77,7 +77,7 @@
         side_t[1] = whole(send(teacher, masks[0], count))
     swapped = [send(value, core_mask, count) for value in (teacher, student)]
     own = join(teacher, student)
-    late_t, late_s = after((teacher, student), (*swapped, own))
+    late_t, late_s = after((teacher, student), swapped)
     for side_t, side_s, masks in reversed(sides):
         side_t[0] = (own, 0, teacher.shape[1])
         for b, mask in enumerate(masks):

time: 53.5 us -> 53 us (level)
  waiting for transfers between devices: 25.8 us -> 27.2 us
  local copies, waits for them, and re-layouts: 1.19 us -> 0.24 us
  Pallas kernels: 3.74 us -> 2.85 us
    unnamed x2 -> x4, local copies, waits for them, and re-layouts: 0.96 us -> 0.01 us
    pallas_call x8, Pallas kernels: 3.74 us -> 2.85 us  [call(): pl.pallas_call(kernel, out_shape=outputs, **options, compiler_params=pltp...]
    ppermute x2, starting transfers between devices: 2.07 us -> 1.2 us  [exchange_sums(): got = lax.ppermute(sums, AXES, pairs).reshape(3, -1, 2, 1 << b, rows)]
    ppermute x2, waiting for transfers between devices: 5.45 us -> 6.32 us  [exchange_sums(): got = lax.ppermute(sums, AXES, pairs).reshape(3, -1, 2, 1 << b, rows)]
    ppermute x19, starting transfers between devices: 19.6 us -> 20.3 us  [send(): return lax.ppermute(value, AXES, [(i, i ^ mask) for i in range(count)])]
    ppermute x19, waiting for transfers between devices: 20.3 us -> 20.9 us  [send(): return lax.ppermute(value, AXES, [(i, i ^ mask) for i in range(count)])]
  transfers between devices with their start and end apart: 21 -> 21, of which waited for: 12 -> 10; matrix products, arithmetic and copies ran while one was open for 0% -> 0% of each run, Pallas kernels for 2% -> 0%
where the time goes in v17:
time: 53 us; the launch traced here: 52.8 us
  waiting for transfers between devices  27.2 us (51%)
  starting transfers between devices  21.5 us (41%)
  Pallas kernels  2.85 us (5%)
  between operations  0.84 us (2%)
    ppermute x19, waiting for transfers between devices, send(): return lax.ppermute(value, AXES, [(i, i ^ mask) for i in range(count)])  20.9 us
    ppermute x19, starting transfers between devices, send(): return lax.ppermute(value, AXES, [(i, i ^ mask) for i in range(count)])  20.3 us
    ppermute x2, waiting for transfers between devices, exchange_sums(): got = lax.ppermute(sums, AXES, pairs).reshape(3, -1, 2, 1 << b, rows)  6.32 us
    pallas_call x8, Pallas kernels, call(): pl.pallas_call(kernel, out_shape=outputs, **options, compiler_params=pltp...  2.85 us
    ppermute x2, starting transfers between devices, exchange_sums(): got = lax.ppermute(sums, AXES, pairs).reshape(3, -1, 2, 1 << b, rows)  1.2 us
  transfers between devices with their start and end apart: 21, of which 10 were waited for; matrix products, arithmetic and copies ran while one was open for 0% of the time, Pallas kernels for 0%

profile of v17, /device:TPU:0, one launch (start us, length us, event | category | flops | bytes accessed | tf_op | source)
XLA Modules:
  0.0 52.8 jit_solution(1047696558361252720)
XLA Ops:
  0.6 0.5 collective-permute-start.2
  1.2 0.1 collective-permute-start.3
  1.2 3.0 %collective-permute-start = (bf16[64,1536]{1,0:T(8,128)(2,1)}, bf16[64,1536]{1,0:T(8,128)(2,1)S(1)}, u32[]{:S(2)}, u32[]{:S(2)}) collective-permute-start(bf16[64,1536]{1,0:T(8,128)(2,1)} %refs_0_.1), channel_id=1, source_target_pairs={{0,1},{1,0},{2,3},{3,2},{4,5},{5,4},{6,7},{7,6},{8,9},{9,8},{10,11... | collective-permute-start | bytes 589832 | tf_op jit(solution)/shard_map/ppermute | solution.py:49
  4.2 2.6 %collective-permute-start.1 = (bf16[64,1536]{1,0:T(8,128)(2,1)}, bf16[64,1536]{1,0:T(8,128)(2,1)S(1)}, u32[]{:S(2)}, u32[]{:S(2)}) collective-permute-start(bf16[64,1536]{1,0:T(8,128)(2,1)} %refs_0_.1), channel_id=1, source_target_pairs={{0,2},{1,3},{2,0},{3,1},{4,6},{5,7},{6,4},{7,5},{8,10},{9,11},{10,... | collective-permute-start | bytes 589832 | tf_op jit(solution)/shard_map/ppermute | solution.py:49
  6.8 1.5 %collective-permute-start.4 = (bf16[64,1536]{1,0:T(8,128)(2,1)}, bf16[64,1536]{1,0:T(8,128)(2,1)S(1)}, u32[]{:S(2)}, u32[]{:S(2)}) collective-permute-start(bf16[64,1536]{1,0:T(8,128)(2,1)} %refs_0_.1), channel_id=1, source_target_pairs={{0,16},{1,17},{2,18},{3,19},{4,20},{5,21},{6,22},{7,23},{8,24},{9,... | collective-permute-start | bytes 589832 | tf_op jit(solution)/shard_map/ppermute | solution.py:49
  8.4 0.5 collective-permute-start.9
  8.9 1.5 %collective-permute-start.6 = (bf16[64,768]{1,0:T(8,128)(2,1)}, bf16[64,768]{1,0:T(8,128)(2,1)S(1)}, u32[]{:S(2)}, u32[]{:S(2)}) collective-permute-start(bf16[64,768]{1,0:T(8,128)(2,1)} %refs_1_.1), channel_id=1, source_target_pairs={{0,8},{1,9},{2,10},{3,11},{4,12},{5,13},{6,14},{7,15},{8,0},{9,1},... | collective-permute-start | bytes 294920 | tf_op jit(solution)/shard_map/ppermute | solution.py:49
  10.4 3.3 %collective-permute-done.refs_1_ = bf16[64,1536]{1,0:T(8,128)(2,1)S(1)} collective-permute-done((bf16[64,1536]{1,0:T(8,128)(2,1)}, bf16[64,1536]{1,0:T(8,128)(2,1)S(1)}, u32[]{:S(2)}, u32[]{:S(2)}) %collective-permute-start) | collective-permute-done | bytes 196640 | tf_op jit(solution)/shard_map/ppermute | solution.py:49
  13.7 2.6 %collective-permute-done.1.refs_0_.refs_5_ = bf16[64,1536]{1,0:T(8,128)(2,1)S(1)} collective-permute-done((bf16[64,1536]{1,0:T(8,128)(2,1)}, bf16[64,1536]{1,0:T(8,128)(2,1)S(1)}, u32[]{:S(2)}, u32[]{:S(2)}) %collective-permute-start.1) | collective-permute-done | bytes 196640 | tf_op jit(solution)/shard_map/ppermute | solution.py:49
  16.5 0.4 collective-permute-start.12
  16.9 1.5 %collective-permute-start.8 = (bf16[64,1536]{1,0:T(8,128)(2,1)S(1)}, bf16[64,1536]{1,0:T(8,128)(2,1)S(1)}, u32[]{:S(2)}, u32[]{:S(2)}) collective-permute-start(bf16[64,1536]{1,0:T(8,128)(2,1)S(1)} %collective-permute-done.1.refs_0_.refs_5_), channel_id=1, source_target_pairs={{0,16},{1,17},{2,18},{3,19},{4,20},{5,21},{6,22},{7,23},{8,24},{9,... | collective-permute-start | bytes 589832 | tf_op jit(solution)/shard_map/ppermute | solution.py:49
  18.4 1.6 %collective-permute-start.5 = (bf16[64,3072]{1,0:T(8,128)(2,1)S(1)}, bf16[64,3072]{1,0:T(8,128)(2,1)S(1)}, u32[]{:S(2)}, u32[]{:S(2)}) collective-permute-start(bf16[64,3072]{1,0:T(8,128)(2,1)S(1)} %shard_map.42), channel_id=1, source_target_pairs={{0,8},{1,9},{2,10},{3,11},{4,12},{5,13},{6,14},{7,15},{8,0},{9,1},... | collective-permute-start | bytes 1179656 | tf_op jit(solution)/shard_map/ppermute | solution.py:49
  20.0 2.8 %collective-permute-start.7 = (bf16[64,1536]{1,0:T(8,128)(2,1)S(1)}, bf16[64,1536]{1,0:T(8,128)(2,1)S(1)}, u32[]{:S(2)}, u32[]{:S(2)}) collective-permute-start(bf16[64,1536]{1,0:T(8,128)(2,1)S(1)} %shard_map.43), channel_id=1, source_target_pairs={{0,1},{1,0},{2,3},{3,2},{4,5},{5,4},{6,7},{7,6},{8,9},{9,8},{10,11... | collective-permute-start | bytes 589832 | tf_op jit(solution)/shard_map/ppermute | solution.py:49
  22.8 6.2 %collective-permute-done.12.refs_11_.refs_1_ = bf16[64,1536]{1,0:T(8,128)(2,1)S(1)} collective-permute-done((bf16[64,1536]{1,0:T(8,128)(2,1)S(1)}, bf16[64,1536]{1,0:T(8,128)(2,1)S(1)}, u32[]{:S(2)}, u32[]{:S(2)}) %collective-permute-start.12) | collective-permute-done | bytes 196640 | tf_op jit(solution)/shard_map/ppermute | solution.py:49
  28.9 0.5 collective-permute-start.11
  29.4 2.1 %collective-permute-done.7.refs_3_ = bf16[64,1536]{1,0:T(8,128)(2,1)S(1)} collective-permute-done((bf16[64,1536]{1,0:T(8,128)(2,1)S(1)}, bf16[64,1536]{1,0:T(8,128)(2,1)S(1)}, u32[]{:S(2)}, u32[]{:S(2)}) %collective-permute-start.7) | collective-permute-done | bytes 196640 | tf_op jit(solution)/shard_map/ppermute | solution.py:49
  31.6 1.0 %shard_map.46 = (f32[256,512]{1,0:T(8,128)S(1)}, f32[256,512]{1,0:T(8,128)S(1)}, f32[3,4,64]{2,1,0:T(4,128)S(1)}, f32[3,8,64]{2,1,0:T(8,128)S(1)}) custom-call(bf16[64,2304]{1,0:T(8,128)(2,1)S(1)} %shard_map.41.refs_0_, bf16[64,1536]{1,0:T(8,128)(2,1)S(1)} %collective-permute-done.refs_1_, bf16[64,3072]{1,0:T(8,128)(2,1)S(1)} %collective-permute-done.5.refs_2_, ...), custom_call_target="tpu_custom_call" | custom-call | flops 603979776 | bytes 4301824 | tf_op jit(solution)/shard_map/pallas_call | solution.py:185
  32.7 1.2 %collective-permute-done.14 = f32[3,12,64]{2,1,0:T(8,128)S(1)} collective-permute-done((f32[3,12,64]{2,1,0:T(8,128)S(1)}, f32[3,12,64]{2,1,0:T(8,128)S(1)}, u32[]{:S(2)}, u32[]{:S(2)}) %collective-permute-start.14) | collective-permute-done | bytes 9248 | tf_op jit(solution)/shard_map/ppermute | solution.py:49
  33.9 0.6 %collective-permute-start.15 = (f32[3,8,64]{2,1,0:T(8,128)S(1)}, f32[3,8,64]{2,1,0:T(8,128)S(1)}, u32[]{:S(2)}, u32[]{:S(2)}) collective-permute-start(f32[3,8,64]{2,1,0:T(8,128)S(1)} %maximum_select_fusion), channel_id=1, source_target_pairs={{0,1},{1,0},{2,3},{3,2},{4,6},{5,7},{6,4},{7,5},{8,9},{9,8},{10,11... | collective-permute-start | bytes 18440 | tf_op jit(solution)/shard_map/ppermute | solution.py:254
  34.5 3.2 %collective-permute-done.15 = f32[3,8,64]{2,1,0:T(8,128)S(1)} collective-permute-done((f32[3,8,64]{2,1,0:T(8,128)S(1)}, f32[3,8,64]{2,1,0:T(8,128)S(1)}, u32[]{:S(2)}, u32[]{:S(2)}) %collective-permute-start.15) | collective-permute-done | bytes 6176 | tf_op jit(solution)/shard_map/ppermute | solution.py:254
  37.8 0.6 %collective-permute-start.16 = (f32[3,8,64]{2,1,0:T(8,128)S(1)}, f32[3,8,64]{2,1,0:T(8,128)S(1)}, u32[]{:S(2)}, u32[]{:S(2)}) collective-permute-start(f32[3,8,64]{2,1,0:T(8,128)S(1)} %add.10), channel_id=1, source_target_pairs={{0,8},{1,9},{2,10},{3,11},{4,20},{5,21},{6,22},{7,23},{8,0},{9,1},... | collective-permute-start | bytes 18440 | tf_op jit(solution)/shard_map/ppermute | solution.py:254
  38.4 3.2 %collective-permute-done.16 = f32[3,8,64]{2,1,0:T(8,128)S(1)} collective-permute-done((f32[3,8,64]{2,1,0:T(8,128)S(1)}, f32[3,8,64]{2,1,0:T(8,128)S(1)}, u32[]{:S(2)}, u32[]{:S(2)}) %collective-permute-start.16) | collective-permute-done | bytes 6176 | tf_op jit(solution)/shard_map/ppermute | solution.py:254
  41.6 1.2 %collective-permute-done.17 = f32[3,8,64]{2,1,0:T(8,128)S(1)} collective-permute-done((f32[3,8,64]{2,1,0:T(8,128)S(1)}, f32[3,8,64]{2,1,0:T(8,128)S(1)}, u32[]{:S(2)}, u32[]{:S(2)}) %collective-permute-start.17) | collective-permute-done | bytes 6176 | tf_op jit(solution)/shard_map/ppermute | solution.py:49
  42.8 0.1 reshape.27.col_sum
  42.9 0.1 reshape.26.row_sum
  43.0 0.9 %shard_map.47 = (f32[64,768]{1,0:T(8,128)S(1)}, f32[8,128]{1,0:T(8,128)S(1)}, f32[64,896]{1,0:T(8,128)S(1)}, f32[64,896]{1,0:T(8,128)S(1)}, f32[64,896]{1,0:T(8,128)S(1)}) custom-call(f32[256,512]{1,0:T(8,128)S(1)} %get-tuple-element.25.gram_s, f32[256,512]{1,0:T(8,128)S(1)} %get-tuple-element.26.gram_t, f32[3,1,256]{2,1,0:T(1,128)S(1)} %reshape.26.row_sum, ...), custom_call_target="tpu_custom_call" | custom-call | flops 402653184 | bytes 3322880 | tf_op jit(solution)/shard_map/pallas_call | solution.py:185
  43.9 0.6 %collective-permute-start.18 = (f16[64,896]{1,0:T(8,128)(2,1)S(1)}, f16[64,896]{1,0:T(8,128)(2,1)S(1)}, u32[]{:S(2)}, u32[]{:S(2)}) collective-permute-start(f16[64,896]{1,0:T(8,128)(2,1)S(1)} %convert_element_type.18), channel_id=1, source_target_pairs={{0,1},{1,0},{2,3},{3,2},{4,5},{5,4},{6,7},{7,6},{8,9},{9,8},{10,11... | collective-permute-start | bytes 344072 | tf_op jit(solution)/shard_map/ppermute | solution.py:49
  44.5 1.6 %collective-permute-start.19 = (f16[64,896]{1,0:T(8,128)(2,1)S(1)}, f16[64,896]{1,0:T(8,128)(2,1)S(1)}, u32[]{:S(2)}, u32[]{:S(2)}) collective-permute-start(f16[64,896]{1,0:T(8,128)(2,1)S(1)} %convert_element_type.20), channel_id=1, source_target_pairs={{0,8},{1,9},{2,10},{3,11},{4,12},{5,13},{6,14},{7,15},{8,0},{9,1},... | collective-permute-start | bytes 344072 | tf_op jit(solution)/shard_map/ppermute | solution.py:49
  46.1 1.5 %collective-permute-start.20 = (f16[64,896]{1,0:T(8,128)(2,1)S(1)}, f16[64,896]{1,0:T(8,128)(2,1)S(1)}, u32[]{:S(2)}, u32[]{:S(2)}) collective-permute-start(f16[64,896]{1,0:T(8,128)(2,1)S(1)} %convert_element_type.22), channel_id=1, source_target_pairs={{0,9},{1,8},{2,11},{3,10},{4,13},{5,12},{6,15},{7,14},{8,1},{9,0},... | collective-permute-start | bytes 344072 | tf_op jit(solution)/shard_map/ppermute | solution.py:49
  47.6 2.3 %collective-permute-done.18 = f16[64,896]{1,0:T(8,128)(2,1)S(1)} collective-permute-done((f16[64,896]{1,0:T(8,128)(2,1)S(1)}, f16[64,896]{1,0:T(8,128)(2,1)S(1)}, u32[]{:S(2)}, u32[]{:S(2)}) %collective-permute-start.18) | collective-permute-done | bytes 114720 | tf_op jit(solution)/shard_map/ppermute | solution.py:49
  50.0 2.0 %collective-permute-done.19 = f16[64,896]{1,0:T(8,128)(2,1)S(1)} collective-permute-done((f16[64,896]{1,0:T(8,128)(2,1)S(1)}, f16[64,896]{1,0:T(8,128)(2,1)S(1)}, u32[]{:S(2)}, u32[]{:S(2)}) %collective-permute-start.19) | collective-permute-done | bytes 114720 | tf_op jit(solution)/shard_map/ppermute | solution.py:49
  52.0 0.8 %shard_map.48 = (f32[64,768]{1,0:T(8,128)}, f32[1,1]{1,0:T(1,128)}) custom-call(f32[64,768]{1,0:T(8,128)S(1)} %get-tuple-element.29.own, f32[8,128]{1,0:T(8,128)S(1)} %get-tuple-element.30.share, f32[64,896]{1,0:T(8,128)S(1)} %convert_element_type.19.refs_0_, f32[64,896]{1,0:T(8,128)S(1)} %convert_element_type.21.refs_1_, ...), custom_call_target="tpu_custom_call" | custom-call | bytes 1085444 | tf_op jit(solution)/shard_map/pallas_call | solution.py:185
  (41 shorter events, 0.6 us)
Async XLA Ops:
  0.6 15.7 %copy-start = (bf16[64,1536]{1,0:T(8,128)(2,1)S(1)}, bf16[64,1536]{1,0:T(8,128)(2,1)}, u32[]{:S(2)}) copy-start(bf16[64,1536]{1,0:T(8,128)(2,1)} %refs_0_.1) | copy-start | bytes 589828
  0.6 15.7 %copy-start.1 = (bf16[64,768]{1,0:T(8,128)(2,1)S(1)}, bf16[64,768]{1,0:T(8,128)(2,1)}, u32[]{:S(2)}) copy-start(bf16[64,768]{1,0:T(8,128)(2,1)} %refs_1_.1) | copy-start | bytes 294916
  0.6 6.2 %collective-permute-start.2 = (bf16[64,1536]{1,0:T(8,128)(2,1)}, bf16[64,1536]{1,0:T(8,128)(2,1)S(1)}, u32[]{:S(2)}, u32[]{:S(2)}) collective-permute-start(bf16[64,1536]{1,0:T(8,128)(2,1)} %refs_0_.1), channel_id=1, source_target_pairs={{0,4},{1,5},{2,6},{3,7},{4,0},{5,1},{6,2},{7,3},{8,12},{9,13},{10,... | collective-permute-start | bytes 589832 | tf_op jit(solution)/shard_map/ppermute | solution.py:49
  1.2 5.7 %collective-permute-start.3 = (bf16[64,768]{1,0:T(8,128)(2,1)}, bf16[64,768]{1,0:T(8,128)(2,1)S(1)}, u32[]{:S(2)}, u32[]{:S(2)}) collective-permute-start(bf16[64,768]{1,0:T(8,128)(2,1)} %refs_1_.1), channel_id=1, source_target_pairs={{0,4},{1,5},{2,6},{3,7},{4,0},{5,1},{6,2},{7,3},{8,12},{9,13},{10,... | collective-permute-start | bytes 294920 | tf_op jit(solution)/shard_map/ppermute | solution.py:49
  1.2 12.4 %collective-permute-start = (bf16[64,1536]{1,0:T(8,128)(2,1)}, bf16[64,1536]{1,0:T(8,128)(2,1)S(1)}, u32[]{:S(2)}, u32[]{:S(2)}) collective-permute-start(bf16[64,1536]{1,0:T(8,128)(2,1)} %refs_0_.1), channel_id=1, source_target_pairs={{0,1},{1,0},{2,3},{3,2},{4,5},{5,4},{6,7},{7,6},{8,9},{9,8},{10,11... | collective-permute-start | bytes 589832 | tf_op jit(solution)/shard_map/ppermute | solution.py:49
  4.2 12.0 %collective-permute-start.1 = (bf16[64,1536]{1,0:T(8,128)(2,1)}, bf16[64,1536]{1,0:T(8,128)(2,1)S(1)}, u32[]{:S(2)}, u32[]{:S(2)}) collective-permute-start(bf16[64,1536]{1,0:T(8,128)(2,1)} %refs_0_.1), channel_id=1, source_target_pairs={{0,2},{1,3},{2,0},{3,1},{4,6},{5,7},{6,4},{7,5},{8,10},{9,11},{10,... | collective-permute-start | bytes 589832 | tf_op jit(solution)/shard_map/ppermute | solution.py:49
  6.8 9.4 %collective-permute-start.4 = (bf16[64,1536]{1,0:T(8,128)(2,1)}, bf16[64,1536]{1,0:T(8,128)(2,1)S(1)}, u32[]{:S(2)}, u32[]{:S(2)}) collective-permute-start(bf16[64,1536]{1,0:T(8,128)(2,1)} %refs_0_.1), channel_id=1, source_target_pairs={{0,16},{1,17},{2,18},{3,19},{4,20},{5,21},{6,22},{7,23},{8,24},{9,... | collective-permute-start | bytes 589832 | tf_op jit(solution)/shard_map/ppermute | solution.py:49
  8.4 7.9 %collective-permute-start.9 = (bf16[64,768]{1,0:T(8,128)(2,1)}, bf16[64,768]{1,0:T(8,128)(2,1)S(1)}, u32[]{:S(2)}, u32[]{:S(2)}) collective-permute-start(bf16[64,768]{1,0:T(8,128)(2,1)} %refs_1_.1), channel_id=1, source_target_pairs={{0,16},{1,17},{2,18},{3,19},{4,20},{5,21},{6,22},{7,23},{8,24},{9,... | collective-permute-start | bytes 294920 | tf_op jit(solution)/shard_map/ppermute | solution.py:49
  8.9 7.6 %collective-permute-start.6 = (bf16[64,768]{1,0:T(8,128)(2,1)}, bf16[64,768]{1,0:T(8,128)(2,1)S(1)}, u32[]{:S(2)}, u32[]{:S(2)}) collective-permute-start(bf16[64,768]{1,0:T(8,128)(2,1)} %refs_1_.1), channel_id=1, source_target_pairs={{0,8},{1,9},{2,10},{3,11},{4,12},{5,13},{6,14},{7,15},{8,0},{9,1},... | collective-permute-start | bytes 294920 | tf_op jit(solution)/shard_map/ppermute | solution.py:49
  16.3 15.3 %collective-permute-start.10 = (bf16[64,3840]{1,0:T(8,128)(2,1)S(1)}, bf16[64,3840]{1,0:T(8,128)(2,1)S(1)}, u32[]{:S(2)}, u32[]{:S(2)}) collective-permute-start(bf16[64,3840]{1,0:T(8,128)(2,1)S(1)} %shard_map.44), channel_id=1, source_target_pairs={{0,4},{1,5},{2,6},{3,7},{4,0},{5,1},{6,2},{7,3},{8,12},{9,13},{10,... | collective-permute-start | bytes 1474568 | tf_op jit(solution)/shard_map/ppermute | solution.py:49
  16.5 12.4 %collective-permute-start.12 = (bf16[64,1536]{1,0:T(8,128)(2,1)S(1)}, bf16[64,1536]{1,0:T(8,128)(2,1)S(1)}, u32[]{:S(2)}, u32[]{:S(2)}) collective-permute-start(bf16[64,1536]{1,0:T(8,128)(2,1)S(1)} %shard_map.45), channel_id=1, source_target_pairs={{0,2},{1,3},{2,0},{3,1},{4,6},{5,7},{6,4},{7,5},{8,10},{9,11},{10,... | collective-permute-start | bytes 589832 | tf_op jit(solution)/shard_map/ppermute | solution.py:49
  16.9 12.1 %collective-permute-start.8 = (bf16[64,1536]{1,0:T(8,128)(2,1)S(1)}, bf16[64,1536]{1,0:T(8,128)(2,1)S(1)}, u32[]{:S(2)}, u32[]{:S(2)}) collective-permute-start(bf16[64,1536]{1,0:T(8,128)(2,1)S(1)} %collective-permute-done.1.refs_0_.refs_5_), channel_id=1, source_target_pairs={{0,16},{1,17},{2,18},{3,19},{4,20},{5,21},{6,22},{7,23},{8,24},{9,... | collective-permute-start | bytes 589832 | tf_op jit(solution)/shard_map/ppermute | solution.py:49
  18.4 13.2 %collective-permute-start.5 = (bf16[64,3072]{1,0:T(8,128)(2,1)S(1)}, bf16[64,3072]{1,0:T(8,128)(2,1)S(1)}, u32[]{:S(2)}, u32[]{:S(2)}) collective-permute-start(bf16[64,3072]{1,0:T(8,128)(2,1)S(1)} %shard_map.42), channel_id=1, source_target_pairs={{0,8},{1,9},{2,10},{3,11},{4,12},{5,13},{6,14},{7,15},{8,0},{9,1},... | collective-permute-start | bytes 1179656 | tf_op jit(solution)/shard_map/ppermute | solution.py:49
  20.0 11.6 %collective-permute-start.7 = (bf16[64,1536]{1,0:T(8,128)(2,1)S(1)}, bf16[64,1536]{1,0:T(8,128)(2,1)S(1)}, u32[]{:S(2)}, u32[]{:S(2)}) collective-permute-start(bf16[64,1536]{1,0:T(8,128)(2,1)S(1)} %shard_map.43), channel_id=1, source_target_pairs={{0,1},{1,0},{2,3},{3,2},{4,5},{5,4},{6,7},{7,6},{8,9},{9,8},{10,11... | collective-permute-start | bytes 589832 | tf_op jit(solution)/shard_map/ppermute | solution.py:49
  28.9 2.7 %collective-permute-start.13 = (bf16[64,1536]{1,0:T(8,128)(2,1)S(1)}, bf16[64,1536]{1,0:T(8,128)(2,1)S(1)}, u32[]{:S(2)}, u32[]{:S(2)}) collective-permute-start(bf16[64,1536]{1,0:T(8,128)(2,1)S(1)} %collective-permute-done.12.refs_11_.refs_1_), channel_id=1, source_target_pairs={{0,4},{1,5},{2,6},{3,7},{4,0},{5,1},{6,2},{7,3},{8,12},{9,13},{10,... | collective-permute-start | bytes 589832 | tf_op jit(solution)/shard_map/ppermute | solution.py:49
  28.9 2.6 %collective-permute-start.11 = (bf16[64,1536]{1,0:T(8,128)(2,1)S(1)}, bf16[64,1536]{1,0:T(8,128)(2,1)S(1)}, u32[]{:S(2)}, u32[]{:S(2)}) collective-permute-start(bf16[64,1536]{1,0:T(8,128)(2,1)S(1)} %collective-permute-done.8.refs_7_), channel_id=1, source_target_pairs={{0,4},{1,5},{2,6},{3,7},{4,0},{5,1},{6,2},{7,3},{8,12},{9,13},{10,... | collective-permute-start | bytes 589832 | tf_op jit(solution)/shard_map/ppermute | solution.py:49
  32.7 1.3 %collective-permute-start.14 = (f32[3,12,64]{2,1,0:T(8,128)S(1)}, f32[3,12,64]{2,1,0:T(8,128)S(1)}, u32[]{:S(2)}, u32[]{:S(2)}) collective-permute-start(f32[3,12,64]{2,1,0:T(8,128)S(1)} %pad_maximum_fusion), channel_id=1, source_target_pairs={{0,4},{1,5},{2,6},{3,7},{4,0},{5,1},{6,2},{7,3},{8,12},{9,13},{10,... | collective-permute-start | bytes 27656 | tf_op jit(solution)/shard_map/ppermute | solution.py:49
  33.9 3.8 %collective-permute-start.15 = (f32[3,8,64]{2,1,0:T(8,128)S(1)}, f32[3,8,64]{2,1,0:T(8,128)S(1)}, u32[]{:S(2)}, u32[]{:S(2)}) collective-permute-start(f32[3,8,64]{2,1,0:T(8,128)S(1)} %maximum_select_fusion), channel_id=1, source_target_pairs={{0,1},{1,0},{2,3},{3,2},{4,6},{5,7},{6,4},{7,5},{8,9},{9,8},{10,11... | collective-permute-start | bytes 18440 | tf_op jit(solution)/shard_map/ppermute | solution.py:254
  37.8 3.8 %collective-permute-start.16 = (f32[3,8,64]{2,1,0:T(8,128)S(1)}, f32[3,8,64]{2,1,0:T(8,128)S(1)}, u32[]{:S(2)}, u32[]{:S(2)}) collective-permute-start(f32[3,8,64]{2,1,0:T(8,128)S(1)} %add.10), channel_id=1, source_target_pairs={{0,8},{1,9},{2,10},{3,11},{4,20},{5,21},{6,22},{7,23},{8,0},{9,1},... | collective-permute-start | bytes 18440 | tf_op jit(solution)/shard_map/ppermute | solution.py:254
  41.5 1.2 %collective-permute-start.17 = (f32[3,8,64]{2,1,0:T(8,128)S(1)}, f32[3,8,64]{2,1,0:T(8,128)S(1)}, u32[]{:S(2)}, u32[]{:S(2)}) collective-permute-start(f32[3,8,64]{2,1,0:T(8,128)S(1)} %add.11), channel_id=1, source_target_pairs={{0,4},{1,5},{2,6},{3,7},{4,0},{5,1},{6,2},{7,3},{8,12},{9,13},{10,... | collective-permute-start | bytes 18440 | tf_op jit(solution)/shard_map/ppermute | solution.py:49
  43.9 6.1 %collective-permute-start.18 = (f16[64,896]{1,0:T(8,128)(2,1)S(1)}, f16[64,896]{1,0:T(8,128)(2,1)S(1)}, u32[]{:S(2)}, u32[]{:S(2)}) collective-permute-start(f16[64,896]{1,0:T(8,128)(2,1)S(1)} %convert_element_type.18), channel_id=1, source_target_pairs={{0,1},{1,0},{2,3},{3,2},{4,5},{5,4},{6,7},{7,6},{8,9},{9,8},{10,11... | collective-permute-start | bytes 344072 | tf_op jit(solution)/shard_map/ppermute | solution.py:49
  44.5 7.5 %collective-permute-start.19 = (f16[64,896]{1,0:T(8,128)(2,1)S(1)}, f16[64,896]{1,0:T(8,128)(2,1)S(1)}, u32[]{:S(2)}, u32[]{:S(2)}) collective-permute-start(f16[64,896]{1,0:T(8,128)(2,1)S(1)} %convert_element_type.20), channel_id=1, source_target_pairs={{0,8},{1,9},{2,10},{3,11},{4,12},{5,13},{6,14},{7,15},{8,0},{9,1},... | collective-permute-start | bytes 344072 | tf_op jit(solution)/shard_map/ppermute | solution.py:49
  46.1 5.9 %collective-permute-start.20 = (f16[64,896]{1,0:T(8,128)(2,1)S(1)}, f16[64,896]{1,0:T(8,128)(2,1)S(1)}, u32[]{:S(2)}, u32[]{:S(2)}) collective-permute-start(f16[64,896]{1,0:T(8,128)(2,1)S(1)} %convert_element_type.22), channel_id=1, source_target_pairs={{0,9},{1,8},{2,11},{3,10},{4,13},{5,12},{6,15},{7,14},{8,1},{9,0},... | collective-permute-start | bytes 344072 | tf_op jit(solution)/shard_map/ppermute | solution.py:49

commit v18 on v17

--- a/solution.py
+++ b/solution.py
@@ -103,7 +103,8 @@
     for b, mask in enumerate(row_masks):
         if b:
             parts = [row_t[p] for p in range(1 << b)]
-            got, start = send(join(*(array[:, i:j] for array, i, j in parts)), mask, count), 0
+            value = after(join(*(array[:, i:j] for array, i, j in parts)), row_s[2][0])
+            got, start = send(value, mask, count), 0
             for p, (_, i, j) in enumerate(parts):
                 row_t[p | 1 << b] = (got, start, start + j - i)
                 start += j - i
@@ -118,7 +119,12 @@
     ]
     for swap in swaps:
         arrays = list({id(side[p][0]): side[p][0] for side, _, p in swap}.values())
-        got = send(join(*arrays) if len(arrays) > 1 else arrays[0], core_mask, count)
+        value = join(*arrays) if len(arrays) > 1 else arrays[0]
+        if swap is swaps[1]:
+            value = after(value, col_s[1][0])
+        if swap is swaps[2]:
+            value = after(value, row_t[max(row_t)][0])
+        got = send(value, core_mask, count)
         starts = {id(array): sum(a.shape[1] for a in arrays[:k]) for k, array in enumerate(arrays)}
         for side, core, p in swap:
             array, start, stop = side[p]

time: 53 us -> 53.3 us (level)
  local copies, waits for them, and re-layouts: 0.24 us -> 2.05 us
  waiting for transfers between devices: 27.2 us -> 26 us
    unnamed x4, local copies, waits for them, and re-layouts: 0.01 us -> 1.82 us
    ppermute x19, waiting for transfers between devices: 20.9 us -> 19.1 us  [send(): return lax.ppermute(value, AXES, [(i, i ^ mask) for i in range(count)])]
  transfers between devices with their start and end apart: 21 -> 21, of which waited for: 10 -> 12; matrix products, arithmetic and copies ran while one was open for 0% -> 0% of each run, Pallas kernels for 0% -> 0%
where the time goes in v18:
time: 53.3 us; the launch traced here: 53.1 us
  waiting for transfers between devices  26 us (49%)
  starting transfers between devices  21.3 us (40%)
  Pallas kernels  2.84 us (5%)
  local copies, waits for them, and re-layouts  2.05 us (4%)
  between operations  0.79 us (1%)
    ppermute x19, starting transfers between devices, send(): return lax.ppermute(value, AXES, [(i, i ^ mask) for i in range(count)])  20.6 us
    ppermute x19, waiting for transfers between devices, send(): return lax.ppermute(value, AXES, [(i, i ^ mask) for i in range(count)])  19.1 us
    ppermute x2, waiting for transfers between devices, exchange_sums(): got = lax.ppermute(sums, AXES, pairs).reshape(3, -1, 2, 1 << b, rows)  6.84 us
    pallas_call x8, Pallas kernels, call(): pl.pallas_call(kernel, out_shape=outputs, **options, compiler_params=pltp...  2.84 us
    unnamed x4, local copies, waits for them, and re-layouts  1.82 us
  transfers between devices with their start and end apart: 21, of which 12 were waited for; matrix products, arithmetic and copies ran while one was open for 0% of the time, Pallas kernels for 0%

profile of v18, /device:TPU:0, one launch (start us, length us, event | category | flops | bytes accessed | tf_op | source)
XLA Modules:
  0.0 53.1 jit_solution(15097848636791789519)
XLA Ops:
  0.6 0.5 collective-permute-start.2
  1.2 3.0 %collective-permute-start = (bf16[64,1536]{1,0:T(8,128)(2,1)}, bf16[64,1536]{1,0:T(8,128)(2,1)S(1)}, u32[]{:S(2)}, u32[]{:S(2)}) collective-permute-start(bf16[64,1536]{1,0:T(8,128)(2,1)} %refs_0_.1), channel_id=1, source_target_pairs={{0,1},{1,0},{2,3},{3,2},{4,5},{5,4},{6,7},{7,6},{8,9},{9,8},{10,11... | collective-permute-start | bytes 589832 | tf_op jit(solution)/shard_map/ppermute | solution.py:49
  4.2 2.6 %collective-permute-start.1 = (bf16[64,1536]{1,0:T(8,128)(2,1)}, bf16[64,1536]{1,0:T(8,128)(2,1)S(1)}, u32[]{:S(2)}, u32[]{:S(2)}) collective-permute-start(bf16[64,1536]{1,0:T(8,128)(2,1)} %refs_0_.1), channel_id=1, source_target_pairs={{0,2},{1,3},{2,0},{3,1},{4,6},{5,7},{6,4},{7,5},{8,10},{9,11},{10,... | collective-permute-start | bytes 589832 | tf_op jit(solution)/shard_map/ppermute | solution.py:49
  6.8 1.5 %collective-permute-start.4 = (bf16[64,1536]{1,0:T(8,128)(2,1)}, bf16[64,1536]{1,0:T(8,128)(2,1)S(1)}, u32[]{:S(2)}, u32[]{:S(2)}) collective-permute-start(bf16[64,1536]{1,0:T(8,128)(2,1)} %refs_0_.1), channel_id=1, source_target_pairs={{0,16},{1,17},{2,18},{3,19},{4,20},{5,21},{6,22},{7,23},{8,24},{9,... | collective-permute-start | bytes 589832 | tf_op jit(solution)/shard_map/ppermute | solution.py:49
  8.3 1.5 %collective-permute-start.5 = (bf16[64,768]{1,0:T(8,128)(2,1)}, bf16[64,768]{1,0:T(8,128)(2,1)S(1)}, u32[]{:S(2)}, u32[]{:S(2)}) collective-permute-start(bf16[64,768]{1,0:T(8,128)(2,1)} %refs_1_.1), channel_id=1, source_target_pairs={{0,8},{1,9},{2,10},{3,11},{4,12},{5,13},{6,14},{7,15},{8,0},{9,1},... | collective-permute-start | bytes 294920 | tf_op jit(solution)/shard_map/ppermute | solution.py:49
  9.8 0.9 %copy-done = bf16[64,1536]{1,0:T(8,128)(2,1)S(1)} copy-done((bf16[64,1536]{1,0:T(8,128)(2,1)S(1)}, bf16[64,1536]{1,0:T(8,128)(2,1)}, u32[]{:S(2)}) %copy-start) | copy-done | bytes 196632
  10.8 0.9 %copy-done.1 = bf16[64,768]{1,0:T(8,128)(2,1)S(1)} copy-done((bf16[64,768]{1,0:T(8,128)(2,1)S(1)}, bf16[64,768]{1,0:T(8,128)(2,1)}, u32[]{:S(2)}) %copy-start.1) | copy-done | bytes 98328
  11.7 0.6 %collective-permute-start.9 = (bf16[64,768]{1,0:T(8,128)(2,1)S(1)}, bf16[64,768]{1,0:T(8,128)(2,1)S(1)}, u32[]{:S(2)}, u32[]{:S(2)}) collective-permute-start(bf16[64,768]{1,0:T(8,128)(2,1)S(1)} %copy-done.1), channel_id=1, source_target_pairs={{0,16},{1,17},{2,18},{3,19},{4,20},{5,21},{6,22},{7,23},{8,24},{9,... | collective-permute-start | bytes 294920 | tf_op jit(solution)/shard_map/ppermute | solution.py:49
  12.3 1.4 %collective-permute-done.refs_1_ = bf16[64,1536]{1,0:T(8,128)(2,1)S(1)} collective-permute-done((bf16[64,1536]{1,0:T(8,128)(2,1)}, bf16[64,1536]{1,0:T(8,128)(2,1)S(1)}, u32[]{:S(2)}, u32[]{:S(2)}) %collective-permute-start) | collective-permute-done | bytes 196640 | tf_op jit(solution)/shard_map/ppermute | solution.py:49
  13.7 2.6 %collective-permute-done.1.refs_0_.refs_5_ = bf16[64,1536]{1,0:T(8,128)(2,1)S(1)} collective-permute-done((bf16[64,1536]{1,0:T(8,128)(2,1)}, bf16[64,1536]{1,0:T(8,128)(2,1)S(1)}, u32[]{:S(2)}, u32[]{:S(2)}) %collective-permute-start.1) | collective-permute-done | bytes 196640 | tf_op jit(solution)/shard_map/ppermute | solution.py:49
  16.3 1.6 %collective-permute-start.6 = (bf16[64,3072]{1,0:T(8,128)(2,1)S(1)}, bf16[64,3072]{1,0:T(8,128)(2,1)S(1)}, u32[]{:S(2)}, u32[]{:S(2)}) collective-permute-start(bf16[64,3072]{1,0:T(8,128)(2,1)S(1)} %shard_map.42), channel_id=1, source_target_pairs={{0,8},{1,9},{2,10},{3,11},{4,12},{5,13},{6,14},{7,15},{8,0},{9,1},... | collective-permute-start | bytes 1179656 | tf_op jit(solution)/shard_map/ppermute | solution.py:49
  18.0 0.4 collective-permute-start.11
  18.4 1.5 %collective-permute-start.8 = (bf16[64,1536]{1,0:T(8,128)(2,1)S(1)}, bf16[64,1536]{1,0:T(8,128)(2,1)S(1)}, u32[]{:S(2)}, u32[]{:S(2)}) collective-permute-start(bf16[64,1536]{1,0:T(8,128)(2,1)S(1)} %collective-permute-done.1.refs_0_.refs_5_), channel_id=1, source_target_pairs={{0,16},{1,17},{2,18},{3,19},{4,20},{5,21},{6,22},{7,23},{8,24},{9,... | collective-permute-start | bytes 589832 | tf_op jit(solution)/shard_map/ppermute | solution.py:49
  19.9 2.8 %collective-permute-start.7 = (bf16[64,1536]{1,0:T(8,128)(2,1)S(1)}, bf16[64,1536]{1,0:T(8,128)(2,1)S(1)}, u32[]{:S(2)}, u32[]{:S(2)}) collective-permute-start(bf16[64,1536]{1,0:T(8,128)(2,1)S(1)} %shard_map.43), channel_id=1, source_target_pairs={{0,1},{1,0},{2,3},{3,2},{4,5},{5,4},{6,7},{7,6},{8,9},{9,8},{10,11... | collective-permute-start | bytes 589832 | tf_op jit(solution)/shard_map/ppermute | solution.py:49
  22.7 7.8 %collective-permute-done.11.refs_11_.refs_1_ = bf16[64,1536]{1,0:T(8,128)(2,1)S(1)} collective-permute-done((bf16[64,1536]{1,0:T(8,128)(2,1)S(1)}, bf16[64,1536]{1,0:T(8,128)(2,1)S(1)}, u32[]{:S(2)}, u32[]{:S(2)}) %collective-permute-start.11) | collective-permute-done | bytes 196640 | tf_op jit(solution)/shard_map/ppermute | solution.py:49
  30.4 0.5 collective-permute-start.13
  30.9 0.8 %collective-permute-done.7.refs_3_ = bf16[64,1536]{1,0:T(8,128)(2,1)S(1)} collective-permute-done((bf16[64,1536]{1,0:T(8,128)(2,1)S(1)}, bf16[64,1536]{1,0:T(8,128)(2,1)S(1)}, u32[]{:S(2)}, u32[]{:S(2)}) %collective-permute-start.7) | collective-permute-done | bytes 196640 | tf_op jit(solution)/shard_map/ppermute | solution.py:49
  31.8 0.1 collective-permute-done.12.refs_10_
  31.9 0.3 collective-permute-done.13.refs_14_.refs_4_
  32.2 1.0 %shard_map.46 = (f32[256,512]{1,0:T(8,128)S(1)}, f32[256,512]{1,0:T(8,128)S(1)}, f32[3,4,64]{2,1,0:T(4,128)S(1)}, f32[3,8,64]{2,1,0:T(8,128)S(1)}) custom-call(bf16[64,2304]{1,0:T(8,128)(2,1)S(1)} %shard_map.41.refs_0_, bf16[64,1536]{1,0:T(8,128)(2,1)S(1)} %collective-permute-done.refs_1_, bf16[64,3072]{1,0:T(8,128)(2,1)S(1)} %collective-permute-done.6.refs_2_, ...), custom_call_target="tpu_custom_call" | custom-call | flops 603979776 | bytes 4301824 | tf_op jit(solution)/shard_map/pallas_call | solution.py:191
  33.2 0.3 collective-permute-start.14
  33.5 1.0 %collective-permute-done.14 = f32[3,12,64]{2,1,0:T(8,128)S(1)} collective-permute-done((f32[3,12,64]{2,1,0:T(8,128)S(1)}, f32[3,12,64]{2,1,0:T(8,128)S(1)}, u32[]{:S(2)}, u32[]{:S(2)}) %collective-permute-start.14) | collective-permute-done | bytes 9248 | tf_op jit(solution)/shard_map/ppermute | solution.py:49
  34.6 3.7 %collective-permute-done.15 = f32[3,8,64]{2,1,0:T(8,128)S(1)} collective-permute-done((f32[3,8,64]{2,1,0:T(8,128)S(1)}, f32[3,8,64]{2,1,0:T(8,128)S(1)}, u32[]{:S(2)}, u32[]{:S(2)}) %collective-permute-start.15) | collective-permute-done | bytes 6176 | tf_op jit(solution)/shard_map/ppermute | solution.py:260
  38.3 0.6 %collective-permute-start.16 = (f32[3,8,64]{2,1,0:T(8,128)S(1)}, f32[3,8,64]{2,1,0:T(8,128)S(1)}, u32[]{:S(2)}, u32[]{:S(2)}) collective-permute-start(f32[3,8,64]{2,1,0:T(8,128)S(1)} %add.10), channel_id=1, source_target_pairs={{0,8},{1,9},{2,10},{3,11},{4,20},{5,21},{6,22},{7,23},{8,0},{9,1},... | collective-permute-start | bytes 18440 | tf_op jit(solution)/shard_map/ppermute | solution.py:260
  38.9 3.2 %collective-permute-done.16 = f32[3,8,64]{2,1,0:T(8,128)S(1)} collective-permute-done((f32[3,8,64]{2,1,0:T(8,128)S(1)}, f32[3,8,64]{2,1,0:T(8,128)S(1)}, u32[]{:S(2)}, u32[]{:S(2)}) %collective-permute-start.16) | collective-permute-done | bytes 6176 | tf_op jit(solution)/shard_map/ppermute | solution.py:260
  42.2 1.2 %collective-permute-done.17 = f32[3,8,64]{2,1,0:T(8,128)S(1)} collective-permute-done((f32[3,8,64]{2,1,0:T(8,128)S(1)}, f32[3,8,64]{2,1,0:T(8,128)S(1)}, u32[]{:S(2)}, u32[]{:S(2)}) %collective-permute-start.17) | collective-permute-done | bytes 6176 | tf_op jit(solution)/shard_map/ppermute | solution.py:49
  43.5 0.9 %shard_map.47 = (f32[64,768]{1,0:T(8,128)S(1)}, f32[8,128]{1,0:T(8,128)S(1)}, f32[64,896]{1,0:T(8,128)S(1)}, f32[64,896]{1,0:T(8,128)S(1)}, f32[64,896]{1,0:T(8,128)S(1)}) custom-call(f32[256,512]{1,0:T(8,128)S(1)} %get-tuple-element.31.gram_s, f32[256,512]{1,0:T(8,128)S(1)} %get-tuple-element.32.gram_t, f32[3,1,256]{2,1,0:T(1,128)S(1)} %reshape.26.row_sum, ...), custom_call_target="tpu_custom_call" | custom-call | flops 402653184 | bytes 3322880 | tf_op jit(solution)/shard_map/pallas_call | solution.py:191
  44.5 0.6 %collective-permute-start.19 = (f16[64,896]{1,0:T(8,128)(2,1)S(1)}, f16[64,896]{1,0:T(8,128)(2,1)S(1)}, u32[]{:S(2)}, u32[]{:S(2)}) collective-permute-start(f16[64,896]{1,0:T(8,128)(2,1)S(1)} %convert_element_type.20), channel_id=1, source_target_pairs={{0,8},{1,9},{2,10},{3,11},{4,12},{5,13},{6,14},{7,15},{8,0},{9,1},... | collective-permute-start | bytes 344072 | tf_op jit(solution)/shard_map/ppermute | solution.py:49
  45.1 3.0 %collective-permute-start.20 = (f16[64,896]{1,0:T(8,128)(2,1)S(1)}, f16[64,896]{1,0:T(8,128)(2,1)S(1)}, u32[]{:S(2)}, u32[]{:S(2)}) collective-permute-start(f16[64,896]{1,0:T(8,128)(2,1)S(1)} %convert_element_type.22), channel_id=1, source_target_pairs={{0,9},{1,8},{2,11},{3,10},{4,13},{5,12},{6,15},{7,14},{8,1},{9,0},... | collective-permute-start | bytes 344072 | tf_op jit(solution)/shard_map/ppermute | solution.py:49
  48.1 2.3 %collective-permute-done.18 = f16[64,896]{1,0:T(8,128)(2,1)S(1)} collective-permute-done((f16[64,896]{1,0:T(8,128)(2,1)S(1)}, f16[64,896]{1,0:T(8,128)(2,1)S(1)}, u32[]{:S(2)}, u32[]{:S(2)}) %collective-permute-start.18) | collective-permute-done | bytes 114720 | tf_op jit(solution)/shard_map/ppermute | solution.py:49
  50.5 1.8 %collective-permute-done.19 = f16[64,896]{1,0:T(8,128)(2,1)S(1)} collective-permute-done((f16[64,896]{1,0:T(8,128)(2,1)S(1)}, f16[64,896]{1,0:T(8,128)(2,1)S(1)}, u32[]{:S(2)}, u32[]{:S(2)}) %collective-permute-start.19) | collective-permute-done | bytes 114720 | tf_op jit(solution)/shard_map/ppermute | solution.py:49
  52.3 0.8 %shard_map.48 = (f32[64,768]{1,0:T(8,128)}, f32[1,1]{1,0:T(1,128)}) custom-call(f32[64,768]{1,0:T(8,128)S(1)} %get-tuple-element.35.own, f32[8,128]{1,0:T(8,128)S(1)} %get-tuple-element.36.share, f32[64,896]{1,0:T(8,128)S(1)} %convert_element_type.19.refs_0_, f32[64,896]{1,0:T(8,128)S(1)} %convert_element_type.21.refs_1_, ...), custom_call_target="tpu_custom_call" | custom-call | bytes 1085444 | tf_op jit(solution)/shard_map/pallas_call | solution.py:191
  (41 shorter events, 0.9 us)
Async XLA Ops:
  0.6 6.2 %collective-permute-start.2 = (bf16[64,1536]{1,0:T(8,128)(2,1)}, bf16[64,1536]{1,0:T(8,128)(2,1)S(1)}, u32[]{:S(2)}, u32[]{:S(2)}) collective-permute-start(bf16[64,1536]{1,0:T(8,128)(2,1)} %refs_0_.1), channel_id=1, source_target_pairs={{0,4},{1,5},{2,6},{3,7},{4,0},{5,1},{6,2},{7,3},{8,12},{9,13},{10,... | collective-permute-start | bytes 589832 | tf_op jit(solution)/shard_map/ppermute | solution.py:49
  1.1 5.7 %collective-permute-start.3 = (bf16[64,768]{1,0:T(8,128)(2,1)}, bf16[64,768]{1,0:T(8,128)(2,1)S(1)}, u32[]{:S(2)}, u32[]{:S(2)}) collective-permute-start(bf16[64,768]{1,0:T(8,128)(2,1)} %refs_1_.1), channel_id=1, source_target_pairs={{0,4},{1,5},{2,6},{3,7},{4,0},{5,1},{6,2},{7,3},{8,12},{9,13},{10,... | collective-permute-start | bytes 294920 | tf_op jit(solution)/shard_map/ppermute | solution.py:49
  1.2 12.4 %collective-permute-start = (bf16[64,1536]{1,0:T(8,128)(2,1)}, bf16[64,1536]{1,0:T(8,128)(2,1)S(1)}, u32[]{:S(2)}, u32[]{:S(2)}) collective-permute-start(bf16[64,1536]{1,0:T(8,128)(2,1)} %refs_0_.1), channel_id=1, source_target_pairs={{0,1},{1,0},{2,3},{3,2},{4,5},{5,4},{6,7},{7,6},{8,9},{9,8},{10,11... | collective-permute-start | bytes 589832 | tf_op jit(solution)/shard_map/ppermute | solution.py:49
  4.2 12.0 %collective-permute-start.1 = (bf16[64,1536]{1,0:T(8,128)(2,1)}, bf16[64,1536]{1,0:T(8,128)(2,1)S(1)}, u32[]{:S(2)}, u32[]{:S(2)}) collective-permute-start(bf16[64,1536]{1,0:T(8,128)(2,1)} %refs_0_.1), channel_id=1, source_target_pairs={{0,2},{1,3},{2,0},{3,1},{4,6},{5,7},{6,4},{7,5},{8,10},{9,11},{10,... | collective-permute-start | bytes 589832 | tf_op jit(solution)/shard_map/ppermute | solution.py:49
  6.8 9.4 %collective-permute-start.4 = (bf16[64,1536]{1,0:T(8,128)(2,1)}, bf16[64,1536]{1,0:T(8,128)(2,1)S(1)}, u32[]{:S(2)}, u32[]{:S(2)}) collective-permute-start(bf16[64,1536]{1,0:T(8,128)(2,1)} %refs_0_.1), channel_id=1, source_target_pairs={{0,16},{1,17},{2,18},{3,19},{4,20},{5,21},{6,22},{7,23},{8,24},{9,... | collective-permute-start | bytes 589832 | tf_op jit(solution)/shard_map/ppermute | solution.py:49
  8.3 7.9 %collective-permute-start.5 = (bf16[64,768]{1,0:T(8,128)(2,1)}, bf16[64,768]{1,0:T(8,128)(2,1)S(1)}, u32[]{:S(2)}, u32[]{:S(2)}) collective-permute-start(bf16[64,768]{1,0:T(8,128)(2,1)} %refs_1_.1), channel_id=1, source_target_pairs={{0,8},{1,9},{2,10},{3,11},{4,12},{5,13},{6,14},{7,15},{8,0},{9,1},... | collective-permute-start | bytes 294920 | tf_op jit(solution)/shard_map/ppermute | solution.py:49
  9.8 0.9 %copy-start = (bf16[64,1536]{1,0:T(8,128)(2,1)S(1)}, bf16[64,1536]{1,0:T(8,128)(2,1)}, u32[]{:S(2)}) copy-start(bf16[64,1536]{1,0:T(8,128)(2,1)} %refs_0_.1) | copy-start | bytes 589828
  10.8 0.9 %copy-start.1 = (bf16[64,768]{1,0:T(8,128)(2,1)S(1)}, bf16[64,768]{1,0:T(8,128)(2,1)}, u32[]{:S(2)}) copy-start(bf16[64,768]{1,0:T(8,128)(2,1)} %refs_1_.1) | copy-start | bytes 294916
  11.7 6.1 %collective-permute-start.9 = (bf16[64,768]{1,0:T(8,128)(2,1)S(1)}, bf16[64,768]{1,0:T(8,128)(2,1)S(1)}, u32[]{:S(2)}, u32[]{:S(2)}) collective-permute-start(bf16[64,768]{1,0:T(8,128)(2,1)S(1)} %copy-done.1), channel_id=1, source_target_pairs={{0,16},{1,17},{2,18},{3,19},{4,20},{5,21},{6,22},{7,23},{8,24},{9,... | collective-permute-start | bytes 294920 | tf_op jit(solution)/shard_map/ppermute | solution.py:49
  16.3 14.2 %collective-permute-start.6 = (bf16[64,3072]{1,0:T(8,128)(2,1)S(1)}, bf16[64,3072]{1,0:T(8,128)(2,1)S(1)}, u32[]{:S(2)}, u32[]{:S(2)}) collective-permute-start(bf16[64,3072]{1,0:T(8,128)(2,1)S(1)} %shard_map.42), channel_id=1, source_target_pairs={{0,8},{1,9},{2,10},{3,11},{4,12},{5,13},{6,14},{7,15},{8,0},{9,1},... | collective-permute-start | bytes 1179656 | tf_op jit(solution)/shard_map/ppermute | solution.py:49
  17.9 14.0 %collective-permute-start.10 = (bf16[64,3840]{1,0:T(8,128)(2,1)S(1)}, bf16[64,3840]{1,0:T(8,128)(2,1)S(1)}, u32[]{:S(2)}, u32[]{:S(2)}) collective-permute-start(bf16[64,3840]{1,0:T(8,128)(2,1)S(1)} %shard_map.44), channel_id=1, source_target_pairs={{0,4},{1,5},{2,6},{3,7},{4,0},{5,1},{6,2},{7,3},{8,12},{9,13},{10,... | collective-permute-start | bytes 1474568 | tf_op jit(solution)/shard_map/ppermute | solution.py:49
  18.0 12.4 %collective-permute-start.11 = (bf16[64,1536]{1,0:T(8,128)(2,1)S(1)}, bf16[64,1536]{1,0:T(8,128)(2,1)S(1)}, u32[]{:S(2)}, u32[]{:S(2)}) collective-permute-start(bf16[64,1536]{1,0:T(8,128)(2,1)S(1)} %shard_map.45), channel_id=1, source_target_pairs={{0,2},{1,3},{2,0},{3,1},{4,6},{5,7},{6,4},{7,5},{8,10},{9,11},{10,... | collective-permute-start | bytes 589832 | tf_op jit(solution)/shard_map/ppermute | solution.py:49
  18.4 12.1 %collective-permute-start.8 = (bf16[64,1536]{1,0:T(8,128)(2,1)S(1)}, bf16[64,1536]{1,0:T(8,128)(2,1)S(1)}, u32[]{:S(2)}, u32[]{:S(2)}) collective-permute-start(bf16[64,1536]{1,0:T(8,128)(2,1)S(1)} %collective-permute-done.1.refs_0_.refs_5_), channel_id=1, source_target_pairs={{0,16},{1,17},{2,18},{3,19},{4,20},{5,21},{6,22},{7,23},{8,24},{9,... | collective-permute-start | bytes 589832 | tf_op jit(solution)/shard_map/ppermute | solution.py:49
  19.9 11.9 %collective-permute-start.7 = (bf16[64,1536]{1,0:T(8,128)(2,1)S(1)}, bf16[64,1536]{1,0:T(8,128)(2,1)S(1)}, u32[]{:S(2)}, u32[]{:S(2)}) collective-permute-start(bf16[64,1536]{1,0:T(8,128)(2,1)S(1)} %shard_map.43), channel_id=1, source_target_pairs={{0,1},{1,0},{2,3},{3,2},{4,5},{5,4},{6,7},{7,6},{8,9},{9,8},{10,11... | collective-permute-start | bytes 589832 | tf_op jit(solution)/shard_map/ppermute | solution.py:49
  30.4 1.4 %collective-permute-start.12 = (bf16[64,1536]{1,0:T(8,128)(2,1)S(1)}, bf16[64,1536]{1,0:T(8,128)(2,1)S(1)}, u32[]{:S(2)}, u32[]{:S(2)}) collective-permute-start(bf16[64,1536]{1,0:T(8,128)(2,1)S(1)} %collective-permute-done.8.refs_7_), channel_id=1, source_target_pairs={{0,4},{1,5},{2,6},{3,7},{4,0},{5,1},{6,2},{7,3},{8,12},{9,13},{10,... | collective-permute-start | bytes 589832 | tf_op jit(solution)/shard_map/ppermute | solution.py:49
  30.4 1.7 %collective-permute-start.13 = (bf16[64,1536]{1,0:T(8,128)(2,1)S(1)}, bf16[64,1536]{1,0:T(8,128)(2,1)S(1)}, u32[]{:S(2)}, u32[]{:S(2)}) collective-permute-start(bf16[64,1536]{1,0:T(8,128)(2,1)S(1)} %collective-permute-done.11.refs_11_.refs_1_), channel_id=1, source_target_pairs={{0,4},{1,5},{2,6},{3,7},{4,0},{5,1},{6,2},{7,3},{8,12},{9,13},{10,... | collective-permute-start | bytes 589832 | tf_op jit(solution)/shard_map/ppermute | solution.py:49
  33.2 1.3 %collective-permute-start.14 = (f32[3,12,64]{2,1,0:T(8,128)S(1)}, f32[3,12,64]{2,1,0:T(8,128)S(1)}, u32[]{:S(2)}, u32[]{:S(2)}) collective-permute-start(f32[3,12,64]{2,1,0:T(8,128)S(1)} %pad_maximum_fusion), channel_id=1, source_target_pairs={{0,4},{1,5},{2,6},{3,7},{4,0},{5,1},{6,2},{7,3},{8,12},{9,13},{10,... | collective-permute-start | bytes 27656 | tf_op jit(solution)/shard_map/ppermute | solution.py:49
  34.5 3.8 %collective-permute-start.15 = (f32[3,8,64]{2,1,0:T(8,128)S(1)}, f32[3,8,64]{2,1,0:T(8,128)S(1)}, u32[]{:S(2)}, u32[]{:S(2)}) collective-permute-start(f32[3,8,64]{2,1,0:T(8,128)S(1)} %maximum_select_fusion), channel_id=1, source_target_pairs={{0,1},{1,0},{2,3},{3,2},{4,6},{5,7},{6,4},{7,5},{8,9},{9,8},{10,11... | collective-permute-start | bytes 18440 | tf_op jit(solution)/shard_map/ppermute | solution.py:260
  38.3 3.8 %collective-permute-start.16 = (f32[3,8,64]{2,1,0:T(8,128)S(1)}, f32[3,8,64]{2,1,0:T(8,128)S(1)}, u32[]{:S(2)}, u32[]{:S(2)}) collective-permute-start(f32[3,8,64]{2,1,0:T(8,128)S(1)} %add.10), channel_id=1, source_target_pairs={{0,8},{1,9},{2,10},{3,11},{4,20},{5,21},{6,22},{7,23},{8,0},{9,1},... | collective-permute-start | bytes 18440 | tf_op jit(solution)/shard_map/ppermute | solution.py:260
  42.1 1.2 %collective-permute-start.17 = (f32[3,8,64]{2,1,0:T(8,128)S(1)}, f32[3,8,64]{2,1,0:T(8,128)S(1)}, u32[]{:S(2)}, u32[]{:S(2)}) collective-permute-start(f32[3,8,64]{2,1,0:T(8,128)S(1)} %add.11), channel_id=1, source_target_pairs={{0,4},{1,5},{2,6},{3,7},{4,0},{5,1},{6,2},{7,3},{8,12},{9,13},{10,... | collective-permute-start | bytes 18440 | tf_op jit(solution)/shard_map/ppermute | solution.py:49
  44.4 6.1 %collective-permute-start.18 = (f16[64,896]{1,0:T(8,128)(2,1)S(1)}, f16[64,896]{1,0:T(8,128)(2,1)S(1)}, u32[]{:S(2)}, u32[]{:S(2)}) collective-permute-start(f16[64,896]{1,0:T(8,128)(2,1)S(1)} %convert_element_type.18), channel_id=1, source_target_pairs={{0,1},{1,0},{2,3},{3,2},{4,5},{5,4},{6,7},{7,6},{8,9},{9,8},{10,11... | collective-permute-start | bytes 344072 | tf_op jit(solution)/shard_map/ppermute | solution.py:49
  44.5 7.7 %collective-permute-start.19 = (f16[64,896]{1,0:T(8,128)(2,1)S(1)}, f16[64,896]{1,0:T(8,128)(2,1)S(1)}, u32[]{:S(2)}, u32[]{:S(2)}) collective-permute-start(f16[64,896]{1,0:T(8,128)(2,1)S(1)} %convert_element_type.20), channel_id=1, source_target_pairs={{0,8},{1,9},{2,10},{3,11},{4,12},{5,13},{6,14},{7,15},{8,0},{9,1},... | collective-permute-start | bytes 344072 | tf_op jit(solution)/shard_map/ppermute | solution.py:49
  45.1 7.1 %collective-permute-start.20 = (f16[64,896]{1,0:T(8,128)(2,1)S(1)}, f16[64,896]{1,0:T(8,128)(2,1)S(1)}, u32[]{:S(2)}, u32[]{:S(2)}) collective-permute-start(f16[64,896]{1,0:T(8,128)(2,1)S(1)} %convert_element_type.22), channel_id=1, source_target_pairs={{0,9},{1,8},{2,11},{3,10},{4,13},{5,12},{6,15},{7,14},{8,1},{9,0},... | collective-permute-start | bytes 344072 | tf_op jit(solution)/shard_map/ppermute | solution.py:49

commit v19 on v17

--- a/solution.py
+++ b/solution.py
@@ -12,6 +12,7 @@
 AXES = ("blk", "inner")
 VMEM = 48 * 2**20
 SHARE_SCALE = 8.0
+EXTRA = 16
 
 
 EPSILON = 1e-06
@@ -207,26 +208,30 @@
     term = jnp.sum(terms, axis=1, keepdims=True)
     share[...] = jnp.broadcast_to(term, share.shape)
     largest = jnp.max(jnp.max(jnp.abs(out), axis=0, keepdims=True), axis=1, keepdims=True)
-    power = jnp.clip(jnp.floor(jnp.log2(largest)), -100.0, 100.0)
+    power = jnp.clip(jnp.floor(jnp.log2(jnp.maximum(largest, 1e-30))), -100.0, 100.0)
     term = term * SHARE_SCALE
     high = term.astype(jnp.bfloat16).astype(jnp.float32)
     middle = (term - high).astype(jnp.bfloat16).astype(jnp.float32)
     low = term - high - middle
-    lane = lax.broadcasted_iota(jnp.int32, (rows, 128), 1)
+    lane = lax.broadcasted_iota(jnp.int32, (EXTRA, 128), 1)
     extra = jnp.where(lane == 0, power, jnp.where(lane == 1, high, jnp.where(lane == 2, middle, low)))
     scaled = out * jnp.exp2(13.0 - power)
     for k, piece in enumerate(pieces):
-        piece[:, :width] = scaled[(k + 1) * rows : (k + 2) * rows]
-        piece[:, width:] = extra
+        for c in range(width // 128):
+            block = scaled[(k + 1) * rows : (k + 2) * rows, c * 128 : (c + 1) * 128]
+            piece[c * rows : (c + 1) * rows, :] = block
+        piece[width // 128 * rows :, :] = extra
 
 
 def final_kernel(total, own, share, *refs):
     *pieces, grad, loss = refs
     width = own.shape[1]
     grads, terms = [own[...]], [share[0:1, 0:1]]
+    rows = own.shape[0]
     for piece in pieces:
-        extra = piece[:, width:]
-        grads.append(piece[:, :width] * jnp.exp2(extra[:, 0:1] - 13.0))
+        extra = piece[width // 128 * rows :, :]
+        blocks = [piece[c * rows : (c + 1) * rows, :] for c in range(width // 128)]
+        grads.append(jnp.concatenate(blocks, 1) * jnp.exp2(extra[0:1, 0:1] - 13.0))
         terms.append((extra[0:1, 1:2] + extra[0:1, 2:3] + extra[0:1, 3:4]) * (1.0 / SHARE_SCALE))
     grad[...] = tree_sum(grads)
     loss[...] = tree_sum(terms) * (1.0 / total)
@@ -289,7 +294,7 @@
     own, share, *pieces = call(
         functools.partial(output_kernel, len(arrays), group, total),
         [gram_s, gram_t, row_sum, col_sum, *arrays],
-        [f32(rows, width), f32(8, 128)] + [f32(rows, width + 128)] * (n_row - 1),
+        [f32(rows, width), f32(8, 128)] + [f32(width // 128 * rows + EXTRA, 128)] * (n_row - 1),
         4 * math.prod(shape) * width,
     )
     got = [

time: 53 us -> 52.7 us (level)
  transfers between devices with their start and end apart: 21 -> 21, of which waited for: 10 -> 11; matrix products, arithmetic and copies ran while one was open for 0% -> 0% of each run, Pallas kernels for 0% -> 0%
where the time goes in v19:
time: 52.7 us; the launch traced here: 52.5 us
  waiting for transfers between devices  26.9 us (51%)
  starting transfers between devices  21.5 us (41%)
  Pallas kernels  2.86 us (5%)
  between operations  0.83 us (2%)
    ppermute x19, waiting for transfers between devices, send(): return lax.ppermute(value, AXES, [(i, i ^ mask) for i in range(count)])  20.6 us
    ppermute x19, starting transfers between devices, send(): return lax.ppermute(value, AXES, [(i, i ^ mask) for i in range(count)])  20.3 us
    ppermute x2, waiting for transfers between devices, exchange_sums(): got = lax.ppermute(sums, AXES, pairs).reshape(3, -1, 2, 1 << b, rows)  6.32 us
    pallas_call x8, Pallas kernels, call(): pl.pallas_call(kernel, out_shape=outputs, **options, compiler_params=pltp...  2.86 us
    ppermute x2, starting transfers between devices, exchange_sums(): got = lax.ppermute(sums, AXES, pairs).reshape(3, -1, 2, 1 << b, rows)  1.2 us
  transfers between devices with their start and end apart: 21, of which 11 were waited for; matrix products, arithmetic and copies ran while one was open for 0% of the time, Pallas kernels for 0%

profile of v19, /device:TPU:0, one launch (start us, length us, event | category | flops | bytes accessed | tf_op | source)
XLA Modules:
  0.0 52.5 jit_solution(17798690147016246712)
XLA Ops:
  0.6 0.5 collective-permute-start.2
  1.2 3.0 %collective-permute-start = (bf16[64,1536]{1,0:T(8,128)(2,1)}, bf16[64,1536]{1,0:T(8,128)(2,1)S(1)}, u32[]{:S(2)}, u32[]{:S(2)}) collective-permute-start(bf16[64,1536]{1,0:T(8,128)(2,1)} %refs_0_.1), channel_id=1, source_target_pairs={{0,1},{1,0},{2,3},{3,2},{4,5},{5,4},{6,7},{7,6},{8,9},{9,8},{10,11... | collective-permute-start | bytes 589832 | tf_op jit(solution)/shard_map/ppermute | solution.py:50
  4.2 2.6 %collective-permute-start.1 = (bf16[64,1536]{1,0:T(8,128)(2,1)}, bf16[64,1536]{1,0:T(8,128)(2,1)S(1)}, u32[]{:S(2)}, u32[]{:S(2)}) collective-permute-start(bf16[64,1536]{1,0:T(8,128)(2,1)} %refs_0_.1), channel_id=1, source_target_pairs={{0,2},{1,3},{2,0},{3,1},{4,6},{5,7},{6,4},{7,5},{8,10},{9,11},{10,... | collective-permute-start | bytes 589832 | tf_op jit(solution)/shard_map/ppermute | solution.py:50
  6.8 1.5 %collective-permute-start.4 = (bf16[64,1536]{1,0:T(8,128)(2,1)}, bf16[64,1536]{1,0:T(8,128)(2,1)S(1)}, u32[]{:S(2)}, u32[]{:S(2)}) collective-permute-start(bf16[64,1536]{1,0:T(8,128)(2,1)} %refs_0_.1), channel_id=1, source_target_pairs={{0,16},{1,17},{2,18},{3,19},{4,20},{5,21},{6,22},{7,23},{8,24},{9,... | collective-permute-start | bytes 589832 | tf_op jit(solution)/shard_map/ppermute | solution.py:50
  8.4 0.5 collective-permute-start.9
  8.9 1.5 %collective-permute-start.6 = (bf16[64,768]{1,0:T(8,128)(2,1)}, bf16[64,768]{1,0:T(8,128)(2,1)S(1)}, u32[]{:S(2)}, u32[]{:S(2)}) collective-permute-start(bf16[64,768]{1,0:T(8,128)(2,1)} %refs_1_.1), channel_id=1, source_target_pairs={{0,8},{1,9},{2,10},{3,11},{4,12},{5,13},{6,14},{7,15},{8,0},{9,1},... | collective-permute-start | bytes 294920 | tf_op jit(solution)/shard_map/ppermute | solution.py:50
  10.4 3.3 %collective-permute-done.refs_1_ = bf16[64,1536]{1,0:T(8,128)(2,1)S(1)} collective-permute-done((bf16[64,1536]{1,0:T(8,128)(2,1)}, bf16[64,1536]{1,0:T(8,128)(2,1)S(1)}, u32[]{:S(2)}, u32[]{:S(2)}) %collective-permute-start) | collective-permute-done | bytes 196640 | tf_op jit(solution)/shard_map/ppermute | solution.py:50
  13.7 2.6 %collective-permute-done.1.refs_0_.refs_5_ = bf16[64,1536]{1,0:T(8,128)(2,1)S(1)} collective-permute-done((bf16[64,1536]{1,0:T(8,128)(2,1)}, bf16[64,1536]{1,0:T(8,128)(2,1)S(1)}, u32[]{:S(2)}, u32[]{:S(2)}) %collective-permute-start.1) | collective-permute-done | bytes 196640 | tf_op jit(solution)/shard_map/ppermute | solution.py:50
  16.5 0.4 collective-permute-start.12
  16.9 1.5 %collective-permute-start.8 = (bf16[64,1536]{1,0:T(8,128)(2,1)S(1)}, bf16[64,1536]{1,0:T(8,128)(2,1)S(1)}, u32[]{:S(2)}, u32[]{:S(2)}) collective-permute-start(bf16[64,1536]{1,0:T(8,128)(2,1)S(1)} %collective-permute-done.1.refs_0_.refs_5_), channel_id=1, source_target_pairs={{0,16},{1,17},{2,18},{3,19},{4,20},{5,21},{6,22},{7,23},{8,24},{9,... | collective-permute-start | bytes 589832 | tf_op jit(solution)/shard_map/ppermute | solution.py:50
  18.4 1.6 %collective-permute-start.5 = (bf16[64,3072]{1,0:T(8,128)(2,1)S(1)}, bf16[64,3072]{1,0:T(8,128)(2,1)S(1)}, u32[]{:S(2)}, u32[]{:S(2)}) collective-permute-start(bf16[64,3072]{1,0:T(8,128)(2,1)S(1)} %shard_map.42), channel_id=1, source_target_pairs={{0,8},{1,9},{2,10},{3,11},{4,12},{5,13},{6,14},{7,15},{8,0},{9,1},... | collective-permute-start | bytes 1179656 | tf_op jit(solution)/shard_map/ppermute | solution.py:50
  20.0 2.8 %collective-permute-start.7 = (bf16[64,1536]{1,0:T(8,128)(2,1)S(1)}, bf16[64,1536]{1,0:T(8,128)(2,1)S(1)}, u32[]{:S(2)}, u32[]{:S(2)}) collective-permute-start(bf16[64,1536]{1,0:T(8,128)(2,1)S(1)} %shard_map.43), channel_id=1, source_target_pairs={{0,1},{1,0},{2,3},{3,2},{4,5},{5,4},{6,7},{7,6},{8,9},{9,8},{10,11... | collective-permute-start | bytes 589832 | tf_op jit(solution)/shard_map/ppermute | solution.py:50
  22.8 6.2 %collective-permute-done.12.refs_11_.refs_1_ = bf16[64,1536]{1,0:T(8,128)(2,1)S(1)} collective-permute-done((bf16[64,1536]{1,0:T(8,128)(2,1)S(1)}, bf16[64,1536]{1,0:T(8,128)(2,1)S(1)}, u32[]{:S(2)}, u32[]{:S(2)}) %collective-permute-start.12) | collective-permute-done | bytes 196640 | tf_op jit(solution)/shard_map/ppermute | solution.py:50
  28.9 0.5 collective-permute-start.11
  29.4 2.1 %collective-permute-done.7.refs_3_ = bf16[64,1536]{1,0:T(8,128)(2,1)S(1)} collective-permute-done((bf16[64,1536]{1,0:T(8,128)(2,1)S(1)}, bf16[64,1536]{1,0:T(8,128)(2,1)S(1)}, u32[]{:S(2)}, u32[]{:S(2)}) %collective-permute-start.7) | collective-permute-done | bytes 196640 | tf_op jit(solution)/shard_map/ppermute | solution.py:50
  31.6 1.0 %shard_map.46 = (f32[256,512]{1,0:T(8,128)S(1)}, f32[256,512]{1,0:T(8,128)S(1)}, f32[3,4,64]{2,1,0:T(4,128)S(1)}, f32[3,8,64]{2,1,0:T(8,128)S(1)}) custom-call(bf16[64,2304]{1,0:T(8,128)(2,1)S(1)} %shard_map.41.refs_0_, bf16[64,1536]{1,0:T(8,128)(2,1)S(1)} %collective-permute-done.refs_1_, bf16[64,3072]{1,0:T(8,128)(2,1)S(1)} %collective-permute-done.5.refs_2_, ...), custom_call_target="tpu_custom_call" | custom-call | flops 603979776 | bytes 4301824 | tf_op jit(solution)/shard_map/pallas_call | solution.py:186
  32.7 1.2 %collective-permute-done.14 = f32[3,12,64]{2,1,0:T(8,128)S(1)} collective-permute-done((f32[3,12,64]{2,1,0:T(8,128)S(1)}, f32[3,12,64]{2,1,0:T(8,128)S(1)}, u32[]{:S(2)}, u32[]{:S(2)}) %collective-permute-start.14) | collective-permute-done | bytes 9248 | tf_op jit(solution)/shard_map/ppermute | solution.py:50
  33.9 0.6 %collective-permute-start.15 = (f32[3,8,64]{2,1,0:T(8,128)S(1)}, f32[3,8,64]{2,1,0:T(8,128)S(1)}, u32[]{:S(2)}, u32[]{:S(2)}) collective-permute-start(f32[3,8,64]{2,1,0:T(8,128)S(1)} %maximum_select_fusion), channel_id=1, source_target_pairs={{0,1},{1,0},{2,3},{3,2},{4,6},{5,7},{6,4},{7,5},{8,9},{9,8},{10,11... | collective-permute-start | bytes 18440 | tf_op jit(solution)/shard_map/ppermute | solution.py:259
  34.5 3.2 %collective-permute-done.15 = f32[3,8,64]{2,1,0:T(8,128)S(1)} collective-permute-done((f32[3,8,64]{2,1,0:T(8,128)S(1)}, f32[3,8,64]{2,1,0:T(8,128)S(1)}, u32[]{:S(2)}, u32[]{:S(2)}) %collective-permute-start.15) | collective-permute-done | bytes 6176 | tf_op jit(solution)/shard_map/ppermute | solution.py:259
  37.8 0.6 %collective-permute-start.16 = (f32[3,8,64]{2,1,0:T(8,128)S(1)}, f32[3,8,64]{2,1,0:T(8,128)S(1)}, u32[]{:S(2)}, u32[]{:S(2)}) collective-permute-start(f32[3,8,64]{2,1,0:T(8,128)S(1)} %add.10), channel_id=1, source_target_pairs={{0,8},{1,9},{2,10},{3,11},{4,20},{5,21},{6,22},{7,23},{8,0},{9,1},... | collective-permute-start | bytes 18440 | tf_op jit(solution)/shard_map/ppermute | solution.py:259
  38.4 3.2 %collective-permute-done.16 = f32[3,8,64]{2,1,0:T(8,128)S(1)} collective-permute-done((f32[3,8,64]{2,1,0:T(8,128)S(1)}, f32[3,8,64]{2,1,0:T(8,128)S(1)}, u32[]{:S(2)}, u32[]{:S(2)}) %collective-permute-start.16) | collective-permute-done | bytes 6176 | tf_op jit(solution)/shard_map/ppermute | solution.py:259
  41.6 1.2 %collective-permute-done.17 = f32[3,8,64]{2,1,0:T(8,128)S(1)} collective-permute-done((f32[3,8,64]{2,1,0:T(8,128)S(1)}, f32[3,8,64]{2,1,0:T(8,128)S(1)}, u32[]{:S(2)}, u32[]{:S(2)}) %collective-permute-start.17) | collective-permute-done | bytes 6176 | tf_op jit(solution)/shard_map/ppermute | solution.py:50
  42.8 0.1 reshape.27.col_sum
  42.9 0.1 reshape.26.row_sum
  43.0 0.9 %shard_map.47 = (f32[64,768]{1,0:T(8,128)S(1)}, f32[8,128]{1,0:T(8,128)S(1)}, f32[400,128]{1,0:T(8,128)S(1)}, f32[400,128]{1,0:T(8,128)S(1)}, f32[400,128]{1,0:T(8,128)S(1)}) custom-call(f32[256,512]{1,0:T(8,128)S(1)} %get-tuple-element.25.gram_s, f32[256,512]{1,0:T(8,128)S(1)} %get-tuple-element.26.gram_t, f32[3,1,256]{2,1,0:T(1,128)S(1)} %reshape.26.row_sum, ...), custom_call_target="tpu_custom_call" | custom-call | flops 402653184 | bytes 3249152 | tf_op jit(solution)/shard_map/pallas_call | solution.py:186
  43.9 0.6 %collective-permute-start.18 = (f16[400,128]{1,0:T(8,128)(2,1)S(1)}, f16[400,128]{1,0:T(8,128)(2,1)S(1)}, u32[]{:S(2)}, u32[]{:S(2)}) collective-permute-start(f16[400,128]{1,0:T(8,128)(2,1)S(1)} %convert_element_type.18), channel_id=1, source_target_pairs={{0,1},{1,0},{2,3},{3,2},{4,5},{5,4},{6,7},{7,6},{8,9},{9,8},{10,11... | collective-permute-start | bytes 307208 | tf_op jit(solution)/shard_map/ppermute | solution.py:50
  44.5 1.6 %collective-permute-start.19 = (f16[400,128]{1,0:T(8,128)(2,1)S(1)}, f16[400,128]{1,0:T(8,128)(2,1)S(1)}, u32[]{:S(2)}, u32[]{:S(2)}) collective-permute-start(f16[400,128]{1,0:T(8,128)(2,1)S(1)} %convert_element_type.20), channel_id=1, source_target_pairs={{0,8},{1,9},{2,10},{3,11},{4,12},{5,13},{6,14},{7,15},{8,0},{9,1},... | collective-permute-start | bytes 307208 | tf_op jit(solution)/shard_map/ppermute | solution.py:50
  46.1 1.5 %collective-permute-start.20 = (f16[400,128]{1,0:T(8,128)(2,1)S(1)}, f16[400,128]{1,0:T(8,128)(2,1)S(1)}, u32[]{:S(2)}, u32[]{:S(2)}) collective-permute-start(f16[400,128]{1,0:T(8,128)(2,1)S(1)} %convert_element_type.22), channel_id=1, source_target_pairs={{0,9},{1,8},{2,11},{3,10},{4,13},{5,12},{6,15},{7,14},{8,1},{9,0},... | collective-permute-start | bytes 307208 | tf_op jit(solution)/shard_map/ppermute | solution.py:50
  47.6 1.9 %collective-permute-done.18 = f16[400,128]{1,0:T(8,128)(2,1)S(1)} collective-permute-done((f16[400,128]{1,0:T(8,128)(2,1)S(1)}, f16[400,128]{1,0:T(8,128)(2,1)S(1)}, u32[]{:S(2)}, u32[]{:S(2)}) %collective-permute-start.18) | collective-permute-done | bytes 102432 | tf_op jit(solution)/shard_map/ppermute | solution.py:50
  49.6 0.9 %collective-permute-done.19 = f16[400,128]{1,0:T(8,128)(2,1)S(1)} collective-permute-done((f16[400,128]{1,0:T(8,128)(2,1)S(1)}, f16[400,128]{1,0:T(8,128)(2,1)S(1)}, u32[]{:S(2)}, u32[]{:S(2)}) %collective-permute-start.19) | collective-permute-done | bytes 102432 | tf_op jit(solution)/shard_map/ppermute | solution.py:50
  50.5 1.2 %collective-permute-done.20 = f16[400,128]{1,0:T(8,128)(2,1)S(1)} collective-permute-done((f16[400,128]{1,0:T(8,128)(2,1)S(1)}, f16[400,128]{1,0:T(8,128)(2,1)S(1)}, u32[]{:S(2)}, u32[]{:S(2)}) %collective-permute-start.20) | collective-permute-done | bytes 102432 | tf_op jit(solution)/shard_map/ppermute | solution.py:50
  51.7 0.8 %shard_map.48 = (f32[64,768]{1,0:T(8,128)}, f32[1,1]{1,0:T(1,128)}) custom-call(f32[64,768]{1,0:T(8,128)S(1)} %get-tuple-element.29.own, f32[8,128]{1,0:T(8,128)S(1)} %get-tuple-element.30.share, f32[400,128]{1,0:T(8,128)S(1)} %convert_element_type.19.refs_0_, f32[400,128]{1,0:T(8,128)S(1)} %convert_element_type.21.refs_1_, ...), custom_call_target="tpu_custom_call" | custom-call | bytes 1011716 | tf_op jit(solution)/shard_map/pallas_call | solution.py:186
  (41 shorter events, 0.7 us)
Async XLA Ops:
  0.6 15.7 %copy-start = (bf16[64,1536]{1,0:T(8,128)(2,1)S(1)}, bf16[64,1536]{1,0:T(8,128)(2,1)}, u32[]{:S(2)}) copy-start(bf16[64,1536]{1,0:T(8,128)(2,1)} %refs_0_.1) | copy-start | bytes 589828
  0.6 15.7 %copy-start.1 = (bf16[64,768]{1,0:T(8,128)(2,1)S(1)}, bf16[64,768]{1,0:T(8,128)(2,1)}, u32[]{:S(2)}) copy-start(bf16[64,768]{1,0:T(8,128)(2,1)} %refs_1_.1) | copy-start | bytes 294916
  0.6 6.2 %collective-permute-start.2 = (bf16[64,1536]{1,0:T(8,128)(2,1)}, bf16[64,1536]{1,0:T(8,128)(2,1)S(1)}, u32[]{:S(2)}, u32[]{:S(2)}) collective-permute-start(bf16[64,1536]{1,0:T(8,128)(2,1)} %refs_0_.1), channel_id=1, source_target_pairs={{0,4},{1,5},{2,6},{3,7},{4,0},{5,1},{6,2},{7,3},{8,12},{9,13},{10,... | collective-permute-start | bytes 589832 | tf_op jit(solution)/shard_map/ppermute | solution.py:50
  1.2 5.7 %collective-permute-start.3 = (bf16[64,768]{1,0:T(8,128)(2,1)}, bf16[64,768]{1,0:T(8,128)(2,1)S(1)}, u32[]{:S(2)}, u32[]{:S(2)}) collective-permute-start(bf16[64,768]{1,0:T(8,128)(2,1)} %refs_1_.1), channel_id=1, source_target_pairs={{0,4},{1,5},{2,6},{3,7},{4,0},{5,1},{6,2},{7,3},{8,12},{9,13},{10,... | collective-permute-start | bytes 294920 | tf_op jit(solution)/shard_map/ppermute | solution.py:50
  1.2 12.4 %collective-permute-start = (bf16[64,1536]{1,0:T(8,128)(2,1)}, bf16[64,1536]{1,0:T(8,128)(2,1)S(1)}, u32[]{:S(2)}, u32[]{:S(2)}) collective-permute-start(bf16[64,1536]{1,0:T(8,128)(2,1)} %refs_0_.1), channel_id=1, source_target_pairs={{0,1},{1,0},{2,3},{3,2},{4,5},{5,4},{6,7},{7,6},{8,9},{9,8},{10,11... | collective-permute-start | bytes 589832 | tf_op jit(solution)/shard_map/ppermute | solution.py:50
  4.2 12.0 %collective-permute-start.1 = (bf16[64,1536]{1,0:T(8,128)(2,1)}, bf16[64,1536]{1,0:T(8,128)(2,1)S(1)}, u32[]{:S(2)}, u32[]{:S(2)}) collective-permute-start(bf16[64,1536]{1,0:T(8,128)(2,1)} %refs_0_.1), channel_id=1, source_target_pairs={{0,2},{1,3},{2,0},{3,1},{4,6},{5,7},{6,4},{7,5},{8,10},{9,11},{10,... | collective-permute-start | bytes 589832 | tf_op jit(solution)/shard_map/ppermute | solution.py:50
  6.8 9.4 %collective-permute-start.4 = (bf16[64,1536]{1,0:T(8,128)(2,1)}, bf16[64,1536]{1,0:T(8,128)(2,1)S(1)}, u32[]{:S(2)}, u32[]{:S(2)}) collective-permute-start(bf16[64,1536]{1,0:T(8,128)(2,1)} %refs_0_.1), channel_id=1, source_target_pairs={{0,16},{1,17},{2,18},{3,19},{4,20},{5,21},{6,22},{7,23},{8,24},{9,... | collective-permute-start | bytes 589832 | tf_op jit(solution)/shard_map/ppermute | solution.py:50
  8.4 7.9 %collective-permute-start.9 = (bf16[64,768]{1,0:T(8,128)(2,1)}, bf16[64,768]{1,0:T(8,128)(2,1)S(1)}, u32[]{:S(2)}, u32[]{:S(2)}) collective-permute-start(bf16[64,768]{1,0:T(8,128)(2,1)} %refs_1_.1), channel_id=1, source_target_pairs={{0,16},{1,17},{2,18},{3,19},{4,20},{5,21},{6,22},{7,23},{8,24},{9,... | collective-permute-start | bytes 294920 | tf_op jit(solution)/shard_map/ppermute | solution.py:50
  8.9 7.6 %collective-permute-start.6 = (bf16[64,768]{1,0:T(8,128)(2,1)}, bf16[64,768]{1,0:T(8,128)(2,1)S(1)}, u32[]{:S(2)}, u32[]{:S(2)}) collective-permute-start(bf16[64,768]{1,0:T(8,128)(2,1)} %refs_1_.1), channel_id=1, source_target_pairs={{0,8},{1,9},{2,10},{3,11},{4,12},{5,13},{6,14},{7,15},{8,0},{9,1},... | collective-permute-start | bytes 294920 | tf_op jit(solution)/shard_map/ppermute | solution.py:50
  16.3 15.3 %collective-permute-start.10 = (bf16[64,3840]{1,0:T(8,128)(2,1)S(1)}, bf16[64,3840]{1,0:T(8,128)(2,1)S(1)}, u32[]{:S(2)}, u32[]{:S(2)}) collective-permute-start(bf16[64,3840]{1,0:T(8,128)(2,1)S(1)} %shard_map.44), channel_id=1, source_target_pairs={{0,4},{1,5},{2,6},{3,7},{4,0},{5,1},{6,2},{7,3},{8,12},{9,13},{10,... | collective-permute-start | bytes 1474568 | tf_op jit(solution)/shard_map/ppermute | solution.py:50
  16.5 12.4 %collective-permute-start.12 = (bf16[64,1536]{1,0:T(8,128)(2,1)S(1)}, bf16[64,1536]{1,0:T(8,128)(2,1)S(1)}, u32[]{:S(2)}, u32[]{:S(2)}) collective-permute-start(bf16[64,1536]{1,0:T(8,128)(2,1)S(1)} %shard_map.45), channel_id=1, source_target_pairs={{0,2},{1,3},{2,0},{3,1},{4,6},{5,7},{6,4},{7,5},{8,10},{9,11},{10,... | collective-permute-start | bytes 589832 | tf_op jit(solution)/shard_map/ppermute | solution.py:50
  16.9 12.1 %collective-permute-start.8 = (bf16[64,1536]{1,0:T(8,128)(2,1)S(1)}, bf16[64,1536]{1,0:T(8,128)(2,1)S(1)}, u32[]{:S(2)}, u32[]{:S(2)}) collective-permute-start(bf16[64,1536]{1,0:T(8,128)(2,1)S(1)} %collective-permute-done.1.refs_0_.refs_5_), channel_id=1, source_target_pairs={{0,16},{1,17},{2,18},{3,19},{4,20},{5,21},{6,22},{7,23},{8,24},{9,... | collective-permute-start | bytes 589832 | tf_op jit(solution)/shard_map/ppermute | solution.py:50
  18.4 13.2 %collective-permute-start.5 = (bf16[64,3072]{1,0:T(8,128)(2,1)S(1)}, bf16[64,3072]{1,0:T(8,128)(2,1)S(1)}, u32[]{:S(2)}, u32[]{:S(2)}) collective-permute-start(bf16[64,3072]{1,0:T(8,128)(2,1)S(1)} %shard_map.42), channel_id=1, source_target_pairs={{0,8},{1,9},{2,10},{3,11},{4,12},{5,13},{6,14},{7,15},{8,0},{9,1},... | collective-permute-start | bytes 1179656 | tf_op jit(solution)/shard_map/ppermute | solution.py:50
  20.0 11.6 %collective-permute-start.7 = (bf16[64,1536]{1,0:T(8,128)(2,1)S(1)}, bf16[64,1536]{1,0:T(8,128)(2,1)S(1)}, u32[]{:S(2)}, u32[]{:S(2)}) collective-permute-start(bf16[64,1536]{1,0:T(8,128)(2,1)S(1)} %shard_map.43), channel_id=1, source_target_pairs={{0,1},{1,0},{2,3},{3,2},{4,5},{5,4},{6,7},{7,6},{8,9},{9,8},{10,11... | collective-permute-start | bytes 589832 | tf_op jit(solution)/shard_map/ppermute | solution.py:50
  28.9 2.7 %collective-permute-start.13 = (bf16[64,1536]{1,0:T(8,128)(2,1)S(1)}, bf16[64,1536]{1,0:T(8,128)(2,1)S(1)}, u32[]{:S(2)}, u32[]{:S(2)}) collective-permute-start(bf16[64,1536]{1,0:T(8,128)(2,1)S(1)} %collective-permute-done.12.refs_11_.refs_1_), channel_id=1, source_target_pairs={{0,4},{1,5},{2,6},{3,7},{4,0},{5,1},{6,2},{7,3},{8,12},{9,13},{10,... | collective-permute-start | bytes 589832 | tf_op jit(solution)/shard_map/ppermute | solution.py:50
  28.9 2.6 %collective-permute-start.11 = (bf16[64,1536]{1,0:T(8,128)(2,1)S(1)}, bf16[64,1536]{1,0:T(8,128)(2,1)S(1)}, u32[]{:S(2)}, u32[]{:S(2)}) collective-permute-start(bf16[64,1536]{1,0:T(8,128)(2,1)S(1)} %collective-permute-done.8.refs_7_), channel_id=1, source_target_pairs={{0,4},{1,5},{2,6},{3,7},{4,0},{5,1},{6,2},{7,3},{8,12},{9,13},{10,... | collective-permute-start | bytes 589832 | tf_op jit(solution)/shard_map/ppermute | solution.py:50
  32.7 1.3 %collective-permute-start.14 = (f32[3,12,64]{2,1,0:T(8,128)S(1)}, f32[3,12,64]{2,1,0:T(8,128)S(1)}, u32[]{:S(2)}, u32[]{:S(2)}) collective-permute-start(f32[3,12,64]{2,1,0:T(8,128)S(1)} %pad_maximum_fusion), channel_id=1, source_target_pairs={{0,4},{1,5},{2,6},{3,7},{4,0},{5,1},{6,2},{7,3},{8,12},{9,13},{10,... | collective-permute-start | bytes 27656 | tf_op jit(solution)/shard_map/ppermute | solution.py:50
  33.9 3.8 %collective-permute-start.15 = (f32[3,8,64]{2,1,0:T(8,128)S(1)}, f32[3,8,64]{2,1,0:T(8,128)S(1)}, u32[]{:S(2)}, u32[]{:S(2)}) collective-permute-start(f32[3,8,64]{2,1,0:T(8,128)S(1)} %maximum_select_fusion), channel_id=1, source_target_pairs={{0,1},{1,0},{2,3},{3,2},{4,6},{5,7},{6,4},{7,5},{8,9},{9,8},{10,11... | collective-permute-start | bytes 18440 | tf_op jit(solution)/shard_map/ppermute | solution.py:259
  37.8 3.8 %collective-permute-start.16 = (f32[3,8,64]{2,1,0:T(8,128)S(1)}, f32[3,8,64]{2,1,0:T(8,128)S(1)}, u32[]{:S(2)}, u32[]{:S(2)}) collective-permute-start(f32[3,8,64]{2,1,0:T(8,128)S(1)} %add.10), channel_id=1, source_target_pairs={{0,8},{1,9},{2,10},{3,11},{4,20},{5,21},{6,22},{7,23},{8,0},{9,1},... | collective-permute-start | bytes 18440 | tf_op jit(solution)/shard_map/ppermute | solution.py:259
  41.5 1.2 %collective-permute-start.17 = (f32[3,8,64]{2,1,0:T(8,128)S(1)}, f32[3,8,64]{2,1,0:T(8,128)S(1)}, u32[]{:S(2)}, u32[]{:S(2)}) collective-permute-start(f32[3,8,64]{2,1,0:T(8,128)S(1)} %add.11), channel_id=1, source_target_pairs={{0,4},{1,5},{2,6},{3,7},{4,0},{5,1},{6,2},{7,3},{8,12},{9,13},{10,... | collective-permute-start | bytes 18440 | tf_op jit(solution)/shard_map/ppermute | solution.py:50
  43.9 5.6 %collective-permute-start.18 = (f16[400,128]{1,0:T(8,128)(2,1)S(1)}, f16[400,128]{1,0:T(8,128)(2,1)S(1)}, u32[]{:S(2)}, u32[]{:S(2)}) collective-permute-start(f16[400,128]{1,0:T(8,128)(2,1)S(1)} %convert_element_type.18), channel_id=1, source_target_pairs={{0,1},{1,0},{2,3},{3,2},{4,5},{5,4},{6,7},{7,6},{8,9},{9,8},{10,11... | collective-permute-start | bytes 307208 | tf_op jit(solution)/shard_map/ppermute | solution.py:50
  44.5 6.0 %collective-permute-start.19 = (f16[400,128]{1,0:T(8,128)(2,1)S(1)}, f16[400,128]{1,0:T(8,128)(2,1)S(1)}, u32[]{:S(2)}, u32[]{:S(2)}) collective-permute-start(f16[400,128]{1,0:T(8,128)(2,1)S(1)} %convert_element_type.20), channel_id=1, source_target_pairs={{0,8},{1,9},{2,10},{3,11},{4,12},{5,13},{6,14},{7,15},{8,0},{9,1},... | collective-permute-start | bytes 307208 | tf_op jit(solution)/shard_map/ppermute | solution.py:50
  46.1 5.6 %collective-permute-start.20 = (f16[400,128]{1,0:T(8,128)(2,1)S(1)}, f16[400,128]{1,0:T(8,128)(2,1)S(1)}, u32[]{:S(2)}, u32[]{:S(2)}) collective-permute-start(f16[400,128]{1,0:T(8,128)(2,1)S(1)} %convert_element_type.22), channel_id=1, source_target_pairs={{0,9},{1,8},{2,11},{3,10},{4,13},{5,12},{6,15},{7,14},{8,1},{9,0},... | collective-permute-start | bytes 307208 | tf_op jit(solution)/shard_map/ppermute | solution.py:50

commit v20 on v19

--- a/solution.py
+++ b/solution.py
@@ -74,11 +74,11 @@
                     top = place.bit_length() - 1
                     side[place] = whole(send(side[place ^ (1 << top)][0], masks[top], count))
 
-    for side_t, _, masks in reversed(sides):
-        side_t[1] = whole(send(teacher, masks[0], count))
+    col_t[1] = whole(send(teacher, plane_masks[0], count))
     swapped = [send(value, core_mask, count) for value in (teacher, student)]
     own = join(teacher, student)
     late_t, late_s = after((teacher, student), swapped)
+    row_t[1] = whole(send(after(teacher, swapped[1]), row_masks[0], count))
     for side_t, side_s, masks in reversed(sides):
         side_t[0] = (own, 0, teacher.shape[1])
         for b, mask in enumerate(masks):

time: 52.7 us -> 52.9 us (level)
  starting transfers between devices: 21.5 us -> 23.7 us
  waiting for transfers between devices: 26.9 us -> 25 us
    ppermute x2, starting transfers between devices: 1.2 us -> 2.32 us  [exchange_sums(): got = lax.ppermute(sums, AXES, pairs).reshape(3, -1, 2, 1 << b, rows)]
    ppermute x2, waiting for transfers between devices: 6.32 us -> 5.21 us  [exchange_sums(): got = lax.ppermute(sums, AXES, pairs).reshape(3, -1, 2, 1 << b, rows)]
    ppermute x19, starting transfers between devices: 20.3 us -> 21.4 us  [send(): return lax.ppermute(value, AXES, [(i, i ^ mask) for i in range(count)])]
    ppermute x19, waiting for transfers between devices: 20.6 us -> 19.8 us  [send(): return lax.ppermute(value, AXES, [(i, i ^ mask) for i in range(count)])]
  transfers between devices with their start and end apart: 21 -> 21, of which waited for: 11 -> 12; matrix products, arithmetic and copies ran while one was open for 0% -> 0% of each run, Pallas kernels for 0% -> 0%
where the time goes in v20:
time: 52.9 us; the launch traced here: 52.8 us
  waiting for transfers between devices  25 us (47%)
  starting transfers between devices  23.7 us (45%)
  Pallas kernels  2.87 us (5%)
  between operations  0.82 us (2%)
    ppermute x19, starting transfers between devices, send(): return lax.ppermute(value, AXES, [(i, i ^ mask) for i in range(count)])  21.4 us
    ppermute x19, waiting for transfers between devices, send(): return lax.ppermute(value, AXES, [(i, i ^ mask) for i in range(count)])  19.8 us
    ppermute x2, waiting for transfers between devices, exchange_sums(): got = lax.ppermute(sums, AXES, pairs).reshape(3, -1, 2, 1 << b, rows)  5.21 us
    pallas_call x8, Pallas kernels, call(): pl.pallas_call(kernel, out_shape=outputs, **options, compiler_params=pltp...  2.87 us
    ppermute x2, starting transfers between devices, exchange_sums(): got = lax.ppermute(sums, AXES, pairs).reshape(3, -1, 2, 1 << b, rows)  2.32 us
  transfers between devices with their start and end apart: 21, of which 12 were waited for; matrix products, arithmetic and copies ran while one was open for 0% of the time, Pallas kernels for 0%

profile of v20, /device:TPU:0, one launch (start us, length us, event | category | flops | bytes accessed | tf_op | source)
XLA Modules:
  0.0 52.8 jit_solution(823154235325207334)
XLA Ops:
  0.6 0.5 collective-permute-start.3
  1.2 4.0 %collective-permute-start.2 = (bf16[64,1536]{1,0:T(8,128)(2,1)}, bf16[64,1536]{1,0:T(8,128)(2,1)S(1)}, u32[]{:S(2)}, u32[]{:S(2)}) collective-permute-start(bf16[64,1536]{1,0:T(8,128)(2,1)} %refs_0_.1), channel_id=1, source_target_pairs={{0,2},{1,3},{2,0},{3,1},{4,6},{5,7},{6,4},{7,5},{8,10},{9,11},{10,... | collective-permute-start | bytes 589832 | tf_op jit(solution)/shard_map/ppermute | solution.py:50
  5.3 1.6 %collective-permute-start.1 = (bf16[64,1536]{1,0:T(8,128)(2,1)}, bf16[64,1536]{1,0:T(8,128)(2,1)S(1)}, u32[]{:S(2)}, u32[]{:S(2)}) collective-permute-start(bf16[64,1536]{1,0:T(8,128)(2,1)} %refs_0_.1), channel_id=1, source_target_pairs={{0,1},{1,0},{2,3},{3,2},{4,5},{5,4},{6,7},{7,6},{8,9},{9,8},{10,11... | collective-permute-start | bytes 589832 | tf_op jit(solution)/shard_map/ppermute | solution.py:50
  6.8 1.5 %collective-permute-start.4 = (bf16[64,1536]{1,0:T(8,128)(2,1)}, bf16[64,1536]{1,0:T(8,128)(2,1)S(1)}, u32[]{:S(2)}, u32[]{:S(2)}) collective-permute-start(bf16[64,1536]{1,0:T(8,128)(2,1)} %refs_0_.1), channel_id=1, source_target_pairs={{0,16},{1,17},{2,18},{3,19},{4,20},{5,21},{6,22},{7,23},{8,24},{9,... | collective-permute-start | bytes 589832 | tf_op jit(solution)/shard_map/ppermute | solution.py:50
  8.4 0.5 collective-permute-start.9
  8.9 1.5 %collective-permute-start.6 = (bf16[64,768]{1,0:T(8,128)(2,1)}, bf16[64,768]{1,0:T(8,128)(2,1)S(1)}, u32[]{:S(2)}, u32[]{:S(2)}) collective-permute-start(bf16[64,768]{1,0:T(8,128)(2,1)} %refs_1_.1), channel_id=1, source_target_pairs={{0,8},{1,9},{2,10},{3,11},{4,12},{5,13},{6,14},{7,15},{8,0},{9,1},... | collective-permute-start | bytes 294920 | tf_op jit(solution)/shard_map/ppermute | solution.py:50
  10.4 4.6 %collective-permute-done.2.refs_0_.refs_5_ = bf16[64,1536]{1,0:T(8,128)(2,1)S(1)} collective-permute-done((bf16[64,1536]{1,0:T(8,128)(2,1)}, bf16[64,1536]{1,0:T(8,128)(2,1)S(1)}, u32[]{:S(2)}, u32[]{:S(2)}) %collective-permute-start.2) | collective-permute-done | bytes 196640 | tf_op jit(solution)/shard_map/ppermute | solution.py:50
  14.9 0.2 collective-permute-done.1.refs_1_
  15.1 0.4 collective-permute-done.9.refs_2_.refs_1_.refs_12_
  15.7 1.8 %collective-permute-start.12 = (bf16[64,1536]{1,0:T(8,128)(2,1)S(1)}, bf16[64,1536]{1,0:T(8,128)(2,1)S(1)}, u32[]{:S(2)}, u32[]{:S(2)}) collective-permute-start(bf16[64,1536]{1,0:T(8,128)(2,1)S(1)} %shard_map.45), channel_id=1, source_target_pairs={{0,2},{1,3},{2,0},{3,1},{4,6},{5,7},{6,4},{7,5},{8,10},{9,11},{10,... | collective-permute-start | bytes 589832 | tf_op jit(solution)/shard_map/ppermute | solution.py:50
  17.5 1.5 %collective-permute-start.8 = (bf16[64,1536]{1,0:T(8,128)(2,1)S(1)}, bf16[64,1536]{1,0:T(8,128)(2,1)S(1)}, u32[]{:S(2)}, u32[]{:S(2)}) collective-permute-start(bf16[64,1536]{1,0:T(8,128)(2,1)S(1)} %collective-permute-done.2.refs_0_.refs_5_), channel_id=1, source_target_pairs={{0,16},{1,17},{2,18},{3,19},{4,20},{5,21},{6,22},{7,23},{8,24},{9,... | collective-permute-start | bytes 589832 | tf_op jit(solution)/shard_map/ppermute | solution.py:50
  19.1 1.6 %collective-permute-start.5 = (bf16[64,3072]{1,0:T(8,128)(2,1)S(1)}, bf16[64,3072]{1,0:T(8,128)(2,1)S(1)}, u32[]{:S(2)}, u32[]{:S(2)}) collective-permute-start(bf16[64,3072]{1,0:T(8,128)(2,1)S(1)} %shard_map.42), channel_id=1, source_target_pairs={{0,8},{1,9},{2,10},{3,11},{4,12},{5,13},{6,14},{7,15},{8,0},{9,1},... | collective-permute-start | bytes 1179656 | tf_op jit(solution)/shard_map/ppermute | solution.py:50
  20.6 2.4 %collective-permute-start.7 = (bf16[64,1536]{1,0:T(8,128)(2,1)S(1)}, bf16[64,1536]{1,0:T(8,128)(2,1)S(1)}, u32[]{:S(2)}, u32[]{:S(2)}) collective-permute-start(bf16[64,1536]{1,0:T(8,128)(2,1)S(1)} %shard_map.43), channel_id=1, source_target_pairs={{0,1},{1,0},{2,3},{3,2},{4,5},{5,4},{6,7},{7,6},{8,9},{9,8},{10,11... | collective-permute-start | bytes 589832 | tf_op jit(solution)/shard_map/ppermute | solution.py:50
  23.0 5.3 %collective-permute-done.12.refs_11_.refs_1_ = bf16[64,1536]{1,0:T(8,128)(2,1)S(1)} collective-permute-done((bf16[64,1536]{1,0:T(8,128)(2,1)S(1)}, bf16[64,1536]{1,0:T(8,128)(2,1)S(1)}, u32[]{:S(2)}, u32[]{:S(2)}) %collective-permute-start.12) | collective-permute-done | bytes 196640 | tf_op jit(solution)/shard_map/ppermute | solution.py:50
  28.3 0.5 collective-permute-start.11
  28.8 2.2 %collective-permute-done.7.refs_3_ = bf16[64,1536]{1,0:T(8,128)(2,1)S(1)} collective-permute-done((bf16[64,1536]{1,0:T(8,128)(2,1)S(1)}, bf16[64,1536]{1,0:T(8,128)(2,1)S(1)}, u32[]{:S(2)}, u32[]{:S(2)}) %collective-permute-start.7) | collective-permute-done | bytes 196640 | tf_op jit(solution)/shard_map/ppermute | solution.py:50
  31.0 1.1 %shard_map.46 = (f32[256,512]{1,0:T(8,128)S(1)}, f32[256,512]{1,0:T(8,128)S(1)}, f32[3,4,64]{2,1,0:T(4,128)S(1)}, f32[3,8,64]{2,1,0:T(8,128)S(1)}) custom-call(bf16[64,2304]{1,0:T(8,128)(2,1)S(1)} %shard_map.41.refs_0_, bf16[64,1536]{1,0:T(8,128)(2,1)S(1)} %collective-permute-done.1.refs_1_, bf16[64,3072]{1,0:T(8,128)(2,1)S(1)} %collective-permute-done.5.refs_2_, ...), custom_call_target="tpu_custom_call" | custom-call | flops 603979776 | bytes 4301824 | tf_op jit(solution)/shard_map/pallas_call | solution.py:186
  32.2 1.2 %collective-permute-done.14 = f32[3,12,64]{2,1,0:T(8,128)S(1)} collective-permute-done((f32[3,12,64]{2,1,0:T(8,128)S(1)}, f32[3,12,64]{2,1,0:T(8,128)S(1)}, u32[]{:S(2)}, u32[]{:S(2)}) %collective-permute-start.14) | collective-permute-done | bytes 9248 | tf_op jit(solution)/shard_map/ppermute | solution.py:50
  33.4 1.4 %collective-permute-start.15 = (f32[3,8,64]{2,1,0:T(8,128)S(1)}, f32[3,8,64]{2,1,0:T(8,128)S(1)}, u32[]{:S(2)}, u32[]{:S(2)}) collective-permute-start(f32[3,8,64]{2,1,0:T(8,128)S(1)} %maximum_select_fusion), channel_id=1, source_target_pairs={{0,1},{1,0},{2,3},{3,2},{4,6},{5,7},{6,4},{7,5},{8,9},{9,8},{10,11... | collective-permute-start | bytes 18440 | tf_op jit(solution)/shard_map/ppermute | solution.py:259
  34.8 2.3 %collective-permute-done.15 = f32[3,8,64]{2,1,0:T(8,128)S(1)} collective-permute-done((f32[3,8,64]{2,1,0:T(8,128)S(1)}, f32[3,8,64]{2,1,0:T(8,128)S(1)}, u32[]{:S(2)}, u32[]{:S(2)}) %collective-permute-start.15) | collective-permute-done | bytes 6176 | tf_op jit(solution)/shard_map/ppermute | solution.py:259
  37.2 0.9 %collective-permute-start.16 = (f32[3,8,64]{2,1,0:T(8,128)S(1)}, f32[3,8,64]{2,1,0:T(8,128)S(1)}, u32[]{:S(2)}, u32[]{:S(2)}) collective-permute-start(f32[3,8,64]{2,1,0:T(8,128)S(1)} %add.10), channel_id=1, source_target_pairs={{0,8},{1,9},{2,10},{3,11},{4,20},{5,21},{6,22},{7,23},{8,0},{9,1},... | collective-permute-start | bytes 18440 | tf_op jit(solution)/shard_map/ppermute | solution.py:259
  38.1 2.9 %collective-permute-done.16 = f32[3,8,64]{2,1,0:T(8,128)S(1)} collective-permute-done((f32[3,8,64]{2,1,0:T(8,128)S(1)}, f32[3,8,64]{2,1,0:T(8,128)S(1)}, u32[]{:S(2)}, u32[]{:S(2)}) %collective-permute-start.16) | collective-permute-done | bytes 6176 | tf_op jit(solution)/shard_map/ppermute | solution.py:259
  41.1 1.2 %collective-permute-done.17 = f32[3,8,64]{2,1,0:T(8,128)S(1)} collective-permute-done((f32[3,8,64]{2,1,0:T(8,128)S(1)}, f32[3,8,64]{2,1,0:T(8,128)S(1)}, u32[]{:S(2)}, u32[]{:S(2)}) %collective-permute-start.17) | collective-permute-done | bytes 6176 | tf_op jit(solution)/shard_map/ppermute | solution.py:50
  42.3 0.1 reshape.26.row_sum
  42.4 0.9 %shard_map.47 = (f32[64,768]{1,0:T(8,128)S(1)}, f32[8,128]{1,0:T(8,128)S(1)}, f32[400,128]{1,0:T(8,128)S(1)}, f32[400,128]{1,0:T(8,128)S(1)}, f32[400,128]{1,0:T(8,128)S(1)}) custom-call(f32[256,512]{1,0:T(8,128)S(1)} %get-tuple-element.27.gram_s, f32[256,512]{1,0:T(8,128)S(1)} %get-tuple-element.28.gram_t, f32[3,1,256]{2,1,0:T(1,128)S(1)} %reshape.26.row_sum, ...), custom_call_target="tpu_custom_call" | custom-call | flops 402653184 | bytes 3249152 | tf_op jit(solution)/shard_map/pallas_call | solution.py:186
  43.3 1.4 %collective-permute-start.18 = (f16[400,128]{1,0:T(8,128)(2,1)S(1)}, f16[400,128]{1,0:T(8,128)(2,1)S(1)}, u32[]{:S(2)}, u32[]{:S(2)}) collective-permute-start(f16[400,128]{1,0:T(8,128)(2,1)S(1)} %convert_element_type.18), channel_id=1, source_target_pairs={{0,1},{1,0},{2,3},{3,2},{4,5},{5,4},{6,7},{7,6},{8,9},{9,8},{10,11... | collective-permute-start | bytes 307208 | tf_op jit(solution)/shard_map/ppermute | solution.py:50
  44.8 1.5 %collective-permute-start.19 = (f16[400,128]{1,0:T(8,128)(2,1)S(1)}, f16[400,128]{1,0:T(8,128)(2,1)S(1)}, u32[]{:S(2)}, u32[]{:S(2)}) collective-permute-start(f16[400,128]{1,0:T(8,128)(2,1)S(1)} %convert_element_type.20), channel_id=1, source_target_pairs={{0,8},{1,9},{2,10},{3,11},{4,12},{5,13},{6,14},{7,15},{8,0},{9,1},... | collective-permute-start | bytes 307208 | tf_op jit(solution)/shard_map/ppermute | solution.py:50
  46.3 0.7 %collective-permute-start.20 = (f16[400,128]{1,0:T(8,128)(2,1)S(1)}, f16[400,128]{1,0:T(8,128)(2,1)S(1)}, u32[]{:S(2)}, u32[]{:S(2)}) collective-permute-start(f16[400,128]{1,0:T(8,128)(2,1)S(1)} %convert_element_type.22), channel_id=1, source_target_pairs={{0,9},{1,8},{2,11},{3,10},{4,13},{5,12},{6,15},{7,14},{8,1},{9,0},... | collective-permute-start | bytes 307208 | tf_op jit(solution)/shard_map/ppermute | solution.py:50
  47.1 1.3 %collective-permute-done.18 = f16[400,128]{1,0:T(8,128)(2,1)S(1)} collective-permute-done((f16[400,128]{1,0:T(8,128)(2,1)S(1)}, f16[400,128]{1,0:T(8,128)(2,1)S(1)}, u32[]{:S(2)}, u32[]{:S(2)}) %collective-permute-start.18) | collective-permute-done | bytes 102432 | tf_op jit(solution)/shard_map/ppermute | solution.py:50
  48.4 2.4 %collective-permute-done.19 = f16[400,128]{1,0:T(8,128)(2,1)S(1)} collective-permute-done((f16[400,128]{1,0:T(8,128)(2,1)S(1)}, f16[400,128]{1,0:T(8,128)(2,1)S(1)}, u32[]{:S(2)}, u32[]{:S(2)}) %collective-permute-start.19) | collective-permute-done | bytes 102432 | tf_op jit(solution)/shard_map/ppermute | solution.py:50
  50.8 1.2 %collective-permute-done.20 = f16[400,128]{1,0:T(8,128)(2,1)S(1)} collective-permute-done((f16[400,128]{1,0:T(8,128)(2,1)S(1)}, f16[400,128]{1,0:T(8,128)(2,1)S(1)}, u32[]{:S(2)}, u32[]{:S(2)}) %collective-permute-start.20) | collective-permute-done | bytes 102432 | tf_op jit(solution)/shard_map/ppermute | solution.py:50
  52.0 0.8 %shard_map.48 = (f32[64,768]{1,0:T(8,128)}, f32[1,1]{1,0:T(1,128)}) custom-call(f32[64,768]{1,0:T(8,128)S(1)} %get-tuple-element.31.own, f32[8,128]{1,0:T(8,128)S(1)} %get-tuple-element.32.share, f32[400,128]{1,0:T(8,128)S(1)} %convert_element_type.19.refs_0_, f32[400,128]{1,0:T(8,128)S(1)} %convert_element_type.21.refs_1_, ...), custom_call_target="tpu_custom_call" | custom-call | bytes 1011716 | tf_op jit(solution)/shard_map/pallas_call | solution.py:186
  (41 shorter events, 0.7 us)
Async XLA Ops:
  0.6 15.0 %copy-start = (bf16[64,1536]{1,0:T(8,128)(2,1)S(1)}, bf16[64,1536]{1,0:T(8,128)(2,1)}, u32[]{:S(2)}) copy-start(bf16[64,1536]{1,0:T(8,128)(2,1)} %refs_0_.1) | copy-start | bytes 589828
  0.6 15.0 %copy-start.1 = (bf16[64,768]{1,0:T(8,128)(2,1)S(1)}, bf16[64,768]{1,0:T(8,128)(2,1)}, u32[]{:S(2)}) copy-start(bf16[64,768]{1,0:T(8,128)(2,1)} %refs_1_.1) | copy-start | bytes 294916
  0.6 6.2 %collective-permute-start.3 = (bf16[64,1536]{1,0:T(8,128)(2,1)}, bf16[64,1536]{1,0:T(8,128)(2,1)S(1)}, u32[]{:S(2)}, u32[]{:S(2)}) collective-permute-start(bf16[64,1536]{1,0:T(8,128)(2,1)} %refs_0_.1), channel_id=1, source_target_pairs={{0,4},{1,5},{2,6},{3,7},{4,0},{5,1},{6,2},{7,3},{8,12},{9,13},{10,... | collective-permute-start | bytes 589832 | tf_op jit(solution)/shard_map/ppermute | solution.py:50
  1.2 4.1 %collective-permute-start = (bf16[64,768]{1,0:T(8,128)(2,1)}, bf16[64,768]{1,0:T(8,128)(2,1)S(1)}, u32[]{:S(2)}, u32[]{:S(2)}) collective-permute-start(bf16[64,768]{1,0:T(8,128)(2,1)} %refs_1_.1), channel_id=1, source_target_pairs={{0,4},{1,5},{2,6},{3,7},{4,0},{5,1},{6,2},{7,3},{8,12},{9,13},{10,... | collective-permute-start | bytes 294920 | tf_op jit(solution)/shard_map/ppermute | solution.py:50
  1.2 13.7 %collective-permute-start.2 = (bf16[64,1536]{1,0:T(8,128)(2,1)}, bf16[64,1536]{1,0:T(8,128)(2,1)S(1)}, u32[]{:S(2)}, u32[]{:S(2)}) collective-permute-start(bf16[64,1536]{1,0:T(8,128)(2,1)} %refs_0_.1), channel_id=1, source_target_pairs={{0,2},{1,3},{2,0},{3,1},{4,6},{5,7},{6,4},{7,5},{8,10},{9,11},{10,... | collective-permute-start | bytes 589832 | tf_op jit(solution)/shard_map/ppermute | solution.py:50
  5.3 9.9 %collective-permute-start.1 = (bf16[64,1536]{1,0:T(8,128)(2,1)}, bf16[64,1536]{1,0:T(8,128)(2,1)S(1)}, u32[]{:S(2)}, u32[]{:S(2)}) collective-permute-start(bf16[64,1536]{1,0:T(8,128)(2,1)} %refs_0_.1), channel_id=1, source_target_pairs={{0,1},{1,0},{2,3},{3,2},{4,5},{5,4},{6,7},{7,6},{8,9},{9,8},{10,11... | collective-permute-start | bytes 589832 | tf_op jit(solution)/shard_map/ppermute | solution.py:50
  6.8 8.3 %collective-permute-start.4 = (bf16[64,1536]{1,0:T(8,128)(2,1)}, bf16[64,1536]{1,0:T(8,128)(2,1)S(1)}, u32[]{:S(2)}, u32[]{:S(2)}) collective-permute-start(bf16[64,1536]{1,0:T(8,128)(2,1)} %refs_0_.1), channel_id=1, source_target_pairs={{0,16},{1,17},{2,18},{3,19},{4,20},{5,21},{6,22},{7,23},{8,24},{9,... | collective-permute-start | bytes 589832 | tf_op jit(solution)/shard_map/ppermute | solution.py:50
  8.4 7.1 %collective-permute-start.9 = (bf16[64,768]{1,0:T(8,128)(2,1)}, bf16[64,768]{1,0:T(8,128)(2,1)S(1)}, u32[]{:S(2)}, u32[]{:S(2)}) collective-permute-start(bf16[64,768]{1,0:T(8,128)(2,1)} %refs_1_.1), channel_id=1, source_target_pairs={{0,16},{1,17},{2,18},{3,19},{4,20},{5,21},{6,22},{7,23},{8,24},{9,... | collective-permute-start | bytes 294920 | tf_op jit(solution)/shard_map/ppermute | solution.py:50
  8.9 6.8 %collective-permute-start.6 = (bf16[64,768]{1,0:T(8,128)(2,1)}, bf16[64,768]{1,0:T(8,128)(2,1)S(1)}, u32[]{:S(2)}, u32[]{:S(2)}) collective-permute-start(bf16[64,768]{1,0:T(8,128)(2,1)} %refs_1_.1), channel_id=1, source_target_pairs={{0,8},{1,9},{2,10},{3,11},{4,12},{5,13},{6,14},{7,15},{8,0},{9,1},... | collective-permute-start | bytes 294920 | tf_op jit(solution)/shard_map/ppermute | solution.py:50
  15.5 15.5 %collective-permute-start.10 = (bf16[64,3840]{1,0:T(8,128)(2,1)S(1)}, bf16[64,3840]{1,0:T(8,128)(2,1)S(1)}, u32[]{:S(2)}, u32[]{:S(2)}) collective-permute-start(bf16[64,3840]{1,0:T(8,128)(2,1)S(1)} %shard_map.44), channel_id=1, source_target_pairs={{0,4},{1,5},{2,6},{3,7},{4,0},{5,1},{6,2},{7,3},{8,12},{9,13},{10,... | collective-permute-start | bytes 1474568 | tf_op jit(solution)/shard_map/ppermute | solution.py:50
  15.7 12.6 %collective-permute-start.12 = (bf16[64,1536]{1,0:T(8,128)(2,1)S(1)}, bf16[64,1536]{1,0:T(8,128)(2,1)S(1)}, u32[]{:S(2)}, u32[]{:S(2)}) collective-permute-start(bf16[64,1536]{1,0:T(8,128)(2,1)S(1)} %shard_map.45), channel_id=1, source_target_pairs={{0,2},{1,3},{2,0},{3,1},{4,6},{5,7},{6,4},{7,5},{8,10},{9,11},{10,... | collective-permute-start | bytes 589832 | tf_op jit(solution)/shard_map/ppermute | solution.py:50
  17.5 10.8 %collective-permute-start.8 = (bf16[64,1536]{1,0:T(8,128)(2,1)S(1)}, bf16[64,1536]{1,0:T(8,128)(2,1)S(1)}, u32[]{:S(2)}, u32[]{:S(2)}) collective-permute-start(bf16[64,1536]{1,0:T(8,128)(2,1)S(1)} %collective-permute-done.2.refs_0_.refs_5_), channel_id=1, source_target_pairs={{0,16},{1,17},{2,18},{3,19},{4,20},{5,21},{6,22},{7,23},{8,24},{9,... | collective-permute-start | bytes 589832 | tf_op jit(solution)/shard_map/ppermute | solution.py:50
  19.1 12.0 %collective-permute-start.5 = (bf16[64,3072]{1,0:T(8,128)(2,1)S(1)}, bf16[64,3072]{1,0:T(8,128)(2,1)S(1)}, u32[]{:S(2)}, u32[]{:S(2)}) collective-permute-start(bf16[64,3072]{1,0:T(8,128)(2,1)S(1)} %shard_map.42), channel_id=1, source_target_pairs={{0,8},{1,9},{2,10},{3,11},{4,12},{5,13},{6,14},{7,15},{8,0},{9,1},... | collective-permute-start | bytes 1179656 | tf_op jit(solution)/shard_map/ppermute | solution.py:50
  20.6 10.4 %collective-permute-start.7 = (bf16[64,1536]{1,0:T(8,128)(2,1)S(1)}, bf16[64,1536]{1,0:T(8,128)(2,1)S(1)}, u32[]{:S(2)}, u32[]{:S(2)}) collective-permute-start(bf16[64,1536]{1,0:T(8,128)(2,1)S(1)} %shard_map.43), channel_id=1, source_target_pairs={{0,1},{1,0},{2,3},{3,2},{4,5},{5,4},{6,7},{7,6},{8,9},{9,8},{10,11... | collective-permute-start | bytes 589832 | tf_op jit(solution)/shard_map/ppermute | solution.py:50
  28.3 2.7 %collective-permute-start.13 = (bf16[64,1536]{1,0:T(8,128)(2,1)S(1)}, bf16[64,1536]{1,0:T(8,128)(2,1)S(1)}, u32[]{:S(2)}, u32[]{:S(2)}) collective-permute-start(bf16[64,1536]{1,0:T(8,128)(2,1)S(1)} %collective-permute-done.12.refs_11_.refs_1_), channel_id=1, source_target_pairs={{0,4},{1,5},{2,6},{3,7},{4,0},{5,1},{6,2},{7,3},{8,12},{9,13},{10,... | collective-permute-start | bytes 589832 | tf_op jit(solution)/shard_map/ppermute | solution.py:50
  28.3 2.7 %collective-permute-start.11 = (bf16[64,1536]{1,0:T(8,128)(2,1)S(1)}, bf16[64,1536]{1,0:T(8,128)(2,1)S(1)}, u32[]{:S(2)}, u32[]{:S(2)}) collective-permute-start(bf16[64,1536]{1,0:T(8,128)(2,1)S(1)} %collective-permute-done.8.refs_7_), channel_id=1, source_target_pairs={{0,4},{1,5},{2,6},{3,7},{4,0},{5,1},{6,2},{7,3},{8,12},{9,13},{10,... | collective-permute-start | bytes 589832 | tf_op jit(solution)/shard_map/ppermute | solution.py:50
  32.1 1.3 %collective-permute-start.14 = (f32[3,12,64]{2,1,0:T(8,128)S(1)}, f32[3,12,64]{2,1,0:T(8,128)S(1)}, u32[]{:S(2)}, u32[]{:S(2)}) collective-permute-start(f32[3,12,64]{2,1,0:T(8,128)S(1)} %pad_maximum_fusion), channel_id=1, source_target_pairs={{0,4},{1,5},{2,6},{3,7},{4,0},{5,1},{6,2},{7,3},{8,12},{9,13},{10,... | collective-permute-start | bytes 27656 | tf_op jit(solution)/shard_map/ppermute | solution.py:50
  33.4 3.8 %collective-permute-start.15 = (f32[3,8,64]{2,1,0:T(8,128)S(1)}, f32[3,8,64]{2,1,0:T(8,128)S(1)}, u32[]{:S(2)}, u32[]{:S(2)}) collective-permute-start(f32[3,8,64]{2,1,0:T(8,128)S(1)} %maximum_select_fusion), channel_id=1, source_target_pairs={{0,1},{1,0},{2,3},{3,2},{4,6},{5,7},{6,4},{7,5},{8,9},{9,8},{10,11... | collective-permute-start | bytes 18440 | tf_op jit(solution)/shard_map/ppermute | solution.py:259
  37.2 3.8 %collective-permute-start.16 = (f32[3,8,64]{2,1,0:T(8,128)S(1)}, f32[3,8,64]{2,1,0:T(8,128)S(1)}, u32[]{:S(2)}, u32[]{:S(2)}) collective-permute-start(f32[3,8,64]{2,1,0:T(8,128)S(1)} %add.10), channel_id=1, source_target_pairs={{0,8},{1,9},{2,10},{3,11},{4,20},{5,21},{6,22},{7,23},{8,0},{9,1},... | collective-permute-start | bytes 18440 | tf_op jit(solution)/shard_map/ppermute | solution.py:259
  41.0 1.2 %collective-permute-start.17 = (f32[3,8,64]{2,1,0:T(8,128)S(1)}, f32[3,8,64]{2,1,0:T(8,128)S(1)}, u32[]{:S(2)}, u32[]{:S(2)}) collective-permute-start(f32[3,8,64]{2,1,0:T(8,128)S(1)} %add.11), channel_id=1, source_target_pairs={{0,4},{1,5},{2,6},{3,7},{4,0},{5,1},{6,2},{7,3},{8,12},{9,13},{10,... | collective-permute-start | bytes 18440 | tf_op jit(solution)/shard_map/ppermute | solution.py:50
  43.3 5.0 %collective-permute-start.18 = (f16[400,128]{1,0:T(8,128)(2,1)S(1)}, f16[400,128]{1,0:T(8,128)(2,1)S(1)}, u32[]{:S(2)}, u32[]{:S(2)}) collective-permute-start(f16[400,128]{1,0:T(8,128)(2,1)S(1)} %convert_element_type.18), channel_id=1, source_target_pairs={{0,1},{1,0},{2,3},{3,2},{4,5},{5,4},{6,7},{7,6},{8,9},{9,8},{10,11... | collective-permute-start | bytes 307208 | tf_op jit(solution)/shard_map/ppermute | solution.py:50
  44.8 6.0 %collective-permute-start.19 = (f16[400,128]{1,0:T(8,128)(2,1)S(1)}, f16[400,128]{1,0:T(8,128)(2,1)S(1)}, u32[]{:S(2)}, u32[]{:S(2)}) collective-permute-start(f16[400,128]{1,0:T(8,128)(2,1)S(1)} %convert_element_type.20), channel_id=1, source_target_pairs={{0,8},{1,9},{2,10},{3,11},{4,12},{5,13},{6,14},{7,15},{8,0},{9,1},... | collective-permute-start | bytes 307208 | tf_op jit(solution)/shard_map/ppermute | solution.py:50
  46.3 5.6 %collective-permute-start.20 = (f16[400,128]{1,0:T(8,128)(2,1)S(1)}, f16[400,128]{1,0:T(8,128)(2,1)S(1)}, u32[]{:S(2)}, u32[]{:S(2)}) collective-permute-start(f16[400,128]{1,0:T(8,128)(2,1)S(1)} %convert_element_type.22), channel_id=1, source_target_pairs={{0,9},{1,8},{2,11},{3,10},{4,13},{5,12},{6,15},{7,14},{8,1},{9,0},... | collective-permute-start | bytes 307208 | tf_op jit(solution)/shard_map/ppermute | solution.py:50

commit v21 on v19

--- a/solution.py
+++ b/solution.py
@@ -223,12 +223,12 @@
         piece[width // 128 * rows :, :] = extra
 
 
-def final_kernel(total, own, share, *refs):
+def final_kernel(order, total, own, share, *refs):
     *pieces, grad, loss = refs
     width = own.shape[1]
     grads, terms = [own[...]], [share[0:1, 0:1]]
     rows = own.shape[0]
-    for piece in pieces:
+    for piece in [pieces[order.index(k)] for k in range(len(pieces))]:
         extra = piece[width // 128 * rows :, :]
         blocks = [piece[c * rows : (c + 1) * rows, :] for c in range(width // 128)]
         grads.append(jnp.concatenate(blocks, 1) * jnp.exp2(extra[0:1, 0:1] - 13.0))
@@ -297,12 +297,11 @@
         [f32(rows, width), f32(8, 128)] + [f32(width // 128 * rows + EXTRA, 128)] * (n_row - 1),
         4 * math.prod(shape) * width,
     )
-    got = [
-        send(value.astype(jnp.float16), mask, count).astype(jnp.float32)
-        for value, mask in zip(pieces, span(row_masks)[1:])
-    ]
+    order = sorted(range(n_row - 1), key=lambda k: ((k + 1).bit_count(), -k))
+    masks = span(row_masks)[1:]
+    got = [send(pieces[k].astype(jnp.float16), masks[k], count).astype(jnp.float32) for k in order]
     grad, loss = call(
-        functools.partial(final_kernel, total), [own, share, *got], [f32(rows, width), f32(1, 1)]
+        functools.partial(final_kernel, order, total), [own, share, *got], [f32(rows, width), f32(1, 1)]
     )
     return (loss[0, 0], grad)
 

time: 52.7 us -> 53.3 us (1.011)
  waiting for transfers between devices: 26.9 us -> 27.6 us
    ppermute x19, waiting for transfers between devices: 20.6 us -> 21.3 us  [send(): return lax.ppermute(value, AXES, [(i, i ^ mask) for i in range(count)])]
where the time goes in v21:
time: 53.3 us; the launch traced here: 53.2 us
  waiting for transfers between devices  27.6 us (52%)
  starting transfers between devices  21.5 us (40%)
  Pallas kernels  2.86 us (5%)
  between operations  0.83 us (2%)
    ppermute x19, waiting for transfers between devices, send(): return lax.ppermute(value, AXES, [(i, i ^ mask) for i in range(count)])  21.3 us
    ppermute x19, starting transfers between devices, send(): return lax.ppermute(value, AXES, [(i, i ^ mask) for i in range(count)])  20.3 us
    ppermute x2, waiting for transfers between devices, exchange_sums(): got = lax.ppermute(sums, AXES, pairs).reshape(3, -1, 2, 1 << b, rows)  6.32 us
    pallas_call x8, Pallas kernels, call(): pl.pallas_call(kernel, out_shape=outputs, **options, compiler_params=pltp...  2.86 us
    ppermute x2, starting transfers between devices, exchange_sums(): got = lax.ppermute(sums, AXES, pairs).reshape(3, -1, 2, 1 << b, rows)  1.2 us
  transfers between devices with their start and end apart: 21, of which 11 were waited for; matrix products, arithmetic and copies ran while one was open for 0% of the time, Pallas kernels for 0%

profile of v21, /device:TPU:0, one launch (start us, length us, event | category | flops | bytes accessed | tf_op | source)
XLA Modules:
  0.0 53.2 jit_solution(11045743445931375672)
XLA Ops:
  0.6 0.5 collective-permute-start.2
  1.2 3.0 %collective-permute-start = (bf16[64,1536]{1,0:T(8,128)(2,1)}, bf16[64,1536]{1,0:T(8,128)(2,1)S(1)}, u32[]{:S(2)}, u32[]{:S(2)}) collective-permute-start(bf16[64,1536]{1,0:T(8,128)(2,1)} %refs_0_.1), channel_id=1, source_target_pairs={{0,1},{1,0},{2,3},{3,2},{4,5},{5,4},{6,7},{7,6},{8,9},{9,8},{10,11... | collective-permute-start | bytes 589832 | tf_op jit(solution)/shard_map/ppermute | solution.py:50
  4.2 2.6 %collective-permute-start.1 = (bf16[64,1536]{1,0:T(8,128)(2,1)}, bf16[64,1536]{1,0:T(8,128)(2,1)S(1)}, u32[]{:S(2)}, u32[]{:S(2)}) collective-permute-start(bf16[64,1536]{1,0:T(8,128)(2,1)} %refs_0_.1), channel_id=1, source_target_pairs={{0,2},{1,3},{2,0},{3,1},{4,6},{5,7},{6,4},{7,5},{8,10},{9,11},{10,... | collective-permute-start | bytes 589832 | tf_op jit(solution)/shard_map/ppermute | solution.py:50
  6.8 1.5 %collective-permute-start.4 = (bf16[64,1536]{1,0:T(8,128)(2,1)}, bf16[64,1536]{1,0:T(8,128)(2,1)S(1)}, u32[]{:S(2)}, u32[]{:S(2)}) collective-permute-start(bf16[64,1536]{1,0:T(8,128)(2,1)} %refs_0_.1), channel_id=1, source_target_pairs={{0,16},{1,17},{2,18},{3,19},{4,20},{5,21},{6,22},{7,23},{8,24},{9,... | collective-permute-start | bytes 589832 | tf_op jit(solution)/shard_map/ppermute | solution.py:50
  8.4 0.5 collective-permute-start.9
  8.9 1.5 %collective-permute-start.6 = (bf16[64,768]{1,0:T(8,128)(2,1)}, bf16[64,768]{1,0:T(8,128)(2,1)S(1)}, u32[]{:S(2)}, u32[]{:S(2)}) collective-permute-start(bf16[64,768]{1,0:T(8,128)(2,1)} %refs_1_.1), channel_id=1, source_target_pairs={{0,8},{1,9},{2,10},{3,11},{4,12},{5,13},{6,14},{7,15},{8,0},{9,1},... | collective-permute-start | bytes 294920 | tf_op jit(solution)/shard_map/ppermute | solution.py:50
  10.4 3.3 %collective-permute-done.refs_1_ = bf16[64,1536]{1,0:T(8,128)(2,1)S(1)} collective-permute-done((bf16[64,1536]{1,0:T(8,128)(2,1)}, bf16[64,1536]{1,0:T(8,128)(2,1)S(1)}, u32[]{:S(2)}, u32[]{:S(2)}) %collective-permute-start) | collective-permute-done | bytes 196640 | tf_op jit(solution)/shard_map/ppermute | solution.py:50
  13.7 2.6 %collective-permute-done.1.refs_0_.refs_5_ = bf16[64,1536]{1,0:T(8,128)(2,1)S(1)} collective-permute-done((bf16[64,1536]{1,0:T(8,128)(2,1)}, bf16[64,1536]{1,0:T(8,128)(2,1)S(1)}, u32[]{:S(2)}, u32[]{:S(2)}) %collective-permute-start.1) | collective-permute-done | bytes 196640 | tf_op jit(solution)/shard_map/ppermute | solution.py:50
  16.5 0.4 collective-permute-start.12
  16.9 1.5 %collective-permute-start.8 = (bf16[64,1536]{1,0:T(8,128)(2,1)S(1)}, bf16[64,1536]{1,0:T(8,128)(2,1)S(1)}, u32[]{:S(2)}, u32[]{:S(2)}) collective-permute-start(bf16[64,1536]{1,0:T(8,128)(2,1)S(1)} %collective-permute-done.1.refs_0_.refs_5_), channel_id=1, source_target_pairs={{0,16},{1,17},{2,18},{3,19},{4,20},{5,21},{6,22},{7,23},{8,24},{9,... | collective-permute-start | bytes 589832 | tf_op jit(solution)/shard_map/ppermute | solution.py:50
  18.4 1.6 %collective-permute-start.5 = (bf16[64,3072]{1,0:T(8,128)(2,1)S(1)}, bf16[64,3072]{1,0:T(8,128)(2,1)S(1)}, u32[]{:S(2)}, u32[]{:S(2)}) collective-permute-start(bf16[64,3072]{1,0:T(8,128)(2,1)S(1)} %shard_map.42), channel_id=1, source_target_pairs={{0,8},{1,9},{2,10},{3,11},{4,12},{5,13},{6,14},{7,15},{8,0},{9,1},... | collective-permute-start | bytes 1179656 | tf_op jit(solution)/shard_map/ppermute | solution.py:50
  20.0 2.8 %collective-permute-start.7 = (bf16[64,1536]{1,0:T(8,128)(2,1)S(1)}, bf16[64,1536]{1,0:T(8,128)(2,1)S(1)}, u32[]{:S(2)}, u32[]{:S(2)}) collective-permute-start(bf16[64,1536]{1,0:T(8,128)(2,1)S(1)} %shard_map.43), channel_id=1, source_target_pairs={{0,1},{1,0},{2,3},{3,2},{4,5},{5,4},{6,7},{7,6},{8,9},{9,8},{10,11... | collective-permute-start | bytes 589832 | tf_op jit(solution)/shard_map/ppermute | solution.py:50
  22.8 6.2 %collective-permute-done.12.refs_11_.refs_1_ = bf16[64,1536]{1,0:T(8,128)(2,1)S(1)} collective-permute-done((bf16[64,1536]{1,0:T(8,128)(2,1)S(1)}, bf16[64,1536]{1,0:T(8,128)(2,1)S(1)}, u32[]{:S(2)}, u32[]{:S(2)}) %collective-permute-start.12) | collective-permute-done | bytes 196640 | tf_op jit(solution)/shard_map/ppermute | solution.py:50
  28.9 0.5 collective-permute-start.11
  29.4 2.1 %collective-permute-done.7.refs_3_ = bf16[64,1536]{1,0:T(8,128)(2,1)S(1)} collective-permute-done((bf16[64,1536]{1,0:T(8,128)(2,1)S(1)}, bf16[64,1536]{1,0:T(8,128)(2,1)S(1)}, u32[]{:S(2)}, u32[]{:S(2)}) %collective-permute-start.7) | collective-permute-done | bytes 196640 | tf_op jit(solution)/shard_map/ppermute | solution.py:50
  31.6 1.0 %shard_map.46 = (f32[256,512]{1,0:T(8,128)S(1)}, f32[256,512]{1,0:T(8,128)S(1)}, f32[3,4,64]{2,1,0:T(4,128)S(1)}, f32[3,8,64]{2,1,0:T(8,128)S(1)}) custom-call(bf16[64,2304]{1,0:T(8,128)(2,1)S(1)} %shard_map.41.refs_0_, bf16[64,1536]{1,0:T(8,128)(2,1)S(1)} %collective-permute-done.refs_1_, bf16[64,3072]{1,0:T(8,128)(2,1)S(1)} %collective-permute-done.5.refs_2_, ...), custom_call_target="tpu_custom_call" | custom-call | flops 603979776 | bytes 4301824 | tf_op jit(solution)/shard_map/pallas_call | solution.py:186
  32.7 1.2 %collective-permute-done.14 = f32[3,12,64]{2,1,0:T(8,128)S(1)} collective-permute-done((f32[3,12,64]{2,1,0:T(8,128)S(1)}, f32[3,12,64]{2,1,0:T(8,128)S(1)}, u32[]{:S(2)}, u32[]{:S(2)}) %collective-permute-start.14) | collective-permute-done | bytes 9248 | tf_op jit(solution)/shard_map/ppermute | solution.py:50
  33.9 0.6 %collective-permute-start.15 = (f32[3,8,64]{2,1,0:T(8,128)S(1)}, f32[3,8,64]{2,1,0:T(8,128)S(1)}, u32[]{:S(2)}, u32[]{:S(2)}) collective-permute-start(f32[3,8,64]{2,1,0:T(8,128)S(1)} %maximum_select_fusion), channel_id=1, source_target_pairs={{0,1},{1,0},{2,3},{3,2},{4,6},{5,7},{6,4},{7,5},{8,9},{9,8},{10,11... | collective-permute-start | bytes 18440 | tf_op jit(solution)/shard_map/ppermute | solution.py:259
  34.5 3.2 %collective-permute-done.15 = f32[3,8,64]{2,1,0:T(8,128)S(1)} collective-permute-done((f32[3,8,64]{2,1,0:T(8,128)S(1)}, f32[3,8,64]{2,1,0:T(8,128)S(1)}, u32[]{:S(2)}, u32[]{:S(2)}) %collective-permute-start.15) | collective-permute-done | bytes 6176 | tf_op jit(solution)/shard_map/ppermute | solution.py:259
  37.8 0.6 %collective-permute-start.16 = (f32[3,8,64]{2,1,0:T(8,128)S(1)}, f32[3,8,64]{2,1,0:T(8,128)S(1)}, u32[]{:S(2)}, u32[]{:S(2)}) collective-permute-start(f32[3,8,64]{2,1,0:T(8,128)S(1)} %add.10), channel_id=1, source_target_pairs={{0,8},{1,9},{2,10},{3,11},{4,20},{5,21},{6,22},{7,23},{8,0},{9,1},... | collective-permute-start | bytes 18440 | tf_op jit(solution)/shard_map/ppermute | solution.py:259
  38.4 3.2 %collective-permute-done.16 = f32[3,8,64]{2,1,0:T(8,128)S(1)} collective-permute-done((f32[3,8,64]{2,1,0:T(8,128)S(1)}, f32[3,8,64]{2,1,0:T(8,128)S(1)}, u32[]{:S(2)}, u32[]{:S(2)}) %collective-permute-start.16) | collective-permute-done | bytes 6176 | tf_op jit(solution)/shard_map/ppermute | solution.py:259
  41.6 1.2 %collective-permute-done.17 = f32[3,8,64]{2,1,0:T(8,128)S(1)} collective-permute-done((f32[3,8,64]{2,1,0:T(8,128)S(1)}, f32[3,8,64]{2,1,0:T(8,128)S(1)}, u32[]{:S(2)}, u32[]{:S(2)}) %collective-permute-start.17) | collective-permute-done | bytes 6176 | tf_op jit(solution)/shard_map/ppermute | solution.py:50
  42.8 0.1 reshape.27.col_sum
  42.9 0.1 reshape.26.row_sum
  43.0 0.9 %shard_map.47 = (f32[64,768]{1,0:T(8,128)S(1)}, f32[8,128]{1,0:T(8,128)S(1)}, f32[400,128]{1,0:T(8,128)S(1)}, f32[400,128]{1,0:T(8,128)S(1)}, f32[400,128]{1,0:T(8,128)S(1)}) custom-call(f32[256,512]{1,0:T(8,128)S(1)} %get-tuple-element.25.gram_s, f32[256,512]{1,0:T(8,128)S(1)} %get-tuple-element.26.gram_t, f32[3,1,256]{2,1,0:T(1,128)S(1)} %reshape.26.row_sum, ...), custom_call_target="tpu_custom_call" | custom-call | flops 402653184 | bytes 3249152 | tf_op jit(solution)/shard_map/pallas_call | solution.py:186
  43.9 0.6 %collective-permute-start.18 = (f16[400,128]{1,0:T(8,128)(2,1)S(1)}, f16[400,128]{1,0:T(8,128)(2,1)S(1)}, u32[]{:S(2)}, u32[]{:S(2)}) collective-permute-start(f16[400,128]{1,0:T(8,128)(2,1)S(1)} %convert_element_type.18), channel_id=1, source_target_pairs={{0,8},{1,9},{2,10},{3,11},{4,12},{5,13},{6,14},{7,15},{8,0},{9,1},... | collective-permute-start | bytes 307208 | tf_op jit(solution)/shard_map/ppermute | solution.py:50
  44.5 1.6 %collective-permute-start.19 = (f16[400,128]{1,0:T(8,128)(2,1)S(1)}, f16[400,128]{1,0:T(8,128)(2,1)S(1)}, u32[]{:S(2)}, u32[]{:S(2)}) collective-permute-start(f16[400,128]{1,0:T(8,128)(2,1)S(1)} %convert_element_type.20), channel_id=1, source_target_pairs={{0,1},{1,0},{2,3},{3,2},{4,5},{5,4},{6,7},{7,6},{8,9},{9,8},{10,11... | collective-permute-start | bytes 307208 | tf_op jit(solution)/shard_map/ppermute | solution.py:50
  46.1 1.5 %collective-permute-start.20 = (f16[400,128]{1,0:T(8,128)(2,1)S(1)}, f16[400,128]{1,0:T(8,128)(2,1)S(1)}, u32[]{:S(2)}, u32[]{:S(2)}) collective-permute-start(f16[400,128]{1,0:T(8,128)(2,1)S(1)} %convert_element_type.22), channel_id=1, source_target_pairs={{0,9},{1,8},{2,11},{3,10},{4,13},{5,12},{6,15},{7,14},{8,1},{9,0},... | collective-permute-start | bytes 307208 | tf_op jit(solution)/shard_map/ppermute | solution.py:50
  47.6 1.3 %collective-permute-done.18 = f16[400,128]{1,0:T(8,128)(2,1)S(1)} collective-permute-done((f16[400,128]{1,0:T(8,128)(2,1)S(1)}, f16[400,128]{1,0:T(8,128)(2,1)S(1)}, u32[]{:S(2)}, u32[]{:S(2)}) %collective-permute-start.18) | collective-permute-done | bytes 102432 | tf_op jit(solution)/shard_map/ppermute | solution.py:50
  48.9 1.3 %collective-permute-done.19 = f16[400,128]{1,0:T(8,128)(2,1)S(1)} collective-permute-done((f16[400,128]{1,0:T(8,128)(2,1)S(1)}, f16[400,128]{1,0:T(8,128)(2,1)S(1)}, u32[]{:S(2)}, u32[]{:S(2)}) %collective-permute-start.19) | collective-permute-done | bytes 102432 | tf_op jit(solution)/shard_map/ppermute | solution.py:50
  50.2 2.2 %collective-permute-done.20 = f16[400,128]{1,0:T(8,128)(2,1)S(1)} collective-permute-done((f16[400,128]{1,0:T(8,128)(2,1)S(1)}, f16[400,128]{1,0:T(8,128)(2,1)S(1)}, u32[]{:S(2)}, u32[]{:S(2)}) %collective-permute-start.20) | collective-permute-done | bytes 102432 | tf_op jit(solution)/shard_map/ppermute | solution.py:50
  52.4 0.8 %shard_map.48 = (f32[64,768]{1,0:T(8,128)}, f32[1,1]{1,0:T(1,128)}) custom-call(f32[64,768]{1,0:T(8,128)S(1)} %get-tuple-element.29.own, f32[8,128]{1,0:T(8,128)S(1)} %get-tuple-element.30.share, f32[400,128]{1,0:T(8,128)S(1)} %convert_element_type.19.refs_0_, f32[400,128]{1,0:T(8,128)S(1)} %convert_element_type.21.refs_1_, ...), custom_call_target="tpu_custom_call" | custom-call | bytes 1011716 | tf_op jit(solution)/shard_map/pallas_call | solution.py:186
  (41 shorter events, 0.7 us)
Async XLA Ops:
  0.6 15.7 %copy-start = (bf16[64,1536]{1,0:T(8,128)(2,1)S(1)}, bf16[64,1536]{1,0:T(8,128)(2,1)}, u32[]{:S(2)}) copy-start(bf16[64,1536]{1,0:T(8,128)(2,1)} %refs_0_.1) | copy-start | bytes 589828
  0.6 15.7 %copy-start.1 = (bf16[64,768]{1,0:T(8,128)(2,1)S(1)}, bf16[64,768]{1,0:T(8,128)(2,1)}, u32[]{:S(2)}) copy-start(bf16[64,768]{1,0:T(8,128)(2,1)} %refs_1_.1) | copy-start | bytes 294916
  0.6 6.2 %collective-permute-start.2 = (bf16[64,1536]{1,0:T(8,128)(2,1)}, bf16[64,1536]{1,0:T(8,128)(2,1)S(1)}, u32[]{:S(2)}, u32[]{:S(2)}) collective-permute-start(bf16[64,1536]{1,0:T(8,128)(2,1)} %refs_0_.1), channel_id=1, source_target_pairs={{0,4},{1,5},{2,6},{3,7},{4,0},{5,1},{6,2},{7,3},{8,12},{9,13},{10,... | collective-permute-start | bytes 589832 | tf_op jit(solution)/shard_map/ppermute | solution.py:50
  1.2 5.7 %collective-permute-start.3 = (bf16[64,768]{1,0:T(8,128)(2,1)}, bf16[64,768]{1,0:T(8,128)(2,1)S(1)}, u32[]{:S(2)}, u32[]{:S(2)}) collective-permute-start(bf16[64,768]{1,0:T(8,128)(2,1)} %refs_1_.1), channel_id=1, source_target_pairs={{0,4},{1,5},{2,6},{3,7},{4,0},{5,1},{6,2},{7,3},{8,12},{9,13},{10,... | collective-permute-start | bytes 294920 | tf_op jit(solution)/shard_map/ppermute | solution.py:50
  1.2 12.4 %collective-permute-start = (bf16[64,1536]{1,0:T(8,128)(2,1)}, bf16[64,1536]{1,0:T(8,128)(2,1)S(1)}, u32[]{:S(2)}, u32[]{:S(2)}) collective-permute-start(bf16[64,1536]{1,0:T(8,128)(2,1)} %refs_0_.1), channel_id=1, source_target_pairs={{0,1},{1,0},{2,3},{3,2},{4,5},{5,4},{6,7},{7,6},{8,9},{9,8},{10,11... | collective-permute-start | bytes 589832 | tf_op jit(solution)/shard_map/ppermute | solution.py:50
  4.2 12.0 %collective-permute-start.1 = (bf16[64,1536]{1,0:T(8,128)(2,1)}, bf16[64,1536]{1,0:T(8,128)(2,1)S(1)}, u32[]{:S(2)}, u32[]{:S(2)}) collective-permute-start(bf16[64,1536]{1,0:T(8,128)(2,1)} %refs_0_.1), channel_id=1, source_target_pairs={{0,2},{1,3},{2,0},{3,1},{4,6},{5,7},{6,4},{7,5},{8,10},{9,11},{10,... | collective-permute-start | bytes 589832 | tf_op jit(solution)/shard_map/ppermute | solution.py:50
  6.8 9.4 %collective-permute-start.4 = (bf16[64,1536]{1,0:T(8,128)(2,1)}, bf16[64,1536]{1,0:T(8,128)(2,1)S(1)}, u32[]{:S(2)}, u32[]{:S(2)}) collective-permute-start(bf16[64,1536]{1,0:T(8,128)(2,1)} %refs_0_.1), channel_id=1, source_target_pairs={{0,16},{1,17},{2,18},{3,19},{4,20},{5,21},{6,22},{7,23},{8,24},{9,... | collective-permute-start | bytes 589832 | tf_op jit(solution)/shard_map/ppermute | solution.py:50
  8.4 7.9 %collective-permute-start.9 = (bf16[64,768]{1,0:T(8,128)(2,1)}, bf16[64,768]{1,0:T(8,128)(2,1)S(1)}, u32[]{:S(2)}, u32[]{:S(2)}) collective-permute-start(bf16[64,768]{1,0:T(8,128)(2,1)} %refs_1_.1), channel_id=1, source_target_pairs={{0,16},{1,17},{2,18},{3,19},{4,20},{5,21},{6,22},{7,23},{8,24},{9,... | collective-permute-start | bytes 294920 | tf_op jit(solution)/shard_map/ppermute | solution.py:50
  8.9 7.6 %collective-permute-start.6 = (bf16[64,768]{1,0:T(8,128)(2,1)}, bf16[64,768]{1,0:T(8,128)(2,1)S(1)}, u32[]{:S(2)}, u32[]{:S(2)}) collective-permute-start(bf16[64,768]{1,0:T(8,128)(2,1)} %refs_1_.1), channel_id=1, source_target_pairs={{0,8},{1,9},{2,10},{3,11},{4,12},{5,13},{6,14},{7,15},{8,0},{9,1},... | collective-permute-start | bytes 294920 | tf_op jit(solution)/shard_map/ppermute | solution.py:50
  16.3 15.3 %collective-permute-start.10 = (bf16[64,3840]{1,0:T(8,128)(2,1)S(1)}, bf16[64,3840]{1,0:T(8,128)(2,1)S(1)}, u32[]{:S(2)}, u32[]{:S(2)}) collective-permute-start(bf16[64,3840]{1,0:T(8,128)(2,1)S(1)} %shard_map.44), channel_id=1, source_target_pairs={{0,4},{1,5},{2,6},{3,7},{4,0},{5,1},{6,2},{7,3},{8,12},{9,13},{10,... | collective-permute-start | bytes 1474568 | tf_op jit(solution)/shard_map/ppermute | solution.py:50
  16.5 12.4 %collective-permute-start.12 = (bf16[64,1536]{1,0:T(8,128)(2,1)S(1)}, bf16[64,1536]{1,0:T(8,128)(2,1)S(1)}, u32[]{:S(2)}, u32[]{:S(2)}) collective-permute-start(bf16[64,1536]{1,0:T(8,128)(2,1)S(1)} %shard_map.45), channel_id=1, source_target_pairs={{0,2},{1,3},{2,0},{3,1},{4,6},{5,7},{6,4},{7,5},{8,10},{9,11},{10,... | collective-permute-start | bytes 589832 | tf_op jit(solution)/shard_map/ppermute | solution.py:50
  16.9 12.1 %collective-permute-start.8 = (bf16[64,1536]{1,0:T(8,128)(2,1)S(1)}, bf16[64,1536]{1,0:T(8,128)(2,1)S(1)}, u32[]{:S(2)}, u32[]{:S(2)}) collective-permute-start(bf16[64,1536]{1,0:T(8,128)(2,1)S(1)} %collective-permute-done.1.refs_0_.refs_5_), channel_id=1, source_target_pairs={{0,16},{1,17},{2,18},{3,19},{4,20},{5,21},{6,22},{7,23},{8,24},{9,... | collective-permute-start | bytes 589832 | tf_op jit(solution)/shard_map/ppermute | solution.py:50
  18.4 13.2 %collective-permute-start.5 = (bf16[64,3072]{1,0:T(8,128)(2,1)S(1)}, bf16[64,3072]{1,0:T(8,128)(2,1)S(1)}, u32[]{:S(2)}, u32[]{:S(2)}) collective-permute-start(bf16[64,3072]{1,0:T(8,128)(2,1)S(1)} %shard_map.42), channel_id=1, source_target_pairs={{0,8},{1,9},{2,10},{3,11},{4,12},{5,13},{6,14},{7,15},{8,0},{9,1},... | collective-permute-start | bytes 1179656 | tf_op jit(solution)/shard_map/ppermute | solution.py:50
  20.0 11.6 %collective-permute-start.7 = (bf16[64,1536]{1,0:T(8,128)(2,1)S(1)}, bf16[64,1536]{1,0:T(8,128)(2,1)S(1)}, u32[]{:S(2)}, u32[]{:S(2)}) collective-permute-start(bf16[64,1536]{1,0:T(8,128)(2,1)S(1)} %shard_map.43), channel_id=1, source_target_pairs={{0,1},{1,0},{2,3},{3,2},{4,5},{5,4},{6,7},{7,6},{8,9},{9,8},{10,11... | collective-permute-start | bytes 589832 | tf_op jit(solution)/shard_map/ppermute | solution.py:50
  28.9 2.7 %collective-permute-start.13 = (bf16[64,1536]{1,0:T(8,128)(2,1)S(1)}, bf16[64,1536]{1,0:T(8,128)(2,1)S(1)}, u32[]{:S(2)}, u32[]{:S(2)}) collective-permute-start(bf16[64,1536]{1,0:T(8,128)(2,1)S(1)} %collective-permute-done.12.refs_11_.refs_1_), channel_id=1, source_target_pairs={{0,4},{1,5},{2,6},{3,7},{4,0},{5,1},{6,2},{7,3},{8,12},{9,13},{10,... | collective-permute-start | bytes 589832 | tf_op jit(solution)/shard_map/ppermute | solution.py:50
  28.9 2.6 %collective-permute-start.11 = (bf16[64,1536]{1,0:T(8,128)(2,1)S(1)}, bf16[64,1536]{1,0:T(8,128)(2,1)S(1)}, u32[]{:S(2)}, u32[]{:S(2)}) collective-permute-start(bf16[64,1536]{1,0:T(8,128)(2,1)S(1)} %collective-permute-done.8.refs_7_), channel_id=1, source_target_pairs={{0,4},{1,5},{2,6},{3,7},{4,0},{5,1},{6,2},{7,3},{8,12},{9,13},{10,... | collective-permute-start | bytes 589832 | tf_op jit(solution)/shard_map/ppermute | solution.py:50
  32.7 1.3 %collective-permute-start.14 = (f32[3,12,64]{2,1,0:T(8,128)S(1)}, f32[3,12,64]{2,1,0:T(8,128)S(1)}, u32[]{:S(2)}, u32[]{:S(2)}) collective-permute-start(f32[3,12,64]{2,1,0:T(8,128)S(1)} %pad_maximum_fusion), channel_id=1, source_target_pairs={{0,4},{1,5},{2,6},{3,7},{4,0},{5,1},{6,2},{7,3},{8,12},{9,13},{10,... | collective-permute-start | bytes 27656 | tf_op jit(solution)/shard_map/ppermute | solution.py:50
  33.9 3.8 %collective-permute-start.15 = (f32[3,8,64]{2,1,0:T(8,128)S(1)}, f32[3,8,64]{2,1,0:T(8,128)S(1)}, u32[]{:S(2)}, u32[]{:S(2)}) collective-permute-start(f32[3,8,64]{2,1,0:T(8,128)S(1)} %maximum_select_fusion), channel_id=1, source_target_pairs={{0,1},{1,0},{2,3},{3,2},{4,6},{5,7},{6,4},{7,5},{8,9},{9,8},{10,11... | collective-permute-start | bytes 18440 | tf_op jit(solution)/shard_map/ppermute | solution.py:259
  37.8 3.8 %collective-permute-start.16 = (f32[3,8,64]{2,1,0:T(8,128)S(1)}, f32[3,8,64]{2,1,0:T(8,128)S(1)}, u32[]{:S(2)}, u32[]{:S(2)}) collective-permute-start(f32[3,8,64]{2,1,0:T(8,128)S(1)} %add.10), channel_id=1, source_target_pairs={{0,8},{1,9},{2,10},{3,11},{4,20},{5,21},{6,22},{7,23},{8,0},{9,1},... | collective-permute-start | bytes 18440 | tf_op jit(solution)/shard_map/ppermute | solution.py:259
  41.5 1.2 %collective-permute-start.17 = (f32[3,8,64]{2,1,0:T(8,128)S(1)}, f32[3,8,64]{2,1,0:T(8,128)S(1)}, u32[]{:S(2)}, u32[]{:S(2)}) collective-permute-start(f32[3,8,64]{2,1,0:T(8,128)S(1)} %add.11), channel_id=1, source_target_pairs={{0,4},{1,5},{2,6},{3,7},{4,0},{5,1},{6,2},{7,3},{8,12},{9,13},{10,... | collective-permute-start | bytes 18440 | tf_op jit(solution)/shard_map/ppermute | solution.py:50
  43.9 5.0 %collective-permute-start.18 = (f16[400,128]{1,0:T(8,128)(2,1)S(1)}, f16[400,128]{1,0:T(8,128)(2,1)S(1)}, u32[]{:S(2)}, u32[]{:S(2)}) collective-permute-start(f16[400,128]{1,0:T(8,128)(2,1)S(1)} %convert_element_type.18), channel_id=1, source_target_pairs={{0,8},{1,9},{2,10},{3,11},{4,12},{5,13},{6,14},{7,15},{8,0},{9,1},... | collective-permute-start | bytes 307208 | tf_op jit(solution)/shard_map/ppermute | solution.py:50
  44.5 5.7 %collective-permute-start.19 = (f16[400,128]{1,0:T(8,128)(2,1)S(1)}, f16[400,128]{1,0:T(8,128)(2,1)S(1)}, u32[]{:S(2)}, u32[]{:S(2)}) collective-permute-start(f16[400,128]{1,0:T(8,128)(2,1)S(1)} %convert_element_type.20), channel_id=1, source_target_pairs={{0,1},{1,0},{2,3},{3,2},{4,5},{5,4},{6,7},{7,6},{8,9},{9,8},{10,11... | collective-permute-start | bytes 307208 | tf_op jit(solution)/shard_map/ppermute | solution.py:50
  46.1 6.3 %collective-permute-start.20 = (f16[400,128]{1,0:T(8,128)(2,1)S(1)}, f16[400,128]{1,0:T(8,128)(2,1)S(1)}, u32[]{:S(2)}, u32[]{:S(2)}) collective-permute-start(f16[400,128]{1,0:T(8,128)(2,1)S(1)} %convert_element_type.22), channel_id=1, source_target_pairs={{0,9},{1,8},{2,11},{3,10},{4,13},{5,12},{6,15},{7,14},{8,1},{9,0},... | collective-permute-start | bytes 307208 | tf_op jit(solution)/shard_map/ppermute | solution.py:50

commit v22 on v21

--- a/solution.py
+++ b/solution.py
@@ -297,7 +297,7 @@
         [f32(rows, width), f32(8, 128)] + [f32(width // 128 * rows + EXTRA, 128)] * (n_row - 1),
         4 * math.prod(shape) * width,
     )
-    order = sorted(range(n_row - 1), key=lambda k: ((k + 1).bit_count(), -k))
+    order = sorted(range(n_row - 1), key=lambda k: (-(k + 1).bit_count(), -k))
     masks = span(row_masks)[1:]
     got = [send(pieces[k].astype(jnp.float16), masks[k], count).astype(jnp.float32) for k in order]
     grad, loss = call(

time: 53.3 us -> 53 us (level)
  transfers between devices with their start and end apart: 21 -> 21, of which waited for: 11 -> 10; matrix products, arithmetic and copies ran while one was open for 0% -> 0% of each run, Pallas kernels for 0% -> 0%
where the time goes in v22:
time: 53 us; the launch traced here: 52.9 us
  waiting for transfers between devices  27.2 us (51%)
  starting transfers between devices  21.5 us (41%)
  Pallas kernels  2.86 us (5%)
  between operations  0.84 us (2%)
    ppermute x19, waiting for transfers between devices, send(): return lax.ppermute(value, AXES, [(i, i ^ mask) for i in range(count)])  20.9 us
    ppermute x19, starting transfers between devices, send(): return lax.ppermute(value, AXES, [(i, i ^ mask) for i in range(count)])  20.3 us
    ppermute x2, waiting for transfers between devices, exchange_sums(): got = lax.ppermute(sums, AXES, pairs).reshape(3, -1, 2, 1 << b, rows)  6.32 us
    pallas_call x8, Pallas kernels, call(): pl.pallas_call(kernel, out_shape=outputs, **options, compiler_params=pltp...  2.86 us
    ppermute x2, starting transfers between devices, exchange_sums(): got = lax.ppermute(sums, AXES, pairs).reshape(3, -1, 2, 1 << b, rows)  1.2 us
  transfers between devices with their start and end apart: 21, of which 10 were waited for; matrix products, arithmetic and copies ran while one was open for 0% of the time, Pallas kernels for 0%

profile of v22, /device:TPU:0, one launch (start us, length us, event | category | flops | bytes accessed | tf_op | source)
XLA Modules:
  0.0 52.9 jit_solution(16310835738523277284)
XLA Ops:
  0.6 0.5 collective-permute-start.2
  1.2 0.1 collective-permute-start.3
  1.2 3.0 %collective-permute-start = (bf16[64,1536]{1,0:T(8,128)(2,1)}, bf16[64,1536]{1,0:T(8,128)(2,1)S(1)}, u32[]{:S(2)}, u32[]{:S(2)}) collective-permute-start(bf16[64,1536]{1,0:T(8,128)(2,1)} %refs_0_.1), channel_id=1, source_target_pairs={{0,1},{1,0},{2,3},{3,2},{4,5},{5,4},{6,7},{7,6},{8,9},{9,8},{10,11... | collective-permute-start | bytes 589832 | tf_op jit(solution)/shard_map/ppermute | solution.py:50
  4.2 2.6 %collective-permute-start.1 = (bf16[64,1536]{1,0:T(8,128)(2,1)}, bf16[64,1536]{1,0:T(8,128)(2,1)S(1)}, u32[]{:S(2)}, u32[]{:S(2)}) collective-permute-start(bf16[64,1536]{1,0:T(8,128)(2,1)} %refs_0_.1), channel_id=1, source_target_pairs={{0,2},{1,3},{2,0},{3,1},{4,6},{5,7},{6,4},{7,5},{8,10},{9,11},{10,... | collective-permute-start | bytes 589832 | tf_op jit(solution)/shard_map/ppermute | solution.py:50
  6.8 1.5 %collective-permute-start.4 = (bf16[64,1536]{1,0:T(8,128)(2,1)}, bf16[64,1536]{1,0:T(8,128)(2,1)S(1)}, u32[]{:S(2)}, u32[]{:S(2)}) collective-permute-start(bf16[64,1536]{1,0:T(8,128)(2,1)} %refs_0_.1), channel_id=1, source_target_pairs={{0,16},{1,17},{2,18},{3,19},{4,20},{5,21},{6,22},{7,23},{8,24},{9,... | collective-permute-start | bytes 589832 | tf_op jit(solution)/shard_map/ppermute | solution.py:50
  8.4 0.5 collective-permute-start.9
  8.9 1.5 %collective-permute-start.6 = (bf16[64,768]{1,0:T(8,128)(2,1)}, bf16[64,768]{1,0:T(8,128)(2,1)S(1)}, u32[]{:S(2)}, u32[]{:S(2)}) collective-permute-start(bf16[64,768]{1,0:T(8,128)(2,1)} %refs_1_.1), channel_id=1, source_target_pairs={{0,8},{1,9},{2,10},{3,11},{4,12},{5,13},{6,14},{7,15},{8,0},{9,1},... | collective-permute-start | bytes 294920 | tf_op jit(solution)/shard_map/ppermute | solution.py:50
  10.4 3.3 %collective-permute-done.refs_1_ = bf16[64,1536]{1,0:T(8,128)(2,1)S(1)} collective-permute-done((bf16[64,1536]{1,0:T(8,128)(2,1)}, bf16[64,1536]{1,0:T(8,128)(2,1)S(1)}, u32[]{:S(2)}, u32[]{:S(2)}) %collective-permute-start) | collective-permute-done | bytes 196640 | tf_op jit(solution)/shard_map/ppermute | solution.py:50
  13.7 2.6 %collective-permute-done.1.refs_0_.refs_5_ = bf16[64,1536]{1,0:T(8,128)(2,1)S(1)} collective-permute-done((bf16[64,1536]{1,0:T(8,128)(2,1)}, bf16[64,1536]{1,0:T(8,128)(2,1)S(1)}, u32[]{:S(2)}, u32[]{:S(2)}) %collective-permute-start.1) | collective-permute-done | bytes 196640 | tf_op jit(solution)/shard_map/ppermute | solution.py:50
  16.5 0.4 collective-permute-start.12
  16.9 1.5 %collective-permute-start.8 = (bf16[64,1536]{1,0:T(8,128)(2,1)S(1)}, bf16[64,1536]{1,0:T(8,128)(2,1)S(1)}, u32[]{:S(2)}, u32[]{:S(2)}) collective-permute-start(bf16[64,1536]{1,0:T(8,128)(2,1)S(1)} %collective-permute-done.1.refs_0_.refs_5_), channel_id=1, source_target_pairs={{0,16},{1,17},{2,18},{3,19},{4,20},{5,21},{6,22},{7,23},{8,24},{9,... | collective-permute-start | bytes 589832 | tf_op jit(solution)/shard_map/ppermute | solution.py:50
  18.4 1.6 %collective-permute-start.5 = (bf16[64,3072]{1,0:T(8,128)(2,1)S(1)}, bf16[64,3072]{1,0:T(8,128)(2,1)S(1)}, u32[]{:S(2)}, u32[]{:S(2)}) collective-permute-start(bf16[64,3072]{1,0:T(8,128)(2,1)S(1)} %shard_map.42), channel_id=1, source_target_pairs={{0,8},{1,9},{2,10},{3,11},{4,12},{5,13},{6,14},{7,15},{8,0},{9,1},... | collective-permute-start | bytes 1179656 | tf_op jit(solution)/shard_map/ppermute | solution.py:50
  20.0 2.8 %collective-permute-start.7 = (bf16[64,1536]{1,0:T(8,128)(2,1)S(1)}, bf16[64,1536]{1,0:T(8,128)(2,1)S(1)}, u32[]{:S(2)}, u32[]{:S(2)}) collective-permute-start(bf16[64,1536]{1,0:T(8,128)(2,1)S(1)} %shard_map.43), channel_id=1, source_target_pairs={{0,1},{1,0},{2,3},{3,2},{4,5},{5,4},{6,7},{7,6},{8,9},{9,8},{10,11... | collective-permute-start | bytes 589832 | tf_op jit(solution)/shard_map/ppermute | solution.py:50
  22.8 6.2 %collective-permute-done.12.refs_11_.refs_1_ = bf16[64,1536]{1,0:T(8,128)(2,1)S(1)} collective-permute-done((bf16[64,1536]{1,0:T(8,128)(2,1)S(1)}, bf16[64,1536]{1,0:T(8,128)(2,1)S(1)}, u32[]{:S(2)}, u32[]{:S(2)}) %collective-permute-start.12) | collective-permute-done | bytes 196640 | tf_op jit(solution)/shard_map/ppermute | solution.py:50
  28.9 0.5 collective-permute-start.11
  29.4 2.1 %collective-permute-done.7.refs_3_ = bf16[64,1536]{1,0:T(8,128)(2,1)S(1)} collective-permute-done((bf16[64,1536]{1,0:T(8,128)(2,1)S(1)}, bf16[64,1536]{1,0:T(8,128)(2,1)S(1)}, u32[]{:S(2)}, u32[]{:S(2)}) %collective-permute-start.7) | collective-permute-done | bytes 196640 | tf_op jit(solution)/shard_map/ppermute | solution.py:50
  31.6 1.0 %shard_map.46 = (f32[256,512]{1,0:T(8,128)S(1)}, f32[256,512]{1,0:T(8,128)S(1)}, f32[3,4,64]{2,1,0:T(4,128)S(1)}, f32[3,8,64]{2,1,0:T(8,128)S(1)}) custom-call(bf16[64,2304]{1,0:T(8,128)(2,1)S(1)} %shard_map.41.refs_0_, bf16[64,1536]{1,0:T(8,128)(2,1)S(1)} %collective-permute-done.refs_1_, bf16[64,3072]{1,0:T(8,128)(2,1)S(1)} %collective-permute-done.5.refs_2_, ...), custom_call_target="tpu_custom_call" | custom-call | flops 603979776 | bytes 4301824 | tf_op jit(solution)/shard_map/pallas_call | solution.py:186
  32.7 1.2 %collective-permute-done.14 = f32[3,12,64]{2,1,0:T(8,128)S(1)} collective-permute-done((f32[3,12,64]{2,1,0:T(8,128)S(1)}, f32[3,12,64]{2,1,0:T(8,128)S(1)}, u32[]{:S(2)}, u32[]{:S(2)}) %collective-permute-start.14) | collective-permute-done | bytes 9248 | tf_op jit(solution)/shard_map/ppermute | solution.py:50
  33.9 0.6 %collective-permute-start.15 = (f32[3,8,64]{2,1,0:T(8,128)S(1)}, f32[3,8,64]{2,1,0:T(8,128)S(1)}, u32[]{:S(2)}, u32[]{:S(2)}) collective-permute-start(f32[3,8,64]{2,1,0:T(8,128)S(1)} %maximum_select_fusion), channel_id=1, source_target_pairs={{0,1},{1,0},{2,3},{3,2},{4,6},{5,7},{6,4},{7,5},{8,9},{9,8},{10,11... | collective-permute-start | bytes 18440 | tf_op jit(solution)/shard_map/ppermute | solution.py:259
  34.5 3.2 %collective-permute-done.15 = f32[3,8,64]{2,1,0:T(8,128)S(1)} collective-permute-done((f32[3,8,64]{2,1,0:T(8,128)S(1)}, f32[3,8,64]{2,1,0:T(8,128)S(1)}, u32[]{:S(2)}, u32[]{:S(2)}) %collective-permute-start.15) | collective-permute-done | bytes 6176 | tf_op jit(solution)/shard_map/ppermute | solution.py:259
  37.8 0.6 %collective-permute-start.16 = (f32[3,8,64]{2,1,0:T(8,128)S(1)}, f32[3,8,64]{2,1,0:T(8,128)S(1)}, u32[]{:S(2)}, u32[]{:S(2)}) collective-permute-start(f32[3,8,64]{2,1,0:T(8,128)S(1)} %add.10), channel_id=1, source_target_pairs={{0,8},{1,9},{2,10},{3,11},{4,20},{5,21},{6,22},{7,23},{8,0},{9,1},... | collective-permute-start | bytes 18440 | tf_op jit(solution)/shard_map/ppermute | solution.py:259
  38.4 3.2 %collective-permute-done.16 = f32[3,8,64]{2,1,0:T(8,128)S(1)} collective-permute-done((f32[3,8,64]{2,1,0:T(8,128)S(1)}, f32[3,8,64]{2,1,0:T(8,128)S(1)}, u32[]{:S(2)}, u32[]{:S(2)}) %collective-permute-start.16) | collective-permute-done | bytes 6176 | tf_op jit(solution)/shard_map/ppermute | solution.py:259
  41.6 1.2 %collective-permute-done.17 = f32[3,8,64]{2,1,0:T(8,128)S(1)} collective-permute-done((f32[3,8,64]{2,1,0:T(8,128)S(1)}, f32[3,8,64]{2,1,0:T(8,128)S(1)}, u32[]{:S(2)}, u32[]{:S(2)}) %collective-permute-start.17) | collective-permute-done | bytes 6176 | tf_op jit(solution)/shard_map/ppermute | solution.py:50
  42.8 0.1 reshape.27.col_sum
  42.9 0.1 reshape.26.row_sum
  43.0 0.9 %shard_map.47 = (f32[64,768]{1,0:T(8,128)S(1)}, f32[8,128]{1,0:T(8,128)S(1)}, f32[400,128]{1,0:T(8,128)S(1)}, f32[400,128]{1,0:T(8,128)S(1)}, f32[400,128]{1,0:T(8,128)S(1)}) custom-call(f32[256,512]{1,0:T(8,128)S(1)} %get-tuple-element.25.gram_s, f32[256,512]{1,0:T(8,128)S(1)} %get-tuple-element.26.gram_t, f32[3,1,256]{2,1,0:T(1,128)S(1)} %reshape.26.row_sum, ...), custom_call_target="tpu_custom_call" | custom-call | flops 402653184 | bytes 3249152 | tf_op jit(solution)/shard_map/pallas_call | solution.py:186
  43.9 1.5 %collective-permute-start.18 = (f16[400,128]{1,0:T(8,128)(2,1)S(1)}, f16[400,128]{1,0:T(8,128)(2,1)S(1)}, u32[]{:S(2)}, u32[]{:S(2)}) collective-permute-start(f16[400,128]{1,0:T(8,128)(2,1)S(1)} %convert_element_type.18), channel_id=1, source_target_pairs={{0,9},{1,8},{2,11},{3,10},{4,13},{5,12},{6,15},{7,14},{8,1},{9,0},... | collective-permute-start | bytes 307208 | tf_op jit(solution)/shard_map/ppermute | solution.py:50
  45.4 0.6 %collective-permute-start.19 = (f16[400,128]{1,0:T(8,128)(2,1)S(1)}, f16[400,128]{1,0:T(8,128)(2,1)S(1)}, u32[]{:S(2)}, u32[]{:S(2)}) collective-permute-start(f16[400,128]{1,0:T(8,128)(2,1)S(1)} %convert_element_type.20), channel_id=1, source_target_pairs={{0,8},{1,9},{2,10},{3,11},{4,12},{5,13},{6,14},{7,15},{8,0},{9,1},... | collective-permute-start | bytes 307208 | tf_op jit(solution)/shard_map/ppermute | solution.py:50
  46.0 1.6 %collective-permute-start.20 = (f16[400,128]{1,0:T(8,128)(2,1)S(1)}, f16[400,128]{1,0:T(8,128)(2,1)S(1)}, u32[]{:S(2)}, u32[]{:S(2)}) collective-permute-start(f16[400,128]{1,0:T(8,128)(2,1)S(1)} %convert_element_type.22), channel_id=1, source_target_pairs={{0,1},{1,0},{2,3},{3,2},{4,5},{5,4},{6,7},{7,6},{8,9},{9,8},{10,11... | collective-permute-start | bytes 307208 | tf_op jit(solution)/shard_map/ppermute | solution.py:50
  47.6 2.8 %collective-permute-done.18 = f16[400,128]{1,0:T(8,128)(2,1)S(1)} collective-permute-done((f16[400,128]{1,0:T(8,128)(2,1)S(1)}, f16[400,128]{1,0:T(8,128)(2,1)S(1)}, u32[]{:S(2)}, u32[]{:S(2)}) %collective-permute-start.18) | collective-permute-done | bytes 102432 | tf_op jit(solution)/shard_map/ppermute | solution.py:50
  50.4 1.6 %collective-permute-done.19 = f16[400,128]{1,0:T(8,128)(2,1)S(1)} collective-permute-done((f16[400,128]{1,0:T(8,128)(2,1)S(1)}, f16[400,128]{1,0:T(8,128)(2,1)S(1)}, u32[]{:S(2)}, u32[]{:S(2)}) %collective-permute-start.19) | collective-permute-done | bytes 102432 | tf_op jit(solution)/shard_map/ppermute | solution.py:50
  52.0 0.8 %shard_map.48 = (f32[64,768]{1,0:T(8,128)}, f32[1,1]{1,0:T(1,128)}) custom-call(f32[64,768]{1,0:T(8,128)S(1)} %get-tuple-element.29.own, f32[8,128]{1,0:T(8,128)S(1)} %get-tuple-element.30.share, f32[400,128]{1,0:T(8,128)S(1)} %convert_element_type.19.refs_0_, f32[400,128]{1,0:T(8,128)S(1)} %convert_element_type.21.refs_1_, ...), custom_call_target="tpu_custom_call" | custom-call | bytes 1011716 | tf_op jit(solution)/shard_map/pallas_call | solution.py:186
  (41 shorter events, 0.6 us)
Async XLA Ops:
  0.6 15.7 %copy-start = (bf16[64,1536]{1,0:T(8,128)(2,1)S(1)}, bf16[64,1536]{1,0:T(8,128)(2,1)}, u32[]{:S(2)}) copy-start(bf16[64,1536]{1,0:T(8,128)(2,1)} %refs_0_.1) | copy-start | bytes 589828
  0.6 15.7 %copy-start.1 = (bf16[64,768]{1,0:T(8,128)(2,1)S(1)}, bf16[64,768]{1,0:T(8,128)(2,1)}, u32[]{:S(2)}) copy-start(bf16[64,768]{1,0:T(8,128)(2,1)} %refs_1_.1) | copy-start | bytes 294916
  0.6 6.2 %collective-permute-start.2 = (bf16[64,1536]{1,0:T(8,128)(2,1)}, bf16[64,1536]{1,0:T(8,128)(2,1)S(1)}, u32[]{:S(2)}, u32[]{:S(2)}) collective-permute-start(bf16[64,1536]{1,0:T(8,128)(2,1)} %refs_0_.1), channel_id=1, source_target_pairs={{0,4},{1,5},{2,6},{3,7},{4,0},{5,1},{6,2},{7,3},{8,12},{9,13},{10,... | collective-permute-start | bytes 589832 | tf_op jit(solution)/shard_map/ppermute | solution.py:50
  1.2 5.7 %collective-permute-start.3 = (bf16[64,768]{1,0:T(8,128)(2,1)}, bf16[64,768]{1,0:T(8,128)(2,1)S(1)}, u32[]{:S(2)}, u32[]{:S(2)}) collective-permute-start(bf16[64,768]{1,0:T(8,128)(2,1)} %refs_1_.1), channel_id=1, source_target_pairs={{0,4},{1,5},{2,6},{3,7},{4,0},{5,1},{6,2},{7,3},{8,12},{9,13},{10,... | collective-permute-start | bytes 294920 | tf_op jit(solution)/shard_map/ppermute | solution.py:50
  1.2 12.4 %collective-permute-start = (bf16[64,1536]{1,0:T(8,128)(2,1)}, bf16[64,1536]{1,0:T(8,128)(2,1)S(1)}, u32[]{:S(2)}, u32[]{:S(2)}) collective-permute-start(bf16[64,1536]{1,0:T(8,128)(2,1)} %refs_0_.1), channel_id=1, source_target_pairs={{0,1},{1,0},{2,3},{3,2},{4,5},{5,4},{6,7},{7,6},{8,9},{9,8},{10,11... | collective-permute-start | bytes 589832 | tf_op jit(solution)/shard_map/ppermute | solution.py:50
  4.2 12.0 %collective-permute-start.1 = (bf16[64,1536]{1,0:T(8,128)(2,1)}, bf16[64,1536]{1,0:T(8,128)(2,1)S(1)}, u32[]{:S(2)}, u32[]{:S(2)}) collective-permute-start(bf16[64,1536]{1,0:T(8,128)(2,1)} %refs_0_.1), channel_id=1, source_target_pairs={{0,2},{1,3},{2,0},{3,1},{4,6},{5,7},{6,4},{7,5},{8,10},{9,11},{10,... | collective-permute-start | bytes 589832 | tf_op jit(solution)/shard_map/ppermute | solution.py:50
  6.8 9.4 %collective-permute-start.4 = (bf16[64,1536]{1,0:T(8,128)(2,1)}, bf16[64,1536]{1,0:T(8,128)(2,1)S(1)}, u32[]{:S(2)}, u32[]{:S(2)}) collective-permute-start(bf16[64,1536]{1,0:T(8,128)(2,1)} %refs_0_.1), channel_id=1, source_target_pairs={{0,16},{1,17},{2,18},{3,19},{4,20},{5,21},{6,22},{7,23},{8,24},{9,... | collective-permute-start | bytes 589832 | tf_op jit(solution)/shard_map/ppermute | solution.py:50
  8.4 7.9 %collective-permute-start.9 = (bf16[64,768]{1,0:T(8,128)(2,1)}, bf16[64,768]{1,0:T(8,128)(2,1)S(1)}, u32[]{:S(2)}, u32[]{:S(2)}) collective-permute-start(bf16[64,768]{1,0:T(8,128)(2,1)} %refs_1_.1), channel_id=1, source_target_pairs={{0,16},{1,17},{2,18},{3,19},{4,20},{5,21},{6,22},{7,23},{8,24},{9,... | collective-permute-start | bytes 294920 | tf_op jit(solution)/shard_map/ppermute | solution.py:50
  8.9 7.6 %collective-permute-start.6 = (bf16[64,768]{1,0:T(8,128)(2,1)}, bf16[64,768]{1,0:T(8,128)(2,1)S(1)}, u32[]{:S(2)}, u32[]{:S(2)}) collective-permute-start(bf16[64,768]{1,0:T(8,128)(2,1)} %refs_1_.1), channel_id=1, source_target_pairs={{0,8},{1,9},{2,10},{3,11},{4,12},{5,13},{6,14},{7,15},{8,0},{9,1},... | collective-permute-start | bytes 294920 | tf_op jit(solution)/shard_map/ppermute | solution.py:50
  16.3 15.3 %collective-permute-start.10 = (bf16[64,3840]{1,0:T(8,128)(2,1)S(1)}, bf16[64,3840]{1,0:T(8,128)(2,1)S(1)}, u32[]{:S(2)}, u32[]{:S(2)}) collective-permute-start(bf16[64,3840]{1,0:T(8,128)(2,1)S(1)} %shard_map.44), channel_id=1, source_target_pairs={{0,4},{1,5},{2,6},{3,7},{4,0},{5,1},{6,2},{7,3},{8,12},{9,13},{10,... | collective-permute-start | bytes 1474568 | tf_op jit(solution)/shard_map/ppermute | solution.py:50
  16.5 12.4 %collective-permute-start.12 = (bf16[64,1536]{1,0:T(8,128)(2,1)S(1)}, bf16[64,1536]{1,0:T(8,128)(2,1)S(1)}, u32[]{:S(2)}, u32[]{:S(2)}) collective-permute-start(bf16[64,1536]{1,0:T(8,128)(2,1)S(1)} %shard_map.45), channel_id=1, source_target_pairs={{0,2},{1,3},{2,0},{3,1},{4,6},{5,7},{6,4},{7,5},{8,10},{9,11},{10,... | collective-permute-start | bytes 589832 | tf_op jit(solution)/shard_map/ppermute | solution.py:50
  16.9 12.1 %collective-permute-start.8 = (bf16[64,1536]{1,0:T(8,128)(2,1)S(1)}, bf16[64,1536]{1,0:T(8,128)(2,1)S(1)}, u32[]{:S(2)}, u32[]{:S(2)}) collective-permute-start(bf16[64,1536]{1,0:T(8,128)(2,1)S(1)} %collective-permute-done.1.refs_0_.refs_5_), channel_id=1, source_target_pairs={{0,16},{1,17},{2,18},{3,19},{4,20},{5,21},{6,22},{7,23},{8,24},{9,... | collective-permute-start | bytes 589832 | tf_op jit(solution)/shard_map/ppermute | solution.py:50
  18.4 13.2 %collective-permute-start.5 = (bf16[64,3072]{1,0:T(8,128)(2,1)S(1)}, bf16[64,3072]{1,0:T(8,128)(2,1)S(1)}, u32[]{:S(2)}, u32[]{:S(2)}) collective-permute-start(bf16[64,3072]{1,0:T(8,128)(2,1)S(1)} %shard_map.42), channel_id=1, source_target_pairs={{0,8},{1,9},{2,10},{3,11},{4,12},{5,13},{6,14},{7,15},{8,0},{9,1},... | collective-permute-start | bytes 1179656 | tf_op jit(solution)/shard_map/ppermute | solution.py:50
  20.0 11.6 %collective-permute-start.7 = (bf16[64,1536]{1,0:T(8,128)(2,1)S(1)}, bf16[64,1536]{1,0:T(8,128)(2,1)S(1)}, u32[]{:S(2)}, u32[]{:S(2)}) collective-permute-start(bf16[64,1536]{1,0:T(8,128)(2,1)S(1)} %shard_map.43), channel_id=1, source_target_pairs={{0,1},{1,0},{2,3},{3,2},{4,5},{5,4},{6,7},{7,6},{8,9},{9,8},{10,11... | collective-permute-start | bytes 589832 | tf_op jit(solution)/shard_map/ppermute | solution.py:50
  28.9 2.7 %collective-permute-start.13 = (bf16[64,1536]{1,0:T(8,128)(2,1)S(1)}, bf16[64,1536]{1,0:T(8,128)(2,1)S(1)}, u32[]{:S(2)}, u32[]{:S(2)}) collective-permute-start(bf16[64,1536]{1,0:T(8,128)(2,1)S(1)} %collective-permute-done.12.refs_11_.refs_1_), channel_id=1, source_target_pairs={{0,4},{1,5},{2,6},{3,7},{4,0},{5,1},{6,2},{7,3},{8,12},{9,13},{10,... | collective-permute-start | bytes 589832 | tf_op jit(solution)/shard_map/ppermute | solution.py:50
  28.9 2.6 %collective-permute-start.11 = (bf16[64,1536]{1,0:T(8,128)(2,1)S(1)}, bf16[64,1536]{1,0:T(8,128)(2,1)S(1)}, u32[]{:S(2)}, u32[]{:S(2)}) collective-permute-start(bf16[64,1536]{1,0:T(8,128)(2,1)S(1)} %collective-permute-done.8.refs_7_), channel_id=1, source_target_pairs={{0,4},{1,5},{2,6},{3,7},{4,0},{5,1},{6,2},{7,3},{8,12},{9,13},{10,... | collective-permute-start | bytes 589832 | tf_op jit(solution)/shard_map/ppermute | solution.py:50
  32.7 1.3 %collective-permute-start.14 = (f32[3,12,64]{2,1,0:T(8,128)S(1)}, f32[3,12,64]{2,1,0:T(8,128)S(1)}, u32[]{:S(2)}, u32[]{:S(2)}) collective-permute-start(f32[3,12,64]{2,1,0:T(8,128)S(1)} %pad_maximum_fusion), channel_id=1, source_target_pairs={{0,4},{1,5},{2,6},{3,7},{4,0},{5,1},{6,2},{7,3},{8,12},{9,13},{10,... | collective-permute-start | bytes 27656 | tf_op jit(solution)/shard_map/ppermute | solution.py:50
  33.9 3.8 %collective-permute-start.15 = (f32[3,8,64]{2,1,0:T(8,128)S(1)}, f32[3,8,64]{2,1,0:T(8,128)S(1)}, u32[]{:S(2)}, u32[]{:S(2)}) collective-permute-start(f32[3,8,64]{2,1,0:T(8,128)S(1)} %maximum_select_fusion), channel_id=1, source_target_pairs={{0,1},{1,0},{2,3},{3,2},{4,6},{5,7},{6,4},{7,5},{8,9},{9,8},{10,11... | collective-permute-start | bytes 18440 | tf_op jit(solution)/shard_map/ppermute | solution.py:259
  37.8 3.8 %collective-permute-start.16 = (f32[3,8,64]{2,1,0:T(8,128)S(1)}, f32[3,8,64]{2,1,0:T(8,128)S(1)}, u32[]{:S(2)}, u32[]{:S(2)}) collective-permute-start(f32[3,8,64]{2,1,0:T(8,128)S(1)} %add.10), channel_id=1, source_target_pairs={{0,8},{1,9},{2,10},{3,11},{4,20},{5,21},{6,22},{7,23},{8,0},{9,1},... | collective-permute-start | bytes 18440 | tf_op jit(solution)/shard_map/ppermute | solution.py:259
  41.5 1.2 %collective-permute-start.17 = (f32[3,8,64]{2,1,0:T(8,128)S(1)}, f32[3,8,64]{2,1,0:T(8,128)S(1)}, u32[]{:S(2)}, u32[]{:S(2)}) collective-permute-start(f32[3,8,64]{2,1,0:T(8,128)S(1)} %add.11), channel_id=1, source_target_pairs={{0,4},{1,5},{2,6},{3,7},{4,0},{5,1},{6,2},{7,3},{8,12},{9,13},{10,... | collective-permute-start | bytes 18440 | tf_op jit(solution)/shard_map/ppermute | solution.py:50
  43.9 6.5 %collective-permute-start.18 = (f16[400,128]{1,0:T(8,128)(2,1)S(1)}, f16[400,128]{1,0:T(8,128)(2,1)S(1)}, u32[]{:S(2)}, u32[]{:S(2)}) collective-permute-start(f16[400,128]{1,0:T(8,128)(2,1)S(1)} %convert_element_type.18), channel_id=1, source_target_pairs={{0,9},{1,8},{2,11},{3,10},{4,13},{5,12},{6,15},{7,14},{8,1},{9,0},... | collective-permute-start | bytes 307208 | tf_op jit(solution)/shard_map/ppermute | solution.py:50
  45.4 6.6 %collective-permute-start.19 = (f16[400,128]{1,0:T(8,128)(2,1)S(1)}, f16[400,128]{1,0:T(8,128)(2,1)S(1)}, u32[]{:S(2)}, u32[]{:S(2)}) collective-permute-start(f16[400,128]{1,0:T(8,128)(2,1)S(1)} %convert_element_type.20), channel_id=1, source_target_pairs={{0,8},{1,9},{2,10},{3,11},{4,12},{5,13},{6,14},{7,15},{8,0},{9,1},... | collective-permute-start | bytes 307208 | tf_op jit(solution)/shard_map/ppermute | solution.py:50
  46.0 6.0 %collective-permute-start.20 = (f16[400,128]{1,0:T(8,128)(2,1)S(1)}, f16[400,128]{1,0:T(8,128)(2,1)S(1)}, u32[]{:S(2)}, u32[]{:S(2)}) collective-permute-start(f16[400,128]{1,0:T(8,128)(2,1)S(1)} %convert_element_type.22), channel_id=1, source_target_pairs={{0,1},{1,0},{2,3},{3,2},{4,5},{5,4},{6,7},{7,6},{8,9},{9,8},{10,11... | collective-permute-start | bytes 307208 | tf_op jit(solution)/shard_map/ppermute | solution.py:50

commit v23 on v19

--- a/solution.py
+++ b/solution.py
@@ -171,12 +171,20 @@
                 sums[k, p : p + 1, :] = source[:, p * rows : (p + 1) * rows]
 
 
-def gram_kernel(groups, *refs):
-    *arrays, gram_s, gram_t, row_part, col_part = refs
+def early_kernel(groups, *refs):
+    *arrays, gram_s, gram_t = refs
     row_t, row_s, col_t, col_s = [load(arrays, group) for group in groups]
     dims = (((1,), (1,)), ((), ()))
-    student = lax.dot_general(row_s, col_s, dims, preferred_element_type=jnp.float32)
-    teacher = lax.dot_general(row_t, col_t, dims, preferred_element_type=jnp.float32)
+    gram_s[...] = lax.dot_general(row_s, col_s, dims, preferred_element_type=jnp.float32)
+    gram_t[...] = lax.dot_general(row_t, col_t, dims, preferred_element_type=jnp.float32)
+
+
+def gram_kernel(groups, early_s, early_t, *refs):
+    *arrays, gram_s, gram_t, row_part, col_part = refs
+    late_t, col_t = [load(arrays, group) for group in groups]
+    dims = (((1,), (1,)), ((), ()))
+    late = lax.dot_general(late_t, col_t, dims, preferred_element_type=jnp.float32)
+    student, teacher = early_s[...], jnp.concatenate([early_t[...], late])
     gram_s[...], gram_t[...] = student, teacher
     put_sums([student * student, teacher * teacher, student * teacher], row_part, col_part)
 
@@ -280,12 +288,22 @@
     def f32(*dims):
         return jax.ShapeDtypeStruct(dims, jnp.float32)
 
-    arrays, groups = operands_of(*pieces)
+    row_t, row_s, col_t, col_s = pieces
+    half = n_row // 2
+    flops = 2 * math.prod(shape) * (teacher.shape[1] + width)
+    arrays, groups = operands_of(row_t[:half], row_s, col_t, col_s)
+    early = call(
+        functools.partial(early_kernel, groups),
+        arrays,
+        [f32(*shape), f32(half * rows, shape[1])],
+        flops // 2,
+    )
+    arrays, groups = operands_of(row_t[half:], col_t)
     gram_s, gram_t, row_part, col_part = call(
         functools.partial(gram_kernel, groups),
-        arrays,
+        [*early, *arrays],
         [f32(*shape), f32(*shape), f32(3, n_row, rows), f32(3, n_col, rows)],
-        2 * math.prod(shape) * (teacher.shape[1] + width),
+        flops // 2,
     )
     row_part, col_part = exchange_sums(row_part, col_part, row_masks, col_masks, count)
     row_sum, col_sum = row_part.reshape(3, 1, -1), col_part.reshape(3, 1, -1)

time: 52.7 us -> 53 us (level)
  Pallas kernels: 2.86 us -> 3.59 us
    pallas_call x8 -> x9, Pallas kernels: 2.86 us -> 3.59 us  [call(): pl.pallas_call(kernel, out_shape=outputs, **options, compiler_params=pltp...]
    ppermute x2, waiting for transfers between devices: 6.32 us -> 6.87 us  [exchange_sums(): got = lax.ppermute(sums, AXES, pairs).reshape(3, -1, 2, 1 << b, rows)]
    ppermute x2, starting transfers between devices: 1.2 us -> 0.65 us  [exchange_sums(): got = lax.ppermute(sums, AXES, pairs).reshape(3, -1, 2, 1 << b, rows)]
  transfers between devices with their start and end apart: 21 -> 21, of which waited for: 11 -> 10; matrix products, arithmetic and copies ran while one was open for 0% -> 0% of each run, Pallas kernels for 0% -> 2%
where the time goes in v23:
time: 53 us; the launch traced here: 52.8 us
  waiting for transfers between devices  27 us (51%)
  starting transfers between devices  21 us (40%)
  Pallas kernels  3.59 us (7%)
  between operations  0.86 us (2%)
    ppermute x19, starting transfers between devices, send(): return lax.ppermute(value, AXES, [(i, i ^ mask) for i in range(count)])  20.3 us
    ppermute x19, waiting for transfers between devices, send(): return lax.ppermute(value, AXES, [(i, i ^ mask) for i in range(count)])  20.1 us
    ppermute x2, waiting for transfers between devices, exchange_sums(): got = lax.ppermute(sums, AXES, pairs).reshape(3, -1, 2, 1 << b, rows)  6.87 us
    pallas_call x9, Pallas kernels, call(): pl.pallas_call(kernel, out_shape=outputs, **options, compiler_params=pltp...  3.59 us
  transfers between devices with their start and end apart: 21, of which 10 were waited for; matrix products, arithmetic and copies ran while one was open for 0% of the time, Pallas kernels for 2%

profile of v23, /device:TPU:0, one launch (start us, length us, event | category | flops | bytes accessed | tf_op | source)
XLA Modules:
  0.0 52.8 jit_solution(9560659015195179440)
XLA Ops:
  0.6 0.5 collective-permute-start.2
  1.2 0.1 collective-permute-start.3
  1.2 3.0 %collective-permute-start = (bf16[64,1536]{1,0:T(8,128)(2,1)}, bf16[64,1536]{1,0:T(8,128)(2,1)S(1)}, u32[]{:S(2)}, u32[]{:S(2)}) collective-permute-start(bf16[64,1536]{1,0:T(8,128)(2,1)} %refs_0_.1), channel_id=1, source_target_pairs={{0,1},{1,0},{2,3},{3,2},{4,5},{5,4},{6,7},{7,6},{8,9},{9,8},{10,11... | collective-permute-start | bytes 589832 | tf_op jit(solution)/shard_map/ppermute | solution.py:50
  4.2 2.6 %collective-permute-start.1 = (bf16[64,1536]{1,0:T(8,128)(2,1)}, bf16[64,1536]{1,0:T(8,128)(2,1)S(1)}, u32[]{:S(2)}, u32[]{:S(2)}) collective-permute-start(bf16[64,1536]{1,0:T(8,128)(2,1)} %refs_0_.1), channel_id=1, source_target_pairs={{0,2},{1,3},{2,0},{3,1},{4,6},{5,7},{6,4},{7,5},{8,10},{9,11},{10,... | collective-permute-start | bytes 589832 | tf_op jit(solution)/shard_map/ppermute | solution.py:50
  6.8 1.5 %collective-permute-start.4 = (bf16[64,1536]{1,0:T(8,128)(2,1)}, bf16[64,1536]{1,0:T(8,128)(2,1)S(1)}, u32[]{:S(2)}, u32[]{:S(2)}) collective-permute-start(bf16[64,1536]{1,0:T(8,128)(2,1)} %refs_0_.1), channel_id=1, source_target_pairs={{0,16},{1,17},{2,18},{3,19},{4,20},{5,21},{6,22},{7,23},{8,24},{9,... | collective-permute-start | bytes 589832 | tf_op jit(solution)/shard_map/ppermute | solution.py:50
  8.4 0.5 collective-permute-start.8
  8.9 1.5 %collective-permute-start.5 = (bf16[64,768]{1,0:T(8,128)(2,1)}, bf16[64,768]{1,0:T(8,128)(2,1)S(1)}, u32[]{:S(2)}, u32[]{:S(2)}) collective-permute-start(bf16[64,768]{1,0:T(8,128)(2,1)} %refs_1_.1), channel_id=1, source_target_pairs={{0,8},{1,9},{2,10},{3,11},{4,12},{5,13},{6,14},{7,15},{8,0},{9,1},... | collective-permute-start | bytes 294920 | tf_op jit(solution)/shard_map/ppermute | solution.py:50
  10.4 3.3 %collective-permute-done.refs_1_ = bf16[64,1536]{1,0:T(8,128)(2,1)S(1)} collective-permute-done((bf16[64,1536]{1,0:T(8,128)(2,1)}, bf16[64,1536]{1,0:T(8,128)(2,1)S(1)}, u32[]{:S(2)}, u32[]{:S(2)}) %collective-permute-start) | collective-permute-done | bytes 196640 | tf_op jit(solution)/shard_map/ppermute | solution.py:50
  13.7 2.6 %collective-permute-done.1.refs_0_.refs_4_.refs_2_ = bf16[64,1536]{1,0:T(8,128)(2,1)S(1)} collective-permute-done((bf16[64,1536]{1,0:T(8,128)(2,1)}, bf16[64,1536]{1,0:T(8,128)(2,1)S(1)}, u32[]{:S(2)}, u32[]{:S(2)}) %collective-permute-start.1) | collective-permute-done | bytes 196640 | tf_op jit(solution)/shard_map/ppermute | solution.py:50
  16.3 0.1 collective-permute-start.9
  16.5 0.4 collective-permute-start.11
  16.8 1.5 %collective-permute-start.7 = (bf16[64,1536]{1,0:T(8,128)(2,1)S(1)}, bf16[64,1536]{1,0:T(8,128)(2,1)S(1)}, u32[]{:S(2)}, u32[]{:S(2)}) collective-permute-start(bf16[64,1536]{1,0:T(8,128)(2,1)S(1)} %collective-permute-done.1.refs_0_.refs_4_.refs_2_), channel_id=1, source_target_pairs={{0,16},{1,17},{2,18},{3,19},{4,20},{5,21},{6,22},{7,23},{8,24},{9,... | collective-permute-start | bytes 589832 | tf_op jit(solution)/shard_map/ppermute | solution.py:50
  18.4 1.6 %collective-permute-start.13 = (bf16[64,3072]{1,0:T(8,128)(2,1)S(1)}, bf16[64,3072]{1,0:T(8,128)(2,1)S(1)}, u32[]{:S(2)}, u32[]{:S(2)}) collective-permute-start(bf16[64,3072]{1,0:T(8,128)(2,1)S(1)} %shard_map.46), channel_id=1, source_target_pairs={{0,8},{1,9},{2,10},{3,11},{4,12},{5,13},{6,14},{7,15},{8,0},{9,1},... | collective-permute-start | bytes 1179656 | tf_op jit(solution)/shard_map/ppermute | solution.py:50
  20.0 2.8 %collective-permute-start.6 = (bf16[64,1536]{1,0:T(8,128)(2,1)S(1)}, bf16[64,1536]{1,0:T(8,128)(2,1)S(1)}, u32[]{:S(2)}, u32[]{:S(2)}) collective-permute-start(bf16[64,1536]{1,0:T(8,128)(2,1)S(1)} %shard_map.42), channel_id=1, source_target_pairs={{0,1},{1,0},{2,3},{3,2},{4,5},{5,4},{6,7},{7,6},{8,9},{9,8},{10,11... | collective-permute-start | bytes 589832 | tf_op jit(solution)/shard_map/ppermute | solution.py:50
  22.8 6.1 %collective-permute-done.11.refs_10_.refs_1_ = bf16[64,1536]{1,0:T(8,128)(2,1)S(1)} collective-permute-done((bf16[64,1536]{1,0:T(8,128)(2,1)S(1)}, bf16[64,1536]{1,0:T(8,128)(2,1)S(1)}, u32[]{:S(2)}, u32[]{:S(2)}) %collective-permute-start.11) | collective-permute-done | bytes 196640 | tf_op jit(solution)/shard_map/ppermute | solution.py:50
  28.9 0.5 collective-permute-start.10
  29.4 2.2 %collective-permute-done.6.refs_2_ = bf16[64,1536]{1,0:T(8,128)(2,1)S(1)} collective-permute-done((bf16[64,1536]{1,0:T(8,128)(2,1)S(1)}, bf16[64,1536]{1,0:T(8,128)(2,1)S(1)}, u32[]{:S(2)}, u32[]{:S(2)}) %collective-permute-start.6) | collective-permute-done | bytes 196640 | tf_op jit(solution)/shard_map/ppermute | solution.py:50
  31.6 0.8 %shard_map.45 = (f32[256,512]{1,0:T(8,128)S(1)}, f32[128,512]{1,0:T(8,128)S(1)}) custom-call(bf16[64,2304]{1,0:T(8,128)(2,1)S(1)} %shard_map.41.refs_0_.refs_1_, bf16[64,1536]{1,0:T(8,128)(2,1)S(1)} %collective-permute-done.refs_1_, bf16[64,1536]{1,0:T(8,128)(2,1)S(1)} %collective-permute-done.6.refs_2_, ...), custom_call_target="tpu_custom_call" | custom-call | flops 301989888 | bytes 3637248 | tf_op jit(solution)/shard_map/pallas_call | solution.py:194
  32.5 0.9 %shard_map.47 = (f32[256,512]{1,0:T(8,128)S(1)}, f32[256,512]{1,0:T(8,128)S(1)}, f32[3,4,64]{2,1,0:T(4,128)S(1)}, f32[3,8,64]{2,1,0:T(8,128)S(1)}) custom-call(f32[256,512]{1,0:T(8,128)S(1)} %get-tuple-element.27.early_s, f32[128,512]{1,0:T(8,128)S(1)} %get-tuple-element.28.early_t, bf16[64,3072]{1,0:T(8,128)(2,1)S(1)} %collective-permute-done.13.refs_0_, ...), custom_call_target="tpu_custom_call" | custom-call | flops 301989888 | bytes 4006912 | tf_op jit(solution)/shard_map/pallas_call | solution.py:194
  33.5 1.2 %collective-permute-done.14 = f32[3,12,64]{2,1,0:T(8,128)S(1)} collective-permute-done((f32[3,12,64]{2,1,0:T(8,128)S(1)}, f32[3,12,64]{2,1,0:T(8,128)S(1)}, u32[]{:S(2)}, u32[]{:S(2)}) %collective-permute-start.14) | collective-permute-done | bytes 9248 | tf_op jit(solution)/shard_map/ppermute | solution.py:50
  34.8 3.7 %collective-permute-done.15 = f32[3,8,64]{2,1,0:T(8,128)S(1)} collective-permute-done((f32[3,8,64]{2,1,0:T(8,128)S(1)}, f32[3,8,64]{2,1,0:T(8,128)S(1)}, u32[]{:S(2)}, u32[]{:S(2)}) %collective-permute-start.15) | collective-permute-done | bytes 6176 | tf_op jit(solution)/shard_map/ppermute | solution.py:267
  38.5 0.6 %collective-permute-start.16 = (f32[3,8,64]{2,1,0:T(8,128)S(1)}, f32[3,8,64]{2,1,0:T(8,128)S(1)}, u32[]{:S(2)}, u32[]{:S(2)}) collective-permute-start(f32[3,8,64]{2,1,0:T(8,128)S(1)} %add.10), channel_id=1, source_target_pairs={{0,8},{1,9},{2,10},{3,11},{4,20},{5,21},{6,22},{7,23},{8,0},{9,1},... | collective-permute-start | bytes 18440 | tf_op jit(solution)/shard_map/ppermute | solution.py:267
  39.1 3.2 %collective-permute-done.16 = f32[3,8,64]{2,1,0:T(8,128)S(1)} collective-permute-done((f32[3,8,64]{2,1,0:T(8,128)S(1)}, f32[3,8,64]{2,1,0:T(8,128)S(1)}, u32[]{:S(2)}, u32[]{:S(2)}) %collective-permute-start.16) | collective-permute-done | bytes 6176 | tf_op jit(solution)/shard_map/ppermute | solution.py:267
  42.4 1.2 %collective-permute-done.17 = f32[3,8,64]{2,1,0:T(8,128)S(1)} collective-permute-done((f32[3,8,64]{2,1,0:T(8,128)S(1)}, f32[3,8,64]{2,1,0:T(8,128)S(1)}, u32[]{:S(2)}, u32[]{:S(2)}) %collective-permute-start.17) | collective-permute-done | bytes 6176 | tf_op jit(solution)/shard_map/ppermute | solution.py:50
  43.5 0.1 reshape.27.col_sum
  43.6 0.1 reshape.26.row_sum
  43.7 0.9 %shard_map.48 = (f32[64,768]{1,0:T(8,128)S(1)}, f32[8,128]{1,0:T(8,128)S(1)}, f32[400,128]{1,0:T(8,128)S(1)}, f32[400,128]{1,0:T(8,128)S(1)}, f32[400,128]{1,0:T(8,128)S(1)}) custom-call(f32[256,512]{1,0:T(8,128)S(1)} %get-tuple-element.29.gram_s, f32[256,512]{1,0:T(8,128)S(1)} %get-tuple-element.30.gram_t, f32[3,1,256]{2,1,0:T(1,128)S(1)} %reshape.26.row_sum, ...), custom_call_target="tpu_custom_call" | custom-call | flops 402653184 | bytes 3249152 | tf_op jit(solution)/shard_map/pallas_call | solution.py:194
  44.7 1.2 %collective-permute-start.19 = (f16[400,128]{1,0:T(8,128)(2,1)S(1)}, f16[400,128]{1,0:T(8,128)(2,1)S(1)}, u32[]{:S(2)}, u32[]{:S(2)}) collective-permute-start(f16[400,128]{1,0:T(8,128)(2,1)S(1)} %convert_element_type.20), channel_id=1, source_target_pairs={{0,8},{1,9},{2,10},{3,11},{4,12},{5,13},{6,14},{7,15},{8,0},{9,1},... | collective-permute-start | bytes 307208 | tf_op jit(solution)/shard_map/ppermute | solution.py:50
  46.0 2.4 %collective-permute-start.20 = (f16[400,128]{1,0:T(8,128)(2,1)S(1)}, f16[400,128]{1,0:T(8,128)(2,1)S(1)}, u32[]{:S(2)}, u32[]{:S(2)}) collective-permute-start(f16[400,128]{1,0:T(8,128)(2,1)S(1)} %convert_element_type.22), channel_id=1, source_target_pairs={{0,9},{1,8},{2,11},{3,10},{4,13},{5,12},{6,15},{7,14},{8,1},{9,0},... | collective-permute-start | bytes 307208 | tf_op jit(solution)/shard_map/ppermute | solution.py:50
  48.4 2.1 %collective-permute-done.18 = f16[400,128]{1,0:T(8,128)(2,1)S(1)} collective-permute-done((f16[400,128]{1,0:T(8,128)(2,1)S(1)}, f16[400,128]{1,0:T(8,128)(2,1)S(1)}, u32[]{:S(2)}, u32[]{:S(2)}) %collective-permute-start.18) | collective-permute-done | bytes 102432 | tf_op jit(solution)/shard_map/ppermute | solution.py:50
  50.4 1.5 %collective-permute-done.19 = f16[400,128]{1,0:T(8,128)(2,1)S(1)} collective-permute-done((f16[400,128]{1,0:T(8,128)(2,1)S(1)}, f16[400,128]{1,0:T(8,128)(2,1)S(1)}, u32[]{:S(2)}, u32[]{:S(2)}) %collective-permute-start.19) | collective-permute-done | bytes 102432 | tf_op jit(solution)/shard_map/ppermute | solution.py:50
  52.0 0.8 %shard_map.49 = (f32[64,768]{1,0:T(8,128)}, f32[1,1]{1,0:T(1,128)}) custom-call(f32[64,768]{1,0:T(8,128)S(1)} %get-tuple-element.33.own, f32[8,128]{1,0:T(8,128)S(1)} %get-tuple-element.34.share, f32[400,128]{1,0:T(8,128)S(1)} %convert_element_type.19.refs_0_, f32[400,128]{1,0:T(8,128)S(1)} %convert_element_type.21.refs_1_, ...), custom_call_target="tpu_custom_call" | custom-call | bytes 1011716 | tf_op jit(solution)/shard_map/pallas_call | solution.py:194
  (42 shorter events, 0.7 us)
Async XLA Ops:
  0.6 15.7 %copy-start = (bf16[64,1536]{1,0:T(8,128)(2,1)S(1)}, bf16[64,1536]{1,0:T(8,128)(2,1)}, u32[]{:S(2)}) copy-start(bf16[64,1536]{1,0:T(8,128)(2,1)} %refs_0_.1) | copy-start | bytes 589828
  0.6 15.7 %copy-start.1 = (bf16[64,768]{1,0:T(8,128)(2,1)S(1)}, bf16[64,768]{1,0:T(8,128)(2,1)}, u32[]{:S(2)}) copy-start(bf16[64,768]{1,0:T(8,128)(2,1)} %refs_1_.1) | copy-start | bytes 294916
  0.6 6.2 %collective-permute-start.2 = (bf16[64,1536]{1,0:T(8,128)(2,1)}, bf16[64,1536]{1,0:T(8,128)(2,1)S(1)}, u32[]{:S(2)}, u32[]{:S(2)}) collective-permute-start(bf16[64,1536]{1,0:T(8,128)(2,1)} %refs_0_.1), channel_id=1, source_target_pairs={{0,4},{1,5},{2,6},{3,7},{4,0},{5,1},{6,2},{7,3},{8,12},{9,13},{10,... | collective-permute-start | bytes 589832 | tf_op jit(solution)/shard_map/ppermute | solution.py:50
  1.2 5.7 %collective-permute-start.3 = (bf16[64,768]{1,0:T(8,128)(2,1)}, bf16[64,768]{1,0:T(8,128)(2,1)S(1)}, u32[]{:S(2)}, u32[]{:S(2)}) collective-permute-start(bf16[64,768]{1,0:T(8,128)(2,1)} %refs_1_.1), channel_id=1, source_target_pairs={{0,4},{1,5},{2,6},{3,7},{4,0},{5,1},{6,2},{7,3},{8,12},{9,13},{10,... | collective-permute-start | bytes 294920 | tf_op jit(solution)/shard_map/ppermute | solution.py:50
  1.2 12.4 %collective-permute-start = (bf16[64,1536]{1,0:T(8,128)(2,1)}, bf16[64,1536]{1,0:T(8,128)(2,1)S(1)}, u32[]{:S(2)}, u32[]{:S(2)}) collective-permute-start(bf16[64,1536]{1,0:T(8,128)(2,1)} %refs_0_.1), channel_id=1, source_target_pairs={{0,1},{1,0},{2,3},{3,2},{4,5},{5,4},{6,7},{7,6},{8,9},{9,8},{10,11... | collective-permute-start | bytes 589832 | tf_op jit(solution)/shard_map/ppermute | solution.py:50
  4.2 12.0 %collective-permute-start.1 = (bf16[64,1536]{1,0:T(8,128)(2,1)}, bf16[64,1536]{1,0:T(8,128)(2,1)S(1)}, u32[]{:S(2)}, u32[]{:S(2)}) collective-permute-start(bf16[64,1536]{1,0:T(8,128)(2,1)} %refs_0_.1), channel_id=1, source_target_pairs={{0,2},{1,3},{2,0},{3,1},{4,6},{5,7},{6,4},{7,5},{8,10},{9,11},{10,... | collective-permute-start | bytes 589832 | tf_op jit(solution)/shard_map/ppermute | solution.py:50
  6.8 9.4 %collective-permute-start.4 = (bf16[64,1536]{1,0:T(8,128)(2,1)}, bf16[64,1536]{1,0:T(8,128)(2,1)S(1)}, u32[]{:S(2)}, u32[]{:S(2)}) collective-permute-start(bf16[64,1536]{1,0:T(8,128)(2,1)} %refs_0_.1), channel_id=1, source_target_pairs={{0,16},{1,17},{2,18},{3,19},{4,20},{5,21},{6,22},{7,23},{8,24},{9,... | collective-permute-start | bytes 589832 | tf_op jit(solution)/shard_map/ppermute | solution.py:50
  8.4 7.9 %collective-permute-start.8 = (bf16[64,768]{1,0:T(8,128)(2,1)}, bf16[64,768]{1,0:T(8,128)(2,1)S(1)}, u32[]{:S(2)}, u32[]{:S(2)}) collective-permute-start(bf16[64,768]{1,0:T(8,128)(2,1)} %refs_1_.1), channel_id=1, source_target_pairs={{0,16},{1,17},{2,18},{3,19},{4,20},{5,21},{6,22},{7,23},{8,24},{9,... | collective-permute-start | bytes 294920 | tf_op jit(solution)/shard_map/ppermute | solution.py:50
  8.9 7.6 %collective-permute-start.5 = (bf16[64,768]{1,0:T(8,128)(2,1)}, bf16[64,768]{1,0:T(8,128)(2,1)S(1)}, u32[]{:S(2)}, u32[]{:S(2)}) collective-permute-start(bf16[64,768]{1,0:T(8,128)(2,1)} %refs_1_.1), channel_id=1, source_target_pairs={{0,8},{1,9},{2,10},{3,11},{4,12},{5,13},{6,14},{7,15},{8,0},{9,1},... | collective-permute-start | bytes 294920 | tf_op jit(solution)/shard_map/ppermute | solution.py:50
  16.3 15.3 %collective-permute-start.9 = (bf16[64,3840]{1,0:T(8,128)(2,1)S(1)}, bf16[64,3840]{1,0:T(8,128)(2,1)S(1)}, u32[]{:S(2)}, u32[]{:S(2)}) collective-permute-start(bf16[64,3840]{1,0:T(8,128)(2,1)S(1)} %shard_map.43), channel_id=1, source_target_pairs={{0,4},{1,5},{2,6},{3,7},{4,0},{5,1},{6,2},{7,3},{8,12},{9,13},{10,... | collective-permute-start | bytes 1474568 | tf_op jit(solution)/shard_map/ppermute | solution.py:50
  16.5 12.4 %collective-permute-start.11 = (bf16[64,1536]{1,0:T(8,128)(2,1)S(1)}, bf16[64,1536]{1,0:T(8,128)(2,1)S(1)}, u32[]{:S(2)}, u32[]{:S(2)}) collective-permute-start(bf16[64,1536]{1,0:T(8,128)(2,1)S(1)} %shard_map.44), channel_id=1, source_target_pairs={{0,2},{1,3},{2,0},{3,1},{4,6},{5,7},{6,4},{7,5},{8,10},{9,11},{10,... | collective-permute-start | bytes 589832 | tf_op jit(solution)/shard_map/ppermute | solution.py:50
  16.8 12.1 %collective-permute-start.7 = (bf16[64,1536]{1,0:T(8,128)(2,1)S(1)}, bf16[64,1536]{1,0:T(8,128)(2,1)S(1)}, u32[]{:S(2)}, u32[]{:S(2)}) collective-permute-start(bf16[64,1536]{1,0:T(8,128)(2,1)S(1)} %collective-permute-done.1.refs_0_.refs_4_.refs_2_), channel_id=1, source_target_pairs={{0,16},{1,17},{2,18},{3,19},{4,20},{5,21},{6,22},{7,23},{8,24},{9,... | collective-permute-start | bytes 589832 | tf_op jit(solution)/shard_map/ppermute | solution.py:50
  18.4 14.0 %collective-permute-start.13 = (bf16[64,3072]{1,0:T(8,128)(2,1)S(1)}, bf16[64,3072]{1,0:T(8,128)(2,1)S(1)}, u32[]{:S(2)}, u32[]{:S(2)}) collective-permute-start(bf16[64,3072]{1,0:T(8,128)(2,1)S(1)} %shard_map.46), channel_id=1, source_target_pairs={{0,8},{1,9},{2,10},{3,11},{4,12},{5,13},{6,14},{7,15},{8,0},{9,1},... | collective-permute-start | bytes 1179656 | tf_op jit(solution)/shard_map/ppermute | solution.py:50
  20.0 11.6 %collective-permute-start.6 = (bf16[64,1536]{1,0:T(8,128)(2,1)S(1)}, bf16[64,1536]{1,0:T(8,128)(2,1)S(1)}, u32[]{:S(2)}, u32[]{:S(2)}) collective-permute-start(bf16[64,1536]{1,0:T(8,128)(2,1)S(1)} %shard_map.42), channel_id=1, source_target_pairs={{0,1},{1,0},{2,3},{3,2},{4,5},{5,4},{6,7},{7,6},{8,9},{9,8},{10,11... | collective-permute-start | bytes 589832 | tf_op jit(solution)/shard_map/ppermute | solution.py:50
  28.9 2.7 %collective-permute-start.12 = (bf16[64,1536]{1,0:T(8,128)(2,1)S(1)}, bf16[64,1536]{1,0:T(8,128)(2,1)S(1)}, u32[]{:S(2)}, u32[]{:S(2)}) collective-permute-start(bf16[64,1536]{1,0:T(8,128)(2,1)S(1)} %collective-permute-done.11.refs_10_.refs_1_), channel_id=1, source_target_pairs={{0,4},{1,5},{2,6},{3,7},{4,0},{5,1},{6,2},{7,3},{8,12},{9,13},{10,... | collective-permute-start | bytes 589832 | tf_op jit(solution)/shard_map/ppermute | solution.py:50
  28.9 2.7 %collective-permute-start.10 = (bf16[64,1536]{1,0:T(8,128)(2,1)S(1)}, bf16[64,1536]{1,0:T(8,128)(2,1)S(1)}, u32[]{:S(2)}, u32[]{:S(2)}) collective-permute-start(bf16[64,1536]{1,0:T(8,128)(2,1)S(1)} %collective-permute-done.7.refs_6_.refs_4_), channel_id=1, source_target_pairs={{0,4},{1,5},{2,6},{3,7},{4,0},{5,1},{6,2},{7,3},{8,12},{9,13},{10,... | collective-permute-start | bytes 589832 | tf_op jit(solution)/shard_map/ppermute | solution.py:50
  33.4 1.3 %collective-permute-start.14 = (f32[3,12,64]{2,1,0:T(8,128)S(1)}, f32[3,12,64]{2,1,0:T(8,128)S(1)}, u32[]{:S(2)}, u32[]{:S(2)}) collective-permute-start(f32[3,12,64]{2,1,0:T(8,128)S(1)} %pad_maximum_fusion), channel_id=1, source_target_pairs={{0,4},{1,5},{2,6},{3,7},{4,0},{5,1},{6,2},{7,3},{8,12},{9,13},{10,... | collective-permute-start | bytes 27656 | tf_op jit(solution)/shard_map/ppermute | solution.py:50
  34.7 3.8 %collective-permute-start.15 = (f32[3,8,64]{2,1,0:T(8,128)S(1)}, f32[3,8,64]{2,1,0:T(8,128)S(1)}, u32[]{:S(2)}, u32[]{:S(2)}) collective-permute-start(f32[3,8,64]{2,1,0:T(8,128)S(1)} %maximum_select_fusion), channel_id=1, source_target_pairs={{0,1},{1,0},{2,3},{3,2},{4,6},{5,7},{6,4},{7,5},{8,9},{9,8},{10,11... | collective-permute-start | bytes 18440 | tf_op jit(solution)/shard_map/ppermute | solution.py:267
  38.5 3.8 %collective-permute-start.16 = (f32[3,8,64]{2,1,0:T(8,128)S(1)}, f32[3,8,64]{2,1,0:T(8,128)S(1)}, u32[]{:S(2)}, u32[]{:S(2)}) collective-permute-start(f32[3,8,64]{2,1,0:T(8,128)S(1)} %add.10), channel_id=1, source_target_pairs={{0,8},{1,9},{2,10},{3,11},{4,20},{5,21},{6,22},{7,23},{8,0},{9,1},... | collective-permute-start | bytes 18440 | tf_op jit(solution)/shard_map/ppermute | solution.py:267
  42.3 1.2 %collective-permute-start.17 = (f32[3,8,64]{2,1,0:T(8,128)S(1)}, f32[3,8,64]{2,1,0:T(8,128)S(1)}, u32[]{:S(2)}, u32[]{:S(2)}) collective-permute-start(f32[3,8,64]{2,1,0:T(8,128)S(1)} %add.11), channel_id=1, source_target_pairs={{0,4},{1,5},{2,6},{3,7},{4,0},{5,1},{6,2},{7,3},{8,12},{9,13},{10,... | collective-permute-start | bytes 18440 | tf_op jit(solution)/shard_map/ppermute | solution.py:50
  44.6 5.8 %collective-permute-start.18 = (f16[400,128]{1,0:T(8,128)(2,1)S(1)}, f16[400,128]{1,0:T(8,128)(2,1)S(1)}, u32[]{:S(2)}, u32[]{:S(2)}) collective-permute-start(f16[400,128]{1,0:T(8,128)(2,1)S(1)} %convert_element_type.18), channel_id=1, source_target_pairs={{0,1},{1,0},{2,3},{3,2},{4,5},{5,4},{6,7},{7,6},{8,9},{9,8},{10,11... | collective-permute-start | bytes 307208 | tf_op jit(solution)/shard_map/ppermute | solution.py:50
  44.7 7.2 %collective-permute-start.19 = (f16[400,128]{1,0:T(8,128)(2,1)S(1)}, f16[400,128]{1,0:T(8,128)(2,1)S(1)}, u32[]{:S(2)}, u32[]{:S(2)}) collective-permute-start(f16[400,128]{1,0:T(8,128)(2,1)S(1)} %convert_element_type.20), channel_id=1, source_target_pairs={{0,8},{1,9},{2,10},{3,11},{4,12},{5,13},{6,14},{7,15},{8,0},{9,1},... | collective-permute-start | bytes 307208 | tf_op jit(solution)/shard_map/ppermute | solution.py:50
  46.0 6.0 %collective-permute-start.20 = (f16[400,128]{1,0:T(8,128)(2,1)S(1)}, f16[400,128]{1,0:T(8,128)(2,1)S(1)}, u32[]{:S(2)}, u32[]{:S(2)}) collective-permute-start(f16[400,128]{1,0:T(8,128)(2,1)S(1)} %convert_element_type.22), channel_id=1, source_target_pairs={{0,9},{1,8},{2,11},{3,10},{4,13},{5,12},{6,15},{7,14},{8,1},{9,0},... | collective-permute-start | bytes 307208 | tf_op jit(solution)/shard_map/ppermute | solution.py:50

commit v24 on v19

--- a/solution.py
+++ b/solution.py
@@ -114,12 +114,11 @@
     rest = [p for p in range(1 << len(plane_masks)) if p.bit_count() > 1]
     swaps = [
         [(col_t, core_t, p) for p in ones] + [(col_s, core_s, p) for p in col_s if p and not p & 1],
-        [(col_t, core_t, p) for p in rest],
-        [(col_s, core_s, p) for p in col_s if p & 1],
+        [(col_t, core_t, p) for p in rest] + [(col_s, core_s, p) for p in col_s if p & 1],
     ]
     for swap in swaps:
         arrays = list({id(side[p][0]): side[p][0] for side, _, p in swap}.values())
-        got = send(join(*arrays) if len(arrays) > 1 else arrays[0], core_mask, count)
+        got = send(after(join(*arrays), row_s[1][0]) if swap is swaps[1] else join(*arrays), core_mask, count)
         starts = {id(array): sum(a.shape[1] for a in arrays[:k]) for k, array in enumerate(arrays)}
         for side, core, p in swap:
             array, start, stop = side[p]

time: 52.7 us -> 52.4 us (level)
  local copies, waits for them, and re-layouts: 0.24 us -> 2.05 us
  waiting for transfers between devices: 26.9 us -> 25.5 us
  starting transfers between devices: 21.5 us -> 20.8 us
    unnamed x4, local copies, waits for them, and re-layouts: 0.01 us -> 1.82 us
    ppermute x19 -> x18, starting transfers between devices: 20.3 us -> 18.6 us  [send(): return lax.ppermute(value, AXES, [(i, i ^ mask) for i in range(count)])]
    ppermute x2, starting transfers between devices: 1.2 us -> 2.21 us  [exchange_sums(): got = lax.ppermute(sums, AXES, pairs).reshape(3, -1, 2, 1 << b, rows)]
    ppermute x2, waiting for transfers between devices: 6.32 us -> 5.32 us  [exchange_sums(): got = lax.ppermute(sums, AXES, pairs).reshape(3, -1, 2, 1 << b, rows)]
    ppermute x19 -> x18, waiting for transfers between devices: 20.6 us -> 20.2 us  [send(): return lax.ppermute(value, AXES, [(i, i ^ mask) for i in range(count)])]
    pallas_call x8 -> x9, Pallas kernels: 2.86 us -> 2.9 us  [call(): pl.pallas_call(kernel, out_shape=outputs, **options, compiler_params=pltp...]
  transfers between devices with their start and end apart: 21 -> 20, of which waited for: 11 -> 12; matrix products, arithmetic and copies ran while one was open for 0% -> 0% of each run, Pallas kernels for 0% -> 0%
where the time goes in v24:
time: 52.4 us; the launch traced here: 52.2 us
  waiting for transfers between devices  25.5 us (49%)
  starting transfers between devices  20.8 us (40%)
  Pallas kernels  2.9 us (6%)
  local copies, waits for them, and re-layouts  2.05 us (4%)
  between operations  0.79 us (2%)
    ppermute x18, waiting for transfers between devices, send(): return lax.ppermute(value, AXES, [(i, i ^ mask) for i in range(count)])  20.2 us
    ppermute x18, starting transfers between devices, send(): return lax.ppermute(value, AXES, [(i, i ^ mask) for i in range(count)])  18.6 us
    ppermute x2, waiting for transfers between devices, exchange_sums(): got = lax.ppermute(sums, AXES, pairs).reshape(3, -1, 2, 1 << b, rows)  5.32 us
    pallas_call x9, Pallas kernels, call(): pl.pallas_call(kernel, out_shape=outputs, **options, compiler_params=pltp...  2.9 us
    ppermute x2, starting transfers between devices, exchange_sums(): got = lax.ppermute(sums, AXES, pairs).reshape(3, -1, 2, 1 << b, rows)  2.21 us
    unnamed x4, local copies, waits for them, and re-layouts  1.82 us
  transfers between devices with their start and end apart: 20, of which 12 were waited for; matrix products, arithmetic and copies ran while one was open for 0% of the time, Pallas kernels for 0%

profile of v24, /device:TPU:0, one launch (start us, length us, event | category | flops | bytes accessed | tf_op | source)
XLA Modules:
  0.0 52.2 jit_solution(5487002536724740974)
XLA Ops:
  0.6 0.5 collective-permute-start.2
  1.2 3.0 %collective-permute-start = (bf16[64,1536]{1,0:T(8,128)(2,1)}, bf16[64,1536]{1,0:T(8,128)(2,1)S(1)}, u32[]{:S(2)}, u32[]{:S(2)}) collective-permute-start(bf16[64,1536]{1,0:T(8,128)(2,1)} %refs_0_.1), channel_id=1, source_target_pairs={{0,1},{1,0},{2,3},{3,2},{4,5},{5,4},{6,7},{7,6},{8,9},{9,8},{10,11... | collective-permute-start | bytes 589832 | tf_op jit(solution)/shard_map/ppermute | solution.py:50
  4.2 2.6 %collective-permute-start.1 = (bf16[64,1536]{1,0:T(8,128)(2,1)}, bf16[64,1536]{1,0:T(8,128)(2,1)S(1)}, u32[]{:S(2)}, u32[]{:S(2)}) collective-permute-start(bf16[64,1536]{1,0:T(8,128)(2,1)} %refs_0_.1), channel_id=1, source_target_pairs={{0,2},{1,3},{2,0},{3,1},{4,6},{5,7},{6,4},{7,5},{8,10},{9,11},{10,... | collective-permute-start | bytes 589832 | tf_op jit(solution)/shard_map/ppermute | solution.py:50
  6.8 1.5 %collective-permute-start.4 = (bf16[64,1536]{1,0:T(8,128)(2,1)}, bf16[64,1536]{1,0:T(8,128)(2,1)S(1)}, u32[]{:S(2)}, u32[]{:S(2)}) collective-permute-start(bf16[64,1536]{1,0:T(8,128)(2,1)} %refs_0_.1), channel_id=1, source_target_pairs={{0,16},{1,17},{2,18},{3,19},{4,20},{5,21},{6,22},{7,23},{8,24},{9,... | collective-permute-start | bytes 589832 | tf_op jit(solution)/shard_map/ppermute | solution.py:50
  8.3 0.5 collective-permute-start.9
  8.9 1.5 %collective-permute-start.6 = (bf16[64,768]{1,0:T(8,128)(2,1)}, bf16[64,768]{1,0:T(8,128)(2,1)S(1)}, u32[]{:S(2)}, u32[]{:S(2)}) collective-permute-start(bf16[64,768]{1,0:T(8,128)(2,1)} %refs_1_.1), channel_id=1, source_target_pairs={{0,8},{1,9},{2,10},{3,11},{4,12},{5,13},{6,14},{7,15},{8,0},{9,1},... | collective-permute-start | bytes 294920 | tf_op jit(solution)/shard_map/ppermute | solution.py:50
  10.3 0.9 %copy-done = bf16[64,1536]{1,0:T(8,128)(2,1)S(1)} copy-done((bf16[64,1536]{1,0:T(8,128)(2,1)S(1)}, bf16[64,1536]{1,0:T(8,128)(2,1)}, u32[]{:S(2)}) %copy-start) | copy-done | bytes 196632
  11.3 0.9 %copy-done.1 = bf16[64,768]{1,0:T(8,128)(2,1)S(1)} copy-done((bf16[64,768]{1,0:T(8,128)(2,1)S(1)}, bf16[64,768]{1,0:T(8,128)(2,1)}, u32[]{:S(2)}) %copy-start.1) | copy-done | bytes 98328
  12.2 3.3 %collective-permute-done.9.refs_2_.refs_1_.refs_12_ = bf16[64,768]{1,0:T(8,128)(2,1)S(1)} collective-permute-done((bf16[64,768]{1,0:T(8,128)(2,1)}, bf16[64,768]{1,0:T(8,128)(2,1)S(1)}, u32[]{:S(2)}, u32[]{:S(2)}) %collective-permute-start.9) | collective-permute-done | bytes 98336 | tf_op jit(solution)/shard_map/ppermute | solution.py:50
  15.5 0.5 collective-permute-start.11
  16.0 0.2 collective-permute-done.1.refs_0_.refs_5_
  16.2 1.5 %collective-permute-start.8 = (bf16[64,1536]{1,0:T(8,128)(2,1)S(1)}, bf16[64,1536]{1,0:T(8,128)(2,1)S(1)}, u32[]{:S(2)}, u32[]{:S(2)}) collective-permute-start(bf16[64,1536]{1,0:T(8,128)(2,1)S(1)} %collective-permute-done.1.refs_0_.refs_5_), channel_id=1, source_target_pairs={{0,16},{1,17},{2,18},{3,19},{4,20},{5,21},{6,22},{7,23},{8,24},{9,... | collective-permute-start | bytes 589832 | tf_op jit(solution)/shard_map/ppermute | solution.py:50
  17.7 1.4 %collective-permute-start.7 = (bf16[64,1536]{1,0:T(8,128)(2,1)S(1)}, bf16[64,1536]{1,0:T(8,128)(2,1)S(1)}, u32[]{:S(2)}, u32[]{:S(2)}) collective-permute-start(bf16[64,1536]{1,0:T(8,128)(2,1)S(1)} %shard_map.43), channel_id=1, source_target_pairs={{0,1},{1,0},{2,3},{3,2},{4,5},{5,4},{6,7},{7,6},{8,9},{9,8},{10,11... | collective-permute-start | bytes 589832 | tf_op jit(solution)/shard_map/ppermute | solution.py:50
  19.4 1.6 %collective-permute-start.5 = (bf16[64,3072]{1,0:T(8,128)(2,1)S(1)}, bf16[64,3072]{1,0:T(8,128)(2,1)S(1)}, u32[]{:S(2)}, u32[]{:S(2)}) collective-permute-start(bf16[64,3072]{1,0:T(8,128)(2,1)S(1)} %shard_map.42), channel_id=1, source_target_pairs={{0,8},{1,9},{2,10},{3,11},{4,12},{5,13},{6,14},{7,15},{8,0},{9,1},... | collective-permute-start | bytes 1179656 | tf_op jit(solution)/shard_map/ppermute | solution.py:50
  20.9 5.1 %collective-permute-done.11.refs_1_.refs_11_ = bf16[64,1536]{1,0:T(8,128)(2,1)S(1)} collective-permute-done((bf16[64,1536]{1,0:T(8,128)(2,1)S(1)}, bf16[64,1536]{1,0:T(8,128)(2,1)S(1)}, u32[]{:S(2)}, u32[]{:S(2)}) %collective-permute-start.11) | collective-permute-done | bytes 196640 | tf_op jit(solution)/shard_map/ppermute | solution.py:50
  26.1 1.2 %collective-permute-done.7.refs_3_ = bf16[64,1536]{1,0:T(8,128)(2,1)S(1)} collective-permute-done((bf16[64,1536]{1,0:T(8,128)(2,1)S(1)}, bf16[64,1536]{1,0:T(8,128)(2,1)S(1)}, u32[]{:S(2)}, u32[]{:S(2)}) %collective-permute-start.7) | collective-permute-done | bytes 196640 | tf_op jit(solution)/shard_map/ppermute | solution.py:50
  27.2 3.7 %collective-permute-done.5.refs_2_ = bf16[64,3072]{1,0:T(8,128)(2,1)S(1)} collective-permute-done((bf16[64,3072]{1,0:T(8,128)(2,1)S(1)}, bf16[64,3072]{1,0:T(8,128)(2,1)S(1)}, u32[]{:S(2)}, u32[]{:S(2)}) %collective-permute-start.5) | collective-permute-done | bytes 393248 | tf_op jit(solution)/shard_map/ppermute | solution.py:50
  30.9 1.0 %shard_map.47 = (f32[256,512]{1,0:T(8,128)S(1)}, f32[256,512]{1,0:T(8,128)S(1)}, f32[3,4,64]{2,1,0:T(4,128)S(1)}, f32[3,8,64]{2,1,0:T(8,128)S(1)}) custom-call(bf16[64,2304]{1,0:T(8,128)(2,1)S(1)} %shard_map.41.refs_0_, bf16[64,1536]{1,0:T(8,128)(2,1)S(1)} %collective-permute-done.refs_1_, bf16[64,3072]{1,0:T(8,128)(2,1)S(1)} %collective-permute-done.5.refs_2_, ...), custom_call_target="tpu_custom_call" | custom-call | flops 603979776 | bytes 4301824 | tf_op jit(solution)/shard_map/pallas_call | solution.py:185
  32.1 1.2 %collective-permute-done.13 = f32[3,12,64]{2,1,0:T(8,128)S(1)} collective-permute-done((f32[3,12,64]{2,1,0:T(8,128)S(1)}, f32[3,12,64]{2,1,0:T(8,128)S(1)}, u32[]{:S(2)}, u32[]{:S(2)}) %collective-permute-start.13) | collective-permute-done | bytes 9248 | tf_op jit(solution)/shard_map/ppermute | solution.py:50
  33.3 0.6 %collective-permute-start.14 = (f32[3,8,64]{2,1,0:T(8,128)S(1)}, f32[3,8,64]{2,1,0:T(8,128)S(1)}, u32[]{:S(2)}, u32[]{:S(2)}) collective-permute-start(f32[3,8,64]{2,1,0:T(8,128)S(1)} %maximum_select_fusion), channel_id=1, source_target_pairs={{0,1},{1,0},{2,3},{3,2},{4,6},{5,7},{6,4},{7,5},{8,9},{9,8},{10,11... | collective-permute-start | bytes 18440 | tf_op jit(solution)/shard_map/ppermute | solution.py:258
  33.9 3.1 %collective-permute-done.14 = f32[3,8,64]{2,1,0:T(8,128)S(1)} collective-permute-done((f32[3,8,64]{2,1,0:T(8,128)S(1)}, f32[3,8,64]{2,1,0:T(8,128)S(1)}, u32[]{:S(2)}, u32[]{:S(2)}) %collective-permute-start.14) | collective-permute-done | bytes 6176 | tf_op jit(solution)/shard_map/ppermute | solution.py:258
  37.1 1.6 %collective-permute-start.15 = (f32[3,8,64]{2,1,0:T(8,128)S(1)}, f32[3,8,64]{2,1,0:T(8,128)S(1)}, u32[]{:S(2)}, u32[]{:S(2)}) collective-permute-start(f32[3,8,64]{2,1,0:T(8,128)S(1)} %add.10), channel_id=1, source_target_pairs={{0,8},{1,9},{2,10},{3,11},{4,20},{5,21},{6,22},{7,23},{8,0},{9,1},... | collective-permute-start | bytes 18440 | tf_op jit(solution)/shard_map/ppermute | solution.py:258
  38.7 2.2 %collective-permute-done.15 = f32[3,8,64]{2,1,0:T(8,128)S(1)} collective-permute-done((f32[3,8,64]{2,1,0:T(8,128)S(1)}, f32[3,8,64]{2,1,0:T(8,128)S(1)}, u32[]{:S(2)}, u32[]{:S(2)}) %collective-permute-start.15) | collective-permute-done | bytes 6176 | tf_op jit(solution)/shard_map/ppermute | solution.py:258
  41.0 1.2 %collective-permute-done.16 = f32[3,8,64]{2,1,0:T(8,128)S(1)} collective-permute-done((f32[3,8,64]{2,1,0:T(8,128)S(1)}, f32[3,8,64]{2,1,0:T(8,128)S(1)}, u32[]{:S(2)}, u32[]{:S(2)}) %collective-permute-start.16) | collective-permute-done | bytes 6176 | tf_op jit(solution)/shard_map/ppermute | solution.py:50
  42.3 0.9 %shard_map.48 = (f32[64,768]{1,0:T(8,128)S(1)}, f32[8,128]{1,0:T(8,128)S(1)}, f32[400,128]{1,0:T(8,128)S(1)}, f32[400,128]{1,0:T(8,128)S(1)}, f32[400,128]{1,0:T(8,128)S(1)}) custom-call(f32[256,512]{1,0:T(8,128)S(1)} %get-tuple-element.27.gram_s, f32[256,512]{1,0:T(8,128)S(1)} %get-tuple-element.28.gram_t, f32[3,1,256]{2,1,0:T(1,128)S(1)} %reshape.26.row_sum, ...), custom_call_target="tpu_custom_call" | custom-call | flops 402653184 | bytes 3445760 | tf_op jit(solution)/shard_map/pallas_call | solution.py:185
  43.3 0.6 %collective-permute-start.17 = (f16[400,128]{1,0:T(8,128)(2,1)S(1)}, f16[400,128]{1,0:T(8,128)(2,1)S(1)}, u32[]{:S(2)}, u32[]{:S(2)}) collective-permute-start(f16[400,128]{1,0:T(8,128)(2,1)S(1)} %convert_element_type.18), channel_id=1, source_target_pairs={{0,1},{1,0},{2,3},{3,2},{4,5},{5,4},{6,7},{7,6},{8,9},{9,8},{10,11... | collective-permute-start | bytes 307208 | tf_op jit(solution)/shard_map/ppermute | solution.py:50
  43.9 1.6 %collective-permute-start.18 = (f16[400,128]{1,0:T(8,128)(2,1)S(1)}, f16[400,128]{1,0:T(8,128)(2,1)S(1)}, u32[]{:S(2)}, u32[]{:S(2)}) collective-permute-start(f16[400,128]{1,0:T(8,128)(2,1)S(1)} %convert_element_type.20), channel_id=1, source_target_pairs={{0,8},{1,9},{2,10},{3,11},{4,12},{5,13},{6,14},{7,15},{8,0},{9,1},... | collective-permute-start | bytes 307208 | tf_op jit(solution)/shard_map/ppermute | solution.py:50
  45.5 1.5 %collective-permute-start.19 = (f16[400,128]{1,0:T(8,128)(2,1)S(1)}, f16[400,128]{1,0:T(8,128)(2,1)S(1)}, u32[]{:S(2)}, u32[]{:S(2)}) collective-permute-start(f16[400,128]{1,0:T(8,128)(2,1)S(1)} %convert_element_type.22), channel_id=1, source_target_pairs={{0,9},{1,8},{2,11},{3,10},{4,13},{5,12},{6,15},{7,14},{8,1},{9,0},... | collective-permute-start | bytes 307208 | tf_op jit(solution)/shard_map/ppermute | solution.py:50
  47.0 1.9 %collective-permute-done.17 = f16[400,128]{1,0:T(8,128)(2,1)S(1)} collective-permute-done((f16[400,128]{1,0:T(8,128)(2,1)S(1)}, f16[400,128]{1,0:T(8,128)(2,1)S(1)}, u32[]{:S(2)}, u32[]{:S(2)}) %collective-permute-start.17) | collective-permute-done | bytes 102432 | tf_op jit(solution)/shard_map/ppermute | solution.py:50
  48.9 1.0 %collective-permute-done.18 = f16[400,128]{1,0:T(8,128)(2,1)S(1)} collective-permute-done((f16[400,128]{1,0:T(8,128)(2,1)S(1)}, f16[400,128]{1,0:T(8,128)(2,1)S(1)}, u32[]{:S(2)}, u32[]{:S(2)}) %collective-permute-start.18) | collective-permute-done | bytes 102432 | tf_op jit(solution)/shard_map/ppermute | solution.py:50
  49.9 1.5 %collective-permute-done.19 = f16[400,128]{1,0:T(8,128)(2,1)S(1)} collective-permute-done((f16[400,128]{1,0:T(8,128)(2,1)S(1)}, f16[400,128]{1,0:T(8,128)(2,1)S(1)}, u32[]{:S(2)}, u32[]{:S(2)}) %collective-permute-start.19) | collective-permute-done | bytes 102432 | tf_op jit(solution)/shard_map/ppermute | solution.py:50
  51.4 0.8 %shard_map.49 = (f32[64,768]{1,0:T(8,128)}, f32[1,1]{1,0:T(1,128)}) custom-call(f32[64,768]{1,0:T(8,128)S(1)} %get-tuple-element.31.own, f32[8,128]{1,0:T(8,128)S(1)} %get-tuple-element.32.share, f32[400,128]{1,0:T(8,128)S(1)} %convert_element_type.19.refs_0_, f32[400,128]{1,0:T(8,128)S(1)} %convert_element_type.21.refs_1_, ...), custom_call_target="tpu_custom_call" | custom-call | bytes 1011716 | tf_op jit(solution)/shard_map/pallas_call | solution.py:185
  (40 shorter events, 0.8 us)
Async XLA Ops:
  0.6 6.2 %collective-permute-start.2 = (bf16[64,1536]{1,0:T(8,128)(2,1)}, bf16[64,1536]{1,0:T(8,128)(2,1)S(1)}, u32[]{:S(2)}, u32[]{:S(2)}) collective-permute-start(bf16[64,1536]{1,0:T(8,128)(2,1)} %refs_0_.1), channel_id=1, source_target_pairs={{0,4},{1,5},{2,6},{3,7},{4,0},{5,1},{6,2},{7,3},{8,12},{9,13},{10,... | collective-permute-start | bytes 589832 | tf_op jit(solution)/shard_map/ppermute | solution.py:50
  1.1 5.7 %collective-permute-start.3 = (bf16[64,768]{1,0:T(8,128)(2,1)}, bf16[64,768]{1,0:T(8,128)(2,1)S(1)}, u32[]{:S(2)}, u32[]{:S(2)}) collective-permute-start(bf16[64,768]{1,0:T(8,128)(2,1)} %refs_1_.1), channel_id=1, source_target_pairs={{0,4},{1,5},{2,6},{3,7},{4,0},{5,1},{6,2},{7,3},{8,12},{9,13},{10,... | collective-permute-start | bytes 294920 | tf_op jit(solution)/shard_map/ppermute | solution.py:50
  1.2 14.8 %collective-permute-start = (bf16[64,1536]{1,0:T(8,128)(2,1)}, bf16[64,1536]{1,0:T(8,128)(2,1)S(1)}, u32[]{:S(2)}, u32[]{:S(2)}) collective-permute-start(bf16[64,1536]{1,0:T(8,128)(2,1)} %refs_0_.1), channel_id=1, source_target_pairs={{0,1},{1,0},{2,3},{3,2},{4,5},{5,4},{6,7},{7,6},{8,9},{9,8},{10,11... | collective-permute-start | bytes 589832 | tf_op jit(solution)/shard_map/ppermute | solution.py:50
  4.2 12.0 %collective-permute-start.1 = (bf16[64,1536]{1,0:T(8,128)(2,1)}, bf16[64,1536]{1,0:T(8,128)(2,1)S(1)}, u32[]{:S(2)}, u32[]{:S(2)}) collective-permute-start(bf16[64,1536]{1,0:T(8,128)(2,1)} %refs_0_.1), channel_id=1, source_target_pairs={{0,2},{1,3},{2,0},{3,1},{4,6},{5,7},{6,4},{7,5},{8,10},{9,11},{10,... | collective-permute-start | bytes 589832 | tf_op jit(solution)/shard_map/ppermute | solution.py:50
  6.8 9.4 %collective-permute-start.4 = (bf16[64,1536]{1,0:T(8,128)(2,1)}, bf16[64,1536]{1,0:T(8,128)(2,1)S(1)}, u32[]{:S(2)}, u32[]{:S(2)}) collective-permute-start(bf16[64,1536]{1,0:T(8,128)(2,1)} %refs_0_.1), channel_id=1, source_target_pairs={{0,16},{1,17},{2,18},{3,19},{4,20},{5,21},{6,22},{7,23},{8,24},{9,... | collective-permute-start | bytes 589832 | tf_op jit(solution)/shard_map/ppermute | solution.py:50
  8.3 7.1 %collective-permute-start.9 = (bf16[64,768]{1,0:T(8,128)(2,1)}, bf16[64,768]{1,0:T(8,128)(2,1)S(1)}, u32[]{:S(2)}, u32[]{:S(2)}) collective-permute-start(bf16[64,768]{1,0:T(8,128)(2,1)} %refs_1_.1), channel_id=1, source_target_pairs={{0,16},{1,17},{2,18},{3,19},{4,20},{5,21},{6,22},{7,23},{8,24},{9,... | collective-permute-start | bytes 294920 | tf_op jit(solution)/shard_map/ppermute | solution.py:50
  8.9 6.6 %collective-permute-start.6 = (bf16[64,768]{1,0:T(8,128)(2,1)}, bf16[64,768]{1,0:T(8,128)(2,1)S(1)}, u32[]{:S(2)}, u32[]{:S(2)}) collective-permute-start(bf16[64,768]{1,0:T(8,128)(2,1)} %refs_1_.1), channel_id=1, source_target_pairs={{0,8},{1,9},{2,10},{3,11},{4,12},{5,13},{6,14},{7,15},{8,0},{9,1},... | collective-permute-start | bytes 294920 | tf_op jit(solution)/shard_map/ppermute | solution.py:50
  10.3 0.9 %copy-start = (bf16[64,1536]{1,0:T(8,128)(2,1)S(1)}, bf16[64,1536]{1,0:T(8,128)(2,1)}, u32[]{:S(2)}) copy-start(bf16[64,1536]{1,0:T(8,128)(2,1)} %refs_0_.1) | copy-start | bytes 589828
  11.3 0.9 %copy-start.1 = (bf16[64,768]{1,0:T(8,128)(2,1)S(1)}, bf16[64,768]{1,0:T(8,128)(2,1)}, u32[]{:S(2)}) copy-start(bf16[64,768]{1,0:T(8,128)(2,1)} %refs_1_.1) | copy-start | bytes 294916
  15.5 10.5 %collective-permute-start.11 = (bf16[64,1536]{1,0:T(8,128)(2,1)S(1)}, bf16[64,1536]{1,0:T(8,128)(2,1)S(1)}, u32[]{:S(2)}, u32[]{:S(2)}) collective-permute-start(bf16[64,1536]{1,0:T(8,128)(2,1)S(1)} %shard_map.45), channel_id=1, source_target_pairs={{0,2},{1,3},{2,0},{3,1},{4,6},{5,7},{6,4},{7,5},{8,10},{9,11},{10,... | collective-permute-start | bytes 589832 | tf_op jit(solution)/shard_map/ppermute | solution.py:50
  16.2 9.8 %collective-permute-start.8 = (bf16[64,1536]{1,0:T(8,128)(2,1)S(1)}, bf16[64,1536]{1,0:T(8,128)(2,1)S(1)}, u32[]{:S(2)}, u32[]{:S(2)}) collective-permute-start(bf16[64,1536]{1,0:T(8,128)(2,1)S(1)} %collective-permute-done.1.refs_0_.refs_5_), channel_id=1, source_target_pairs={{0,16},{1,17},{2,18},{3,19},{4,20},{5,21},{6,22},{7,23},{8,24},{9,... | collective-permute-start | bytes 589832 | tf_op jit(solution)/shard_map/ppermute | solution.py:50
  17.7 9.5 %collective-permute-start.7 = (bf16[64,1536]{1,0:T(8,128)(2,1)S(1)}, bf16[64,1536]{1,0:T(8,128)(2,1)S(1)}, u32[]{:S(2)}, u32[]{:S(2)}) collective-permute-start(bf16[64,1536]{1,0:T(8,128)(2,1)S(1)} %shard_map.43), channel_id=1, source_target_pairs={{0,1},{1,0},{2,3},{3,2},{4,5},{5,4},{6,7},{7,6},{8,9},{9,8},{10,11... | collective-permute-start | bytes 589832 | tf_op jit(solution)/shard_map/ppermute | solution.py:50
  19.2 11.7 %collective-permute-start.10 = (bf16[64,3840]{1,0:T(8,128)(2,1)S(1)}, bf16[64,3840]{1,0:T(8,128)(2,1)S(1)}, u32[]{:S(2)}, u32[]{:S(2)}) collective-permute-start(bf16[64,3840]{1,0:T(8,128)(2,1)S(1)} %shard_map.44), channel_id=1, source_target_pairs={{0,4},{1,5},{2,6},{3,7},{4,0},{5,1},{6,2},{7,3},{8,12},{9,13},{10,... | collective-permute-start | bytes 1474568 | tf_op jit(solution)/shard_map/ppermute | solution.py:50
  19.4 11.6 %collective-permute-start.5 = (bf16[64,3072]{1,0:T(8,128)(2,1)S(1)}, bf16[64,3072]{1,0:T(8,128)(2,1)S(1)}, u32[]{:S(2)}, u32[]{:S(2)}) collective-permute-start(bf16[64,3072]{1,0:T(8,128)(2,1)S(1)} %shard_map.42), channel_id=1, source_target_pairs={{0,8},{1,9},{2,10},{3,11},{4,12},{5,13},{6,14},{7,15},{8,0},{9,1},... | collective-permute-start | bytes 1179656 | tf_op jit(solution)/shard_map/ppermute | solution.py:50
  27.2 3.7 %collective-permute-start.12 = (bf16[64,3072]{1,0:T(8,128)(2,1)S(1)}, bf16[64,3072]{1,0:T(8,128)(2,1)S(1)}, u32[]{:S(2)}, u32[]{:S(2)}) collective-permute-start(bf16[64,3072]{1,0:T(8,128)(2,1)S(1)} %shard_map.46), channel_id=1, source_target_pairs={{0,4},{1,5},{2,6},{3,7},{4,0},{5,1},{6,2},{7,3},{8,12},{9,13},{10,... | collective-permute-start | bytes 1179656 | tf_op jit(solution)/shard_map/ppermute | solution.py:50
  32.0 1.3 %collective-permute-start.13 = (f32[3,12,64]{2,1,0:T(8,128)S(1)}, f32[3,12,64]{2,1,0:T(8,128)S(1)}, u32[]{:S(2)}, u32[]{:S(2)}) collective-permute-start(f32[3,12,64]{2,1,0:T(8,128)S(1)} %pad_maximum_fusion), channel_id=1, source_target_pairs={{0,4},{1,5},{2,6},{3,7},{4,0},{5,1},{6,2},{7,3},{8,12},{9,13},{10,... | collective-permute-start | bytes 27656 | tf_op jit(solution)/shard_map/ppermute | solution.py:50
  33.3 3.8 %collective-permute-start.14 = (f32[3,8,64]{2,1,0:T(8,128)S(1)}, f32[3,8,64]{2,1,0:T(8,128)S(1)}, u32[]{:S(2)}, u32[]{:S(2)}) collective-permute-start(f32[3,8,64]{2,1,0:T(8,128)S(1)} %maximum_select_fusion), channel_id=1, source_target_pairs={{0,1},{1,0},{2,3},{3,2},{4,6},{5,7},{6,4},{7,5},{8,9},{9,8},{10,11... | collective-permute-start | bytes 18440 | tf_op jit(solution)/shard_map/ppermute | solution.py:258
  37.1 3.8 %collective-permute-start.15 = (f32[3,8,64]{2,1,0:T(8,128)S(1)}, f32[3,8,64]{2,1,0:T(8,128)S(1)}, u32[]{:S(2)}, u32[]{:S(2)}) collective-permute-start(f32[3,8,64]{2,1,0:T(8,128)S(1)} %add.10), channel_id=1, source_target_pairs={{0,8},{1,9},{2,10},{3,11},{4,20},{5,21},{6,22},{7,23},{8,0},{9,1},... | collective-permute-start | bytes 18440 | tf_op jit(solution)/shard_map/ppermute | solution.py:258
  40.9 1.2 %collective-permute-start.16 = (f32[3,8,64]{2,1,0:T(8,128)S(1)}, f32[3,8,64]{2,1,0:T(8,128)S(1)}, u32[]{:S(2)}, u32[]{:S(2)}) collective-permute-start(f32[3,8,64]{2,1,0:T(8,128)S(1)} %add.11), channel_id=1, source_target_pairs={{0,4},{1,5},{2,6},{3,7},{4,0},{5,1},{6,2},{7,3},{8,12},{9,13},{10,... | collective-permute-start | bytes 18440 | tf_op jit(solution)/shard_map/ppermute | solution.py:50
  43.3 5.6 %collective-permute-start.17 = (f16[400,128]{1,0:T(8,128)(2,1)S(1)}, f16[400,128]{1,0:T(8,128)(2,1)S(1)}, u32[]{:S(2)}, u32[]{:S(2)}) collective-permute-start(f16[400,128]{1,0:T(8,128)(2,1)S(1)} %convert_element_type.18), channel_id=1, source_target_pairs={{0,1},{1,0},{2,3},{3,2},{4,5},{5,4},{6,7},{7,6},{8,9},{9,8},{10,11... | collective-permute-start | bytes 307208 | tf_op jit(solution)/shard_map/ppermute | solution.py:50
  43.9 6.0 %collective-permute-start.18 = (f16[400,128]{1,0:T(8,128)(2,1)S(1)}, f16[400,128]{1,0:T(8,128)(2,1)S(1)}, u32[]{:S(2)}, u32[]{:S(2)}) collective-permute-start(f16[400,128]{1,0:T(8,128)(2,1)S(1)} %convert_element_type.20), channel_id=1, source_target_pairs={{0,8},{1,9},{2,10},{3,11},{4,12},{5,13},{6,14},{7,15},{8,0},{9,1},... | collective-permute-start | bytes 307208 | tf_op jit(solution)/shard_map/ppermute | solution.py:50
  45.5 5.9 %collective-permute-start.19 = (f16[400,128]{1,0:T(8,128)(2,1)S(1)}, f16[400,128]{1,0:T(8,128)(2,1)S(1)}, u32[]{:S(2)}, u32[]{:S(2)}) collective-permute-start(f16[400,128]{1,0:T(8,128)(2,1)S(1)} %convert_element_type.22), channel_id=1, source_target_pairs={{0,9},{1,8},{2,11},{3,10},{4,13},{5,12},{6,15},{7,14},{8,1},{9,0},... | collective-permute-start | bytes 307208 | tf_op jit(solution)/shard_map/ppermute | solution.py:50

commit v25 on v24

--- a/solution.py
+++ b/solution.py
@@ -74,11 +74,11 @@
                     top = place.bit_length() - 1
                     side[place] = whole(send(side[place ^ (1 << top)][0], masks[top], count))
 
-    for side_t, _, masks in reversed(sides):
-        side_t[1] = whole(send(teacher, masks[0], count))
+    col_t[1] = whole(send(teacher, plane_masks[0], count))
     swapped = [send(value, core_mask, count) for value in (teacher, student)]
     own = join(teacher, student)
     late_t, late_s = after((teacher, student), swapped)
+    row_t[1] = whole(send(after(teacher, swapped[1]), row_masks[0], count))
     for side_t, side_s, masks in reversed(sides):
         side_t[0] = (own, 0, teacher.shape[1])
         for b, mask in enumerate(masks):

time: 52.4 us -> 53.3 us (1.017)
  starting transfers between devices: 20.8 us -> 22.2 us
    ppermute x2, waiting for transfers between devices: 5.32 us -> 4.33 us  [exchange_sums(): got = lax.ppermute(sums, AXES, pairs).reshape(3, -1, 2, 1 << b, rows)]
    ppermute x2, starting transfers between devices: 2.21 us -> 3.2 us  [exchange_sums(): got = lax.ppermute(sums, AXES, pairs).reshape(3, -1, 2, 1 << b, rows)]
  transfers between devices with their start and end apart: 20 -> 20, of which waited for: 12 -> 11; matrix products, arithmetic and copies ran while one was open for 0% -> 0% of each run, Pallas kernels for 0% -> 0%
where the time goes in v25:
time: 53.3 us; the launch traced here: 53.1 us
  waiting for transfers between devices  25 us (47%)
  starting transfers between devices  22.2 us (42%)
  Pallas kernels  2.9 us (5%)
  local copies, waits for them, and re-layouts  2.05 us (4%)
  between operations  0.8 us (2%)
    ppermute x18, waiting for transfers between devices, send(): return lax.ppermute(value, AXES, [(i, i ^ mask) for i in range(count)])  20.7 us
    ppermute x18, starting transfers between devices, send(): return lax.ppermute(value, AXES, [(i, i ^ mask) for i in range(count)])  19 us
    ppermute x2, waiting for transfers between devices, exchange_sums(): got = lax.ppermute(sums, AXES, pairs).reshape(3, -1, 2, 1 << b, rows)  4.33 us
    ppermute x2, starting transfers between devices, exchange_sums(): got = lax.ppermute(sums, AXES, pairs).reshape(3, -1, 2, 1 << b, rows)  3.2 us
    pallas_call x9, Pallas kernels, call(): pl.pallas_call(kernel, out_shape=outputs, **options, compiler_params=pltp...  2.9 us
    unnamed x4, local copies, waits for them, and re-layouts  1.82 us
  transfers between devices with their start and end apart: 20, of which 11 were waited for; matrix products, arithmetic and copies ran while one was open for 0% of the time, Pallas kernels for 0%

profile of v25, /device:TPU:0, one launch (start us, length us, event | category | flops | bytes accessed | tf_op | source)
XLA Modules:
  0.0 53.1 jit_solution(5663632151124496523)
XLA Ops:
  0.6 0.5 collective-permute-start.3
  1.2 4.0 %collective-permute-start.2 = (bf16[64,1536]{1,0:T(8,128)(2,1)}, bf16[64,1536]{1,0:T(8,128)(2,1)S(1)}, u32[]{:S(2)}, u32[]{:S(2)}) collective-permute-start(bf16[64,1536]{1,0:T(8,128)(2,1)} %refs_0_.1), channel_id=1, source_target_pairs={{0,2},{1,3},{2,0},{3,1},{4,6},{5,7},{6,4},{7,5},{8,10},{9,11},{10,... | collective-permute-start | bytes 589832 | tf_op jit(solution)/shard_map/ppermute | solution.py:50
  5.2 1.6 %collective-permute-start.1 = (bf16[64,1536]{1,0:T(8,128)(2,1)}, bf16[64,1536]{1,0:T(8,128)(2,1)S(1)}, u32[]{:S(2)}, u32[]{:S(2)}) collective-permute-start(bf16[64,1536]{1,0:T(8,128)(2,1)} %refs_0_.1), channel_id=1, source_target_pairs={{0,1},{1,0},{2,3},{3,2},{4,5},{5,4},{6,7},{7,6},{8,9},{9,8},{10,11... | collective-permute-start | bytes 589832 | tf_op jit(solution)/shard_map/ppermute | solution.py:50
  6.8 1.5 %collective-permute-start.4 = (bf16[64,1536]{1,0:T(8,128)(2,1)}, bf16[64,1536]{1,0:T(8,128)(2,1)S(1)}, u32[]{:S(2)}, u32[]{:S(2)}) collective-permute-start(bf16[64,1536]{1,0:T(8,128)(2,1)} %refs_0_.1), channel_id=1, source_target_pairs={{0,16},{1,17},{2,18},{3,19},{4,20},{5,21},{6,22},{7,23},{8,24},{9,... | collective-permute-start | bytes 589832 | tf_op jit(solution)/shard_map/ppermute | solution.py:50
  8.3 0.5 collective-permute-start.9
  8.9 1.5 %collective-permute-start.6 = (bf16[64,768]{1,0:T(8,128)(2,1)}, bf16[64,768]{1,0:T(8,128)(2,1)S(1)}, u32[]{:S(2)}, u32[]{:S(2)}) collective-permute-start(bf16[64,768]{1,0:T(8,128)(2,1)} %refs_1_.1), channel_id=1, source_target_pairs={{0,8},{1,9},{2,10},{3,11},{4,12},{5,13},{6,14},{7,15},{8,0},{9,1},... | collective-permute-start | bytes 294920 | tf_op jit(solution)/shard_map/ppermute | solution.py:50
  10.3 0.9 %copy-done = bf16[64,1536]{1,0:T(8,128)(2,1)S(1)} copy-done((bf16[64,1536]{1,0:T(8,128)(2,1)S(1)}, bf16[64,1536]{1,0:T(8,128)(2,1)}, u32[]{:S(2)}) %copy-start) | copy-done | bytes 196632
  11.3 0.9 %copy-done.1 = bf16[64,768]{1,0:T(8,128)(2,1)S(1)} copy-done((bf16[64,768]{1,0:T(8,128)(2,1)S(1)}, bf16[64,768]{1,0:T(8,128)(2,1)}, u32[]{:S(2)}) %copy-start.1) | copy-done | bytes 98328
  12.2 3.3 %collective-permute-done.9.refs_2_.refs_1_.refs_12_ = bf16[64,768]{1,0:T(8,128)(2,1)S(1)} collective-permute-done((bf16[64,768]{1,0:T(8,128)(2,1)}, bf16[64,768]{1,0:T(8,128)(2,1)S(1)}, u32[]{:S(2)}, u32[]{:S(2)}) %collective-permute-start.9) | collective-permute-done | bytes 98336 | tf_op jit(solution)/shard_map/ppermute | solution.py:50
  15.5 1.8 %collective-permute-start.11 = (bf16[64,1536]{1,0:T(8,128)(2,1)S(1)}, bf16[64,1536]{1,0:T(8,128)(2,1)S(1)}, u32[]{:S(2)}, u32[]{:S(2)}) collective-permute-start(bf16[64,1536]{1,0:T(8,128)(2,1)S(1)} %shard_map.45), channel_id=1, source_target_pairs={{0,2},{1,3},{2,0},{3,1},{4,6},{5,7},{6,4},{7,5},{8,10},{9,11},{10,... | collective-permute-start | bytes 589832 | tf_op jit(solution)/shard_map/ppermute | solution.py:50
  17.3 1.6 %collective-permute-start.8 = (bf16[64,1536]{1,0:T(8,128)(2,1)S(1)}, bf16[64,1536]{1,0:T(8,128)(2,1)S(1)}, u32[]{:S(2)}, u32[]{:S(2)}) collective-permute-start(bf16[64,1536]{1,0:T(8,128)(2,1)S(1)} %collective-permute-done.2.refs_0_.refs_5_), channel_id=1, source_target_pairs={{0,16},{1,17},{2,18},{3,19},{4,20},{5,21},{6,22},{7,23},{8,24},{9,... | collective-permute-start | bytes 589832 | tf_op jit(solution)/shard_map/ppermute | solution.py:50
  18.9 0.4 collective-permute-start.7
  19.5 1.6 %collective-permute-start.5 = (bf16[64,3072]{1,0:T(8,128)(2,1)S(1)}, bf16[64,3072]{1,0:T(8,128)(2,1)S(1)}, u32[]{:S(2)}, u32[]{:S(2)}) collective-permute-start(bf16[64,3072]{1,0:T(8,128)(2,1)S(1)} %shard_map.42), channel_id=1, source_target_pairs={{0,8},{1,9},{2,10},{3,11},{4,12},{5,13},{6,14},{7,15},{8,0},{9,1},... | collective-permute-start | bytes 1179656 | tf_op jit(solution)/shard_map/ppermute | solution.py:50
  21.1 4.9 %collective-permute-done.11.refs_1_.refs_11_ = bf16[64,1536]{1,0:T(8,128)(2,1)S(1)} collective-permute-done((bf16[64,1536]{1,0:T(8,128)(2,1)S(1)}, bf16[64,1536]{1,0:T(8,128)(2,1)S(1)}, u32[]{:S(2)}, u32[]{:S(2)}) %collective-permute-start.11) | collective-permute-done | bytes 196640 | tf_op jit(solution)/shard_map/ppermute | solution.py:50
  26.1 2.1 %collective-permute-done.7.refs_3_ = bf16[64,1536]{1,0:T(8,128)(2,1)S(1)} collective-permute-done((bf16[64,1536]{1,0:T(8,128)(2,1)S(1)}, bf16[64,1536]{1,0:T(8,128)(2,1)S(1)}, u32[]{:S(2)}, u32[]{:S(2)}) %collective-permute-start.7) | collective-permute-done | bytes 196640 | tf_op jit(solution)/shard_map/ppermute | solution.py:50
  28.2 2.9 %collective-permute-done.5.refs_2_ = bf16[64,3072]{1,0:T(8,128)(2,1)S(1)} collective-permute-done((bf16[64,3072]{1,0:T(8,128)(2,1)S(1)}, bf16[64,3072]{1,0:T(8,128)(2,1)S(1)}, u32[]{:S(2)}, u32[]{:S(2)}) %collective-permute-start.5) | collective-permute-done | bytes 393248 | tf_op jit(solution)/shard_map/ppermute | solution.py:50
  31.1 1.0 %shard_map.47 = (f32[256,512]{1,0:T(8,128)S(1)}, f32[256,512]{1,0:T(8,128)S(1)}, f32[3,4,64]{2,1,0:T(4,128)S(1)}, f32[3,8,64]{2,1,0:T(8,128)S(1)}) custom-call(bf16[64,2304]{1,0:T(8,128)(2,1)S(1)} %shard_map.41.refs_0_, bf16[64,1536]{1,0:T(8,128)(2,1)S(1)} %collective-permute-done.1.refs_1_, bf16[64,3072]{1,0:T(8,128)(2,1)S(1)} %collective-permute-done.5.refs_2_, ...), custom_call_target="tpu_custom_call" | custom-call | flops 603979776 | bytes 4301824 | tf_op jit(solution)/shard_map/pallas_call | solution.py:185
  32.3 1.2 %collective-permute-done.13 = f32[3,12,64]{2,1,0:T(8,128)S(1)} collective-permute-done((f32[3,12,64]{2,1,0:T(8,128)S(1)}, f32[3,12,64]{2,1,0:T(8,128)S(1)}, u32[]{:S(2)}, u32[]{:S(2)}) %collective-permute-start.13) | collective-permute-done | bytes 9248 | tf_op jit(solution)/shard_map/ppermute | solution.py:50
  33.5 1.6 %collective-permute-start.14 = (f32[3,8,64]{2,1,0:T(8,128)S(1)}, f32[3,8,64]{2,1,0:T(8,128)S(1)}, u32[]{:S(2)}, u32[]{:S(2)}) collective-permute-start(f32[3,8,64]{2,1,0:T(8,128)S(1)} %maximum_select_fusion), channel_id=1, source_target_pairs={{0,1},{1,0},{2,3},{3,2},{4,6},{5,7},{6,4},{7,5},{8,9},{9,8},{10,11... | collective-permute-start | bytes 18440 | tf_op jit(solution)/shard_map/ppermute | solution.py:258
  35.1 2.1 %collective-permute-done.14 = f32[3,8,64]{2,1,0:T(8,128)S(1)} collective-permute-done((f32[3,8,64]{2,1,0:T(8,128)S(1)}, f32[3,8,64]{2,1,0:T(8,128)S(1)}, u32[]{:S(2)}, u32[]{:S(2)}) %collective-permute-start.14) | collective-permute-done | bytes 6176 | tf_op jit(solution)/shard_map/ppermute | solution.py:258
  37.3 1.6 %collective-permute-start.15 = (f32[3,8,64]{2,1,0:T(8,128)S(1)}, f32[3,8,64]{2,1,0:T(8,128)S(1)}, u32[]{:S(2)}, u32[]{:S(2)}) collective-permute-start(f32[3,8,64]{2,1,0:T(8,128)S(1)} %add.10), channel_id=1, source_target_pairs={{0,8},{1,9},{2,10},{3,11},{4,20},{5,21},{6,22},{7,23},{8,0},{9,1},... | collective-permute-start | bytes 18440 | tf_op jit(solution)/shard_map/ppermute | solution.py:258
  38.8 2.2 %collective-permute-done.15 = f32[3,8,64]{2,1,0:T(8,128)S(1)} collective-permute-done((f32[3,8,64]{2,1,0:T(8,128)S(1)}, f32[3,8,64]{2,1,0:T(8,128)S(1)}, u32[]{:S(2)}, u32[]{:S(2)}) %collective-permute-start.15) | collective-permute-done | bytes 6176 | tf_op jit(solution)/shard_map/ppermute | solution.py:258
  41.1 1.2 %collective-permute-done.16 = f32[3,8,64]{2,1,0:T(8,128)S(1)} collective-permute-done((f32[3,8,64]{2,1,0:T(8,128)S(1)}, f32[3,8,64]{2,1,0:T(8,128)S(1)}, u32[]{:S(2)}, u32[]{:S(2)}) %collective-permute-start.16) | collective-permute-done | bytes 6176 | tf_op jit(solution)/shard_map/ppermute | solution.py:50
  42.4 0.1 reshape.26.row_sum
  42.5 0.9 %shard_map.48 = (f32[64,768]{1,0:T(8,128)S(1)}, f32[8,128]{1,0:T(8,128)S(1)}, f32[400,128]{1,0:T(8,128)S(1)}, f32[400,128]{1,0:T(8,128)S(1)}, f32[400,128]{1,0:T(8,128)S(1)}) custom-call(f32[256,512]{1,0:T(8,128)S(1)} %get-tuple-element.29.gram_s, f32[256,512]{1,0:T(8,128)S(1)} %get-tuple-element.30.gram_t, f32[3,1,256]{2,1,0:T(1,128)S(1)} %reshape.26.row_sum, ...), custom_call_target="tpu_custom_call" | custom-call | flops 402653184 | bytes 3445760 | tf_op jit(solution)/shard_map/pallas_call | solution.py:185
  43.4 1.6 %collective-permute-start.17 = (f16[400,128]{1,0:T(8,128)(2,1)S(1)}, f16[400,128]{1,0:T(8,128)(2,1)S(1)}, u32[]{:S(2)}, u32[]{:S(2)}) collective-permute-start(f16[400,128]{1,0:T(8,128)(2,1)S(1)} %convert_element_type.18), channel_id=1, source_target_pairs={{0,1},{1,0},{2,3},{3,2},{4,5},{5,4},{6,7},{7,6},{8,9},{9,8},{10,11... | collective-permute-start | bytes 307208 | tf_op jit(solution)/shard_map/ppermute | solution.py:50
  45.1 1.6 %collective-permute-start.18 = (f16[400,128]{1,0:T(8,128)(2,1)S(1)}, f16[400,128]{1,0:T(8,128)(2,1)S(1)}, u32[]{:S(2)}, u32[]{:S(2)}) collective-permute-start(f16[400,128]{1,0:T(8,128)(2,1)S(1)} %convert_element_type.20), channel_id=1, source_target_pairs={{0,8},{1,9},{2,10},{3,11},{4,12},{5,13},{6,14},{7,15},{8,0},{9,1},... | collective-permute-start | bytes 307208 | tf_op jit(solution)/shard_map/ppermute | solution.py:50
  46.7 0.5 collective-permute-start.19
  47.1 1.3 %collective-permute-done.17 = f16[400,128]{1,0:T(8,128)(2,1)S(1)} collective-permute-done((f16[400,128]{1,0:T(8,128)(2,1)S(1)}, f16[400,128]{1,0:T(8,128)(2,1)S(1)}, u32[]{:S(2)}, u32[]{:S(2)}) %collective-permute-start.17) | collective-permute-done | bytes 102432 | tf_op jit(solution)/shard_map/ppermute | solution.py:50
  48.5 2.6 %collective-permute-done.18 = f16[400,128]{1,0:T(8,128)(2,1)S(1)} collective-permute-done((f16[400,128]{1,0:T(8,128)(2,1)S(1)}, f16[400,128]{1,0:T(8,128)(2,1)S(1)}, u32[]{:S(2)}, u32[]{:S(2)}) %collective-permute-start.18) | collective-permute-done | bytes 102432 | tf_op jit(solution)/shard_map/ppermute | solution.py:50
  51.0 1.2 %collective-permute-done.19 = f16[400,128]{1,0:T(8,128)(2,1)S(1)} collective-permute-done((f16[400,128]{1,0:T(8,128)(2,1)S(1)}, f16[400,128]{1,0:T(8,128)(2,1)S(1)}, u32[]{:S(2)}, u32[]{:S(2)}) %collective-permute-start.19) | collective-permute-done | bytes 102432 | tf_op jit(solution)/shard_map/ppermute | solution.py:50
  52.3 0.8 %shard_map.49 = (f32[64,768]{1,0:T(8,128)}, f32[1,1]{1,0:T(1,128)}) custom-call(f32[64,768]{1,0:T(8,128)S(1)} %get-tuple-element.33.own, f32[8,128]{1,0:T(8,128)S(1)} %get-tuple-element.34.share, f32[400,128]{1,0:T(8,128)S(1)} %convert_element_type.19.refs_0_, f32[400,128]{1,0:T(8,128)S(1)} %convert_element_type.21.refs_1_, ...), custom_call_target="tpu_custom_call" | custom-call | bytes 1011716 | tf_op jit(solution)/shard_map/pallas_call | solution.py:185
  (40 shorter events, 0.8 us)
Async XLA Ops:
  0.6 6.2 %collective-permute-start.3 = (bf16[64,1536]{1,0:T(8,128)(2,1)}, bf16[64,1536]{1,0:T(8,128)(2,1)S(1)}, u32[]{:S(2)}, u32[]{:S(2)}) collective-permute-start(bf16[64,1536]{1,0:T(8,128)(2,1)} %refs_0_.1), channel_id=1, source_target_pairs={{0,4},{1,5},{2,6},{3,7},{4,0},{5,1},{6,2},{7,3},{8,12},{9,13},{10,... | collective-permute-start | bytes 589832 | tf_op jit(solution)/shard_map/ppermute | solution.py:50
  1.1 4.1 %collective-permute-start = (bf16[64,768]{1,0:T(8,128)(2,1)}, bf16[64,768]{1,0:T(8,128)(2,1)S(1)}, u32[]{:S(2)}, u32[]{:S(2)}) collective-permute-start(bf16[64,768]{1,0:T(8,128)(2,1)} %refs_1_.1), channel_id=1, source_target_pairs={{0,4},{1,5},{2,6},{3,7},{4,0},{5,1},{6,2},{7,3},{8,12},{9,13},{10,... | collective-permute-start | bytes 294920 | tf_op jit(solution)/shard_map/ppermute | solution.py:50
  1.2 16.1 %collective-permute-start.2 = (bf16[64,1536]{1,0:T(8,128)(2,1)}, bf16[64,1536]{1,0:T(8,128)(2,1)S(1)}, u32[]{:S(2)}, u32[]{:S(2)}) collective-permute-start(bf16[64,1536]{1,0:T(8,128)(2,1)} %refs_0_.1), channel_id=1, source_target_pairs={{0,2},{1,3},{2,0},{3,1},{4,6},{5,7},{6,4},{7,5},{8,10},{9,11},{10,... | collective-permute-start | bytes 589832 | tf_op jit(solution)/shard_map/ppermute | solution.py:50
  5.2 12.1 %collective-permute-start.1 = (bf16[64,1536]{1,0:T(8,128)(2,1)}, bf16[64,1536]{1,0:T(8,128)(2,1)S(1)}, u32[]{:S(2)}, u32[]{:S(2)}) collective-permute-start(bf16[64,1536]{1,0:T(8,128)(2,1)} %refs_0_.1), channel_id=1, source_target_pairs={{0,1},{1,0},{2,3},{3,2},{4,5},{5,4},{6,7},{7,6},{8,9},{9,8},{10,11... | collective-permute-start | bytes 589832 | tf_op jit(solution)/shard_map/ppermute | solution.py:50
  6.8 10.5 %collective-permute-start.4 = (bf16[64,1536]{1,0:T(8,128)(2,1)}, bf16[64,1536]{1,0:T(8,128)(2,1)S(1)}, u32[]{:S(2)}, u32[]{:S(2)}) collective-permute-start(bf16[64,1536]{1,0:T(8,128)(2,1)} %refs_0_.1), channel_id=1, source_target_pairs={{0,16},{1,17},{2,18},{3,19},{4,20},{5,21},{6,22},{7,23},{8,24},{9,... | collective-permute-start | bytes 589832 | tf_op jit(solution)/shard_map/ppermute | solution.py:50
  8.3 7.1 %collective-permute-start.9 = (bf16[64,768]{1,0:T(8,128)(2,1)}, bf16[64,768]{1,0:T(8,128)(2,1)S(1)}, u32[]{:S(2)}, u32[]{:S(2)}) collective-permute-start(bf16[64,768]{1,0:T(8,128)(2,1)} %refs_1_.1), channel_id=1, source_target_pairs={{0,16},{1,17},{2,18},{3,19},{4,20},{5,21},{6,22},{7,23},{8,24},{9,... | collective-permute-start | bytes 294920 | tf_op jit(solution)/shard_map/ppermute | solution.py:50
  8.9 6.6 %collective-permute-start.6 = (bf16[64,768]{1,0:T(8,128)(2,1)}, bf16[64,768]{1,0:T(8,128)(2,1)S(1)}, u32[]{:S(2)}, u32[]{:S(2)}) collective-permute-start(bf16[64,768]{1,0:T(8,128)(2,1)} %refs_1_.1), channel_id=1, source_target_pairs={{0,8},{1,9},{2,10},{3,11},{4,12},{5,13},{6,14},{7,15},{8,0},{9,1},... | collective-permute-start | bytes 294920 | tf_op jit(solution)/shard_map/ppermute | solution.py:50
  10.3 0.9 %copy-start = (bf16[64,1536]{1,0:T(8,128)(2,1)S(1)}, bf16[64,1536]{1,0:T(8,128)(2,1)}, u32[]{:S(2)}) copy-start(bf16[64,1536]{1,0:T(8,128)(2,1)} %refs_0_.1) | copy-start | bytes 589828
  11.3 0.9 %copy-start.1 = (bf16[64,768]{1,0:T(8,128)(2,1)S(1)}, bf16[64,768]{1,0:T(8,128)(2,1)}, u32[]{:S(2)}) copy-start(bf16[64,768]{1,0:T(8,128)(2,1)} %refs_1_.1) | copy-start | bytes 294916
  15.5 10.5 %collective-permute-start.11 = (bf16[64,1536]{1,0:T(8,128)(2,1)S(1)}, bf16[64,1536]{1,0:T(8,128)(2,1)S(1)}, u32[]{:S(2)}, u32[]{:S(2)}) collective-permute-start(bf16[64,1536]{1,0:T(8,128)(2,1)S(1)} %shard_map.45), channel_id=1, source_target_pairs={{0,2},{1,3},{2,0},{3,1},{4,6},{5,7},{6,4},{7,5},{8,10},{9,11},{10,... | collective-permute-start | bytes 589832 | tf_op jit(solution)/shard_map/ppermute | solution.py:50
  17.3 8.7 %collective-permute-start.8 = (bf16[64,1536]{1,0:T(8,128)(2,1)S(1)}, bf16[64,1536]{1,0:T(8,128)(2,1)S(1)}, u32[]{:S(2)}, u32[]{:S(2)}) collective-permute-start(bf16[64,1536]{1,0:T(8,128)(2,1)S(1)} %collective-permute-done.2.refs_0_.refs_5_), channel_id=1, source_target_pairs={{0,16},{1,17},{2,18},{3,19},{4,20},{5,21},{6,22},{7,23},{8,24},{9,... | collective-permute-start | bytes 589832 | tf_op jit(solution)/shard_map/ppermute | solution.py:50
  18.9 9.3 %collective-permute-start.7 = (bf16[64,1536]{1,0:T(8,128)(2,1)S(1)}, bf16[64,1536]{1,0:T(8,128)(2,1)S(1)}, u32[]{:S(2)}, u32[]{:S(2)}) collective-permute-start(bf16[64,1536]{1,0:T(8,128)(2,1)S(1)} %shard_map.43), channel_id=1, source_target_pairs={{0,1},{1,0},{2,3},{3,2},{4,5},{5,4},{6,7},{7,6},{8,9},{9,8},{10,11... | collective-permute-start | bytes 589832 | tf_op jit(solution)/shard_map/ppermute | solution.py:50
  19.4 11.7 %collective-permute-start.10 = (bf16[64,3840]{1,0:T(8,128)(2,1)S(1)}, bf16[64,3840]{1,0:T(8,128)(2,1)S(1)}, u32[]{:S(2)}, u32[]{:S(2)}) collective-permute-start(bf16[64,3840]{1,0:T(8,128)(2,1)S(1)} %shard_map.44), channel_id=1, source_target_pairs={{0,4},{1,5},{2,6},{3,7},{4,0},{5,1},{6,2},{7,3},{8,12},{9,13},{10,... | collective-permute-start | bytes 1474568 | tf_op jit(solution)/shard_map/ppermute | solution.py:50
  19.5 11.6 %collective-permute-start.5 = (bf16[64,3072]{1,0:T(8,128)(2,1)S(1)}, bf16[64,3072]{1,0:T(8,128)(2,1)S(1)}, u32[]{:S(2)}, u32[]{:S(2)}) collective-permute-start(bf16[64,3072]{1,0:T(8,128)(2,1)S(1)} %shard_map.42), channel_id=1, source_target_pairs={{0,8},{1,9},{2,10},{3,11},{4,12},{5,13},{6,14},{7,15},{8,0},{9,1},... | collective-permute-start | bytes 1179656 | tf_op jit(solution)/shard_map/ppermute | solution.py:50
  28.2 2.9 %collective-permute-start.12 = (bf16[64,3072]{1,0:T(8,128)(2,1)S(1)}, bf16[64,3072]{1,0:T(8,128)(2,1)S(1)}, u32[]{:S(2)}, u32[]{:S(2)}) collective-permute-start(bf16[64,3072]{1,0:T(8,128)(2,1)S(1)} %shard_map.46), channel_id=1, source_target_pairs={{0,4},{1,5},{2,6},{3,7},{4,0},{5,1},{6,2},{7,3},{8,12},{9,13},{10,... | collective-permute-start | bytes 1179656 | tf_op jit(solution)/shard_map/ppermute | solution.py:50
  32.2 1.3 %collective-permute-start.13 = (f32[3,12,64]{2,1,0:T(8,128)S(1)}, f32[3,12,64]{2,1,0:T(8,128)S(1)}, u32[]{:S(2)}, u32[]{:S(2)}) collective-permute-start(f32[3,12,64]{2,1,0:T(8,128)S(1)} %pad_maximum_fusion), channel_id=1, source_target_pairs={{0,4},{1,5},{2,6},{3,7},{4,0},{5,1},{6,2},{7,3},{8,12},{9,13},{10,... | collective-permute-start | bytes 27656 | tf_op jit(solution)/shard_map/ppermute | solution.py:50
  33.5 3.8 %collective-permute-start.14 = (f32[3,8,64]{2,1,0:T(8,128)S(1)}, f32[3,8,64]{2,1,0:T(8,128)S(1)}, u32[]{:S(2)}, u32[]{:S(2)}) collective-permute-start(f32[3,8,64]{2,1,0:T(8,128)S(1)} %maximum_select_fusion), channel_id=1, source_target_pairs={{0,1},{1,0},{2,3},{3,2},{4,6},{5,7},{6,4},{7,5},{8,9},{9,8},{10,11... | collective-permute-start | bytes 18440 | tf_op jit(solution)/shard_map/ppermute | solution.py:258
  37.3 3.8 %collective-permute-start.15 = (f32[3,8,64]{2,1,0:T(8,128)S(1)}, f32[3,8,64]{2,1,0:T(8,128)S(1)}, u32[]{:S(2)}, u32[]{:S(2)}) collective-permute-start(f32[3,8,64]{2,1,0:T(8,128)S(1)} %add.10), channel_id=1, source_target_pairs={{0,8},{1,9},{2,10},{3,11},{4,20},{5,21},{6,22},{7,23},{8,0},{9,1},... | collective-permute-start | bytes 18440 | tf_op jit(solution)/shard_map/ppermute | solution.py:258
  41.0 1.2 %collective-permute-start.16 = (f32[3,8,64]{2,1,0:T(8,128)S(1)}, f32[3,8,64]{2,1,0:T(8,128)S(1)}, u32[]{:S(2)}, u32[]{:S(2)}) collective-permute-start(f32[3,8,64]{2,1,0:T(8,128)S(1)} %add.11), channel_id=1, source_target_pairs={{0,4},{1,5},{2,6},{3,7},{4,0},{5,1},{6,2},{7,3},{8,12},{9,13},{10,... | collective-permute-start | bytes 18440 | tf_op jit(solution)/shard_map/ppermute | solution.py:50
  43.4 5.0 %collective-permute-start.17 = (f16[400,128]{1,0:T(8,128)(2,1)S(1)}, f16[400,128]{1,0:T(8,128)(2,1)S(1)}, u32[]{:S(2)}, u32[]{:S(2)}) collective-permute-start(f16[400,128]{1,0:T(8,128)(2,1)S(1)} %convert_element_type.18), channel_id=1, source_target_pairs={{0,1},{1,0},{2,3},{3,2},{4,5},{5,4},{6,7},{7,6},{8,9},{9,8},{10,11... | collective-permute-start | bytes 307208 | tf_op jit(solution)/shard_map/ppermute | solution.py:50
  45.1 5.9 %collective-permute-start.18 = (f16[400,128]{1,0:T(8,128)(2,1)S(1)}, f16[400,128]{1,0:T(8,128)(2,1)S(1)}, u32[]{:S(2)}, u32[]{:S(2)}) collective-permute-start(f16[400,128]{1,0:T(8,128)(2,1)S(1)} %convert_element_type.20), channel_id=1, source_target_pairs={{0,8},{1,9},{2,10},{3,11},{4,12},{5,13},{6,14},{7,15},{8,0},{9,1},... | collective-permute-start | bytes 307208 | tf_op jit(solution)/shard_map/ppermute | solution.py:50
  46.7 5.6 %collective-permute-start.19 = (f16[400,128]{1,0:T(8,128)(2,1)S(1)}, f16[400,128]{1,0:T(8,128)(2,1)S(1)}, u32[]{:S(2)}, u32[]{:S(2)}) collective-permute-start(f16[400,128]{1,0:T(8,128)(2,1)S(1)} %convert_element_type.22), channel_id=1, source_target_pairs={{0,9},{1,8},{2,11},{3,10},{4,13},{5,12},{6,15},{7,14},{8,1},{9,0},... | collective-permute-start | bytes 307208 | tf_op jit(solution)/shard_map/ppermute | solution.py:50
